TPU v7x, 128 devices: a whole 4x4x4 slice. The times are simulated.
128 devices in a mesh: dp: 16 (over y, z_lo, core), row: 4 (over x), col: 2 (over z_hi).
Axes of the slice: x: 4, y: 4, z: 4 (z_hi: 2, z_lo: 2; z = z_hi * 2 + z_lo), core: 2. Of those that a mesh axis runs over, the one named last changes fastest.
Arguments:
- tokens: bfloat16 [20480, 2048], P(('dp', 'row', 'col')), may hold values from -6 to 6
- cotangent: bfloat16 [20480, 2048], P(('dp', 'row', 'col')), may hold values from -6 to 6
- gain_one: float32 [2048], replicated, may hold values from 0.5 to 1.5
- qkv_weight: bfloat16 [2048, 2560], P('col', 'row'), may hold values from -0.125 to 0.125
- out_weight: bfloat16 [2048, 2048], P(('row', 'col')), may hold values from -0.5 to 0.5
- gate_weight: bfloat16 [2048, 5632], P('col', 'row'), may hold values from -0.125 to 0.125
- up_weight: bfloat16 [2048, 5632], P('col', 'row'), may hold values from -0.125 to 0.125
- down_weight: bfloat16 [5632, 2048], P(('row', 'col')), may hold values from -0.15625 to 0.15625
- gain_two: float32 [2048], replicated, may hold values from 0.5 to 1.5
- seq_lengths: int32 [32], replicated, may hold values from 1 to 1280, as said below
- seq_replica: int32 [32], replicated, may hold values from 0 to 15, as said below
Outputs:
- layer_out: bfloat16 [20480, 2048], P(('dp', 'row', 'col'))
- input_grad: bfloat16 [20480, 2048], P(('dp', 'row', 'col'))
- grad_gain_one: float32 [2048], replicated
- grad_qkv: float32 [2048, 2560], P('col', 'row')
- grad_out: float32 [2048, 2048], P(('row', 'col'))
- grad_gate: float32 [2048, 5632], P('col', 'row')
- grad_up: float32 [2048, 5632], P('col', 'row')
- grad_down: float32 [5632, 2048], P(('row', 'col'))
- grad_gain_two: float32 [2048], replicated
Inputs may be any that keep to these rules, and one draw needn't show every extreme that they name: `seq_lengths`: sequence i is dealt to replica seq_replica[i]; every replica receives sequences whose lengths sum to 1280 or less, one replica's exactly to 1280; the lowest-numbered sequence of each replica is longer than 1120, and a replica holds one or three sequences. `seq_replica`: each of the 32 sequences names its replica.
All inputs are finite; a program needn't handle non-finite values.
Results may differ from a plain program's by a relative error of at most 0.035.
Values may be sent and summed in bfloat16 or wider, within the bound.
No kernel may reach another device: no remote copies, remote signals or barrier semaphores. Data moves between devices by JAX's collectives and lax.ppermute only.
A program may use at most 192 MiB of HBM per device.

v0:
```python
import math

import jax
import jax.numpy as jnp
from jax import lax
from jax.sharding import PartitionSpec as P

HEADS = 32
KV = 4
HD = 64


EPSILON = 1e-05
ROTARY_BASE = 10000.0
MASKED = -1e30


def normed(values, scale_gain):
    inverse_rms = lax.rsqrt(jnp.mean(values * values, axis=-1, keepdims=True) + EPSILON)
    return values * inverse_rms * scale_gain


def layout(lengths, replica, replica_id, capacity):
    is_own = replica == replica_id
    seq_sizes = jnp.where(is_own, lengths, 0)
    starts = jnp.cumsum(seq_sizes) - seq_sizes
    row_ids = jnp.arange(capacity, dtype=jnp.int32)
    inside = (row_ids[:, None] >= starts[None, :]) & (
        row_ids[:, None] < (starts + seq_sizes)[None, :]
    )
    number = jnp.arange(1, lengths.shape[0] + 1, dtype=jnp.int32)
    segment = jnp.sum(jnp.where(inside, number[None, :], 0), axis=1)
    seq_begin = jnp.sum(jnp.where(inside, starts[None, :], 0), axis=1)
    filled = jnp.sum(seq_sizes)
    seq_begin = seq_begin + jnp.where(segment == 0, filled, 0)
    return (segment, row_ids - seq_begin)


def rotary(position, head_size):
    half_size = head_size // 2
    frequency = ROTARY_BASE ** (-jnp.arange(half_size, dtype=jnp.float32) * (2.0 / head_size))
    angles = position.astype(jnp.float32)[:, None] * frequency[None, :]
    return (jnp.cos(angles)[:, None, :], jnp.sin(angles)[:, None, :])


def rotate(values, cosine, sine):
    half_size = values.shape[-1] // 2
    lower_half = values[..., :half_size]
    upper_half = values[..., half_size:]
    return jnp.concatenate(
        [lower_half * cosine - upper_half * sine, upper_half * cosine + lower_half * sine], axis=-1
    )


def contract_rows(left, right):
    return lax.dot_general(
        left, right, (((0,), (0,)), ((), ())), preferred_element_type=jnp.float32
    )


def contract_cols(left, right):
    return lax.dot_general(
        left, right, (((1,), (1,)), ((), ())), preferred_element_type=jnp.float32
    )


def replica_sum(first_grad, second_grad, third_grad):
    return (
        lax.psum(first_grad.astype(jnp.bfloat16), "dp").astype(jnp.float32),
        lax.psum(second_grad.astype(jnp.bfloat16), "dp").astype(jnp.float32),
        lax.psum(third_grad.astype(jnp.bfloat16), "dp").astype(jnp.float32),
    )


def gather_rows(values):
    return lax.all_gather(values, ("row", "col"), axis=0, tiled=True)


def on_device(
    tokens,
    cotangent,
    gain_one,
    qkv_weight,
    out_weight,
    gate_weight,
    up_weight,
    down_weight,
    gain_two,
    seq_lengths,
    seq_replica,
):
    row_count = lax.axis_size("row")
    col_count = lax.axis_size("col")
    col_index = lax.axis_index("col")
    local_rows = tokens.shape[0]
    model_width = tokens.shape[1]
    half_width = qkv_weight.shape[0]
    capacity = local_rows * row_count * col_count
    per_kv = HEADS // KV
    q_col = per_kv // col_count
    q_first = col_index * q_col
    my_cols = col_index * half_width
    score_scale = HD ** (-0.5)
    segment, position = layout(seq_lengths, seq_replica, lax.axis_index("dp"), capacity)
    cosine, sine = rotary(position, HD)
    block_rows = math.gcd(capacity, 512)
    block_count = capacity // block_rows
    row_ids = jnp.arange(capacity, dtype=jnp.int32)
    firsts = jnp.arange(block_count, dtype=jnp.int32) * block_rows

    def back_reduce(half_term):
        return lax.psum_scatter(
            lax.dynamic_update_slice_in_dim(
                jnp.zeros((local_rows * lax.axis_size(("row", "col")), model_width), jnp.float32),
                half_term(jnp.int32(0), local_rows * lax.axis_size(("row", "col"))),
                my_cols,
                1,
            ).astype(jnp.bfloat16),
            ("row", "col"),
            scatter_dimension=0,
            tiled=True,
        ).astype(jnp.float32)

    resid_in = tokens.astype(jnp.float32)
    normed_one = normed(resid_in, gain_one).astype(jnp.bfloat16)
    gathered_one = gather_rows(normed_one)
    mine_one = lax.dynamic_slice_in_dim(gathered_one, my_cols, half_width, 1)
    mixed = lax.psum(
        jnp.dot(mine_one, qkv_weight, preferred_element_type=jnp.float32).astype(jnp.bfloat16),
        "col",
    ).astype(jnp.float32)
    all_queries = mixed[:, : per_kv * HD].reshape(capacity, per_kv, HD)
    queries = lax.dynamic_slice_in_dim(all_queries, q_first, q_col, 1)
    queries = rotate(queries, cosine, sine).astype(jnp.bfloat16)
    key_heads = rotate(
        mixed[:, per_kv * HD : (per_kv + 1) * HD].reshape(capacity, 1, HD), cosine, sine
    ).astype(jnp.bfloat16)
    value_heads = mixed[:, (per_kv + 1) * HD :].reshape(capacity, 1, HD).astype(jnp.bfloat16)
    key_rep = jnp.broadcast_to(key_heads, (capacity, q_col, HD))
    value_rep = jnp.broadcast_to(value_heads, (capacity, q_col, HD))

    def scores_of(first_row, query_block):
        raw_scores = (
            jnp.einsum("qhd,khd->hqk", query_block, key_rep, preferred_element_type=jnp.float32)
            * score_scale
        )
        block_ids = first_row + jnp.arange(block_rows, dtype=jnp.int32)
        block_segment = lax.dynamic_slice_in_dim(segment, first_row, block_rows)
        allowed = (block_segment[:, None] == segment[None, :]) & (
            block_ids[:, None] >= row_ids[None, :]
        )
        return jnp.where(allowed[None], raw_scores, MASKED)

    def forward_block(scan_item):
        first_row, query_block = scan_item
        scores = scores_of(first_row, query_block)
        row_max = jnp.max(scores, axis=-1, keepdims=True)
        expvals = jnp.exp(scores - row_max)
        denominator = jnp.sum(expvals, axis=-1, keepdims=True)
        weights = (expvals / denominator).astype(jnp.bfloat16)
        result = jnp.einsum("hqk,khd->qhd", weights, value_rep, preferred_element_type=jnp.float32)
        return (result.astype(jnp.bfloat16), row_max + jnp.log(denominator))

    query_blocks = queries.reshape(block_count, block_rows, q_col, HD)
    attended, logsum = lax.map(forward_block, (firsts, query_blocks))
    attended = attended.reshape(capacity, q_col * HD)
    att_rows = attended
    after_attn = resid_in + lax.psum_scatter(
        jnp.dot(att_rows, out_weight, preferred_element_type=jnp.float32).astype(jnp.bfloat16),
        ("row", "col"),
        scatter_dimension=0,
        tiled=True,
    ).astype(jnp.float32)
    normed_two = normed(after_attn, gain_two).astype(jnp.bfloat16)
    gathered_two = gather_rows(normed_two)
    mine_two = lax.dynamic_slice_in_dim(gathered_two, my_cols, half_width, 1)
    gate, up_value = (
        lax.psum_scatter(
            jnp.dot(mine_two, gate_weight, preferred_element_type=jnp.float32).astype(jnp.bfloat16),
            "col",
            scatter_dimension=1,
            tiled=True,
        ).astype(jnp.float32),
        lax.psum_scatter(
            jnp.dot(mine_two, up_weight, preferred_element_type=jnp.float32).astype(jnp.bfloat16),
            "col",
            scatter_dimension=1,
            tiled=True,
        ).astype(jnp.float32),
    )
    sigmoid_gate = jax.nn.sigmoid(gate)
    activated = gate * sigmoid_gate
    hidden = (activated * up_value).astype(jnp.bfloat16)
    hidden_rows = hidden
    layer_out = after_attn + lax.psum_scatter(
        jnp.dot(hidden_rows, down_weight, preferred_element_type=jnp.float32).astype(jnp.bfloat16),
        ("row", "col"),
        scatter_dimension=0,
        tiled=True,
    ).astype(jnp.float32)
    shard_rows = lax.all_gather(cotangent, ("row", "col"), axis=0, tiled=True)
    hidden_rows = hidden
    accum_grad = contract_rows(hidden_rows, shard_rows)
    partial_rows = contract_cols(shard_rows, down_weight)
    grad_down = accum_grad
    d_hidden = partial_rows
    d_gate = (d_hidden * up_value * sigmoid_gate * (1.0 + gate * (1.0 - sigmoid_gate))).astype(
        jnp.bfloat16
    )
    d_up = (d_hidden * activated).astype(jnp.bfloat16)
    gate_grad_all, up_grad_all = (
        lax.all_gather(d_gate, "col", axis=1, tiled=True),
        lax.all_gather(d_up, "col", axis=1, tiled=True),
    )
    grad_gate = contract_rows(mine_two, gate_grad_all)
    grad_up = contract_rows(mine_two, up_grad_all)

    def ffn_back_term(offset, row_total):
        return contract_cols(gate_grad_all, gate_weight) + contract_cols(up_grad_all, up_weight)

    d_normed_two = back_reduce(ffn_back_term)
    _, norm_pull_two = jax.vjp(normed, after_attn, gain_two)
    norm_back_two, gain_grad_two = norm_pull_two(d_normed_two)
    after_grad = cotangent.astype(jnp.float32) + norm_back_two
    shard_rows = lax.all_gather(after_grad.astype(jnp.bfloat16), ("row", "col"), axis=0, tiled=True)
    att_rows = attended
    accum_grad = contract_rows(att_rows, shard_rows)
    partial_rows = contract_cols(shard_rows, out_weight)
    grad_out = accum_grad
    d_attended = partial_rows
    d_attended = d_attended.astype(jnp.bfloat16).reshape(block_count, block_rows, q_col, HD)

    def back_block(carried, scan_item):
        key_grad, value_grad = carried
        first_row, query_block, out_grad_block, logsum_block = scan_item
        scores = scores_of(first_row, query_block)
        weights = jnp.exp(scores - logsum_block)
        d_weights = jnp.einsum(
            "qhd,khd->hqk", out_grad_block, value_rep, preferred_element_type=jnp.float32
        )
        row_dot = jnp.sum(d_weights * weights, axis=-1, keepdims=True)
        d_scores = (weights * (d_weights - row_dot)).astype(jnp.bfloat16)
        query_grad = (
            jnp.einsum("hqk,khd->qhd", d_scores, key_rep, preferred_element_type=jnp.float32)
            * score_scale
        )
        key_grad = (
            key_grad
            + jnp.einsum("hqk,qhd->khd", d_scores, query_block, preferred_element_type=jnp.float32)
            * score_scale
        )
        value_grad = value_grad + jnp.einsum(
            "hqk,qhd->khd",
            weights.astype(jnp.bfloat16),
            out_grad_block,
            preferred_element_type=jnp.float32,
        )
        return ((key_grad, value_grad), query_grad)

    zero_state = jnp.zeros((capacity, q_col, HD), jnp.float32)
    (key_grad, value_grad), query_grad = lax.scan(
        back_block, (zero_state, zero_state), (firsts, query_blocks, d_attended, logsum)
    )
    query_grad = query_grad.reshape(capacity, q_col, HD)
    widened = lax.dynamic_update_slice_in_dim(
        jnp.zeros((capacity, per_kv, HD), jnp.float32), query_grad, q_first, 1
    )
    query_raw = rotate(widened, cosine, -sine).reshape(capacity, per_kv * HD)
    key_raw = rotate(jnp.sum(key_grad, axis=1, keepdims=True), cosine, -sine).reshape(capacity, HD)
    value_raw = jnp.sum(value_grad, axis=1)
    d_mixed = jnp.concatenate([query_raw, key_raw, value_raw], axis=1)
    d_mixed = lax.psum(d_mixed.astype(jnp.bfloat16), "col")
    grad_qkv = contract_rows(mine_one, d_mixed)

    def qkv_back_term(offset, row_total):
        return contract_cols(d_mixed, qkv_weight)

    d_normed_one = back_reduce(qkv_back_term)
    _, norm_pull_one = jax.vjp(normed, resid_in, gain_one)
    norm_back_one, gain_grad_one = norm_pull_one(d_normed_one)
    input_grad = (after_grad + norm_back_one).astype(jnp.bfloat16)
    gain_grad_one, gain_grad_two = lax.psum((gain_grad_one, gain_grad_two), ("row", "col"))
    grad_gate, grad_up, grad_down = replica_sum(grad_gate, grad_up, grad_down)
    grad_qkv, grad_out, gain_pair = replica_sum(
        grad_qkv, grad_out, jnp.stack([gain_grad_one, gain_grad_two])
    )
    return (
        layer_out.astype(jnp.bfloat16),
        input_grad,
        gain_pair[0],
        grad_qkv,
        grad_out,
        grad_gate,
        grad_up,
        grad_down,
        gain_pair[1],
    )


def solution(mesh):
    return jax.shard_map(
        on_device,
        mesh=mesh,
        in_specs=(
            P(("dp", "row", "col"), None),
            P(("dp", "row", "col"), None),
            P(),
            P("col", "row"),
            P(("row", "col"), None),
            P("col", "row"),
            P("col", "row"),
            P(("row", "col"), None),
            P(),
            P(),
            P(),
        ),
        out_specs=(
            P(("dp", "row", "col"), None),
            P(("dp", "row", "col"), None),
            P(),
            P("col", "row"),
            P(("row", "col"), None),
            P("col", "row"),
            P("col", "row"),
            P(("row", "col"), None),
            P(),
        ),
        check_vma=False,
    )
```

profile of v0, /device:TPU:1, one launch (start us, length us, event | category | flops | bytes accessed | tf_op | source)
XLA Modules:
  0.0 1564.5 jit_solution(8422881418917158577)
XLA Ops:
  11.0 83.2 %all-gather.7.cloned.1.call-done = bf16[1280,2048]{1,0:T(8,128)(2,1)} async-done(((bf16[160,2048]{1,0:T(8,128)(2,1)}), bf16[1280,2048]{1,0:T(8,128)(2,1)}) %all-gather.7.cloned.1.call-update) | async-done | bytes 5242896 | tf_op jit(solution)/shard_map/all_gather | solution.py:76
  94.1 5.2 convolution_convert_fusion.7
  103.1 55.6 %all-reduce.6.cloned.1.call-done = bf16[1280,640]{0,1:T(8,128)(2,1)} async-done(((bf16[1280,640]{0,1:T(8,128)(2,1)}), bf16[1280,640]{0,1:T(8,128)(2,1)}) %all-reduce.6.cloned.1.call-update) | async-done | bytes 1638416 | tf_op jit(solution)/shard_map/psum | solution.py:128
  168.4 49.0 %while.28 = (s32[]{:T(128)}, bf16[5,256,4,64]{1,3,2,0:T(8,128)(2,1)}, f32[5,4,256,1]{2,1,3,0:T(4,128)}, s32[5]{0:T(128)}, s32[1280]{0:T(1024)S(1)}, /*index=5*/b...) while((s32[]{:T(128)}, ...), condition=%wide.region_9.10_spmd.clone, body=%wide.region_6.9_spmd.clone.sunk | while | flops 347077888 | bytes 17018532 | solution.py:165
  220.2 3.9 convolution_convert_fusion.3
  224.4 89.8 %reduce-scatter.7.cloned.1.call-done = bf16[160,2048]{1,0:T(8,128)(2,1)} async-done(((bf16[1280,2048]{1,0:T(8,128)(2,1)}), bf16[160,2048]{1,0:T(8,128)(2,1)}) %reduce-scatter.7.cloned.1.call-update) | async-done | bytes 655376 | tf_op jit(solution)/shard_map/reduce_scatter | solution.py:168
  319.5 78.7 %all-gather.9.cloned.1.call-done = bf16[1280,2048]{1,0:T(8,128)(2,1)} async-done(((bf16[160,2048]{1,0:T(8,128)(2,1)}), bf16[1280,2048]{1,0:T(8,128)(2,1)}) %all-gather.9.cloned.1.call-update) | async-done | bytes 5242896 | tf_op jit(solution)/shard_map/all_gather | solution.py:76
  398.3 7.5 convolution_convert_fusion
  405.8 8.5 convolution_convert_fusion.1
  414.4 64.1 %all-gather.11.cloned.1.call-done = bf16[1280,2048]{1,0:T(8,128)(2,1)} async-done(((bf16[160,2048]{1,0:T(8,128)(2,1)}), bf16[1280,2048]{1,0:T(8,128)(2,1)}) %all-gather.11.cloned.1.call-update) | async-done | bytes 5242896 | tf_op jit(solution)/shard_map/all_gather | solution.py:201
  478.5 53.5 %reduce-scatter.11.cloned.1.call-done = bf16[1280,704]{0,1:T(8,128)(2,1)} async-done(((bf16[1280,1408]{0,1:T(8,128)(2,1)}), bf16[1280,704]{0,1:T(8,128)(2,1)}) %reduce-scatter.11.cloned.1.call-update) | async-done | bytes 1802256 | tf_op jit(solution)/shard_map/reduce_scatter | solution.py:184
  532.0 54.9 %reduce-scatter.9.cloned.1.call-done = bf16[1280,704]{0,1:T(8,128)(2,1)} async-done(((bf16[1280,1408]{0,1:T(8,128)(2,1)}), bf16[1280,704]{0,1:T(8,128)(2,1)}) %reduce-scatter.9.cloned.1.call-update) | async-done | bytes 1802256 | tf_op jit(solution)/shard_map/reduce_scatter | solution.py:178
  586.9 11.2 multiply_convert_fusion.1
  599.3 52.5 %all-gather.13.cloned.1.call-done = bf16[1280,1408]{0,1:T(8,128)(2,1)} async-done(((bf16[1280,704]{0,1:T(8,128)(2,1)}), bf16[1280,1408]{0,1:T(8,128)(2,1)}) %all-gather.13.cloned.1.call-update) | async-done | bytes 3604496 | tf_op jit(solution)/shard_map/all_gather | solution.py:212
  651.8 9.6 fusion.111
  661.3 46.2 %all-gather.15.cloned.1.call-done = bf16[1280,1408]{0,1:T(8,128)(2,1)} async-done(((bf16[1280,704]{0,1:T(8,128)(2,1)}), bf16[1280,1408]{0,1:T(8,128)(2,1)}) %all-gather.15.cloned.1.call-update) | async-done | bytes 3604496 | tf_op jit(solution)/shard_map/all_gather | solution.py:213
  710.6 7.4 add_dynamic-update-slice_fusion
  718.1 90.0 %reduce-scatter.15.cloned.1.call-done = bf16[160,2048]{1,0:T(8,128)(2,1)} async-done(((bf16[1280,2048]{1,0:T(8,128)(2,1)}), bf16[160,2048]{1,0:T(8,128)(2,1)}) %reduce-scatter.15.cloned.1.call-update) | async-done | bytes 655376 | tf_op jit(solution)/shard_map/reduce_scatter | solution.py:112
  813.2 79.2 %all-gather.17.cloned.1.call-done = bf16[1280,2048]{1,0:T(8,128)(2,1)} async-done(((bf16[160,2048]{1,0:T(8,128)(2,1)}), bf16[1280,2048]{1,0:T(8,128)(2,1)}) %all-gather.17.cloned.1.call-update) | async-done | bytes 5242896 | tf_op jit(solution)/shard_map/all_gather | solution.py:225
  892.4 4.1 convolution_convert_fusion.9
  898.5 128.5 %while.29 = (s32[]{:T(128)}, f32[1280,4,64]{0,2,1:T(8,128)}, f32[1280,4,64]{0,2,1:T(8,128)}, f32[5,256,4,64]{1,0,3,2:T(8,128)}, bf16[5,256,4,64]{1,3,2,0:T(8,128...) while((s32[]{:T(128)}, f32[1280,4,64]{0,2,1:T(8,128)}, ...), condition=%wide.region_19.20_spmd.clone, body=%wide.region_17.19_spmd.clone.sunk | while | flops 853343488 | bytes 96075784 | solution.py:261
  911.1 6.9 dynamic_update_slice.37
  936.0 6.9 dynamic_update_slice.37
  943.0 3.2 fusion.167
  946.2 3.1 fusion.168
  961.9 6.9 dynamic_update_slice.37
  968.8 3.2 fusion.167
  987.8 6.9 dynamic_update_slice.37
  994.7 3.2 fusion.167
  997.9 3.1 fusion.168
  1013.7 6.9 dynamic_update_slice.37
  1020.6 3.2 fusion.167
  1023.8 3.1 fusion.168
  1036.8 59.3 %all-reduce.8.cloned.1.call-done = bf16[1280,640]{0,1:T(8,128)(2,1)} async-done(((bf16[1280,640]{0,1:T(8,128)(2,1)}), bf16[1280,640]{0,1:T(8,128)(2,1)}) %all-reduce.8.cloned.1.call-update) | async-done | bytes 1638416 | tf_op jit(solution)/shard_map/psum | solution.py:272
  1099.2 5.1 convolution_dynamic-update-slice_fusion
  1106.0 8.4 convolution_convert_fusion.2
  1115.9 8.9 convolution_convert_fusion.6
  1124.9 7.7 convolution_convert_fusion.4
  1132.6 7.6 convolution_convert_fusion.5
  1142.8 3.3 fusion.60
  1146.3 48.1 %reduce-scatter.17.cloned.1.call-done = bf16[160,2048]{1,0:T(8,128)(2,1)} async-done(((bf16[1280,2048]{1,0:T(8,128)(2,1)}), bf16[160,2048]{1,0:T(8,128)(2,1)}) %reduce-scatter.17.cloned.1.call-update) | async-done | bytes 655376 | tf_op jit(solution)/shard_map/reduce_scatter | solution.py:112
  1196.1 31.2 %all-reduce = (bf16[2048]{0:T(1024)(128)(2,1)S(1)}, bf16[2048]{0:T(1024)(128)(2,1)S(1)}) all-reduce(f32[2048]{0:T(1024)S(1)} %copy-done.36, f32[2048]{0:T(1024)S(1)} %get-tuple-element.289), channel_id=1, replica_groups=mesh['dp'=16,'row'=4,'col'=2] {'row','col'}, use_global_device_ids=true, to_apply=%region_28.29 | all-reduce | flops 4096 | bytes 24576 | tf_op jit(solution)/shard_map/psum | solution.py:282
  1227.4 37.0 %psum.74 = bf16[2,2048]{1,0:T(2,128)(2,1)S(1)} all-reduce(bf16[2,2048]{1,0:T(2,128)(2,1)S(1)} %pad_maximum_fusion.4), channel_id=1, replica_groups=mesh['dp'=16,'row'=4,'col'=2] {'dp'}, use_global_device_ids=true, to_apply=%region_29.30 | all-reduce | flops 4096 | bytes 16384 | tf_op jit(solution)/shard_map/psum | solution.py:71
  1265.0 25.6 %reduce-scatter.13.cloned.1.call-done = bf16[160,2048]{1,0:T(8,128)(2,1)} async-done(((bf16[1280,2048]{1,0:T(8,128)(2,1)}), bf16[160,2048]{1,0:T(8,128)(2,1)}) %reduce-scatter.13.cloned.1.call-update) | async-done | bytes 655376 | tf_op jit(solution)/shard_map/reduce_scatter | solution.py:195
  1290.6 3.4 fusion.73
  1294.0 248.7 %all-reduce.10.cloned.1.call-done = (bf16[1024,640]{1,0:T(8,128)(2,1)}, bf16[256,2048]{1,0:T(8,128)(2,1)}, bf16[1024,1408]{1,0:T(8,128)(2,1)}, bf16[1024,1408]{1,0:T(8,128)(2,1)}, bf16[704,2048]{1,0:T(8,128)(2,1)}) async-done(((bf16[1024,640]{1,0:T(8,128)(2,1)}, bf16[256,2048]{1,0:T(8,128)(2,1)}, bf16[1024,1408]{1,0:T(8,128)(2,1)}, bf16[1024,1408]{1,0:T(8,128)(2,1)}, bf16[704,2048]{1,0:T(8,128)(2,1)}), ...) | async-done | bytes 11010064 | tf_op jit(solution)/shard_map/psum | solution.py:69
  1542.7 4.9 convert_element_type.174
  1550.6 3.3 convert_element_type.178
  (376 shorter events, 165.1 us)
Async XLA Ops:
  7.2 391.1 %copy-start = (bf16[1024,1408]{1,0:T(8,128)(2,1)S(1)}, bf16[1024,1408]{1,0:T(8,128)(2,1)}, u32[]{:S(2)}) copy-start(bf16[1024,1408]{1,0:T(8,128)(2,1)} %param.21) | copy-start | bytes 8650756
  7.2 86.9 %all-gather.7.cloned.1.call-start = ((), (), s32[]{:S(2)}) async-start(), calls=%async_computation.6 | async-start | bytes 5898240 | tf_op jit(solution)/shard_map/all_gather | solution.py:76
  8.7 90.6 %copy-start.44 = (f32[160]{0:T(256)}, f32[160]{0:T(256)S(1)}, u32[]{:S(2)}) copy-start(f32[160]{0:T(256)S(1)} %fusion.74) | copy-start | bytes 1924
  8.7 90.6 %copy-start.40 = (f32[160]{0:T(256)}, f32[160]{0:T(256)S(1)}, u32[]{:S(2)}) copy-start(f32[160]{0:T(256)S(1)} %fusion.103) | copy-start | bytes 1924
  10.9 147.8 %all-reduce.6.cloned.1.call-start = ((), (), s32[]{:S(2)}) async-start(), calls=%async_computation.7 | async-start | bytes 3276800 | tf_op jit(solution)/shard_map/psum | solution.py:128
  10.9 88.5 %copy-start.51 = (s32[32]{0:T(128)S(1)}, s32[32]{0:T(128)}, u32[]{:S(2)}) copy-start(s32[32]{0:T(128)} %param.24) | copy-start | bytes 388
  11.0 88.5 %copy-start.52 = (s32[32]{0:T(128)S(1)}, s32[32]{0:T(128)}, u32[]{:S(2)}) copy-start(s32[32]{0:T(128)} %param.25) | copy-start | bytes 388
  99.4 214.8 %reduce-scatter.7.cloned.1.call-start = ((), (), s32[]{:S(2)}) async-start(), calls=%async_computation.8 | async-start | bytes 5898240 | tf_op jit(solution)/shard_map/reduce_scatter | solution.py:168
  100.4 59.8 %copy-start.48 = (f32[32]{0:T(128)}, f32[32]{0:T(128)S(1)}, u32[]{:S(2)}) copy-start(f32[32]{0:T(128)S(1)} %multiply_power_fusion) | copy-start | bytes 388
  101.7 65.6 %copy-start.33 = (f32[1280]{0:T(1024)}, f32[1280]{0:T(1024)S(1)}, u32[]{:S(2)}) copy-start(f32[1280]{0:T(1024)S(1)} %subtract_convert_fusion.2) | copy-start | bytes 15364
  103.1 57.2 %copy-start.25 = (f32[1280,32]{0,1:T(8,128)}, f32[1280,32]{0,1:T(8,128)S(1)}, u32[]{:S(2)}) copy-start(f32[1280,32]{0,1:T(8,128)S(1)} %get-tuple-element.358) | copy-start | bytes 491524
  224.1 90.1 %copy-start.6 = (bf16[160,2048]{1,0:T(8,128)(2,1)S(1)}, bf16[160,2048]{1,0:T(8,128)(2,1)}, u32[]{:S(2)}) copy-start(bf16[160,2048]{1,0:T(8,128)(2,1)} %param.15) | copy-start | bytes 1966084
  224.1 92.6 %copy-start.32 = (f32[2048]{0:T(1024)S(1)}, f32[2048]{0:T(1024)}, u32[]{:S(2)}) copy-start(f32[2048]{0:T(1024)} %param.23) | copy-start | bytes 24580
  224.1 174.2 %all-gather.9.cloned.1.call-start = ((), (), s32[]{:S(2)}) async-start(), calls=%async_computation.9 | async-start | bytes 5898240 | tf_op jit(solution)/shard_map/all_gather | solution.py:76
  318.9 159.6 %all-gather.11.cloned.1.call-start = ((), (), s32[]{:S(2)}) async-start(), calls=%async_computation.13 | async-start | bytes 5898240 | tf_op jit(solution)/shard_map/all_gather | solution.py:201
  319.5 212.6 %reduce-scatter.11.cloned.1.call-start = ((), (), s32[]{:S(2)}) async-start(), calls=%async_computation.11 | async-start | bytes 5406720 | tf_op jit(solution)/shard_map/reduce_scatter | solution.py:184
  405.8 181.1 %reduce-scatter.9.cloned.1.call-start = ((), (), s32[]{:S(2)}) async-start(), calls=%async_computation.10 | async-start | bytes 5406720 | tf_op jit(solution)/shard_map/reduce_scatter | solution.py:178
  414.4 237.4 %all-gather.13.cloned.1.call-start = ((), (), s32[]{:S(2)}) async-start(), calls=%async_computation.14 | async-start | bytes 5406720 | tf_op jit(solution)/shard_map/all_gather | solution.py:212
  598.1 109.4 %all-gather.15.cloned.1.call-start = ((), (), s32[]{:S(2)}) async-start(), calls=%async_computation.15 | async-start | bytes 5406720 | tf_op jit(solution)/shard_map/all_gather | solution.py:213
  598.9 209.2 %reduce-scatter.15.cloned.1.call-start = ((), (), s32[]{:S(2)}) async-start(), calls=%async_computation.16 | async-start | bytes 5898240 | tf_op jit(solution)/shard_map/reduce_scatter | solution.py:112
  718.0 90.1 %copy-start.10 = (bf16[160,2048]{1,0:T(8,128)(2,1)S(1)}, bf16[160,2048]{1,0:T(8,128)(2,1)}, u32[]{:S(2)}) copy-start(bf16[160,2048]{1,0:T(8,128)(2,1)} %reduce-scatter.7.cloned.1.call-done) | copy-start | bytes 1966084
  718.0 90.1 %copy-start.38 = (f32[160]{0:T(256)S(1)}, f32[160]{0:T(256)}, u32[]{:S(2)}) copy-start(f32[160]{0:T(256)} %copy-done.37) | copy-start | bytes 1924
  718.0 92.4 %copy-start.47 = (f32[160]{0:T(256)S(1)}, f32[160]{0:T(256)}, u32[]{:S(2)}) copy-start(f32[160]{0:T(256)} %copy-done.46) | copy-start | bytes 1924
  718.0 92.4 %copy-start.19 = (bf16[160,2048]{1,0:T(8,128)(2,1)S(1)}, bf16[160,2048]{1,0:T(8,128)(2,1)}, u32[]{:S(2)}) copy-start(bf16[160,2048]{1,0:T(8,128)(2,1)} %param.16) | copy-start | bytes 1966084
  718.0 174.4 %copy-start.29 = (bf16[256,2048]{1,0:T(8,128)(2,1)S(1)}, bf16[256,2048]{1,0:T(8,128)(2,1)}, u32[]{:S(2)}) copy-start(bf16[256,2048]{1,0:T(8,128)(2,1)} %param.19) | copy-start | bytes 3145732
  718.0 174.4 %all-gather.17.cloned.1.call-start = ((), (), s32[]{:S(2)}) async-start(), calls=%async_computation.17 | async-start | bytes 5898240 | tf_op jit(solution)/shard_map/all_gather | solution.py:225
  810.4 82.0 %copy-start.42 = (f32[160]{0:T(256)}, f32[160]{0:T(256)S(1)}, u32[]{:S(2)}) copy-start(f32[160]{0:T(256)S(1)} %multiply_multiply_fusion.1) | copy-start | bytes 1924
  812.9 283.2 %all-reduce.8.cloned.1.call-start = ((), (), s32[]{:S(2)}) async-start(), calls=%async_computation.18 | async-start | bytes 3276800 | tf_op jit(solution)/shard_map/psum | solution.py:272
  923.4 6.9 copy-start.16
  1036.8 157.6 %reduce-scatter.17.cloned.1.call-start = ((), (), s32[]{:S(2)}) async-start(), calls=%async_computation.19 | async-start | bytes 5898240 | tf_op jit(solution)/shard_map/reduce_scatter | solution.py:112
  1104.3 186.4 %reduce-scatter.13.cloned.1.call-start = ((), (), s32[]{:S(2)}) async-start(), calls=%async_computation.12 | async-start | bytes 5898240 | tf_op jit(solution)/shard_map/reduce_scatter | solution.py:195
  1114.5 428.2 %all-reduce.10.cloned.1.call-start = ((), (), s32[]{:S(2)}) async-start(), calls=%async_computation.20 | async-start | bytes 22020096 | tf_op jit(solution)/shard_map/psum | solution.py:69
  1115.9 8.9 copy-start.55
  1124.9 7.7 copy-start.53
  1124.9 15.4 slice-start.3
  1124.9 17.9 %slice-start.1 = ((s8[5242880]{0:T(1024)(128)(4,1)}), s8[4194304]{0:T(1024)(128)(4,1)S(1)}, s32[]{:S(2)}) async-start(s8[5242880]{0:T(1024)(128)(4,1)} %bitcast.129), calls=%async_computation.22 | async-start | bytes 8388608
  1132.6 7.6 copy-start.22
  1132.6 7.6 slice-start.4
  1132.6 10.2 slice-start.2
  1146.2 48.2 %copy-start.35 = (f32[2048]{0:T(1024)S(1)}, f32[2048]{0:T(1024)}, u32[]{:S(2)}) copy-start(f32[2048]{0:T(1024)} %param.17) | copy-start | bytes 24580
  1146.2 48.2 %copy-start.41 = (f32[160]{0:T(256)S(1)}, f32[160]{0:T(256)}, u32[]{:S(2)}) copy-start(f32[160]{0:T(256)} %copy-done.40) | copy-start | bytes 1924
  1146.2 49.9 %copy-start.36 = (f32[2048]{0:T(1024)S(1)}, f32[2048]{0:T(1024)}, u32[]{:S(2)}) copy-start(f32[2048]{0:T(1024)} %get-tuple-element.287) | copy-start | bytes 24580
  1146.2 118.2 %copy-start.45 = (f32[160]{0:T(256)S(1)}, f32[160]{0:T(256)}, u32[]{:S(2)}) copy-start(f32[160]{0:T(256)} %copy-done.44) | copy-start | bytes 1924
  1146.2 144.4 %copy-start.11 = (bf16[160,2048]{1,0:T(8,128)(2,1)S(1)}, bf16[160,2048]{1,0:T(8,128)(2,1)}, u32[]{:S(2)}) copy-start(bf16[160,2048]{1,0:T(8,128)(2,1)} %reduce-scatter.7.cloned.1.call-done) | copy-start | bytes 1966084
  1146.2 144.4 %copy-start.18 = (bf16[160,2048]{1,0:T(8,128)(2,1)S(1)}, bf16[160,2048]{1,0:T(8,128)(2,1)}, u32[]{:S(2)}) copy-start(bf16[160,2048]{1,0:T(8,128)(2,1)} %reduce-scatter.15.cloned.1.call-done) | copy-start | bytes 1966084
  1146.2 144.4 %copy-start.20 = (bf16[160,2048]{1,0:T(8,128)(2,1)S(1)}, bf16[160,2048]{1,0:T(8,128)(2,1)}, u32[]{:S(2)}) copy-start(bf16[160,2048]{1,0:T(8,128)(2,1)} %param.16) | copy-start | bytes 1966084
  1146.2 144.4 %copy-start.39 = (f32[160]{0:T(256)S(1)}, f32[160]{0:T(256)}, u32[]{:S(2)}) copy-start(f32[160]{0:T(256)} %copy-done.37) | copy-start | bytes 1924
  1146.2 144.4 %copy-start.43 = (f32[160]{0:T(256)S(1)}, f32[160]{0:T(256)}, u32[]{:S(2)}) copy-start(f32[160]{0:T(256)} %copy-done.42) | copy-start | bytes 1924
  (62 other events, 183.9 us)
Sparse Core Ops, SparseCore 0:
  11.0 83.0 all-gather.6
  99.5 59.1 all-reduce.5
  224.2 89.8 reduce-scatter.6
  319.0 79.2 all-gather.8
  400.4 78.0 all-gather.10
  481.3 50.6 reduce-scatter.10
  535.1 51.7 reduce-scatter.8
  598.2 53.4 all-gather.12
  654.0 53.4 all-gather.14
  718.1 89.8 reduce-scatter.14
  813.1 79.2 all-gather.16
  1036.9 59.2 all-reduce.7
  1104.4 89.8 reduce-scatter.16
  1199.2 91.4 reduce-scatter.12
  1294.0 248.7 all-reduce.9
where the time goes:
time: 1580 us; the launch traced here: 1560 us
  waiting for transfers between devices  1130 us (72%)
  matrix products  177 us (11%)
  local copies, waits for them, and re-layouts  86.4 us (5%)
  blocking collectives  68.2 us (4%)
  other arithmetic  65.7 us (4%)
  loops' own time  20 us (1%)
    psum x1, waiting for transfers between devices, replica_sum(): lax.psum(first_grad.astype(jnp.bfloat16), 'dp').astype(jnp.float32)  249 us
    all_gather x2, waiting for transfers between devices, gather_rows(): return lax.all_gather(values, ('row', 'col'), axis=0, tiled=True)  162 us
    reduce_scatter x2, waiting for transfers between devices, back_reduce(): lax.psum_scatter(lax.dynamic_update_slice_in_dim(jnp.zeros((local_rows *...  138 us
    reduce_scatter x1, waiting for transfers between devices, on_device(): lax.psum_scatter(jnp.dot(att_rows, out_weight, preferred_element_type=jnp...  89.8 us
    all_gather x1, waiting for transfers between devices, on_device(): lax.all_gather(after_grad.astype(jnp.bfloat16), ('row', 'col'), axis=0, t...  79.2 us
    all_gather x1, waiting for transfers between devices, on_device(): shard_rows = lax.all_gather(cotangent, ('row', 'col'), axis=0, tiled=True)  64.1 us
    psum x1, waiting for transfers between devices, on_device(): d_mixed = lax.psum(d_mixed.astype(jnp.bfloat16), 'col')  59.3 us
    psum x1, waiting for transfers between devices, on_device(): lax.psum(jnp.dot(mine_one, qkv_weight, preferred_element_type=jnp.float32...  55.6 us
  transfers between devices with their start and end apart: 15, of which 15 were waited for; matrix products, arithmetic and copies ran while one was open for 5% of the time, Pallas kernels for 0%

commit v1 on v0

v1 whole, which is shorter than its diff:
```python
import jax
import jax.numpy as jnp
from jax import lax
from jax.experimental import pallas as pl
from jax.experimental.pallas import tpu as pltpu
from jax.sharding import Mesh
from jax.sharding import PartitionSpec as P

HEADS = 32
KV = 4
HD = 64
EPSILON = 1e-05
ROTARY_BASE = 10000.0
MASKED = -1e30

AXES = ("y", "zl", "core", "x", "zh")
SIZES = (4, 2, 2, 4, 2)
BLK = 160
HALF = BLK // 2
ROWS = 4 * BLK
CAP = 2 * ROWS
D = 2048
DH = D // 2
QW = 640
AW = 512
FF4 = 1408
TILE = 256
F32 = jnp.float32
BF16 = jnp.bfloat16
VLIM = 60 * 1024 * 1024


def spec(memory=pltpu.VMEM):
    return pl.BlockSpec(memory_space=memory)


def params(**kw):
    return pltpu.CompilerParams(vmem_limit_bytes=VLIM, **kw)


def cost(flops, nbytes):
    return pl.CostEstimate(flops=int(flops), bytes_accessed=int(nbytes), transcendentals=0)


def sds(shape, dtype=BF16):
    return jax.ShapeDtypeStruct(shape, dtype)


def dot(a, b):
    return jnp.dot(a, b, preferred_element_type=F32)


def dot_t(a, b):
    return lax.dot_general(a, b, (((1,), (1,)), ((), ())), preferred_element_type=F32)


def t_dot(a, b):
    return lax.dot_general(a, b, (((0,), (0,)), ((), ())), preferred_element_type=F32)


def shift(n, s):
    return [(i, (i + s) % n) for i in range(n)]


def gather_x(v):
    from_prev = lax.ppermute(v, "x", shift(4, 1))
    from_next = lax.ppermute(v, "x", shift(4, -1))
    opp_a = lax.ppermute(from_prev[:HALF], "x", shift(4, 1))
    opp_b = lax.ppermute(from_next[HALF:], "x", shift(4, -1))
    return v, from_next, opp_a, opp_b, from_prev


def scatter_x(parts):
    p0, p1, p2a, p2b, p3 = parts
    got_a = lax.ppermute(p2a, "x", shift(4, 1))
    got_b = lax.ppermute(p2b, "x", shift(4, -1))
    q1 = jnp.concatenate([(p1[:HALF].astype(F32) + got_a.astype(F32)).astype(BF16), p1[HALF:]], 0)
    q3 = jnp.concatenate([p3[:HALF], (p3[HALF:].astype(F32) + got_b.astype(F32)).astype(BF16)], 0)
    from_prev = lax.ppermute(q1, "x", shift(4, 1))
    from_next = lax.ppermute(q3, "x", shift(4, -1))
    return p0.astype(F32) + from_prev.astype(F32) + from_next.astype(F32)


PIECES = ((0, BLK), (1, BLK), (2, HALF), (2, HALF), (3, BLK))
PIECE_ROW = (0, BLK, 2 * BLK, 2 * BLK + HALF, 3 * BLK)


def part_shapes(width, dtype=BF16):
    return tuple(sds((n, width), dtype) for _, n in PIECES)


def low_lanes(shape):
    return lax.broadcasted_iota(jnp.int32, shape, 1) < HD


def swap_halves(v):
    lane = lax.broadcasted_iota(jnp.int32, v.shape, 1) % HD
    return jnp.where(lane < HD // 2, pltpu.roll(v, 128 - HD // 2, 1), pltpu.roll(v, HD // 2, 1))


def rows_at(block):
    return pl.ds(pl.multiple_of(block * BLK, 32), BLK)


def qkv_body(idx, n0, n1, n2a, n2b, n3, w_own, w_par, cosine, sine, q_ref, kv_ref):
    x = idx[0]
    lo = low_lanes((BLK, 128))
    for d in range(4):
        if d == 2:
            rows = jnp.concatenate([n2a[...], n2b[...]], 0)
        else:
            rows = (n0, n1, None, n3)[d][...]
        acc = dot(rows[:, :DH], w_own[...]) + dot(rows[:, DH:], w_par[...])
        at = rows_at((x + d) & 3)
        cs = cosine[at, :]
        sn = sine[at, :]
        for p in range(4):
            v = acc[:, p * 128 : (p + 1) * 128]
            v = v * cs + swap_halves(v) * sn
            q_ref[at, p * 128 : (p + 1) * 128] = (v * HD**-0.5).astype(BF16)
        v = acc[:, AW:]
        kv_ref[at, :] = jnp.where(lo, v * cs + swap_halves(v) * sn, v).astype(BF16)


def qkv_forward(idx, pieces, w_own, w_par, cosine, sine):
    return pl.pallas_call(
        qkv_body,
        out_shape=(sds((ROWS, AW)), sds((ROWS, 128))),
        in_specs=[spec(pltpu.SMEM)] + [spec()] * 9,
        out_specs=(spec(), spec()),
        compiler_params=params(),
        cost_estimate=cost(2 * ROWS * D * QW, 7e6),
        name="qkv_forward",
    )(idx, *pieces, w_own, w_par, cosine, sine)


def spread_keys(zh, kv_own, kv_par, kk, vv):
    lo = low_lanes((BLK, 128))
    for j in range(4):
        for src, off in ((kv_own, zh), (kv_par, 1 - zh)):
            v = src[j * BLK : (j + 1) * BLK, :].astype(F32)
            w = pltpu.roll(v, HD, 1)
            at = rows_at(2 * j + off)
            kk[at, :] = jnp.where(lo, v, w).astype(BF16)
            vv[at, :] = jnp.where(lo, w, v).astype(BF16)


def fill_bias(zh, j, n, first, bias):
    t = (2 * j + zh) * BLK + lax.broadcasted_iota(jnp.int32, (BLK, n), 0)
    u = lax.broadcasted_iota(jnp.int32, (BLK, n), 1)
    start = first[j * BLK : (j + 1) * BLK, :]
    value = jnp.where((u <= t) & (u >= start), 0.0, MASKED)
    bias[0:BLK, 0:n] = value
    bias[BLK : 2 * BLK, 0:n] = value


def two_heads(v):
    lo = low_lanes(v.shape)
    zero = jnp.zeros_like(v)
    return jnp.concatenate([jnp.where(lo, v, zero), jnp.where(lo, zero, v)], 0)


def attend_body(idx, q, kv_own, kv_par, first, att, lse_ref, kk, vv, bias):
    x, zh = idx[0], idx[1]
    spread_keys(zh, kv_own, kv_par, kk, vv)
    lo = low_lanes((BLK, 128))
    lane = lax.broadcasted_iota(jnp.int32, (BLK, 128), 1)
    for j in range(4):
        n = 2 * BLK * (j + 1)
        fill_bias(zh, j, n, first, bias)
        rel = (j - x) & 3

        def pair(p, lse):
            cols = pl.ds(pl.multiple_of(p * 128, 128), 128)
            q2 = two_heads(q[j * BLK : (j + 1) * BLK, cols])
            s = dot_t(q2, kk[0:n, :]) + bias[:, 0:n]
            top = jnp.max(s, axis=1, keepdims=True)
            e = jnp.exp(s - top)
            total = jnp.sum(e, axis=1, keepdims=True)
            o = dot(e.astype(BF16), vv[0:n, :]) / total
            att[rel, :, cols] = jnp.where(lo, o[:BLK], o[BLK:]).astype(BF16)
            ls = top + jnp.log(total)
            lse = jnp.where(lane == 2 * p, ls[:BLK], lse)
            return jnp.where(lane == 2 * p + 1, ls[BLK:], lse)

        lse_ref[j * BLK : (j + 1) * BLK, :] = lax.fori_loop(0, 4, pair, jnp.zeros((BLK, 128), F32))


def attend(idx, q, kv_own, kv_par, first):
    return pl.pallas_call(
        attend_body,
        out_shape=(sds((4, BLK, AW)), sds((ROWS, 128), F32)),
        in_specs=[spec(pltpu.SMEM)] + [spec()] * 4,
        out_specs=(spec(), spec()),
        scratch_shapes=[
            pltpu.VMEM((CAP, 128), BF16),
            pltpu.VMEM((CAP, 128), BF16),
            pltpu.VMEM((2 * BLK, CAP), F32),
        ],
        compiler_params=params(),
        cost_estimate=cost(1.2e10, 3e6),
        name="attend",
    )(idx, q, kv_own, kv_par, first)


def ordered(zh, own, par):
    own, par = own[...], par[...]
    return jnp.where(zh == 0, own, par), jnp.where(zh == 0, par, own)


def out_body(idx, att, w_own, w_par, o0, o1, o2a, o2b, o3):
    w_lo, w_hi = ordered(idx[1], w_own, w_par)
    for d, ref in ((2, None), (1, o1), (3, o3), (0, o0)):
        a = att[d]
        res = (dot(a[:, : AW // 2], w_lo) + dot(a[:, AW // 2 :], w_hi)).astype(BF16)
        if d == 2:
            o2a[...] = res[:HALF]
            o2b[...] = res[HALF:]
        else:
            ref[...] = res


def out_project(idx, att, w_own, w_par):
    return pl.pallas_call(
        out_body,
        out_shape=part_shapes(D),
        in_specs=[spec(pltpu.SMEM)] + [spec()] * 3,
        out_specs=(spec(),) * 5,
        compiler_params=params(),
        cost_estimate=cost(2 * ROWS * D * AW, 5.5e6),
        name="out_project",
    )(idx, att, w_own, w_par)


def attend_back_body(
    idx, q, kv_own, kv_par, first, lse_ref, att, b0, b1, b2a, b2b, b3, w_own, w_par,
    dq_ref, dkv_own, dkv_par, kk, vv, bias, dout, dkk, dvv,
):
    x, zh = idx[0], idx[1]
    spread_keys(zh, kv_own, kv_par, kk, vv)
    w_lo, w_hi = ordered(zh, w_own, w_par)
    for d in range(4):
        if d == 2:
            rows = jnp.concatenate([b2a[...], b2b[...]], 0)
        else:
            rows = (b0, b1, None, b3)[d][...]
        at = rows_at((x + d) & 3)
        dout[at, : AW // 2] = dot_t(rows, w_lo).astype(BF16)
        dout[at, AW // 2 :] = dot_t(rows, w_hi).astype(BF16)
    dkk[...] = jnp.zeros_like(dkk)
    dvv[...] = jnp.zeros_like(dvv)
    lo = low_lanes((BLK, 128))
    lane = lax.broadcasted_iota(jnp.int32, (BLK, 128), 1)
    for j in range(4):
        n = 2 * BLK * (j + 1)
        fill_bias(zh, j, n, first, bias)
        rel = (j - x) & 3
        lse_all = lse_ref[j * BLK : (j + 1) * BLK, :]

        def pair(p, carry):
            cols = pl.ds(pl.multiple_of(p * 128, 128), 128)
            q2 = two_heads(q[j * BLK : (j + 1) * BLK, cols])
            do = dout[j * BLK : (j + 1) * BLK, cols]
            do2 = two_heads(do)
            prod = two_heads(do.astype(F32) * att[rel, :, cols].astype(F32))
            delta = jnp.sum(prod, axis=1, keepdims=True)
            ls = jnp.concatenate(
                [
                    jnp.sum(jnp.where(lane == 2 * p, lse_all, 0.0), axis=1, keepdims=True),
                    jnp.sum(jnp.where(lane == 2 * p + 1, lse_all, 0.0), axis=1, keepdims=True),
                ],
                0,
            )
            s = dot_t(q2, kk[0:n, :]) + bias[:, 0:n]
            e = jnp.exp(s - ls)
            dp = dot_t(do2, vv[0:n, :])
            ds = (e * (dp - delta)).astype(BF16)
            dvv[0:n, :] += t_dot(e.astype(BF16), do2)
            dkk[0:n, :] += t_dot(ds, q2)
            dq = dot(ds, kk[0:n, :]) * HD**-0.5
            dq_ref[j * BLK : (j + 1) * BLK, cols] = jnp.where(lo, dq[:BLK], dq[BLK:])
            return carry

        lax.fori_loop(0, 4, pair, 0)
    for j in range(4):
        for dst, off in ((dkv_own, zh), (dkv_par, 1 - zh)):
            at = rows_at(2 * j + off)
            dk, dv = dkk[at, :], dvv[at, :]
            both = jnp.where(lo, dk + pltpu.roll(dk, HD, 1), dv + pltpu.roll(dv, HD, 1))
            dst[j * BLK : (j + 1) * BLK, :] = both.astype(dst.dtype)


def attend_back(idx, q, kv_own, kv_par, first, lse, att, branch, w_own, w_par):
    return pl.pallas_call(
        attend_back_body,
        out_shape=(sds((ROWS, AW), F32), sds((ROWS, 128), F32), sds((ROWS, 128))),
        in_specs=[spec(pltpu.SMEM)] + [spec()] * 13,
        out_specs=(spec(),) * 3,
        scratch_shapes=[
            pltpu.VMEM((CAP, 128), BF16),
            pltpu.VMEM((CAP, 128), BF16),
            pltpu.VMEM((2 * BLK, CAP), F32),
            pltpu.VMEM((ROWS, AW), BF16),
            pltpu.VMEM((CAP, 128), F32),
            pltpu.VMEM((CAP, 128), F32),
        ],
        compiler_params=params(),
        cost_estimate=cost(3e10, 8e6),
        name="attend_back",
    )(idx, q, kv_own, kv_par, first, lse, att, *branch, w_own, w_par)


def qkv_back_body(
    idx, dq, dkv_own, dkv_got, cosine, sine, w_own, w_par, dm_ref, o0, o1, o2a, o2b, o3
):
    x = idx[0]
    lo = low_lanes((BLK, 128))
    for d, ref in ((2, None), (1, o1), (3, o3), (0, o0)):
        at = rows_at((x + d) & 3)
        cs = cosine[at, :]
        sn = sine[at, :]
        mine = pl.ds(d * BLK, BLK)
        for p in range(4):
            v = dq[at, p * 128 : (p + 1) * 128]
            dm_ref[mine, p * 128 : (p + 1) * 128] = (v * cs - swap_halves(v) * sn).astype(BF16)
        v = dkv_own[at, :] + dkv_got[at, :].astype(F32)
        dm_ref[mine, AW:] = jnp.where(lo, v * cs - swap_halves(v) * sn, v).astype(BF16)
        rows = dm_ref[mine, :]
        r_own = dot_t(rows, w_own[...]).astype(BF16)
        r_par = dot_t(rows, w_par[...]).astype(BF16)
        if d == 2:
            o2a[:, :DH], o2b[:, :DH] = r_own[:HALF], r_own[HALF:]
            o2a[:, DH:], o2b[:, DH:] = r_par[:HALF], r_par[HALF:]
        else:
            ref[:, :DH], ref[:, DH:] = r_own, r_par


def qkv_back(idx, dq, dkv_own, dkv_got, cosine, sine, w_own, w_par):
    res = pl.pallas_call(
        qkv_back_body,
        out_shape=(sds((ROWS, QW)),) + part_shapes(D),
        in_specs=[spec(pltpu.SMEM)] + [spec()] * 7,
        out_specs=(spec(),) * 6,
        compiler_params=params(),
        cost_estimate=cost(2 * ROWS * D * QW, 8e6),
        name="qkv_back",
    )(idx, dq, dkv_own, dkv_got, cosine, sine, w_own, w_par)
    return res[0], res[1:]


def ffn_body(
    n0, n1, n2a, n2b, n3, c0, c1, c2a, c2b, c3, g_own, g_par, u_own, u_par, down,
    n_all, c_all, hid, dgate, dup,
):
    @pl.when(pl.program_id(0) == 0)
    def _():
        for refs, dst in (((n0, n1, n2a, n2b, n3), n_all), ((c0, c1, c2a, c2b, c3), c_all)):
            for ref, row, (_, n) in zip(refs, PIECE_ROW, PIECES):
                dst[row : row + n, :] = ref[...]

    gate = dot(n_all[:, :DH], g_own[...]) + dot(n_all[:, DH:], g_par[...])
    up = dot(n_all[:, :DH], u_own[...]) + dot(n_all[:, DH:], u_par[...])
    dh = dot_t(c_all[...], down[...])
    sig = 1.0 / (1.0 + jnp.exp(-gate))
    act = gate * sig
    hid[...] = (act * up).astype(BF16)
    dgate[...] = (dh * up * sig * (1.0 + gate * (1.0 - sig))).astype(BF16)
    dup[...] = (dh * act).astype(BF16)


def ffn(normed, cots, g_own, g_par, u_own, u_par, down):
    whole = lambda n, w: pl.BlockSpec((n, w), lambda i: (0, 0))
    pieces = [whole(n, D) for _, n in PIECES]
    column = pl.BlockSpec((DH, TILE), lambda i: (0, i))
    hidden = pl.BlockSpec((ROWS, TILE), lambda i: (0, i))
    return pl.pallas_call(
        ffn_body,
        grid=(pl.cdiv(FF4, TILE),),
        out_shape=(sds((ROWS, D)),) * 2 + (sds((ROWS, FF4)),) * 3,
        in_specs=pieces * 2 + [column] * 4 + [pl.BlockSpec((TILE, D), lambda i: (i, 0))],
        out_specs=[whole(ROWS, D)] * 2 + [hidden] * 3,
        compiler_params=params(),
        cost_estimate=cost(6 * ROWS * D * FF4, 3.4e7),
        name="ffn",
    )(*normed, *cots, g_own, g_par, u_own, u_par, down)


def store_parts(res, refs):
    for ref, row, (_, n) in zip(refs, PIECE_ROW, PIECES):
        ref[...] = res[row : row + n].astype(BF16)


def part_specs():
    return [pl.BlockSpec((n, TILE), lambda i: (0, i)) for _, n in PIECES]


def down_body(hid, down, *refs):
    store_parts(dot(hid[...], down[...]), refs)


def down_project(hid, down):
    return pl.pallas_call(
        down_body,
        grid=(D // TILE,),
        out_shape=part_shapes(D),
        in_specs=[
            pl.BlockSpec((ROWS, FF4), lambda i: (0, 0)),
            pl.BlockSpec((FF4, TILE), lambda i: (0, i)),
        ],
        out_specs=part_specs(),
        compiler_params=params(),
        cost_estimate=cost(2 * ROWS * D * FF4, 1.1e7),
        name="down_project",
    )(hid, down)


def ffn_back_body(dgate, dup, g_own, g_par, u_own, u_par, *refs):
    half = pl.num_programs(0) // 2

    @pl.when(pl.program_id(0) < half)
    def _():
        store_parts(dot_t(dgate[...], g_own[...]) + dot_t(dup[...], u_own[...]), refs)

    @pl.when(pl.program_id(0) >= half)
    def _():
        store_parts(dot_t(dgate[...], g_par[...]) + dot_t(dup[...], u_par[...]), refs)


def ffn_back(dgate, dup, g_own, g_par, u_own, u_par):
    half = DH // TILE
    all_rows = pl.BlockSpec((ROWS, FF4), lambda i: (0, 0))
    own = pl.BlockSpec((TILE, FF4), lambda i: (jnp.minimum(i, half - 1), 0))
    par = pl.BlockSpec((TILE, FF4), lambda i: (jnp.maximum(i - half, 0), 0))
    return pl.pallas_call(
        ffn_back_body,
        grid=(D // TILE,),
        out_shape=part_shapes(D),
        in_specs=[all_rows, all_rows, own, par, own, par],
        out_specs=part_specs(),
        compiler_params=params(),
        cost_estimate=cost(4 * ROWS * D * FF4, 1.8e7),
        name="ffn_back",
    )(dgate, dup, g_own, g_par, u_own, u_par)


def inverse_rms(v):
    return lax.rsqrt(jnp.mean(v * v, axis=-1, keepdims=True) + EPSILON)


def norm_back(v, r, gain, grad):
    pulled = grad * gain
    inner = jnp.mean(v * pulled, axis=-1, keepdims=True)
    return r * pulled - v * (r * r * r) * inner, jnp.sum(grad * v * r, axis=0)


def replica_layout(lengths, replica, replica_id):
    sizes = jnp.where(replica == replica_id, lengths, 0)
    starts = jnp.cumsum(sizes) - sizes
    row_ids = jnp.arange(CAP, dtype=jnp.int32)
    inside = (row_ids[:, None] >= starts[None, :]) & (row_ids[:, None] < (starts + sizes)[None, :])
    begin = jnp.sum(jnp.where(inside, starts[None, :], 0), axis=1)
    begin = begin + jnp.where(jnp.any(inside, axis=1), 0, jnp.sum(sizes))
    return begin, row_ids - begin


def on_device(
    tokens, cotangent, gain_one, qkv_weight, out_weight, gate_weight, up_weight, down_weight,
    gain_two, seq_lengths, seq_replica,
):
    x, zh, core = lax.axis_index("x"), lax.axis_index("zh"), lax.axis_index("core")
    eighth = lax.axis_index("y") * 2 + core
    idx = jnp.stack([x, zh, core]).astype(jnp.int32)

    def roll_features(v):
        return jnp.where(zh == 0, v, jnp.concatenate([v[..., DH:], v[..., :DH]], -1))

    def partner(w):
        rows = w.shape[0] // 8
        mine = lax.dynamic_slice_in_dim(w, eighth * rows, rows, 0)
        got = lax.ppermute(mine, "zh", shift(2, 1))
        return lax.all_gather(got, ("y", "core"), axis=0, tiled=True)

    def in_order(own, par):
        return jnp.where(
            zh == 0, jnp.concatenate([own, par], 0), jnp.concatenate([par, own], 0)
        )

    def reduce_grad(g):
        rows = g.shape[1]
        part = lax.psum_scatter(
            g.reshape(2 * 2 * 4 * 2, rows // 16 * 2, g.shape[2])[:, : rows // 16 * 2]
            .reshape(2, 8, rows // 8, g.shape[2]),
            ("y", "core"), scatter_dimension=1, tiled=True,
        )
        return part

    qkv_par = partner(qkv_weight)
    tok = tokens.astype(F32)
    s_one = inverse_rms(tok)
    normed_one = gather_x(roll_features((tok * s_one * gain_one).astype(BF16)))
    cots = gather_x(cotangent)

    begin, position = replica_layout(
        seq_lengths, seq_replica,
        (lax.axis_index("y") * 2 + lax.axis_index("zl")) * 2 + core,
    )
    half_rows = lambda v: lax.dynamic_index_in_dim(v.reshape(4, 2, BLK), zh, 1, False).reshape(ROWS, 1)
    first = half_rows(begin)
    lane = jnp.arange(128, dtype=jnp.int32)
    frequency = ROTARY_BASE ** (-(lane % 32).astype(F32) * (2.0 / HD))
    angles = half_rows(position).astype(F32) * frequency[None, :]
    cosine = jnp.cos(angles)
    sine = jnp.where((lane % HD) < HD // 2, -1.0, 1.0)[None, :] * jnp.sin(angles)

    q, kv_own = qkv_forward(idx, normed_one, qkv_weight, qkv_par, cosine, sine)
    kv_par = lax.ppermute(kv_own, "zh", shift(2, 1))
    att, lse = attend(idx, q, kv_own, kv_par, first)
    out_par = partner(out_weight)
    after_attn = tok + scatter_x(out_project(idx, att, out_weight, out_par))

    r_two = inverse_rms(after_attn)
    normed_two = gather_x(roll_features((after_attn * r_two * gain_two).astype(BF16)))
    gate_par, up_par = partner(gate_weight), partner(up_weight)
    down = in_order(down_weight, partner(down_weight))
    n_two, cot_all, hid, dgate, dup = ffn(
        normed_two, cots, gate_weight, gate_par, up_weight, up_par, down
    )
    d_two = roll_features(
        scatter_x(ffn_back(dgate, dup, gate_weight, gate_par, up_weight, up_par))
    )
    layer_out = after_attn + scatter_x(down_project(hid, down))
    back_two, gain_grad_two = norm_back(after_attn, r_two, gain_two, d_two)
    after_grad = cotangent.astype(F32) + back_two
    branch = gather_x(after_grad.astype(BF16))
    dq, dkv_own, dkv_par = attend_back(
        idx, q, kv_own, kv_par, first, lse, att, branch, out_weight, out_par
    )
    dkv_got = lax.ppermute(dkv_par, "zh", shift(2, 1))
    d_mixed, parts = qkv_back(idx, dq, dkv_own, dkv_got, cosine, sine, qkv_weight, qkv_par)
    d_one = roll_features(scatter_x(parts))
    back_one, gain_grad_one = norm_back(tok, s_one, gain_one, d_one)
    input_grad = (after_grad + back_one).astype(BF16)

    n_one = jnp.concatenate(normed_one, 0)
    branch_all = jnp.concatenate(branch, 0)

    def halves(g):
        return jnp.stack([g[: g.shape[0] // 2], g[g.shape[0] // 2 :]]).astype(BF16)

    def finish(g, rolled):
        g = g.astype(BF16)
        rows, columns = g.shape[0] // 2, g.shape[1]
        part = lax.psum_scatter(
            g.reshape(2, 8, rows // 8, columns).swapaxes(0, 1),
            ("y", "core"), scatter_dimension=0, tiled=True,
        ).reshape(2, rows // 8, columns)
        if rolled:
            own, other = part[0], part[1]
        else:
            own, other = jnp.where(zh == 0, part[0], part[1]), jnp.where(zh == 0, part[1], part[0])
        own = own.astype(F32) + lax.ppermute(other, "zh", shift(2, 1)).astype(F32)
        low = own.astype(BF16)
        own = low.astype(F32) + lax.ppermute(low, "zl", shift(2, 1)).astype(F32)
        return lax.all_gather(own.astype(BF16), ("y", "core"), axis=0, tiled=True).astype(F32)

    grad_down = finish(t_dot(hid, cot_all), False)
    grad_gate = finish(t_dot(n_two, dgate), True)
    grad_up = finish(t_dot(n_two, dup), True)
    grad_out = finish(t_dot(att.reshape(ROWS, AW), branch_all), False)
    grad_qkv = finish(t_dot(n_one, d_mixed), True)

    gains = jnp.stack([gain_grad_one, gain_grad_two])
    for axis, n in (("x", 4), ("zh", 2), ("zl", 2), ("y", 4), ("core", 2)):
        gains = gains + sum(lax.ppermute(gains, axis, shift(n, s)) for s in range(1, n))
    return (
        layer_out.astype(BF16), input_grad, gains[0], grad_qkv, grad_out, grad_gate, grad_up,
        grad_down, gains[1],
    )


def solution(mesh):
    grid = Mesh(mesh.devices.reshape(SIZES), AXES)
    rows = P(AXES, None)
    both = P(("x", "zh"), None)
    return jax.shard_map(
        on_device,
        mesh=grid,
        in_specs=(
            rows, rows, P(), P("zh", "x"), both, P("zh", "x"), P("zh", "x"), both, P(), P(), P(),
        ),
        out_specs=(
            rows, rows, P(), P("zh", "x"), both, P("zh", "x"), P("zh", "x"), both, P(),
        ),
        check_vma=False,
    )
```

time: 1580 us -> 673 us (0.43)
  waiting for transfers between devices: 1130 us -> 325 us
  matrix products: 177 us -> 27.6 us
  starting transfers between devices: 1.62 us -> 105 us
  Pallas kernels: 0 us -> 103 us
  blocking collectives: 68.2 us -> 0 us
  local copies, waits for them, and re-layouts: 86.4 us -> 40 us
  loops' own time: 20 us -> 0 us
    psum x3 -> x0, waiting for transfers between devices: 364 us -> none  [the longest x1 249 us: replica_sum(): lax.psum(first_grad.astype(jnp.bfloat16), 'dp').astype(jnp.float32)]
    all_gather x6 -> x10, waiting for transfers between devices: 404 us -> 52.5 us  [the longest x5 52.5 us: finish(): lax.all_gather(own.astype(BF16), ('y', 'core'), axis=0, tiled=True)]
    reduce_scatter x6 -> x5, waiting for transfers between devices: 362 us -> 83.7 us  [finish(): lax.psum_scatter(g.reshape(2, 8, rows // 8, columns).swapaxes(0, 1), ('y'...]
    ppermute x0 -> x58, waiting for transfers between devices: none -> 189 us  [the longest x4 40.7 us: gather_x(): from_prev = lax.ppermute(v, 'x', shift(4, 1))]
    dot_general x50 -> x5, matrix products: 177 us -> 27.6 us  [t_dot(): lax.dot_general(a, b, (((0,), (0,)), ((), ())), preferred_element_type=F32)]
    ppermute x0 -> x58, starting transfers between devices: none -> 104 us  [the longest x9 23 us: on_device(): lax.ppermute(gains, axis, shift(n, s))]
    pallas_call x0 -> x8, Pallas kernels: none -> 103 us  [the longest x1 25.3 us: attend_back(): pl.pallas_call(attend_back_body, out_shape=(sds((ROWS, AW), F32), sds((RO...]
    psum x2 -> x0, blocking collectives: 68.2 us -> none  [the longest x1 37 us: replica_sum(): lax.psum(third_grad.astype(jnp.bfloat16), 'dp').astype(jnp.float32)]
  transfers between devices with their start and end apart: 15 -> 73, of which waited for: 15 -> 47; matrix products, arithmetic and copies ran while one was open for 5% -> 15% of each run, Pallas kernels for 0% -> 11%
where the time goes in v1:
time: 673 us; the launch traced here: 666 us
  waiting for transfers between devices  325 us (48%)
  starting transfers between devices  105 us (16%)
  Pallas kernels  103 us (15%)
  other arithmetic  50.9 us (8%)
  local copies, waits for them, and re-layouts  40 us (6%)
  matrix products  27.6 us (4%)
  between operations  15.4 us (2%)
    reduce_scatter x5, waiting for transfers between devices, finish(): lax.psum_scatter(g.reshape(2, 8, rows // 8, columns).swapaxes(0, 1), ('y'...  83.7 us
    all_gather x5, waiting for transfers between devices, finish(): lax.all_gather(own.astype(BF16), ('y', 'core'), axis=0, tiled=True)  52.5 us
    ppermute x4, waiting for transfers between devices, gather_x(): from_prev = lax.ppermute(v, 'x', shift(4, 1))  40.7 us
    ppermute x4, waiting for transfers between devices, scatter_x(): from_next = lax.ppermute(q3, 'x', shift(4, -1))  30 us
    dot_general x5, matrix products, t_dot(): lax.dot_general(a, b, (((0,), (0,)), ((), ())), preferred_element_type=F32)  27.6 us
    pallas_call x1, Pallas kernels, attend_back(): pl.pallas_call(attend_back_body, out_shape=(sds((ROWS, AW), F32), sds((RO...  25.3 us
    ppermute x5, waiting for transfers between devices, finish(): own = low.astype(F32) + lax.ppermute(low, 'zl', shift(2, 1)).astype(F32)  24.1 us
    ppermute x9, starting transfers between devices, on_device(): lax.ppermute(gains, axis, shift(n, s))  23 us
  transfers between devices with their start and end apart: 73, of which 47 were waited for; matrix products, arithmetic and copies ran while one was open for 15% of the time, Pallas kernels for 11%

profile of v1, /device:TPU:1, one launch (start us, length us, event | category | flops | bytes accessed | tf_op | source)
XLA Modules:
  0.0 666.3 jit_solution(17129272547650276554)
XLA Ops:
  8.2 4.5 collective-permute-start.4
  12.7 3.9 collective-permute-done.4
  28.2 6.4 collective-permute-done.21
  39.0 5.7 collective-permute-done.20
  51.9 8.6 %collective-permute-done.1.n3 = bf16[160,2048]{1,0:T(8,128)(2,1)S(1)} collective-permute-done((bf16[160,2048]{1,0:T(8,128)(2,1)S(1)}, bf16[160,2048]{1,0:T(8,128)(2,1)S(1)}, u32[]{:S(2)}, u32[]{:S(2)}) %collective-permute-start.1) | collective-permute-done | bytes 655392 | tf_op jit(solution)/shard_map/ppermute | solution.py:66
  69.3 5.9 qkv_forward.1
  81.7 17.2 %attend.1 = (bf16[4,160,512]{2,1,0:T(8,128)(2,1)}, f32[640,128]{1,0:T(8,128)}) custom-call(s32[3]{0:T(128)} %pad_add_fusion.idx, bf16[640,512]{1,0:T(8,128)(2,1)} %get-tuple-element.42.q, bf16[640,128]{1,0:T(8,128)(2,1)} %get-tuple-element.43.kv_own, bf16[640,128]{1,0:T(8,128)(2,1)} %copy-done.50, s32[640,1]{1,0:T(8,128)} %reshape.204.first), custom_call_target="tpu_custom_call" | custom-call | flops 12000000000 | bytes 3000000 | tf_op jit(solution)/shard_map/attend/pallas_call | solution.py:190
  98.9 4.1 out_project.1
  119.1 5.2 collective-permute-done.10
  124.3 6.2 collective-permute-done.8
  134.5 7.7 %collective-permute-done.16.c3 = bf16[160,2048]{1,0:T(8,128)(2,1)S(1)} collective-permute-done((bf16[160,2048]{1,0:T(8,128)(2,1)S(1)}, bf16[160,2048]{1,0:T(8,128)(2,1)S(1)}, u32[]{:S(2)}, u32[]{:S(2)}) %collective-permute-start.16) | collective-permute-done | bytes 655392 | tf_op jit(solution)/shard_map/ppermute | solution.py:66
  145.8 10.4 %collective-permute-done.12.n3 = bf16[160,2048]{1,0:T(8,128)(2,1)S(1)} collective-permute-done((bf16[160,2048]{1,0:T(8,128)(2,1)S(1)}, bf16[160,2048]{1,0:T(8,128)(2,1)S(1)}, u32[]{:S(2)}, u32[]{:S(2)}) %collective-permute-start.12) | collective-permute-done | bytes 655392 | tf_op jit(solution)/shard_map/ppermute | solution.py:66
  160.2 7.6 %maximum_select_fusion.down = bf16[1408,2048]{1,0:T(8,128)(2,1)} fusion(bf16[704,2048]{1,0:T(8,128)(2,1)} %all-gather.19.cloned.1.call-done, bf16[704,2048]{1,0:T(8,128)(2,1)} %param.18, pred[]{:T(512)S(6)} %eq.9), kind=kLoop, calls=%fused_computation.3 | loop fusion | flops 25952256 | bytes 11534337 | tf_op jit(solution)/shard_map/jit(_where)/select_n | solution.py:484
  170.3 19.1 %ffn.1 = (bf16[640,2048]{1,0:T(8,128)(2,1)}, bf16[640,2048]{1,0:T(8,128)(2,1)}, bf16[640,1408]{1,0:T(8,128)(2,1)}, bf16[640,1408]{1,0:T(8,128)(2,1)}, bf16[640,1408]{1,0:T(8,128)(2,1)}) custom-call(bf16[160,2048]{1,0:T(8,128)(2,1)} %copy-done.25, bf16[160,2048]{1,0:T(8,128)(2,1)} %copy-done.40, bf16[80,2048]{1,0:T(8,128)(2,1)} %collective-permute-done.13.n2a, ...), custom_call_target="tpu_custom_call" | custom-call | flops 11072962560 | bytes 34000000 | tf_op jit(solution)/shard_map/ffn/pallas_call | solution.py:376
  189.3 9.5 %down_project.1 = (bf16[160,2048]{1,0:T(8,128)(2,1)}, bf16[160,2048]{1,0:T(8,128)(2,1)}, bf16[80,2048]{1,0:T(8,128)(2,1)}, bf16[80,2048]{1,0:T(8,128)(2,1)}, bf16[160,2048]{1,0:T(8,128)(2,1)}) custom-call(bf16[640,1408]{1,0:T(8,128)(2,1)} %get-tuple-element.50.hid, bf16[1408,2048]{1,0:T(8,128)(2,1)} %maximum_select_fusion.down), custom_call_target="tpu_custom_call" | custom-call | flops 3690987520 | bytes 11000000 | tf_op jit(solution)/shard_map/down_project/pallas_call | solution.py:402
  198.9 14.2 %ffn_back.1 = (bf16[160,2048]{1,0:T(8,128)(2,1)}, bf16[160,2048]{1,0:T(8,128)(2,1)}, bf16[80,2048]{1,0:T(8,128)(2,1)}, bf16[80,2048]{1,0:T(8,128)(2,1)}, bf16[160,2048]{1,0:T(8,128)(2,1)}) custom-call(bf16[640,1408]{1,0:T(8,128)(2,1)} %get-tuple-element.56.dgate, bf16[640,1408]{1,0:T(8,128)(2,1)} %get-tuple-element.57.dup, bf16[1024,1408]{1,0:T(8,128)(2,1)} %g_own.3, ...), custom_call_target="tpu_custom_call" | custom-call | flops 7381975040 | bytes 18000000 | tf_op jit(solution)/shard_map/ffn_back/pallas_call | solution.py:434
  226.7 15.2 %collective-permute-done.29 = bf16[160,2048]{1,0:T(8,128)(2,1)S(1)} collective-permute-done((bf16[160,2048]{1,0:T(8,128)(2,1)S(1)}, bf16[160,2048]{1,0:T(8,128)(2,1)S(1)}, u32[]{:S(2)}, u32[]{:S(2)}) %collective-permute-start.29) | collective-permute-done | bytes 655392 | tf_op jit(solution)/shard_map/ppermute | solution.py:80
  242.3 11.1 %collective-permute-done.23 = bf16[160,2048]{1,0:T(8,128)(2,1)S(1)} collective-permute-done((bf16[160,2048]{1,0:T(8,128)(2,1)S(1)}, bf16[160,2048]{1,0:T(8,128)(2,1)S(1)}, u32[]{:S(2)}, u32[]{:S(2)}) %collective-permute-start.23) | collective-permute-done | bytes 655392 | tf_op jit(solution)/shard_map/ppermute | solution.py:79
  258.2 14.0 %collective-permute-done.31.b3 = bf16[160,2048]{1,0:T(8,128)(2,1)S(1)} collective-permute-done((bf16[160,2048]{1,0:T(8,128)(2,1)S(1)}, bf16[160,2048]{1,0:T(8,128)(2,1)S(1)}, u32[]{:S(2)}, u32[]{:S(2)}) %collective-permute-start.31) | collective-permute-done | bytes 655392 | tf_op jit(solution)/shard_map/ppermute | solution.py:66
  275.5 5.5 collective-permute-done.32.b2a
  288.6 25.3 %attend_back.1 = (f32[640,512]{1,0:T(8,128)}, f32[640,128]{1,0:T(8,128)}, bf16[640,128]{1,0:T(8,128)(2,1)}) custom-call(s32[3]{0:T(128)} %pad_add_fusion.idx, bf16[640,512]{1,0:T(8,128)(2,1)} %get-tuple-element.42.q, bf16[640,128]{1,0:T(8,128)(2,1)} %get-tuple-element.43.kv_own, bf16[640,128]{1,0:T(8,128)(2,1)} %copy-done.50, s32[640,1]{1,0:T(8,128)} %reshape.204.first, ...), custom_call_target="tpu_custom_call" | custom-call | flops 30000001024 | bytes 8000000 | tf_op jit(solution)/shard_map/attend_back/pallas_call | solution.py:294
  320.6 7.4 %qkv_back.1 = (bf16[640,640]{1,0:T(8,128)(2,1)}, bf16[160,2048]{1,0:T(8,128)(2,1)}, bf16[160,2048]{1,0:T(8,128)(2,1)}, bf16[80,2048]{1,0:T(8,128)(2,1)}, bf16[80...) custom-call(s32[3]{0:T(128)} %pad_add_fusion.idx, f32[640,512]{1,0:T(8,128)} %get-tuple-element.64.dq, ...), custom_call_target="tpu_custom_call" | custom-call | flops 1677721600 | bytes 8000000 | tf_op jit(solution)/shard_map/qkv_back/pallas_call | solution.py:339
  328.0 4.5 convolution_convert_fusion.3
  334.3 7.0 %convolution_convert_fusion = bf16[1408,2048]{1,0:T(8,128)(2,1)S(1)} fusion(bf16[640,1408]{1,0:T(8,128)(2,1)} %get-tuple-element.50.hid, bf16[640,2048]{1,0:T(8,128)(2,1)} %get-tuple-element.74), kind=kOutput, calls=%fused_computation | convolution fusion | flops 3693871104 | bytes 10190848 | tf_op jit(solution)/shard_map/dot_general | solution.py:58
  344.6 7.1 %convolution_convert_fusion.1 = bf16[2048,1408]{1,0:T(8,128)(2,1)S(1)} fusion(bf16[640,2048]{1,0:T(8,128)(2,1)} %get-tuple-element.73, bf16[640,1408]{1,0:T(8,128)(2,1)} %get-tuple-element.57.dup), kind=kOutput, calls=%fused_computation.1 | convolution fusion | flops 3693871104 | bytes 10190848 | tf_op jit(solution)/shard_map/dot_general | solution.py:58
  354.9 7.1 %convolution_convert_fusion.2 = bf16[2048,1408]{1,0:T(8,128)(2,1)S(1)} fusion(bf16[640,2048]{1,0:T(8,128)(2,1)} %get-tuple-element.73, bf16[640,1408]{1,0:T(8,128)(2,1)} %get-tuple-element.56.dgate), kind=kOutput, calls=%fused_computation.2 | convolution fusion | flops 3693871104 | bytes 10190848 | tf_op jit(solution)/shard_map/dot_general | solution.py:58
  377.7 4.1 reduce-scatter.6.cloned.1.call-done
  385.9 3.5 collective-permute-done.48
  391.1 5.1 collective-permute-done.49
  397.0 29.1 %reduce-scatter.14.cloned.1.call-done = bf16[1,2,88,2048]{3,2,1,0:T(8,128)(2,1)} async-done(((bf16[8,2,88,2048]{3,2,1,0:T(8,128)(2,1)}), bf16[1,2,88,2048]{3,2,1,0:T(8,128)(2,1)}) %reduce-scatter.14.cloned.1.call-update) | async-done | bytes 720912 | tf_op jit(solution)/shard_map/reduce_scatter | solution.py:553
  430.2 5.9 collective-permute-done.56
  437.8 5.9 collective-permute-done.57
  444.6 25.4 %reduce-scatter.12.cloned.1.call-done = bf16[1,2,128,1408]{3,2,1,0:T(8,128)(2,1)} async-done(((bf16[8,2,128,1408]{3,2,1,0:T(8,128)(2,1)}), bf16[1,2,128,1408]{3,2,1,0:T(8,128)(2,1)}) %reduce-scatter.12.cloned.1.call-update) | async-done | bytes 720912 | tf_op jit(solution)/shard_map/reduce_scatter | solution.py:553
  474.0 6.1 collective-permute-done.54
  482.5 5.5 collective-permute-done.55
  488.8 25.1 %reduce-scatter.10.cloned.1.call-done = bf16[1,2,128,1408]{3,2,1,0:T(8,128)(2,1)} async-done(((bf16[8,2,128,1408]{3,2,1,0:T(8,128)(2,1)}), bf16[1,2,128,1408]{3,2,1,0:T(8,128)(2,1)}) %reduce-scatter.10.cloned.1.call-update) | async-done | bytes 720912 | tf_op jit(solution)/shard_map/reduce_scatter | solution.py:553
  526.7 4.9 collective-permute-done.53
  535.3 9.7 %collective-permute-done.38 = bf16[160,2048]{1,0:T(8,128)(2,1)S(1)} collective-permute-done((bf16[160,2048]{1,0:T(8,128)(2,1)S(1)}, bf16[160,2048]{1,0:T(8,128)(2,1)S(1)}, u32[]{:S(2)}, u32[]{:S(2)}) %collective-permute-start.38) | collective-permute-done | bytes 655392 | tf_op jit(solution)/shard_map/ppermute | solution.py:80
  545.0 3.6 collective-permute-done.36
  561.9 12.3 %collective-permute-start.46 = (f32[2,2048]{1,0:T(2,128)S(1)}, f32[2,2048]{1,0:T(2,128)S(1)}, u32[]{:S(2)}, u32[]{:S(2)}) collective-permute-start(f32[2,2048]{1,0:T(2,128)S(1)} %add.240), channel_id=1, source_target_pairs={{0,96},{32,0},{64,32},{96,64},{1,97},{33,1},{65,33},{97,65},{2,98}... | collective-permute-start | bytes 49160 | tf_op jit(solution)/shard_map/ppermute | solution.py:574
  575.1 3.2 collective-permute-done.45
  578.4 6.3 collective-permute-start.47
  592.3 4.0 all-gather.29.cloned.1.call-done
  596.3 5.1 convert_element_type.372
  601.5 23.9 %all-gather.27.cloned.1.call-done = bf16[1024,1408]{1,0:T(8,128)(2,1)} async-done(((bf16[128,1408]{1,0:T(8,128)(2,1)}), bf16[1024,1408]{1,0:T(8,128)(2,1)}) %all-gather.27.cloned.1.call-update) | async-done | bytes 2883600 | tf_op jit(solution)/shard_map/all_gather | solution.py:564
  625.3 4.7 convert_element_type.363
  630.0 24.6 %all-gather.25.cloned.1.call-done = bf16[1024,1408]{1,0:T(8,128)(2,1)} async-done(((bf16[128,1408]{1,0:T(8,128)(2,1)}), bf16[1024,1408]{1,0:T(8,128)(2,1)}) %all-gather.25.cloned.1.call-update) | async-done | bytes 2883600 | tf_op jit(solution)/shard_map/all_gather | solution.py:564
  654.6 4.7 convert_element_type.354
  (344 shorter events, 187.8 us)
Async XLA Ops:
  7.2 61.2 %all-gather.11.cloned.1.call-start = ((), (), s32[]{:S(2)}) async-start(), calls=%async_computation.5 | async-start | bytes 1474560 | tf_op jit(solution)/shard_map/all_gather | solution.py:481
  8.2 8.4 %collective-permute-start.4 = (bf16[128,640]{1,0:T(8,128)(2,1)S(1)}, bf16[128,640]{1,0:T(8,128)(2,1)S(1)}, u32[]{:S(2)}, u32[]{:S(2)}) collective-permute-start(bf16[128,640]{1,0:T(8,128)(2,1)S(1)} %constant_dynamic-slice_fusion.4), channel_id=1, source_target_pairs={{0,1},{1,0},{2,3},{3,2},{4,5},{5,4},{6,7},{7,6},{8,9},{9,8},{10,11... | collective-permute-start | bytes 491528 | tf_op jit(solution)/shard_map/ppermute | solution.py:480
  17.3 81.6 %all-gather.13.cloned.1.call-start = ((), (), s32[]{:S(2)}) async-start(), calls=%async_computation.6 | async-start | bytes 1179648 | tf_op jit(solution)/shard_map/all_gather | solution.py:481
  24.4 135.7 %all-gather.19.cloned.1.call-start = ((), (), s32[]{:S(2)}) async-start(), calls=%async_computation.9 | async-start | bytes 3244032 | tf_op jit(solution)/shard_map/all_gather | solution.py:481
  25.5 9.1 %collective-permute-start.21 = (bf16[88,2048]{1,0:T(8,128)(2,1)S(1)}, bf16[88,2048]{1,0:T(8,128)(2,1)S(1)}, u32[]{:S(2)}, u32[]{:S(2)}) collective-permute-start(bf16[88,2048]{1,0:T(8,128)(2,1)S(1)} %constant_dynamic-slice_fusion), channel_id=1, source_target_pairs={{0,1},{1,0},{2,3},{3,2},{4,5},{5,4},{6,7},{7,6},{8,9},{9,8},{10,11... | collective-permute-start | bytes 1081352 | tf_op jit(solution)/shard_map/ppermute | solution.py:480
  35.4 134.9 %all-gather.17.cloned.1.call-start = ((), (), s32[]{:S(2)}) async-start(), calls=%async_computation.8 | async-start | bytes 3244032 | tf_op jit(solution)/shard_map/all_gather | solution.py:481
  45.4 124.9 %all-gather.15.cloned.1.call-start = ((), (), s32[]{:S(2)}) async-start(), calls=%async_computation.7 | async-start | bytes 3244032 | tf_op jit(solution)/shard_map/all_gather | solution.py:481
  47.2 13.3 %collective-permute-start.1 = (bf16[160,2048]{1,0:T(8,128)(2,1)S(1)}, bf16[160,2048]{1,0:T(8,128)(2,1)S(1)}, u32[]{:S(2)}, u32[]{:S(2)}) collective-permute-start(bf16[160,2048]{1,0:T(8,128)(2,1)S(1)} %get-tuple-element.83.n0), channel_id=1, source_target_pairs={{0,2},{2,4},{4,6},{6,0},{1,3},{3,5},{5,7},{7,1},{8,10},{10,12},{12... | collective-permute-start | bytes 1966088 | tf_op jit(solution)/shard_map/ppermute | solution.py:66
  48.4 12.2 %collective-permute-start = (bf16[160,2048]{1,0:T(8,128)(2,1)S(1)}, bf16[160,2048]{1,0:T(8,128)(2,1)S(1)}, u32[]{:S(2)}, u32[]{:S(2)}) collective-permute-start(bf16[160,2048]{1,0:T(8,128)(2,1)S(1)} %get-tuple-element.83.n0), channel_id=1, source_target_pairs={{0,6},{2,0},{4,2},{6,4},{1,7},{3,1},{5,3},{7,5},{8,14},{10,8},{12,... | collective-permute-start | bytes 1966088 | tf_op jit(solution)/shard_map/ppermute | solution.py:67
  78.7 27.0 %collective-permute-start.19 = (bf16[128,1408]{1,0:T(8,128)(2,1)S(1)}, bf16[128,1408]{1,0:T(8,128)(2,1)S(1)}, u32[]{:S(2)}, u32[]{:S(2)}) collective-permute-start(bf16[128,1408]{1,0:T(8,128)(2,1)S(1)} %constant_dynamic-slice_fusion.2), channel_id=1, source_target_pairs={{0,1},{1,0},{2,3},{3,2},{4,5},{5,4},{6,7},{7,6},{8,9},{9,8},{10,11... | collective-permute-start | bytes 1081352 | tf_op jit(solution)/shard_map/ppermute | solution.py:480
  106.5 258.8 %reduce-scatter.8.cloned.1.call-start = ((), (), s32[]{:S(2)}) async-start(), calls=%async_computation.12 | async-start | bytes 2359296 | tf_op jit(solution)/shard_map/reduce_scatter | solution.py:553
  110.2 14.1 %collective-permute-start.10 = (bf16[160,2048]{1,0:T(8,128)(2,1)S(1)}, bf16[160,2048]{1,0:T(8,128)(2,1)S(1)}, u32[]{:S(2)}, u32[]{:S(2)}) collective-permute-start(bf16[160,2048]{1,0:T(8,128)(2,1)S(1)} %pad_maximum_fusion.1), channel_id=1, source_target_pairs={{0,6},{2,0},{4,2},{6,4},{1,7},{3,1},{5,3},{7,5},{8,14},{10,8},{12,... | collective-permute-start | bytes 1966088 | tf_op jit(solution)/shard_map/ppermute | solution.py:80
  116.3 14.2 %collective-permute-start.8 = (bf16[160,2048]{1,0:T(8,128)(2,1)S(1)}, bf16[160,2048]{1,0:T(8,128)(2,1)S(1)}, u32[]{:S(2)}, u32[]{:S(2)}) collective-permute-start(bf16[160,2048]{1,0:T(8,128)(2,1)S(1)} %pad_maximum_fusion), channel_id=1, source_target_pairs={{0,2},{2,4},{4,6},{6,0},{1,3},{3,5},{5,7},{7,1},{8,10},{10,12},{12... | collective-permute-start | bytes 1966088 | tf_op jit(solution)/shard_map/ppermute | solution.py:79
  116.4 25.8 %collective-permute-start.16 = (bf16[160,2048]{1,0:T(8,128)(2,1)S(1)}, bf16[160,2048]{1,0:T(8,128)(2,1)S(1)}, u32[]{:S(2)}, u32[]{:S(2)}) collective-permute-start(bf16[160,2048]{1,0:T(8,128)(2,1)S(1)} %copy-done.10), channel_id=1, source_target_pairs={{0,2},{2,4},{4,6},{6,0},{1,3},{3,5},{5,7},{7,1},{8,10},{10,12},{12... | collective-permute-start | bytes 1966088 | tf_op jit(solution)/shard_map/ppermute | solution.py:66
  116.5 26.6 %collective-permute-start.15 = (bf16[160,2048]{1,0:T(8,128)(2,1)S(1)}, bf16[160,2048]{1,0:T(8,128)(2,1)S(1)}, u32[]{:S(2)}, u32[]{:S(2)}) collective-permute-start(bf16[160,2048]{1,0:T(8,128)(2,1)S(1)} %copy-done.10), channel_id=1, source_target_pairs={{0,6},{2,0},{4,2},{6,4},{1,7},{3,1},{5,3},{7,5},{8,14},{10,8},{12,... | collective-permute-start | bytes 1966088 | tf_op jit(solution)/shard_map/ppermute | solution.py:67
  131.8 24.5 %collective-permute-start.12 = (bf16[160,2048]{1,0:T(8,128)(2,1)S(1)}, bf16[160,2048]{1,0:T(8,128)(2,1)S(1)}, u32[]{:S(2)}, u32[]{:S(2)}) collective-permute-start(bf16[160,2048]{1,0:T(8,128)(2,1)S(1)} %maximum_select_fusion.4.n0), channel_id=1, source_target_pairs={{0,2},{2,4},{4,6},{6,0},{1,3},{3,5},{5,7},{7,1},{8,10},{10,12},{12... | collective-permute-start | bytes 1966088 | tf_op jit(solution)/shard_map/ppermute | solution.py:66
  131.8 24.5 %collective-permute-start.11 = (bf16[160,2048]{1,0:T(8,128)(2,1)S(1)}, bf16[160,2048]{1,0:T(8,128)(2,1)S(1)}, u32[]{:S(2)}, u32[]{:S(2)}) collective-permute-start(bf16[160,2048]{1,0:T(8,128)(2,1)S(1)} %maximum_select_fusion.4.n0), channel_id=1, source_target_pairs={{0,6},{2,0},{4,2},{6,4},{1,7},{3,1},{5,3},{7,5},{8,14},{10,8},{12,... | collective-permute-start | bytes 1966088 | tf_op jit(solution)/shard_map/ppermute | solution.py:67
  143.0 24.7 %collective-permute-start.17 = (bf16[80,2048]{1,0:T(8,128)(2,1)}, bf16[80,2048]{1,0:T(8,128)(2,1)}, u32[]{:S(2)}, u32[]{:S(2)}) collective-permute-start(bf16[80,2048]{1,0:T(8,128)(2,1)} %slice.198), channel_id=1, source_target_pairs={{0,2},{2,4},{4,6},{6,0},{1,3},{3,5},{5,7},{7,1},{8,10},{10,12},{12... | collective-permute-start | bytes 983048 | tf_op jit(solution)/shard_map/ppermute | solution.py:68
  143.1 24.7 %collective-permute-start.18 = (bf16[80,2048]{1,0:T(8,128)(2,1)S(1)}, bf16[80,2048]{1,0:T(8,128)(2,1)}, u32[]{:S(2)}, u32[]{:S(2)}) collective-permute-start(bf16[80,2048]{1,0:T(8,128)(2,1)S(1)} %slice.199), channel_id=1, source_target_pairs={{0,6},{2,0},{4,2},{6,4},{1,7},{3,1},{5,3},{7,5},{8,14},{10,8},{12,... | collective-permute-start | bytes 983048 | tf_op jit(solution)/shard_map/ppermute | solution.py:69
  156.3 14.0 %collective-permute-start.13 = (bf16[80,2048]{1,0:T(8,128)(2,1)S(1)}, bf16[80,2048]{1,0:T(8,128)(2,1)}, u32[]{:S(2)}, u32[]{:S(2)}) collective-permute-start(bf16[80,2048]{1,0:T(8,128)(2,1)S(1)} %slice.196), channel_id=1, source_target_pairs={{0,2},{2,4},{4,6},{6,0},{1,3},{3,5},{5,7},{7,1},{8,10},{10,12},{12... | collective-permute-start | bytes 983048 | tf_op jit(solution)/shard_map/ppermute | solution.py:68
  157.4 12.9 %collective-permute-start.14 = (bf16[80,2048]{1,0:T(8,128)(2,1)}, bf16[80,2048]{1,0:T(8,128)(2,1)}, u32[]{:S(2)}, u32[]{:S(2)}) collective-permute-start(bf16[80,2048]{1,0:T(8,128)(2,1)} %slice.197), channel_id=1, source_target_pairs={{0,6},{2,0},{4,2},{6,4},{1,7},{3,1},{5,3},{7,5},{8,14},{10,8},{12,... | collective-permute-start | bytes 983048 | tf_op jit(solution)/shard_map/ppermute | solution.py:69
  198.8 18.6 %collective-permute-start.24 = (bf16[80,2048]{1,0:T(8,128)(2,1)}, bf16[80,2048]{1,0:T(8,128)(2,1)}, u32[]{:S(2)}, u32[]{:S(2)}) collective-permute-start(bf16[80,2048]{1,0:T(8,128)(2,1)} %get-tuple-element.55), channel_id=1, source_target_pairs={{0,6},{2,0},{4,2},{6,4},{1,7},{3,1},{5,3},{7,5},{8,14},{10,8},{12,... | collective-permute-start | bytes 983048 | tf_op jit(solution)/shard_map/ppermute | solution.py:76
  214.5 11.7 %collective-permute-start.26 = (bf16[80,2048]{1,0:T(8,128)(2,1)S(1)}, bf16[80,2048]{1,0:T(8,128)(2,1)S(1)}, u32[]{:S(2)}, u32[]{:S(2)}) collective-permute-start(bf16[80,2048]{1,0:T(8,128)(2,1)S(1)} %copy-done.48), channel_id=1, source_target_pairs={{0,2},{2,4},{4,6},{6,0},{1,3},{3,5},{5,7},{7,1},{8,10},{10,12},{12... | collective-permute-start | bytes 983048 | tf_op jit(solution)/shard_map/ppermute | solution.py:75
  217.2 9.2 %collective-permute-start.22 = (bf16[80,2048]{1,0:T(8,128)(2,1)S(1)}, bf16[80,2048]{1,0:T(8,128)(2,1)S(1)}, u32[]{:S(2)}, u32[]{:S(2)}) collective-permute-start(bf16[80,2048]{1,0:T(8,128)(2,1)S(1)} %copy-done.47), channel_id=1, source_target_pairs={{0,2},{2,4},{4,6},{6,0},{1,3},{3,5},{5,7},{7,1},{8,10},{10,12},{12... | collective-permute-start | bytes 983048 | tf_op jit(solution)/shard_map/ppermute | solution.py:75
  218.6 23.8 %collective-permute-start.25 = (bf16[160,2048]{1,0:T(8,128)(2,1)S(1)}, bf16[160,2048]{1,0:T(8,128)(2,1)S(1)}, u32[]{:S(2)}, u32[]{:S(2)}) collective-permute-start(bf16[160,2048]{1,0:T(8,128)(2,1)S(1)} %pad_maximum_fusion.3), channel_id=1, source_target_pairs={{0,6},{2,0},{4,2},{6,4},{1,7},{3,1},{5,3},{7,5},{8,14},{10,8},{12,... | collective-permute-start | bytes 1966088 | tf_op jit(solution)/shard_map/ppermute | solution.py:80
  224.3 17.5 %collective-permute-start.29 = (bf16[160,2048]{1,0:T(8,128)(2,1)S(1)}, bf16[160,2048]{1,0:T(8,128)(2,1)S(1)}, u32[]{:S(2)}, u32[]{:S(2)}) collective-permute-start(bf16[160,2048]{1,0:T(8,128)(2,1)S(1)} %pad_maximum_fusion.5), channel_id=1, source_target_pairs={{0,6},{2,0},{4,2},{6,4},{1,7},{3,1},{5,3},{7,5},{8,14},{10,8},{12,... | collective-permute-start | bytes 1966088 | tf_op jit(solution)/shard_map/ppermute | solution.py:80
  226.4 15.5 %collective-permute-start.27 = (bf16[160,2048]{1,0:T(8,128)(2,1)S(1)}, bf16[160,2048]{1,0:T(8,128)(2,1)S(1)}, u32[]{:S(2)}, u32[]{:S(2)}) collective-permute-start(bf16[160,2048]{1,0:T(8,128)(2,1)S(1)} %pad_maximum_fusion.4), channel_id=1, source_target_pairs={{0,2},{2,4},{4,6},{6,0},{1,3},{3,5},{5,7},{7,1},{8,10},{10,12},{12... | collective-permute-start | bytes 1966088 | tf_op jit(solution)/shard_map/ppermute | solution.py:79
  226.6 26.8 %collective-permute-start.23 = (bf16[160,2048]{1,0:T(8,128)(2,1)S(1)}, bf16[160,2048]{1,0:T(8,128)(2,1)S(1)}, u32[]{:S(2)}, u32[]{:S(2)}) collective-permute-start(bf16[160,2048]{1,0:T(8,128)(2,1)S(1)} %pad_maximum_fusion.2), channel_id=1, source_target_pairs={{0,2},{2,4},{4,6},{6,0},{1,3},{3,5},{5,7},{7,1},{8,10},{10,12},{12... | collective-permute-start | bytes 1966088 | tf_op jit(solution)/shard_map/ppermute | solution.py:79
  255.4 16.8 %collective-permute-start.31 = (bf16[160,2048]{1,0:T(8,128)(2,1)S(1)}, bf16[160,2048]{1,0:T(8,128)(2,1)S(1)}, u32[]{:S(2)}, u32[]{:S(2)}) collective-permute-start(bf16[160,2048]{1,0:T(8,128)(2,1)S(1)} %get-tuple-element.80.b0), channel_id=1, source_target_pairs={{0,2},{2,4},{4,6},{6,0},{1,3},{3,5},{5,7},{7,1},{8,10},{10,12},{12... | collective-permute-start | bytes 1966088 | tf_op jit(solution)/shard_map/ppermute | solution.py:66
  255.5 16.8 %collective-permute-start.30 = (bf16[160,2048]{1,0:T(8,128)(2,1)S(1)}, bf16[160,2048]{1,0:T(8,128)(2,1)S(1)}, u32[]{:S(2)}, u32[]{:S(2)}) collective-permute-start(bf16[160,2048]{1,0:T(8,128)(2,1)S(1)} %get-tuple-element.80.b0), channel_id=1, source_target_pairs={{0,6},{2,0},{4,2},{6,4},{1,7},{3,1},{5,3},{7,5},{8,14},{10,8},{12,... | collective-permute-start | bytes 1966088 | tf_op jit(solution)/shard_map/ppermute | solution.py:67
  272.2 8.9 %collective-permute-start.32 = (bf16[80,2048]{1,0:T(8,128)(2,1)S(1)}, bf16[80,2048]{1,0:T(8,128)(2,1)S(1)}, u32[]{:S(2)}, u32[]{:S(2)}) collective-permute-start(bf16[80,2048]{1,0:T(8,128)(2,1)S(1)} %slice.202), channel_id=1, source_target_pairs={{0,2},{2,4},{4,6},{6,0},{1,3},{3,5},{5,7},{7,1},{8,10},{10,12},{12... | collective-permute-start | bytes 983048 | tf_op jit(solution)/shard_map/ppermute | solution.py:68
  272.4 8.8 %collective-permute-start.33 = (bf16[80,2048]{1,0:T(8,128)(2,1)S(1)}, bf16[80,2048]{1,0:T(8,128)(2,1)S(1)}, u32[]{:S(2)}, u32[]{:S(2)}) collective-permute-start(bf16[80,2048]{1,0:T(8,128)(2,1)S(1)} %slice.203), channel_id=1, source_target_pairs={{0,6},{2,0},{4,2},{6,4},{1,7},{3,1},{5,3},{7,5},{8,14},{10,8},{12,... | collective-permute-start | bytes 983048 | tf_op jit(solution)/shard_map/ppermute | solution.py:69
  285.2 96.7 %reduce-scatter.6.cloned.1.call-start = ((), (), s32[]{:S(2)}) async-start(), calls=%async_computation.10 | async-start | bytes 2949120 | tf_op jit(solution)/shard_map/reduce_scatter | solution.py:553
  334.3 91.8 %reduce-scatter.14.cloned.1.call-start = ((), (), s32[]{:S(2)}) async-start(), calls=%async_computation.18 | async-start | bytes 6488064 | tf_op jit(solution)/shard_map/reduce_scatter | solution.py:553
  344.4 125.7 %reduce-scatter.12.cloned.1.call-start = ((), (), s32[]{:S(2)}) async-start(), calls=%async_computation.16 | async-start | bytes 6488064 | tf_op jit(solution)/shard_map/reduce_scatter | solution.py:553
  354.9 159.0 %reduce-scatter.10.cloned.1.call-start = ((), (), s32[]{:S(2)}) async-start(), calls=%async_computation.14 | async-start | bytes 6488064 | tf_op jit(solution)/shard_map/reduce_scatter | solution.py:553
  365.2 221.3 %all-gather.23.cloned.1.call-start = ((), (), s32[]{:S(2)}) async-start(), calls=%async_computation.13 | async-start | bytes 1179648 | tf_op jit(solution)/shard_map/all_gather | solution.py:564
  377.7 211.6 %all-gather.21.cloned.1.call-start = ((), (), s32[]{:S(2)}) async-start(), calls=%async_computation.11 | async-start | bytes 1474560 | tf_op jit(solution)/shard_map/all_gather | solution.py:564
  397.0 199.4 %all-gather.29.cloned.1.call-start = ((), (), s32[]{:S(2)}) async-start(), calls=%async_computation.19 | async-start | bytes 3244032 | tf_op jit(solution)/shard_map/all_gather | solution.py:564
  427.3 8.9 %collective-permute-start.56 = (bf16[88,2048]{1,0:T(8,128)(2,1)S(1)}, bf16[88,2048]{1,0:T(8,128)(2,1)S(1)}, u32[]{:S(2)}, u32[]{:S(2)}) collective-permute-start(bf16[88,2048]{1,0:T(8,128)(2,1)S(1)} %select_bitcast_fusion), channel_id=1, source_target_pairs={{0,1},{1,0},{2,3},{3,2},{4,5},{5,4},{6,7},{7,6},{8,9},{9,8},{10,11... | collective-permute-start | bytes 1081352 | tf_op jit(solution)/shard_map/ppermute | solution.py:561
  444.5 180.8 %all-gather.27.cloned.1.call-start = ((), (), s32[]{:S(2)}) async-start(), calls=%async_computation.17 | async-start | bytes 3244032 | tf_op jit(solution)/shard_map/all_gather | solution.py:564
  471.1 9.0 %collective-permute-start.54 = (bf16[128,1408]{1,0:T(8,128)(2,1)S(1)}, bf16[128,1408]{1,0:T(8,128)(2,1)S(1)}, u32[]{:S(2)}, u32[]{:S(2)}) collective-permute-start(bf16[128,1408]{1,0:T(8,128)(2,1)S(1)} %slice_bitcast_fusion), channel_id=1, source_target_pairs={{0,1},{1,0},{2,3},{3,2},{4,5},{5,4},{6,7},{7,6},{8,9},{9,8},{10,11... | collective-permute-start | bytes 1081352 | tf_op jit(solution)/shard_map/ppermute | solution.py:561
  488.8 165.8 %all-gather.25.cloned.1.call-start = ((), (), s32[]{:S(2)}) async-start(), calls=%async_computation.15 | async-start | bytes 3244032 | tf_op jit(solution)/shard_map/all_gather | solution.py:564
  515.0 9.0 %collective-permute-start.52 = (bf16[128,1408]{1,0:T(8,128)(2,1)S(1)}, bf16[128,1408]{1,0:T(8,128)(2,1)S(1)}, u32[]{:S(2)}, u32[]{:S(2)}) collective-permute-start(bf16[128,1408]{1,0:T(8,128)(2,1)S(1)} %slice_bitcast_fusion.2), channel_id=1, source_target_pairs={{0,1},{1,0},{2,3},{3,2},{4,5},{5,4},{6,7},{7,6},{8,9},{9,8},{10,11... | collective-permute-start | bytes 1081352 | tf_op jit(solution)/shard_map/ppermute | solution.py:561
  519.0 15.9 %collective-permute-start.35 = (bf16[80,2048]{1,0:T(8,128)(2,1)}, bf16[80,2048]{1,0:T(8,128)(2,1)S(1)}, u32[]{:S(2)}, u32[]{:S(2)}) collective-permute-start(bf16[80,2048]{1,0:T(8,128)(2,1)} %get-tuple-element.69), channel_id=1, source_target_pairs={{0,2},{2,4},{4,6},{6,0},{1,3},{3,5},{5,7},{7,1},{8,10},{10,12},{12... | collective-permute-start | bytes 983048 | tf_op jit(solution)/shard_map/ppermute | solution.py:75
  532.5 12.5 %collective-permute-start.38 = (bf16[160,2048]{1,0:T(8,128)(2,1)S(1)}, bf16[160,2048]{1,0:T(8,128)(2,1)S(1)}, u32[]{:S(2)}, u32[]{:S(2)}) collective-permute-start(bf16[160,2048]{1,0:T(8,128)(2,1)S(1)} %pad_maximum_fusion.7), channel_id=1, source_target_pairs={{0,6},{2,0},{4,2},{6,4},{1,7},{3,1},{5,3},{7,5},{8,14},{10,8},{12,... | collective-permute-start | bytes 1966088 | tf_op jit(solution)/shard_map/ppermute | solution.py:80
  535.0 13.6 %collective-permute-start.36 = (bf16[160,2048]{1,0:T(8,128)(2,1)S(1)}, bf16[160,2048]{1,0:T(8,128)(2,1)S(1)}, u32[]{:S(2)}, u32[]{:S(2)}) collective-permute-start(bf16[160,2048]{1,0:T(8,128)(2,1)S(1)} %pad_maximum_fusion.6), channel_id=1, source_target_pairs={{0,2},{2,4},{4,6},{6,0},{1,3},{3,5},{5,7},{7,1},{8,10},{10,12},{12... | collective-permute-start | bytes 1966088 | tf_op jit(solution)/shard_map/ppermute | solution.py:79
  561.9 13.2 %collective-permute-start.46 = (f32[2,2048]{1,0:T(2,128)S(1)}, f32[2,2048]{1,0:T(2,128)S(1)}, u32[]{:S(2)}, u32[]{:S(2)}) collective-permute-start(f32[2,2048]{1,0:T(2,128)S(1)} %add.240), channel_id=1, source_target_pairs={{0,96},{32,0},{64,32},{96,64},{1,97},{33,1},{65,33},{97,65},{2,98}... | collective-permute-start | bytes 49160 | tf_op jit(solution)/shard_map/ppermute | solution.py:574
  (77 other events, 575.7 us)
Sparse Core Ops, SparseCore 0:
  17.4 26.5 all-gather.10
  46.3 23.4 all-gather.12
  71.5 26.5 all-gather.18
  100.2 27.1 all-gather.16
  129.5 27.1 all-gather.14
  285.3 45.2 reduce-scatter.7
  334.4 47.4 reduce-scatter.5
  384.8 41.1 reduce-scatter.13
  429.1 40.9 reduce-scatter.11
  472.9 40.9 reduce-scatter.9
  516.2 25.3 all-gather.22
  543.7 23.6 all-gather.20
  569.2 27.1 all-gather.28
  598.4 26.8 all-gather.26
  627.4 27.1 all-gather.24

commit v2 on v1

v2 whole, which is shorter than its diff:
```python
import jax
import jax.numpy as jnp
from jax import lax
from jax.experimental import pallas as pl
from jax.experimental.pallas import tpu as pltpu
from jax.sharding import Mesh
from jax.sharding import PartitionSpec as P

HEADS = 32
KV = 4
HD = 64
EPSILON = 1e-05
ROTARY_BASE = 10000.0
MASKED = -1e30

AXES = ("y", "zl", "core", "x", "zh")
SIZES = (4, 2, 2, 4, 2)
BLK = 160
HALF = BLK // 2
ROWS = 4 * BLK
CAP = 2 * ROWS
D = 2048
DH = D // 2
QW = 640
AW = 512
FF4 = 1408
TILE = 256
F32 = jnp.float32
BF16 = jnp.bfloat16
VLIM = 60 * 1024 * 1024


def spec(memory=pltpu.VMEM):
    return pl.BlockSpec(memory_space=memory)


def params(**kw):
    return pltpu.CompilerParams(vmem_limit_bytes=VLIM, **kw)


def cost(flops, nbytes):
    return pl.CostEstimate(flops=int(flops), bytes_accessed=int(nbytes), transcendentals=0)


def sds(shape, dtype=BF16):
    return jax.ShapeDtypeStruct(shape, dtype)


def dot(a, b):
    return jnp.dot(a, b, preferred_element_type=F32)


def dot_t(a, b):
    return lax.dot_general(a, b, (((1,), (1,)), ((), ())), preferred_element_type=F32)


def t_dot(a, b):
    return lax.dot_general(a, b, (((0,), (0,)), ((), ())), preferred_element_type=F32)


def tie(v, *deps):
    return lax.optimization_barrier((v,) + deps)[0]


def shift(n, s):
    return [(i, (i + s) % n) for i in range(n)]


def gather_x(v):
    from_prev = lax.ppermute(v, "x", shift(4, 1))
    from_next = lax.ppermute(v, "x", shift(4, -1))
    opp_a = lax.ppermute(from_prev[:HALF], "x", shift(4, 1))
    opp_b = lax.ppermute(from_next[HALF:], "x", shift(4, -1))
    return v, from_next, opp_a, opp_b, from_prev


def gather_direct(v):
    return v, *(lax.ppermute(v, "x", shift(4, -s)) for s in (1, 2, 3))


def scatter_direct(parts):
    got = [lax.ppermute(parts[s], "x", shift(4, s)) for s in (1, 2, 3)]
    return sum((g.astype(F32) for g in got), parts[0].astype(F32))


def scatter_x(parts):
    p0, p1, p2a, p2b, p3 = parts
    got_a = lax.ppermute(p2a, "x", shift(4, 1))
    got_b = lax.ppermute(p2b, "x", shift(4, -1))
    q1 = jnp.concatenate([(p1[:HALF].astype(F32) + got_a.astype(F32)).astype(BF16), p1[HALF:]], 0)
    q3 = jnp.concatenate([p3[:HALF], (p3[HALF:].astype(F32) + got_b.astype(F32)).astype(BF16)], 0)
    from_prev = lax.ppermute(q1, "x", shift(4, 1))
    from_next = lax.ppermute(q3, "x", shift(4, -1))
    return p0.astype(F32) + from_prev.astype(F32) + from_next.astype(F32)


PIECES = ((0, BLK), (1, BLK), (2, HALF), (2, HALF), (3, BLK))
PIECE_ROW = (0, BLK, 2 * BLK, 2 * BLK + HALF, 3 * BLK)


def part_shapes(width, dtype=BF16):
    return tuple(sds((n, width), dtype) for _, n in PIECES)


def low_lanes(shape):
    return lax.broadcasted_iota(jnp.int32, shape, 1) < HD


def swap_halves(v):
    lane = lax.broadcasted_iota(jnp.int32, v.shape, 1) % HD
    return jnp.where(lane < HD // 2, pltpu.roll(v, 128 - HD // 2, 1), pltpu.roll(v, HD // 2, 1))


def rows_at(block):
    return pl.ds(pl.multiple_of(block * BLK, 32), BLK)


def fetch_partner(w, core):
    half = w.shape[0] // 2
    got = lax.ppermute(lax.dynamic_slice_in_dim(w, core * half, half, 0), "zh", shift(2, 1))
    return w, got, lax.ppermute(got, "core", shift(2, 1))


def weight_rows(idx, rows):
    zh, core = idx[1], idx[2]
    far = (1 - zh) * rows
    half = rows // 2
    at = lambda first, n: pl.ds(pl.multiple_of(first, half), n)
    return at(zh * rows, rows), at(far + core * half, half), at(far + (1 - core) * half, half)


def qkv_body(idx, n0, n1, n2a, n2b, n3, w0, w1, w2, cosine, sine, q_ref, kv_ref, rows):
    x = idx[0]
    lo = low_lanes((BLK, 128))
    for ref, row, (_, n) in zip((n0, n1, n2a, n2b, n3), PIECE_ROW, PIECES):
        rows[row : row + n, :] = ref[...]
    s0, s1, s2 = weight_rows(idx, DH)
    acc = dot(rows[:, s0], w0[...]) + dot(rows[:, s1], w1[...]) + dot(rows[:, s2], w2[...])
    for d in range(4):
        at = rows_at((x + d) & 3)
        cs = cosine[at, :]
        sn = sine[at, :]
        for p in range(5):
            v = acc[d * BLK : (d + 1) * BLK, p * 128 : (p + 1) * 128]
            r = v * cs + swap_halves(v) * sn
            if p < 4:
                q_ref[at, p * 128 : (p + 1) * 128] = (r * HD**-0.5).astype(BF16)
            else:
                kv_ref[at, :] = jnp.where(lo, r, v).astype(BF16)


def qkv_forward(idx, pieces, weight, cosine, sine):
    return pl.pallas_call(
        qkv_body,
        out_shape=(sds((ROWS, AW)), sds((ROWS, 128))),
        in_specs=[spec(pltpu.SMEM)] + [spec()] * 10,
        out_specs=(spec(), spec()),
        scratch_shapes=[pltpu.VMEM((ROWS, D), BF16)],
        compiler_params=params(),
        cost_estimate=cost(2 * ROWS * D * QW, 7e6),
        name="qkv_forward",
    )(idx, *pieces, *weight, cosine, sine)


def spread_keys(zh, kv_own, kv_par, kk, vv):
    lo = low_lanes((BLK, 128))
    for j in range(4):
        for src, off in ((kv_own, zh), (kv_par, 1 - zh)):
            v = src[j * BLK : (j + 1) * BLK, :].astype(F32)
            w = pltpu.roll(v, HD, 1)
            at = rows_at(2 * j + off)
            kk[at, :] = jnp.where(lo, v, w).astype(BF16)
            vv[at, :] = jnp.where(lo, w, v).astype(BF16)


def fill_bias(zh, j, n, first, bias):
    t = (2 * j + zh) * BLK + lax.broadcasted_iota(jnp.int32, (BLK, n), 0)
    u = lax.broadcasted_iota(jnp.int32, (BLK, n), 1)
    start = first[j * BLK : (j + 1) * BLK, :]
    value = jnp.where((u <= t) & (u >= start), 0.0, MASKED)
    bias[0:BLK, 0:n] = value
    bias[BLK : 2 * BLK, 0:n] = value


def two_heads(v):
    lo = low_lanes(v.shape)
    zero = jnp.zeros_like(v)
    return jnp.concatenate([jnp.where(lo, v, zero), jnp.where(lo, zero, v)], 0)


def attend_body(idx, q, kv_own, kv_par, first, att, lse_ref, kk, vv, bias):
    x, zh = idx[0], idx[1]
    spread_keys(zh, kv_own, kv_par, kk, vv)
    lo = low_lanes((BLK, 128))
    lane = lax.broadcasted_iota(jnp.int32, (BLK, 128), 1)
    for j in range(4):
        n = 2 * BLK * (j + 1)
        fill_bias(zh, j, n, first, bias)
        rel = (j - x) & 3

        def pair(p, lse):
            cols = pl.ds(pl.multiple_of(p * 128, 128), 128)
            q2 = two_heads(q[j * BLK : (j + 1) * BLK, cols])
            s = dot_t(q2, kk[0:n, :]) + bias[:, 0:n]
            top = jnp.max(s, axis=1, keepdims=True)
            e = jnp.exp(s - top)
            total = jnp.sum(e, axis=1, keepdims=True)
            o = dot(e.astype(BF16), vv[0:n, :]) / total
            att[rel, :, cols] = jnp.where(lo, o[:BLK], o[BLK:]).astype(BF16)
            ls = top + jnp.log(total)
            lse = jnp.where(lane == 2 * p, ls[:BLK], lse)
            return jnp.where(lane == 2 * p + 1, ls[BLK:], lse)

        lse_ref[j * BLK : (j + 1) * BLK, :] = lax.fori_loop(0, 4, pair, jnp.zeros((BLK, 128), F32))


def attend(idx, q, kv_own, kv_par, first):
    return pl.pallas_call(
        attend_body,
        out_shape=(sds((4, BLK, AW)), sds((ROWS, 128), F32)),
        in_specs=[spec(pltpu.SMEM)] + [spec()] * 4,
        out_specs=(spec(), spec()),
        scratch_shapes=[
            pltpu.VMEM((CAP, 128), BF16),
            pltpu.VMEM((CAP, 128), BF16),
            pltpu.VMEM((2 * BLK, CAP), F32),
        ],
        compiler_params=params(),
        cost_estimate=cost(1.2e10, 3e6),
        name="attend",
    )(idx, q, kv_own, kv_par, first)


def out_body(idx, att, w0, w1, w2, o0, o1, o2a, o2b, o3):
    s0, s1, s2 = weight_rows(idx, AW // 2)
    for d, ref in ((2, None), (1, o1), (3, o3), (0, o0)):
        a = att.at[d]
        res = dot(a[:, s0], w0[...]) + dot(a[:, s1], w1[...]) + dot(a[:, s2], w2[...])
        res = res.astype(BF16)
        if d == 2:
            o2a[...] = res[:HALF]
            o2b[...] = res[HALF:]
        else:
            ref[...] = res


def out_project(idx, att, weight):
    return pl.pallas_call(
        out_body,
        out_shape=part_shapes(D),
        in_specs=[spec(pltpu.SMEM)] + [spec()] * 4,
        out_specs=(spec(),) * 5,
        compiler_params=params(),
        cost_estimate=cost(2 * ROWS * D * AW, 5.5e6),
        name="out_project",
    )(idx, att, *weight)


def attend_back_body(
    idx, q, kv_own, kv_par, first, lse_ref, att, b0, b1, b2a, b2b, b3, w0, w1, w2,
    dq_ref, dkv_own, dkv_par, kk, vv, bias, dout, dkk, dvv,
):
    x, zh = idx[0], idx[1]
    spread_keys(zh, kv_own, kv_par, kk, vv)
    s0, s1, s2 = weight_rows(idx, AW // 2)
    for d in range(4):
        if d == 2:
            rows = jnp.concatenate([b2a[...], b2b[...]], 0)
        else:
            rows = (b0, b1, None, b3)[d][...]
        at = rows_at((x + d) & 3)
        for s, w in ((s0, w0), (s1, w1), (s2, w2)):
            dout[at, s] = dot_t(rows, w[...]).astype(BF16)
    dkk[...] = jnp.zeros_like(dkk)
    dvv[...] = jnp.zeros_like(dvv)
    lo = low_lanes((BLK, 128))
    lane = lax.broadcasted_iota(jnp.int32, (BLK, 128), 1)
    for j in range(4):
        n = 2 * BLK * (j + 1)
        fill_bias(zh, j, n, first, bias)
        rel = (j - x) & 3
        lse_all = lse_ref[j * BLK : (j + 1) * BLK, :]

        def pair(p, carry):
            cols = pl.ds(pl.multiple_of(p * 128, 128), 128)
            q2 = two_heads(q[j * BLK : (j + 1) * BLK, cols])
            do = dout[j * BLK : (j + 1) * BLK, cols]
            do2 = two_heads(do)
            prod = two_heads(do.astype(F32) * att[rel, :, cols].astype(F32))
            delta = jnp.sum(prod, axis=1, keepdims=True)
            ls = jnp.concatenate(
                [
                    jnp.sum(jnp.where(lane == 2 * p, lse_all, 0.0), axis=1, keepdims=True),
                    jnp.sum(jnp.where(lane == 2 * p + 1, lse_all, 0.0), axis=1, keepdims=True),
                ],
                0,
            )
            s = dot_t(q2, kk[0:n, :]) + bias[:, 0:n]
            e = jnp.exp(s - ls)
            dp = dot_t(do2, vv[0:n, :])
            ds = (e * (dp - delta)).astype(BF16)
            dvv[0:n, :] += t_dot(e.astype(BF16), do2)
            dkk[0:n, :] += t_dot(ds, q2)
            dq = dot(ds, kk[0:n, :]) * HD**-0.5
            dq_ref[j * BLK : (j + 1) * BLK, cols] = jnp.where(lo, dq[:BLK], dq[BLK:])
            return carry

        lax.fori_loop(0, 4, pair, 0)
    for j in range(4):
        for dst, off in ((dkv_own, zh), (dkv_par, 1 - zh)):
            at = rows_at(2 * j + off)
            dk, dv = dkk[at, :], dvv[at, :]
            both = jnp.where(lo, dk + pltpu.roll(dk, HD, 1), dv + pltpu.roll(dv, HD, 1))
            dst[j * BLK : (j + 1) * BLK, :] = both.astype(dst.dtype)


def attend_back(idx, q, kv_own, kv_par, first, lse, att, branch, weight):
    return pl.pallas_call(
        attend_back_body,
        out_shape=(sds((ROWS, AW), F32), sds((ROWS, 128), F32), sds((ROWS, 128))),
        in_specs=[spec(pltpu.SMEM)] + [spec()] * 14,
        out_specs=(spec(),) * 3,
        scratch_shapes=[
            pltpu.VMEM((CAP, 128), BF16),
            pltpu.VMEM((CAP, 128), BF16),
            pltpu.VMEM((2 * BLK, CAP), F32),
            pltpu.VMEM((ROWS, AW), BF16),
            pltpu.VMEM((CAP, 128), F32),
            pltpu.VMEM((CAP, 128), F32),
        ],
        compiler_params=params(),
        cost_estimate=cost(3e10, 8e6),
        name="attend_back",
    )(idx, q, kv_own, kv_par, first, lse, att, *branch, *weight)


def qkv_back_body(
    idx, dq, dkv_own, dkv_got, cosine, sine, w0, w1, w2, n0, n1, n2a, n2b, n3, gain,
    dm_ref, n_all, gain_ref, o0, o1, o2a, o2b, o3, out,
):
    x = idx[0]
    lo = low_lanes((BLK, 128))
    for ref, row, (_, n) in zip((n0, n1, n2a, n2b, n3), PIECE_ROW, PIECES):
        n_all[row : row + n, :] = ref[...]
    slots = weight_rows(idx, DH)
    total = jnp.zeros((8, D), F32)
    for d, ref in ((2, None), (1, o1), (3, o3), (0, o0)):
        at = rows_at((x + d) & 3)
        cs = cosine[at, :]
        sn = sine[at, :]
        mine = pl.ds(d * BLK, BLK)
        for p in range(4):
            v = dq[at, p * 128 : (p + 1) * 128]
            dm_ref[mine, p * 128 : (p + 1) * 128] = (v * cs - swap_halves(v) * sn).astype(BF16)
        v = dkv_own[at, :] + dkv_got[at, :].astype(F32)
        dm_ref[mine, AW:] = jnp.where(lo, v * cs - swap_halves(v) * sn, v).astype(BF16)
        rows = dm_ref[mine, :]
        for s, w in zip(slots, (w0, w1, w2)):
            out[:, s] = dot_t(rows, w[...])
        res = out[...]
        total = total + jnp.sum((res * n_all[mine, :].astype(F32)).reshape(BLK // 8, 8, D), axis=0)
        res = res.astype(BF16)
        if d == 2:
            o2a[...], o2b[...] = res[:HALF], res[HALF:]
        else:
            ref[...] = res
    gain_ref[...] = jnp.sum(total, axis=0, keepdims=True) / gain[...]


def qkv_back(idx, dq, dkv_own, dkv_got, cosine, sine, weight, pieces, gain):
    res = pl.pallas_call(
        qkv_back_body,
        out_shape=(sds((ROWS, QW)), sds((ROWS, D)), sds((1, D), F32)) + part_shapes(D),
        in_specs=[spec(pltpu.SMEM)] + [spec()] * 14,
        out_specs=(spec(),) * 8,
        scratch_shapes=[pltpu.VMEM((BLK, D), F32)],
        compiler_params=params(),
        cost_estimate=cost(2 * ROWS * D * QW, 1.3e7),
        name="qkv_back",
    )(idx, dq, dkv_own, dkv_got, cosine, sine, *weight, *pieces, gain.reshape(1, D))
    return res[0], res[1], res[2], res[3:]


TILES = 6
FFP = TILES * TILE


def load_down(idx, refs, dst, sem):
    copies = []
    for k, (s, ref) in enumerate(zip(weight_rows(idx, FF4 // 2), refs)):
        copies.append(pltpu.make_async_copy(ref, dst.at[s], sem.at[k]))
    return copies


def ffn_body(
    idx, n0, n1, n2a, n2b, n3, c0, c1, c2, c3, gate_w, up_w, w0, w1, w2,
    n_all, c_all, hid, dgate, dup, down, sem,
):
    i = pl.program_id(0)

    @pl.when(i == 0)
    def _():
        copies = load_down(idx, (w0, w1, w2), down, sem)
        for c in copies:
            c.start()
        down[FF4:, :] = jnp.zeros((FFP - FF4, D), BF16)
        for ref, row, (_, n) in zip((n0, n1, n2a, n2b, n3), PIECE_ROW, PIECES):
            n_all[row : row + n, :] = ref[...]
        for d, ref in enumerate((c0, c1, c2, c3)):
            c_all[d * BLK : (d + 1) * BLK, :] = ref[...]
        for c in copies:
            c.wait()

    gate = dot(n_all[...], gate_w[...])
    up = dot(n_all[...], up_w[...])
    dh = dot_t(c_all[...], down[pl.ds(pl.multiple_of(i * TILE, TILE), TILE), :])
    sig = 1.0 / (1.0 + jnp.exp(-gate))
    act = gate * sig
    hid[...] = (act * up).astype(BF16)
    dgate[...] = (dh * up * sig * (1.0 + gate * (1.0 - sig))).astype(BF16)
    dup[...] = (dh * act).astype(BF16)


def whole(n, w):
    return pl.BlockSpec((n, w), lambda i: (0, 0))


def ffn(idx, normed, cots, gate_up, down):
    column = lambda first: pl.BlockSpec((D, TILE), lambda i: (0, i + first))
    hidden = pl.BlockSpec((ROWS, TILE), lambda i: (0, i))
    return pl.pallas_call(
        ffn_body,
        grid=(TILES,),
        out_shape=(sds((ROWS, D)),) * 2 + (sds((ROWS, FF4)),) + (sds((ROWS, FFP)),) * 2,
        in_specs=[spec(pltpu.SMEM)]
        + [whole(n, D) for _, n in PIECES]
        + [whole(BLK, D)] * 4
        + [column(0), column(TILES)]
        + [spec(pl.ANY)] * 3,
        out_specs=[whole(ROWS, D)] * 2 + [hidden] * 3,
        scratch_shapes=[pltpu.VMEM((FFP, D), BF16), pltpu.SemaphoreType.DMA((3,))],
        compiler_params=params(),
        cost_estimate=cost(6 * ROWS * D * FF4, 3.4e7),
        name="ffn",
    )(idx, *normed, *cots, gate_up, gate_up, *down)


def down_body(idx, hid, w0, w1, w2, o0, o1, o2, o3, down, sem):
    copies = load_down(idx, (w0, w1, w2), down, sem)
    for c in copies:
        c.start()
    for c in copies:
        c.wait()
    for n in range(D // 512):
        cols = slice(n * 512, (n + 1) * 512)
        res = dot(hid[...], down[:, cols]).astype(BF16)
        for d, ref in enumerate((o0, o1, o2, o3)):
            ref[:, cols] = res[d * BLK : (d + 1) * BLK]


def down_project(idx, hid, down):
    return pl.pallas_call(
        down_body,
        out_shape=(sds((BLK, D)),) * 4,
        in_specs=[spec(pltpu.SMEM), spec()] + [spec(pl.ANY)] * 3,
        out_specs=(spec(),) * 4,
        scratch_shapes=[pltpu.VMEM((FF4, D), BF16), pltpu.SemaphoreType.DMA((3,))],
        compiler_params=params(),
        cost_estimate=cost(2 * ROWS * D * FF4, 1.1e7),
        name="down_project",
    )(idx, hid, *down)


def ffn_back_body(dgate, dup, gate_up, *refs):
    res = dot_t(dgate[...], gate_up[:, :FFP]) + dot_t(dup[...], gate_up[:, FFP:])
    for ref, row, (_, n) in zip(refs, PIECE_ROW, PIECES):
        ref[...] = res[row : row + n].astype(BF16)


def ffn_back(dgate, dup, gate_up):
    return pl.pallas_call(
        ffn_back_body,
        grid=(D // TILE,),
        out_shape=part_shapes(D),
        in_specs=[whole(ROWS, FFP)] * 2 + [pl.BlockSpec((TILE, 2 * FFP), lambda i: (i, 0))],
        out_specs=[pl.BlockSpec((n, TILE), lambda i: (0, i)) for _, n in PIECES],
        compiler_params=params(),
        cost_estimate=cost(4 * ROWS * D * FF4, 1.8e7),
        name="ffn_back",
    )(dgate, dup, gate_up)


GU_ROWS = FF4 // 128 * 64
PIECE = 2 * GU_ROWS + FF4 // 2


def ffn_grads_body(na, nb, cot, hid, dgate, dup, out, hid_t):
    @pl.when(pl.program_id(0) == 0)
    def _():
        hid_t[...] = hid[...].T

    rows = jnp.concatenate([na[...], nb[...]], 1).T
    for k, ref in enumerate((dgate, dup)):
        g = dot(rows, ref[:, :FF4]).astype(BF16)
        for h in range(2):
            for q in range(2):
                r = g[(2 * h + q) * 64 : (2 * h + q + 1) * 64]
                for c in range(FF4 // 128):
                    first = k * GU_ROWS + c * 64
                    out[h, q, first : first + 64, :] = r[:, c * 128 : (c + 1) * 128]
    g = dot(hid_t[...], cot[...]).astype(BF16)
    for h in range(2):
        for q in range(2):
            out[h, q, 2 * GU_ROWS :, :] = g[
                h * (FF4 // 2) : (h + 1) * (FF4 // 2), q * 128 : (q + 1) * 128
            ]


def ffn_grads(n_all, c_all, hid, dgate, dup):
    return pl.pallas_call(
        ffn_grads_body,
        grid=(8,),
        out_shape=sds((2, 16, PIECE, 128)),
        in_specs=[
            pl.BlockSpec((ROWS, 128), lambda i: (0, i)),
            pl.BlockSpec((ROWS, 128), lambda i: (0, i + 8)),
            pl.BlockSpec((ROWS, 256), lambda i: (0, i)),
            whole(ROWS, FF4),
            whole(ROWS, FFP),
            whole(ROWS, FFP),
        ],
        out_specs=pl.BlockSpec((2, 2, PIECE, 128), lambda i: (0, i, 0, 0)),
        scratch_shapes=[pltpu.VMEM((FF4, ROWS), BF16)],
        compiler_params=params(),
        cost_estimate=cost(6 * ROWS * D * FF4, 3e7),
        name="ffn_grads",
    )(n_all, n_all, c_all, hid, dgate, dup)


def unpack_body(piece, gate, up, down):
    for k, ref in enumerate((gate, up)):
        for c in range(FF4 // 128):
            first = k * GU_ROWS + c * 64
            ref[:, c * 128 : (c + 1) * 128] = piece[0, first : first + 64, :].astype(F32)
    down[...] = piece[0, 2 * GU_ROWS :, :].astype(F32)


def unpack(pieces):
    return pl.pallas_call(
        unpack_body,
        grid=(16,),
        out_shape=(sds((DH, FF4), F32), sds((DH, FF4), F32), sds((FF4 // 2, D), F32)),
        in_specs=[pl.BlockSpec((1, PIECE, 128), lambda i: (i, 0, 0))],
        out_specs=[
            pl.BlockSpec((64, FF4), lambda i: (i, 0)),
            pl.BlockSpec((64, FF4), lambda i: (i, 0)),
            pl.BlockSpec((FF4 // 2, 128), lambda i: (0, i)),
        ],
        compiler_params=params(),
        cost_estimate=cost(1e6, 2.6e7),
        name="unpack",
    )(pieces)


QP = 5 * 128
OP = 2 * (AW // 2)
TAIL = QP + OP + 16


def attn_grads_body(n_all, dm, att, branch, gain_one, gain_two, out):
    rows = n_all[...].T
    g = dot(rows, dm[...]).astype(BF16)
    for h in range(2):
        for c in range(5):
            out[0, h, c * 128 : (c + 1) * 128, :] = g[h * 128 : (h + 1) * 128, c * 128 : (c + 1) * 128]
    g = dot(att[...].T, branch[...]).astype(BF16)
    gains = [r[:, c * 128 : (c + 1) * 128] for r in (gain_one, gain_two) for c in range(2)]
    gains = jnp.concatenate(gains + [jnp.zeros((12, 128), F32)], 0).astype(BF16)
    for h in range(2):
        for c in range(2):
            first = QP + c * (AW // 2)
            out[0, h, first : first + AW // 2, :] = g[
                h * (AW // 2) : (h + 1) * (AW // 2), c * 128 : (c + 1) * 128
            ]
        out[0, h, QP + OP :, :] = gains


def attn_grads_kernel(na, nb, dm, att, branch, gain_one, gain_two, out, rows):
    rows[:, :128] = na[...]
    rows[:, 128:] = nb[...]
    attn_grads_body(rows, dm, att, branch, gain_one, gain_two, out)


def attn_grads(n_all, dm, att, branch, gain_one, gain_two):
    return pl.pallas_call(
        attn_grads_kernel,
        grid=(8,),
        out_shape=sds((8, 2, TAIL, 128)),
        in_specs=[
            pl.BlockSpec((ROWS, 128), lambda i: (0, i)),
            pl.BlockSpec((ROWS, 128), lambda i: (0, i + 8)),
            whole(ROWS, QW),
            whole(ROWS, AW),
            pl.BlockSpec((ROWS, 256), lambda i: (0, i)),
            pl.BlockSpec((1, 256), lambda i: (0, i)),
            pl.BlockSpec((1, 256), lambda i: (0, i)),
        ],
        out_specs=pl.BlockSpec((1, 2, TAIL, 128), lambda i: (i, 0, 0, 0)),
        scratch_shapes=[pltpu.VMEM((ROWS, 256), BF16)],
        compiler_params=params(),
        cost_estimate=cost(2 * ROWS * D * (QW + AW), 1.5e7),
        name="attn_grads",
    )(n_all, n_all, dm, att, branch, gain_one, gain_two)


def unpack_tail_body(piece, qkv, out, gains):
    for c in range(5):
        qkv[:, c * 128 : (c + 1) * 128] = piece[0, c * 128 : (c + 1) * 128, :].astype(F32)
    for c in range(2):
        first = QP + c * (AW // 2)
        out[:, c * 128 : (c + 1) * 128] = piece[0, first : first + AW // 2, :].astype(F32)
    rows = piece[0, QP + OP :, :].astype(F32)
    for c in range(2):
        gains[0:1, c * 128 : (c + 1) * 128] = rows[c : c + 1]
        gains[1:2, c * 128 : (c + 1) * 128] = rows[2 + c : 3 + c]


def unpack_tail(pieces):
    return pl.pallas_call(
        unpack_tail_body,
        grid=(8,),
        out_shape=(sds((DH, QW), F32), sds((AW // 2, D), F32), sds((2, D), F32)),
        in_specs=[pl.BlockSpec((1, TAIL, 128), lambda i: (i, 0, 0))],
        out_specs=[
            pl.BlockSpec((128, QW), lambda i: (i, 0)),
            pl.BlockSpec((AW // 2, 256), lambda i: (0, i)),
            pl.BlockSpec((2, 256), lambda i: (0, i)),
        ],
        compiler_params=params(),
        cost_estimate=cost(1e6, 7e6),
        name="unpack_tail",
    )(pieces)


def bf_sum(*values):
    return sum((v.astype(F32) for v in values[1:]), values[0].astype(F32)).astype(BF16)


def sum_tail(g, y, zl, zh, core):
    g = g.reshape(4, 2, 2, TAIL, 128)
    pick = lambda v, i, axis: lax.dynamic_index_in_dim(v, i, axis, False)
    g = bf_sum(pick(g, core, 1), lax.ppermute(pick(g, 1 - core, 1), "core", shift(2, 1)))
    got = [lax.ppermute(pick(g, (y + s) % 4, 0), "y", shift(4, s)) for s in (1, 2, 3)]
    g = bf_sum(pick(g, y, 0), *got)
    own, other = pick(g, zh, 0), pick(g, 1 - zh, 0)
    cross = [(2 * a + b, 2 * (1 - a) + (1 - b)) for a in range(2) for b in range(2)]
    g = bf_sum(
        own,
        lax.ppermute(own, "zl", shift(2, 1)),
        lax.ppermute(other, "zh", shift(2, 1)),
        lax.ppermute(other, ("zl", "zh"), cross),
    )
    parts = jnp.stack([g] + [lax.ppermute(g, "y", shift(4, s)) for s in (1, 2, 3)])
    other = lax.ppermute(parts, "core", shift(2, 1))
    both = jnp.where(core == 0, jnp.stack([parts, other], 1), jnp.stack([other, parts], 1))
    both = jnp.take(both, (y - jnp.arange(4)) % 4, axis=0)
    return both.reshape(8, TAIL, 128)


def inverse_rms(v):
    return lax.rsqrt(jnp.mean(v * v, axis=-1, keepdims=True) + EPSILON)


def norm_back(v, r, gain, grad):
    pulled = grad * gain
    inner = jnp.mean(v * pulled, axis=-1, keepdims=True)
    return r * pulled - v * (r * r * r) * inner, jnp.sum(grad * v * r, axis=0)


def replica_layout(lengths, replica, replica_id):
    sizes = jnp.where(replica == replica_id, lengths, 0)
    starts = jnp.cumsum(sizes) - sizes
    row_ids = jnp.arange(CAP, dtype=jnp.int32)
    inside = (row_ids[:, None] >= starts[None, :]) & (row_ids[:, None] < (starts + sizes)[None, :])
    begin = jnp.sum(jnp.where(inside, starts[None, :], 0), axis=1)
    begin = begin + jnp.where(jnp.any(inside, axis=1), 0, jnp.sum(sizes))
    return begin, row_ids - begin


def on_device(
    tokens, cotangent, gain_one, qkv_weight, out_weight, gate_weight, up_weight, down_weight,
    gain_two, seq_lengths, seq_replica,
):
    x, zh, core = lax.axis_index("x"), lax.axis_index("zh"), lax.axis_index("core")
    y, zl = lax.axis_index("y"), lax.axis_index("zl")
    idx = jnp.stack([x, zh, core]).astype(jnp.int32)

    tok = tokens.astype(F32)
    s_one = inverse_rms(tok)
    normed_one = gather_x((tok * s_one * gain_one).astype(BF16))
    qkv_all = fetch_partner(qkv_weight, core)
    out_all = fetch_partner(tie(out_weight, qkv_all[1]), core)
    down_all = fetch_partner(tie(down_weight, out_all[1]), core)
    rows = DH // 8
    mine = lambda w: jnp.pad(
        lax.dynamic_slice_in_dim(w, (y * 2 + core) * rows, rows, 0), ((0, 0), (0, FFP - FF4))
    )
    gate_up = lax.all_gather(
        jnp.concatenate([mine(gate_weight), mine(up_weight)], 1), ("zh", "y", "core"), axis=0, tiled=True
    )
    cots = gather_direct(tie(cotangent, normed_one[2]))

    begin, position = replica_layout(seq_lengths, seq_replica, (y * 2 + zl) * 2 + core)
    half_rows = lambda v: lax.dynamic_index_in_dim(v.reshape(4, 2, BLK), zh, 1, False).reshape(ROWS, 1)
    first = half_rows(begin)
    lane = jnp.arange(128, dtype=jnp.int32)
    frequency = ROTARY_BASE ** (-(lane % 32).astype(F32) * (2.0 / HD))
    angles = half_rows(position).astype(F32) * frequency[None, :]
    cosine = jnp.cos(angles)
    sine = jnp.where((lane % HD) < HD // 2, -1.0, 1.0)[None, :] * jnp.sin(angles)

    q, kv_own = qkv_forward(idx, normed_one, qkv_all, cosine, sine)
    kv_par = lax.ppermute(kv_own, "zh", shift(2, 1))
    att, lse = attend(idx, q, kv_own, kv_par, first)
    att = tie(att, down_all[1], *cots)
    after_attn = tok + scatter_x(out_project(idx, att, out_all))

    r_two = inverse_rms(after_attn)
    normed_two = gather_x((after_attn * r_two * gain_two).astype(BF16))
    n_two, cot_all, hid, dgate, dup = ffn(idx, normed_two, cots, gate_up, down_all)
    grads = ffn_grads(n_two, cot_all, hid, dgate, dup)
    grads = lax.psum_scatter(
        grads.reshape(32, PIECE, 128), ("zh", "zl", "y", "core"), scatter_dimension=0, tiled=True
    )
    grads = lax.all_gather(grads, ("zl", "y", "core"), axis=0, tiled=True)
    grad_gate, grad_up, grad_down = unpack(grads)

    d_two = scatter_x(ffn_back(dgate, dup, gate_up))
    back_two, gain_grad_two = norm_back(after_attn, r_two, gain_two, d_two)
    after_grad = cotangent.astype(F32) + back_two
    branch = gather_x(after_grad.astype(BF16))
    layer_parts = down_project(idx, tie(hid, after_grad), down_all)
    layer_parts = [tie(p, branch[2], branch[3]) for p in layer_parts]
    layer_out = after_attn + scatter_direct(layer_parts)
    att = tie(att, *layer_parts)
    dq, dkv_own, dkv_par = attend_back(idx, q, kv_own, kv_par, first, lse, att, branch, out_all)
    dkv_got = lax.ppermute(dkv_par, "zh", shift(2, 1))
    layer_out = layer_out.astype(BF16)
    d_mixed, n_one, gain_grad_one, parts = qkv_back(
        idx, tie(dq, layer_out), dkv_own, dkv_got, cosine, sine, qkv_all, normed_one, gain_one
    )
    d_one = scatter_x(parts)
    back_one, _ = norm_back(tok, s_one, gain_one, d_one)
    input_grad = (after_grad + back_one).astype(BF16)

    over_x = lambda v: sum((lax.ppermute(v, "x", shift(4, s)) for s in (1, 2, 3)), v)
    tail = attn_grads(
        n_one, d_mixed, att.reshape(ROWS, AW), jnp.concatenate(branch, 0),
        gain_grad_one, gain_grad_two.reshape(1, D),
    )
    grad_qkv, grad_out, gains = unpack_tail(sum_tail(tail, y, zl, zh, core))
    gains = over_x(gains)
    return (
        layer_out, input_grad, gains[0], grad_qkv, grad_out, grad_gate, grad_up,
        grad_down, gains[1],
    )


def solution(mesh):
    grid = Mesh(mesh.devices.reshape(SIZES), AXES)
    rows = P(AXES, None)
    both = P(("x", "zh"), None)
    return jax.shard_map(
        on_device,
        mesh=grid,
        in_specs=(
            rows, rows, P(), P("zh", "x"), both, P("zh", "x"), P("zh", "x"), both, P(), P(), P(),
        ),
        out_specs=(
            rows, rows, P(), P("zh", "x"), both, P("zh", "x"), P("zh", "x"), both, P(),
        ),
        check_vma=False,
    )
```

time: 673 us -> 592 us (0.88)
  Pallas kernels: 103 us -> 160 us
  waiting for transfers between devices: 325 us -> 268 us
  matrix products: 27.6 us -> 0 us
  starting transfers between devices: 105 us -> 80.2 us
  other arithmetic: 50.9 us -> 27.8 us
  local copies, waits for them, and re-layouts: 40 us -> 32.2 us
    pallas_call x3 -> x7, Pallas kernels: 36 us -> 91.3 us  [the longest x1 20.9 us: ffn_grads(): pl.pallas_call(ffn_grads_body, grid=(8,), out_shape=sds((2, 16, PIECE, 12...]
    all_gather x10 -> x2, waiting for transfers between devices: 52.5 us -> 0.01 us  [the longest x1 0.01 us: on_device(): lax.all_gather(jnp.concatenate([mine(gate_weight), mine(up_weight)], 1),...]
    ppermute x1, waiting for transfers between devices: 0.65 us -> 45.4 us  [on_device(): kv_par = lax.ppermute(kv_own, 'zh', shift(2, 1))]
    ppermute x4 -> x3, waiting for transfers between devices: 40.7 us -> 12.7 us  [gather_x(): from_prev = lax.ppermute(v, 'x', shift(4, 1))]
    dot_general x5 -> x0, matrix products: 27.6 us -> none  [t_dot(): lax.dot_general(a, b, (((0,), (0,)), ((), ())), preferred_element_type=F32)]
    convert_element_type x17 -> x6, other arithmetic: 27.9 us -> 7.71 us  [the longest x3 4.91 us: bf_sum(): sum((v.astype(F32) for v in values[1:]), values[0].astype(F32)).astype(BF16)]
    reshape x5 -> x0, local copies, waits for them, and re-layouts: 12.4 us -> none  [finish(): g.reshape(2, 8, rows // 8, columns).swapaxes(0, 1)]
    ppermute x24 -> x26, starting transfers between devices: 57.5 us -> 45.7 us  [the longest x3 15.6 us: fetch_partner(): return (w, got, lax.ppermute(got, 'core', shift(2, 1)))]
  transfers between devices with their start and end apart: 73 -> 55, of which waited for: 47 -> 27; matrix products, arithmetic and copies ran while one was open for 15% -> 9% of each run, Pallas kernels for 11% -> 18%
where the time goes in v2:
time: 592 us; the launch traced here: 583 us
  waiting for transfers between devices  268 us (45%)
  Pallas kernels  160 us (27%)
  starting transfers between devices  80.2 us (14%)
  local copies, waits for them, and re-layouts  32.2 us (5%)
  other arithmetic  27.8 us (5%)
  between operations  14.6 us (2%)
    reduce_scatter x1, waiting for transfers between devices, on_device(): lax.psum_scatter(grads.reshape(32, PIECE, 128), ('zh', 'zl', 'y', 'core')...  76.2 us
    ppermute x1, waiting for transfers between devices, on_device(): kv_par = lax.ppermute(kv_own, 'zh', shift(2, 1))  45.4 us
    ppermute x3, waiting for transfers between devices, scatter_x(): from_prev = lax.ppermute(q1, 'x', shift(4, 1))  25.2 us
    pallas_call x1, Pallas kernels, attend_back(): pl.pallas_call(attend_back_body, out_shape=(sds((ROWS, AW), F32), sds((RO...  25.1 us
    ppermute x3, waiting for transfers between devices, sum_tail(): lax.ppermute(pick(g, (y + s) % 4, 0), 'y', shift(4, s))  24.7 us
    pallas_call x1, Pallas kernels, ffn_grads(): pl.pallas_call(ffn_grads_body, grid=(8,), out_shape=sds((2, 16, PIECE, 12...  20.9 us
    pallas_call x1, Pallas kernels, ffn(): pl.pallas_call(ffn_body, grid=(TILES,), out_shape=(sds((ROWS, D)),) * 2 +...  20.7 us
    ppermute x3, waiting for transfers between devices, scatter_x(): from_next = lax.ppermute(q3, 'x', shift(4, -1))  18.9 us
  transfers between devices with their start and end apart: 55, of which 27 were waited for; matrix products, arithmetic and copies ran while one was open for 9% of the time, Pallas kernels for 18%

profile of v2, /device:TPU:1, one launch (start us, length us, event | category | flops | bytes accessed | tf_op | source)
XLA Modules:
  0.0 583.0 jit_solution(12958112336320609633)
XLA Ops:
  10.9 4.4 collective-permute-start.4
  15.8 2.5 collective-permute-start
  19.5 12.7 %collective-permute-done.4.w1 = bf16[512,640]{1,0:T(8,128)(2,1)S(1)} collective-permute-done((bf16[512,640]{1,0:T(8,128)(2,1)}, bf16[512,640]{1,0:T(8,128)(2,1)S(1)}, u32[]{:S(2)}, u32[]{:S(2)}) %collective-permute-start.4) | collective-permute-done | bytes 655392 | tf_op jit(solution)/shard_map/ppermute | solution.py:120
  34.3 3.7 collective-permute-start.7
  38.7 4.1 collective-permute-start.5
  48.6 2.6 constant_dynamic-slice_fusion.2
  52.1 3.6 collective-permute-done.2.n2a
  56.5 7.3 %qkv_forward.1 = (bf16[640,512]{1,0:T(8,128)(2,1)}, bf16[640,128]{1,0:T(8,128)(2,1)}) custom-call(s32[3]{0:T(128)} %pad_add_fusion.idx, bf16[160,2048]{1,0:T(8,128)(2,1)} %copy-done.4, bf16[160,2048]{1,0:T(8,128)(2,1)} %copy-done.12, bf16[80,2048]{1,0:T(8,128)(2,1)} %copy-done.29, bf16[80,2048]{1,0:T(8,128)(2,1)} %copy-done.30, ...), custom_call_target="tpu_custom_call" | custom-call | flops 1677721600 | bytes 7000000 | tf_op jit(solution)/shard_map/qkv_forward/pallas_call | solution.py:153
  64.8 2.4 collective-permute-start.9
  68.3 45.4 %collective-permute-done.6.kv_par = bf16[640,128]{1,0:T(8,128)(2,1)S(1)} collective-permute-done((bf16[640,128]{1,0:T(8,128)(2,1)}, bf16[640,128]{1,0:T(8,128)(2,1)S(1)}, u32[]{:S(2)}, u32[]{:S(2)}) %collective-permute-start.6) | collective-permute-done | bytes 163872 | tf_op jit(solution)/shard_map/ppermute | solution.py:723
  113.7 10.3 %collective-permute-start.12 = (bf16[128,2048]{1,0:T(8,128)(2,1)}, bf16[128,2048]{1,0:T(8,128)(2,1)S(1)}, u32[]{:S(2)}, u32[]{:S(2)}) collective-permute-start(bf16[128,2048]{1,0:T(8,128)(2,1)} %collective-permute-done.7.w1), channel_id=1, source_target_pairs={{0,8},{8,0},{1,9},{9,1},{2,10},{10,2},{3,11},{11,3},{4,12},{12,4},... | collective-permute-start | bytes 1572872 | tf_op jit(solution)/shard_map/ppermute | solution.py:121
  124.0 17.4 %attend.1 = (bf16[4,160,512]{2,1,0:T(8,128)(2,1)}, f32[640,128]{1,0:T(8,128)}) custom-call(s32[3]{0:T(128)} %pad_add_fusion.idx, bf16[640,512]{1,0:T(8,128)(2,1)} %get-tuple-element.60.q, bf16[640,128]{1,0:T(8,128)(2,1)} %get-tuple-element.61.kv_own, bf16[640,128]{1,0:T(8,128)(2,1)} %copy-done.49, s32[640,1]{1,0:T(8,128)} %reshape.220.first), custom_call_target="tpu_custom_call" | custom-call | flops 12000000000 | bytes 3000000 | tf_op jit(solution)/shard_map/attend/pallas_call | solution.py:218
  142.3 4.8 out_project.1
  150.8 6.1 %collective-permute-done.15 = bf16[80,2048]{1,0:T(8,128)(2,1)S(1)} collective-permute-done((bf16[80,2048]{1,0:T(8,128)(2,1)}, bf16[80,2048]{1,0:T(8,128)(2,1)S(1)}, u32[]{:S(2)}, u32[]{:S(2)}) %collective-permute-start.15) | collective-permute-done | bytes 327712 | tf_op jit(solution)/shard_map/ppermute | solution.py:89
  161.8 10.9 %collective-permute-done.16 = bf16[160,2048]{1,0:T(8,128)(2,1)S(1)} collective-permute-done((bf16[160,2048]{1,0:T(8,128)(2,1)S(1)}, bf16[160,2048]{1,0:T(8,128)(2,1)S(1)}, u32[]{:S(2)}, u32[]{:S(2)}) %collective-permute-start.16) | collective-permute-done | bytes 655392 | tf_op jit(solution)/shard_map/ppermute | solution.py:93
  172.7 4.2 collective-permute-done.14
  177.9 2.7 collective-permute-start.17
  180.6 12.7 %collective-permute-done.18.n3 = bf16[160,2048]{1,0:T(8,128)(2,1)S(1)} collective-permute-done((bf16[160,2048]{1,0:T(8,128)(2,1)S(1)}, bf16[160,2048]{1,0:T(8,128)(2,1)S(1)}, u32[]{:S(2)}, u32[]{:S(2)}) %collective-permute-start.18) | collective-permute-done | bytes 655392 | tf_op jit(solution)/shard_map/ppermute | solution.py:70
  193.5 2.9 collective-permute-start.20
  196.4 4.5 collective-permute-done.19.n2a
  201.6 20.7 %ffn.1 = (bf16[640,2048]{1,0:T(8,128)(2,1)}, bf16[640,2048]{1,0:T(8,128)(2,1)}, bf16[640,1408]{1,0:T(8,128)(2,1)}, bf16[640,1536]{1,0:T(8,128)(2,1)}, bf16[640,1536]{1,0:T(8,128)(2,1)}) custom-call(s32[3]{0:T(128)} %pad_add_fusion.idx, bf16[160,2048]{1,0:T(8,128)(2,1)} %copy-done.21, bf16[160,2048]{1,0:T(8,128)(2,1)} %copy-done.33, ...), custom_call_target="tpu_custom_call" | custom-call | flops 11072962560 | bytes 34000000 | tf_op jit(solution)/shard_map/ffn/pallas_call | solution.py:431
  222.3 20.9 %ffn_grads.1 = bf16[2,16,2112,128]{3,2,1,0:T(8,128)(2,1)} custom-call(bf16[640,2048]{1,0:T(8,128)(2,1)} %get-tuple-element.106.na.nb, bf16[640,2048]{1,0:T(8,128)(2,1)} %get-tuple-element.106.na.nb, bf16[640,2048]{1,0:T(8,128)(2,1)} %get-tuple-element.107.cot, bf16[640,1408]{1,0:T(8,128)(2,1)} %get-tuple-element.80.hid, ...), custom_call_target="tpu_custom_call" | custom-call | flops 11072962560 | bytes 30000000 | tf_op jit(solution)/shard_map/ffn_grads/pallas_call | solution.py:520
  243.3 13.9 %ffn_back.1 = (bf16[160,2048]{1,0:T(8,128)(2,1)}, bf16[160,2048]{1,0:T(8,128)(2,1)}, bf16[80,2048]{1,0:T(8,128)(2,1)}, bf16[80,2048]{1,0:T(8,128)(2,1)}, bf16[160,2048]{1,0:T(8,128)(2,1)}) custom-call(bf16[640,1536]{1,0:T(8,128)(2,1)} %get-tuple-element.73.dgate, bf16[640,1536]{1,0:T(8,128)(2,1)} %get-tuple-element.74.dup, ...), custom_call_target="tpu_custom_call" | custom-call | flops 7381975040 | bytes 18000000 | tf_op jit(solution)/shard_map/ffn_back/pallas_call | solution.py:481
  263.7 3.1 collective-permute-start.25
  268.7 8.0 %collective-permute-done.25 = bf16[160,2048]{1,0:T(8,128)(2,1)S(1)} collective-permute-done((bf16[160,2048]{1,0:T(8,128)(2,1)S(1)}, bf16[160,2048]{1,0:T(8,128)(2,1)S(1)}, u32[]{:S(2)}, u32[]{:S(2)}) %collective-permute-start.25) | collective-permute-done | bytes 655392 | tf_op jit(solution)/shard_map/ppermute | solution.py:93
  276.8 4.9 collective-permute-done.23
  285.1 2.7 collective-permute-start.28
  287.7 76.2 %reduce-scatter.2.cloned.1.call-done = bf16[1,2112,128]{2,1,0:T(8,128)(2,1)} async-done(((bf16[32,2112,128]{2,1,0:T(8,128)(2,1)}), bf16[1,2112,128]{2,1,0:T(8,128)(2,1)}) %reduce-scatter.2.cloned.1.call-update) | async-done | bytes 540688 | tf_op jit(solution)/shard_map/reduce_scatter | solution.py:732
  368.5 9.8 %down_project.1 = (bf16[160,2048]{1,0:T(8,128)(2,1)}, bf16[160,2048]{1,0:T(8,128)(2,1)}, bf16[160,2048]{1,0:T(8,128)(2,1)}, bf16[160,2048]{1,0:T(8,128)(2,1)}) custom-call(s32[3]{0:T(128)} %pad_add_fusion.idx, bf16[640,1408]{1,0:T(8,128)(2,1)} %get-tuple-element.80.hid, bf16[704,2048]{1,0:T(8,128)(2,1)} %w0.5, bf16[352,2048]{1,0:T(8,128)(2,1)} %collective-permute-done.8.w1, ...), custom_call_target="tpu_custom_call" | custom-call | flops 3690987520 | bytes 11000000 | tf_op jit(solution)/shard_map/down_project/pallas_call | solution.py:462
  381.6 25.1 %attend_back.1 = (f32[640,512]{1,0:T(8,128)}, f32[640,128]{1,0:T(8,128)}, bf16[640,128]{1,0:T(8,128)(2,1)}) custom-call(s32[3]{0:T(128)} %pad_add_fusion.idx, bf16[640,512]{1,0:T(8,128)(2,1)} %get-tuple-element.60.q, bf16[640,128]{1,0:T(8,128)(2,1)} %get-tuple-element.61.kv_own, bf16[640,128]{1,0:T(8,128)(2,1)} %copy-done.49, s32[640,1]{1,0:T(8,128)} %reshape.220.first, ...), custom_call_target="tpu_custom_call" | custom-call | flops 30000001024 | bytes 8000000 | tf_op jit(solution)/shard_map/attend_back/pallas_call | solution.py:318
  406.7 2.8 collective-permute-start.33
  413.8 2.4 add_convert_fusion
  418.0 9.8 %qkv_back.1 = (bf16[640,640]{1,0:T(8,128)(2,1)}, bf16[640,2048]{1,0:T(8,128)(2,1)}, f32[1,2048]{1,0:T(1,128)}, bf16[160,2048]{1,0:T(8,128)(2,1)}, bf16[160,2048]...) custom-call(s32[3]{0:T(128)} %pad_add_fusion.idx, ...), custom_call_target="tpu_custom_call" | custom-call | flops 1677721600 | bytes 13000000 | tf_op jit(solution)/shard_map/qkv_back/pallas_call | solution.py:371
  427.8 10.4 %attn_grads.1 = bf16[8,2,1168,128]{3,2,1,0:T(8,128)(2,1)} custom-call(bf16[640,2048]{1,0:T(8,128)(2,1)} %get-tuple-element.100.na.nb, bf16[640,2048]{1,0:T(8,128)(2,1)} %get-tuple-element.100.na.nb, bf16[640,640]{1,0:T(8,128)(2,1)} %get-tuple-element.101.dm, bf16[640,512]{1,0:T(8,128)(2,1)} %bitcast.44, ...), custom_call_target="tpu_custom_call" | custom-call | flops 3019898880 | bytes 15000000 | tf_op jit(solution)/shard_map/attn_grads/pallas_call | solution.py:595
  440.0 4.1 collective-permute-start.38
  444.1 4.3 collective-permute-done.38
  448.5 3.0 fusion
  452.8 2.4 collective-permute-start.41
  459.9 8.7 %collective-permute-done.41 = bf16[2,1168,128]{2,1,0:T(8,128)(2,1)} collective-permute-done((bf16[2,1168,128]{2,1,0:T(8,128)(2,1)}, bf16[2,1168,128]{2,1,0:T(8,128)(2,1)}, u32[]{:S(2)}, u32[]{:S(2)}) %collective-permute-start.41) | collective-permute-done | bytes 598048 | tf_op jit(solution)/shard_map/ppermute | solution.py:653
  468.6 2.8 collective-permute-done.40
  471.4 13.2 %collective-permute-done.39 = bf16[2,1168,128]{2,1,0:T(8,128)(2,1)} collective-permute-done((bf16[2,1168,128]{2,1,0:T(8,128)(2,1)}, bf16[2,1168,128]{2,1,0:T(8,128)(2,1)}, u32[]{:S(2)}, u32[]{:S(2)}) %collective-permute-start.39) | collective-permute-done | bytes 598048 | tf_op jit(solution)/shard_map/ppermute | solution.py:653
  492.1 9.8 %collective-permute-done.44 = bf16[1168,128]{1,0:T(8,128)(2,1)S(1)} collective-permute-done((bf16[1168,128]{1,0:T(8,128)(2,1)S(1)}, bf16[1168,128]{1,0:T(8,128)(2,1)S(1)}, u32[]{:S(2)}, u32[]{:S(2)}) %collective-permute-start.44) | collective-permute-done | bytes 299040 | tf_op jit(solution)/shard_map/ppermute | solution.py:661
  504.4 4.7 collective-permute-done.47
  510.7 8.8 %collective-permute-done.45 = bf16[1168,128]{1,0:T(8,128)(2,1)S(1)} collective-permute-done((bf16[1168,128]{1,0:T(8,128)(2,1)S(1)}, bf16[1168,128]{1,0:T(8,128)(2,1)S(1)}, u32[]{:S(2)}, u32[]{:S(2)}) %collective-permute-start.45) | collective-permute-done | bytes 299040 | tf_op jit(solution)/shard_map/ppermute | solution.py:663
  524.4 16.1 %collective-permute-done.35 = bf16[160,2048]{1,0:T(8,128)(2,1)S(1)} collective-permute-done((bf16[160,2048]{1,0:T(8,128)(2,1)}, bf16[160,2048]{1,0:T(8,128)(2,1)S(1)}, u32[]{:S(2)}, u32[]{:S(2)}) %collective-permute-start.35) | collective-permute-done | bytes 655392 | tf_op jit(solution)/shard_map/ppermute | solution.py:92
  546.3 3.5 bitcast_select_fusion.piece
  549.8 6.3 %unpack_tail.1 = (f32[1024,640]{1,0:T(8,128)}, f32[256,2048]{1,0:T(8,128)}, f32[2,2048]{1,0:T(2,128)}) custom-call(bf16[8,1168,128]{2,1,0:T(8,128)(2,1)} %bitcast_select_fusion.piece), custom_call_target="tpu_custom_call" | custom-call | flops 1000000 | bytes 7000000 | tf_op jit(solution)/shard_map/unpack_tail/pallas_call | solution.py:629
  562.8 13.5 %unpack.1 = (f32[1024,1408]{1,0:T(8,128)}, f32[1024,1408]{1,0:T(8,128)}, f32[704,2048]{1,0:T(8,128)}) custom-call(bf16[16,2112,128]{2,1,0:T(8,128)(2,1)} %all-gather.5.cloned.1.call-done.piece), custom_call_target="tpu_custom_call" | custom-call | flops 1000000 | bytes 26000000 | tf_op jit(solution)/shard_map/unpack/pallas_call | solution.py:549
  (256 shorter events, 91.3 us)
Async XLA Ops:
  7.2 194.4 %all-gather.3.cloned.1.call-start = ((), (), s32[]{:S(2)}) async-start(), calls=%async_computation.1 | async-start | bytes 13369344 | tf_op jit(solution)/shard_map/all_gather | solution.py:708
  9.4 354.6 %reduce-scatter.2.cloned.1.call-start = ((), (), s32[]{:S(2)}) async-start(), calls=%async_computation.2 | async-start | bytes 17842176 | tf_op jit(solution)/shard_map/reduce_scatter | solution.py:732
  10.9 21.3 %collective-permute-start.4 = (bf16[512,640]{1,0:T(8,128)(2,1)}, bf16[512,640]{1,0:T(8,128)(2,1)S(1)}, u32[]{:S(2)}, u32[]{:S(2)}) collective-permute-start(bf16[512,640]{1,0:T(8,128)(2,1)} %constant_dynamic-slice_fusion.5), channel_id=1, source_target_pairs={{0,1},{1,0},{2,3},{3,2},{4,5},{5,4},{6,7},{7,6},{8,9},{9,8},{10,11... | collective-permute-start | bytes 1966088 | tf_op jit(solution)/shard_map/ppermute | solution.py:120
  15.8 30.4 %collective-permute-start = (bf16[160,2048]{1,0:T(8,128)(2,1)S(1)}, bf16[160,2048]{1,0:T(8,128)(2,1)S(1)}, u32[]{:S(2)}, u32[]{:S(2)}) collective-permute-start(bf16[160,2048]{1,0:T(8,128)(2,1)S(1)} %fusion.5.n0), channel_id=1, source_target_pairs={{0,6},{2,0},{4,2},{6,4},{1,7},{3,1},{5,3},{7,5},{8,14},{10,8},{12,... | collective-permute-start | bytes 1966088 | tf_op jit(solution)/shard_map/ppermute | solution.py:71
  18.3 26.7 %collective-permute-start.1 = (bf16[160,2048]{1,0:T(8,128)(2,1)S(1)}, bf16[160,2048]{1,0:T(8,128)(2,1)S(1)}, u32[]{:S(2)}, u32[]{:S(2)}) collective-permute-start(bf16[160,2048]{1,0:T(8,128)(2,1)S(1)} %fusion.5.n0), channel_id=1, source_target_pairs={{0,2},{2,4},{4,6},{6,0},{1,3},{3,5},{5,7},{7,1},{8,10},{10,12},{12... | collective-permute-start | bytes 1966088 | tf_op jit(solution)/shard_map/ppermute | solution.py:70
  34.3 14.2 %collective-permute-start.7 = (bf16[128,2048]{1,0:T(8,128)(2,1)}, bf16[128,2048]{1,0:T(8,128)(2,1)}, u32[]{:S(2)}, u32[]{:S(2)}) collective-permute-start(bf16[128,2048]{1,0:T(8,128)(2,1)} %constant_dynamic-slice_fusion.3), channel_id=1, source_target_pairs={{0,1},{1,0},{2,3},{3,2},{4,5},{5,4},{6,7},{7,6},{8,9},{9,8},{10,11... | collective-permute-start | bytes 1572872 | tf_op jit(solution)/shard_map/ppermute | solution.py:120
  38.7 17.0 %collective-permute-start.5 = (bf16[512,640]{1,0:T(8,128)(2,1)S(1)}, bf16[512,640]{1,0:T(8,128)(2,1)}, u32[]{:S(2)}, u32[]{:S(2)}) collective-permute-start(bf16[512,640]{1,0:T(8,128)(2,1)S(1)} %collective-permute-done.4.w1), channel_id=1, source_target_pairs={{0,8},{8,0},{1,9},{9,1},{2,10},{10,2},{3,11},{11,3},{4,12},{12,4},... | collective-permute-start | bytes 1966088 | tf_op jit(solution)/shard_map/ppermute | solution.py:121
  45.1 10.6 %collective-permute-start.2 = (bf16[80,2048]{1,0:T(8,128)(2,1)S(1)}, bf16[80,2048]{1,0:T(8,128)(2,1)S(1)}, u32[]{:S(2)}, u32[]{:S(2)}) collective-permute-start(bf16[80,2048]{1,0:T(8,128)(2,1)S(1)} %slice.82), channel_id=1, source_target_pairs={{0,2},{2,4},{4,6},{6,0},{1,3},{3,5},{5,7},{7,1},{8,10},{10,12},{12... | collective-permute-start | bytes 983048 | tf_op jit(solution)/shard_map/ppermute | solution.py:72
  46.2 9.5 %collective-permute-start.3 = (bf16[80,2048]{1,0:T(8,128)(2,1)S(1)}, bf16[80,2048]{1,0:T(8,128)(2,1)S(1)}, u32[]{:S(2)}, u32[]{:S(2)}) collective-permute-start(bf16[80,2048]{1,0:T(8,128)(2,1)S(1)} %slice.83), channel_id=1, source_target_pairs={{0,6},{2,0},{4,2},{6,4},{1,7},{3,1},{5,3},{7,5},{8,14},{10,8},{12,... | collective-permute-start | bytes 983048 | tf_op jit(solution)/shard_map/ppermute | solution.py:73
  51.2 90.3 %collective-permute-start.8 = (bf16[352,2048]{1,0:T(8,128)(2,1)}, bf16[352,2048]{1,0:T(8,128)(2,1)}, u32[]{:S(2)}, u32[]{:S(2)}) collective-permute-start(bf16[352,2048]{1,0:T(8,128)(2,1)} %constant_dynamic-slice_fusion.2), channel_id=1, source_target_pairs={{0,1},{1,0},{2,3},{3,2},{4,5},{5,4},{6,7},{7,6},{8,9},{9,8},{10,11... | collective-permute-start | bytes 4325384 | tf_op jit(solution)/shard_map/ppermute | solution.py:120
  63.8 49.8 %collective-permute-start.6 = (bf16[640,128]{1,0:T(8,128)(2,1)}, bf16[640,128]{1,0:T(8,128)(2,1)S(1)}, u32[]{:S(2)}, u32[]{:S(2)}) collective-permute-start(bf16[640,128]{1,0:T(8,128)(2,1)} %get-tuple-element.61.kv_own), channel_id=1, source_target_pairs={{0,1},{1,0},{2,3},{3,2},{4,5},{5,4},{6,7},{7,6},{8,9},{9,8},{10,11... | collective-permute-start | bytes 491528 | tf_op jit(solution)/shard_map/ppermute | solution.py:723
  64.8 76.6 %collective-permute-start.9 = (bf16[160,2048]{1,0:T(8,128)(2,1)S(1)}, bf16[160,2048]{1,0:T(8,128)(2,1)S(1)}, u32[]{:S(2)}, u32[]{:S(2)}) collective-permute-start(bf16[160,2048]{1,0:T(8,128)(2,1)S(1)} %copy-done.18), channel_id=1, source_target_pairs={{0,6},{2,0},{4,2},{6,4},{1,7},{3,1},{5,3},{7,5},{8,14},{10,8},{12,... | collective-permute-start | bytes 1966088 | tf_op jit(solution)/shard_map/ppermute | solution.py:78
  67.3 74.2 %collective-permute-start.10 = (bf16[160,2048]{1,0:T(8,128)(2,1)S(1)}, bf16[160,2048]{1,0:T(8,128)(2,1)S(1)}, u32[]{:S(2)}, u32[]{:S(2)}) collective-permute-start(bf16[160,2048]{1,0:T(8,128)(2,1)S(1)} %copy-done.18), channel_id=1, source_target_pairs={{0,4},{2,6},{4,0},{6,2},{1,5},{3,7},{5,1},{7,3},{8,12},{10,14},{12... | collective-permute-start | bytes 1966088 | tf_op jit(solution)/shard_map/ppermute | solution.py:78
  67.8 73.6 %collective-permute-start.11 = (bf16[160,2048]{1,0:T(8,128)(2,1)S(1)}, bf16[160,2048]{1,0:T(8,128)(2,1)S(1)}, u32[]{:S(2)}, u32[]{:S(2)}) collective-permute-start(bf16[160,2048]{1,0:T(8,128)(2,1)S(1)} %copy-done.18), channel_id=1, source_target_pairs={{0,2},{2,4},{4,6},{6,0},{1,3},{3,5},{5,7},{7,1},{8,10},{10,12},{12... | collective-permute-start | bytes 1966088 | tf_op jit(solution)/shard_map/ppermute | solution.py:78
  113.7 27.8 %collective-permute-start.12 = (bf16[128,2048]{1,0:T(8,128)(2,1)}, bf16[128,2048]{1,0:T(8,128)(2,1)S(1)}, u32[]{:S(2)}, u32[]{:S(2)}) collective-permute-start(bf16[128,2048]{1,0:T(8,128)(2,1)} %collective-permute-done.7.w1), channel_id=1, source_target_pairs={{0,8},{8,0},{1,9},{9,1},{2,10},{10,2},{3,11},{11,3},{4,12},{12,4},... | collective-permute-start | bytes 1572872 | tf_op jit(solution)/shard_map/ppermute | solution.py:121
  147.1 9.7 %collective-permute-start.15 = (bf16[80,2048]{1,0:T(8,128)(2,1)}, bf16[80,2048]{1,0:T(8,128)(2,1)S(1)}, u32[]{:S(2)}, u32[]{:S(2)}) collective-permute-start(bf16[80,2048]{1,0:T(8,128)(2,1)} %get-tuple-element.71), channel_id=1, source_target_pairs={{0,6},{2,0},{4,2},{6,4},{1,7},{3,1},{5,3},{7,5},{8,14},{10,8},{12,... | collective-permute-start | bytes 983048 | tf_op jit(solution)/shard_map/ppermute | solution.py:89
  150.1 10.3 %collective-permute-start.13 = (bf16[80,2048]{1,0:T(8,128)(2,1)S(1)}, bf16[80,2048]{1,0:T(8,128)(2,1)S(1)}, u32[]{:S(2)}, u32[]{:S(2)}) collective-permute-start(bf16[80,2048]{1,0:T(8,128)(2,1)S(1)} %copy-done.48), channel_id=1, source_target_pairs={{0,2},{2,4},{4,6},{6,0},{1,3},{3,5},{5,7},{7,1},{8,10},{10,12},{12... | collective-permute-start | bytes 983048 | tf_op jit(solution)/shard_map/ppermute | solution.py:88
  157.1 15.7 %collective-permute-start.16 = (bf16[160,2048]{1,0:T(8,128)(2,1)S(1)}, bf16[160,2048]{1,0:T(8,128)(2,1)S(1)}, u32[]{:S(2)}, u32[]{:S(2)}) collective-permute-start(bf16[160,2048]{1,0:T(8,128)(2,1)S(1)} %pad_maximum_fusion.2), channel_id=1, source_target_pairs={{0,6},{2,0},{4,2},{6,4},{1,7},{3,1},{5,3},{7,5},{8,14},{10,8},{12,... | collective-permute-start | bytes 1966088 | tf_op jit(solution)/shard_map/ppermute | solution.py:93
  160.6 16.4 %collective-permute-start.14 = (bf16[160,2048]{1,0:T(8,128)(2,1)S(1)}, bf16[160,2048]{1,0:T(8,128)(2,1)S(1)}, u32[]{:S(2)}, u32[]{:S(2)}) collective-permute-start(bf16[160,2048]{1,0:T(8,128)(2,1)S(1)} %pad_maximum_fusion.1), channel_id=1, source_target_pairs={{0,2},{2,4},{4,6},{6,0},{1,3},{3,5},{5,7},{7,1},{8,10},{10,12},{12... | collective-permute-start | bytes 1966088 | tf_op jit(solution)/shard_map/ppermute | solution.py:92
  160.6 35.7 %collective-permute-start.21 = (bf16[352,2048]{1,0:T(8,128)(2,1)}, bf16[352,2048]{1,0:T(8,128)(2,1)S(1)}, u32[]{:S(2)}, u32[]{:S(2)}) collective-permute-start(bf16[352,2048]{1,0:T(8,128)(2,1)} %collective-permute-done.8.w1), channel_id=1, source_target_pairs={{0,8},{8,0},{1,9},{9,1},{2,10},{10,2},{3,11},{11,3},{4,12},{12,4},... | collective-permute-start | bytes 4325384 | tf_op jit(solution)/shard_map/ppermute | solution.py:121
  177.8 15.5 %collective-permute-start.18 = (bf16[160,2048]{1,0:T(8,128)(2,1)S(1)}, bf16[160,2048]{1,0:T(8,128)(2,1)S(1)}, u32[]{:S(2)}, u32[]{:S(2)}) collective-permute-start(bf16[160,2048]{1,0:T(8,128)(2,1)S(1)} %multiply_convert_fusion.n0), channel_id=1, source_target_pairs={{0,2},{2,4},{4,6},{6,0},{1,3},{3,5},{5,7},{7,1},{8,10},{10,12},{12... | collective-permute-start | bytes 1966088 | tf_op jit(solution)/shard_map/ppermute | solution.py:70
  177.9 15.5 %collective-permute-start.17 = (bf16[160,2048]{1,0:T(8,128)(2,1)S(1)}, bf16[160,2048]{1,0:T(8,128)(2,1)S(1)}, u32[]{:S(2)}, u32[]{:S(2)}) collective-permute-start(bf16[160,2048]{1,0:T(8,128)(2,1)S(1)} %multiply_convert_fusion.n0), channel_id=1, source_target_pairs={{0,6},{2,0},{4,2},{6,4},{1,7},{3,1},{5,3},{7,5},{8,14},{10,8},{12,... | collective-permute-start | bytes 1966088 | tf_op jit(solution)/shard_map/ppermute | solution.py:71
  193.5 8.1 %collective-permute-start.20 = (bf16[80,2048]{1,0:T(8,128)(2,1)S(1)}, bf16[80,2048]{1,0:T(8,128)(2,1)}, u32[]{:S(2)}, u32[]{:S(2)}) collective-permute-start(bf16[80,2048]{1,0:T(8,128)(2,1)S(1)} %slice.85), channel_id=1, source_target_pairs={{0,6},{2,0},{4,2},{6,4},{1,7},{3,1},{5,3},{7,5},{8,14},{10,8},{12,... | collective-permute-start | bytes 983048 | tf_op jit(solution)/shard_map/ppermute | solution.py:73
  243.2 319.5 %all-gather.5.cloned.1.call-start = ((), (), s32[]{:S(2)}) async-start(), calls=%async_computation.3 | async-start | bytes 9191424 | tf_op jit(solution)/shard_map/all_gather | solution.py:735
  263.7 13.0 %collective-permute-start.25 = (bf16[160,2048]{1,0:T(8,128)(2,1)S(1)}, bf16[160,2048]{1,0:T(8,128)(2,1)S(1)}, u32[]{:S(2)}, u32[]{:S(2)}) collective-permute-start(bf16[160,2048]{1,0:T(8,128)(2,1)S(1)} %pad_maximum_fusion.4), channel_id=1, source_target_pairs={{0,6},{2,0},{4,2},{6,4},{1,7},{3,1},{5,3},{7,5},{8,14},{10,8},{12,... | collective-permute-start | bytes 1966088 | tf_op jit(solution)/shard_map/ppermute | solution.py:93
  268.7 13.0 %collective-permute-start.23 = (bf16[160,2048]{1,0:T(8,128)(2,1)S(1)}, bf16[160,2048]{1,0:T(8,128)(2,1)S(1)}, u32[]{:S(2)}, u32[]{:S(2)}) collective-permute-start(bf16[160,2048]{1,0:T(8,128)(2,1)S(1)} %pad_maximum_fusion.3), channel_id=1, source_target_pairs={{0,2},{2,4},{4,6},{6,0},{1,3},{3,5},{5,7},{7,1},{8,10},{10,12},{12... | collective-permute-start | bytes 1966088 | tf_op jit(solution)/shard_map/ppermute | solution.py:92
  285.1 78.9 %collective-permute-start.26 = (bf16[160,2048]{1,0:T(8,128)(2,1)}, bf16[160,2048]{1,0:T(8,128)(2,1)S(1)}, u32[]{:S(2)}, u32[]{:S(2)}) collective-permute-start(bf16[160,2048]{1,0:T(8,128)(2,1)} %get-tuple-element.114.b0), channel_id=1, source_target_pairs={{0,2},{2,4},{4,6},{6,0},{1,3},{3,5},{5,7},{7,1},{8,10},{10,12},{12... | collective-permute-start | bytes 1966088 | tf_op jit(solution)/shard_map/ppermute | solution.py:70
  285.1 81.0 %collective-permute-start.28 = (bf16[160,2048]{1,0:T(8,128)(2,1)}, bf16[160,2048]{1,0:T(8,128)(2,1)S(1)}, u32[]{:S(2)}, u32[]{:S(2)}) collective-permute-start(bf16[160,2048]{1,0:T(8,128)(2,1)} %get-tuple-element.114.b0), channel_id=1, source_target_pairs={{0,6},{2,0},{4,2},{6,4},{1,7},{3,1},{5,3},{7,5},{8,14},{10,8},{12,... | collective-permute-start | bytes 1966088 | tf_op jit(solution)/shard_map/ppermute | solution.py:71
  364.8 14.3 %collective-permute-start.27 = (bf16[80,2048]{1,0:T(8,128)(2,1)}, bf16[80,2048]{1,0:T(8,128)(2,1)S(1)}, u32[]{:S(2)}, u32[]{:S(2)}) collective-permute-start(bf16[80,2048]{1,0:T(8,128)(2,1)} %slice.86), channel_id=1, source_target_pairs={{0,2},{2,4},{4,6},{6,0},{1,3},{3,5},{5,7},{7,1},{8,10},{10,12},{12... | collective-permute-start | bytes 983048 | tf_op jit(solution)/shard_map/ppermute | solution.py:72
  366.9 12.2 %collective-permute-start.29 = (bf16[80,2048]{1,0:T(8,128)(2,1)}, bf16[80,2048]{1,0:T(8,128)(2,1)}, u32[]{:S(2)}, u32[]{:S(2)}) collective-permute-start(bf16[80,2048]{1,0:T(8,128)(2,1)} %slice.87), channel_id=1, source_target_pairs={{0,6},{2,0},{4,2},{6,4},{1,7},{3,1},{5,3},{7,5},{8,14},{10,8},{12,... | collective-permute-start | bytes 983048 | tf_op jit(solution)/shard_map/ppermute | solution.py:73
  379.1 34.6 %collective-permute-start.32 = (bf16[160,2048]{1,0:T(8,128)(2,1)}, bf16[160,2048]{1,0:T(8,128)(2,1)S(1)}, u32[]{:S(2)}, u32[]{:S(2)}) collective-permute-start(bf16[160,2048]{1,0:T(8,128)(2,1)} %get-tuple-element.88), channel_id=1, source_target_pairs={{0,6},{2,0},{4,2},{6,4},{1,7},{3,1},{5,3},{7,5},{8,14},{10,8},{12,... | collective-permute-start | bytes 1966088 | tf_op jit(solution)/shard_map/ppermute | solution.py:82
  380.5 33.3 %collective-permute-start.31 = (bf16[160,2048]{1,0:T(8,128)(2,1)}, bf16[160,2048]{1,0:T(8,128)(2,1)S(1)}, u32[]{:S(2)}, u32[]{:S(2)}) collective-permute-start(bf16[160,2048]{1,0:T(8,128)(2,1)} %get-tuple-element.86), channel_id=1, source_target_pairs={{0,4},{2,6},{4,0},{6,2},{1,5},{3,7},{5,1},{7,3},{8,12},{10,14},{12... | collective-permute-start | bytes 1966088 | tf_op jit(solution)/shard_map/ppermute | solution.py:82
  381.1 32.7 %collective-permute-start.30 = (bf16[160,2048]{1,0:T(8,128)(2,1)}, bf16[160,2048]{1,0:T(8,128)(2,1)}, u32[]{:S(2)}, u32[]{:S(2)}) collective-permute-start(bf16[160,2048]{1,0:T(8,128)(2,1)} %get-tuple-element.84), channel_id=1, source_target_pairs={{0,2},{2,4},{4,6},{6,0},{1,3},{3,5},{5,7},{7,1},{8,10},{10,12},{12... | collective-permute-start | bytes 1966088 | tf_op jit(solution)/shard_map/ppermute | solution.py:82
  406.7 10.7 %collective-permute-start.33 = (bf16[640,128]{1,0:T(8,128)(2,1)}, bf16[640,128]{1,0:T(8,128)(2,1)S(1)}, u32[]{:S(2)}, u32[]{:S(2)}) collective-permute-start(bf16[640,128]{1,0:T(8,128)(2,1)} %get-tuple-element.94), channel_id=1, source_target_pairs={{0,1},{1,0},{2,3},{3,2},{4,5},{5,4},{6,7},{7,6},{8,9},{9,8},{10,11... | collective-permute-start | bytes 491528 | tf_op jit(solution)/shard_map/ppermute | solution.py:747
  440.0 8.4 %collective-permute-start.38 = (bf16[4,2,1168,128]{3,2,1,0:T(8,128)(2,1)S(1)}, bf16[4,2,1168,128]{3,2,1,0:T(8,128)(2,1)}, u32[]{:S(2)}, u32[]{:S(2)}) collective-permute-start(bf16[4,2,1168,128]{3,2,1,0:T(8,128)(2,1)S(1)} %dynamic-slice_bitcast_fusion), channel_id=1, source_target_pairs={{0,8},{8,0},{1,9},{9,1},{2,10},{10,2},{3,11},{11,3},{4,12},{12,4},... | collective-permute-start | bytes 7176200 | tf_op jit(solution)/shard_map/ppermute | solution.py:652
  452.8 15.9 %collective-permute-start.41 = (bf16[2,1168,128]{2,1,0:T(8,128)(2,1)}, bf16[2,1168,128]{2,1,0:T(8,128)(2,1)}, u32[]{:S(2)}, u32[]{:S(2)}) collective-permute-start(bf16[2,1168,128]{2,1,0:T(8,128)(2,1)} %get-tuple-element.121), channel_id=1, source_target_pairs={{0,96},{32,0},{64,32},{96,64},{1,97},{33,1},{65,33},{97,65},{2,98}... | collective-permute-start | bytes 1794056 | tf_op jit(solution)/shard_map/ppermute | solution.py:653
  455.1 16.3 %collective-permute-start.40 = (bf16[2,1168,128]{2,1,0:T(8,128)(2,1)}, bf16[2,1168,128]{2,1,0:T(8,128)(2,1)}, u32[]{:S(2)}, u32[]{:S(2)}) collective-permute-start(bf16[2,1168,128]{2,1,0:T(8,128)(2,1)} %get-tuple-element.122), channel_id=1, source_target_pairs={{0,64},{32,96},{64,0},{96,32},{1,65},{33,97},{65,1},{97,33},{2,66}... | collective-permute-start | bytes 1794056 | tf_op jit(solution)/shard_map/ppermute | solution.py:653
  455.1 29.5 %collective-permute-start.39 = (bf16[2,1168,128]{2,1,0:T(8,128)(2,1)}, bf16[2,1168,128]{2,1,0:T(8,128)(2,1)}, u32[]{:S(2)}, u32[]{:S(2)}) collective-permute-start(bf16[2,1168,128]{2,1,0:T(8,128)(2,1)} %get-tuple-element.120), channel_id=1, source_target_pairs={{0,32},{32,64},{64,96},{96,0},{1,33},{33,65},{65,97},{97,1},{2,34}... | collective-permute-start | bytes 1794056 | tf_op jit(solution)/shard_map/ppermute | solution.py:653
  455.7 34.1 %collective-permute-start.36 = (bf16[80,2048]{1,0:T(8,128)(2,1)}, bf16[80,2048]{1,0:T(8,128)(2,1)S(1)}, u32[]{:S(2)}, u32[]{:S(2)}) collective-permute-start(bf16[80,2048]{1,0:T(8,128)(2,1)} %get-tuple-element.99), channel_id=1, source_target_pairs={{0,6},{2,0},{4,2},{6,4},{1,7},{3,1},{5,3},{7,5},{8,14},{10,8},{12,... | collective-permute-start | bytes 983048 | tf_op jit(solution)/shard_map/ppermute | solution.py:89
  459.8 44.5 %collective-permute-start.34 = (bf16[80,2048]{1,0:T(8,128)(2,1)}, bf16[80,2048]{1,0:T(8,128)(2,1)S(1)}, u32[]{:S(2)}, u32[]{:S(2)}) collective-permute-start(bf16[80,2048]{1,0:T(8,128)(2,1)} %get-tuple-element.97), channel_id=1, source_target_pairs={{0,2},{2,4},{4,6},{6,0},{1,3},{3,5},{5,7},{7,1},{8,10},{10,12},{12... | collective-permute-start | bytes 983048 | tf_op jit(solution)/shard_map/ppermute | solution.py:88
  486.4 15.5 %collective-permute-start.44 = (bf16[1168,128]{1,0:T(8,128)(2,1)S(1)}, bf16[1168,128]{1,0:T(8,128)(2,1)S(1)}, u32[]{:S(2)}, u32[]{:S(2)}) collective-permute-start(bf16[1168,128]{1,0:T(8,128)(2,1)S(1)} %get-tuple-element.126), channel_id=1, source_target_pairs={{0,17},{1,16},{16,1},{17,0},{2,19},{3,18},{18,3},{19,2},{4,21},{5,... | collective-permute-start | bytes 897032 | tf_op jit(solution)/shard_map/ppermute | solution.py:661
  487.5 14.4 %collective-permute-start.43 = (bf16[1168,128]{1,0:T(8,128)(2,1)S(1)}, bf16[1168,128]{1,0:T(8,128)(2,1)S(1)}, u32[]{:S(2)}, u32[]{:S(2)}) collective-permute-start(bf16[1168,128]{1,0:T(8,128)(2,1)S(1)} %get-tuple-element.126), channel_id=1, source_target_pairs={{0,1},{1,0},{2,3},{3,2},{4,5},{5,4},{6,7},{7,6},{8,9},{9,8},{10,11... | collective-permute-start | bytes 897032 | tf_op jit(solution)/shard_map/ppermute | solution.py:660
  488.4 13.9 %collective-permute-start.42 = (bf16[1168,128]{1,0:T(8,128)(2,1)S(1)}, bf16[1168,128]{1,0:T(8,128)(2,1)S(1)}, u32[]{:S(2)}, u32[]{:S(2)}) collective-permute-start(bf16[1168,128]{1,0:T(8,128)(2,1)S(1)} %get-tuple-element.125), channel_id=1, source_target_pairs={{0,16},{16,0},{1,17},{17,1},{2,18},{18,2},{3,19},{19,3},{4,20},{20... | collective-permute-start | bytes 897032 | tf_op jit(solution)/shard_map/ppermute | solution.py:659
  489.9 34.5 %collective-permute-start.37 = (bf16[160,2048]{1,0:T(8,128)(2,1)S(1)}, bf16[160,2048]{1,0:T(8,128)(2,1)S(1)}, u32[]{:S(2)}, u32[]{:S(2)}) collective-permute-start(bf16[160,2048]{1,0:T(8,128)(2,1)S(1)} %pad_maximum_fusion.6), channel_id=1, source_target_pairs={{0,6},{2,0},{4,2},{6,4},{1,7},{3,1},{5,3},{7,5},{8,14},{10,8},{12,... | collective-permute-start | bytes 1966088 | tf_op jit(solution)/shard_map/ppermute | solution.py:93
  502.6 8.2 %collective-permute-start.46 = (bf16[1168,128]{1,0:T(8,128)(2,1)S(1)}, bf16[1168,128]{1,0:T(8,128)(2,1)S(1)}, u32[]{:S(2)}, u32[]{:S(2)}) collective-permute-start(bf16[1168,128]{1,0:T(8,128)(2,1)S(1)} %add_convert_fusion.7), channel_id=1, source_target_pairs={{0,64},{32,96},{64,0},{96,32},{1,65},{33,97},{65,1},{97,33},{2,66}... | collective-permute-start | bytes 897032 | tf_op jit(solution)/shard_map/ppermute | solution.py:663
  503.6 16.0 %collective-permute-start.45 = (bf16[1168,128]{1,0:T(8,128)(2,1)S(1)}, bf16[1168,128]{1,0:T(8,128)(2,1)S(1)}, u32[]{:S(2)}, u32[]{:S(2)}) collective-permute-start(bf16[1168,128]{1,0:T(8,128)(2,1)S(1)} %add_convert_fusion.7), channel_id=1, source_target_pairs={{0,32},{32,64},{64,96},{96,0},{1,33},{33,65},{65,97},{97,1},{2,34}... | collective-permute-start | bytes 897032 | tf_op jit(solution)/shard_map/ppermute | solution.py:663
  521.2 20.1 %collective-permute-start.48 = (bf16[4,1168,128]{2,1,0:T(8,128)(2,1)}, bf16[4,1168,128]{2,1,0:T(8,128)(2,1)}, u32[]{:S(2)}, u32[]{:S(2)}) collective-permute-start(bf16[4,1168,128]{2,1,0:T(8,128)(2,1)} %get-tuple-element.124), channel_id=1, source_target_pairs={{0,8},{8,0},{1,9},{9,1},{2,10},{10,2},{3,11},{11,3},{4,12},{12,4},... | collective-permute-start | bytes 3588104 | tf_op jit(solution)/shard_map/ppermute | solution.py:664
  522.6 17.9 %collective-permute-start.35 = (bf16[160,2048]{1,0:T(8,128)(2,1)}, bf16[160,2048]{1,0:T(8,128)(2,1)S(1)}, u32[]{:S(2)}, u32[]{:S(2)}) collective-permute-start(bf16[160,2048]{1,0:T(8,128)(2,1)} %pad_maximum_fusion.5), channel_id=1, source_target_pairs={{0,2},{2,4},{4,6},{6,0},{1,3},{3,5},{5,7},{7,1},{8,10},{10,12},{12... | collective-permute-start | bytes 1966088 | tf_op jit(solution)/shard_map/ppermute | solution.py:92
  (57 other events, 451.0 us)
Sparse Core Ops, SparseCore 0:
  11.0 129.5 all-gather.2
  243.4 120.5 reduce-scatter.1
  365.7 57.7 all-gather.4

commit v3 on v2

--- a/solution.py
+++ b/solution.py
@@ -66,12 +66,13 @@
     return [(i, (i + s) % n) for i in range(n)]
 
 
-def gather_x(v):
+def gather_x(v, *deps):
     from_prev = lax.ppermute(v, "x", shift(4, 1))
     from_next = lax.ppermute(v, "x", shift(4, -1))
-    opp_a = lax.ppermute(from_prev[:HALF], "x", shift(4, 1))
-    opp_b = lax.ppermute(from_next[HALF:], "x", shift(4, -1))
-    return v, from_next, opp_a, opp_b, from_prev
+    send_a, send_b = tie(from_prev[:HALF], *deps), tie(from_next[HALF:], *deps)
+    opp_a = lax.ppermute(send_a, "x", shift(4, 1))
+    opp_b = lax.ppermute(send_b, "x", shift(4, -1))
+    return (v, from_next, opp_a, opp_b, from_prev), (send_a, send_b)
 
 
 def gather_direct(v):
@@ -115,14 +116,18 @@
     return pl.ds(pl.multiple_of(block * BLK, 32), BLK)
 
 
-def fetch_partner(w, core):
+def fetch_half(w, core):
     half = w.shape[0] // 2
-    got = lax.ppermute(lax.dynamic_slice_in_dim(w, core * half, half, 0), "zh", shift(2, 1))
+    return lax.ppermute(lax.dynamic_slice_in_dim(w, core * half, half, 0), "zh", shift(2, 1))
+
+
+def fetch_partner(w, core, *deps):
+    got = fetch_half(tie(w, *deps), core)
     return w, got, lax.ppermute(got, "core", shift(2, 1))
 
 
 def weight_rows(idx, rows):
-    zh, core = idx[1], idx[2]
+    zh, core = idx[1], idx[3]
     far = (1 - zh) * rows
     half = rows // 2
     at = lambda first, n: pl.ds(pl.multiple_of(first, half), n)
@@ -257,7 +262,7 @@
 
 
 def attend_back_body(
-    idx, q, kv_own, kv_par, first, lse_ref, att, b0, b1, b2a, b2b, b3, w0, w1, w2,
+    idx, q, kv_own, kv_par, first, lse_ref, att, cosine, sine, b0, b1, b2a, b2b, b3, w0, w1, w2,
     dq_ref, dkv_own, dkv_par, kk, vv, bias, dout, dkk, dvv,
 ):
     x, zh = idx[0], idx[1]
@@ -302,7 +307,9 @@
             dvv[0:n, :] += t_dot(e.astype(BF16), do2)
             dkk[0:n, :] += t_dot(ds, q2)
             dq = dot(ds, kk[0:n, :]) * HD**-0.5
-            dq_ref[j * BLK : (j + 1) * BLK, cols] = jnp.where(lo, dq[:BLK], dq[BLK:])
+            v = jnp.where(lo, dq[:BLK], dq[BLK:])
+            here = slice(j * BLK, (j + 1) * BLK)
+            dq_ref[rel, :, cols] = (v * cosine[here, :] - swap_halves(v) * sine[here, :]).astype(BF16)
             return carry
 
         lax.fori_loop(0, 4, pair, 0)
@@ -314,11 +321,11 @@
             dst[j * BLK : (j + 1) * BLK, :] = both.astype(dst.dtype)
 
 
-def attend_back(idx, q, kv_own, kv_par, first, lse, att, branch, weight):
+def attend_back(idx, q, kv_own, kv_par, first, lse, att, cosine, sine, branch, weight):
     return pl.pallas_call(
         attend_back_body,
-        out_shape=(sds((ROWS, AW), F32), sds((ROWS, 128), F32), sds((ROWS, 128))),
-        in_specs=[spec(pltpu.SMEM)] + [spec()] * 14,
+        out_shape=(sds((4, BLK, AW)), sds((ROWS, 128), F32), sds((ROWS, 128))),
+        in_specs=[spec(pltpu.SMEM)] + [spec()] * 16,
         out_specs=(spec(),) * 3,
         scratch_shapes=[
             pltpu.VMEM((CAP, 128), BF16),
@@ -331,14 +338,14 @@
         compiler_params=params(),
         cost_estimate=cost(3e10, 8e6),
         name="attend_back",
-    )(idx, q, kv_own, kv_par, first, lse, att, *branch, *weight)
+    )(idx, q, kv_own, kv_par, first, lse, att, cosine, sine, *branch, *weight)
 
 
 def qkv_back_body(
-    idx, dq, dkv_own, dkv_got, cosine, sine, w0, w1, w2, n0, n1, n2a, n2b, n3, gain,
-    dm_ref, n_all, gain_ref, o0, o1, o2a, o2b, o3, out,
+    idx, dqm, dkv_own, dkv_got, cosine, sine, w0, w1, w2, n0, n1, n2a, n2b, n3, gain_one, gain_grad_two,
+    mine, theirs, o0, o1, o2a, o2b, o3, n_all, dkv, out, grad, gains,
 ):
-    x = idx[0]
+    x, y, core = idx[0], idx[2], idx[3]
     lo = low_lanes((BLK, 128))
     for ref, row, (_, n) in zip((n0, n1, n2a, n2b, n3), PIECE_ROW, PIECES):
         n_all[row : row + n, :] = ref[...]
@@ -346,43 +353,58 @@
     total = jnp.zeros((8, D), F32)
     for d, ref in ((2, None), (1, o1), (3, o3), (0, o0)):
         at = rows_at((x + d) & 3)
-        cs = cosine[at, :]
-        sn = sine[at, :]
-        mine = pl.ds(d * BLK, BLK)
-        for p in range(4):
-            v = dq[at, p * 128 : (p + 1) * 128]
-            dm_ref[mine, p * 128 : (p + 1) * 128] = (v * cs - swap_halves(v) * sn).astype(BF16)
         v = dkv_own[at, :] + dkv_got[at, :].astype(F32)
-        dm_ref[mine, AW:] = jnp.where(lo, v * cs - swap_halves(v) * sn, v).astype(BF16)
-        rows = dm_ref[mine, :]
+        v = jnp.where(lo, v * cosine[at, :] - swap_halves(v) * sine[at, :], v).astype(BF16)
+        here = slice(d * BLK, (d + 1) * BLK)
+        dkv[here, :] = v
+        rows = jnp.concatenate([dqm[d], v], 1)
         for s, w in zip(slots, (w0, w1, w2)):
             out[:, s] = dot_t(rows, w[...])
         res = out[...]
-        total = total + jnp.sum((res * n_all[mine, :].astype(F32)).reshape(BLK // 8, 8, D), axis=0)
+        total = total + jnp.sum((res * n_all[here, :].astype(F32)).reshape(BLK // 8, 8, D), axis=0)
         res = res.astype(BF16)
         if d == 2:
             o2a[...], o2b[...] = res[:HALF], res[HALF:]
         else:
             ref[...] = res
-    gain_ref[...] = jnp.sum(total, axis=0, keepdims=True) / gain[...]
-
-
-def qkv_back(idx, dq, dkv_own, dkv_got, cosine, sine, weight, pieces, gain):
+    grad[...] = dot(dkv[...].T, n_all[...]).astype(BF16)
+    gains[0:1, :] = jnp.sum(total, axis=0, keepdims=True) / gain_one[...]
+    gains[1:2, :] = gain_grad_two[...]
+    for s in range(4):
+        for k, ref in enumerate((mine, theirs)):
+            p = ((y + s) & 3) * 2 + (core if k == 0 else 1 - core)
+            both = gains[:, pl.ds(pl.multiple_of(p * 256, 256), 256)]
+            both = jnp.concatenate([both[:, :128], both[:, 128:], jnp.zeros((12, 128), F32)], 0)
+            for h in range(2):
+                ref[s, h, :128, :] = grad[:, pl.ds(pl.multiple_of(h * DH + p * 128, 128), 128)]
+                ref[s, h, 128:, :] = both.astype(BF16)
+
+
+def qkv_back(idx, dqm, dkv_own, dkv_got, cosine, sine, weight, pieces, gain_one, gain_grad_two):
     res = pl.pallas_call(
         qkv_back_body,
-        out_shape=(sds((ROWS, QW)), sds((ROWS, D)), sds((1, D), F32)) + part_shapes(D),
-        in_specs=[spec(pltpu.SMEM)] + [spec()] * 14,
-        out_specs=(spec(),) * 8,
-        scratch_shapes=[pltpu.VMEM((BLK, D), F32)],
+        out_shape=(sds((4, 2, KVP, 128)),) * 2 + part_shapes(D),
+        in_specs=[spec(pltpu.SMEM)] + [spec()] * 15,
+        out_specs=(spec(),) * 7,
+        scratch_shapes=[
+            pltpu.VMEM((ROWS, D), BF16),
+            pltpu.VMEM((ROWS, 128), BF16),
+            pltpu.VMEM((BLK, D), F32),
+            pltpu.VMEM((128, D), BF16),
+            pltpu.VMEM((2, D), F32),
+        ],
         compiler_params=params(),
         cost_estimate=cost(2 * ROWS * D * QW, 1.3e7),
         name="qkv_back",
-    )(idx, dq, dkv_own, dkv_got, cosine, sine, *weight, *pieces, gain.reshape(1, D))
-    return res[0], res[1], res[2], res[3:]
+    )(
+        idx, dqm, dkv_own, dkv_got, cosine, sine, *weight, *pieces,
+        gain_one.reshape(1, D), gain_grad_two.reshape(1, D),
+    )
+    return res[0], res[1], res[2:]
 
 
 TILES = 6
-FFP = TILES * TILE
+GAP = TILES * TILE
 
 
 def load_down(idx, refs, dst, sem):
@@ -393,17 +415,17 @@
 
 
 def ffn_body(
-    idx, n0, n1, n2a, n2b, n3, c0, c1, c2, c3, gate_w, up_w, w0, w1, w2,
-    n_all, c_all, hid, dgate, dup, down, sem,
+    idx, n0, n1, n2a, n2b, n3, c0, c1, c2, c3, gate_own, up_own, gate_par, up_par, w0, w1, w2,
+    hid, dgate, dup, n_all, c_all, down, sem,
 ):
     i = pl.program_id(0)
+    zh = idx[1]
 
     @pl.when(i == 0)
     def _():
         copies = load_down(idx, (w0, w1, w2), down, sem)
         for c in copies:
             c.start()
-        down[FF4:, :] = jnp.zeros((FFP - FF4, D), BF16)
         for ref, row, (_, n) in zip((n0, n1, n2a, n2b, n3), PIECE_ROW, PIECES):
             n_all[row : row + n, :] = ref[...]
         for d, ref in enumerate((c0, c1, c2, c3)):
@@ -411,8 +433,10 @@
         for c in copies:
             c.wait()
 
-    gate = dot(n_all[...], gate_w[...])
-    up = dot(n_all[...], up_w[...])
+    own = n_all[:, pl.ds(pl.multiple_of(zh * DH, DH), DH)]
+    par = n_all[:, pl.ds(pl.multiple_of((1 - zh) * DH, DH), DH)]
+    gate = dot(own, gate_own[...]) + dot(par, gate_par[...])
+    up = dot(own, up_own[...]) + dot(par, up_par[...])
     dh = dot_t(c_all[...], down[pl.ds(pl.multiple_of(i * TILE, TILE), TILE), :])
     sig = 1.0 / (1.0 + jnp.exp(-gate))
     act = gate * sig
@@ -425,24 +449,29 @@
     return pl.BlockSpec((n, w), lambda i: (0, 0))
 
 
-def ffn(idx, normed, cots, gate_up, down):
-    column = lambda first: pl.BlockSpec((D, TILE), lambda i: (0, i + first))
+def ffn(idx, normed, cots, gate, up, gate_up, down):
+    column = lambda first: pl.BlockSpec((DH, TILE), lambda i: (0, i + first))
     hidden = pl.BlockSpec((ROWS, TILE), lambda i: (0, i))
     return pl.pallas_call(
         ffn_body,
         grid=(TILES,),
-        out_shape=(sds((ROWS, D)),) * 2 + (sds((ROWS, FF4)),) + (sds((ROWS, FFP)),) * 2,
+        out_shape=(sds((ROWS, FF4)),) * 3,
         in_specs=[spec(pltpu.SMEM)]
         + [whole(n, D) for _, n in PIECES]
         + [whole(BLK, D)] * 4
-        + [column(0), column(TILES)]
+        + [column(0), column(0), column(0), column(TILES)]
         + [spec(pl.ANY)] * 3,
-        out_specs=[whole(ROWS, D)] * 2 + [hidden] * 3,
-        scratch_shapes=[pltpu.VMEM((FFP, D), BF16), pltpu.SemaphoreType.DMA((3,))],
+        out_specs=[hidden] * 3,
+        scratch_shapes=[
+            pltpu.VMEM((ROWS, D), BF16),
+            pltpu.VMEM((ROWS, D), BF16),
+            pltpu.VMEM((GAP, D), BF16),
+            pltpu.SemaphoreType.DMA((3,)),
+        ],
         compiler_params=params(),
         cost_estimate=cost(6 * ROWS * D * FF4, 3.4e7),
         name="ffn",
-    )(idx, *normed, *cots, gate_up, gate_up, *down)
+    )(idx, *normed, *cots, gate, up, gate_up, gate_up, *down)
 
 
 def down_body(idx, hid, w0, w1, w2, o0, o1, o2, o3, down, sem):
@@ -471,44 +500,66 @@
     )(idx, hid, *down)
 
 
-def ffn_back_body(dgate, dup, gate_up, *refs):
-    res = dot_t(dgate[...], gate_up[:, :FFP]) + dot_t(dup[...], gate_up[:, FFP:])
-    for ref, row, (_, n) in zip(refs, PIECE_ROW, PIECES):
-        ref[...] = res[row : row + n].astype(BF16)
-
-
-def ffn_back(dgate, dup, gate_up):
+def ffn_back_body(idx, dgate, dup, gate_own, up_own, par, *refs):
+    half = pl.num_programs(0) // 2
+
+    def store(res):
+        for ref, row, (_, n) in zip(refs, PIECE_ROW, PIECES):
+            ref[...] = res[row : row + n].astype(BF16)
+
+    @pl.when(pl.program_id(0) < half)
+    def _():
+        store(dot_t(dgate[...], gate_own[...]) + dot_t(dup[...], up_own[...]))
+
+    @pl.when(pl.program_id(0) >= half)
+    def _():
+        store(dot_t(dgate[...], par[:, :FF4]) + dot_t(dup[...], par[:, GAP:]))
+
+
+def ffn_back(idx, dgate, dup, gate, up, gate_up):
+    half = DH // TILE
+    rows = pl.BlockSpec((ROWS, FF4), lambda i, idx: (0, 0))
+    own = pl.BlockSpec((TILE, FF4), lambda i, idx: (jnp.minimum(i, half - 1), 0))
+    par = pl.BlockSpec((TILE, GAP + FF4), lambda i, idx: (jnp.maximum(i - half, 0), 0))
+    place = lambda i, idx: (0, i ^ (idx[1] * half))
     return pl.pallas_call(
         ffn_back_body,
-        grid=(D // TILE,),
+        grid_spec=pltpu.PrefetchScalarGridSpec(
+            num_scalar_prefetch=1,
+            grid=(D // TILE,),
+            in_specs=[rows, rows, own, own, par],
+            out_specs=[pl.BlockSpec((n, TILE), place) for _, n in PIECES],
+        ),
         out_shape=part_shapes(D),
-        in_specs=[whole(ROWS, FFP)] * 2 + [pl.BlockSpec((TILE, 2 * FFP), lambda i: (i, 0))],
-        out_specs=[pl.BlockSpec((n, TILE), lambda i: (0, i)) for _, n in PIECES],
         compiler_params=params(),
         cost_estimate=cost(4 * ROWS * D * FF4, 1.8e7),
         name="ffn_back",
-    )(dgate, dup, gate_up)
+    )(idx, dgate, dup, gate, up, gate_up)
 
 
 GU_ROWS = FF4 // 128 * 64
 PIECE = 2 * GU_ROWS + FF4 // 2
 
 
-def ffn_grads_body(na, nb, cot, hid, dgate, dup, out, hid_t):
+def ffn_grads_body(*refs):
+    na, nb, cots = refs[0:5], refs[5:10], refs[10:14]
+    hid, dgate, dup, out, hid_t = refs[14:]
+
     @pl.when(pl.program_id(0) == 0)
     def _():
         hid_t[...] = hid[...].T
 
-    rows = jnp.concatenate([na[...], nb[...]], 1).T
+    stack = lambda parts: jnp.concatenate([r[...] for r in parts], 0)
+    rows = jnp.concatenate([stack(na), stack(nb)], 1).T
     for k, ref in enumerate((dgate, dup)):
-        g = dot(rows, ref[:, :FF4]).astype(BF16)
+        g = dot(rows, ref[...]).astype(BF16)
         for h in range(2):
             for q in range(2):
                 r = g[(2 * h + q) * 64 : (2 * h + q + 1) * 64]
                 for c in range(FF4 // 128):
                     first = k * GU_ROWS + c * 64
                     out[h, q, first : first + 64, :] = r[:, c * 128 : (c + 1) * 128]
-    g = dot(hid_t[...], cot[...]).astype(BF16)
+    g = dot(hid_t[...], stack(cots)).astype(BF16)
     for h in range(2):
         for q in range(2):
             out[h, q, 2 * GU_ROWS :, :] = g[
@@ -516,25 +567,21 @@
             ]
 
 
-def ffn_grads(n_all, c_all, hid, dgate, dup):
+def ffn_grads(normed, cots, hid, dgate, dup):
     return pl.pallas_call(
         ffn_grads_body,
         grid=(8,),
         out_shape=sds((2, 16, PIECE, 128)),
-        in_specs=[
-            pl.BlockSpec((ROWS, 128), lambda i: (0, i)),
-            pl.BlockSpec((ROWS, 128), lambda i: (0, i + 8)),
-            pl.BlockSpec((ROWS, 256), lambda i: (0, i)),
-            whole(ROWS, FF4),
-            whole(ROWS, FFP),
-            whole(ROWS, FFP),
-        ],
+        in_specs=[pl.BlockSpec((n, 128), lambda i: (0, i)) for _, n in PIECES]
+        + [pl.BlockSpec((n, 128), lambda i: (0, i + 8)) for _, n in PIECES]
+        + [pl.BlockSpec((BLK, 256), lambda i: (0, i))] * 4
+        + [whole(ROWS, FF4)] * 3,
         out_specs=pl.BlockSpec((2, 2, PIECE, 128), lambda i: (0, i, 0, 0)),
         scratch_shapes=[pltpu.VMEM((FF4, ROWS), BF16)],
         compiler_params=params(),
         cost_estimate=cost(6 * ROWS * D * FF4, 3e7),
         name="ffn_grads",
-    )(n_all, n_all, c_all, hid, dgate, dup)
+    )(*normed, *normed, *cots, hid, dgate, dup)
 
 
 def unpack_body(piece, gate, up, down):
@@ -562,109 +609,138 @@
     )(pieces)
 
 
-QP = 5 * 128
+QP = 4 * 128
 OP = 2 * (AW // 2)
-TAIL = QP + OP + 16
-
-
-def attn_grads_body(n_all, dm, att, branch, gain_one, gain_two, out):
-    rows = n_all[...].T
-    g = dot(rows, dm[...]).astype(BF16)
+QOP = QP + OP
+KVP = 128 + 16
+TAIL = QOP + KVP
+
+
+def attn_grads_body(idx, *refs):
+    na, nb, branch = refs[0:5], refs[5:10], refs[10:15]
+    dqm, att, mine, theirs, att_t = refs[15:]
+    core = idx[3]
+
+    @pl.when(pl.program_id(0) == 0)
+    def _():
+        att_t[...] = att[...].T
+
+    stack = lambda parts: jnp.concatenate([r[...] for r in parts], 0)
+
+    def store(h, first, n, zero, one):
+        mine[0, h, first : first + n, :] = jnp.where(core == 0, zero, one)
+        theirs[0, h, first : first + n, :] = jnp.where(core == 0, one, zero)
+
+    for h, cols in enumerate((na, nb)):
+        g = dot(stack(cols).T, dqm[...]).astype(BF16)
+        for c in range(4):
+            lanes = slice(c * 128, (c + 1) * 128)
+            store(h, c * 128, 128, g[:128, lanes], g[128:, lanes])
+    g = dot(att_t[...], stack(branch)).astype(BF16)
     for h in range(2):
-        for c in range(5):
-            out[0, h, c * 128 : (c + 1) * 128, :] = g[h * 128 : (h + 1) * 128, c * 128 : (c + 1) * 128]
-    g = dot(att[...].T, branch[...]).astype(BF16)
-    gains = [r[:, c * 128 : (c + 1) * 128] for r in (gain_one, gain_two) for c in range(2)]
-    gains = jnp.concatenate(gains + [jnp.zeros((12, 128), F32)], 0).astype(BF16)
-    for h in range(2):
+        r = g[h * (AW // 2) : (h + 1) * (AW // 2)]
+        for c in range(2):
+            lanes = lambda k: slice(k * 256 + c * 128, k * 256 + (c + 1) * 128)
+            store(h, QP + c * (AW // 2), AW // 2, r[:, lanes(0)], r[:, lanes(1)])
+
+
+def attn_grads(idx, normed, branch, dqm, att):
+    turn = lambda s, idx: (s + idx[2]) & 3
+    piece = pl.BlockSpec((1, 2, QOP, 128), lambda s, idx: (s, 0, 0, 0))
+    fixed = pl.BlockSpec((ROWS, AW), lambda s, idx: (0, 0))
+    return pl.pallas_call(
+        attn_grads_body,
+        grid_spec=pltpu.PrefetchScalarGridSpec(
+            num_scalar_prefetch=1,
+            grid=(4,),
+            in_specs=[pl.BlockSpec((n, 256), lambda s, idx: (0, turn(s, idx))) for _, n in PIECES]
+            + [pl.BlockSpec((n, 256), lambda s, idx: (0, turn(s, idx) + 4)) for _, n in PIECES]
+            + [pl.BlockSpec((n, 512), lambda s, idx: (0, turn(s, idx))) for _, n in PIECES]
+            + [fixed, fixed],
+            out_specs=[piece, piece],
+            scratch_shapes=[pltpu.VMEM((AW, ROWS), BF16)],
+        ),
+        out_shape=(sds((4, 2, QOP, 128)),) * 2,
+        compiler_params=params(),
+        cost_estimate=cost(4 * ROWS * D * AW, 1e7),
+        name="attn_grads",
+    )(idx, *normed, *normed, *branch, dqm, att)
+
+
+def small_call(body, out_shape, *args, name):
+    return pl.pallas_call(
+        body,
+        out_shape=out_shape,
+        in_specs=[spec(pltpu.SMEM)] + [spec()] * (len(args) - 1),
+        out_specs=jax.tree.map(lambda _: spec(), out_shape),
+        compiler_params=params(),
+        cost_estimate=cost(1e6, 4e6),
+        name=name,
+    )(*args)
+
+
+def add(*values):
+    return sum((v.astype(F32) for v in values[1:]), values[0].astype(F32)).astype(BF16)
+
+
+def sum_core_body(idx, a, b, c, d, *outs):
+    for s, out in enumerate(outs):
+        out[:, :QOP, :] = add(a[s], b[s])
+        out[:, QOP:, :] = add(c[s], d[s])
+
+
+def sum_y_body(idx, a, b, c, d, own, other):
+    zh = idx[1]
+    own[...] = add(a[zh], b[zh], c[zh], d[zh])
+    far = 1 - zh
+    other[...] = add(a[far], b[far], c[far], d[far])
+
+
+def sum_z_body(idx, a, b, c, d, out):
+    out[...] = add(a[...], b[...], c[...], d[...])
+
+
+def unpack_tail_body(idx, *refs):
+    y, core = idx[2], idx[3]
+    qkv, out, gains = refs[8:]
+    for k in range(8):
+        piece = refs[k]
+        p = ((y - k % 4) & 3) * 2 + (core if k < 4 else 1 - core)
+        rows = pl.ds(pl.multiple_of(p * 128, 128), 128)
+        for c in range(4):
+            qkv[rows, c * 128 : (c + 1) * 128] = piece[c * 128 : (c + 1) * 128, :].astype(F32)
+        qkv[rows, AW:] = piece[QOP : QOP + 128, :].astype(F32).T
+        g = piece[QOP + 128 :, :].astype(F32)
         for c in range(2):
             first = QP + c * (AW // 2)
-            out[0, h, first : first + AW // 2, :] = g[
-                h * (AW // 2) : (h + 1) * (AW // 2), c * 128 : (c + 1) * 128
-            ]
-        out[0, h, QP + OP :, :] = gains
-
-
-def attn_grads_kernel(na, nb, dm, att, branch, gain_one, gain_two, out, rows):
-    rows[:, :128] = na[...]
-    rows[:, 128:] = nb[...]
-    attn_grads_body(rows, dm, att, branch, gain_one, gain_two, out)
-
-
-def attn_grads(n_all, dm, att, branch, gain_one, gain_two):
-    return pl.pallas_call(
-        attn_grads_kernel,
-        grid=(8,),
-        out_shape=sds((8, 2, TAIL, 128)),
-        in_specs=[
-            pl.BlockSpec((ROWS, 128), lambda i: (0, i)),
-            pl.BlockSpec((ROWS, 128), lambda i: (0, i + 8)),
-            whole(ROWS, QW),
-            whole(ROWS, AW),
-            pl.BlockSpec((ROWS, 256), lambda i: (0, i)),
-            pl.BlockSpec((1, 256), lambda i: (0, i)),
-            pl.BlockSpec((1, 256), lambda i: (0, i)),
-        ],
-        out_specs=pl.BlockSpec((1, 2, TAIL, 128), lambda i: (i, 0, 0, 0)),
-        scratch_shapes=[pltpu.VMEM((ROWS, 256), BF16)],
-        compiler_params=params(),
-        cost_estimate=cost(2 * ROWS * D * (QW + AW), 1.5e7),
-        name="attn_grads",
-    )(n_all, n_all, dm, att, branch, gain_one, gain_two)
-
-
-def unpack_tail_body(piece, qkv, out, gains):
-    for c in range(5):
-        qkv[:, c * 128 : (c + 1) * 128] = piece[0, c * 128 : (c + 1) * 128, :].astype(F32)
-    for c in range(2):
-        first = QP + c * (AW // 2)
-        out[:, c * 128 : (c + 1) * 128] = piece[0, first : first + AW // 2, :].astype(F32)
-    rows = piece[0, QP + OP :, :].astype(F32)
-    for c in range(2):
-        gains[0:1, c * 128 : (c + 1) * 128] = rows[c : c + 1]
-        gains[1:2, c * 128 : (c + 1) * 128] = rows[2 + c : 3 + c]
-
-
-def unpack_tail(pieces):
-    return pl.pallas_call(
-        unpack_tail_body,
-        grid=(8,),
-        out_shape=(sds((DH, QW), F32), sds((AW // 2, D), F32), sds((2, D), F32)),
-        in_specs=[pl.BlockSpec((1, TAIL, 128), lambda i: (i, 0, 0))],
-        out_specs=[
-            pl.BlockSpec((128, QW), lambda i: (i, 0)),
-            pl.BlockSpec((AW // 2, 256), lambda i: (0, i)),
-            pl.BlockSpec((2, 256), lambda i: (0, i)),
-        ],
-        compiler_params=params(),
-        cost_estimate=cost(1e6, 7e6),
-        name="unpack_tail",
-    )(pieces)
-
-
-def bf_sum(*values):
-    return sum((v.astype(F32) for v in values[1:]), values[0].astype(F32)).astype(BF16)
-
-
-def sum_tail(g, y, zl, zh, core):
-    g = g.reshape(4, 2, 2, TAIL, 128)
-    pick = lambda v, i, axis: lax.dynamic_index_in_dim(v, i, axis, False)
-    g = bf_sum(pick(g, core, 1), lax.ppermute(pick(g, 1 - core, 1), "core", shift(2, 1)))
-    got = [lax.ppermute(pick(g, (y + s) % 4, 0), "y", shift(4, s)) for s in (1, 2, 3)]
-    g = bf_sum(pick(g, y, 0), *got)
-    own, other = pick(g, zh, 0), pick(g, 1 - zh, 0)
+            cols = pl.ds(pl.multiple_of(p * 256 + c * 128, 128), 128)
+            out[:, cols] = piece[first : first + AW // 2, :].astype(F32)
+            gains[:, cols] = g[2 * c : 2 * c + 2]
+
+
+def sum_tail(idx, first, second):
+    got_a = lax.ppermute(first[1], "core", shift(2, 1))
+    got_b = lax.ppermute(second[1], "core", shift(2, 1))
+    part = sds((2, TAIL, 128))
+    g = small_call(sum_core_body, (part,) * 4, idx, first[0], got_a, second[0], got_b, name="sum_core")
+    got = [lax.ppermute(g[s], "y", shift(4, s)) for s in (2, 1, 3)]
+    part = sds((TAIL, 128))
+    own, other = small_call(sum_y_body, (part,) * 2, idx, g[0], *got, name="sum_y")
     cross = [(2 * a + b, 2 * (1 - a) + (1 - b)) for a in range(2) for b in range(2)]
-    g = bf_sum(
+    g = small_call(
+        sum_z_body,
+        part,
+        idx,
         own,
         lax.ppermute(own, "zl", shift(2, 1)),
         lax.ppermute(other, "zh", shift(2, 1)),
         lax.ppermute(other, ("zl", "zh"), cross),
+        name="sum_z",
     )
-    parts = jnp.stack([g] + [lax.ppermute(g, "y", shift(4, s)) for s in (1, 2, 3)])
-    other = lax.ppermute(parts, "core", shift(2, 1))
-    both = jnp.where(core == 0, jnp.stack([parts, other], 1), jnp.stack([other, parts], 1))
-    both = jnp.take(both, (y - jnp.arange(4)) % 4, axis=0)
-    return both.reshape(8, TAIL, 128)
+    mine = [g] + [lax.ppermute(g, "y", shift(4, s)) for s in (1, 2, 3)]
+    theirs = [lax.ppermute(v, "core", shift(2, 1)) for v in mine]
+    shapes = (sds((DH, QW), F32), sds((AW // 2, D), F32), sds((2, D), F32))
+    return small_call(unpack_tail_body, shapes, idx, *mine, *theirs, name="unpack_tail")
 
 
 def inverse_rms(v):
@@ -693,21 +769,30 @@
 ):
     x, zh, core = lax.axis_index("x"), lax.axis_index("zh"), lax.axis_index("core")
     y, zl = lax.axis_index("y"), lax.axis_index("zl")
-    idx = jnp.stack([x, zh, core]).astype(jnp.int32)
+    idx = jnp.stack([x, zh, y, core]).astype(jnp.int32)
 
     tok = tokens.astype(F32)
     s_one = inverse_rms(tok)
-    normed_one = gather_x((tok * s_one * gain_one).astype(BF16))
-    qkv_all = fetch_partner(qkv_weight, core)
-    out_all = fetch_partner(tie(out_weight, qkv_all[1]), core)
-    down_all = fetch_partner(tie(down_weight, out_all[1]), core)
+    qkv_got = fetch_half(qkv_weight, core)
+    normed_one, sent = gather_x((tok * s_one * gain_one).astype(BF16), qkv_got)
+    qkv_all = qkv_weight, qkv_got, lax.ppermute(tie(qkv_got, *sent), "core", shift(2, 1))
     rows = DH // 8
-    mine = lambda w: jnp.pad(
-        lax.dynamic_slice_in_dim(w, (y * 2 + core) * rows, rows, 0), ((0, 0), (0, FFP - FF4))
+    mine = lambda w: lax.dynamic_slice_in_dim(w, (y * 2 + core) * rows, rows, 0)
+    cross = [(2 * a + b, 2 * (1 - a) + (1 - b)) for a in range(2) for b in range(2)]
+    gate_up = lax.ppermute(
+        jnp.concatenate(
+            [
+                tie(mine(gate_weight), normed_one[2]),
+                jnp.zeros((rows, GAP - FF4), BF16),
+                mine(up_weight),
+            ],
+            1,
+        ),
+        ("zl", "zh"),
+        cross,
     )
-    gate_up = lax.all_gather(
-        jnp.concatenate([mine(gate_weight), mine(up_weight)], 1), ("zh", "y", "core"), axis=0, tiled=True
-    )
+    out_all = fetch_partner(out_weight, core, *sent)
+    gate_up = lax.all_gather(gate_up, ("y", "core"), axis=0, tiled=True)
     cots = gather_direct(tie(cotangent, normed_one[2]))
 
     begin, position = replica_layout(seq_lengths, seq_replica, (y * 2 + zl) * 2 + core)
@@ -721,44 +806,44 @@
 
     q, kv_own = qkv_forward(idx, normed_one, qkv_all, cosine, sine)
     kv_par = lax.ppermute(kv_own, "zh", shift(2, 1))
+    down_all = fetch_partner(down_weight, core, kv_par)
     att, lse = attend(idx, q, kv_own, kv_par, first)
-    att = tie(att, down_all[1], *cots)
+    att = tie(att, *cots)
     after_attn = tok + scatter_x(out_project(idx, att, out_all))
 
     r_two = inverse_rms(after_attn)
-    normed_two = gather_x((after_attn * r_two * gain_two).astype(BF16))
-    n_two, cot_all, hid, dgate, dup = ffn(idx, normed_two, cots, gate_up, down_all)
-    grads = ffn_grads(n_two, cot_all, hid, dgate, dup)
+    normed_two, _ = gather_x((after_attn * r_two * gain_two).astype(BF16))
+    hid, dgate, dup = ffn(idx, normed_two, cots, gate_weight, up_weight, gate_up, down_all)
+    own_grads = ffn_grads(normed_two, cots, hid, dgate, dup)
     grads = lax.psum_scatter(
-        grads.reshape(32, PIECE, 128), ("zh", "zl", "y", "core"), scatter_dimension=0, tiled=True
+        own_grads.reshape(32, PIECE, 128), ("zh", "zl", "y", "core"), scatter_dimension=0, tiled=True
     )
-    grads = lax.all_gather(grads, ("zl", "y", "core"), axis=0, tiled=True)
-    grad_gate, grad_up, grad_down = unpack(grads)
-
-    d_two = scatter_x(ffn_back(dgate, dup, gate_up))
+    d_two = scatter_x(ffn_back(idx, tie(dgate, own_grads), dup, gate_weight, up_weight, gate_up))
     back_two, gain_grad_two = norm_back(after_attn, r_two, gain_two, d_two)
     after_grad = cotangent.astype(F32) + back_two
-    branch = gather_x(after_grad.astype(BF16))
+    branch, _ = gather_x(after_grad.astype(BF16))
     layer_parts = down_project(idx, tie(hid, after_grad), down_all)
     layer_parts = [tie(p, branch[2], branch[3]) for p in layer_parts]
     layer_out = after_attn + scatter_direct(layer_parts)
     att = tie(att, *layer_parts)
-    dq, dkv_own, dkv_par = attend_back(idx, q, kv_own, kv_par, first, lse, att, branch, out_all)
+    dqm, dkv_own, dkv_par = attend_back(
+        idx, q, kv_own, kv_par, first, lse, att, cosine, sine, branch, out_all
+    )
     dkv_got = lax.ppermute(dkv_par, "zh", shift(2, 1))
+    tail = attn_grads(idx, normed_one, branch, dqm.reshape(ROWS, AW), att.reshape(ROWS, AW))
     layer_out = layer_out.astype(BF16)
-    d_mixed, n_one, gain_grad_one, parts = qkv_back(
-        idx, tie(dq, layer_out), dkv_own, dkv_got, cosine, sine, qkv_all, normed_one, gain_one
+    *tail_kv, parts = qkv_back(
+        idx, dqm, tie(dkv_own, layer_out), dkv_got, cosine, sine, qkv_all, normed_one, gain_one,
+        gain_grad_two,
     )
+    grads = lax.all_gather(tie(grads, dkv_got), ("zl", "y", "core"), axis=0, tiled=True)
+    grad_gate, grad_up, grad_down = unpack(grads)
     d_one = scatter_x(parts)
     back_one, _ = norm_back(tok, s_one, gain_one, d_one)
     input_grad = (after_grad + back_one).astype(BF16)
 
     over_x = lambda v: sum((lax.ppermute(v, "x", shift(4, s)) for s in (1, 2, 3)), v)
-    tail = attn_grads(
-        n_one, d_mixed, att.reshape(ROWS, AW), jnp.concatenate(branch, 0),
-        gain_grad_one, gain_grad_two.reshape(1, D),
-    )
-    grad_qkv, grad_out, gains = unpack_tail(sum_tail(tail, y, zl, zh, core))
+    grad_qkv, grad_out, gains = sum_tail(idx, tail, tail_kv)
     gains = over_x(gains)
     return (
         layer_out, input_grad, gains[0], grad_qkv, grad_out, grad_gate, grad_up,

time: 592 us -> 537 us (0.907)
  waiting for transfers between devices: 268 us -> 220 us
  local copies, waits for them, and re-layouts: 32.2 us -> 20 us
  Pallas kernels: 160 us -> 167 us
  other arithmetic: 27.8 us -> 21.4 us
    reduce_scatter x1, waiting for transfers between devices: 76.2 us -> 17 us  [on_device(): lax.psum_scatter(own_grads.reshape(32, PIECE, 128), ('zh', 'zl', 'y', 'co...]
    ppermute x1, waiting for transfers between devices: 45.4 us -> 0.01 us  [on_device(): kv_par = lax.ppermute(kv_own, 'zh', shift(2, 1))]
    ppermute x3, waiting for transfers between devices: 0.01 us -> 21.3 us  [gather_x(): from_next = lax.ppermute(v, 'x', shift(4, -1))]
    ppermute x3, waiting for transfers between devices: 25.2 us -> 8.09 us  [scatter_x(): from_prev = lax.ppermute(q1, 'x', shift(4, 1))]
    ppermute x3, waiting for transfers between devices: 0.01 us -> 15.7 us  [scatter_direct(): got = [lax.ppermute(parts[s], 'x', shift(4, s)) for s in (1, 2, 3)]]
    ppermute x17 -> x23, starting transfers between devices: 27.1 us -> 41.8 us  [the longest x4 11.2 us: sum_tail(): theirs = [lax.ppermute(v, 'core', shift(2, 1)) for v in mine]]
    ppermute x3, waiting for transfers between devices: 12.7 us -> 26.1 us  [gather_x(): from_prev = lax.ppermute(v, 'x', shift(4, 1))]
    ppermute x3 -> x2, starting transfers between devices: 15.6 us -> 3.72 us  [fetch_partner(): return (w, got, lax.ppermute(got, 'core', shift(2, 1)))]
  transfers between devices with their start and end apart: 55 -> 60, of which waited for: 27 -> 34; matrix products, arithmetic and copies ran while one was open for 9% -> 6% of each run, Pallas kernels for 18% -> 21%
where the time goes in v3:
time: 537 us; the launch traced here: 529 us
  waiting for transfers between devices  220 us (41%)
  Pallas kernels  167 us (31%)
  starting transfers between devices  85.8 us (16%)
  other arithmetic  21.4 us (4%)
  local copies, waits for them, and re-layouts  20 us (4%)
  between operations  14.6 us (3%)
    pallas_call x1, Pallas kernels, attend_back(): pl.pallas_call(attend_back_body, out_shape=(sds((4, BLK, AW)), sds((ROWS,...  26.1 us
    ppermute x3, waiting for transfers between devices, gather_x(): from_prev = lax.ppermute(v, 'x', shift(4, 1))  26.1 us
    ppermute x3, waiting for transfers between devices, sum_tail(): got = [lax.ppermute(g[s], 'y', shift(4, s)) for s in (2, 1, 3)]  24.1 us
    ppermute x3, waiting for transfers between devices, scatter_x(): from_next = lax.ppermute(q3, 'x', shift(4, -1))  21.7 us
    ppermute x3, waiting for transfers between devices, gather_x(): from_next = lax.ppermute(v, 'x', shift(4, -1))  21.3 us
    pallas_call x1, Pallas kernels, ffn_grads(): pl.pallas_call(ffn_grads_body, grid=(8,), out_shape=sds((2, 16, PIECE, 12...  21.1 us
    pallas_call x1, Pallas kernels, ffn(): pl.pallas_call(ffn_body, grid=(TILES,), out_shape=(sds((ROWS, FF4)),) * 3...  20.8 us
    pallas_call x1, Pallas kernels, attend(): pl.pallas_call(attend_body, out_shape=(sds((4, BLK, AW)), sds((ROWS, 128)...  17.3 us
  transfers between devices with their start and end apart: 60, of which 34 were waited for; matrix products, arithmetic and copies ran while one was open for 6% of the time, Pallas kernels for 21%

profile of v3, /device:TPU:1, one launch (start us, length us, event | category | flops | bytes accessed | tf_op | source)
XLA Modules:
  0.0 528.6 jit_solution(16802719829948602015)
XLA Ops:
  13.0 3.6 collective-permute-start.2
  16.6 10.8 %collective-permute-done.1.n3.refs_4_.refs_9_ = bf16[160,2048]{1,0:T(8,128)(2,1)S(1)} collective-permute-done((bf16[160,2048]{1,0:T(8,128)(2,1)S(1)}, bf16[160,2048]{1,0:T(8,128)(2,1)S(1)}, u32[]{:S(2)}, u32[]{:S(2)}) %collective-permute-start.1) | collective-permute-done | bytes 655392 | tf_op jit(solution)/shard_map/ppermute | solution.py:70
  27.4 3.5 collective-permute-done.2.w1
  34.2 5.6 %collective-permute-done.3.n2a.refs_2_.refs_7_ = bf16[80,2048]{1,0:T(8,128)(2,1)S(1)} collective-permute-done((bf16[80,2048]{1,0:T(8,128)(2,1)S(1)}, bf16[80,2048]{1,0:T(8,128)(2,1)S(1)}, u32[]{:S(2)}, u32[]{:S(2)}) %collective-permute-start.3) | collective-permute-done | bytes 327712 | tf_op jit(solution)/shard_map/ppermute | solution.py:73
  42.5 14.6 %collective-permute-done.20 = bf16[128,2944]{1,0:T(8,128)(2,1)S(1)} collective-permute-done((bf16[128,2944]{1,0:T(8,128)(2,1)S(1)}, bf16[128,2944]{1,0:T(8,128)(2,1)S(1)}, u32[]{:S(2)}, u32[]{:S(2)}) %collective-permute-start.20) | collective-permute-done | bytes 753696 | tf_op jit(solution)/shard_map/ppermute | solution.py:782
  60.4 10.6 %collective-permute-done.n1.refs_1_.refs_6_ = bf16[160,2048]{1,0:T(8,128)(2,1)S(1)} collective-permute-done((bf16[160,2048]{1,0:T(8,128)(2,1)S(1)}, bf16[160,2048]{1,0:T(8,128)(2,1)S(1)}, u32[]{:S(2)}, u32[]{:S(2)}) %collective-permute-start) | collective-permute-done | bytes 655392 | tf_op jit(solution)/shard_map/ppermute | solution.py:71
  71.0 4.4 collective-permute-start.5
  81.5 3.9 collective-permute-done.4.n2b.refs_3_.refs_8_
  86.4 6.5 %qkv_forward.1 = (bf16[640,512]{1,0:T(8,128)(2,1)}, bf16[640,128]{1,0:T(8,128)(2,1)}) custom-call(s32[4]{0:T(128)} %pad_add_fusion.idx, bf16[160,2048]{1,0:T(8,128)(2,1)} %copy-done.2, bf16[160,2048]{1,0:T(8,128)(2,1)} %copy-done.6, bf16[80,2048]{1,0:T(8,128)(2,1)} %copy-done.22, bf16[80,2048]{1,0:T(8,128)(2,1)} %copy-done.23, bf16[160,2048]{1,0:T(8,128)(2,1)} %copy-done.5, ...), custom_call_target="tpu_custom_call" | custom-call | flops 1677721600 | bytes 7000000 | tf_op jit(solution)/shard_map/qkv_forward/pallas_call | solution.py:158
  94.7 3.9 collective-permute-start.8
  101.3 17.3 %attend.1 = (bf16[4,160,512]{2,1,0:T(8,128)(2,1)}, f32[640,128]{1,0:T(8,128)}) custom-call(s32[4]{0:T(128)} %pad_add_fusion.idx, bf16[640,512]{1,0:T(8,128)(2,1)} %get-tuple-element.74.q, bf16[640,128]{1,0:T(8,128)(2,1)} %get-tuple-element.75.kv_own, bf16[640,128]{1,0:T(8,128)(2,1)} %copy-done.50, s32[640,1]{1,0:T(8,128)} %reshape.149.first), custom_call_target="tpu_custom_call" | custom-call | flops 12000000000 | bytes 3000000 | tf_op jit(solution)/shard_map/attend/pallas_call | solution.py:223
  118.5 7.8 %collective-permute-done.8.c2.refs_12_ = bf16[160,2048]{1,0:T(8,128)(2,1)S(1)} collective-permute-done((bf16[160,2048]{1,0:T(8,128)(2,1)S(1)}, bf16[160,2048]{1,0:T(8,128)(2,1)S(1)}, u32[]{:S(2)}, u32[]{:S(2)}) %collective-permute-start.8) | collective-permute-done | bytes 655392 | tf_op jit(solution)/shard_map/ppermute | solution.py:79
  128.1 4.9 out_project.1
  138.0 4.3 collective-permute-done.14
  143.4 3.5 collective-permute-start.15
  147.6 12.0 %collective-permute-done.15 = bf16[160,2048]{1,0:T(8,128)(2,1)S(1)} collective-permute-done((bf16[160,2048]{1,0:T(8,128)(2,1)S(1)}, bf16[160,2048]{1,0:T(8,128)(2,1)S(1)}, u32[]{:S(2)}, u32[]{:S(2)}) %collective-permute-start.15) | collective-permute-done | bytes 655392 | tf_op jit(solution)/shard_map/ppermute | solution.py:94
  159.6 3.4 collective-permute-done.13
  163.5 5.9 %collective-permute-done.21.w1 = bf16[352,2048]{1,0:T(8,128)(2,1)S(1)} collective-permute-done((bf16[352,2048]{1,0:T(8,128)(2,1)S(1)}, bf16[352,2048]{1,0:T(8,128)(2,1)S(1)}, u32[]{:S(2)}, u32[]{:S(2)}) %collective-permute-start.21) | collective-permute-done | bytes 1441824 | tf_op jit(solution)/shard_map/ppermute | solution.py:121
  174.1 14.9 %collective-permute-done.17.n3.refs_4_.refs_9_ = bf16[160,2048]{1,0:T(8,128)(2,1)S(1)} collective-permute-done((bf16[160,2048]{1,0:T(8,128)(2,1)S(1)}, bf16[160,2048]{1,0:T(8,128)(2,1)S(1)}, u32[]{:S(2)}, u32[]{:S(2)}) %collective-permute-start.17) | collective-permute-done | bytes 655392 | tf_op jit(solution)/shard_map/ppermute | solution.py:70
  192.0 6.7 %collective-permute-done.18.n2a.refs_2_.refs_7_ = bf16[80,2048]{1,0:T(8,128)(2,1)S(1)} collective-permute-done((bf16[80,2048]{1,0:T(8,128)(2,1)S(1)}, bf16[80,2048]{1,0:T(8,128)(2,1)S(1)}, u32[]{:S(2)}, u32[]{:S(2)}) %collective-permute-start.18) | collective-permute-done | bytes 327712 | tf_op jit(solution)/shard_map/ppermute | solution.py:73
  200.2 20.8 %ffn.1 = (bf16[640,1408]{1,0:T(8,128)(2,1)}, bf16[640,1408]{1,0:T(8,128)(2,1)}, bf16[640,1408]{1,0:T(8,128)(2,1)}) custom-call(s32[4]{0:T(128)} %pad_add_fusion.idx, bf16[160,2048]{1,0:T(8,128)(2,1)} %copy-done.14, bf16[160,2048]{1,0:T(8,128)(2,1)} %copy-done.36, bf16[80,2048]{1,0:T(8,128)(2,1)} %copy-done.47, bf16[80,2048]{1,0:T(8,128)(2,1)} %copy-done.49, ...), custom_call_target="tpu_custom_call" | custom-call | flops 11072962560 | bytes 34000000 | tf_op jit(solution)/shard_map/ffn/pallas_call | solution.py:455
  221.0 21.1 %ffn_grads.1 = bf16[2,16,2112,128]{3,2,1,0:T(8,128)(2,1)} custom-call(bf16[160,2048]{1,0:T(8,128)(2,1)} %copy-done.14, bf16[160,2048]{1,0:T(8,128)(2,1)} %copy-done.36, bf16[80,2048]{1,0:T(8,128)(2,1)} %copy-done.47, bf16[80,2048]{1,0:T(8,128)(2,1)} %copy-done.49, bf16[160,2048]{1,0:T(8,128)(2,1)} %copy-done.35, bf16[160,2048]{1,0:T(8,128)(2,1)} %copy-done.14, ...), custom_call_target="tpu_custom_call" | custom-call | flops 11072962560 | bytes 30000000 | tf_op jit(solution)/shard_map/ffn_grads/pallas_call | solution.py:571
  242.2 15.7 %ffn_back.1 = (bf16[160,2048]{1,0:T(8,128)(2,1)}, bf16[160,2048]{1,0:T(8,128)(2,1)}, bf16[80,2048]{1,0:T(8,128)(2,1)}, bf16[80,2048]{1,0:T(8,128)(2,1)}, bf16[160,2048]{1,0:T(8,128)(2,1)}) custom-call(s32[4]{0:T(128)} %pad_add_fusion.idx, bf16[640,1408]{1,0:T(8,128)(2,1)} %get-tuple-element.90.refs_15_.dgate, ...), custom_call_target="tpu_custom_call" | custom-call | flops 7381975040 | bytes 18000000 | tf_op jit(solution)/shard_map/ffn_back/pallas_call | solution.py:525
  262.1 3.5 collective-permute-done.25
  265.8 3.2 collective-permute-start.26
  270.6 9.7 %collective-permute-done.26 = bf16[160,2048]{1,0:T(8,128)(2,1)S(1)} collective-permute-done((bf16[160,2048]{1,0:T(8,128)(2,1)S(1)}, bf16[160,2048]{1,0:T(8,128)(2,1)S(1)}, u32[]{:S(2)}, u32[]{:S(2)}) %collective-permute-start.26) | collective-permute-done | bytes 655392 | tf_op jit(solution)/shard_map/ppermute | solution.py:94
  280.3 4.7 collective-permute-done.24
  288.4 10.7 %collective-permute-done.29.b1.refs_11_ = bf16[160,2048]{1,0:T(8,128)(2,1)S(1)} collective-permute-done((bf16[160,2048]{1,0:T(8,128)(2,1)S(1)}, bf16[160,2048]{1,0:T(8,128)(2,1)S(1)}, u32[]{:S(2)}, u32[]{:S(2)}) %collective-permute-start.29) | collective-permute-done | bytes 655392 | tf_op jit(solution)/shard_map/ppermute | solution.py:71
  302.3 9.9 %down_project.1 = (bf16[160,2048]{1,0:T(8,128)(2,1)}, bf16[160,2048]{1,0:T(8,128)(2,1)}, bf16[160,2048]{1,0:T(8,128)(2,1)}, bf16[160,2048]{1,0:T(8,128)(2,1)}) custom-call(s32[4]{0:T(128)} %pad_add_fusion.idx, bf16[640,1408]{1,0:T(8,128)(2,1)} %get-tuple-element.96.refs_14_.hid, bf16[704,2048]{1,0:T(8,128)(2,1)} %w0.9, bf16[352,2048]{1,0:T(8,128)(2,1)} %copy-done.42, ...), custom_call_target="tpu_custom_call" | custom-call | flops 3690987520 | bytes 11000000 | tf_op jit(solution)/shard_map/down_project/pallas_call | solution.py:491
  312.3 26.1 %attend_back.1 = (bf16[4,160,512]{2,1,0:T(8,128)(2,1)}, f32[640,128]{1,0:T(8,128)}, bf16[640,128]{1,0:T(8,128)(2,1)}) custom-call(s32[4]{0:T(128)} %pad_add_fusion.idx, bf16[640,512]{1,0:T(8,128)(2,1)} %get-tuple-element.74.q, bf16[640,128]{1,0:T(8,128)(2,1)} %get-tuple-element.75.kv_own, bf16[640,128]{1,0:T(8,128)(2,1)} %copy-done.50, ...), custom_call_target="tpu_custom_call" | custom-call | flops 30000001024 | bytes 8000000 | tf_op jit(solution)/shard_map/attend_back/pallas_call | solution.py:325
  340.0 4.3 collective-permute-done.34.dkv_got
  344.3 17.0 %reduce-scatter.2.cloned.1.call-done = bf16[1,2112,128]{2,1,0:T(8,128)(2,1)} async-done(((bf16[32,2112,128]{2,1,0:T(8,128)(2,1)}), bf16[1,2112,128]{2,1,0:T(8,128)(2,1)}) %reduce-scatter.2.cloned.1.call-update) | async-done | bytes 540688 | tf_op jit(solution)/shard_map/reduce_scatter | solution.py:818
  366.1 9.2 %attn_grads.1 = (bf16[4,2,1024,128]{3,2,1,0:T(8,128)(2,1)}, bf16[4,2,1024,128]{3,2,1,0:T(8,128)(2,1)}) custom-call(s32[4]{0:T(128)} %pad_add_fusion.idx, bf16[160,2048]{1,0:T(8,128)(2,1)} %copy-done.2, bf16[160,2048]{1,0:T(8,128)(2,1)} %copy-done.6, bf16[80,2048]{1,0:T(8,128)(2,1)} %copy-done.22, bf16[80,2048]{1,0:T(8,128)(2,1)} %copy-done.23, ...), custom_call_target="tpu_custom_call" | custom-call | flops 2684354560 | bytes 10000000 | tf_op jit(solution)/shard_map/attn_grads/pallas_call | solution.py:651
  377.9 15.6 %collective-permute-done.32 = bf16[160,2048]{1,0:T(8,128)(2,1)} collective-permute-done((bf16[160,2048]{1,0:T(8,128)(2,1)}, bf16[160,2048]{1,0:T(8,128)(2,1)}, u32[]{:S(2)}, u32[]{:S(2)}) %collective-permute-start.32) | collective-permute-done | bytes 655392 | tf_op jit(solution)/shard_map/ppermute | solution.py:83
  396.6 9.0 %qkv_back.1 = (bf16[4,2,144,128]{3,2,1,0:T(8,128)(2,1)}, bf16[4,2,144,128]{3,2,1,0:T(8,128)(2,1)}, bf16[160,2048]{1,0:T(8,128)(2,1)}, bf16[160,2048]{1,0:T(8,128...) custom-call(s32[4]{0:T(128)} %pad_add_fusion.idx, ...), custom_call_target="tpu_custom_call" | custom-call | flops 1677721600 | bytes 13000000 | tf_op jit(solution)/shard_map/qkv_back/pallas_call | solution.py:384
  405.6 3.6 collective-permute-start.37
  411.9 4.2 collective-permute-done.37
  417.2 3.3 collective-permute-start.38
  421.2 4.0 sum_core.1
  431.2 9.4 %collective-permute-done.41.b = bf16[2,1168,128]{2,1,0:T(8,128)(2,1)} collective-permute-done((bf16[2,1168,128]{2,1,0:T(8,128)(2,1)}, bf16[2,1168,128]{2,1,0:T(8,128)(2,1)}, u32[]{:S(2)}, u32[]{:S(2)}) %collective-permute-start.41) | collective-permute-done | bytes 598048 | tf_op jit(solution)/shard_map/ppermute | solution.py:726
  440.5 14.7 %collective-permute-done.42.c = bf16[2,1168,128]{2,1,0:T(8,128)(2,1)} collective-permute-done((bf16[2,1168,128]{2,1,0:T(8,128)(2,1)}, bf16[2,1168,128]{2,1,0:T(8,128)(2,1)}, u32[]{:S(2)}, u32[]{:S(2)}) %collective-permute-start.42) | collective-permute-done | bytes 598048 | tf_op jit(solution)/shard_map/ppermute | solution.py:726
  461.2 5.2 collective-permute-done.44.b
  468.1 5.7 %collective-permute-done.45.c = bf16[1168,128]{1,0:T(8,128)(2,1)} collective-permute-done((bf16[1168,128]{1,0:T(8,128)(2,1)}, bf16[1168,128]{1,0:T(8,128)(2,1)}, u32[]{:S(2)}, u32[]{:S(2)}) %collective-permute-start.45) | collective-permute-done | bytes 299040 | tf_op jit(solution)/shard_map/ppermute | solution.py:736
  483.0 4.8 collective-permute-start.53
  487.8 3.1 collective-permute-start.52
  490.9 3.3 collective-permute-done.47.refs_1_
  498.1 4.2 unpack_tail.1
  508.3 13.5 %unpack.1 = (f32[1024,1408]{1,0:T(8,128)}, f32[1024,1408]{1,0:T(8,128)}, f32[704,2048]{1,0:T(8,128)}) custom-call(bf16[16,2112,128]{2,1,0:T(8,128)(2,1)} %all-gather.5.cloned.1.call-done.piece), custom_call_target="tpu_custom_call" | custom-call | flops 1000000 | bytes 26000000 | tf_op jit(solution)/shard_map/unpack/pallas_call | solution.py:596
  (255 shorter events, 106.4 us)
Async XLA Ops:
  7.2 193.0 %all-gather.3.cloned.1.call-start = ((), (), s32[]{:S(2)}) async-start(), calls=%async_computation.1 | async-start | bytes 6782976 | tf_op jit(solution)/shard_map/all_gather | solution.py:795
  10.0 17.4 %collective-permute-start.1 = (bf16[160,2048]{1,0:T(8,128)(2,1)S(1)}, bf16[160,2048]{1,0:T(8,128)(2,1)S(1)}, u32[]{:S(2)}, u32[]{:S(2)}) collective-permute-start(bf16[160,2048]{1,0:T(8,128)(2,1)S(1)} %fusion.2.n0.refs_0_.refs_5_), channel_id=1, source_target_pairs={{0,2},{2,4},{4,6},{6,0},{1,3},{3,5},{5,7},{7,1},{8,10},{10,12},{12... | collective-permute-start | bytes 1966088 | tf_op jit(solution)/shard_map/ppermute | solution.py:70
  13.0 17.9 %collective-permute-start.2 = (bf16[512,640]{1,0:T(8,128)(2,1)}, bf16[512,640]{1,0:T(8,128)(2,1)S(1)}, u32[]{:S(2)}, u32[]{:S(2)}) collective-permute-start(bf16[512,640]{1,0:T(8,128)(2,1)} %constant_dynamic-slice_fusion.4), channel_id=1, source_target_pairs={{0,1},{1,0},{2,3},{3,2},{4,5},{5,4},{6,7},{7,6},{8,9},{9,8},{10,11... | collective-permute-start | bytes 1966088 | tf_op jit(solution)/shard_map/ppermute | solution.py:121
  39.9 17.2 %collective-permute-start.20 = (bf16[128,2944]{1,0:T(8,128)(2,1)S(1)}, bf16[128,2944]{1,0:T(8,128)(2,1)S(1)}, u32[]{:S(2)}, u32[]{:S(2)}) collective-permute-start(bf16[128,2944]{1,0:T(8,128)(2,1)S(1)} %pad_maximum_fusion), channel_id=1, source_target_pairs={{0,17},{1,16},{16,1},{17,0},{2,19},{3,18},{18,3},{19,2},{4,21},{5,... | collective-permute-start | bytes 2261000 | tf_op jit(solution)/shard_map/ppermute | solution.py:782
  58.0 303.3 %reduce-scatter.2.cloned.1.call-start = ((), (), s32[]{:S(2)}) async-start(), calls=%async_computation.2 | async-start | bytes 17842176 | tf_op jit(solution)/shard_map/reduce_scatter | solution.py:818
  58.0 12.9 %collective-permute-start = (bf16[160,2048]{1,0:T(8,128)(2,1)S(1)}, bf16[160,2048]{1,0:T(8,128)(2,1)S(1)}, u32[]{:S(2)}, u32[]{:S(2)}) collective-permute-start(bf16[160,2048]{1,0:T(8,128)(2,1)S(1)} %fusion.2.n0.refs_0_.refs_5_), channel_id=1, source_target_pairs={{0,6},{2,0},{4,2},{6,4},{1,7},{3,1},{5,3},{7,5},{8,14},{10,8},{12,... | collective-permute-start | bytes 1966088 | tf_op jit(solution)/shard_map/ppermute | solution.py:71
  71.0 14.5 %collective-permute-start.5 = (bf16[512,640]{1,0:T(8,128)(2,1)S(1)}, bf16[512,640]{1,0:T(8,128)(2,1)S(1)}, u32[]{:S(2)}, u32[]{:S(2)}) collective-permute-start(bf16[512,640]{1,0:T(8,128)(2,1)S(1)} %collective-permute-done.2.w1), channel_id=1, source_target_pairs={{0,8},{8,0},{1,9},{9,1},{2,10},{10,2},{3,11},{11,3},{4,12},{12,4},... | collective-permute-start | bytes 1966088 | tf_op jit(solution)/shard_map/ppermute | solution.py:778
  76.0 9.4 %collective-permute-start.4 = (bf16[80,2048]{1,0:T(8,128)(2,1)S(1)}, bf16[80,2048]{1,0:T(8,128)(2,1)S(1)}, u32[]{:S(2)}, u32[]{:S(2)}) collective-permute-start(bf16[80,2048]{1,0:T(8,128)(2,1)S(1)} %slice.81), channel_id=1, source_target_pairs={{0,6},{2,0},{4,2},{6,4},{1,7},{3,1},{5,3},{7,5},{8,14},{10,8},{12,... | collective-permute-start | bytes 983048 | tf_op jit(solution)/shard_map/ppermute | solution.py:74
  78.6 20.0 %collective-permute-start.10 = (bf16[128,2048]{1,0:T(8,128)(2,1)S(1)}, bf16[128,2048]{1,0:T(8,128)(2,1)}, u32[]{:S(2)}, u32[]{:S(2)}) collective-permute-start(bf16[128,2048]{1,0:T(8,128)(2,1)S(1)} %constant_dynamic-slice_fusion.3), channel_id=1, source_target_pairs={{0,1},{1,0},{2,3},{3,2},{4,5},{5,4},{6,7},{7,6},{8,9},{9,8},{10,11... | collective-permute-start | bytes 1572872 | tf_op jit(solution)/shard_map/ppermute | solution.py:121
  94.7 23.8 %collective-permute-start.9 = (bf16[160,2048]{1,0:T(8,128)(2,1)S(1)}, bf16[160,2048]{1,0:T(8,128)(2,1)S(1)}, u32[]{:S(2)}, u32[]{:S(2)}) collective-permute-start(bf16[160,2048]{1,0:T(8,128)(2,1)S(1)} %copy-done.9), channel_id=1, source_target_pairs={{0,2},{2,4},{4,6},{6,0},{1,3},{3,5},{5,7},{7,1},{8,10},{10,12},{12... | collective-permute-start | bytes 1966088 | tf_op jit(solution)/shard_map/ppermute | solution.py:79
  94.7 31.7 %collective-permute-start.8 = (bf16[160,2048]{1,0:T(8,128)(2,1)S(1)}, bf16[160,2048]{1,0:T(8,128)(2,1)S(1)}, u32[]{:S(2)}, u32[]{:S(2)}) collective-permute-start(bf16[160,2048]{1,0:T(8,128)(2,1)S(1)} %copy-done.9), channel_id=1, source_target_pairs={{0,4},{2,6},{4,0},{6,2},{1,5},{3,7},{5,1},{7,3},{8,12},{10,14},{12... | collective-permute-start | bytes 1966088 | tf_op jit(solution)/shard_map/ppermute | solution.py:79
  98.6 27.8 %collective-permute-start.7 = (bf16[160,2048]{1,0:T(8,128)(2,1)S(1)}, bf16[160,2048]{1,0:T(8,128)(2,1)S(1)}, u32[]{:S(2)}, u32[]{:S(2)}) collective-permute-start(bf16[160,2048]{1,0:T(8,128)(2,1)S(1)} %copy-done.9), channel_id=1, source_target_pairs={{0,6},{2,0},{4,2},{6,4},{1,7},{3,1},{5,3},{7,5},{8,14},{10,8},{12,... | collective-permute-start | bytes 1966088 | tf_op jit(solution)/shard_map/ppermute | solution.py:79
  98.6 29.6 %collective-permute-start.11 = (bf16[128,2048]{1,0:T(8,128)(2,1)}, bf16[128,2048]{1,0:T(8,128)(2,1)}, u32[]{:S(2)}, u32[]{:S(2)}) collective-permute-start(bf16[128,2048]{1,0:T(8,128)(2,1)} %collective-permute-done.10.w1), channel_id=1, source_target_pairs={{0,8},{8,0},{1,9},{9,1},{2,10},{10,2},{3,11},{11,3},{4,12},{12,4},... | collective-permute-start | bytes 1572872 | tf_op jit(solution)/shard_map/ppermute | solution.py:126
  133.0 9.2 %collective-permute-start.14 = (bf16[80,2048]{1,0:T(8,128)(2,1)}, bf16[80,2048]{1,0:T(8,128)(2,1)}, u32[]{:S(2)}, u32[]{:S(2)}) collective-permute-start(bf16[80,2048]{1,0:T(8,128)(2,1)} %get-tuple-element.84), channel_id=1, source_target_pairs={{0,6},{2,0},{4,2},{6,4},{1,7},{3,1},{5,3},{7,5},{8,14},{10,8},{12,... | collective-permute-start | bytes 983048 | tf_op jit(solution)/shard_map/ppermute | solution.py:90
  135.5 33.9 %collective-permute-start.21 = (bf16[352,2048]{1,0:T(8,128)(2,1)S(1)}, bf16[352,2048]{1,0:T(8,128)(2,1)S(1)}, u32[]{:S(2)}, u32[]{:S(2)}) collective-permute-start(bf16[352,2048]{1,0:T(8,128)(2,1)S(1)} %constant_dynamic-slice_fusion), channel_id=1, source_target_pairs={{0,1},{1,0},{2,3},{3,2},{4,5},{5,4},{6,7},{7,6},{8,9},{9,8},{10,11... | collective-permute-start | bytes 4325384 | tf_op jit(solution)/shard_map/ppermute | solution.py:121
  137.9 9.4 %collective-permute-start.12 = (bf16[80,2048]{1,0:T(8,128)(2,1)S(1)}, bf16[80,2048]{1,0:T(8,128)(2,1)S(1)}, u32[]{:S(2)}, u32[]{:S(2)}) collective-permute-start(bf16[80,2048]{1,0:T(8,128)(2,1)S(1)} %copy-done.46), channel_id=1, source_target_pairs={{0,2},{2,4},{4,6},{6,0},{1,3},{3,5},{5,7},{7,1},{8,10},{10,12},{12... | collective-permute-start | bytes 983048 | tf_op jit(solution)/shard_map/ppermute | solution.py:89
  143.4 16.2 %collective-permute-start.15 = (bf16[160,2048]{1,0:T(8,128)(2,1)S(1)}, bf16[160,2048]{1,0:T(8,128)(2,1)S(1)}, u32[]{:S(2)}, u32[]{:S(2)}) collective-permute-start(bf16[160,2048]{1,0:T(8,128)(2,1)S(1)} %pad_maximum_fusion.2), channel_id=1, source_target_pairs={{0,6},{2,0},{4,2},{6,4},{1,7},{3,1},{5,3},{7,5},{8,14},{10,8},{12,... | collective-permute-start | bytes 1966088 | tf_op jit(solution)/shard_map/ppermute | solution.py:94
  147.5 15.5 %collective-permute-start.13 = (bf16[160,2048]{1,0:T(8,128)(2,1)S(1)}, bf16[160,2048]{1,0:T(8,128)(2,1)S(1)}, u32[]{:S(2)}, u32[]{:S(2)}) collective-permute-start(bf16[160,2048]{1,0:T(8,128)(2,1)S(1)} %pad_maximum_fusion.1), channel_id=1, source_target_pairs={{0,2},{2,4},{4,6},{6,0},{1,3},{3,5},{5,7},{7,1},{8,10},{10,12},{12... | collective-permute-start | bytes 1966088 | tf_op jit(solution)/shard_map/ppermute | solution.py:93
  169.5 30.7 %collective-permute-start.22 = (bf16[352,2048]{1,0:T(8,128)(2,1)S(1)}, bf16[352,2048]{1,0:T(8,128)(2,1)}, u32[]{:S(2)}, u32[]{:S(2)}) collective-permute-start(bf16[352,2048]{1,0:T(8,128)(2,1)S(1)} %collective-permute-done.21.w1), channel_id=1, source_target_pairs={{0,8},{8,0},{1,9},{9,1},{2,10},{10,2},{3,11},{11,3},{4,12},{12,4},... | collective-permute-start | bytes 4325384 | tf_op jit(solution)/shard_map/ppermute | solution.py:126
  171.3 17.6 %collective-permute-start.17 = (bf16[160,2048]{1,0:T(8,128)(2,1)S(1)}, bf16[160,2048]{1,0:T(8,128)(2,1)S(1)}, u32[]{:S(2)}, u32[]{:S(2)}) collective-permute-start(bf16[160,2048]{1,0:T(8,128)(2,1)S(1)} %multiply_convert_fusion.n0.refs_0_.refs_5_), channel_id=1, source_target_pairs={{0,2},{2,4},{4,6},{6,0},{1,3},{3,5},{5,7},{7,1},{8,10},{10,12},{12... | collective-permute-start | bytes 1966088 | tf_op jit(solution)/shard_map/ppermute | solution.py:70
  171.4 17.7 %collective-permute-start.16 = (bf16[160,2048]{1,0:T(8,128)(2,1)S(1)}, bf16[160,2048]{1,0:T(8,128)(2,1)S(1)}, u32[]{:S(2)}, u32[]{:S(2)}) collective-permute-start(bf16[160,2048]{1,0:T(8,128)(2,1)S(1)} %multiply_convert_fusion.n0.refs_0_.refs_5_), channel_id=1, source_target_pairs={{0,6},{2,0},{4,2},{6,4},{1,7},{3,1},{5,3},{7,5},{8,14},{10,8},{12,... | collective-permute-start | bytes 1966088 | tf_op jit(solution)/shard_map/ppermute | solution.py:71
  189.0 9.7 %collective-permute-start.18 = (bf16[80,2048]{1,0:T(8,128)(2,1)S(1)}, bf16[80,2048]{1,0:T(8,128)(2,1)S(1)}, u32[]{:S(2)}, u32[]{:S(2)}) collective-permute-start(bf16[80,2048]{1,0:T(8,128)(2,1)S(1)} %slice.82), channel_id=1, source_target_pairs={{0,2},{2,4},{4,6},{6,0},{1,3},{3,5},{5,7},{7,1},{8,10},{10,12},{12... | collective-permute-start | bytes 983048 | tf_op jit(solution)/shard_map/ppermute | solution.py:73
  189.1 9.6 %collective-permute-start.19 = (bf16[80,2048]{1,0:T(8,128)(2,1)S(1)}, bf16[80,2048]{1,0:T(8,128)(2,1)S(1)}, u32[]{:S(2)}, u32[]{:S(2)}) collective-permute-start(bf16[80,2048]{1,0:T(8,128)(2,1)S(1)} %slice.83), channel_id=1, source_target_pairs={{0,6},{2,0},{4,2},{6,4},{1,7},{3,1},{5,3},{7,5},{8,14},{10,8},{12,... | collective-permute-start | bytes 983048 | tf_op jit(solution)/shard_map/ppermute | solution.py:74
  242.1 266.2 %all-gather.5.cloned.1.call-start = ((), (), s32[]{:S(2)}) async-start(), calls=%async_computation.3 | async-start | bytes 9191424 | tf_op jit(solution)/shard_map/all_gather | solution.py:839
  265.8 14.5 %collective-permute-start.26 = (bf16[160,2048]{1,0:T(8,128)(2,1)S(1)}, bf16[160,2048]{1,0:T(8,128)(2,1)S(1)}, u32[]{:S(2)}, u32[]{:S(2)}) collective-permute-start(bf16[160,2048]{1,0:T(8,128)(2,1)S(1)} %pad_maximum_fusion.4), channel_id=1, source_target_pairs={{0,6},{2,0},{4,2},{6,4},{1,7},{3,1},{5,3},{7,5},{8,14},{10,8},{12,... | collective-permute-start | bytes 1966088 | tf_op jit(solution)/shard_map/ppermute | solution.py:94
  270.5 14.4 %collective-permute-start.24 = (bf16[160,2048]{1,0:T(8,128)(2,1)S(1)}, bf16[160,2048]{1,0:T(8,128)(2,1)S(1)}, u32[]{:S(2)}, u32[]{:S(2)}) collective-permute-start(bf16[160,2048]{1,0:T(8,128)(2,1)S(1)} %pad_maximum_fusion.3), channel_id=1, source_target_pairs={{0,2},{2,4},{4,6},{6,0},{1,3},{3,5},{5,7},{7,1},{8,10},{10,12},{12... | collective-permute-start | bytes 1966088 | tf_op jit(solution)/shard_map/ppermute | solution.py:93
  286.8 12.3 %collective-permute-start.29 = (bf16[160,2048]{1,0:T(8,128)(2,1)S(1)}, bf16[160,2048]{1,0:T(8,128)(2,1)S(1)}, u32[]{:S(2)}, u32[]{:S(2)}) collective-permute-start(bf16[160,2048]{1,0:T(8,128)(2,1)S(1)} %get-tuple-element.135.b0.refs_10_), channel_id=1, source_target_pairs={{0,6},{2,0},{4,2},{6,4},{1,7},{3,1},{5,3},{7,5},{8,14},{10,8},{12,... | collective-permute-start | bytes 1966088 | tf_op jit(solution)/shard_map/ppermute | solution.py:71
  287.7 13.4 %collective-permute-start.27 = (bf16[160,2048]{1,0:T(8,128)(2,1)S(1)}, bf16[160,2048]{1,0:T(8,128)(2,1)S(1)}, u32[]{:S(2)}, u32[]{:S(2)}) collective-permute-start(bf16[160,2048]{1,0:T(8,128)(2,1)S(1)} %get-tuple-element.135.b0.refs_10_), channel_id=1, source_target_pairs={{0,2},{2,4},{4,6},{6,0},{1,3},{3,5},{5,7},{7,1},{8,10},{10,12},{12... | collective-permute-start | bytes 1966088 | tf_op jit(solution)/shard_map/ppermute | solution.py:70
  299.2 13.1 %collective-permute-start.30 = (bf16[80,2048]{1,0:T(8,128)(2,1)S(1)}, bf16[80,2048]{1,0:T(8,128)(2,1)}, u32[]{:S(2)}, u32[]{:S(2)}) collective-permute-start(bf16[80,2048]{1,0:T(8,128)(2,1)S(1)} %slice.85), channel_id=1, source_target_pairs={{0,6},{2,0},{4,2},{6,4},{1,7},{3,1},{5,3},{7,5},{8,14},{10,8},{12,... | collective-permute-start | bytes 983048 | tf_op jit(solution)/shard_map/ppermute | solution.py:74
  302.1 10.2 %collective-permute-start.28 = (bf16[80,2048]{1,0:T(8,128)(2,1)}, bf16[80,2048]{1,0:T(8,128)(2,1)}, u32[]{:S(2)}, u32[]{:S(2)}) collective-permute-start(bf16[80,2048]{1,0:T(8,128)(2,1)} %slice.84), channel_id=1, source_target_pairs={{0,2},{2,4},{4,6},{6,0},{1,3},{3,5},{5,7},{7,1},{8,10},{10,12},{12... | collective-permute-start | bytes 983048 | tf_op jit(solution)/shard_map/ppermute | solution.py:73
  361.3 16.6 %collective-permute-start.31 = (bf16[160,2048]{1,0:T(8,128)(2,1)}, bf16[160,2048]{1,0:T(8,128)(2,1)}, u32[]{:S(2)}, u32[]{:S(2)}) collective-permute-start(bf16[160,2048]{1,0:T(8,128)(2,1)} %get-tuple-element.100), channel_id=1, source_target_pairs={{0,2},{2,4},{4,6},{6,0},{1,3},{3,5},{5,7},{7,1},{8,10},{10,12},{12... | collective-permute-start | bytes 1966088 | tf_op jit(solution)/shard_map/ppermute | solution.py:83
  363.1 30.4 %collective-permute-start.32 = (bf16[160,2048]{1,0:T(8,128)(2,1)}, bf16[160,2048]{1,0:T(8,128)(2,1)}, u32[]{:S(2)}, u32[]{:S(2)}) collective-permute-start(bf16[160,2048]{1,0:T(8,128)(2,1)} %get-tuple-element.102), channel_id=1, source_target_pairs={{0,4},{2,6},{4,0},{6,2},{1,5},{3,7},{5,1},{7,3},{8,12},{10,14},{12... | collective-permute-start | bytes 1966088 | tf_op jit(solution)/shard_map/ppermute | solution.py:83
  365.5 28.0 %collective-permute-start.33 = (bf16[160,2048]{1,0:T(8,128)(2,1)}, bf16[160,2048]{1,0:T(8,128)(2,1)}, u32[]{:S(2)}, u32[]{:S(2)}) collective-permute-start(bf16[160,2048]{1,0:T(8,128)(2,1)} %get-tuple-element.104), channel_id=1, source_target_pairs={{0,6},{2,0},{4,2},{6,4},{1,7},{3,1},{5,3},{7,5},{8,14},{10,8},{12,... | collective-permute-start | bytes 1966088 | tf_op jit(solution)/shard_map/ppermute | solution.py:83
  375.3 45.2 %collective-permute-start.39 = (bf16[4,2,1024,128]{3,2,1,0:T(8,128)(2,1)}, bf16[4,2,1024,128]{3,2,1,0:T(8,128)(2,1)}, u32[]{:S(2)}, u32[]{:S(2)}) collective-permute-start(bf16[4,2,1024,128]{3,2,1,0:T(8,128)(2,1)} %get-tuple-element.117), channel_id=1, source_target_pairs={{0,8},{8,0},{1,9},{9,1},{2,10},{10,2},{3,11},{11,3},{4,12},{12,4},... | collective-permute-start | bytes 6291464 | tf_op jit(solution)/shard_map/ppermute | solution.py:722
  405.6 10.6 %collective-permute-start.37 = (bf16[80,2048]{1,0:T(8,128)(2,1)}, bf16[80,2048]{1,0:T(8,128)(2,1)S(1)}, u32[]{:S(2)}, u32[]{:S(2)}) collective-permute-start(bf16[80,2048]{1,0:T(8,128)(2,1)} %get-tuple-element.115), channel_id=1, source_target_pairs={{0,6},{2,0},{4,2},{6,4},{1,7},{3,1},{5,3},{7,5},{8,14},{10,8},{12,... | collective-permute-start | bytes 983048 | tf_op jit(solution)/shard_map/ppermute | solution.py:90
  409.1 11.3 %collective-permute-start.40 = (bf16[4,2,144,128]{3,2,1,0:T(8,128)(2,1)}, bf16[4,2,144,128]{3,2,1,0:T(8,128)(2,1)S(1)}, u32[]{:S(2)}, u32[]{:S(2)}) collective-permute-start(bf16[4,2,144,128]{3,2,1,0:T(8,128)(2,1)} %get-tuple-element.119), channel_id=1, source_target_pairs={{0,8},{8,0},{1,9},{9,1},{2,10},{10,2},{3,11},{11,3},{4,12},{12,4},... | collective-permute-start | bytes 884744 | tf_op jit(solution)/shard_map/ppermute | solution.py:723
  411.8 17.4 %collective-permute-start.35 = (bf16[80,2048]{1,0:T(8,128)(2,1)}, bf16[80,2048]{1,0:T(8,128)(2,1)}, u32[]{:S(2)}, u32[]{:S(2)}) collective-permute-start(bf16[80,2048]{1,0:T(8,128)(2,1)} %get-tuple-element.113), channel_id=1, source_target_pairs={{0,2},{2,4},{4,6},{6,0},{1,3},{3,5},{5,7},{7,1},{8,10},{10,12},{12... | collective-permute-start | bytes 983048 | tf_op jit(solution)/shard_map/ppermute | solution.py:89
  417.2 60.9 %collective-permute-start.38 = (bf16[160,2048]{1,0:T(8,128)(2,1)}, bf16[160,2048]{1,0:T(8,128)(2,1)S(1)}, u32[]{:S(2)}, u32[]{:S(2)}) collective-permute-start(bf16[160,2048]{1,0:T(8,128)(2,1)} %pad_maximum_fusion.6), channel_id=1, source_target_pairs={{0,6},{2,0},{4,2},{6,4},{1,7},{3,1},{5,3},{7,5},{8,14},{10,8},{12,... | collective-permute-start | bytes 1966088 | tf_op jit(solution)/shard_map/ppermute | solution.py:94
  425.2 15.4 %collective-permute-start.41 = (bf16[2,1168,128]{2,1,0:T(8,128)(2,1)}, bf16[2,1168,128]{2,1,0:T(8,128)(2,1)}, u32[]{:S(2)}, u32[]{:S(2)}) collective-permute-start(bf16[2,1168,128]{2,1,0:T(8,128)(2,1)} %get-tuple-element.121), channel_id=1, source_target_pairs={{0,64},{32,96},{64,0},{96,32},{1,65},{33,97},{65,1},{97,33},{2,66}... | collective-permute-start | bytes 1794056 | tf_op jit(solution)/shard_map/ppermute | solution.py:726
  426.5 28.7 %collective-permute-start.42 = (bf16[2,1168,128]{2,1,0:T(8,128)(2,1)}, bf16[2,1168,128]{2,1,0:T(8,128)(2,1)}, u32[]{:S(2)}, u32[]{:S(2)}) collective-permute-start(bf16[2,1168,128]{2,1,0:T(8,128)(2,1)} %get-tuple-element.122), channel_id=1, source_target_pairs={{0,32},{32,64},{64,96},{96,0},{1,33},{33,65},{65,97},{97,1},{2,34}... | collective-permute-start | bytes 1794056 | tf_op jit(solution)/shard_map/ppermute | solution.py:726
  426.8 28.4 %collective-permute-start.43 = (bf16[2,1168,128]{2,1,0:T(8,128)(2,1)}, bf16[2,1168,128]{2,1,0:T(8,128)(2,1)}, u32[]{:S(2)}, u32[]{:S(2)}) collective-permute-start(bf16[2,1168,128]{2,1,0:T(8,128)(2,1)} %get-tuple-element.123), channel_id=1, source_target_pairs={{0,96},{32,0},{64,32},{96,64},{1,97},{33,1},{65,33},{97,65},{2,98}... | collective-permute-start | bytes 1794056 | tf_op jit(solution)/shard_map/ppermute | solution.py:726
  431.2 63.8 %collective-permute-start.36 = (bf16[160,2048]{1,0:T(8,128)(2,1)}, bf16[160,2048]{1,0:T(8,128)(2,1)}, u32[]{:S(2)}, u32[]{:S(2)}) collective-permute-start(bf16[160,2048]{1,0:T(8,128)(2,1)} %pad_maximum_fusion.5), channel_id=1, source_target_pairs={{0,2},{2,4},{4,6},{6,0},{1,3},{3,5},{5,7},{7,1},{8,10},{10,12},{12... | collective-permute-start | bytes 1966088 | tf_op jit(solution)/shard_map/ppermute | solution.py:93
  457.9 10.2 %collective-permute-start.46 = (bf16[1168,128]{1,0:T(8,128)(2,1)}, bf16[1168,128]{1,0:T(8,128)(2,1)}, u32[]{:S(2)}, u32[]{:S(2)}) collective-permute-start(bf16[1168,128]{1,0:T(8,128)(2,1)} %get-tuple-element.125), channel_id=1, source_target_pairs={{0,17},{1,16},{16,1},{17,0},{2,19},{3,18},{18,3},{19,2},{4,21},{5,... | collective-permute-start | bytes 897032 | tf_op jit(solution)/shard_map/ppermute | solution.py:737
  459.3 14.5 %collective-permute-start.45 = (bf16[1168,128]{1,0:T(8,128)(2,1)}, bf16[1168,128]{1,0:T(8,128)(2,1)}, u32[]{:S(2)}, u32[]{:S(2)}) collective-permute-start(bf16[1168,128]{1,0:T(8,128)(2,1)} %get-tuple-element.125), channel_id=1, source_target_pairs={{0,1},{1,0},{2,3},{3,2},{4,5},{5,4},{6,7},{7,6},{8,9},{9,8},{10,11... | collective-permute-start | bytes 897032 | tf_op jit(solution)/shard_map/ppermute | solution.py:736
  477.3 10.5 %collective-permute-start.48 = (bf16[1168,128]{1,0:T(8,128)(2,1)}, bf16[1168,128]{1,0:T(8,128)(2,1)S(1)}, u32[]{:S(2)}, u32[]{:S(2)}) collective-permute-start(bf16[1168,128]{1,0:T(8,128)(2,1)} %sum_z.1.refs_0_), channel_id=1, source_target_pairs={{0,64},{32,96},{64,0},{96,32},{1,65},{33,97},{65,1},{97,33},{2,66}... | collective-permute-start | bytes 897032 | tf_op jit(solution)/shard_map/ppermute | solution.py:740
  477.5 16.7 %collective-permute-start.47 = (bf16[1168,128]{1,0:T(8,128)(2,1)}, bf16[1168,128]{1,0:T(8,128)(2,1)S(1)}, u32[]{:S(2)}, u32[]{:S(2)}) collective-permute-start(bf16[1168,128]{1,0:T(8,128)(2,1)} %sum_z.1.refs_0_), channel_id=1, source_target_pairs={{0,32},{32,64},{64,96},{96,0},{1,33},{33,65},{65,97},{97,1},{2,34}... | collective-permute-start | bytes 897032 | tf_op jit(solution)/shard_map/ppermute | solution.py:740
  478.1 18.5 %collective-permute-start.50 = (bf16[1168,128]{1,0:T(8,128)(2,1)}, bf16[1168,128]{1,0:T(8,128)(2,1)S(1)}, u32[]{:S(2)}, u32[]{:S(2)}) collective-permute-start(bf16[1168,128]{1,0:T(8,128)(2,1)} %sum_z.1.refs_0_), channel_id=1, source_target_pairs={{0,8},{8,0},{1,9},{9,1},{2,10},{10,2},{3,11},{11,3},{4,12},{12,4},... | collective-permute-start | bytes 897032 | tf_op jit(solution)/shard_map/ppermute | solution.py:741
  483.0 13.6 %collective-permute-start.53 = (bf16[1168,128]{1,0:T(8,128)(2,1)S(1)}, bf16[1168,128]{1,0:T(8,128)(2,1)S(1)}, u32[]{:S(2)}, u32[]{:S(2)}) collective-permute-start(bf16[1168,128]{1,0:T(8,128)(2,1)S(1)} %collective-permute-done.49.refs_3_), channel_id=1, source_target_pairs={{0,8},{8,0},{1,9},{9,1},{2,10},{10,2},{3,11},{11,3},{4,12},{12,4},... | collective-permute-start | bytes 897032 | tf_op jit(solution)/shard_map/ppermute | solution.py:741
  (63 other events, 639.6 us)
Sparse Core Ops, SparseCore 0:
  58.1 42.5 all-gather.2
  242.2 118.9 reduce-scatter.1
  363.0 53.8 all-gather.4

commit v4 on v3

--- a/solution.py
+++ b/solution.py
@@ -69,7 +69,8 @@
 def gather_x(v, *deps):
     from_prev = lax.ppermute(v, "x", shift(4, 1))
     from_next = lax.ppermute(v, "x", shift(4, -1))
-    send_a, send_b = tie(from_prev[:HALF], *deps), tie(from_next[HALF:], *deps)
+    send_a = tie(from_prev[:HALF], from_next, *deps)
+    send_b = tie(from_next[HALF:], from_prev, *deps)
     opp_a = lax.ppermute(send_a, "x", shift(4, 1))
     opp_b = lax.ppermute(send_b, "x", shift(4, -1))
     return (v, from_next, opp_a, opp_b, from_prev), (send_a, send_b)
@@ -149,7 +150,11 @@
             v = acc[d * BLK : (d + 1) * BLK, p * 128 : (p + 1) * 128]
             r = v * cs + swap_halves(v) * sn
             if p < 4:
-                q_ref[at, p * 128 : (p + 1) * 128] = (r * HD**-0.5).astype(BF16)
+                r = r * (HD**-0.5 * LOG2E)
+                a = (x + d) & 3
+                for k, w in enumerate((r, pltpu.roll(r, HD, 1))):
+                    head = slice((2 * p + k) * BLK, (2 * p + k + 1) * BLK)
+                    q_ref[a, head, :] = jnp.where(lo, w, 0.0).astype(BF16)
             else:
                 kv_ref[at, :] = jnp.where(lo, r, v).astype(BF16)
 
@@ -157,7 +162,7 @@
 def qkv_forward(idx, pieces, weight, cosine, sine):
     return pl.pallas_call(
         qkv_body,
-        out_shape=(sds((ROWS, AW)), sds((ROWS, 128))),
+        out_shape=(sds((4, QALL, 128)), sds((ROWS, 128))),
         in_specs=[spec(pltpu.SMEM)] + [spec()] * 10,
         out_specs=(spec(), spec()),
         scratch_shapes=[pltpu.VMEM((ROWS, D), BF16)],
@@ -167,68 +172,98 @@
     )(idx, *pieces, *weight, cosine, sine)
 
 
-def spread_keys(zh, kv_own, kv_par, kk, vv):
-    lo = low_lanes((BLK, 128))
+QALL = 8 * BLK
+PAIR = 2 * BLK
+LOG2E = 1.4426950408889634
+LN2 = 0.6931471805599453
+
+
+def split3(v):
+    a = v.astype(BF16).astype(F32)
+    b = (v - a).astype(BF16).astype(F32)
+    return a, b, v - a - b
+
+
+def with_lanes(v, parts):
+    lane = lax.broadcasted_iota(jnp.int32, v.shape, 1)
+    out = jnp.where(lane < HD, v, 0.0)
+    for k, part in enumerate(parts):
+        out = jnp.where(lane == HD + k, part, out)
+    return out
+
+
+def spread_keys(zh, kv_own, kv_par, kk, vv, fill):
+    shape = (BLK, 128)
+    lo = low_lanes(shape)
+    rest = fill(lax.broadcasted_iota(jnp.int32, shape, 1) - HD)
     for j in range(4):
         for src, off in ((kv_own, zh), (kv_par, 1 - zh)):
             v = src[j * BLK : (j + 1) * BLK, :].astype(F32)
-            w = pltpu.roll(v, HD, 1)
             at = rows_at(2 * j + off)
-            kk[at, :] = jnp.where(lo, v, w).astype(BF16)
-            vv[at, :] = jnp.where(lo, w, v).astype(BF16)
-
-
-def fill_bias(zh, j, n, first, bias):
-    t = (2 * j + zh) * BLK + lax.broadcasted_iota(jnp.int32, (BLK, n), 0)
-    u = lax.broadcasted_iota(jnp.int32, (BLK, n), 1)
-    start = first[j * BLK : (j + 1) * BLK, :]
-    value = jnp.where((u <= t) & (u >= start), 0.0, MASKED)
-    bias[0:BLK, 0:n] = value
-    bias[BLK : 2 * BLK, 0:n] = value
-
-
-def two_heads(v):
-    lo = low_lanes(v.shape)
-    zero = jnp.zeros_like(v)
-    return jnp.concatenate([jnp.where(lo, v, zero), jnp.where(lo, zero, v)], 0)
-
-
-def attend_body(idx, q, kv_own, kv_par, first, att, lse_ref, kk, vv, bias):
+            kk[at, :] = jnp.where(lo, v, rest).astype(BF16)
+            vv[at, :] = jnp.where(lo, pltpu.roll(v, HD, 1), rest).astype(BF16)
+
+
+def masked(s, zh, j, kb, first):
+    if j < 3 and kb < j:
+        return s
+    u = kb * PAIR + lax.broadcasted_iota(jnp.int32, (PAIR, QALL), 0)
+    allowed = None
+    if kb == j:
+        t = (2 * j + zh) * BLK + lax.broadcasted_iota(jnp.int32, (1, QALL), 1) % BLK
+        allowed = u <= t
+    if j == 3:
+        later = u >= first[...]
+        allowed = later if allowed is None else allowed & later
+    return jnp.where(allowed, s, MASKED)
+
+
+def attend_body(idx, q, kv_own, kv_par, first, att, qx, kk, vv, vt, s_ref, e_ref):
     x, zh = idx[0], idx[1]
-    spread_keys(zh, kv_own, kv_par, kk, vv)
+    spread_keys(zh, kv_own, kv_par, kk, vv, lambda lane: 1.0)
+    vt[...] = vv[...].T
     lo = low_lanes((BLK, 128))
-    lane = lax.broadcasted_iota(jnp.int32, (BLK, 128), 1)
     for j in range(4):
-        n = 2 * BLK * (j + 1)
-        fill_bias(zh, j, n, first, bias)
+        n = PAIR * (j + 1)
+        qj = q[j]
+        top = jnp.full((1, QALL), MASKED, F32)
+        for kb in range(j + 1):
+            rows = slice(kb * PAIR, (kb + 1) * PAIR)
+            s = masked(dot_t(kk[rows, :], qj), zh, j, kb, first)
+            s_ref[rows, :] = s
+            top = jnp.maximum(top, jnp.max(s, axis=0, keepdims=True))
+        for k in range(n // 64):
+            rows = slice(k * 64, (k + 1) * 64)
+            e_ref[rows, :] = jnp.exp2(s_ref[rows, :] - top).astype(BF16)
+        o = dot(vt[:, :n], e_ref[:n, :])
+        lse = split3(top + jnp.log(o[HD : HD + 1, :]) * LOG2E)
+        row = lax.broadcasted_iota(jnp.int32, (128, QALL), 0)
+        extra = jnp.zeros((128, QALL), F32)
+        for k, part in enumerate(lse):
+            extra = jnp.where(row == HD + k, part, extra)
+        qx[j] = (qj.astype(F32) + extra.T).astype(BF16)
+        o = o.T
+        r = pltpu.roll(o, HD, 1)
         rel = (j - x) & 3
-
-        def pair(p, lse):
-            cols = pl.ds(pl.multiple_of(p * 128, 128), 128)
-            q2 = two_heads(q[j * BLK : (j + 1) * BLK, cols])
-            s = dot_t(q2, kk[0:n, :]) + bias[:, 0:n]
-            top = jnp.max(s, axis=1, keepdims=True)
-            e = jnp.exp(s - top)
-            total = jnp.sum(e, axis=1, keepdims=True)
-            o = dot(e.astype(BF16), vv[0:n, :]) / total
-            att[rel, :, cols] = jnp.where(lo, o[:BLK], o[BLK:]).astype(BF16)
-            ls = top + jnp.log(total)
-            lse = jnp.where(lane == 2 * p, ls[:BLK], lse)
-            return jnp.where(lane == 2 * p + 1, ls[BLK:], lse)
-
-        lse_ref[j * BLK : (j + 1) * BLK, :] = lax.fori_loop(0, 4, pair, jnp.zeros((BLK, 128), F32))
+        for p in range(4):
+            even, odd = slice(2 * p * BLK, (2 * p + 1) * BLK), slice((2 * p + 1) * BLK, (2 * p + 2) * BLK)
+            num = jnp.where(lo, o[even], r[odd])
+            den = jnp.where(lo, r[even], o[odd])
+            att[rel, :, p * 128 : (p + 1) * 128] = (num / den).astype(BF16)
 
 
 def attend(idx, q, kv_own, kv_par, first):
     return pl.pallas_call(
         attend_body,
-        out_shape=(sds((4, BLK, AW)), sds((ROWS, 128), F32)),
+        out_shape=(sds((4, BLK, AW)), sds((4, QALL, 128))),
         in_specs=[spec(pltpu.SMEM)] + [spec()] * 4,
         out_specs=(spec(), spec()),
         scratch_shapes=[
             pltpu.VMEM((CAP, 128), BF16),
             pltpu.VMEM((CAP, 128), BF16),
-            pltpu.VMEM((2 * BLK, CAP), F32),
+            pltpu.VMEM((128, CAP), BF16),
+            pltpu.VMEM((CAP, QALL), F32),
+            pltpu.VMEM((CAP, QALL), BF16),
         ],
         compiler_params=params(),
         cost_estimate=cost(1.2e10, 3e6),
@@ -261,12 +296,16 @@
     )(idx, att, *weight)
 
 
+def stack_heads(v):
+    return v, pltpu.roll(v, HD, 1)
+
+
 def attend_back_body(
-    idx, q, kv_own, kv_par, first, lse_ref, att, cosine, sine, b0, b1, b2a, b2b, b3, w0, w1, w2,
-    dq_ref, dkv_own, dkv_par, kk, vv, bias, dout, dkk, dvv,
+    idx, qx, kv_own, kv_par, first, att, cosine, sine, b0, b1, b2a, b2b, b3, w0, w1, w2,
+    dq_ref, dkv_own, dkv_par, kk, vv, dout, do_all, dkk, dvv, e_ref, ds_ref, dq_acc,
 ):
     x, zh = idx[0], idx[1]
-    spread_keys(zh, kv_own, kv_par, kk, vv)
+    spread_keys(zh, kv_own, kv_par, kk, vv, lambda lane: jnp.where(lane < 3, -1.0, 0.0))
     s0, s1, s2 = weight_rows(idx, AW // 2)
     for d in range(4):
         if d == 2:
@@ -276,69 +315,68 @@
         at = rows_at((x + d) & 3)
         for s, w in ((s0, w0), (s1, w1), (s2, w2)):
             dout[at, s] = dot_t(rows, w[...]).astype(BF16)
-    dkk[...] = jnp.zeros_like(dkk)
-    dvv[...] = jnp.zeros_like(dvv)
     lo = low_lanes((BLK, 128))
-    lane = lax.broadcasted_iota(jnp.int32, (BLK, 128), 1)
     for j in range(4):
-        n = 2 * BLK * (j + 1)
-        fill_bias(zh, j, n, first, bias)
         rel = (j - x) & 3
-        lse_all = lse_ref[j * BLK : (j + 1) * BLK, :]
-
-        def pair(p, carry):
-            cols = pl.ds(pl.multiple_of(p * 128, 128), 128)
-            q2 = two_heads(q[j * BLK : (j + 1) * BLK, cols])
-            do = dout[j * BLK : (j + 1) * BLK, cols]
-            do2 = two_heads(do)
-            prod = two_heads(do.astype(F32) * att[rel, :, cols].astype(F32))
-            delta = jnp.sum(prod, axis=1, keepdims=True)
-            ls = jnp.concatenate(
-                [
-                    jnp.sum(jnp.where(lane == 2 * p, lse_all, 0.0), axis=1, keepdims=True),
-                    jnp.sum(jnp.where(lane == 2 * p + 1, lse_all, 0.0), axis=1, keepdims=True),
-                ],
-                0,
-            )
-            s = dot_t(q2, kk[0:n, :]) + bias[:, 0:n]
-            e = jnp.exp(s - ls)
-            dp = dot_t(do2, vv[0:n, :])
-            ds = (e * (dp - delta)).astype(BF16)
-            dvv[0:n, :] += t_dot(e.astype(BF16), do2)
-            dkk[0:n, :] += t_dot(ds, q2)
-            dq = dot(ds, kk[0:n, :]) * HD**-0.5
-            v = jnp.where(lo, dq[:BLK], dq[BLK:])
-            here = slice(j * BLK, (j + 1) * BLK)
-            dq_ref[rel, :, cols] = (v * cosine[here, :] - swap_halves(v) * sine[here, :]).astype(BF16)
-            return carry
-
-        lax.fori_loop(0, 4, pair, 0)
+        here = slice(j * BLK, (j + 1) * BLK)
+        for p in range(4):
+            cols = slice(p * 128, (p + 1) * 128)
+            do = dout[here, cols].astype(F32)
+            prod = do * att[rel, :, cols].astype(F32)
+            for k, (v, w) in enumerate(zip(stack_heads(do), stack_heads(prod))):
+                delta = jnp.sum(jnp.where(lo, w, 0.0), axis=1, keepdims=True)
+                head = slice((2 * p + k) * BLK, (2 * p + k + 1) * BLK)
+                do_all[head, :] = with_lanes(v, split3(delta)).astype(BF16)
+        for kb in range(j + 1):
+            rows = slice(kb * PAIR, (kb + 1) * PAIR)
+            e = jnp.exp2(masked(dot_t(kk[rows, :], qx[j]), zh, j, kb, first))
+            e_ref[...] = e.astype(BF16)
+            ds_ref[...] = (e * dot_t(vv[rows, :], do_all[...])).astype(BF16)
+            dv = dot(e_ref[...], do_all[...])
+            dk = dot(ds_ref[...], qx[j])
+            dq = t_dot(ds_ref[...], kk[rows, :])
+            if kb == j:
+                dvv[rows, :], dkk[rows, :] = dv, dk
+            else:
+                dvv[rows, :] += dv
+                dkk[rows, :] += dk
+            if kb == 0:
+                dq_acc[...] = dq
+            else:
+                dq_acc[...] += dq
+        for p in range(4):
+            even, odd = slice(2 * p * BLK, (2 * p + 1) * BLK), slice((2 * p + 1) * BLK, (2 * p + 2) * BLK)
+            v = jnp.where(lo, dq_acc[even, :], pltpu.roll(dq_acc[odd, :], HD, 1)) * HD**-0.5
+            v = v * cosine[here, :] - swap_halves(v) * sine[here, :]
+            dq_ref[rel, :, p * 128 : (p + 1) * 128] = v.astype(BF16)
     for j in range(4):
         for dst, off in ((dkv_own, zh), (dkv_par, 1 - zh)):
             at = rows_at(2 * j + off)
-            dk, dv = dkk[at, :], dvv[at, :]
-            both = jnp.where(lo, dk + pltpu.roll(dk, HD, 1), dv + pltpu.roll(dv, HD, 1))
+            both = jnp.where(lo, dkk[at, :] * LN2, pltpu.roll(dvv[at, :], HD, 1))
             dst[j * BLK : (j + 1) * BLK, :] = both.astype(dst.dtype)
 
 
-def attend_back(idx, q, kv_own, kv_par, first, lse, att, cosine, sine, branch, weight):
+def attend_back(idx, qx, kv_own, kv_par, first, att, cosine, sine, branch, weight):
     return pl.pallas_call(
         attend_back_body,
         out_shape=(sds((4, BLK, AW)), sds((ROWS, 128), F32), sds((ROWS, 128))),
-        in_specs=[spec(pltpu.SMEM)] + [spec()] * 16,
+        in_specs=[spec(pltpu.SMEM)] + [spec()] * 15,
         out_specs=(spec(),) * 3,
         scratch_shapes=[
             pltpu.VMEM((CAP, 128), BF16),
             pltpu.VMEM((CAP, 128), BF16),
-            pltpu.VMEM((2 * BLK, CAP), F32),
             pltpu.VMEM((ROWS, AW), BF16),
+            pltpu.VMEM((QALL, 128), BF16),
             pltpu.VMEM((CAP, 128), F32),
             pltpu.VMEM((CAP, 128), F32),
+            pltpu.VMEM((PAIR, QALL), BF16),
+            pltpu.VMEM((PAIR, QALL), BF16),
+            pltpu.VMEM((QALL, 128), F32),
         ],
         compiler_params=params(),
         cost_estimate=cost(3e10, 8e6),
         name="attend_back",
-    )(idx, q, kv_own, kv_par, first, lse, att, cosine, sine, *branch, *weight)
+    )(idx, qx, kv_own, kv_par, first, att, cosine, sine, *branch, *weight)
 
 
 def qkv_back_body(
@@ -776,13 +814,14 @@
     qkv_got = fetch_half(qkv_weight, core)
     normed_one, sent = gather_x((tok * s_one * gain_one).astype(BF16), qkv_got)
     qkv_all = qkv_weight, qkv_got, lax.ppermute(tie(qkv_got, *sent), "core", shift(2, 1))
+    out_all = fetch_partner(out_weight, core, *sent)
     rows = DH // 8
     mine = lambda w: lax.dynamic_slice_in_dim(w, (y * 2 + core) * rows, rows, 0)
     cross = [(2 * a + b, 2 * (1 - a) + (1 - b)) for a in range(2) for b in range(2)]
     gate_up = lax.ppermute(
         jnp.concatenate(
             [
-                tie(mine(gate_weight), normed_one[2]),
+                tie(mine(gate_weight), out_all[1], normed_one[2], normed_one[3]),
                 jnp.zeros((rows, GAP - FF4), BF16),
                 mine(up_weight),
             ],
@@ -791,13 +830,11 @@
         ("zl", "zh"),
         cross,
     )
-    out_all = fetch_partner(out_weight, core, *sent)
-    gate_up = lax.all_gather(gate_up, ("y", "core"), axis=0, tiled=True)
     cots = gather_direct(tie(cotangent, normed_one[2]))
 
     begin, position = replica_layout(seq_lengths, seq_replica, (y * 2 + zl) * 2 + core)
     half_rows = lambda v: lax.dynamic_index_in_dim(v.reshape(4, 2, BLK), zh, 1, False).reshape(ROWS, 1)
-    first = half_rows(begin)
+    first = jnp.tile(half_rows(begin)[3 * BLK :, 0], 8).reshape(1, QALL)
     lane = jnp.arange(128, dtype=jnp.int32)
     frequency = ROTARY_BASE ** (-(lane % 32).astype(F32) * (2.0 / HD))
     angles = half_rows(position).astype(F32) * frequency[None, :]
@@ -806,10 +843,11 @@
 
     q, kv_own = qkv_forward(idx, normed_one, qkv_all, cosine, sine)
     kv_par = lax.ppermute(kv_own, "zh", shift(2, 1))
+    gate_up = lax.all_gather(tie(gate_up, kv_par), ("y", "core"), axis=0, tiled=True)
     down_all = fetch_partner(down_weight, core, kv_par)
-    att, lse = attend(idx, q, kv_own, kv_par, first)
-    att = tie(att, *cots)
-    after_attn = tok + scatter_x(out_project(idx, att, out_all))
+    att, qx = attend(idx, q, kv_own, kv_par, first)
+    parts = [tie(p, *cots) for p in out_project(idx, att, out_all)]
+    after_attn = tok + scatter_x(parts)
 
     r_two = inverse_rms(after_attn)
     normed_two, _ = gather_x((after_attn * r_two * gain_two).astype(BF16))
@@ -823,22 +861,22 @@
     after_grad = cotangent.astype(F32) + back_two
     branch, _ = gather_x(after_grad.astype(BF16))
     layer_parts = down_project(idx, tie(hid, after_grad), down_all)
-    layer_parts = [tie(p, branch[2], branch[3]) for p in layer_parts]
-    layer_out = after_attn + scatter_direct(layer_parts)
     att = tie(att, *layer_parts)
     dqm, dkv_own, dkv_par = attend_back(
-        idx, q, kv_own, kv_par, first, lse, att, cosine, sine, branch, out_all
+        idx, qx, kv_own, kv_par, first, att, cosine, sine, branch, out_all
     )
     dkv_got = lax.ppermute(dkv_par, "zh", shift(2, 1))
     tail = attn_grads(idx, normed_one, branch, dqm.reshape(ROWS, AW), att.reshape(ROWS, AW))
-    layer_out = layer_out.astype(BF16)
+    dkv_got = tie(dkv_got, tail[0])
     *tail_kv, parts = qkv_back(
-        idx, dqm, tie(dkv_own, layer_out), dkv_got, cosine, sine, qkv_all, normed_one, gain_one,
+        idx, dqm, dkv_own, dkv_got, cosine, sine, qkv_all, normed_one, gain_one,
         gain_grad_two,
     )
     grads = lax.all_gather(tie(grads, dkv_got), ("zl", "y", "core"), axis=0, tiled=True)
     grad_gate, grad_up, grad_down = unpack(grads)
     d_one = scatter_x(parts)
+    layer_parts = [tie(p, d_one) for p in layer_parts]
+    layer_out = (after_attn + scatter_direct(layer_parts)).astype(BF16)
     back_one, _ = norm_back(tok, s_one, gain_one, d_one)
     input_grad = (after_grad + back_one).astype(BF16)
 

time: 537 us -> 512 us (0.953)
  waiting for transfers between devices: 220 us -> 204 us
  Pallas kernels: 167 us -> 152 us
  starting transfers between devices: 85.8 us -> 92.7 us
    ppermute x3, waiting for transfers between devices: 24.1 us -> 41.1 us  [sum_tail(): got = [lax.ppermute(g[s], 'y', shift(4, s)) for s in (2, 1, 3)]]
    ppermute x1, waiting for transfers between devices: 14.6 us -> 0.01 us  [on_device(): lax.ppermute(jnp.concatenate([tie(mine(gate_weight), out_all[1], normed_o...]
    ppermute x3, waiting for transfers between devices: 21.3 us -> 7.39 us  [gather_x(): from_next = lax.ppermute(v, 'x', shift(4, -1))]
    ppermute x3, waiting for transfers between devices: 21.7 us -> 10.8 us  [scatter_x(): from_next = lax.ppermute(q3, 'x', shift(4, -1))]
    ppermute x3, waiting for transfers between devices: 12.3 us -> 3.5 us  [gather_x(): opp_a = lax.ppermute(send_a, 'x', shift(4, 1))]
    pallas_call x2, Pallas kernels: 23.7 us -> 15.5 us  [the longest x1 8.64 us: attend(): pl.pallas_call(attend_body, out_shape=(sds((4, BLK, AW)), sds((4, QALL, 1...]
    ppermute x3, waiting for transfers between devices: 8.09 us -> 15.9 us  [scatter_x(): from_prev = lax.ppermute(q1, 'x', shift(4, 1))]
    pallas_call x1, Pallas kernels: 26.1 us -> 20.1 us  [attend_back(): pl.pallas_call(attend_back_body, out_shape=(sds((4, BLK, AW)), sds((ROWS,...]
  transfers between devices with their start and end apart: 60 -> 60, of which waited for: 34 -> 31; matrix products, arithmetic and copies ran while one was open for 6% -> 6% of each run, Pallas kernels for 21% -> 19%
where the time goes in v4:
time: 512 us; the launch traced here: 504 us
  waiting for transfers between devices  204 us (40%)
  Pallas kernels  152 us (30%)
  starting transfers between devices  92.7 us (18%)
  local copies, waits for them, and re-layouts  20.7 us (4%)
  other arithmetic  19.5 us (4%)
  between operations  14.8 us (3%)
    ppermute x3, waiting for transfers between devices, sum_tail(): got = [lax.ppermute(g[s], 'y', shift(4, s)) for s in (2, 1, 3)]  41.1 us
    ppermute x3, waiting for transfers between devices, gather_x(): from_prev = lax.ppermute(v, 'x', shift(4, 1))  25.6 us
    pallas_call x1, Pallas kernels, ffn_grads(): pl.pallas_call(ffn_grads_body, grid=(8,), out_shape=sds((2, 16, PIECE, 12...  21.1 us
    pallas_call x1, Pallas kernels, ffn(): pl.pallas_call(ffn_body, grid=(TILES,), out_shape=(sds((ROWS, FF4)),) * 3...  20.8 us
    pallas_call x1, Pallas kernels, attend_back(): pl.pallas_call(attend_back_body, out_shape=(sds((4, BLK, AW)), sds((ROWS,...  20.1 us
    ppermute x3, waiting for transfers between devices, scatter_direct(): got = [lax.ppermute(parts[s], 'x', shift(4, s)) for s in (1, 2, 3)]  17.7 us
    reduce_scatter x1, waiting for transfers between devices, on_device(): lax.psum_scatter(own_grads.reshape(32, PIECE, 128), ('zh', 'zl', 'y', 'co...  17.2 us
    ppermute x3, waiting for transfers between devices, scatter_x(): from_prev = lax.ppermute(q1, 'x', shift(4, 1))  15.9 us
  transfers between devices with their start and end apart: 60, of which 31 were waited for; matrix products, arithmetic and copies ran while one was open for 6% of the time, Pallas kernels for 19%

profile of v4, /device:TPU:1, one launch (start us, length us, event | category | flops | bytes accessed | tf_op | source)
XLA Modules:
  0.0 503.6 jit_solution(11496012604108241862)
XLA Ops:
  14.4 3.7 collective-permute-start.2
  20.1 7.4 %collective-permute-done.n1.refs_1_.refs_6_ = bf16[160,2048]{1,0:T(8,128)(2,1)S(1)} collective-permute-done((bf16[160,2048]{1,0:T(8,128)(2,1)S(1)}, bf16[160,2048]{1,0:T(8,128)(2,1)S(1)}, u32[]{:S(2)}, u32[]{:S(2)}) %collective-permute-start) | collective-permute-done | bytes 655392 | tf_op jit(solution)/shard_map/ppermute | solution.py:71
  28.3 3.9 collective-permute-done.2.w1
  34.0 2.8 collective-permute-start.7
  41.6 3.1 collective-permute-start.5
  53.6 6.8 %qkv_forward.1 = (bf16[4,1280,128]{2,1,0:T(8,128)(2,1)}, bf16[640,128]{1,0:T(8,128)(2,1)}) custom-call(s32[4]{0:T(128)} %pad_add_fusion.idx, bf16[160,2048]{1,0:T(8,128)(2,1)} %copy-done.2, bf16[160,2048]{1,0:T(8,128)(2,1)} %copy-done.5, bf16[80,2048]{1,0:T(8,128)(2,1)} %copy-done.19, bf16[80,2048]{1,0:T(8,128)(2,1)} %collective-permute-done.4.n2b.refs_3_.refs_8_, ...), custom_call_target="tpu_custom_call" | custom-call | flops 1677721600 | bytes 7000000 | tf_op jit(solution)/shard_map/qkv_forward/pallas_call | solution.py:163
  60.4 6.0 %collective-permute-done.6.kv_par = bf16[640,128]{1,0:T(8,128)(2,1)S(1)} collective-permute-done((bf16[640,128]{1,0:T(8,128)(2,1)}, bf16[640,128]{1,0:T(8,128)(2,1)S(1)}, u32[]{:S(2)}, u32[]{:S(2)}) %collective-permute-start.6) | collective-permute-done | bytes 163872 | tf_op jit(solution)/shard_map/ppermute | solution.py:845
  71.7 6.0 %collective-permute-start.8 = (bf16[128,2048]{1,0:T(8,128)(2,1)}, bf16[128,2048]{1,0:T(8,128)(2,1)S(1)}, u32[]{:S(2)}, u32[]{:S(2)}) collective-permute-start(bf16[128,2048]{1,0:T(8,128)(2,1)} %collective-permute-done.7.w1), channel_id=1, source_target_pairs={{0,8},{8,0},{1,9},{9,1},{2,10},{10,2},{3,11},{11,3},{4,12},{12,4},... | collective-permute-start | bytes 1572872 | tf_op jit(solution)/shard_map/ppermute | solution.py:127
  77.8 8.6 %attend.1 = (bf16[4,160,512]{2,1,0:T(8,128)(2,1)}, bf16[4,1280,128]{2,1,0:T(8,128)(2,1)}) custom-call(s32[4]{0:T(128)} %pad_add_fusion.idx, bf16[4,1280,128]{2,1,0:T(8,128)(2,1)} %get-tuple-element.83.q, bf16[640,128]{1,0:T(8,128)(2,1)} %get-tuple-element.84.kv_own, bf16[640,128]{1,0:T(8,128)(2,1)} %copy-done.47, s32[1,1280]{1,0:T(1,128)} %reshape_tile.3.first), custom_call_target="tpu_custom_call" | custom-call | flops 12000000000 | bytes 3000000 | tf_op jit(solution)/shard_map/attend/pallas_call | solution.py:256
  87.2 4.8 out_project.1
  94.4 5.2 %collective-permute-done.9.c1.refs_11_ = bf16[160,2048]{1,0:T(8,128)(2,1)S(1)} collective-permute-done((bf16[160,2048]{1,0:T(8,128)(2,1)S(1)}, bf16[160,2048]{1,0:T(8,128)(2,1)S(1)}, u32[]{:S(2)}, u32[]{:S(2)}) %collective-permute-start.9) | collective-permute-done | bytes 655392 | tf_op jit(solution)/shard_map/ppermute | solution.py:80
  106.6 4.7 collective-permute-done.12
  116.2 11.1 %collective-permute-done.13 = bf16[160,2048]{1,0:T(8,128)(2,1)S(1)} collective-permute-done((bf16[160,2048]{1,0:T(8,128)(2,1)S(1)}, bf16[160,2048]{1,0:T(8,128)(2,1)S(1)}, u32[]{:S(2)}, u32[]{:S(2)}) %collective-permute-start.13) | collective-permute-done | bytes 655392 | tf_op jit(solution)/shard_map/ppermute | solution.py:94
  129.1 9.0 %collective-permute-done.21.w1 = bf16[352,2048]{1,0:T(8,128)(2,1)S(1)} collective-permute-done((bf16[352,2048]{1,0:T(8,128)(2,1)S(1)}, bf16[352,2048]{1,0:T(8,128)(2,1)S(1)}, u32[]{:S(2)}, u32[]{:S(2)}) %collective-permute-start.21) | collective-permute-done | bytes 1441824 | tf_op jit(solution)/shard_map/ppermute | solution.py:122
  142.6 14.9 %collective-permute-done.17.n3.refs_4_.refs_9_ = bf16[160,2048]{1,0:T(8,128)(2,1)S(1)} collective-permute-done((bf16[160,2048]{1,0:T(8,128)(2,1)S(1)}, bf16[160,2048]{1,0:T(8,128)(2,1)S(1)}, u32[]{:S(2)}, u32[]{:S(2)}) %collective-permute-start.17) | collective-permute-done | bytes 655392 | tf_op jit(solution)/shard_map/ppermute | solution.py:70
  157.6 2.8 collective-permute-start.19
  160.4 6.1 %collective-permute-done.19.n2b.refs_3_.refs_8_ = bf16[80,2048]{1,0:T(8,128)(2,1)S(1)} collective-permute-done((bf16[80,2048]{1,0:T(8,128)(2,1)S(1)}, bf16[80,2048]{1,0:T(8,128)(2,1)S(1)}, u32[]{:S(2)}, u32[]{:S(2)}) %collective-permute-start.19) | collective-permute-done | bytes 327712 | tf_op jit(solution)/shard_map/ppermute | solution.py:75
  166.5 2.9 collective-permute-done.18.n2a.refs_2_.refs_7_
  170.1 20.8 %ffn.1 = (bf16[640,1408]{1,0:T(8,128)(2,1)}, bf16[640,1408]{1,0:T(8,128)(2,1)}, bf16[640,1408]{1,0:T(8,128)(2,1)}) custom-call(s32[4]{0:T(128)} %pad_add_fusion.idx, bf16[160,2048]{1,0:T(8,128)(2,1)} %copy-done.12, bf16[160,2048]{1,0:T(8,128)(2,1)} %copy-done.32, bf16[80,2048]{1,0:T(8,128)(2,1)} %copy-done.46, bf16[80,2048]{1,0:T(8,128)(2,1)} %copy-done.44, ...), custom_call_target="tpu_custom_call" | custom-call | flops 11072962560 | bytes 34000000 | tf_op jit(solution)/shard_map/ffn/pallas_call | solution.py:493
  191.0 21.1 %ffn_grads.1 = bf16[2,16,2112,128]{3,2,1,0:T(8,128)(2,1)} custom-call(bf16[160,2048]{1,0:T(8,128)(2,1)} %copy-done.12, bf16[160,2048]{1,0:T(8,128)(2,1)} %copy-done.32, bf16[80,2048]{1,0:T(8,128)(2,1)} %copy-done.46, bf16[80,2048]{1,0:T(8,128)(2,1)} %copy-done.44, bf16[160,2048]{1,0:T(8,128)(2,1)} %copy-done.31, bf16[160,2048]{1,0:T(8,128)(2,1)} %copy-done.12, ...), custom_call_target="tpu_custom_call" | custom-call | flops 11072962560 | bytes 30000000 | tf_op jit(solution)/shard_map/ffn_grads/pallas_call | solution.py:609
  212.2 15.7 %ffn_back.1 = (bf16[160,2048]{1,0:T(8,128)(2,1)}, bf16[160,2048]{1,0:T(8,128)(2,1)}, bf16[80,2048]{1,0:T(8,128)(2,1)}, bf16[80,2048]{1,0:T(8,128)(2,1)}, bf16[160,2048]{1,0:T(8,128)(2,1)}) custom-call(s32[4]{0:T(128)} %pad_add_fusion.idx, bf16[640,1408]{1,0:T(8,128)(2,1)} %get-tuple-element.106.refs_15_.dgate, ...), custom_call_target="tpu_custom_call" | custom-call | flops 7381975040 | bytes 18000000 | tf_op jit(solution)/shard_map/ffn_back/pallas_call | solution.py:563
  231.5 3.3 collective-permute-done.25
  235.0 3.1 collective-permute-start.26
  239.8 9.5 %collective-permute-done.26 = bf16[160,2048]{1,0:T(8,128)(2,1)S(1)} collective-permute-done((bf16[160,2048]{1,0:T(8,128)(2,1)S(1)}, bf16[160,2048]{1,0:T(8,128)(2,1)S(1)}, u32[]{:S(2)}, u32[]{:S(2)}) %collective-permute-start.26) | collective-permute-done | bytes 655392 | tf_op jit(solution)/shard_map/ppermute | solution.py:95
  249.3 4.8 collective-permute-done.24
  258.8 10.8 %collective-permute-done.28.b3.refs_14_ = bf16[160,2048]{1,0:T(8,128)(2,1)S(1)} collective-permute-done((bf16[160,2048]{1,0:T(8,128)(2,1)S(1)}, bf16[160,2048]{1,0:T(8,128)(2,1)S(1)}, u32[]{:S(2)}, u32[]{:S(2)}) %collective-permute-start.28) | collective-permute-done | bytes 655392 | tf_op jit(solution)/shard_map/ppermute | solution.py:70
  272.9 10.0 %down_project.1 = (bf16[160,2048]{1,0:T(8,128)(2,1)}, bf16[160,2048]{1,0:T(8,128)(2,1)}, bf16[160,2048]{1,0:T(8,128)(2,1)}, bf16[160,2048]{1,0:T(8,128)(2,1)}) custom-call(s32[4]{0:T(128)} %pad_add_fusion.idx, bf16[640,1408]{1,0:T(8,128)(2,1)} %get-tuple-element.112.refs_14_.hid, bf16[704,2048]{1,0:T(8,128)(2,1)} %w0.9, bf16[352,2048]{1,0:T(8,128)(2,1)} %copy-done.38, ...), custom_call_target="tpu_custom_call" | custom-call | flops 3690987520 | bytes 11000000 | tf_op jit(solution)/shard_map/down_project/pallas_call | solution.py:529
  282.9 20.1 %attend_back.1 = (bf16[4,160,512]{2,1,0:T(8,128)(2,1)}, f32[640,128]{1,0:T(8,128)}, bf16[640,128]{1,0:T(8,128)(2,1)}) custom-call(s32[4]{0:T(128)} %pad_add_fusion.idx, bf16[4,1280,128]{2,1,0:T(8,128)(2,1)} %get-tuple-element.114.qx, bf16[640,128]{1,0:T(8,128)(2,1)} %get-tuple-element.84.kv_own, bf16[640,128]{1,0:T(8,128)(2,1)} %copy-done.47, ...), custom_call_target="tpu_custom_call" | custom-call | flops 30000001024 | bytes 8000000 | tf_op jit(solution)/shard_map/attend_back/pallas_call | solution.py:360
  303.0 9.0 %attn_grads.1 = (bf16[4,2,1024,128]{3,2,1,0:T(8,128)(2,1)}, bf16[4,2,1024,128]{3,2,1,0:T(8,128)(2,1)}) custom-call(s32[4]{0:T(128)} %pad_add_fusion.idx, bf16[160,2048]{1,0:T(8,128)(2,1)} %copy-done.2, bf16[160,2048]{1,0:T(8,128)(2,1)} %copy-done.5, bf16[80,2048]{1,0:T(8,128)(2,1)} %copy-done.19, ...), custom_call_target="tpu_custom_call" | custom-call | flops 2684354560 | bytes 10000000 | tf_op jit(solution)/shard_map/attn_grads/pallas_call | solution.py:689
  312.1 17.2 %reduce-scatter.2.cloned.1.call-done = bf16[1,2112,128]{2,1,0:T(8,128)(2,1)} async-done(((bf16[32,2112,128]{2,1,0:T(8,128)(2,1)}), bf16[1,2112,128]{2,1,0:T(8,128)(2,1)}) %reduce-scatter.2.cloned.1.call-update) | async-done | bytes 540688 | tf_op jit(solution)/shard_map/reduce_scatter | solution.py:856
  331.2 8.9 %qkv_back.1 = (bf16[4,2,144,128]{3,2,1,0:T(8,128)(2,1)}, bf16[4,2,144,128]{3,2,1,0:T(8,128)(2,1)}, bf16[160,2048]{1,0:T(8,128)(2,1)}, bf16[160,2048]{1,0:T(8,128...) custom-call(s32[4]{0:T(128)} %pad_add_fusion.idx, ...), custom_call_target="tpu_custom_call" | custom-call | flops 1677721600 | bytes 13000000 | tf_op jit(solution)/shard_map/qkv_back/pallas_call | solution.py:422
  344.9 5.0 collective-permute-done.34
  350.9 3.3 collective-permute-start.35
  354.2 4.0 sum_core.1
  365.5 21.5 %collective-permute-done.41.b = bf16[2,1168,128]{2,1,0:T(8,128)(2,1)} collective-permute-done((bf16[2,1168,128]{2,1,0:T(8,128)(2,1)}, bf16[2,1168,128]{2,1,0:T(8,128)(2,1)}, u32[]{:S(2)}, u32[]{:S(2)}) %collective-permute-start.41) | collective-permute-done | bytes 598048 | tf_op jit(solution)/shard_map/ppermute | solution.py:764
  387.0 19.3 %collective-permute-done.42.c = bf16[2,1168,128]{2,1,0:T(8,128)(2,1)} collective-permute-done((bf16[2,1168,128]{2,1,0:T(8,128)(2,1)}, bf16[2,1168,128]{2,1,0:T(8,128)(2,1)}, u32[]{:S(2)}, u32[]{:S(2)}) %collective-permute-start.42) | collective-permute-done | bytes 598048 | tf_op jit(solution)/shard_map/ppermute | solution.py:764
  413.0 3.2 collective-permute-done.44.b
  416.2 3.6 collective-permute-done.46.d
  419.8 6.1 %collective-permute-done.45.c = bf16[1168,128]{1,0:T(8,128)(2,1)} collective-permute-done((bf16[1168,128]{1,0:T(8,128)(2,1)}, bf16[1168,128]{1,0:T(8,128)(2,1)}, u32[]{:S(2)}, u32[]{:S(2)}) %collective-permute-start.45) | collective-permute-done | bytes 299040 | tf_op jit(solution)/shard_map/ppermute | solution.py:774
  430.0 2.8 collective-permute-start.50
  436.1 3.7 collective-permute-start.53
  441.8 5.8 %collective-permute-start.36 = (bf16[160,2048]{1,0:T(8,128)(2,1)}, bf16[160,2048]{1,0:T(8,128)(2,1)}, u32[]{:S(2)}, u32[]{:S(2)}) collective-permute-start(bf16[160,2048]{1,0:T(8,128)(2,1)} %get-tuple-element.132), channel_id=1, source_target_pairs={{0,2},{2,4},{4,6},{6,0},{1,3},{3,5},{5,7},{7,1},{8,10},{10,12},{12... | collective-permute-start | bytes 1966088 | tf_op jit(solution)/shard_map/ppermute | solution.py:84
  447.6 3.0 collective-permute-start.37
  454.9 4.2 unpack_tail.1
  462.0 2.7 collective-permute-done.36
  464.7 15.0 %collective-permute-done.37 = bf16[160,2048]{1,0:T(8,128)(2,1)} collective-permute-done((bf16[160,2048]{1,0:T(8,128)(2,1)}, bf16[160,2048]{1,0:T(8,128)(2,1)}, u32[]{:S(2)}, u32[]{:S(2)}) %collective-permute-start.37) | collective-permute-done | bytes 655392 | tf_op jit(solution)/shard_map/ppermute | solution.py:84
  479.7 2.8 add_convert_fusion
  483.1 13.5 %unpack.1 = (f32[1024,1408]{1,0:T(8,128)}, f32[1024,1408]{1,0:T(8,128)}, f32[704,2048]{1,0:T(8,128)}) custom-call(bf16[16,2112,128]{2,1,0:T(8,128)(2,1)} %all-gather.5.cloned.1.call-done.piece), custom_call_target="tpu_custom_call" | custom-call | flops 1000000 | bytes 26000000 | tf_op jit(solution)/shard_map/unpack/pallas_call | solution.py:634
  (250 shorter events, 105.5 us)
Async XLA Ops:
  7.2 163.0 %all-gather.3.cloned.1.call-start = ((), (), s32[]{:S(2)}) async-start(), calls=%async_computation.1 | async-start | bytes 6782976 | tf_op jit(solution)/shard_map/all_gather | solution.py:846
  10.0 18.3 %collective-permute-start.1 = (bf16[160,2048]{1,0:T(8,128)(2,1)S(1)}, bf16[160,2048]{1,0:T(8,128)(2,1)S(1)}, u32[]{:S(2)}, u32[]{:S(2)}) collective-permute-start(bf16[160,2048]{1,0:T(8,128)(2,1)S(1)} %fusion.2.n0.refs_0_.refs_5_), channel_id=1, source_target_pairs={{0,2},{2,4},{4,6},{6,0},{1,3},{3,5},{5,7},{7,1},{8,10},{10,12},{12... | collective-permute-start | bytes 1966088 | tf_op jit(solution)/shard_map/ppermute | solution.py:70
  12.1 15.4 %collective-permute-start = (bf16[160,2048]{1,0:T(8,128)(2,1)S(1)}, bf16[160,2048]{1,0:T(8,128)(2,1)S(1)}, u32[]{:S(2)}, u32[]{:S(2)}) collective-permute-start(bf16[160,2048]{1,0:T(8,128)(2,1)S(1)} %fusion.2.n0.refs_0_.refs_5_), channel_id=1, source_target_pairs={{0,6},{2,0},{4,2},{6,4},{1,7},{3,1},{5,3},{7,5},{8,14},{10,8},{12,... | collective-permute-start | bytes 1966088 | tf_op jit(solution)/shard_map/ppermute | solution.py:71
  14.4 17.8 %collective-permute-start.2 = (bf16[512,640]{1,0:T(8,128)(2,1)}, bf16[512,640]{1,0:T(8,128)(2,1)}, u32[]{:S(2)}, u32[]{:S(2)}) collective-permute-start(bf16[512,640]{1,0:T(8,128)(2,1)} %constant_dynamic-slice_fusion.5), channel_id=1, source_target_pairs={{0,1},{1,0},{2,3},{3,2},{4,5},{5,4},{6,7},{7,6},{8,9},{9,8},{10,11... | collective-permute-start | bytes 1966088 | tf_op jit(solution)/shard_map/ppermute | solution.py:122
  34.0 13.2 %collective-permute-start.7 = (bf16[128,2048]{1,0:T(8,128)(2,1)S(1)}, bf16[128,2048]{1,0:T(8,128)(2,1)}, u32[]{:S(2)}, u32[]{:S(2)}) collective-permute-start(bf16[128,2048]{1,0:T(8,128)(2,1)S(1)} %constant_dynamic-slice_fusion.3), channel_id=1, source_target_pairs={{0,1},{1,0},{2,3},{3,2},{4,5},{5,4},{6,7},{7,6},{8,9},{9,8},{10,11... | collective-permute-start | bytes 1572872 | tf_op jit(solution)/shard_map/ppermute | solution.py:122
  41.6 11.2 %collective-permute-start.5 = (bf16[512,640]{1,0:T(8,128)(2,1)}, bf16[512,640]{1,0:T(8,128)(2,1)S(1)}, u32[]{:S(2)}, u32[]{:S(2)}) collective-permute-start(bf16[512,640]{1,0:T(8,128)(2,1)} %collective-permute-done.2.w1), channel_id=1, source_target_pairs={{0,8},{8,0},{1,9},{9,1},{2,10},{10,2},{3,11},{11,3},{4,12},{12,4},... | collective-permute-start | bytes 1966088 | tf_op jit(solution)/shard_map/ppermute | solution.py:816
  47.4 19.0 %collective-permute-start.20 = (bf16[128,2944]{1,0:T(8,128)(2,1)S(1)}, bf16[128,2944]{1,0:T(8,128)(2,1)S(1)}, u32[]{:S(2)}, u32[]{:S(2)}) collective-permute-start(bf16[128,2944]{1,0:T(8,128)(2,1)S(1)} %pad_maximum_fusion), channel_id=1, source_target_pairs={{0,17},{1,16},{16,1},{17,0},{2,19},{3,18},{18,3},{19,2},{4,21},{5,... | collective-permute-start | bytes 2261000 | tf_op jit(solution)/shard_map/ppermute | solution.py:821
  67.4 261.9 %reduce-scatter.2.cloned.1.call-start = ((), (), s32[]{:S(2)}) async-start(), calls=%async_computation.2 | async-start | bytes 17842176 | tf_op jit(solution)/shard_map/reduce_scatter | solution.py:856
  68.1 23.8 %collective-permute-start.11 = (bf16[160,2048]{1,0:T(8,128)(2,1)S(1)}, bf16[160,2048]{1,0:T(8,128)(2,1)S(1)}, u32[]{:S(2)}, u32[]{:S(2)}) collective-permute-start(bf16[160,2048]{1,0:T(8,128)(2,1)S(1)} %copy-done.7), channel_id=1, source_target_pairs={{0,2},{2,4},{4,6},{6,0},{1,3},{3,5},{5,7},{7,1},{8,10},{10,12},{12... | collective-permute-start | bytes 1966088 | tf_op jit(solution)/shard_map/ppermute | solution.py:80
  68.1 26.3 %collective-permute-start.10 = (bf16[160,2048]{1,0:T(8,128)(2,1)S(1)}, bf16[160,2048]{1,0:T(8,128)(2,1)S(1)}, u32[]{:S(2)}, u32[]{:S(2)}) collective-permute-start(bf16[160,2048]{1,0:T(8,128)(2,1)S(1)} %copy-done.7), channel_id=1, source_target_pairs={{0,4},{2,6},{4,0},{6,2},{1,5},{3,7},{5,1},{7,3},{8,12},{10,14},{12... | collective-permute-start | bytes 1966088 | tf_op jit(solution)/shard_map/ppermute | solution.py:80
  70.6 29.0 %collective-permute-start.9 = (bf16[160,2048]{1,0:T(8,128)(2,1)S(1)}, bf16[160,2048]{1,0:T(8,128)(2,1)S(1)}, u32[]{:S(2)}, u32[]{:S(2)}) collective-permute-start(bf16[160,2048]{1,0:T(8,128)(2,1)S(1)} %copy-done.7), channel_id=1, source_target_pairs={{0,6},{2,0},{4,2},{6,4},{1,7},{3,1},{5,3},{7,5},{8,14},{10,8},{12,... | collective-permute-start | bytes 1966088 | tf_op jit(solution)/shard_map/ppermute | solution.py:80
  71.7 14.7 %collective-permute-start.8 = (bf16[128,2048]{1,0:T(8,128)(2,1)}, bf16[128,2048]{1,0:T(8,128)(2,1)S(1)}, u32[]{:S(2)}, u32[]{:S(2)}) collective-permute-start(bf16[128,2048]{1,0:T(8,128)(2,1)} %collective-permute-done.7.w1), channel_id=1, source_target_pairs={{0,8},{8,0},{1,9},{9,1},{2,10},{10,2},{3,11},{11,3},{4,12},{12,4},... | collective-permute-start | bytes 1572872 | tf_op jit(solution)/shard_map/ppermute | solution.py:127
  100.4 10.8 %collective-permute-start.12 = (bf16[80,2048]{1,0:T(8,128)(2,1)}, bf16[80,2048]{1,0:T(8,128)(2,1)S(1)}, u32[]{:S(2)}, u32[]{:S(2)}) collective-permute-start(bf16[80,2048]{1,0:T(8,128)(2,1)} %get-tuple-element.93), channel_id=1, source_target_pairs={{0,2},{2,4},{4,6},{6,0},{1,3},{3,5},{5,7},{7,1},{8,10},{10,12},{12... | collective-permute-start | bytes 983048 | tf_op jit(solution)/shard_map/ppermute | solution.py:90
  104.1 34.0 %collective-permute-start.21 = (bf16[352,2048]{1,0:T(8,128)(2,1)S(1)}, bf16[352,2048]{1,0:T(8,128)(2,1)S(1)}, u32[]{:S(2)}, u32[]{:S(2)}) collective-permute-start(bf16[352,2048]{1,0:T(8,128)(2,1)S(1)} %constant_dynamic-slice_fusion), channel_id=1, source_target_pairs={{0,1},{1,0},{2,3},{3,2},{4,5},{5,4},{6,7},{7,6},{8,9},{9,8},{10,11... | collective-permute-start | bytes 4325384 | tf_op jit(solution)/shard_map/ppermute | solution.py:122
  111.4 15.9 %collective-permute-start.13 = (bf16[160,2048]{1,0:T(8,128)(2,1)S(1)}, bf16[160,2048]{1,0:T(8,128)(2,1)S(1)}, u32[]{:S(2)}, u32[]{:S(2)}) collective-permute-start(bf16[160,2048]{1,0:T(8,128)(2,1)S(1)} %pad_maximum_fusion.1), channel_id=1, source_target_pairs={{0,2},{2,4},{4,6},{6,0},{1,3},{3,5},{5,7},{7,1},{8,10},{10,12},{12... | collective-permute-start | bytes 1966088 | tf_op jit(solution)/shard_map/ppermute | solution.py:94
  113.8 14.7 %collective-permute-start.15 = (bf16[160,2048]{1,0:T(8,128)(2,1)S(1)}, bf16[160,2048]{1,0:T(8,128)(2,1)S(1)}, u32[]{:S(2)}, u32[]{:S(2)}) collective-permute-start(bf16[160,2048]{1,0:T(8,128)(2,1)S(1)} %pad_maximum_fusion.2), channel_id=1, source_target_pairs={{0,6},{2,0},{4,2},{6,4},{1,7},{3,1},{5,3},{7,5},{8,14},{10,8},{12,... | collective-permute-start | bytes 1966088 | tf_op jit(solution)/shard_map/ppermute | solution.py:95
  138.1 32.0 %collective-permute-start.22 = (bf16[352,2048]{1,0:T(8,128)(2,1)S(1)}, bf16[352,2048]{1,0:T(8,128)(2,1)}, u32[]{:S(2)}, u32[]{:S(2)}) collective-permute-start(bf16[352,2048]{1,0:T(8,128)(2,1)S(1)} %collective-permute-done.21.w1), channel_id=1, source_target_pairs={{0,8},{8,0},{1,9},{9,1},{2,10},{10,2},{3,11},{11,3},{4,12},{12,4},... | collective-permute-start | bytes 4325384 | tf_op jit(solution)/shard_map/ppermute | solution.py:127
  139.9 17.6 %collective-permute-start.17 = (bf16[160,2048]{1,0:T(8,128)(2,1)S(1)}, bf16[160,2048]{1,0:T(8,128)(2,1)S(1)}, u32[]{:S(2)}, u32[]{:S(2)}) collective-permute-start(bf16[160,2048]{1,0:T(8,128)(2,1)S(1)} %multiply_convert_fusion.n0.refs_0_.refs_5_), channel_id=1, source_target_pairs={{0,2},{2,4},{4,6},{6,0},{1,3},{3,5},{5,7},{7,1},{8,10},{10,12},{12... | collective-permute-start | bytes 1966088 | tf_op jit(solution)/shard_map/ppermute | solution.py:70
  140.0 17.6 %collective-permute-start.16 = (bf16[160,2048]{1,0:T(8,128)(2,1)S(1)}, bf16[160,2048]{1,0:T(8,128)(2,1)S(1)}, u32[]{:S(2)}, u32[]{:S(2)}) collective-permute-start(bf16[160,2048]{1,0:T(8,128)(2,1)S(1)} %multiply_convert_fusion.n0.refs_0_.refs_5_), channel_id=1, source_target_pairs={{0,6},{2,0},{4,2},{6,4},{1,7},{3,1},{5,3},{7,5},{8,14},{10,8},{12,... | collective-permute-start | bytes 1966088 | tf_op jit(solution)/shard_map/ppermute | solution.py:71
  160.4 9.0 %collective-permute-start.18 = (bf16[80,2048]{1,0:T(8,128)(2,1)S(1)}, bf16[80,2048]{1,0:T(8,128)(2,1)S(1)}, u32[]{:S(2)}, u32[]{:S(2)}) collective-permute-start(bf16[80,2048]{1,0:T(8,128)(2,1)S(1)} %slice.87), channel_id=1, source_target_pairs={{0,2},{2,4},{4,6},{6,0},{1,3},{3,5},{5,7},{7,1},{8,10},{10,12},{12... | collective-permute-start | bytes 983048 | tf_op jit(solution)/shard_map/ppermute | solution.py:74
  212.1 271.0 %all-gather.5.cloned.1.call-start = ((), (), s32[]{:S(2)}) async-start(), calls=%async_computation.3 | async-start | bytes 9191424 | tf_op jit(solution)/shard_map/all_gather | solution.py:875
  235.0 14.3 %collective-permute-start.26 = (bf16[160,2048]{1,0:T(8,128)(2,1)S(1)}, bf16[160,2048]{1,0:T(8,128)(2,1)S(1)}, u32[]{:S(2)}, u32[]{:S(2)}) collective-permute-start(bf16[160,2048]{1,0:T(8,128)(2,1)S(1)} %pad_maximum_fusion.4), channel_id=1, source_target_pairs={{0,6},{2,0},{4,2},{6,4},{1,7},{3,1},{5,3},{7,5},{8,14},{10,8},{12,... | collective-permute-start | bytes 1966088 | tf_op jit(solution)/shard_map/ppermute | solution.py:95
  239.7 14.4 %collective-permute-start.24 = (bf16[160,2048]{1,0:T(8,128)(2,1)S(1)}, bf16[160,2048]{1,0:T(8,128)(2,1)S(1)}, u32[]{:S(2)}, u32[]{:S(2)}) collective-permute-start(bf16[160,2048]{1,0:T(8,128)(2,1)S(1)} %pad_maximum_fusion.3), channel_id=1, source_target_pairs={{0,2},{2,4},{4,6},{6,0},{1,3},{3,5},{5,7},{7,1},{8,10},{10,12},{12... | collective-permute-start | bytes 1966088 | tf_op jit(solution)/shard_map/ppermute | solution.py:94
  256.0 13.5 %collective-permute-start.28 = (bf16[160,2048]{1,0:T(8,128)(2,1)S(1)}, bf16[160,2048]{1,0:T(8,128)(2,1)S(1)}, u32[]{:S(2)}, u32[]{:S(2)}) collective-permute-start(bf16[160,2048]{1,0:T(8,128)(2,1)S(1)} %get-tuple-element.155.b0.refs_10_), channel_id=1, source_target_pairs={{0,2},{2,4},{4,6},{6,0},{1,3},{3,5},{5,7},{7,1},{8,10},{10,12},{12... | collective-permute-start | bytes 1966088 | tf_op jit(solution)/shard_map/ppermute | solution.py:70
  256.9 12.7 %collective-permute-start.27 = (bf16[160,2048]{1,0:T(8,128)(2,1)S(1)}, bf16[160,2048]{1,0:T(8,128)(2,1)S(1)}, u32[]{:S(2)}, u32[]{:S(2)}) collective-permute-start(bf16[160,2048]{1,0:T(8,128)(2,1)S(1)} %get-tuple-element.155.b0.refs_10_), channel_id=1, source_target_pairs={{0,6},{2,0},{4,2},{6,4},{1,7},{3,1},{5,3},{7,5},{8,14},{10,8},{12,... | collective-permute-start | bytes 1966088 | tf_op jit(solution)/shard_map/ppermute | solution.py:71
  270.6 12.3 %collective-permute-start.30 = (bf16[80,2048]{1,0:T(8,128)(2,1)}, bf16[80,2048]{1,0:T(8,128)(2,1)}, u32[]{:S(2)}, u32[]{:S(2)}) collective-permute-start(bf16[80,2048]{1,0:T(8,128)(2,1)} %slice.90), channel_id=1, source_target_pairs={{0,6},{2,0},{4,2},{6,4},{1,7},{3,1},{5,3},{7,5},{8,14},{10,8},{12,... | collective-permute-start | bytes 983048 | tf_op jit(solution)/shard_map/ppermute | solution.py:75
  272.7 10.2 %collective-permute-start.29 = (bf16[80,2048]{1,0:T(8,128)(2,1)S(1)}, bf16[80,2048]{1,0:T(8,128)(2,1)}, u32[]{:S(2)}, u32[]{:S(2)}) collective-permute-start(bf16[80,2048]{1,0:T(8,128)(2,1)S(1)} %slice.89), channel_id=1, source_target_pairs={{0,2},{2,4},{4,6},{6,0},{1,3},{3,5},{5,7},{7,1},{8,10},{10,12},{12... | collective-permute-start | bytes 983048 | tf_op jit(solution)/shard_map/ppermute | solution.py:74
  329.3 25.0 %collective-permute-start.39 = (bf16[4,2,1024,128]{3,2,1,0:T(8,128)(2,1)}, bf16[4,2,1024,128]{3,2,1,0:T(8,128)(2,1)}, u32[]{:S(2)}, u32[]{:S(2)}) collective-permute-start(bf16[4,2,1024,128]{3,2,1,0:T(8,128)(2,1)} %get-tuple-element.135), channel_id=1, source_target_pairs={{0,8},{8,0},{1,9},{9,1},{2,10},{10,2},{3,11},{11,3},{4,12},{12,4},... | collective-permute-start | bytes 6291464 | tf_op jit(solution)/shard_map/ppermute | solution.py:760
  340.1 9.9 %collective-permute-start.34 = (bf16[80,2048]{1,0:T(8,128)(2,1)}, bf16[80,2048]{1,0:T(8,128)(2,1)S(1)}, u32[]{:S(2)}, u32[]{:S(2)}) collective-permute-start(bf16[80,2048]{1,0:T(8,128)(2,1)} %get-tuple-element.130), channel_id=1, source_target_pairs={{0,6},{2,0},{4,2},{6,4},{1,7},{3,1},{5,3},{7,5},{8,14},{10,8},{12,... | collective-permute-start | bytes 983048 | tf_op jit(solution)/shard_map/ppermute | solution.py:91
  342.5 11.7 %collective-permute-start.40 = (bf16[4,2,144,128]{3,2,1,0:T(8,128)(2,1)}, bf16[4,2,144,128]{3,2,1,0:T(8,128)(2,1)}, u32[]{:S(2)}, u32[]{:S(2)}) collective-permute-start(bf16[4,2,144,128]{3,2,1,0:T(8,128)(2,1)} %get-tuple-element.137), channel_id=1, source_target_pairs={{0,8},{8,0},{1,9},{9,1},{2,10},{10,2},{3,11},{11,3},{4,12},{12,4},... | collective-permute-start | bytes 884744 | tf_op jit(solution)/shard_map/ppermute | solution.py:761
  344.8 18.6 %collective-permute-start.32 = (bf16[80,2048]{1,0:T(8,128)(2,1)}, bf16[80,2048]{1,0:T(8,128)(2,1)}, u32[]{:S(2)}, u32[]{:S(2)}) collective-permute-start(bf16[80,2048]{1,0:T(8,128)(2,1)} %get-tuple-element.128), channel_id=1, source_target_pairs={{0,2},{2,4},{4,6},{6,0},{1,3},{3,5},{5,7},{7,1},{8,10},{10,12},{12... | collective-permute-start | bytes 983048 | tf_op jit(solution)/shard_map/ppermute | solution.py:90
  350.9 83.5 %collective-permute-start.35 = (bf16[160,2048]{1,0:T(8,128)(2,1)}, bf16[160,2048]{1,0:T(8,128)(2,1)}, u32[]{:S(2)}, u32[]{:S(2)}) collective-permute-start(bf16[160,2048]{1,0:T(8,128)(2,1)} %pad_maximum_fusion.6), channel_id=1, source_target_pairs={{0,6},{2,0},{4,2},{6,4},{1,7},{3,1},{5,3},{7,5},{8,14},{10,8},{12,... | collective-permute-start | bytes 1966088 | tf_op jit(solution)/shard_map/ppermute | solution.py:95
  358.2 28.8 %collective-permute-start.41 = (bf16[2,1168,128]{2,1,0:T(8,128)(2,1)}, bf16[2,1168,128]{2,1,0:T(8,128)(2,1)}, u32[]{:S(2)}, u32[]{:S(2)}) collective-permute-start(bf16[2,1168,128]{2,1,0:T(8,128)(2,1)} %get-tuple-element.139), channel_id=1, source_target_pairs={{0,64},{32,96},{64,0},{96,32},{1,65},{33,97},{65,1},{97,33},{2,66}... | collective-permute-start | bytes 1794056 | tf_op jit(solution)/shard_map/ppermute | solution.py:764
  360.8 45.5 %collective-permute-start.42 = (bf16[2,1168,128]{2,1,0:T(8,128)(2,1)}, bf16[2,1168,128]{2,1,0:T(8,128)(2,1)}, u32[]{:S(2)}, u32[]{:S(2)}) collective-permute-start(bf16[2,1168,128]{2,1,0:T(8,128)(2,1)} %get-tuple-element.140), channel_id=1, source_target_pairs={{0,32},{32,64},{64,96},{96,0},{1,33},{33,65},{65,97},{97,1},{2,34}... | collective-permute-start | bytes 1794056 | tf_op jit(solution)/shard_map/ppermute | solution.py:764
  361.4 45.2 %collective-permute-start.43 = (bf16[2,1168,128]{2,1,0:T(8,128)(2,1)}, bf16[2,1168,128]{2,1,0:T(8,128)(2,1)}, u32[]{:S(2)}, u32[]{:S(2)}) collective-permute-start(bf16[2,1168,128]{2,1,0:T(8,128)(2,1)} %get-tuple-element.141), channel_id=1, source_target_pairs={{0,96},{32,0},{64,32},{96,64},{1,97},{33,1},{65,33},{97,65},{2,98}... | collective-permute-start | bytes 1794056 | tf_op jit(solution)/shard_map/ppermute | solution.py:764
  365.5 74.3 %collective-permute-start.33 = (bf16[160,2048]{1,0:T(8,128)(2,1)}, bf16[160,2048]{1,0:T(8,128)(2,1)}, u32[]{:S(2)}, u32[]{:S(2)}) collective-permute-start(bf16[160,2048]{1,0:T(8,128)(2,1)} %pad_maximum_fusion.5), channel_id=1, source_target_pairs={{0,2},{2,4},{4,6},{6,0},{1,3},{3,5},{5,7},{7,1},{8,10},{10,12},{12... | collective-permute-start | bytes 1966088 | tf_op jit(solution)/shard_map/ppermute | solution.py:94
  410.5 9.3 %collective-permute-start.46 = (bf16[1168,128]{1,0:T(8,128)(2,1)}, bf16[1168,128]{1,0:T(8,128)(2,1)}, u32[]{:S(2)}, u32[]{:S(2)}) collective-permute-start(bf16[1168,128]{1,0:T(8,128)(2,1)} %get-tuple-element.143), channel_id=1, source_target_pairs={{0,17},{1,16},{16,1},{17,0},{2,19},{3,18},{18,3},{19,2},{4,21},{5,... | collective-permute-start | bytes 897032 | tf_op jit(solution)/shard_map/ppermute | solution.py:775
  412.3 13.5 %collective-permute-start.45 = (bf16[1168,128]{1,0:T(8,128)(2,1)}, bf16[1168,128]{1,0:T(8,128)(2,1)}, u32[]{:S(2)}, u32[]{:S(2)}) collective-permute-start(bf16[1168,128]{1,0:T(8,128)(2,1)} %get-tuple-element.143), channel_id=1, source_target_pairs={{0,1},{1,0},{2,3},{3,2},{4,5},{5,4},{6,7},{7,6},{8,9},{9,8},{10,11... | collective-permute-start | bytes 897032 | tf_op jit(solution)/shard_map/ppermute | solution.py:774
  430.0 17.6 %collective-permute-start.50 = (bf16[1168,128]{1,0:T(8,128)(2,1)}, bf16[1168,128]{1,0:T(8,128)(2,1)S(1)}, u32[]{:S(2)}, u32[]{:S(2)}) collective-permute-start(bf16[1168,128]{1,0:T(8,128)(2,1)} %sum_z.1.refs_0_), channel_id=1, source_target_pairs={{0,8},{8,0},{1,9},{9,1},{2,10},{10,2},{3,11},{11,3},{4,12},{12,4},... | collective-permute-start | bytes 897032 | tf_op jit(solution)/shard_map/ppermute | solution.py:779
  432.7 17.8 %collective-permute-start.48 = (bf16[1168,128]{1,0:T(8,128)(2,1)}, bf16[1168,128]{1,0:T(8,128)(2,1)S(1)}, u32[]{:S(2)}, u32[]{:S(2)}) collective-permute-start(bf16[1168,128]{1,0:T(8,128)(2,1)} %sum_z.1.refs_0_), channel_id=1, source_target_pairs={{0,64},{32,96},{64,0},{96,32},{1,65},{33,97},{65,1},{97,33},{2,66}... | collective-permute-start | bytes 897032 | tf_op jit(solution)/shard_map/ppermute | solution.py:778
  434.4 16.5 %collective-permute-start.47 = (bf16[1168,128]{1,0:T(8,128)(2,1)}, bf16[1168,128]{1,0:T(8,128)(2,1)S(1)}, u32[]{:S(2)}, u32[]{:S(2)}) collective-permute-start(bf16[1168,128]{1,0:T(8,128)(2,1)} %sum_z.1.refs_0_), channel_id=1, source_target_pairs={{0,32},{32,64},{64,96},{96,0},{1,33},{33,65},{65,97},{97,1},{2,34}... | collective-permute-start | bytes 897032 | tf_op jit(solution)/shard_map/ppermute | solution.py:778
  436.1 15.9 %collective-permute-start.53 = (bf16[1168,128]{1,0:T(8,128)(2,1)S(1)}, bf16[1168,128]{1,0:T(8,128)(2,1)S(1)}, u32[]{:S(2)}, u32[]{:S(2)}) collective-permute-start(bf16[1168,128]{1,0:T(8,128)(2,1)S(1)} %collective-permute-done.49.refs_3_), channel_id=1, source_target_pairs={{0,8},{8,0},{1,9},{9,1},{2,10},{10,2},{3,11},{11,3},{4,12},{12,4},... | collective-permute-start | bytes 897032 | tf_op jit(solution)/shard_map/ppermute | solution.py:779
  441.8 22.9 %collective-permute-start.36 = (bf16[160,2048]{1,0:T(8,128)(2,1)}, bf16[160,2048]{1,0:T(8,128)(2,1)}, u32[]{:S(2)}, u32[]{:S(2)}) collective-permute-start(bf16[160,2048]{1,0:T(8,128)(2,1)} %get-tuple-element.132), channel_id=1, source_target_pairs={{0,2},{2,4},{4,6},{6,0},{1,3},{3,5},{5,7},{7,1},{8,10},{10,12},{12... | collective-permute-start | bytes 1966088 | tf_op jit(solution)/shard_map/ppermute | solution.py:84
  447.6 32.1 %collective-permute-start.37 = (bf16[160,2048]{1,0:T(8,128)(2,1)}, bf16[160,2048]{1,0:T(8,128)(2,1)}, u32[]{:S(2)}, u32[]{:S(2)}) collective-permute-start(bf16[160,2048]{1,0:T(8,128)(2,1)} %get-tuple-element.133), channel_id=1, source_target_pairs={{0,4},{2,6},{4,0},{6,2},{1,5},{3,7},{5,1},{7,3},{8,12},{10,14},{12... | collective-permute-start | bytes 1966088 | tf_op jit(solution)/shard_map/ppermute | solution.py:84
  450.6 29.1 %collective-permute-start.38 = (bf16[160,2048]{1,0:T(8,128)(2,1)}, bf16[160,2048]{1,0:T(8,128)(2,1)}, u32[]{:S(2)}, u32[]{:S(2)}) collective-permute-start(bf16[160,2048]{1,0:T(8,128)(2,1)} %get-tuple-element.134), channel_id=1, source_target_pairs={{0,6},{2,0},{4,2},{6,4},{1,7},{3,1},{5,3},{7,5},{8,14},{10,8},{12,... | collective-permute-start | bytes 1966088 | tf_op jit(solution)/shard_map/ppermute | solution.py:84
  459.1 23.4 %collective-permute-start.56 = (f32[2,2048]{1,0:T(2,128)}, f32[2,2048]{1,0:T(2,128)S(1)}, u32[]{:S(2)}, u32[]{:S(2)}) collective-permute-start(f32[2,2048]{1,0:T(2,128)} %get-tuple-element.144), channel_id=1, source_target_pairs={{0,6},{2,0},{4,2},{6,4},{1,7},{3,1},{5,3},{7,5},{8,14},{10,8},{12,... | collective-permute-start | bytes 49160 | tf_op jit(solution)/shard_map/ppermute | solution.py:883
  460.0 22.5 %collective-permute-start.55 = (f32[2,2048]{1,0:T(2,128)}, f32[2,2048]{1,0:T(2,128)S(1)}, u32[]{:S(2)}, u32[]{:S(2)}) collective-permute-start(f32[2,2048]{1,0:T(2,128)} %get-tuple-element.144), channel_id=1, source_target_pairs={{0,4},{2,6},{4,0},{6,2},{1,5},{3,7},{5,1},{7,3},{8,12},{10,14},{12... | collective-permute-start | bytes 49160 | tf_op jit(solution)/shard_map/ppermute | solution.py:883
  464.7 17.8 %collective-permute-start.54 = (f32[2,2048]{1,0:T(2,128)}, f32[2,2048]{1,0:T(2,128)S(1)}, u32[]{:S(2)}, u32[]{:S(2)}) collective-permute-start(f32[2,2048]{1,0:T(2,128)} %get-tuple-element.144), channel_id=1, source_target_pairs={{0,2},{2,4},{4,6},{6,0},{1,3},{3,5},{5,7},{7,1},{8,10},{10,12},{12... | collective-permute-start | bytes 49160 | tf_op jit(solution)/shard_map/ppermute | solution.py:883
  (60 other events, 542.1 us)
Sparse Core Ops, SparseCore 0:
  67.5 44.5 all-gather.2
  212.2 116.9 reduce-scatter.1
  331.0 79.6 all-gather.4

commit v5 on v4

--- a/solution.py
+++ b/solution.py
@@ -66,23 +66,14 @@
     return [(i, (i + s) % n) for i in range(n)]
 
 
-def gather_x(v, *deps):
+def gather_x(v):
     from_prev = lax.ppermute(v, "x", shift(4, 1))
     from_next = lax.ppermute(v, "x", shift(4, -1))
-    send_a = tie(from_prev[:HALF], from_next, *deps)
-    send_b = tie(from_next[HALF:], from_prev, *deps)
+    send_a = tie(from_prev[:HALF], from_next)
+    send_b = tie(from_next[HALF:], from_prev)
     opp_a = lax.ppermute(send_a, "x", shift(4, 1))
     opp_b = lax.ppermute(send_b, "x", shift(4, -1))
-    return (v, from_next, opp_a, opp_b, from_prev), (send_a, send_b)
-
-
-def gather_direct(v):
-    return v, *(lax.ppermute(v, "x", shift(4, -s)) for s in (1, 2, 3))
-
-
-def scatter_direct(parts):
-    got = [lax.ppermute(parts[s], "x", shift(4, s)) for s in (1, 2, 3)]
-    return sum((g.astype(F32) for g in got), parts[0].astype(F32))
+    return v, from_next, opp_a, opp_b, from_prev
 
 
 def scatter_x(parts):
@@ -93,7 +84,7 @@
     q3 = jnp.concatenate([p3[:HALF], (p3[HALF:].astype(F32) + got_b.astype(F32)).astype(BF16)], 0)
     from_prev = lax.ppermute(q1, "x", shift(4, 1))
     from_next = lax.ppermute(q3, "x", shift(4, -1))
-    return p0.astype(F32) + from_prev.astype(F32) + from_next.astype(F32)
+    return p0.astype(F32) + from_prev.astype(F32) + from_next.astype(F32), (got_a, got_b)
 
 
 PIECES = ((0, BLK), (1, BLK), (2, HALF), (2, HALF), (3, BLK))
@@ -269,6 +260,11 @@
         cost_estimate=cost(1.2e10, 3e6),
         name="attend",
     )(idx, q, kv_own, kv_par, first)
+
+
+def store_parts(res, refs):
+    for ref, row, (_, n) in zip(refs, PIECE_ROW, PIECES):
+        ref[...] = res[row : row + n].astype(BF16)
 
 
 def out_body(idx, att, w0, w1, w2, o0, o1, o2a, o2b, o3):
@@ -380,33 +376,28 @@
 
 
 def qkv_back_body(
-    idx, dqm, dkv_own, dkv_got, cosine, sine, w0, w1, w2, n0, n1, n2a, n2b, n3, gain_one, gain_grad_two,
-    mine, theirs, o0, o1, o2a, o2b, o3, n_all, dkv, out, grad, gains,
+    idx, dqm, dkv_own, dkv_got, cosine, sine, w0, w1, w2, n0, n1, n2a, n2b, n3, gain_one,
+    gain_grad_two,
+    mine, theirs, o0, o1, o2a, o2b, o3, n_all, dkv, grad, gains,
 ):
     x, y, core = idx[0], idx[2], idx[3]
     lo = low_lanes((BLK, 128))
     for ref, row, (_, n) in zip((n0, n1, n2a, n2b, n3), PIECE_ROW, PIECES):
         n_all[row : row + n, :] = ref[...]
-    slots = weight_rows(idx, DH)
-    total = jnp.zeros((8, D), F32)
-    for d, ref in ((2, None), (1, o1), (3, o3), (0, o0)):
+    for d in range(4):
         at = rows_at((x + d) & 3)
         v = dkv_own[at, :] + dkv_got[at, :].astype(F32)
         v = jnp.where(lo, v * cosine[at, :] - swap_halves(v) * sine[at, :], v).astype(BF16)
-        here = slice(d * BLK, (d + 1) * BLK)
-        dkv[here, :] = v
-        rows = jnp.concatenate([dqm[d], v], 1)
-        for s, w in zip(slots, (w0, w1, w2)):
-            out[:, s] = dot_t(rows, w[...])
-        res = out[...]
-        total = total + jnp.sum((res * n_all[here, :].astype(F32)).reshape(BLK // 8, 8, D), axis=0)
-        res = res.astype(BF16)
-        if d == 2:
-            o2a[...], o2b[...] = res[:HALF], res[HALF:]
-        else:
-            ref[...] = res
+        dkv[d * BLK : (d + 1) * BLK, :] = v
+    rows = jnp.concatenate([dqm[...], dkv[...]], 1)
+    for s, w in zip(weight_rows(idx, DH), (w0, w1, w2)):
+        for c in range(w.shape[0] // 512):
+            cols = pl.ds(pl.multiple_of(s.start + c * 512, 512), 512)
+            res = dot_t(rows, w[c * 512 : (c + 1) * 512, :])
+            part = (res * n_all[:, cols].astype(F32)).reshape(ROWS // 8, 8, 512)
+            gains[0:1, cols] = jnp.sum(jnp.sum(part, axis=0), axis=0, keepdims=True) / gain_one[:, cols]
+            store_parts(res, [r.at[:, cols] for r in (o0, o1, o2a, o2b, o3)])
     grad[...] = dot(dkv[...].T, n_all[...]).astype(BF16)
-    gains[0:1, :] = jnp.sum(total, axis=0, keepdims=True) / gain_one[...]
     gains[1:2, :] = gain_grad_two[...]
     for s in range(4):
         for k, ref in enumerate((mine, theirs)):
@@ -427,7 +418,6 @@
         scratch_shapes=[
             pltpu.VMEM((ROWS, D), BF16),
             pltpu.VMEM((ROWS, 128), BF16),
-            pltpu.VMEM((BLK, D), F32),
             pltpu.VMEM((128, D), BF16),
             pltpu.VMEM((2, D), F32),
         ],
@@ -453,7 +443,7 @@
 
 
 def ffn_body(
-    idx, n0, n1, n2a, n2b, n3, c0, c1, c2, c3, gate_own, up_own, gate_par, up_par, w0, w1, w2,
+    idx, n0, n1, n2a, n2b, n3, c0, c1, c2a, c2b, c3, gate_own, up_own, gate_par, up_par, w0, w1, w2,
     hid, dgate, dup, n_all, c_all, down, sem,
 ):
     i = pl.program_id(0)
@@ -464,10 +454,9 @@
         copies = load_down(idx, (w0, w1, w2), down, sem)
         for c in copies:
             c.start()
-        for ref, row, (_, n) in zip((n0, n1, n2a, n2b, n3), PIECE_ROW, PIECES):
-            n_all[row : row + n, :] = ref[...]
-        for d, ref in enumerate((c0, c1, c2, c3)):
-            c_all[d * BLK : (d + 1) * BLK, :] = ref[...]
+        for refs, dst in (((n0, n1, n2a, n2b, n3), n_all), ((c0, c1, c2a, c2b, c3), c_all)):
+            for ref, row, (_, n) in zip(refs, PIECE_ROW, PIECES):
+                dst[row : row + n, :] = ref[...]
         for c in copies:
             c.wait()
 
@@ -495,8 +484,7 @@
         grid=(TILES,),
         out_shape=(sds((ROWS, FF4)),) * 3,
         in_specs=[spec(pltpu.SMEM)]
-        + [whole(n, D) for _, n in PIECES]
-        + [whole(BLK, D)] * 4
+        + [whole(n, D) for _, n in PIECES] * 2
         + [column(0), column(0), column(0), column(TILES)]
         + [spec(pl.ANY)] * 3,
         out_specs=[hidden] * 3,
@@ -541,17 +529,13 @@
 def ffn_back_body(idx, dgate, dup, gate_own, up_own, par, *refs):
     half = pl.num_programs(0) // 2
 
-    def store(res):
-        for ref, row, (_, n) in zip(refs, PIECE_ROW, PIECES):
-            ref[...] = res[row : row + n].astype(BF16)
-
     @pl.when(pl.program_id(0) < half)
     def _():
-        store(dot_t(dgate[...], gate_own[...]) + dot_t(dup[...], up_own[...]))
+        store_parts(dot_t(dgate[...], gate_own[...]) + dot_t(dup[...], up_own[...]), refs)
 
     @pl.when(pl.program_id(0) >= half)
     def _():
-        store(dot_t(dgate[...], par[:, :FF4]) + dot_t(dup[...], par[:, GAP:]))
+        store_parts(dot_t(dgate[...], par[:, :FF4]) + dot_t(dup[...], par[:, GAP:]), refs)
 
 
 def ffn_back(idx, dgate, dup, gate, up, gate_up):
@@ -577,11 +561,12 @@
 
 GU_ROWS = FF4 // 128 * 64
 PIECE = 2 * GU_ROWS + FF4 // 2
+QS = 4
 
 
 def ffn_grads_body(*refs):
-    na, nb, cots = refs[0:5], refs[5:10], refs[10:14]
-    hid, dgate, dup, out, hid_t = refs[14:]
+    na, nb, cots = refs[0:5], refs[5:10], refs[10:15]
+    hid, dgate, dup, out, hid_t = refs[15:]
 
     @pl.when(pl.program_id(0) == 0)
     def _():
@@ -592,14 +577,14 @@
     for k, ref in enumerate((dgate, dup)):
         g = dot(rows, ref[...]).astype(BF16)
         for h in range(2):
-            for q in range(2):
-                r = g[(2 * h + q) * 64 : (2 * h + q + 1) * 64]
+            for q in range(QS):
+                r = g[(QS * h + q) * 64 : (QS * h + q + 1) * 64]
                 for c in range(FF4 // 128):
                     first = k * GU_ROWS + c * 64
                     out[h, q, first : first + 64, :] = r[:, c * 128 : (c + 1) * 128]
     g = dot(hid_t[...], stack(cots)).astype(BF16)
     for h in range(2):
-        for q in range(2):
+        for q in range(QS):
             out[h, q, 2 * GU_ROWS :, :] = g[
                 h * (FF4 // 2) : (h + 1) * (FF4 // 2), q * 128 : (q + 1) * 128
             ]
@@ -608,13 +593,13 @@
 def ffn_grads(normed, cots, hid, dgate, dup):
     return pl.pallas_call(
         ffn_grads_body,
-        grid=(8,),
+        grid=(16 // QS,),
         out_shape=sds((2, 16, PIECE, 128)),
-        in_specs=[pl.BlockSpec((n, 128), lambda i: (0, i)) for _, n in PIECES]
-        + [pl.BlockSpec((n, 128), lambda i: (0, i + 8)) for _, n in PIECES]
-        + [pl.BlockSpec((BLK, 256), lambda i: (0, i))] * 4
+        in_specs=[pl.BlockSpec((n, 64 * QS), lambda i: (0, i)) for _, n in PIECES]
+        + [pl.BlockSpec((n, 64 * QS), lambda i: (0, i + 16 // QS)) for _, n in PIECES]
+        + [pl.BlockSpec((n, 128 * QS), lambda i: (0, i)) for _, n in PIECES]
         + [whole(ROWS, FF4)] * 3,
-        out_specs=pl.BlockSpec((2, 2, PIECE, 128), lambda i: (0, i, 0, 0)),
+        out_specs=pl.BlockSpec((2, QS, PIECE, 128), lambda i: (0, i, 0, 0)),
         scratch_shapes=[pltpu.VMEM((FF4, ROWS), BF16)],
         compiler_params=params(),
         cost_estimate=cost(6 * ROWS * D * FF4, 3e7),
@@ -623,23 +608,25 @@
 
 
 def unpack_body(piece, gate, up, down):
-    for k, ref in enumerate((gate, up)):
-        for c in range(FF4 // 128):
-            first = k * GU_ROWS + c * 64
-            ref[:, c * 128 : (c + 1) * 128] = piece[0, first : first + 64, :].astype(F32)
-    down[...] = piece[0, 2 * GU_ROWS :, :].astype(F32)
+    for q in range(QS):
+        rows = slice(q * 64, (q + 1) * 64)
+        for k, ref in enumerate((gate, up)):
+            for c in range(FF4 // 128):
+                first = k * GU_ROWS + c * 64
+                ref[rows, c * 128 : (c + 1) * 128] = piece[q, first : first + 64, :].astype(F32)
+        down[:, q * 128 : (q + 1) * 128] = piece[q, 2 * GU_ROWS :, :].astype(F32)
 
 
 def unpack(pieces):
     return pl.pallas_call(
         unpack_body,
-        grid=(16,),
+        grid=(16 // QS,),
         out_shape=(sds((DH, FF4), F32), sds((DH, FF4), F32), sds((FF4 // 2, D), F32)),
-        in_specs=[pl.BlockSpec((1, PIECE, 128), lambda i: (i, 0, 0))],
+        in_specs=[pl.BlockSpec((QS, PIECE, 128), lambda i: (i, 0, 0))],
         out_specs=[
-            pl.BlockSpec((64, FF4), lambda i: (i, 0)),
-            pl.BlockSpec((64, FF4), lambda i: (i, 0)),
-            pl.BlockSpec((FF4 // 2, 128), lambda i: (0, i)),
+            pl.BlockSpec((64 * QS, FF4), lambda i: (i, 0)),
+            pl.BlockSpec((64 * QS, FF4), lambda i: (i, 0)),
+            pl.BlockSpec((FF4 // 2, 128 * QS), lambda i: (0, i)),
         ],
         compiler_params=params(),
         cost_estimate=cost(1e6, 2.6e7),
@@ -756,12 +743,13 @@
             gains[:, cols] = g[2 * c : 2 * c + 2]
 
 
-def sum_tail(idx, first, second):
+def sum_tail(idx, first, second, before):
     got_a = lax.ppermute(first[1], "core", shift(2, 1))
     got_b = lax.ppermute(second[1], "core", shift(2, 1))
     part = sds((2, TAIL, 128))
     g = small_call(sum_core_body, (part,) * 4, idx, first[0], got_a, second[0], got_b, name="sum_core")
-    got = [lax.ppermute(g[s], "y", shift(4, s)) for s in (2, 1, 3)]
+    summed = g[0]
+    got = [tie(lax.ppermute(g[s], "y", shift(4, s)), before) for s in (2, 1, 3)]
     part = sds((TAIL, 128))
     own, other = small_call(sum_y_body, (part,) * 2, idx, g[0], *got, name="sum_y")
     cross = [(2 * a + b, 2 * (1 - a) + (1 - b)) for a in range(2) for b in range(2)]
@@ -778,7 +766,7 @@
     mine = [g] + [lax.ppermute(g, "y", shift(4, s)) for s in (1, 2, 3)]
     theirs = [lax.ppermute(v, "core", shift(2, 1)) for v in mine]
     shapes = (sds((DH, QW), F32), sds((AW // 2, D), F32), sds((2, D), F32))
-    return small_call(unpack_tail_body, shapes, idx, *mine, *theirs, name="unpack_tail")
+    return summed, small_call(unpack_tail_body, shapes, idx, *mine, *theirs, name="unpack_tail")
 
 
 def inverse_rms(v):
@@ -811,17 +799,29 @@
 
     tok = tokens.astype(F32)
     s_one = inverse_rms(tok)
-    qkv_got = fetch_half(qkv_weight, core)
-    normed_one, sent = gather_x((tok * s_one * gain_one).astype(BF16), qkv_got)
-    qkv_all = qkv_weight, qkv_got, lax.ppermute(tie(qkv_got, *sent), "core", shift(2, 1))
-    out_all = fetch_partner(out_weight, core, *sent)
+    qkv_all = fetch_partner(qkv_weight, core)
+    normed_one = gather_x((tok * s_one * gain_one).astype(BF16))
+    out_all = fetch_partner(out_weight, core, normed_one[2])
+    cots = gather_x(tie(cotangent, normed_one[2]))
+
+    begin, position = replica_layout(seq_lengths, seq_replica, (y * 2 + zl) * 2 + core)
+    half_rows = lambda v: lax.dynamic_index_in_dim(v.reshape(4, 2, BLK), zh, 1, False).reshape(ROWS, 1)
+    first = jnp.tile(half_rows(begin)[3 * BLK :, 0], 8).reshape(1, QALL)
+    lane = jnp.arange(128, dtype=jnp.int32)
+    frequency = ROTARY_BASE ** (-(lane % 32).astype(F32) * (2.0 / HD))
+    angles = half_rows(position).astype(F32) * frequency[None, :]
+    cosine = jnp.cos(angles)
+    sine = jnp.where((lane % HD) < HD // 2, -1.0, 1.0)[None, :] * jnp.sin(angles)
+
+    q, kv_own = qkv_forward(idx, normed_one, qkv_all, cosine, sine)
+    kv_par = lax.ppermute(kv_own, "zh", shift(2, 1))
     rows = DH // 8
     mine = lambda w: lax.dynamic_slice_in_dim(w, (y * 2 + core) * rows, rows, 0)
     cross = [(2 * a + b, 2 * (1 - a) + (1 - b)) for a in range(2) for b in range(2)]
     gate_up = lax.ppermute(
         jnp.concatenate(
             [
-                tie(mine(gate_weight), out_all[1], normed_one[2], normed_one[3]),
+                tie(mine(gate_weight), kv_par),
                 jnp.zeros((rows, GAP - FF4), BF16),
                 mine(up_weight),
             ],
@@ -830,58 +830,54 @@
         ("zl", "zh"),
         cross,
     )
-    cots = gather_direct(tie(cotangent, normed_one[2]))
-
-    begin, position = replica_layout(seq_lengths, seq_replica, (y * 2 + zl) * 2 + core)
-    half_rows = lambda v: lax.dynamic_index_in_dim(v.reshape(4, 2, BLK), zh, 1, False).reshape(ROWS, 1)
-    first = jnp.tile(half_rows(begin)[3 * BLK :, 0], 8).reshape(1, QALL)
-    lane = jnp.arange(128, dtype=jnp.int32)
-    frequency = ROTARY_BASE ** (-(lane % 32).astype(F32) * (2.0 / HD))
-    angles = half_rows(position).astype(F32) * frequency[None, :]
-    cosine = jnp.cos(angles)
-    sine = jnp.where((lane % HD) < HD // 2, -1.0, 1.0)[None, :] * jnp.sin(angles)
-
-    q, kv_own = qkv_forward(idx, normed_one, qkv_all, cosine, sine)
-    kv_par = lax.ppermute(kv_own, "zh", shift(2, 1))
-    gate_up = lax.all_gather(tie(gate_up, kv_par), ("y", "core"), axis=0, tiled=True)
-    down_all = fetch_partner(down_weight, core, kv_par)
+    down_got = fetch_half(tie(down_weight, kv_par), core)
+    q = tie(q, cots[1], cots[4], out_all[1])
     att, qx = attend(idx, q, kv_own, kv_par, first)
-    parts = [tie(p, *cots) for p in out_project(idx, att, out_all)]
-    after_attn = tok + scatter_x(parts)
+    gate_up = lax.all_gather(tie(gate_up, qx), ("y", "core"), axis=0, tiled=True)
+    parts = [tie(p, cots[2], cots[3]) for p in out_project(idx, att, out_all)]
+    after_attn = tok + scatter_x(parts)[0]
 
     r_two = inverse_rms(after_attn)
-    normed_two, _ = gather_x((after_attn * r_two * gain_two).astype(BF16))
+    normed_two = gather_x((after_attn * r_two * gain_two).astype(BF16))
+    down_all = down_weight, down_got, lax.ppermute(tie(down_got, normed_two[1], normed_two[4]), "core", shift(2, 1))
     hid, dgate, dup = ffn(idx, normed_two, cots, gate_weight, up_weight, gate_up, down_all)
     own_grads = ffn_grads(normed_two, cots, hid, dgate, dup)
     grads = lax.psum_scatter(
         own_grads.reshape(32, PIECE, 128), ("zh", "zl", "y", "core"), scatter_dimension=0, tiled=True
     )
-    d_two = scatter_x(ffn_back(idx, tie(dgate, own_grads), dup, gate_weight, up_weight, gate_up))
+    d_two, _ = scatter_x(
+        ffn_back(idx, tie(dgate, own_grads), dup, gate_weight, up_weight, gate_up)
+    )
     back_two, gain_grad_two = norm_back(after_attn, r_two, gain_two, d_two)
     after_grad = cotangent.astype(F32) + back_two
-    branch, _ = gather_x(after_grad.astype(BF16))
+    branch = gather_x(after_grad.astype(BF16))
     layer_parts = down_project(idx, tie(hid, after_grad), down_all)
     att = tie(att, *layer_parts)
+    layer = [layer_parts[0]] + [
+        lax.ppermute(tie(layer_parts[k], branch[2], branch[3]), "x", shift(4, k)) for k in (1, 3)
+    ]
     dqm, dkv_own, dkv_par = attend_back(
         idx, qx, kv_own, kv_par, first, att, cosine, sine, branch, out_all
     )
     dkv_got = lax.ppermute(dkv_par, "zh", shift(2, 1))
-    tail = attn_grads(idx, normed_one, branch, dqm.reshape(ROWS, AW), att.reshape(ROWS, AW))
-    dkv_got = tie(dkv_got, tail[0])
+    tail = attn_grads(
+        idx, normed_one, branch, dqm.reshape(ROWS, AW), tie(att, *layer).reshape(ROWS, AW)
+    )
     *tail_kv, parts = qkv_back(
-        idx, dqm, dkv_own, dkv_got, cosine, sine, qkv_all, normed_one, gain_one,
+        idx, dqm.reshape(ROWS, AW), dkv_own, dkv_got, cosine, sine, qkv_all, normed_one, gain_one,
         gain_grad_two,
     )
-    grads = lax.all_gather(tie(grads, dkv_got), ("zl", "y", "core"), axis=0, tiled=True)
-    grad_gate, grad_up, grad_down = unpack(grads)
-    d_one = scatter_x(parts)
-    layer_parts = [tie(p, d_one) for p in layer_parts]
-    layer_out = (after_attn + scatter_direct(layer_parts)).astype(BF16)
+    d_one, first_step = scatter_x(parts)
+    layer.append(lax.ppermute(tie(layer_parts[2], d_one), "x", shift(4, 2)))
+    layer_out = sum((v.astype(F32) for v in layer), after_attn).astype(BF16)
     back_one, _ = norm_back(tok, s_one, gain_one, d_one)
     input_grad = (after_grad + back_one).astype(BF16)
 
     over_x = lambda v: sum((lax.ppermute(v, "x", shift(4, s)) for s in (1, 2, 3)), v)
-    grad_qkv, grad_out, gains = sum_tail(idx, tail, tail_kv)
+    tail = tie(tail[0], *first_step), tie(tail[1], dkv_got)
+    summed, (grad_qkv, grad_out, gains) = sum_tail(idx, tail, tail_kv, d_one)
+    grads = lax.all_gather(tie(grads, summed), ("zl", "y", "core"), axis=0, tiled=True)
+    grad_gate, grad_up, grad_down = unpack(grads)
     gains = over_x(gains)
     return (
         layer_out, input_grad, gains[0], grad_qkv, grad_out, grad_gate, grad_up,

time: 512 us -> 490 us (0.957)
  waiting for transfers between devices: 204 us -> 182 us
  Pallas kernels: 152 us -> 146 us
    ppermute x11 -> x8, waiting for transfers between devices: 66.4 us -> 40.3 us  [the longest x3 31.3 us: sum_tail(): got = [tie(lax.ppermute(g[s], 'y', shift(4, s)), before) for s in (2, 1, 3)]]
    ppermute x3 -> x4, waiting for transfers between devices: 25.6 us -> 2.03 us  [gather_x(): from_prev = lax.ppermute(v, 'x', shift(4, 1))]
    ppermute x3, waiting for transfers between devices: 15 us -> 34.1 us  [fetch_half(): lax.ppermute(lax.dynamic_slice_in_dim(w, core * half, half, 0), 'zh', shi...]
    reduce_scatter x1, waiting for transfers between devices: 17.2 us -> 0.01 us  [on_device(): lax.psum_scatter(own_grads.reshape(32, PIECE, 128), ('zh', 'zl', 'y', 'co...]
    ppermute x4, starting transfers between devices: 7.66 us -> 18.2 us  [sum_tail(): theirs = [lax.ppermute(v, 'core', shift(2, 1)) for v in mine]]
    ppermute x11 -> x8, starting transfers between devices: 23.7 us -> 14.8 us  [the longest x3 5.26 us: sum_tail(): got = [tie(lax.ppermute(g[s], 'y', shift(4, s)), before) for s in (2, 1, 3)]]
    ppermute x3, waiting for transfers between devices: 10.8 us -> 18.4 us  [scatter_x(): from_next = lax.ppermute(q3, 'x', shift(4, -1))]
    ppermute x3, waiting for transfers between devices: 6.1 us -> 12.4 us  [scatter_x(): got_a = lax.ppermute(p2a, 'x', shift(4, 1))]
  transfers between devices with their start and end apart: 60 -> 61, of which waited for: 31 -> 28; matrix products, arithmetic and copies ran while one was open for 6% -> 6% of each run, Pallas kernels for 19% -> 20%
where the time goes in v5:
time: 490 us; the launch traced here: 482 us
  waiting for transfers between devices  182 us (37%)
  Pallas kernels  146 us (30%)
  starting transfers between devices  96.7 us (20%)
  local copies, waits for them, and re-layouts  24.2 us (5%)
  other arithmetic  18.3 us (4%)
  between operations  15.1 us (3%)
    ppermute x3, waiting for transfers between devices, fetch_half(): lax.ppermute(lax.dynamic_slice_in_dim(w, core * half, half, 0), 'zh', shi...  34.1 us
    ppermute x3, waiting for transfers between devices, sum_tail(): got = [tie(lax.ppermute(g[s], 'y', shift(4, s)), before) for s in (2, 1, 3)]  31.3 us
    pallas_call x1, Pallas kernels, ffn(): pl.pallas_call(ffn_body, grid=(TILES,), out_shape=(sds((ROWS, FF4)),) * 3...  20.9 us
    pallas_call x1, Pallas kernels, ffn_grads(): pl.pallas_call(ffn_grads_body, grid=(16 // QS,), out_shape=sds((2, 16, PI...  20.8 us
    pallas_call x1, Pallas kernels, attend_back(): pl.pallas_call(attend_back_body, out_shape=(sds((4, BLK, AW)), sds((ROWS,...  19.8 us
    ppermute x3, waiting for transfers between devices, scatter_x(): from_next = lax.ppermute(q3, 'x', shift(4, -1))  18.4 us
    ppermute x4, starting transfers between devices, sum_tail(): theirs = [lax.ppermute(v, 'core', shift(2, 1)) for v in mine]  18.2 us
    pallas_call x1, Pallas kernels, ffn_back(): pl.pallas_call(ffn_back_body, grid_spec=pltpu.PrefetchScalarGridSpec(num_...  15.8 us
  transfers between devices with their start and end apart: 61, of which 28 were waited for; matrix products, arithmetic and copies ran while one was open for 6% of the time, Pallas kernels for 20%

profile of v5, /device:TPU:1, one launch (start us, length us, event | category | flops | bytes accessed | tf_op | source)
XLA Modules:
  0.0 482.1 jit_solution(4982622055713460356)
XLA Ops:
  14.4 3.7 collective-permute-start.4
  21.8 10.4 %collective-permute-done.4.w1 = bf16[512,640]{1,0:T(8,128)(2,1)} collective-permute-done((bf16[512,640]{1,0:T(8,128)(2,1)}, bf16[512,640]{1,0:T(8,128)(2,1)}, u32[]{:S(2)}, u32[]{:S(2)}) %collective-permute-start.4) | collective-permute-done | bytes 655392 | tf_op jit(solution)/shard_map/ppermute | solution.py:113
  39.5 7.4 %collective-permute-done.2.n2a.refs_2_.refs_7_ = bf16[80,2048]{1,0:T(8,128)(2,1)S(1)} collective-permute-done((bf16[80,2048]{1,0:T(8,128)(2,1)S(1)}, bf16[80,2048]{1,0:T(8,128)(2,1)S(1)}, u32[]{:S(2)}, u32[]{:S(2)}) %collective-permute-start.2) | collective-permute-done | bytes 327712 | tf_op jit(solution)/shard_map/ppermute | solution.py:74
  46.9 2.7 collective-permute-start.6
  50.3 6.8 %qkv_forward.1 = (bf16[4,1280,128]{2,1,0:T(8,128)(2,1)}, bf16[640,128]{1,0:T(8,128)(2,1)}) custom-call(s32[4]{0:T(128)} %pad_add_fusion.idx, bf16[160,2048]{1,0:T(8,128)(2,1)} %copy-done.2, bf16[160,2048]{1,0:T(8,128)(2,1)} %copy-done.5, bf16[80,2048]{1,0:T(8,128)(2,1)} %copy-done.25, bf16[80,2048]{1,0:T(8,128)(2,1)} %copy-done.24, ...), custom_call_target="tpu_custom_call" | custom-call | flops 1677721600 | bytes 7000000 | tf_op jit(solution)/shard_map/qkv_forward/pallas_call | solution.py:154
  57.0 3.0 collective-permute-start.9
  63.0 3.4 collective-permute-start.21
  66.5 7.7 %collective-permute-done.8.w1 = bf16[128,2048]{1,0:T(8,128)(2,1)S(1)} collective-permute-done((bf16[128,2048]{1,0:T(8,128)(2,1)S(1)}, bf16[128,2048]{1,0:T(8,128)(2,1)S(1)}, u32[]{:S(2)}, u32[]{:S(2)}) %collective-permute-start.8) | collective-permute-done | bytes 524320 | tf_op jit(solution)/shard_map/ppermute | solution.py:113
  75.0 8.7 %attend.1 = (bf16[4,160,512]{2,1,0:T(8,128)(2,1)}, bf16[4,1280,128]{2,1,0:T(8,128)(2,1)}) custom-call(s32[4]{0:T(128)} %pad_add_fusion.idx, bf16[4,1280,128]{2,1,0:T(8,128)(2,1)} %get-tuple-element.92.q, bf16[640,128]{1,0:T(8,128)(2,1)} %get-tuple-element.93.kv_own, bf16[640,128]{1,0:T(8,128)(2,1)} %copy-done.63, s32[1,1280]{1,0:T(1,128)} %reshape_tile.3.first), custom_call_target="tpu_custom_call" | custom-call | flops 12000000000 | bytes 3000000 | tf_op jit(solution)/shard_map/attend/pallas_call | solution.py:247
  83.7 9.0 %collective-permute-done.21 = bf16[128,2944]{1,0:T(8,128)(2,1)S(1)} collective-permute-done((bf16[128,2944]{1,0:T(8,128)(2,1)S(1)}, bf16[128,2944]{1,0:T(8,128)(2,1)S(1)}, u32[]{:S(2)}, u32[]{:S(2)}) %collective-permute-start.21) | collective-permute-done | bytes 753696 | tf_op jit(solution)/shard_map/ppermute | solution.py:821
  98.5 4.8 out_project.1
  111.5 4.9 %collective-permute-done.13 = bf16[80,2048]{1,0:T(8,128)(2,1)S(1)} collective-permute-done((bf16[80,2048]{1,0:T(8,128)(2,1)}, bf16[80,2048]{1,0:T(8,128)(2,1)S(1)}, u32[]{:S(2)}, u32[]{:S(2)}) %collective-permute-start.13) | collective-permute-done | bytes 327712 | tf_op jit(solution)/shard_map/ppermute | solution.py:81
  117.3 3.6 collective-permute-start.16
  122.5 2.7 collective-permute-start.22
  125.2 7.0 %collective-permute-done.14 = bf16[160,2048]{1,0:T(8,128)(2,1)S(1)} collective-permute-done((bf16[160,2048]{1,0:T(8,128)(2,1)S(1)}, bf16[160,2048]{1,0:T(8,128)(2,1)S(1)}, u32[]{:S(2)}, u32[]{:S(2)}) %collective-permute-start.14) | collective-permute-done | bytes 655392 | tf_op jit(solution)/shard_map/ppermute | solution.py:85
  135.1 3.6 collective-permute-start.17
  138.7 16.0 %collective-permute-done.22.w1 = bf16[352,2048]{1,0:T(8,128)(2,1)S(1)} collective-permute-done((bf16[352,2048]{1,0:T(8,128)(2,1)S(1)}, bf16[352,2048]{1,0:T(8,128)(2,1)S(1)}, u32[]{:S(2)}, u32[]{:S(2)}) %collective-permute-start.22) | collective-permute-done | bytes 1441824 | tf_op jit(solution)/shard_map/ppermute | solution.py:113
  154.7 3.4 collective-permute-start.23
  159.8 7.9 %collective-permute-done.20.n2b.refs_3_.refs_8_ = bf16[80,2048]{1,0:T(8,128)(2,1)S(1)} collective-permute-done((bf16[80,2048]{1,0:T(8,128)(2,1)S(1)}, bf16[80,2048]{1,0:T(8,128)(2,1)S(1)}, u32[]{:S(2)}, u32[]{:S(2)}) %collective-permute-start.20) | collective-permute-done | bytes 327712 | tf_op jit(solution)/shard_map/ppermute | solution.py:75
  169.4 20.9 %ffn.1 = (bf16[640,1408]{1,0:T(8,128)(2,1)}, bf16[640,1408]{1,0:T(8,128)(2,1)}, bf16[640,1408]{1,0:T(8,128)(2,1)}) custom-call(s32[4]{0:T(128)} %pad_add_fusion.idx, bf16[160,2048]{1,0:T(8,128)(2,1)} %copy-done.15, bf16[160,2048]{1,0:T(8,128)(2,1)} %copy-done.42, bf16[80,2048]{1,0:T(8,128)(2,1)} %copy-done.62, bf16[80,2048]{1,0:T(8,128)(2,1)} %copy-done.60, ...), custom_call_target="tpu_custom_call" | custom-call | flops 11072962560 | bytes 34000000 | tf_op jit(solution)/shard_map/ffn/pallas_call | solution.py:482
  190.3 20.8 %ffn_grads.1 = bf16[2,16,2112,128]{3,2,1,0:T(8,128)(2,1)} custom-call(bf16[160,2048]{1,0:T(8,128)(2,1)} %copy-done.15, bf16[160,2048]{1,0:T(8,128)(2,1)} %copy-done.42, bf16[80,2048]{1,0:T(8,128)(2,1)} %copy-done.62, bf16[80,2048]{1,0:T(8,128)(2,1)} %copy-done.60, bf16[160,2048]{1,0:T(8,128)(2,1)} %copy-done.41, bf16[160,2048]{1,0:T(8,128)(2,1)} %copy-done.15, ...), custom_call_target="tpu_custom_call" | custom-call | flops 11072962560 | bytes 30000000 | tf_op jit(solution)/shard_map/ffn_grads/pallas_call | solution.py:594
  211.1 15.8 %ffn_back.1 = (bf16[160,2048]{1,0:T(8,128)(2,1)}, bf16[160,2048]{1,0:T(8,128)(2,1)}, bf16[80,2048]{1,0:T(8,128)(2,1)}, bf16[80,2048]{1,0:T(8,128)(2,1)}, bf16[160,2048]{1,0:T(8,128)(2,1)}) custom-call(s32[4]{0:T(128)} %pad_add_fusion.idx, bf16[640,1408]{1,0:T(8,128)(2,1)} %get-tuple-element.117.refs_16_.dgate, ...), custom_call_target="tpu_custom_call" | custom-call | flops 7381975040 | bytes 18000000 | tf_op jit(solution)/shard_map/ffn_back/pallas_call | solution.py:547
  230.6 4.3 collective-permute-done.26
  235.1 3.0 collective-permute-start.27
  239.9 10.7 %collective-permute-done.27 = bf16[160,2048]{1,0:T(8,128)(2,1)S(1)} collective-permute-done((bf16[160,2048]{1,0:T(8,128)(2,1)S(1)}, bf16[160,2048]{1,0:T(8,128)(2,1)S(1)}, u32[]{:S(2)}, u32[]{:S(2)}) %collective-permute-start.27) | collective-permute-done | bytes 655392 | tf_op jit(solution)/shard_map/ppermute | solution.py:86
  250.6 4.8 collective-permute-done.25
  259.8 12.0 %collective-permute-done.29.b1.refs_11_ = bf16[160,2048]{1,0:T(8,128)(2,1)S(1)} collective-permute-done((bf16[160,2048]{1,0:T(8,128)(2,1)S(1)}, bf16[160,2048]{1,0:T(8,128)(2,1)S(1)}, u32[]{:S(2)}, u32[]{:S(2)}) %collective-permute-start.29) | collective-permute-done | bytes 655392 | tf_op jit(solution)/shard_map/ppermute | solution.py:71
  276.7 10.0 %down_project.1 = (bf16[160,2048]{1,0:T(8,128)(2,1)}, bf16[160,2048]{1,0:T(8,128)(2,1)}, bf16[160,2048]{1,0:T(8,128)(2,1)}, bf16[160,2048]{1,0:T(8,128)(2,1)}) custom-call(s32[4]{0:T(128)} %pad_add_fusion.idx, bf16[640,1408]{1,0:T(8,128)(2,1)} %get-tuple-element.123.refs_15_.hid, bf16[704,2048]{1,0:T(8,128)(2,1)} %w0.9, bf16[352,2048]{1,0:T(8,128)(2,1)} %copy-done.48, ...), custom_call_target="tpu_custom_call" | custom-call | flops 3690987520 | bytes 11000000 | tf_op jit(solution)/shard_map/down_project/pallas_call | solution.py:517
  288.1 2.7 collective-permute-start.33
  290.8 19.8 %attend_back.1 = (bf16[4,160,512]{2,1,0:T(8,128)(2,1)}, f32[640,128]{1,0:T(8,128)}, bf16[640,128]{1,0:T(8,128)(2,1)}) custom-call(s32[4]{0:T(128)} %pad_add_fusion.idx, bf16[4,1280,128]{2,1,0:T(8,128)(2,1)} %get-tuple-element.110.qx, bf16[640,128]{1,0:T(8,128)(2,1)} %get-tuple-element.93.kv_own, bf16[640,128]{1,0:T(8,128)(2,1)} %copy-done.63, ...), custom_call_target="tpu_custom_call" | custom-call | flops 30000001024 | bytes 8000000 | tf_op jit(solution)/shard_map/attend_back/pallas_call | solution.py:356
  310.6 3.4 collective-permute-start.34
  314.0 8.9 %attn_grads.1 = (bf16[4,2,1024,128]{3,2,1,0:T(8,128)(2,1)}, bf16[4,2,1024,128]{3,2,1,0:T(8,128)(2,1)}) custom-call(s32[4]{0:T(128)} %pad_add_fusion.idx, bf16[160,2048]{1,0:T(8,128)(2,1)} %copy-done.2, bf16[160,2048]{1,0:T(8,128)(2,1)} %copy-done.5, bf16[80,2048]{1,0:T(8,128)(2,1)} %copy-done.25, bf16[80,2048]{1,0:T(8,128)(2,1)} %copy-done.24, ...), custom_call_target="tpu_custom_call" | custom-call | flops 2684354560 | bytes 10000000 | tf_op jit(solution)/shard_map/attn_grads/pallas_call | solution.py:676
  323.0 5.3 %collective-permute-start.40 = (bf16[4,2,1024,128]{3,2,1,0:T(8,128)(2,1)}, bf16[4,2,1024,128]{3,2,1,0:T(8,128)(2,1)}, u32[]{:S(2)}, u32[]{:S(2)}) collective-permute-start(bf16[4,2,1024,128]{3,2,1,0:T(8,128)(2,1)} %get-tuple-element.146), channel_id=1, source_target_pairs={{0,8},{8,0},{1,9},{9,1},{2,10},{10,2},{3,11},{11,3},{4,12},{12,4},... | collective-permute-start | bytes 6291464 | tf_op jit(solution)/shard_map/ppermute | solution.py:747
  328.3 7.3 %qkv_back.1 = (bf16[4,2,144,128]{3,2,1,0:T(8,128)(2,1)}, bf16[4,2,144,128]{3,2,1,0:T(8,128)(2,1)}, bf16[160,2048]{1,0:T(8,128)(2,1)}, bf16[160,2048]{1,0:T(8,128...) custom-call(s32[4]{0:T(128)} %pad_add_fusion.idx, ...), custom_call_target="tpu_custom_call" | custom-call | flops 1677721600 | bytes 13000000 | tf_op jit(solution)/shard_map/qkv_back/pallas_call | solution.py:413
  339.5 6.2 %collective-permute-done.35 = bf16[80,2048]{1,0:T(8,128)(2,1)S(1)} collective-permute-done((bf16[80,2048]{1,0:T(8,128)(2,1)}, bf16[80,2048]{1,0:T(8,128)(2,1)S(1)}, u32[]{:S(2)}, u32[]{:S(2)}) %collective-permute-start.35) | collective-permute-done | bytes 327712 | tf_op jit(solution)/shard_map/ppermute | solution.py:81
  346.6 3.9 sum_core.1
  359.8 7.1 %collective-permute-done.38 = bf16[160,2048]{1,0:T(8,128)(2,1)S(1)} collective-permute-done((bf16[160,2048]{1,0:T(8,128)(2,1)S(1)}, bf16[160,2048]{1,0:T(8,128)(2,1)S(1)}, u32[]{:S(2)}, u32[]{:S(2)}) %collective-permute-start.38) | collective-permute-done | bytes 655392 | tf_op jit(solution)/shard_map/ppermute | solution.py:86
  366.9 3.1 collective-permute-done.36
  370.5 5.7 %collective-permute-done.42.b = bf16[2,1168,128]{2,1,0:T(8,128)(2,1)} collective-permute-done((bf16[2,1168,128]{2,1,0:T(8,128)(2,1)S(1)}, bf16[2,1168,128]{2,1,0:T(8,128)(2,1)}, u32[]{:S(2)}, u32[]{:S(2)}) %collective-permute-start.42) | collective-permute-done | bytes 598048 | tf_op jit(solution)/shard_map/ppermute | solution.py:752
  376.2 25.6 %collective-permute-done.43.c = bf16[2,1168,128]{2,1,0:T(8,128)(2,1)} collective-permute-done((bf16[2,1168,128]{2,1,0:T(8,128)(2,1)S(1)}, bf16[2,1168,128]{2,1,0:T(8,128)(2,1)}, u32[]{:S(2)}, u32[]{:S(2)}) %collective-permute-start.43) | collective-permute-done | bytes 598048 | tf_op jit(solution)/shard_map/ppermute | solution.py:752
  404.5 3.5 collective-permute-start.46
  408.1 7.7 %collective-permute-done.45.b = bf16[1168,128]{1,0:T(8,128)(2,1)S(1)} collective-permute-done((bf16[1168,128]{1,0:T(8,128)(2,1)}, bf16[1168,128]{1,0:T(8,128)(2,1)S(1)}, u32[]{:S(2)}, u32[]{:S(2)}) %collective-permute-start.45) | collective-permute-done | bytes 299040 | tf_op jit(solution)/shard_map/ppermute | solution.py:761
  415.8 12.2 %collective-permute-done.46.c = bf16[1168,128]{1,0:T(8,128)(2,1)} collective-permute-done((bf16[1168,128]{1,0:T(8,128)(2,1)}, bf16[1168,128]{1,0:T(8,128)(2,1)}, u32[]{:S(2)}, u32[]{:S(2)}) %collective-permute-start.46) | collective-permute-done | bytes 299040 | tf_op jit(solution)/shard_map/ppermute | solution.py:762
  431.5 9.6 %collective-permute-start.51 = (bf16[1168,128]{1,0:T(8,128)(2,1)}, bf16[1168,128]{1,0:T(8,128)(2,1)S(1)}, u32[]{:S(2)}, u32[]{:S(2)}) collective-permute-start(bf16[1168,128]{1,0:T(8,128)(2,1)} %sum_z.1.refs_0_), channel_id=1, source_target_pairs={{0,8},{8,0},{1,9},{9,1},{2,10},{10,2},{3,11},{11,3},{4,12},{12,4},... | collective-permute-start | bytes 897032 | tf_op jit(solution)/shard_map/ppermute | solution.py:767
  441.1 3.3 collective-permute-start.54
  446.6 3.1 collective-permute-start.52
  453.9 4.2 unpack_tail.1
  465.4 9.8 %unpack.1 = (f32[1024,1408]{1,0:T(8,128)}, f32[1024,1408]{1,0:T(8,128)}, f32[704,2048]{1,0:T(8,128)}) custom-call(bf16[16,2112,128]{2,1,0:T(8,128)(2,1)} %all-gather.5.cloned.1.call-done.piece), custom_call_target="tpu_custom_call" | custom-call | flops 1000000 | bytes 26000000 | tf_op jit(solution)/shard_map/unpack/pallas_call | solution.py:621
  (286 shorter events, 96.0 us)
Async XLA Ops:
  7.2 162.2 %all-gather.3.cloned.1.call-start = ((), (), s32[]{:S(2)}) async-start(), calls=%async_computation.1 | async-start | bytes 6782976 | tf_op jit(solution)/shard_map/all_gather | solution.py:836
  10.0 25.2 %collective-permute-start.1 = (bf16[160,2048]{1,0:T(8,128)(2,1)S(1)}, bf16[160,2048]{1,0:T(8,128)(2,1)S(1)}, u32[]{:S(2)}, u32[]{:S(2)}) collective-permute-start(bf16[160,2048]{1,0:T(8,128)(2,1)S(1)} %fusion.2.n0.refs_0_.refs_5_), channel_id=1, source_target_pairs={{0,2},{2,4},{4,6},{6,0},{1,3},{3,5},{5,7},{7,1},{8,10},{10,12},{12... | collective-permute-start | bytes 1966088 | tf_op jit(solution)/shard_map/ppermute | solution.py:70
  12.1 23.1 %collective-permute-start = (bf16[160,2048]{1,0:T(8,128)(2,1)S(1)}, bf16[160,2048]{1,0:T(8,128)(2,1)S(1)}, u32[]{:S(2)}, u32[]{:S(2)}) collective-permute-start(bf16[160,2048]{1,0:T(8,128)(2,1)S(1)} %fusion.2.n0.refs_0_.refs_5_), channel_id=1, source_target_pairs={{0,6},{2,0},{4,2},{6,4},{1,7},{3,1},{5,3},{7,5},{8,14},{10,8},{12,... | collective-permute-start | bytes 1966088 | tf_op jit(solution)/shard_map/ppermute | solution.py:71
  14.4 17.8 %collective-permute-start.4 = (bf16[512,640]{1,0:T(8,128)(2,1)}, bf16[512,640]{1,0:T(8,128)(2,1)}, u32[]{:S(2)}, u32[]{:S(2)}) collective-permute-start(bf16[512,640]{1,0:T(8,128)(2,1)} %constant_dynamic-slice_fusion.5), channel_id=1, source_target_pairs={{0,1},{1,0},{2,3},{3,2},{4,5},{5,4},{6,7},{7,6},{8,9},{9,8},{10,11... | collective-permute-start | bytes 1966088 | tf_op jit(solution)/shard_map/ppermute | solution.py:113
  32.2 17.3 %collective-permute-start.5 = (bf16[512,640]{1,0:T(8,128)(2,1)}, bf16[512,640]{1,0:T(8,128)(2,1)}, u32[]{:S(2)}, u32[]{:S(2)}) collective-permute-start(bf16[512,640]{1,0:T(8,128)(2,1)} %collective-permute-done.4.w1), channel_id=1, source_target_pairs={{0,8},{8,0},{1,9},{9,1},{2,10},{10,2},{3,11},{11,3},{4,12},{12,4},... | collective-permute-start | bytes 1966088 | tf_op jit(solution)/shard_map/ppermute | solution.py:118
  35.3 14.3 %collective-permute-start.3 = (bf16[80,2048]{1,0:T(8,128)(2,1)S(1)}, bf16[80,2048]{1,0:T(8,128)(2,1)S(1)}, u32[]{:S(2)}, u32[]{:S(2)}) collective-permute-start(bf16[80,2048]{1,0:T(8,128)(2,1)S(1)} %slice.94), channel_id=1, source_target_pairs={{0,6},{2,0},{4,2},{6,4},{1,7},{3,1},{5,3},{7,5},{8,14},{10,8},{12,... | collective-permute-start | bytes 983048 | tf_op jit(solution)/shard_map/ppermute | solution.py:75
  36.6 10.2 %collective-permute-start.2 = (bf16[80,2048]{1,0:T(8,128)(2,1)S(1)}, bf16[80,2048]{1,0:T(8,128)(2,1)S(1)}, u32[]{:S(2)}, u32[]{:S(2)}) collective-permute-start(bf16[80,2048]{1,0:T(8,128)(2,1)S(1)} %slice.93), channel_id=1, source_target_pairs={{0,2},{2,4},{4,6},{6,0},{1,3},{3,5},{5,7},{7,1},{8,10},{10,12},{12... | collective-permute-start | bytes 983048 | tf_op jit(solution)/shard_map/ppermute | solution.py:74
  46.9 27.3 %collective-permute-start.7 = (bf16[160,2048]{1,0:T(8,128)(2,1)S(1)}, bf16[160,2048]{1,0:T(8,128)(2,1)}, u32[]{:S(2)}, u32[]{:S(2)}) collective-permute-start(bf16[160,2048]{1,0:T(8,128)(2,1)S(1)} %copy-done.7), channel_id=1, source_target_pairs={{0,2},{2,4},{4,6},{6,0},{1,3},{3,5},{5,7},{7,1},{8,10},{10,12},{12... | collective-permute-start | bytes 1966088 | tf_op jit(solution)/shard_map/ppermute | solution.py:70
  46.9 27.3 %collective-permute-start.6 = (bf16[160,2048]{1,0:T(8,128)(2,1)S(1)}, bf16[160,2048]{1,0:T(8,128)(2,1)}, u32[]{:S(2)}, u32[]{:S(2)}) collective-permute-start(bf16[160,2048]{1,0:T(8,128)(2,1)S(1)} %copy-done.7), channel_id=1, source_target_pairs={{0,6},{2,0},{4,2},{6,4},{1,7},{3,1},{5,3},{7,5},{8,14},{10,8},{12,... | collective-permute-start | bytes 1966088 | tf_op jit(solution)/shard_map/ppermute | solution.py:71
  61.1 13.1 %collective-permute-start.8 = (bf16[128,2048]{1,0:T(8,128)(2,1)S(1)}, bf16[128,2048]{1,0:T(8,128)(2,1)S(1)}, u32[]{:S(2)}, u32[]{:S(2)}) collective-permute-start(bf16[128,2048]{1,0:T(8,128)(2,1)S(1)} %constant_dynamic-slice_fusion.4), channel_id=1, source_target_pairs={{0,1},{1,0},{2,3},{3,2},{4,5},{5,4},{6,7},{7,6},{8,9},{9,8},{10,11... | collective-permute-start | bytes 1572872 | tf_op jit(solution)/shard_map/ppermute | solution.py:113
  63.0 29.6 %collective-permute-start.21 = (bf16[128,2944]{1,0:T(8,128)(2,1)S(1)}, bf16[128,2944]{1,0:T(8,128)(2,1)S(1)}, u32[]{:S(2)}, u32[]{:S(2)}) collective-permute-start(bf16[128,2944]{1,0:T(8,128)(2,1)S(1)} %pad_maximum_fusion), channel_id=1, source_target_pairs={{0,17},{1,16},{16,1},{17,0},{2,19},{3,18},{18,3},{19,2},{4,21},{5,... | collective-permute-start | bytes 2261000 | tf_op jit(solution)/shard_map/ppermute | solution.py:821
  93.5 257.0 %reduce-scatter.2.cloned.1.call-start = ((), (), s32[]{:S(2)}) async-start(), calls=%async_computation.2 | async-start | bytes 17842176 | tf_op jit(solution)/shard_map/reduce_scatter | solution.py:845
  96.3 10.4 %collective-permute-start.11 = (bf16[80,2048]{1,0:T(8,128)(2,1)S(1)}, bf16[80,2048]{1,0:T(8,128)(2,1)S(1)}, u32[]{:S(2)}, u32[]{:S(2)}) collective-permute-start(bf16[80,2048]{1,0:T(8,128)(2,1)S(1)} %slice.95), channel_id=1, source_target_pairs={{0,2},{2,4},{4,6},{6,0},{1,3},{3,5},{5,7},{7,1},{8,10},{10,12},{12... | collective-permute-start | bytes 983048 | tf_op jit(solution)/shard_map/ppermute | solution.py:74
  106.6 9.7 %collective-permute-start.13 = (bf16[80,2048]{1,0:T(8,128)(2,1)}, bf16[80,2048]{1,0:T(8,128)(2,1)S(1)}, u32[]{:S(2)}, u32[]{:S(2)}) collective-permute-start(bf16[80,2048]{1,0:T(8,128)(2,1)} %get-tuple-element.102), channel_id=1, source_target_pairs={{0,2},{2,4},{4,6},{6,0},{1,3},{3,5},{5,7},{7,1},{8,10},{10,12},{12... | collective-permute-start | bytes 983048 | tf_op jit(solution)/shard_map/ppermute | solution.py:81
  116.5 15.7 %collective-permute-start.14 = (bf16[160,2048]{1,0:T(8,128)(2,1)S(1)}, bf16[160,2048]{1,0:T(8,128)(2,1)S(1)}, u32[]{:S(2)}, u32[]{:S(2)}) collective-permute-start(bf16[160,2048]{1,0:T(8,128)(2,1)S(1)} %pad_maximum_fusion.1), channel_id=1, source_target_pairs={{0,2},{2,4},{4,6},{6,0},{1,3},{3,5},{5,7},{7,1},{8,10},{10,12},{12... | collective-permute-start | bytes 1966088 | tf_op jit(solution)/shard_map/ppermute | solution.py:85
  117.3 15.5 %collective-permute-start.16 = (bf16[160,2048]{1,0:T(8,128)(2,1)S(1)}, bf16[160,2048]{1,0:T(8,128)(2,1)}, u32[]{:S(2)}, u32[]{:S(2)}) collective-permute-start(bf16[160,2048]{1,0:T(8,128)(2,1)S(1)} %pad_maximum_fusion.2), channel_id=1, source_target_pairs={{0,6},{2,0},{4,2},{6,4},{1,7},{3,1},{5,3},{7,5},{8,14},{10,8},{12,... | collective-permute-start | bytes 1966088 | tf_op jit(solution)/shard_map/ppermute | solution.py:86
  122.5 32.2 %collective-permute-start.22 = (bf16[352,2048]{1,0:T(8,128)(2,1)S(1)}, bf16[352,2048]{1,0:T(8,128)(2,1)S(1)}, u32[]{:S(2)}, u32[]{:S(2)}) collective-permute-start(bf16[352,2048]{1,0:T(8,128)(2,1)S(1)} %constant_dynamic-slice_fusion), channel_id=1, source_target_pairs={{0,1},{1,0},{2,3},{3,2},{4,5},{5,4},{6,7},{7,6},{8,9},{9,8},{10,11... | collective-permute-start | bytes 4325384 | tf_op jit(solution)/shard_map/ppermute | solution.py:113
  134.6 20.1 %collective-permute-start.18 = (bf16[160,2048]{1,0:T(8,128)(2,1)S(1)}, bf16[160,2048]{1,0:T(8,128)(2,1)S(1)}, u32[]{:S(2)}, u32[]{:S(2)}) collective-permute-start(bf16[160,2048]{1,0:T(8,128)(2,1)S(1)} %multiply_convert_fusion.n0.refs_0_.refs_5_), channel_id=1, source_target_pairs={{0,2},{2,4},{4,6},{6,0},{1,3},{3,5},{5,7},{7,1},{8,10},{10,12},{12... | collective-permute-start | bytes 1966088 | tf_op jit(solution)/shard_map/ppermute | solution.py:70
  135.1 19.6 %collective-permute-start.17 = (bf16[160,2048]{1,0:T(8,128)(2,1)S(1)}, bf16[160,2048]{1,0:T(8,128)(2,1)S(1)}, u32[]{:S(2)}, u32[]{:S(2)}) collective-permute-start(bf16[160,2048]{1,0:T(8,128)(2,1)S(1)} %multiply_convert_fusion.n0.refs_0_.refs_5_), channel_id=1, source_target_pairs={{0,6},{2,0},{4,2},{6,4},{1,7},{3,1},{5,3},{7,5},{8,14},{10,8},{12,... | collective-permute-start | bytes 1966088 | tf_op jit(solution)/shard_map/ppermute | solution.py:71
  154.7 14.6 %collective-permute-start.23 = (bf16[352,2048]{1,0:T(8,128)(2,1)S(1)}, bf16[352,2048]{1,0:T(8,128)(2,1)}, u32[]{:S(2)}, u32[]{:S(2)}) collective-permute-start(bf16[352,2048]{1,0:T(8,128)(2,1)S(1)} %collective-permute-done.22.w1), channel_id=1, source_target_pairs={{0,8},{8,0},{1,9},{9,1},{2,10},{10,2},{3,11},{11,3},{4,12},{12,4},... | collective-permute-start | bytes 4325384 | tf_op jit(solution)/shard_map/ppermute | solution.py:842
  158.4 10.2 %collective-permute-start.19 = (bf16[80,2048]{1,0:T(8,128)(2,1)S(1)}, bf16[80,2048]{1,0:T(8,128)(2,1)S(1)}, u32[]{:S(2)}, u32[]{:S(2)}) collective-permute-start(bf16[80,2048]{1,0:T(8,128)(2,1)S(1)} %slice.97), channel_id=1, source_target_pairs={{0,2},{2,4},{4,6},{6,0},{1,3},{3,5},{5,7},{7,1},{8,10},{10,12},{12... | collective-permute-start | bytes 983048 | tf_op jit(solution)/shard_map/ppermute | solution.py:74
  211.1 254.3 %all-gather.5.cloned.1.call-start = ((), (), s32[]{:S(2)}) async-start(), calls=%async_computation.3 | async-start | bytes 9191424 | tf_op jit(solution)/shard_map/all_gather | solution.py:879
  235.1 15.4 %collective-permute-start.27 = (bf16[160,2048]{1,0:T(8,128)(2,1)S(1)}, bf16[160,2048]{1,0:T(8,128)(2,1)S(1)}, u32[]{:S(2)}, u32[]{:S(2)}) collective-permute-start(bf16[160,2048]{1,0:T(8,128)(2,1)S(1)} %pad_maximum_fusion.4), channel_id=1, source_target_pairs={{0,6},{2,0},{4,2},{6,4},{1,7},{3,1},{5,3},{7,5},{8,14},{10,8},{12,... | collective-permute-start | bytes 1966088 | tf_op jit(solution)/shard_map/ppermute | solution.py:86
  239.6 15.8 %collective-permute-start.25 = (bf16[160,2048]{1,0:T(8,128)(2,1)S(1)}, bf16[160,2048]{1,0:T(8,128)(2,1)S(1)}, u32[]{:S(2)}, u32[]{:S(2)}) collective-permute-start(bf16[160,2048]{1,0:T(8,128)(2,1)S(1)} %pad_maximum_fusion.3), channel_id=1, source_target_pairs={{0,2},{2,4},{4,6},{6,0},{1,3},{3,5},{5,7},{7,1},{8,10},{10,12},{12... | collective-permute-start | bytes 1966088 | tf_op jit(solution)/shard_map/ppermute | solution.py:85
  258.4 13.5 %collective-permute-start.29 = (bf16[160,2048]{1,0:T(8,128)(2,1)S(1)}, bf16[160,2048]{1,0:T(8,128)(2,1)S(1)}, u32[]{:S(2)}, u32[]{:S(2)}) collective-permute-start(bf16[160,2048]{1,0:T(8,128)(2,1)S(1)} %get-tuple-element.169.b0.refs_10_), channel_id=1, source_target_pairs={{0,6},{2,0},{4,2},{6,4},{1,7},{3,1},{5,3},{7,5},{8,14},{10,8},{12,... | collective-permute-start | bytes 1966088 | tf_op jit(solution)/shard_map/ppermute | solution.py:71
  259.2 14.7 %collective-permute-start.28 = (bf16[160,2048]{1,0:T(8,128)(2,1)S(1)}, bf16[160,2048]{1,0:T(8,128)(2,1)S(1)}, u32[]{:S(2)}, u32[]{:S(2)}) collective-permute-start(bf16[160,2048]{1,0:T(8,128)(2,1)S(1)} %get-tuple-element.169.b0.refs_10_), channel_id=1, source_target_pairs={{0,2},{2,4},{4,6},{6,0},{1,3},{3,5},{5,7},{7,1},{8,10},{10,12},{12... | collective-permute-start | bytes 1966088 | tf_op jit(solution)/shard_map/ppermute | solution.py:70
  273.9 12.7 %collective-permute-start.30 = (bf16[80,2048]{1,0:T(8,128)(2,1)S(1)}, bf16[80,2048]{1,0:T(8,128)(2,1)S(1)}, u32[]{:S(2)}, u32[]{:S(2)}) collective-permute-start(bf16[80,2048]{1,0:T(8,128)(2,1)S(1)} %slice.99), channel_id=1, source_target_pairs={{0,2},{2,4},{4,6},{6,0},{1,3},{3,5},{5,7},{7,1},{8,10},{10,12},{12... | collective-permute-start | bytes 983048 | tf_op jit(solution)/shard_map/ppermute | solution.py:74
  274.8 12.6 %collective-permute-start.31 = (bf16[80,2048]{1,0:T(8,128)(2,1)S(1)}, bf16[80,2048]{1,0:T(8,128)(2,1)S(1)}, u32[]{:S(2)}, u32[]{:S(2)}) collective-permute-start(bf16[80,2048]{1,0:T(8,128)(2,1)S(1)} %slice.100), channel_id=1, source_target_pairs={{0,6},{2,0},{4,2},{6,4},{1,7},{3,1},{5,3},{7,5},{8,14},{10,8},{12,... | collective-permute-start | bytes 983048 | tf_op jit(solution)/shard_map/ppermute | solution.py:75
  288.1 25.9 %collective-permute-start.32 = (bf16[160,2048]{1,0:T(8,128)(2,1)}, bf16[160,2048]{1,0:T(8,128)(2,1)S(1)}, u32[]{:S(2)}, u32[]{:S(2)}) collective-permute-start(bf16[160,2048]{1,0:T(8,128)(2,1)} %get-tuple-element.128), channel_id=1, source_target_pairs={{0,2},{2,4},{4,6},{6,0},{1,3},{3,5},{5,7},{7,1},{8,10},{10,12},{12... | collective-permute-start | bytes 1966088 | tf_op jit(solution)/shard_map/ppermute | solution.py:857
  288.1 25.9 %collective-permute-start.33 = (bf16[160,2048]{1,0:T(8,128)(2,1)}, bf16[160,2048]{1,0:T(8,128)(2,1)S(1)}, u32[]{:S(2)}, u32[]{:S(2)}) collective-permute-start(bf16[160,2048]{1,0:T(8,128)(2,1)} %get-tuple-element.130), channel_id=1, source_target_pairs={{0,6},{2,0},{4,2},{6,4},{1,7},{3,1},{5,3},{7,5},{8,14},{10,8},{12,... | collective-permute-start | bytes 1966088 | tf_op jit(solution)/shard_map/ppermute | solution.py:857
  310.6 12.4 %collective-permute-start.34 = (bf16[640,128]{1,0:T(8,128)(2,1)}, bf16[640,128]{1,0:T(8,128)(2,1)S(1)}, u32[]{:S(2)}, u32[]{:S(2)}) collective-permute-start(bf16[640,128]{1,0:T(8,128)(2,1)} %get-tuple-element.135), channel_id=1, source_target_pairs={{0,1},{1,0},{2,3},{3,2},{4,5},{5,4},{6,7},{7,6},{8,9},{9,8},{10,11... | collective-permute-start | bytes 491528 | tf_op jit(solution)/shard_map/ppermute | solution.py:862
  323.0 22.7 %collective-permute-start.40 = (bf16[4,2,1024,128]{3,2,1,0:T(8,128)(2,1)}, bf16[4,2,1024,128]{3,2,1,0:T(8,128)(2,1)}, u32[]{:S(2)}, u32[]{:S(2)}) collective-permute-start(bf16[4,2,1024,128]{3,2,1,0:T(8,128)(2,1)} %get-tuple-element.146), channel_id=1, source_target_pairs={{0,8},{8,0},{1,9},{9,1},{2,10},{10,2},{3,11},{11,3},{4,12},{12,4},... | collective-permute-start | bytes 6291464 | tf_op jit(solution)/shard_map/ppermute | solution.py:747
  335.5 10.1 %collective-permute-start.35 = (bf16[80,2048]{1,0:T(8,128)(2,1)}, bf16[80,2048]{1,0:T(8,128)(2,1)S(1)}, u32[]{:S(2)}, u32[]{:S(2)}) collective-permute-start(bf16[80,2048]{1,0:T(8,128)(2,1)} %get-tuple-element.138), channel_id=1, source_target_pairs={{0,2},{2,4},{4,6},{6,0},{1,3},{3,5},{5,7},{7,1},{8,10},{10,12},{12... | collective-permute-start | bytes 983048 | tf_op jit(solution)/shard_map/ppermute | solution.py:81
  335.6 10.1 %collective-permute-start.37 = (bf16[80,2048]{1,0:T(8,128)(2,1)}, bf16[80,2048]{1,0:T(8,128)(2,1)S(1)}, u32[]{:S(2)}, u32[]{:S(2)}) collective-permute-start(bf16[80,2048]{1,0:T(8,128)(2,1)} %get-tuple-element.140), channel_id=1, source_target_pairs={{0,6},{2,0},{4,2},{6,4},{1,7},{3,1},{5,3},{7,5},{8,14},{10,8},{12,... | collective-permute-start | bytes 983048 | tf_op jit(solution)/shard_map/ppermute | solution.py:82
  352.0 14.9 %collective-permute-start.38 = (bf16[160,2048]{1,0:T(8,128)(2,1)S(1)}, bf16[160,2048]{1,0:T(8,128)(2,1)S(1)}, u32[]{:S(2)}, u32[]{:S(2)}) collective-permute-start(bf16[160,2048]{1,0:T(8,128)(2,1)S(1)} %pad_maximum_fusion.6), channel_id=1, source_target_pairs={{0,6},{2,0},{4,2},{6,4},{1,7},{3,1},{5,3},{7,5},{8,14},{10,8},{12,... | collective-permute-start | bytes 1966088 | tf_op jit(solution)/shard_map/ppermute | solution.py:86
  354.4 15.5 %collective-permute-start.36 = (bf16[160,2048]{1,0:T(8,128)(2,1)S(1)}, bf16[160,2048]{1,0:T(8,128)(2,1)S(1)}, u32[]{:S(2)}, u32[]{:S(2)}) collective-permute-start(bf16[160,2048]{1,0:T(8,128)(2,1)S(1)} %pad_maximum_fusion.5), channel_id=1, source_target_pairs={{0,2},{2,4},{4,6},{6,0},{1,3},{3,5},{5,7},{7,1},{8,10},{10,12},{12... | collective-permute-start | bytes 1966088 | tf_op jit(solution)/shard_map/ppermute | solution.py:85
  354.5 21.7 %collective-permute-start.42 = (bf16[2,1168,128]{2,1,0:T(8,128)(2,1)S(1)}, bf16[2,1168,128]{2,1,0:T(8,128)(2,1)}, u32[]{:S(2)}, u32[]{:S(2)}) collective-permute-start(bf16[2,1168,128]{2,1,0:T(8,128)(2,1)S(1)} %copy-done.51), channel_id=1, source_target_pairs={{0,64},{32,96},{64,0},{96,32},{1,65},{33,97},{65,1},{97,33},{2,66}... | collective-permute-start | bytes 1794056 | tf_op jit(solution)/shard_map/ppermute | solution.py:752
  357.1 44.7 %collective-permute-start.43 = (bf16[2,1168,128]{2,1,0:T(8,128)(2,1)S(1)}, bf16[2,1168,128]{2,1,0:T(8,128)(2,1)}, u32[]{:S(2)}, u32[]{:S(2)}) collective-permute-start(bf16[2,1168,128]{2,1,0:T(8,128)(2,1)S(1)} %copy-done.50), channel_id=1, source_target_pairs={{0,32},{32,64},{64,96},{96,0},{1,33},{33,65},{65,97},{97,1},{2,34}... | collective-permute-start | bytes 1794056 | tf_op jit(solution)/shard_map/ppermute | solution.py:752
  357.1 44.7 %collective-permute-start.44 = (bf16[2,1168,128]{2,1,0:T(8,128)(2,1)S(1)}, bf16[2,1168,128]{2,1,0:T(8,128)(2,1)}, u32[]{:S(2)}, u32[]{:S(2)}) collective-permute-start(bf16[2,1168,128]{2,1,0:T(8,128)(2,1)S(1)} %copy-done.49), channel_id=1, source_target_pairs={{0,96},{32,0},{64,32},{96,64},{1,97},{33,1},{65,33},{97,65},{2,98}... | collective-permute-start | bytes 1794056 | tf_op jit(solution)/shard_map/ppermute | solution.py:752
  404.5 11.3 %collective-permute-start.45 = (bf16[1168,128]{1,0:T(8,128)(2,1)}, bf16[1168,128]{1,0:T(8,128)(2,1)S(1)}, u32[]{:S(2)}, u32[]{:S(2)}) collective-permute-start(bf16[1168,128]{1,0:T(8,128)(2,1)} %get-tuple-element.156.a), channel_id=1, source_target_pairs={{0,16},{16,0},{1,17},{17,1},{2,18},{18,2},{3,19},{19,3},{4,20},{20... | collective-permute-start | bytes 897032 | tf_op jit(solution)/shard_map/ppermute | solution.py:761
  404.5 11.3 %collective-permute-start.47 = (bf16[1168,128]{1,0:T(8,128)(2,1)}, bf16[1168,128]{1,0:T(8,128)(2,1)}, u32[]{:S(2)}, u32[]{:S(2)}) collective-permute-start(bf16[1168,128]{1,0:T(8,128)(2,1)} %get-tuple-element.157), channel_id=1, source_target_pairs={{0,17},{1,16},{16,1},{17,0},{2,19},{3,18},{18,3},{19,2},{4,21},{5,... | collective-permute-start | bytes 897032 | tf_op jit(solution)/shard_map/ppermute | solution.py:763
  404.5 23.4 %collective-permute-start.46 = (bf16[1168,128]{1,0:T(8,128)(2,1)}, bf16[1168,128]{1,0:T(8,128)(2,1)}, u32[]{:S(2)}, u32[]{:S(2)}) collective-permute-start(bf16[1168,128]{1,0:T(8,128)(2,1)} %get-tuple-element.157), channel_id=1, source_target_pairs={{0,1},{1,0},{2,3},{3,2},{4,5},{5,4},{6,7},{7,6},{8,9},{9,8},{10,11... | collective-permute-start | bytes 897032 | tf_op jit(solution)/shard_map/ppermute | solution.py:762
  430.0 11.0 %collective-permute-start.50 = (bf16[1168,128]{1,0:T(8,128)(2,1)}, bf16[1168,128]{1,0:T(8,128)(2,1)S(1)}, u32[]{:S(2)}, u32[]{:S(2)}) collective-permute-start(bf16[1168,128]{1,0:T(8,128)(2,1)} %sum_z.1.refs_0_), channel_id=1, source_target_pairs={{0,96},{32,0},{64,32},{96,64},{1,97},{33,1},{65,33},{97,65},{2,98}... | collective-permute-start | bytes 897032 | tf_op jit(solution)/shard_map/ppermute | solution.py:766
  430.0 14.4 %collective-permute-start.49 = (bf16[1168,128]{1,0:T(8,128)(2,1)}, bf16[1168,128]{1,0:T(8,128)(2,1)S(1)}, u32[]{:S(2)}, u32[]{:S(2)}) collective-permute-start(bf16[1168,128]{1,0:T(8,128)(2,1)} %sum_z.1.refs_0_), channel_id=1, source_target_pairs={{0,64},{32,96},{64,0},{96,32},{1,65},{33,97},{65,1},{97,33},{2,66}... | collective-permute-start | bytes 897032 | tf_op jit(solution)/shard_map/ppermute | solution.py:766
  430.1 16.6 %collective-permute-start.48 = (bf16[1168,128]{1,0:T(8,128)(2,1)}, bf16[1168,128]{1,0:T(8,128)(2,1)S(1)}, u32[]{:S(2)}, u32[]{:S(2)}) collective-permute-start(bf16[1168,128]{1,0:T(8,128)(2,1)} %sum_z.1.refs_0_), channel_id=1, source_target_pairs={{0,32},{32,64},{64,96},{96,0},{1,33},{33,65},{65,97},{97,1},{2,34}... | collective-permute-start | bytes 897032 | tf_op jit(solution)/shard_map/ppermute | solution.py:766
  431.5 29.6 %collective-permute-start.39 = (bf16[160,2048]{1,0:T(8,128)(2,1)}, bf16[160,2048]{1,0:T(8,128)(2,1)}, u32[]{:S(2)}, u32[]{:S(2)}) collective-permute-start(bf16[160,2048]{1,0:T(8,128)(2,1)} %get-tuple-element.141), channel_id=1, source_target_pairs={{0,4},{2,6},{4,0},{6,2},{1,5},{3,7},{5,1},{7,3},{8,12},{10,14},{12... | collective-permute-start | bytes 1966088 | tf_op jit(solution)/shard_map/ppermute | solution.py:871
  431.5 20.8 %collective-permute-start.51 = (bf16[1168,128]{1,0:T(8,128)(2,1)}, bf16[1168,128]{1,0:T(8,128)(2,1)S(1)}, u32[]{:S(2)}, u32[]{:S(2)}) collective-permute-start(bf16[1168,128]{1,0:T(8,128)(2,1)} %sum_z.1.refs_0_), channel_id=1, source_target_pairs={{0,8},{8,0},{1,9},{9,1},{2,10},{10,2},{3,11},{11,3},{4,12},{12,4},... | collective-permute-start | bytes 897032 | tf_op jit(solution)/shard_map/ppermute | solution.py:767
  441.1 11.3 %collective-permute-start.54 = (bf16[1168,128]{1,0:T(8,128)(2,1)S(1)}, bf16[1168,128]{1,0:T(8,128)(2,1)S(1)}, u32[]{:S(2)}, u32[]{:S(2)}) collective-permute-start(bf16[1168,128]{1,0:T(8,128)(2,1)S(1)} %collective-permute-done.50.refs_3_), channel_id=1, source_target_pairs={{0,8},{8,0},{1,9},{9,1},{2,10},{10,2},{3,11},{11,3},{4,12},{12,4},... | collective-permute-start | bytes 897032 | tf_op jit(solution)/shard_map/ppermute | solution.py:767
  (77 other events, 583.9 us)
Sparse Core Ops, SparseCore 0:
  93.7 38.9 all-gather.2
  211.2 118.7 reduce-scatter.1
  350.7 84.6 all-gather.4

commit v6 on v5

--- a/solution.py
+++ b/solution.py
@@ -76,10 +76,10 @@
     return v, from_next, opp_a, opp_b, from_prev
 
 
-def scatter_x(parts):
+def scatter_x(parts, *deps):
     p0, p1, p2a, p2b, p3 = parts
     got_a = lax.ppermute(p2a, "x", shift(4, 1))
-    got_b = lax.ppermute(p2b, "x", shift(4, -1))
+    got_b = tie(lax.ppermute(p2b, "x", shift(4, -1)), *deps)
     q1 = jnp.concatenate([(p1[:HALF].astype(F32) + got_a.astype(F32)).astype(BF16), p1[HALF:]], 0)
     q3 = jnp.concatenate([p3[:HALF], (p3[HALF:].astype(F32) + got_b.astype(F32)).astype(BF16)], 0)
     from_prev = lax.ppermute(q1, "x", shift(4, 1))
@@ -748,7 +748,6 @@
     got_b = lax.ppermute(second[1], "core", shift(2, 1))
     part = sds((2, TAIL, 128))
     g = small_call(sum_core_body, (part,) * 4, idx, first[0], got_a, second[0], got_b, name="sum_core")
-    summed = g[0]
     got = [tie(lax.ppermute(g[s], "y", shift(4, s)), before) for s in (2, 1, 3)]
     part = sds((TAIL, 128))
     own, other = small_call(sum_y_body, (part,) * 2, idx, g[0], *got, name="sum_y")
@@ -766,7 +765,7 @@
     mine = [g] + [lax.ppermute(g, "y", shift(4, s)) for s in (1, 2, 3)]
     theirs = [lax.ppermute(v, "core", shift(2, 1)) for v in mine]
     shapes = (sds((DH, QW), F32), sds((AW // 2, D), F32), sds((2, D), F32))
-    return summed, small_call(unpack_tail_body, shapes, idx, *mine, *theirs, name="unpack_tail")
+    return own, small_call(unpack_tail_body, shapes, idx, *mine, *theirs, name="unpack_tail")
 
 
 def inverse_rms(v):
@@ -801,7 +800,22 @@
     s_one = inverse_rms(tok)
     qkv_all = fetch_partner(qkv_weight, core)
     normed_one = gather_x((tok * s_one * gain_one).astype(BF16))
-    out_all = fetch_partner(out_weight, core, normed_one[2])
+    out_all = fetch_partner(out_weight, core, qkv_all[1], normed_one[1], normed_one[4])
+    rows = DH // 8
+    mine = lambda w: lax.dynamic_slice_in_dim(w, (y * 2 + core) * rows, rows, 0)
+    cross = [(2 * a + b, 2 * (1 - a) + (1 - b)) for a in range(2) for b in range(2)]
+    gate_up = lax.ppermute(
+        jnp.concatenate(
+            [
+                tie(mine(gate_weight), out_all[1], normed_one[2], normed_one[3]),
+                jnp.zeros((rows, GAP - FF4), BF16),
+                mine(up_weight),
+            ],
+            1,
+        ),
+        ("zl", "zh"),
+        cross,
+    )
     cots = gather_x(tie(cotangent, normed_one[2]))
 
     begin, position = replica_layout(seq_lengths, seq_replica, (y * 2 + zl) * 2 + core)
@@ -813,29 +827,14 @@
     cosine = jnp.cos(angles)
     sine = jnp.where((lane % HD) < HD // 2, -1.0, 1.0)[None, :] * jnp.sin(angles)
 
-    q, kv_own = qkv_forward(idx, normed_one, qkv_all, cosine, sine)
-    kv_par = lax.ppermute(kv_own, "zh", shift(2, 1))
-    rows = DH // 8
-    mine = lambda w: lax.dynamic_slice_in_dim(w, (y * 2 + core) * rows, rows, 0)
-    cross = [(2 * a + b, 2 * (1 - a) + (1 - b)) for a in range(2) for b in range(2)]
-    gate_up = lax.ppermute(
-        jnp.concatenate(
-            [
-                tie(mine(gate_weight), kv_par),
-                jnp.zeros((rows, GAP - FF4), BF16),
-                mine(up_weight),
-            ],
-            1,
-        ),
-        ("zl", "zh"),
-        cross,
-    )
-    down_got = fetch_half(tie(down_weight, kv_par), core)
-    q = tie(q, cots[1], cots[4], out_all[1])
+    q, kv_own = qkv_forward(idx, normed_one, qkv_all, tie(cosine, out_all[1]), sine)
+    kv_par = lax.ppermute(tie(kv_own, cots[1], cots[4]), "zh", shift(2, 1))
+    down_got = fetch_half(tie(down_weight, gate_up), core)
+    q = tie(q, cots[1], cots[4], gate_up)
     att, qx = attend(idx, q, kv_own, kv_par, first)
-    gate_up = lax.all_gather(tie(gate_up, qx), ("y", "core"), axis=0, tiled=True)
-    parts = [tie(p, cots[2], cots[3]) for p in out_project(idx, att, out_all)]
-    after_attn = tok + scatter_x(parts)[0]
+    gate_up = lax.all_gather(tie(gate_up, kv_par), ("y", "core"), axis=0, tiled=True)
+    parts = out_project(idx, tie(att, cots[2], cots[3]), out_all)
+    after_attn = tok + scatter_x(parts, down_got)[0]
 
     r_two = inverse_rms(after_attn)
     normed_two = gather_x((after_attn * r_two * gain_two).astype(BF16))
@@ -863,6 +862,7 @@
     tail = attn_grads(
         idx, normed_one, branch, dqm.reshape(ROWS, AW), tie(att, *layer).reshape(ROWS, AW)
     )
+    dkv_got = tie(dkv_got, tail[0])
     *tail_kv, parts = qkv_back(
         idx, dqm.reshape(ROWS, AW), dkv_own, dkv_got, cosine, sine, qkv_all, normed_one, gain_one,
         gain_grad_two,

time: 490 us -> 483 us (0.986)
  waiting for transfers between devices: 182 us -> 160 us
  starting transfers between devices: 96.7 us -> 105 us
    ppermute x3, waiting for transfers between devices: 34.1 us -> 12.1 us  [fetch_half(): lax.ppermute(lax.dynamic_slice_in_dim(w, core * half, half, 0), 'zh', shi...]
    ppermute x4, waiting for transfers between devices: 2.03 us -> 22.5 us  [gather_x(): from_prev = lax.ppermute(v, 'x', shift(4, 1))]
    ppermute x1, waiting for transfers between devices: 12.2 us -> 0.01 us  [sum_tail(): lax.ppermute(other, 'zh', shift(2, 1))]
    ppermute x1, waiting for transfers between devices: 0.01 us -> 12.1 us  [sum_tail(): lax.ppermute(other, ('zl', 'zh'), cross)]
    ppermute x3, waiting for transfers between devices: 31.3 us -> 19.9 us  [sum_tail(): got = [tie(lax.ppermute(g[s], 'y', shift(4, s)), before) for s in (2, 1, 3)]]
    ppermute x5, starting transfers between devices: 12.7 us -> 4.82 us  [the longest x3 3.63 us: scatter_x(): got_b = tie(lax.ppermute(p2b, 'x', shift(4, -1)), *deps)]
    ppermute x2, starting transfers between devices: 2.44 us -> 9.7 us  [fetch_partner(): return (w, got, lax.ppermute(got, 'core', shift(2, 1)))]
    ppermute x3, waiting for transfers between devices: 0.01 us -> 5.61 us  [sum_tail(): mine = [g] + [lax.ppermute(g, 'y', shift(4, s)) for s in (1, 2, 3)]]
  transfers between devices with their start and end apart: 61 -> 61, of which waited for: 28 -> 29; matrix products, arithmetic and copies ran while one was open for 6% -> 7% of each run, Pallas kernels for 20% -> 20%
where the time goes in v6:
time: 483 us; the launch traced here: 473 us
  waiting for transfers between devices  160 us (33%)
  Pallas kernels  147 us (30%)
  starting transfers between devices  105 us (22%)
  local copies, waits for them, and re-layouts  25.3 us (5%)
  other arithmetic  21.4 us (4%)
  between operations  14.9 us (3%)
    ppermute x4, starting transfers between devices, sum_tail(): theirs = [lax.ppermute(v, 'core', shift(2, 1)) for v in mine]  23.6 us
    ppermute x4, waiting for transfers between devices, gather_x(): from_prev = lax.ppermute(v, 'x', shift(4, 1))  22.5 us
    pallas_call x1, Pallas kernels, ffn(): pl.pallas_call(ffn_body, grid=(TILES,), out_shape=(sds((ROWS, FF4)),) * 3...  20.9 us
    pallas_call x1, Pallas kernels, ffn_grads(): pl.pallas_call(ffn_grads_body, grid=(16 // QS,), out_shape=sds((2, 16, PI...  20.8 us
    ppermute x3, waiting for transfers between devices, sum_tail(): got = [tie(lax.ppermute(g[s], 'y', shift(4, s)), before) for s in (2, 1, 3)]  19.9 us
    pallas_call x1, Pallas kernels, attend_back(): pl.pallas_call(attend_back_body, out_shape=(sds((4, BLK, AW)), sds((ROWS,...  19.8 us
    ppermute x3, waiting for transfers between devices, scatter_x(): from_next = lax.ppermute(q3, 'x', shift(4, -1))  18 us
    pallas_call x1, Pallas kernels, ffn_back(): pl.pallas_call(ffn_back_body, grid_spec=pltpu.PrefetchScalarGridSpec(num_...  16 us
  transfers between devices with their start and end apart: 61, of which 29 were waited for; matrix products, arithmetic and copies ran while one was open for 7% of the time, Pallas kernels for 20%

profile of v6, /device:TPU:1, one launch (start us, length us, event | category | flops | bytes accessed | tf_op | source)
XLA Modules:
  0.0 473.2 jit_solution(5803515855766433681)
XLA Ops:
  14.4 3.7 collective-permute-start.4
  20.1 7.4 %collective-permute-done.1.n3.refs_4_.refs_9_ = bf16[160,2048]{1,0:T(8,128)(2,1)S(1)} collective-permute-done((bf16[160,2048]{1,0:T(8,128)(2,1)S(1)}, bf16[160,2048]{1,0:T(8,128)(2,1)S(1)}, u32[]{:S(2)}, u32[]{:S(2)}) %collective-permute-start.1) | collective-permute-done | bytes 655392 | tf_op jit(solution)/shard_map/ppermute | solution.py:70
  27.5 4.7 collective-permute-done.4.w1
  41.0 3.1 collective-permute-start.5
  44.1 2.8 collective-permute-done.2.n2a.refs_2_.refs_7_
  53.0 6.8 %qkv_forward.1 = (bf16[4,1280,128]{2,1,0:T(8,128)(2,1)}, bf16[640,128]{1,0:T(8,128)(2,1)}) custom-call(s32[4]{0:T(128)} %pad_add_fusion.idx, bf16[160,2048]{1,0:T(8,128)(2,1)} %copy-done.2, bf16[160,2048]{1,0:T(8,128)(2,1)} %copy-done.6, bf16[80,2048]{1,0:T(8,128)(2,1)} %copy-done.23, bf16[80,2048]{1,0:T(8,128)(2,1)} %copy-done.22, ...), custom_call_target="tpu_custom_call" | custom-call | flops 1677721600 | bytes 7000000 | tf_op jit(solution)/shard_map/qkv_forward/pallas_call | solution.py:154
  61.8 5.3 %collective-permute-done.10.kv_par = bf16[640,128]{1,0:T(8,128)(2,1)S(1)} collective-permute-done((bf16[640,128]{1,0:T(8,128)(2,1)}, bf16[640,128]{1,0:T(8,128)(2,1)S(1)}, u32[]{:S(2)}, u32[]{:S(2)}) %collective-permute-start.10) | collective-permute-done | bytes 163872 | tf_op jit(solution)/shard_map/ppermute | solution.py:831
  68.8 6.6 %collective-permute-start.13 = (bf16[128,2048]{1,0:T(8,128)(2,1)}, bf16[128,2048]{1,0:T(8,128)(2,1)S(1)}, u32[]{:S(2)}, u32[]{:S(2)}) collective-permute-start(bf16[128,2048]{1,0:T(8,128)(2,1)} %collective-permute-done.6.w1), channel_id=1, source_target_pairs={{0,8},{8,0},{1,9},{9,1},{2,10},{10,2},{3,11},{11,3},{4,12},{12,4},... | collective-permute-start | bytes 1572872 | tf_op jit(solution)/shard_map/ppermute | solution.py:118
  81.4 8.8 %attend.1 = (bf16[4,160,512]{2,1,0:T(8,128)(2,1)}, bf16[4,1280,128]{2,1,0:T(8,128)(2,1)}) custom-call(s32[4]{0:T(128)} %pad_add_fusion.idx, bf16[4,1280,128]{2,1,0:T(8,128)(2,1)} %get-tuple-element.94.q, bf16[640,128]{1,0:T(8,128)(2,1)} %get-tuple-element.96.kv_own, bf16[640,128]{1,0:T(8,128)(2,1)} %copy-done.51, s32[1,1280]{1,0:T(1,128)} %reshape_tile.3.first), custom_call_target="tpu_custom_call" | custom-call | flops 12000000000 | bytes 3000000 | tf_op jit(solution)/shard_map/attend/pallas_call | solution.py:247
  91.8 4.8 %out_project.1 = (bf16[160,2048]{1,0:T(8,128)(2,1)}, bf16[160,2048]{1,0:T(8,128)(2,1)}, bf16[80,2048]{1,0:T(8,128)(2,1)}, bf16[80,2048]{1,0:T(8,128)(2,1)}, bf16[160,2048]{1,0:T(8,128)(2,1)}) custom-call(s32[4]{0:T(128)} %pad_add_fusion.idx, bf16[4,160,512]{2,1,0:T(8,128)(2,1)} %get-tuple-element.135.att, bf16[256,2048]{1,0:T(8,128)(2,1)} %w0.10, ...), custom_call_target="tpu_custom_call" | custom-call | flops 1342177280 | bytes 5500000 | tf_op jit(solution)/shard_map/out_project/pallas_call | solution.py:284
  101.5 5.4 %collective-permute-done.14 = bf16[80,2048]{1,0:T(8,128)(2,1)S(1)} collective-permute-done((bf16[80,2048]{1,0:T(8,128)(2,1)}, bf16[80,2048]{1,0:T(8,128)(2,1)S(1)}, u32[]{:S(2)}, u32[]{:S(2)}) %collective-permute-start.14) | collective-permute-done | bytes 327712 | tf_op jit(solution)/shard_map/ppermute | solution.py:81
  107.8 7.4 %collective-permute-done.17.w1 = bf16[352,2048]{1,0:T(8,128)(2,1)} collective-permute-done((bf16[352,2048]{1,0:T(8,128)(2,1)S(1)}, bf16[352,2048]{1,0:T(8,128)(2,1)}, u32[]{:S(2)}, u32[]{:S(2)}) %collective-permute-start.17) | collective-permute-done | bytes 1441824 | tf_op jit(solution)/shard_map/ppermute | solution.py:113
  118.0 5.4 %collective-permute-done.15 = bf16[160,2048]{1,0:T(8,128)(2,1)S(1)} collective-permute-done((bf16[160,2048]{1,0:T(8,128)(2,1)S(1)}, bf16[160,2048]{1,0:T(8,128)(2,1)S(1)}, u32[]{:S(2)}, u32[]{:S(2)}) %collective-permute-start.15) | collective-permute-done | bytes 655392 | tf_op jit(solution)/shard_map/ppermute | solution.py:85
  123.4 7.2 %collective-permute-done.18 = bf16[160,2048]{1,0:T(8,128)(2,1)S(1)} collective-permute-done((bf16[160,2048]{1,0:T(8,128)(2,1)S(1)}, bf16[160,2048]{1,0:T(8,128)(2,1)S(1)}, u32[]{:S(2)}, u32[]{:S(2)}) %collective-permute-start.18) | collective-permute-done | bytes 655392 | tf_op jit(solution)/shard_map/ppermute | solution.py:86
  131.6 3.4 collective-permute-start.19
  135.1 12.6 %collective-permute-done.20.n3.refs_4_.refs_9_ = bf16[160,2048]{1,0:T(8,128)(2,1)S(1)} collective-permute-done((bf16[160,2048]{1,0:T(8,128)(2,1)S(1)}, bf16[160,2048]{1,0:T(8,128)(2,1)S(1)}, u32[]{:S(2)}, u32[]{:S(2)}) %collective-permute-start.20) | collective-permute-done | bytes 655392 | tf_op jit(solution)/shard_map/ppermute | solution.py:70
  147.7 3.1 collective-permute-start.23
  154.0 6.7 %collective-permute-done.22.n2b.refs_3_.refs_8_ = bf16[80,2048]{1,0:T(8,128)(2,1)S(1)} collective-permute-done((bf16[80,2048]{1,0:T(8,128)(2,1)S(1)}, bf16[80,2048]{1,0:T(8,128)(2,1)S(1)}, u32[]{:S(2)}, u32[]{:S(2)}) %collective-permute-start.22) | collective-permute-done | bytes 327712 | tf_op jit(solution)/shard_map/ppermute | solution.py:75
  160.7 3.5 collective-permute-done.21.n2a.refs_2_.refs_7_
  165.0 20.9 %ffn.1 = (bf16[640,1408]{1,0:T(8,128)(2,1)}, bf16[640,1408]{1,0:T(8,128)(2,1)}, bf16[640,1408]{1,0:T(8,128)(2,1)}) custom-call(s32[4]{0:T(128)} %pad_add_fusion.idx, bf16[160,2048]{1,0:T(8,128)(2,1)} %copy-done.14, bf16[160,2048]{1,0:T(8,128)(2,1)} %copy-done.36, bf16[80,2048]{1,0:T(8,128)(2,1)} %copy-done.48, bf16[80,2048]{1,0:T(8,128)(2,1)} %copy-done.46, ...), custom_call_target="tpu_custom_call" | custom-call | flops 11072962560 | bytes 34000000 | tf_op jit(solution)/shard_map/ffn/pallas_call | solution.py:482
  185.8 20.8 %ffn_grads.1 = bf16[2,16,2112,128]{3,2,1,0:T(8,128)(2,1)} custom-call(bf16[160,2048]{1,0:T(8,128)(2,1)} %copy-done.14, bf16[160,2048]{1,0:T(8,128)(2,1)} %copy-done.36, bf16[80,2048]{1,0:T(8,128)(2,1)} %copy-done.48, bf16[80,2048]{1,0:T(8,128)(2,1)} %copy-done.46, bf16[160,2048]{1,0:T(8,128)(2,1)} %copy-done.35, bf16[160,2048]{1,0:T(8,128)(2,1)} %copy-done.14, ...), custom_call_target="tpu_custom_call" | custom-call | flops 11072962560 | bytes 30000000 | tf_op jit(solution)/shard_map/ffn_grads/pallas_call | solution.py:594
  206.7 16.0 %ffn_back.1 = (bf16[160,2048]{1,0:T(8,128)(2,1)}, bf16[160,2048]{1,0:T(8,128)(2,1)}, bf16[80,2048]{1,0:T(8,128)(2,1)}, bf16[80,2048]{1,0:T(8,128)(2,1)}, bf16[160,2048]{1,0:T(8,128)(2,1)}) custom-call(s32[4]{0:T(128)} %pad_add_fusion.idx, bf16[640,1408]{1,0:T(8,128)(2,1)} %get-tuple-element.115.refs_16_.dgate, ...), custom_call_target="tpu_custom_call" | custom-call | flops 7381975040 | bytes 18000000 | tf_op jit(solution)/shard_map/ffn_back/pallas_call | solution.py:547
  226.5 4.6 collective-permute-done.26
  235.5 10.8 %collective-permute-done.27 = bf16[160,2048]{1,0:T(8,128)(2,1)S(1)} collective-permute-done((bf16[160,2048]{1,0:T(8,128)(2,1)S(1)}, bf16[160,2048]{1,0:T(8,128)(2,1)S(1)}, u32[]{:S(2)}, u32[]{:S(2)}) %collective-permute-start.27) | collective-permute-done | bytes 655392 | tf_op jit(solution)/shard_map/ppermute | solution.py:86
  246.3 4.9 %collective-permute-done.25 = bf16[160,2048]{1,0:T(8,128)(2,1)S(1)} collective-permute-done((bf16[160,2048]{1,0:T(8,128)(2,1)S(1)}, bf16[160,2048]{1,0:T(8,128)(2,1)S(1)}, u32[]{:S(2)}, u32[]{:S(2)}) %collective-permute-start.25) | collective-permute-done | bytes 655392 | tf_op jit(solution)/shard_map/ppermute | solution.py:85
  252.5 2.8 fusion.18
  256.7 12.2 %collective-permute-done.29.b1.refs_11_ = bf16[160,2048]{1,0:T(8,128)(2,1)S(1)} collective-permute-done((bf16[160,2048]{1,0:T(8,128)(2,1)S(1)}, bf16[160,2048]{1,0:T(8,128)(2,1)S(1)}, u32[]{:S(2)}, u32[]{:S(2)}) %collective-permute-start.29) | collective-permute-done | bytes 655392 | tf_op jit(solution)/shard_map/ppermute | solution.py:71
  273.0 10.1 %down_project.1 = (bf16[160,2048]{1,0:T(8,128)(2,1)}, bf16[160,2048]{1,0:T(8,128)(2,1)}, bf16[160,2048]{1,0:T(8,128)(2,1)}, bf16[160,2048]{1,0:T(8,128)(2,1)}) custom-call(s32[4]{0:T(128)} %pad_add_fusion.idx, bf16[640,1408]{1,0:T(8,128)(2,1)} %get-tuple-element.121.refs_15_.hid, bf16[704,2048]{1,0:T(8,128)(2,1)} %w0.9, ...), custom_call_target="tpu_custom_call" | custom-call | flops 3690987520 | bytes 11000000 | tf_op jit(solution)/shard_map/down_project/pallas_call | solution.py:517
  285.9 19.8 %attend_back.1 = (bf16[4,160,512]{2,1,0:T(8,128)(2,1)}, f32[640,128]{1,0:T(8,128)}, bf16[640,128]{1,0:T(8,128)(2,1)}) custom-call(s32[4]{0:T(128)} %pad_add_fusion.idx, bf16[4,1280,128]{2,1,0:T(8,128)(2,1)} %get-tuple-element.130.qx, bf16[640,128]{1,0:T(8,128)(2,1)} %get-tuple-element.96.kv_own, bf16[640,128]{1,0:T(8,128)(2,1)} %copy-done.51, ...), custom_call_target="tpu_custom_call" | custom-call | flops 30000001024 | bytes 8000000 | tf_op jit(solution)/shard_map/attend_back/pallas_call | solution.py:356
  305.7 8.9 %attn_grads.1 = (bf16[4,2,1024,128]{3,2,1,0:T(8,128)(2,1)}, bf16[4,2,1024,128]{3,2,1,0:T(8,128)(2,1)}) custom-call(s32[4]{0:T(128)} %pad_add_fusion.idx, bf16[160,2048]{1,0:T(8,128)(2,1)} %copy-done.2, bf16[160,2048]{1,0:T(8,128)(2,1)} %copy-done.6, bf16[80,2048]{1,0:T(8,128)(2,1)} %copy-done.23, bf16[80,2048]{1,0:T(8,128)(2,1)} %copy-done.22, ...), custom_call_target="tpu_custom_call" | custom-call | flops 2684354560 | bytes 10000000 | tf_op jit(solution)/shard_map/attn_grads/pallas_call | solution.py:676
  315.4 7.3 %qkv_back.1 = (bf16[4,2,144,128]{3,2,1,0:T(8,128)(2,1)}, bf16[4,2,144,128]{3,2,1,0:T(8,128)(2,1)}, bf16[160,2048]{1,0:T(8,128)(2,1)}, bf16[160,2048]{1,0:T(8,128...) custom-call(s32[4]{0:T(128)} %pad_add_fusion.idx, ...), custom_call_target="tpu_custom_call" | custom-call | flops 1677721600 | bytes 13000000 | tf_op jit(solution)/shard_map/qkv_back/pallas_call | solution.py:413
  322.8 6.4 %collective-permute-start.40 = (bf16[4,2,1024,128]{3,2,1,0:T(8,128)(2,1)}, bf16[4,2,1024,128]{3,2,1,0:T(8,128)(2,1)S(1)}, u32[]{:S(2)}, u32[]{:S(2)}) collective-permute-start(bf16[4,2,1024,128]{3,2,1,0:T(8,128)(2,1)} %get-tuple-element.146), channel_id=1, source_target_pairs={{0,8},{8,0},{1,9},{9,1},{2,10},{10,2},{3,11},{11,3},{4,12},{12,4},... | collective-permute-start | bytes 6291464 | tf_op jit(solution)/shard_map/ppermute | solution.py:747
  334.9 6.8 %collective-permute-done.35 = bf16[80,2048]{1,0:T(8,128)(2,1)S(1)} collective-permute-done((bf16[80,2048]{1,0:T(8,128)(2,1)S(1)}, bf16[80,2048]{1,0:T(8,128)(2,1)S(1)}, u32[]{:S(2)}, u32[]{:S(2)}) %collective-permute-start.35) | collective-permute-done | bytes 327712 | tf_op jit(solution)/shard_map/ppermute | solution.py:81
  347.5 3.9 sum_core.1
  351.4 2.9 collective-permute-start.42
  361.6 6.4 %collective-permute-done.42.b = bf16[2,1168,128]{2,1,0:T(8,128)(2,1)} collective-permute-done((bf16[2,1168,128]{2,1,0:T(8,128)(2,1)}, bf16[2,1168,128]{2,1,0:T(8,128)(2,1)}, u32[]{:S(2)}, u32[]{:S(2)}) %collective-permute-start.42) | collective-permute-done | bytes 598048 | tf_op jit(solution)/shard_map/ppermute | solution.py:751
  368.0 13.5 %collective-permute-done.43.c = bf16[2,1168,128]{2,1,0:T(8,128)(2,1)} collective-permute-done((bf16[2,1168,128]{2,1,0:T(8,128)(2,1)}, bf16[2,1168,128]{2,1,0:T(8,128)(2,1)}, u32[]{:S(2)}, u32[]{:S(2)}) %collective-permute-start.43) | collective-permute-done | bytes 598048 | tf_op jit(solution)/shard_map/ppermute | solution.py:751
  387.8 12.1 %collective-permute-done.47.d = bf16[1168,128]{1,0:T(8,128)(2,1)S(1)} collective-permute-done((bf16[1168,128]{1,0:T(8,128)(2,1)}, bf16[1168,128]{1,0:T(8,128)(2,1)S(1)}, u32[]{:S(2)}, u32[]{:S(2)}) %collective-permute-start.47) | collective-permute-done | bytes 299040 | tf_op jit(solution)/shard_map/ppermute | solution.py:762
  399.9 4.8 %collective-permute-done.45.b = bf16[1168,128]{1,0:T(8,128)(2,1)} collective-permute-done((bf16[1168,128]{1,0:T(8,128)(2,1)}, bf16[1168,128]{1,0:T(8,128)(2,1)}, u32[]{:S(2)}, u32[]{:S(2)}) %collective-permute-start.45) | collective-permute-done | bytes 299040 | tf_op jit(solution)/shard_map/ppermute | solution.py:760
  406.9 4.3 collective-permute-start.50
  411.8 4.6 collective-permute-start.51
  416.4 2.8 collective-permute-done.50.refs_3_
  419.2 9.3 %collective-permute-start.54 = (bf16[1168,128]{1,0:T(8,128)(2,1)S(1)}, bf16[1168,128]{1,0:T(8,128)(2,1)S(1)}, u32[]{:S(2)}, u32[]{:S(2)}) collective-permute-start(bf16[1168,128]{1,0:T(8,128)(2,1)S(1)} %collective-permute-done.50.refs_3_), channel_id=1, source_target_pairs={{0,8},{8,0},{1,9},{9,1},{2,10},{10,2},{3,11},{11,3},{4,12},{12,4},... | collective-permute-start | bytes 897032 | tf_op jit(solution)/shard_map/ppermute | solution.py:766
  428.5 4.8 %collective-permute-start.53 = (bf16[1168,128]{1,0:T(8,128)(2,1)S(1)}, bf16[1168,128]{1,0:T(8,128)(2,1)S(1)}, u32[]{:S(2)}, u32[]{:S(2)}) collective-permute-start(bf16[1168,128]{1,0:T(8,128)(2,1)S(1)} %collective-permute-done.49.refs_2_), channel_id=1, source_target_pairs={{0,8},{8,0},{1,9},{9,1},{2,10},{10,2},{3,11},{11,3},{4,12},{12,4},... | collective-permute-start | bytes 897032 | tf_op jit(solution)/shard_map/ppermute | solution.py:766
  433.3 2.8 collective-permute-done.48.refs_1_
  436.1 4.9 %collective-permute-start.52 = (bf16[1168,128]{1,0:T(8,128)(2,1)S(1)}, bf16[1168,128]{1,0:T(8,128)(2,1)}, u32[]{:S(2)}, u32[]{:S(2)}) collective-permute-start(bf16[1168,128]{1,0:T(8,128)(2,1)S(1)} %collective-permute-done.48.refs_1_), channel_id=1, source_target_pairs={{0,8},{8,0},{1,9},{9,1},{2,10},{10,2},{3,11},{11,3},{4,12},{12,4},... | collective-permute-start | bytes 897032 | tf_op jit(solution)/shard_map/ppermute | solution.py:766
  445.2 4.2 unpack_tail.1
  456.5 9.8 %unpack.1 = (f32[1024,1408]{1,0:T(8,128)}, f32[1024,1408]{1,0:T(8,128)}, f32[704,2048]{1,0:T(8,128)}) custom-call(bf16[16,2112,128]{2,1,0:T(8,128)(2,1)} %all-gather.5.cloned.1.call-done.piece), custom_call_target="tpu_custom_call" | custom-call | flops 1000000 | bytes 26000000 | tf_op jit(solution)/shard_map/unpack/pallas_call | solution.py:621
  (262 shorter events, 106.2 us)
Async XLA Ops:
  7.2 157.8 %all-gather.3.cloned.1.call-start = ((), (), s32[]{:S(2)}) async-start(), calls=%async_computation.1 | async-start | bytes 6782976 | tf_op jit(solution)/shard_map/all_gather | solution.py:835
  10.0 17.5 %collective-permute-start.1 = (bf16[160,2048]{1,0:T(8,128)(2,1)S(1)}, bf16[160,2048]{1,0:T(8,128)(2,1)S(1)}, u32[]{:S(2)}, u32[]{:S(2)}) collective-permute-start(bf16[160,2048]{1,0:T(8,128)(2,1)S(1)} %fusion.2.n0.refs_0_.refs_5_), channel_id=1, source_target_pairs={{0,2},{2,4},{4,6},{6,0},{1,3},{3,5},{5,7},{7,1},{8,10},{10,12},{12... | collective-permute-start | bytes 1966088 | tf_op jit(solution)/shard_map/ppermute | solution.py:70
  12.1 15.4 %collective-permute-start = (bf16[160,2048]{1,0:T(8,128)(2,1)S(1)}, bf16[160,2048]{1,0:T(8,128)(2,1)S(1)}, u32[]{:S(2)}, u32[]{:S(2)}) collective-permute-start(bf16[160,2048]{1,0:T(8,128)(2,1)S(1)} %fusion.2.n0.refs_0_.refs_5_), channel_id=1, source_target_pairs={{0,6},{2,0},{4,2},{6,4},{1,7},{3,1},{5,3},{7,5},{8,14},{10,8},{12,... | collective-permute-start | bytes 1966088 | tf_op jit(solution)/shard_map/ppermute | solution.py:71
  14.4 17.8 %collective-permute-start.4 = (bf16[512,640]{1,0:T(8,128)(2,1)}, bf16[512,640]{1,0:T(8,128)(2,1)}, u32[]{:S(2)}, u32[]{:S(2)}) collective-permute-start(bf16[512,640]{1,0:T(8,128)(2,1)} %constant_dynamic-slice_fusion.5), channel_id=1, source_target_pairs={{0,1},{1,0},{2,3},{3,2},{4,5},{5,4},{6,7},{7,6},{8,9},{9,8},{10,11... | collective-permute-start | bytes 1966088 | tf_op jit(solution)/shard_map/ppermute | solution.py:113
  33.3 16.3 %collective-permute-start.6 = (bf16[128,2048]{1,0:T(8,128)(2,1)S(1)}, bf16[128,2048]{1,0:T(8,128)(2,1)}, u32[]{:S(2)}, u32[]{:S(2)}) collective-permute-start(bf16[128,2048]{1,0:T(8,128)(2,1)S(1)} %constant_dynamic-slice_fusion.4), channel_id=1, source_target_pairs={{0,1},{1,0},{2,3},{3,2},{4,5},{5,4},{6,7},{7,6},{8,9},{9,8},{10,11... | collective-permute-start | bytes 1572872 | tf_op jit(solution)/shard_map/ppermute | solution.py:113
  37.7 12.0 %collective-permute-start.3 = (bf16[80,2048]{1,0:T(8,128)(2,1)}, bf16[80,2048]{1,0:T(8,128)(2,1)S(1)}, u32[]{:S(2)}, u32[]{:S(2)}) collective-permute-start(bf16[80,2048]{1,0:T(8,128)(2,1)} %slice.94), channel_id=1, source_target_pairs={{0,6},{2,0},{4,2},{6,4},{1,7},{3,1},{5,3},{7,5},{8,14},{10,8},{12,... | collective-permute-start | bytes 983048 | tf_op jit(solution)/shard_map/ppermute | solution.py:75
  41.0 11.9 %collective-permute-start.5 = (bf16[512,640]{1,0:T(8,128)(2,1)}, bf16[512,640]{1,0:T(8,128)(2,1)}, u32[]{:S(2)}, u32[]{:S(2)}) collective-permute-start(bf16[512,640]{1,0:T(8,128)(2,1)} %collective-permute-done.4.w1), channel_id=1, source_target_pairs={{0,8},{8,0},{1,9},{9,1},{2,10},{10,2},{3,11},{11,3},{4,12},{12,4},... | collective-permute-start | bytes 1966088 | tf_op jit(solution)/shard_map/ppermute | solution.py:118
  46.9 14.2 %collective-permute-start.8 = (bf16[160,2048]{1,0:T(8,128)(2,1)}, bf16[160,2048]{1,0:T(8,128)(2,1)}, u32[]{:S(2)}, u32[]{:S(2)}) collective-permute-start(bf16[160,2048]{1,0:T(8,128)(2,1)} %refs_10_), channel_id=1, source_target_pairs={{0,2},{2,4},{4,6},{6,0},{1,3},{3,5},{5,7},{7,1},{8,10},{10,12},{12... | collective-permute-start | bytes 1966088 | tf_op jit(solution)/shard_map/ppermute | solution.py:70
  46.9 14.2 %collective-permute-start.7 = (bf16[160,2048]{1,0:T(8,128)(2,1)}, bf16[160,2048]{1,0:T(8,128)(2,1)}, u32[]{:S(2)}, u32[]{:S(2)}) collective-permute-start(bf16[160,2048]{1,0:T(8,128)(2,1)} %refs_10_), channel_id=1, source_target_pairs={{0,6},{2,0},{4,2},{6,4},{1,7},{3,1},{5,3},{7,5},{8,14},{10,8},{12,... | collective-permute-start | bytes 1966088 | tf_op jit(solution)/shard_map/ppermute | solution.py:71
  49.8 17.4 %collective-permute-start.9 = (bf16[128,2944]{1,0:T(8,128)(2,1)S(1)}, bf16[128,2944]{1,0:T(8,128)(2,1)S(1)}, u32[]{:S(2)}, u32[]{:S(2)}) collective-permute-start(bf16[128,2944]{1,0:T(8,128)(2,1)S(1)} %pad_maximum_fusion), channel_id=1, source_target_pairs={{0,17},{1,16},{16,1},{17,0},{2,19},{3,18},{18,3},{19,2},{4,21},{5,... | collective-permute-start | bytes 2261000 | tf_op jit(solution)/shard_map/ppermute | solution.py:807
  68.1 316.1 %reduce-scatter.2.cloned.1.call-start = ((), (), s32[]{:S(2)}) async-start(), calls=%async_computation.2 | async-start | bytes 17842176 | tf_op jit(solution)/shard_map/reduce_scatter | solution.py:844
  68.8 21.4 %collective-permute-start.13 = (bf16[128,2048]{1,0:T(8,128)(2,1)}, bf16[128,2048]{1,0:T(8,128)(2,1)S(1)}, u32[]{:S(2)}, u32[]{:S(2)}) collective-permute-start(bf16[128,2048]{1,0:T(8,128)(2,1)} %collective-permute-done.6.w1), channel_id=1, source_target_pairs={{0,8},{8,0},{1,9},{9,1},{2,10},{10,2},{3,11},{11,3},{4,12},{12,4},... | collective-permute-start | bytes 1572872 | tf_op jit(solution)/shard_map/ppermute | solution.py:118
  77.5 12.7 %collective-permute-start.12 = (bf16[80,2048]{1,0:T(8,128)(2,1)S(1)}, bf16[80,2048]{1,0:T(8,128)(2,1)S(1)}, u32[]{:S(2)}, u32[]{:S(2)}) collective-permute-start(bf16[80,2048]{1,0:T(8,128)(2,1)S(1)} %slice.96), channel_id=1, source_target_pairs={{0,6},{2,0},{4,2},{6,4},{1,7},{3,1},{5,3},{7,5},{8,14},{10,8},{12,... | collective-permute-start | bytes 983048 | tf_op jit(solution)/shard_map/ppermute | solution.py:75
  79.1 11.1 %collective-permute-start.11 = (bf16[80,2048]{1,0:T(8,128)(2,1)S(1)}, bf16[80,2048]{1,0:T(8,128)(2,1)S(1)}, u32[]{:S(2)}, u32[]{:S(2)}) collective-permute-start(bf16[80,2048]{1,0:T(8,128)(2,1)S(1)} %slice.95), channel_id=1, source_target_pairs={{0,2},{2,4},{4,6},{6,0},{1,3},{3,5},{5,7},{7,1},{8,10},{10,12},{12... | collective-permute-start | bytes 983048 | tf_op jit(solution)/shard_map/ppermute | solution.py:74
  80.6 34.6 %collective-permute-start.17 = (bf16[352,2048]{1,0:T(8,128)(2,1)S(1)}, bf16[352,2048]{1,0:T(8,128)(2,1)}, u32[]{:S(2)}, u32[]{:S(2)}) collective-permute-start(bf16[352,2048]{1,0:T(8,128)(2,1)S(1)} %constant_dynamic-slice_fusion), channel_id=1, source_target_pairs={{0,1},{1,0},{2,3},{3,2},{4,5},{5,4},{6,7},{7,6},{8,9},{9,8},{10,11... | collective-permute-start | bytes 4325384 | tf_op jit(solution)/shard_map/ppermute | solution.py:113
  96.5 10.4 %collective-permute-start.14 = (bf16[80,2048]{1,0:T(8,128)(2,1)}, bf16[80,2048]{1,0:T(8,128)(2,1)S(1)}, u32[]{:S(2)}, u32[]{:S(2)}) collective-permute-start(bf16[80,2048]{1,0:T(8,128)(2,1)} %get-tuple-element.103), channel_id=1, source_target_pairs={{0,2},{2,4},{4,6},{6,0},{1,3},{3,5},{5,7},{7,1},{8,10},{10,12},{12... | collective-permute-start | bytes 983048 | tf_op jit(solution)/shard_map/ppermute | solution.py:81
  107.1 16.2 %collective-permute-start.15 = (bf16[160,2048]{1,0:T(8,128)(2,1)S(1)}, bf16[160,2048]{1,0:T(8,128)(2,1)S(1)}, u32[]{:S(2)}, u32[]{:S(2)}) collective-permute-start(bf16[160,2048]{1,0:T(8,128)(2,1)S(1)} %pad_maximum_fusion.1), channel_id=1, source_target_pairs={{0,2},{2,4},{4,6},{6,0},{1,3},{3,5},{5,7},{7,1},{8,10},{10,12},{12... | collective-permute-start | bytes 1966088 | tf_op jit(solution)/shard_map/ppermute | solution.py:85
  115.4 15.2 %collective-permute-start.18 = (bf16[160,2048]{1,0:T(8,128)(2,1)S(1)}, bf16[160,2048]{1,0:T(8,128)(2,1)S(1)}, u32[]{:S(2)}, u32[]{:S(2)}) collective-permute-start(bf16[160,2048]{1,0:T(8,128)(2,1)S(1)} %pad_maximum_fusion.2), channel_id=1, source_target_pairs={{0,6},{2,0},{4,2},{6,4},{1,7},{3,1},{5,3},{7,5},{8,14},{10,8},{12,... | collective-permute-start | bytes 1966088 | tf_op jit(solution)/shard_map/ppermute | solution.py:86
  131.5 16.2 %collective-permute-start.20 = (bf16[160,2048]{1,0:T(8,128)(2,1)S(1)}, bf16[160,2048]{1,0:T(8,128)(2,1)S(1)}, u32[]{:S(2)}, u32[]{:S(2)}) collective-permute-start(bf16[160,2048]{1,0:T(8,128)(2,1)S(1)} %multiply_convert_fusion.n0.refs_0_.refs_5_), channel_id=1, source_target_pairs={{0,2},{2,4},{4,6},{6,0},{1,3},{3,5},{5,7},{7,1},{8,10},{10,12},{12... | collective-permute-start | bytes 1966088 | tf_op jit(solution)/shard_map/ppermute | solution.py:70
  131.6 16.0 %collective-permute-start.19 = (bf16[160,2048]{1,0:T(8,128)(2,1)S(1)}, bf16[160,2048]{1,0:T(8,128)(2,1)S(1)}, u32[]{:S(2)}, u32[]{:S(2)}) collective-permute-start(bf16[160,2048]{1,0:T(8,128)(2,1)S(1)} %multiply_convert_fusion.n0.refs_0_.refs_5_), channel_id=1, source_target_pairs={{0,6},{2,0},{4,2},{6,4},{1,7},{3,1},{5,3},{7,5},{8,14},{10,8},{12,... | collective-permute-start | bytes 1966088 | tf_op jit(solution)/shard_map/ppermute | solution.py:71
  147.7 17.3 %collective-permute-start.23 = (bf16[352,2048]{1,0:T(8,128)(2,1)}, bf16[352,2048]{1,0:T(8,128)(2,1)}, u32[]{:S(2)}, u32[]{:S(2)}) collective-permute-start(bf16[352,2048]{1,0:T(8,128)(2,1)} %collective-permute-done.17.w1), channel_id=1, source_target_pairs={{0,8},{8,0},{1,9},{9,1},{2,10},{10,2},{3,11},{11,3},{4,12},{12,4},... | collective-permute-start | bytes 4325384 | tf_op jit(solution)/shard_map/ppermute | solution.py:841
  153.5 10.7 %collective-permute-start.21 = (bf16[80,2048]{1,0:T(8,128)(2,1)S(1)}, bf16[80,2048]{1,0:T(8,128)(2,1)S(1)}, u32[]{:S(2)}, u32[]{:S(2)}) collective-permute-start(bf16[80,2048]{1,0:T(8,128)(2,1)S(1)} %slice.97), channel_id=1, source_target_pairs={{0,2},{2,4},{4,6},{6,0},{1,3},{3,5},{5,7},{7,1},{8,10},{10,12},{12... | collective-permute-start | bytes 983048 | tf_op jit(solution)/shard_map/ppermute | solution.py:74
  206.7 249.8 %all-gather.5.cloned.1.call-start = ((), (), s32[]{:S(2)}) async-start(), calls=%async_computation.3 | async-start | bytes 9191424 | tf_op jit(solution)/shard_map/all_gather | solution.py:879
  231.2 15.1 %collective-permute-start.27 = (bf16[160,2048]{1,0:T(8,128)(2,1)S(1)}, bf16[160,2048]{1,0:T(8,128)(2,1)S(1)}, u32[]{:S(2)}, u32[]{:S(2)}) collective-permute-start(bf16[160,2048]{1,0:T(8,128)(2,1)S(1)} %pad_maximum_fusion.4), channel_id=1, source_target_pairs={{0,6},{2,0},{4,2},{6,4},{1,7},{3,1},{5,3},{7,5},{8,14},{10,8},{12,... | collective-permute-start | bytes 1966088 | tf_op jit(solution)/shard_map/ppermute | solution.py:86
  235.4 15.8 %collective-permute-start.25 = (bf16[160,2048]{1,0:T(8,128)(2,1)S(1)}, bf16[160,2048]{1,0:T(8,128)(2,1)S(1)}, u32[]{:S(2)}, u32[]{:S(2)}) collective-permute-start(bf16[160,2048]{1,0:T(8,128)(2,1)S(1)} %pad_maximum_fusion.3), channel_id=1, source_target_pairs={{0,2},{2,4},{4,6},{6,0},{1,3},{3,5},{5,7},{7,1},{8,10},{10,12},{12... | collective-permute-start | bytes 1966088 | tf_op jit(solution)/shard_map/ppermute | solution.py:85
  255.3 13.7 %collective-permute-start.29 = (bf16[160,2048]{1,0:T(8,128)(2,1)S(1)}, bf16[160,2048]{1,0:T(8,128)(2,1)S(1)}, u32[]{:S(2)}, u32[]{:S(2)}) collective-permute-start(bf16[160,2048]{1,0:T(8,128)(2,1)S(1)} %get-tuple-element.169.b0.refs_10_), channel_id=1, source_target_pairs={{0,6},{2,0},{4,2},{6,4},{1,7},{3,1},{5,3},{7,5},{8,14},{10,8},{12,... | collective-permute-start | bytes 1966088 | tf_op jit(solution)/shard_map/ppermute | solution.py:71
  255.3 14.8 %collective-permute-start.28 = (bf16[160,2048]{1,0:T(8,128)(2,1)S(1)}, bf16[160,2048]{1,0:T(8,128)(2,1)S(1)}, u32[]{:S(2)}, u32[]{:S(2)}) collective-permute-start(bf16[160,2048]{1,0:T(8,128)(2,1)S(1)} %get-tuple-element.169.b0.refs_10_), channel_id=1, source_target_pairs={{0,2},{2,4},{4,6},{6,0},{1,3},{3,5},{5,7},{7,1},{8,10},{10,12},{12... | collective-permute-start | bytes 1966088 | tf_op jit(solution)/shard_map/ppermute | solution.py:70
  270.1 13.0 %collective-permute-start.30 = (bf16[80,2048]{1,0:T(8,128)(2,1)S(1)}, bf16[80,2048]{1,0:T(8,128)(2,1)}, u32[]{:S(2)}, u32[]{:S(2)}) collective-permute-start(bf16[80,2048]{1,0:T(8,128)(2,1)S(1)} %slice.99), channel_id=1, source_target_pairs={{0,2},{2,4},{4,6},{6,0},{1,3},{3,5},{5,7},{7,1},{8,10},{10,12},{12... | collective-permute-start | bytes 983048 | tf_op jit(solution)/shard_map/ppermute | solution.py:74
  270.9 12.2 %collective-permute-start.31 = (bf16[80,2048]{1,0:T(8,128)(2,1)S(1)}, bf16[80,2048]{1,0:T(8,128)(2,1)}, u32[]{:S(2)}, u32[]{:S(2)}) collective-permute-start(bf16[80,2048]{1,0:T(8,128)(2,1)S(1)} %slice.100), channel_id=1, source_target_pairs={{0,6},{2,0},{4,2},{6,4},{1,7},{3,1},{5,3},{7,5},{8,14},{10,8},{12,... | collective-permute-start | bytes 983048 | tf_op jit(solution)/shard_map/ppermute | solution.py:75
  283.1 22.6 %collective-permute-start.32 = (bf16[160,2048]{1,0:T(8,128)(2,1)}, bf16[160,2048]{1,0:T(8,128)(2,1)S(1)}, u32[]{:S(2)}, u32[]{:S(2)}) collective-permute-start(bf16[160,2048]{1,0:T(8,128)(2,1)} %get-tuple-element.126), channel_id=1, source_target_pairs={{0,2},{2,4},{4,6},{6,0},{1,3},{3,5},{5,7},{7,1},{8,10},{10,12},{12... | collective-permute-start | bytes 1966088 | tf_op jit(solution)/shard_map/ppermute | solution.py:856
  283.2 22.5 %collective-permute-start.33 = (bf16[160,2048]{1,0:T(8,128)(2,1)}, bf16[160,2048]{1,0:T(8,128)(2,1)S(1)}, u32[]{:S(2)}, u32[]{:S(2)}) collective-permute-start(bf16[160,2048]{1,0:T(8,128)(2,1)} %get-tuple-element.128), channel_id=1, source_target_pairs={{0,6},{2,0},{4,2},{6,4},{1,7},{3,1},{5,3},{7,5},{8,14},{10,8},{12,... | collective-permute-start | bytes 1966088 | tf_op jit(solution)/shard_map/ppermute | solution.py:856
  322.8 22.7 %collective-permute-start.40 = (bf16[4,2,1024,128]{3,2,1,0:T(8,128)(2,1)}, bf16[4,2,1024,128]{3,2,1,0:T(8,128)(2,1)S(1)}, u32[]{:S(2)}, u32[]{:S(2)}) collective-permute-start(bf16[4,2,1024,128]{3,2,1,0:T(8,128)(2,1)} %get-tuple-element.146), channel_id=1, source_target_pairs={{0,8},{8,0},{1,9},{9,1},{2,10},{10,2},{3,11},{11,3},{4,12},{12,4},... | collective-permute-start | bytes 6291464 | tf_op jit(solution)/shard_map/ppermute | solution.py:747
  331.2 10.6 %collective-permute-start.35 = (bf16[80,2048]{1,0:T(8,128)(2,1)S(1)}, bf16[80,2048]{1,0:T(8,128)(2,1)S(1)}, u32[]{:S(2)}, u32[]{:S(2)}) collective-permute-start(bf16[80,2048]{1,0:T(8,128)(2,1)S(1)} %copy-done.45), channel_id=1, source_target_pairs={{0,2},{2,4},{4,6},{6,0},{1,3},{3,5},{5,7},{7,1},{8,10},{10,12},{12... | collective-permute-start | bytes 983048 | tf_op jit(solution)/shard_map/ppermute | solution.py:81
  333.9 23.1 %collective-permute-start.38 = (bf16[160,2048]{1,0:T(8,128)(2,1)}, bf16[160,2048]{1,0:T(8,128)(2,1)}, u32[]{:S(2)}, u32[]{:S(2)}) collective-permute-start(bf16[160,2048]{1,0:T(8,128)(2,1)} %pad_maximum_fusion.6), channel_id=1, source_target_pairs={{0,6},{2,0},{4,2},{6,4},{1,7},{3,1},{5,3},{7,5},{8,14},{10,8},{12,... | collective-permute-start | bytes 1966088 | tf_op jit(solution)/shard_map/ppermute | solution.py:86
  342.7 16.9 %collective-permute-start.36 = (bf16[160,2048]{1,0:T(8,128)(2,1)}, bf16[160,2048]{1,0:T(8,128)(2,1)}, u32[]{:S(2)}, u32[]{:S(2)}) collective-permute-start(bf16[160,2048]{1,0:T(8,128)(2,1)} %pad_maximum_fusion.5), channel_id=1, source_target_pairs={{0,2},{2,4},{4,6},{6,0},{1,3},{3,5},{5,7},{7,1},{8,10},{10,12},{12... | collective-permute-start | bytes 1966088 | tf_op jit(solution)/shard_map/ppermute | solution.py:85
  351.4 16.6 %collective-permute-start.42 = (bf16[2,1168,128]{2,1,0:T(8,128)(2,1)}, bf16[2,1168,128]{2,1,0:T(8,128)(2,1)}, u32[]{:S(2)}, u32[]{:S(2)}) collective-permute-start(bf16[2,1168,128]{2,1,0:T(8,128)(2,1)} %get-tuple-element.150), channel_id=1, source_target_pairs={{0,64},{32,96},{64,0},{96,32},{1,65},{33,97},{65,1},{97,33},{2,66}... | collective-permute-start | bytes 1794056 | tf_op jit(solution)/shard_map/ppermute | solution.py:751
  354.3 27.1 %collective-permute-start.43 = (bf16[2,1168,128]{2,1,0:T(8,128)(2,1)}, bf16[2,1168,128]{2,1,0:T(8,128)(2,1)}, u32[]{:S(2)}, u32[]{:S(2)}) collective-permute-start(bf16[2,1168,128]{2,1,0:T(8,128)(2,1)} %get-tuple-element.152), channel_id=1, source_target_pairs={{0,32},{32,64},{64,96},{96,0},{1,33},{33,65},{65,97},{97,1},{2,34}... | collective-permute-start | bytes 1794056 | tf_op jit(solution)/shard_map/ppermute | solution.py:751
  354.8 26.6 %collective-permute-start.44 = (bf16[2,1168,128]{2,1,0:T(8,128)(2,1)}, bf16[2,1168,128]{2,1,0:T(8,128)(2,1)}, u32[]{:S(2)}, u32[]{:S(2)}) collective-permute-start(bf16[2,1168,128]{2,1,0:T(8,128)(2,1)} %get-tuple-element.154), channel_id=1, source_target_pairs={{0,96},{32,0},{64,32},{96,64},{1,97},{33,1},{65,33},{97,65},{2,98}... | collective-permute-start | bytes 1794056 | tf_op jit(solution)/shard_map/ppermute | solution.py:751
  384.2 15.7 %collective-permute-start.47 = (bf16[1168,128]{1,0:T(8,128)(2,1)}, bf16[1168,128]{1,0:T(8,128)(2,1)S(1)}, u32[]{:S(2)}, u32[]{:S(2)}) collective-permute-start(bf16[1168,128]{1,0:T(8,128)(2,1)} %get-tuple-element.157), channel_id=1, source_target_pairs={{0,17},{1,16},{16,1},{17,0},{2,19},{3,18},{18,3},{19,2},{4,21},{5,... | collective-permute-start | bytes 897032 | tf_op jit(solution)/shard_map/ppermute | solution.py:762
  385.1 14.8 %collective-permute-start.46 = (bf16[1168,128]{1,0:T(8,128)(2,1)}, bf16[1168,128]{1,0:T(8,128)(2,1)}, u32[]{:S(2)}, u32[]{:S(2)}) collective-permute-start(bf16[1168,128]{1,0:T(8,128)(2,1)} %get-tuple-element.157), channel_id=1, source_target_pairs={{0,1},{1,0},{2,3},{3,2},{4,5},{5,4},{6,7},{7,6},{8,9},{9,8},{10,11... | collective-permute-start | bytes 897032 | tf_op jit(solution)/shard_map/ppermute | solution.py:761
  386.4 18.3 %collective-permute-start.45 = (bf16[1168,128]{1,0:T(8,128)(2,1)}, bf16[1168,128]{1,0:T(8,128)(2,1)}, u32[]{:S(2)}, u32[]{:S(2)}) collective-permute-start(bf16[1168,128]{1,0:T(8,128)(2,1)} %get-tuple-element.156.a), channel_id=1, source_target_pairs={{0,16},{16,0},{1,17},{17,1},{2,18},{18,2},{3,19},{19,3},{4,20},{20... | collective-permute-start | bytes 897032 | tf_op jit(solution)/shard_map/ppermute | solution.py:760
  406.9 12.3 %collective-permute-start.50 = (bf16[1168,128]{1,0:T(8,128)(2,1)}, bf16[1168,128]{1,0:T(8,128)(2,1)S(1)}, u32[]{:S(2)}, u32[]{:S(2)}) collective-permute-start(bf16[1168,128]{1,0:T(8,128)(2,1)} %sum_z.1.refs_0_), channel_id=1, source_target_pairs={{0,96},{32,0},{64,32},{96,64},{1,97},{33,1},{65,33},{97,65},{2,98}... | collective-permute-start | bytes 897032 | tf_op jit(solution)/shard_map/ppermute | solution.py:765
  411.2 17.3 %collective-permute-start.49 = (bf16[1168,128]{1,0:T(8,128)(2,1)}, bf16[1168,128]{1,0:T(8,128)(2,1)S(1)}, u32[]{:S(2)}, u32[]{:S(2)}) collective-permute-start(bf16[1168,128]{1,0:T(8,128)(2,1)} %sum_z.1.refs_0_), channel_id=1, source_target_pairs={{0,64},{32,96},{64,0},{96,32},{1,65},{33,97},{65,1},{97,33},{2,66}... | collective-permute-start | bytes 897032 | tf_op jit(solution)/shard_map/ppermute | solution.py:765
  411.2 24.9 %collective-permute-start.48 = (bf16[1168,128]{1,0:T(8,128)(2,1)}, bf16[1168,128]{1,0:T(8,128)(2,1)S(1)}, u32[]{:S(2)}, u32[]{:S(2)}) collective-permute-start(bf16[1168,128]{1,0:T(8,128)(2,1)} %sum_z.1.refs_0_), channel_id=1, source_target_pairs={{0,32},{32,64},{64,96},{96,0},{1,33},{33,65},{65,97},{97,1},{2,34}... | collective-permute-start | bytes 897032 | tf_op jit(solution)/shard_map/ppermute | solution.py:765
  411.8 40.4 %collective-permute-start.39 = (bf16[160,2048]{1,0:T(8,128)(2,1)}, bf16[160,2048]{1,0:T(8,128)(2,1)}, u32[]{:S(2)}, u32[]{:S(2)}) collective-permute-start(bf16[160,2048]{1,0:T(8,128)(2,1)} %get-tuple-element.143), channel_id=1, source_target_pairs={{0,4},{2,6},{4,0},{6,2},{1,5},{3,7},{5,1},{7,3},{8,12},{10,14},{12... | collective-permute-start | bytes 1966088 | tf_op jit(solution)/shard_map/ppermute | solution.py:871
  411.8 31.9 %collective-permute-start.51 = (bf16[1168,128]{1,0:T(8,128)(2,1)}, bf16[1168,128]{1,0:T(8,128)(2,1)S(1)}, u32[]{:S(2)}, u32[]{:S(2)}) collective-permute-start(bf16[1168,128]{1,0:T(8,128)(2,1)} %sum_z.1.refs_0_), channel_id=1, source_target_pairs={{0,8},{8,0},{1,9},{9,1},{2,10},{10,2},{3,11},{11,3},{4,12},{12,4},... | collective-permute-start | bytes 897032 | tf_op jit(solution)/shard_map/ppermute | solution.py:766
  419.2 24.5 %collective-permute-start.54 = (bf16[1168,128]{1,0:T(8,128)(2,1)S(1)}, bf16[1168,128]{1,0:T(8,128)(2,1)S(1)}, u32[]{:S(2)}, u32[]{:S(2)}) collective-permute-start(bf16[1168,128]{1,0:T(8,128)(2,1)S(1)} %collective-permute-done.50.refs_3_), channel_id=1, source_target_pairs={{0,8},{8,0},{1,9},{9,1},{2,10},{10,2},{3,11},{11,3},{4,12},{12,4},... | collective-permute-start | bytes 897032 | tf_op jit(solution)/shard_map/ppermute | solution.py:766
  428.5 15.2 %collective-permute-start.53 = (bf16[1168,128]{1,0:T(8,128)(2,1)S(1)}, bf16[1168,128]{1,0:T(8,128)(2,1)S(1)}, u32[]{:S(2)}, u32[]{:S(2)}) collective-permute-start(bf16[1168,128]{1,0:T(8,128)(2,1)S(1)} %collective-permute-done.49.refs_2_), channel_id=1, source_target_pairs={{0,8},{8,0},{1,9},{9,1},{2,10},{10,2},{3,11},{11,3},{4,12},{12,4},... | collective-permute-start | bytes 897032 | tf_op jit(solution)/shard_map/ppermute | solution.py:766
  (65 other events, 593.2 us)
Sparse Core Ops, SparseCore 0:
  68.2 44.2 all-gather.2
  206.8 115.9 reduce-scatter.1
  384.3 68.9 all-gather.4

commit v7 on v5

--- a/solution.py
+++ b/solution.py
@@ -66,22 +66,36 @@
     return [(i, (i + s) % n) for i in range(n)]
 
 
-def gather_x(v):
+def gather_x(v, wait=()):
     from_prev = lax.ppermute(v, "x", shift(4, 1))
     from_next = lax.ppermute(v, "x", shift(4, -1))
-    send_a = tie(from_prev[:HALF], from_next)
-    send_b = tie(from_next[HALF:], from_prev)
+    send_a = tie(from_prev[:HALF], from_next, *wait)
+    send_b = tie(from_next[HALF:], from_prev, *wait)
     opp_a = lax.ppermute(send_a, "x", shift(4, 1))
     opp_b = lax.ppermute(send_b, "x", shift(4, -1))
     return v, from_next, opp_a, opp_b, from_prev
+
+
+def relay_body(p1, got_a, p3, got_b, q1, q3):
+    q1[:HALF, :] = (p1[:HALF, :].astype(F32) + got_a[...].astype(F32)).astype(BF16)
+    q1[HALF:, :] = p1[HALF:, :]
+    q3[:HALF, :] = p3[:HALF, :]
+    q3[HALF:, :] = (p3[HALF:, :].astype(F32) + got_b[...].astype(F32)).astype(BF16)
 
 
 def scatter_x(parts):
     p0, p1, p2a, p2b, p3 = parts
     got_a = lax.ppermute(p2a, "x", shift(4, 1))
     got_b = lax.ppermute(p2b, "x", shift(4, -1))
-    q1 = jnp.concatenate([(p1[:HALF].astype(F32) + got_a.astype(F32)).astype(BF16), p1[HALF:]], 0)
-    q3 = jnp.concatenate([p3[:HALF], (p3[HALF:].astype(F32) + got_b.astype(F32)).astype(BF16)], 0)
+    q1, q3 = pl.pallas_call(
+        relay_body,
+        out_shape=(sds((BLK, D)),) * 2,
+        in_specs=[spec()] * 4,
+        out_specs=(spec(),) * 2,
+        compiler_params=params(),
+        cost_estimate=cost(1e6, 3e6),
+        name="relay",
+    )(p1, got_a, p3, got_b)
     from_prev = lax.ppermute(q1, "x", shift(4, 1))
     from_next = lax.ppermute(q3, "x", shift(4, -1))
     return p0.astype(F32) + from_prev.astype(F32) + from_next.astype(F32), (got_a, got_b)
@@ -748,7 +762,6 @@
     got_b = lax.ppermute(second[1], "core", shift(2, 1))
     part = sds((2, TAIL, 128))
     g = small_call(sum_core_body, (part,) * 4, idx, first[0], got_a, second[0], got_b, name="sum_core")
-    summed = g[0]
     got = [tie(lax.ppermute(g[s], "y", shift(4, s)), before) for s in (2, 1, 3)]
     part = sds((TAIL, 128))
     own, other = small_call(sum_y_body, (part,) * 2, idx, g[0], *got, name="sum_y")
@@ -766,7 +779,7 @@
     mine = [g] + [lax.ppermute(g, "y", shift(4, s)) for s in (1, 2, 3)]
     theirs = [lax.ppermute(v, "core", shift(2, 1)) for v in mine]
     shapes = (sds((DH, QW), F32), sds((AW // 2, D), F32), sds((2, D), F32))
-    return summed, small_call(unpack_tail_body, shapes, idx, *mine, *theirs, name="unpack_tail")
+    return own, small_call(unpack_tail_body, shapes, idx, *mine, *theirs, name="unpack_tail")
 
 
 def inverse_rms(v):
@@ -799,10 +812,10 @@
 
     tok = tokens.astype(F32)
     s_one = inverse_rms(tok)
-    qkv_all = fetch_partner(qkv_weight, core)
+    qkv_got = fetch_half(qkv_weight, core)
     normed_one = gather_x((tok * s_one * gain_one).astype(BF16))
-    out_all = fetch_partner(out_weight, core, normed_one[2])
-    cots = gather_x(tie(cotangent, normed_one[2]))
+    qkv_all = qkv_weight, qkv_got, lax.ppermute(tie(qkv_got, normed_one[2], normed_one[3]), "core", shift(2, 1))
+    out_all = fetch_partner(out_weight, core, qkv_got, normed_one[2], normed_one[3])
 
     begin, position = replica_layout(seq_lengths, seq_replica, (y * 2 + zl) * 2 + core)
     half_rows = lambda v: lax.dynamic_index_in_dim(v.reshape(4, 2, BLK), zh, 1, False).reshape(ROWS, 1)
@@ -814,14 +827,14 @@
     sine = jnp.where((lane % HD) < HD // 2, -1.0, 1.0)[None, :] * jnp.sin(angles)
 
     q, kv_own = qkv_forward(idx, normed_one, qkv_all, cosine, sine)
-    kv_par = lax.ppermute(kv_own, "zh", shift(2, 1))
+    cots = gather_x(tie(cotangent, normed_one[2], normed_one[3]), (kv_own,))
     rows = DH // 8
     mine = lambda w: lax.dynamic_slice_in_dim(w, (y * 2 + core) * rows, rows, 0)
     cross = [(2 * a + b, 2 * (1 - a) + (1 - b)) for a in range(2) for b in range(2)]
     gate_up = lax.ppermute(
         jnp.concatenate(
             [
-                tie(mine(gate_weight), kv_par),
+                tie(mine(gate_weight), out_all[1], kv_own),
                 jnp.zeros((rows, GAP - FF4), BF16),
                 mine(up_weight),
             ],
@@ -830,12 +843,12 @@
         ("zl", "zh"),
         cross,
     )
-    down_got = fetch_half(tie(down_weight, kv_par), core)
-    q = tie(q, cots[1], cots[4], out_all[1])
-    att, qx = attend(idx, q, kv_own, kv_par, first)
+    kv_par = lax.ppermute(tie(kv_own, cots[1], cots[4]), "zh", shift(2, 1))
+    down_got = fetch_half(tie(down_weight, gate_up), core)
+    att, qx = attend(idx, tie(q, cots[2], cots[3]), kv_own, kv_par, first)
     gate_up = lax.all_gather(tie(gate_up, qx), ("y", "core"), axis=0, tiled=True)
-    parts = [tie(p, cots[2], cots[3]) for p in out_project(idx, att, out_all)]
-    after_attn = tok + scatter_x(parts)[0]
+    parts = out_project(idx, att, out_all)
+    after_attn = tie(tok, down_got) + scatter_x(parts)[0]
 
     r_two = inverse_rms(after_attn)
     normed_two = gather_x((after_attn * r_two * gain_two).astype(BF16))
@@ -863,6 +876,7 @@
     tail = attn_grads(
         idx, normed_one, branch, dqm.reshape(ROWS, AW), tie(att, *layer).reshape(ROWS, AW)
     )
+    dkv_got = tie(dkv_got, tail[0])
     *tail_kv, parts = qkv_back(
         idx, dqm.reshape(ROWS, AW), dkv_own, dkv_got, cosine, sine, qkv_all, normed_one, gain_one,
         gain_grad_two,

time: 490 us -> 486 us (level)
  waiting for transfers between devices: 182 us -> 154 us
  starting transfers between devices: 96.7 us -> 120 us
  Pallas kernels: 146 us -> 155 us
    ppermute x3, waiting for transfers between devices: 34.1 us -> 11.4 us  [fetch_half(): lax.ppermute(lax.dynamic_slice_in_dim(w, core * half, half, 0), 'zh', shi...]
    ppermute x3, waiting for transfers between devices: 18.4 us -> 0.01 us  [scatter_x(): from_next = lax.ppermute(q3, 'x', shift(4, -1))]
    ppermute x4, waiting for transfers between devices: 2.03 us -> 19 us  [gather_x(): from_prev = lax.ppermute(v, 'x', shift(4, 1))]
    ppermute x1, waiting for transfers between devices: 0.01 us -> 12.2 us  [sum_tail(): lax.ppermute(other, ('zl', 'zh'), cross)]
    ppermute x1, waiting for transfers between devices: 12.2 us -> 0.01 us  [sum_tail(): lax.ppermute(other, 'zh', shift(2, 1))]
    ppermute x1, starting transfers between devices: 3.45 us -> 13.9 us  [on_device(): lax.ppermute(tie(down_got, normed_two[1], normed_two[4]), 'core', shift(2...]
    ppermute x3, waiting for transfers between devices: 31.3 us -> 21.3 us  [sum_tail(): got = [tie(lax.ppermute(g[s], 'y', shift(4, s)), before) for s in (2, 1, 3)]]
    ppermute x3, waiting for transfers between devices: 12.4 us -> 22.3 us  [scatter_x(): got_a = lax.ppermute(p2a, 'x', shift(4, 1))]
  transfers between devices with their start and end apart: 61 -> 61, of which waited for: 28 -> 26; matrix products, arithmetic and copies ran while one was open for 6% -> 5% of each run, Pallas kernels for 20% -> 21%
where the time goes in v7:
time: 486 us; the launch traced here: 483 us
  Pallas kernels  155 us (32%)
  waiting for transfers between devices  154 us (32%)
  starting transfers between devices  120 us (25%)
  local copies, waits for them, and re-layouts  21 us (4%)
  other arithmetic  18 us (4%)
  between operations  14.6 us (3%)
    ppermute x4, starting transfers between devices, sum_tail(): theirs = [lax.ppermute(v, 'core', shift(2, 1)) for v in mine]  23 us
    ppermute x3, waiting for transfers between devices, scatter_x(): got_a = lax.ppermute(p2a, 'x', shift(4, 1))  22.3 us
    ppermute x3, waiting for transfers between devices, sum_tail(): got = [tie(lax.ppermute(g[s], 'y', shift(4, s)), before) for s in (2, 1, 3)]  21.3 us
    pallas_call x1, Pallas kernels, ffn(): pl.pallas_call(ffn_body, grid=(TILES,), out_shape=(sds((ROWS, FF4)),) * 3...  20.9 us
    pallas_call x1, Pallas kernels, ffn_grads(): pl.pallas_call(ffn_grads_body, grid=(16 // QS,), out_shape=sds((2, 16, PI...  20.8 us
    pallas_call x1, Pallas kernels, attend_back(): pl.pallas_call(attend_back_body, out_shape=(sds((4, BLK, AW)), sds((ROWS,...  19.8 us
    ppermute x4, waiting for transfers between devices, gather_x(): from_prev = lax.ppermute(v, 'x', shift(4, 1))  19 us
    ppermute x4, waiting for transfers between devices, gather_x(): from_next = lax.ppermute(v, 'x', shift(4, -1))  17.1 us
  transfers between devices with their start and end apart: 61, of which 26 were waited for; matrix products, arithmetic and copies ran while one was open for 5% of the time, Pallas kernels for 21%

profile of v7, /device:TPU:1, one launch (start us, length us, event | category | flops | bytes accessed | tf_op | source)
XLA Modules:
  0.0 482.6 jit_solution(13363188555524369610)
XLA Ops:
  10.0 3.4 collective-permute-start.2
  14.3 3.6 collective-permute-start
  20.9 5.8 %collective-permute-done.2.n1.refs_1_.refs_6_ = bf16[160,2048]{1,0:T(8,128)(2,1)S(1)} collective-permute-done((bf16[160,2048]{1,0:T(8,128)(2,1)S(1)}, bf16[160,2048]{1,0:T(8,128)(2,1)S(1)}, u32[]{:S(2)}, u32[]{:S(2)}) %collective-permute-start.2) | collective-permute-done | bytes 655392 | tf_op jit(solution)/shard_map/ppermute | solution.py:71
  26.8 3.2 collective-permute-done.1.n3.refs_4_.refs_9_
  33.8 5.0 %collective-permute-done.3.n2a.refs_2_.refs_7_ = bf16[80,2048]{1,0:T(8,128)(2,1)S(1)} collective-permute-done((bf16[80,2048]{1,0:T(8,128)(2,1)S(1)}, bf16[80,2048]{1,0:T(8,128)(2,1)S(1)}, u32[]{:S(2)}, u32[]{:S(2)}) %collective-permute-start.3) | collective-permute-done | bytes 327712 | tf_op jit(solution)/shard_map/ppermute | solution.py:74
  41.1 3.2 collective-permute-start.6
  44.4 3.6 collective-permute-start.5
  51.6 6.8 %qkv_forward.1 = (bf16[4,1280,128]{2,1,0:T(8,128)(2,1)}, bf16[640,128]{1,0:T(8,128)(2,1)}) custom-call(s32[4]{0:T(128)} %pad_add_fusion.idx, bf16[160,2048]{1,0:T(8,128)(2,1)} %copy-done.2, bf16[160,2048]{1,0:T(8,128)(2,1)} %copy-done.4, bf16[80,2048]{1,0:T(8,128)(2,1)} %copy-done.19, bf16[80,2048]{1,0:T(8,128)(2,1)} %copy-done.20, ...), custom_call_target="tpu_custom_call" | custom-call | flops 1677721600 | bytes 7000000 | tf_op jit(solution)/shard_map/qkv_forward/pallas_call | solution.py:168
  63.2 3.0 collective-permute-start.12
  67.2 4.8 collective-permute-done.11.c2a.refs_12_
  73.4 8.7 %attend.1 = (bf16[4,160,512]{2,1,0:T(8,128)(2,1)}, bf16[4,1280,128]{2,1,0:T(8,128)(2,1)}) custom-call(s32[4]{0:T(128)} %pad_add_fusion.idx, bf16[4,1280,128]{2,1,0:T(8,128)(2,1)} %get-tuple-element.104.q, bf16[640,128]{1,0:T(8,128)(2,1)} %get-tuple-element.105.kv_own, bf16[640,128]{1,0:T(8,128)(2,1)} %copy-done.54, s32[1,1280]{1,0:T(1,128)} %reshape_tile.3.first), custom_call_target="tpu_custom_call" | custom-call | flops 12000000000 | bytes 3000000 | tf_op jit(solution)/shard_map/attend/pallas_call | solution.py:261
  84.6 3.5 collective-permute-start.14
  91.5 4.8 out_project.1
  98.9 7.9 %collective-permute-done.15.got_a = bf16[80,2048]{1,0:T(8,128)(2,1)S(1)} collective-permute-done((bf16[80,2048]{1,0:T(8,128)(2,1)}, bf16[80,2048]{1,0:T(8,128)(2,1)S(1)}, u32[]{:S(2)}, u32[]{:S(2)}) %collective-permute-start.15) | collective-permute-done | bytes 327712 | tf_op jit(solution)/shard_map/ppermute | solution.py:88
  113.1 11.4 %collective-permute-done.8.w1 = bf16[352,2048]{1,0:T(8,128)(2,1)} collective-permute-done((bf16[352,2048]{1,0:T(8,128)(2,1)S(1)}, bf16[352,2048]{1,0:T(8,128)(2,1)}, u32[]{:S(2)}, u32[]{:S(2)}) %collective-permute-start.8) | collective-permute-done | bytes 1441824 | tf_op jit(solution)/shard_map/ppermute | solution.py:127
  130.6 12.8 %collective-permute-done.20.n3.refs_4_.refs_9_ = bf16[160,2048]{1,0:T(8,128)(2,1)S(1)} collective-permute-done((bf16[160,2048]{1,0:T(8,128)(2,1)S(1)}, bf16[160,2048]{1,0:T(8,128)(2,1)S(1)}, u32[]{:S(2)}, u32[]{:S(2)}) %collective-permute-start.20) | collective-permute-done | bytes 655392 | tf_op jit(solution)/shard_map/ppermute | solution.py:70
  143.4 13.9 %collective-permute-start.23 = (bf16[352,2048]{1,0:T(8,128)(2,1)}, bf16[352,2048]{1,0:T(8,128)(2,1)}, u32[]{:S(2)}, u32[]{:S(2)}) collective-permute-start(bf16[352,2048]{1,0:T(8,128)(2,1)} %collective-permute-done.8.w1), channel_id=1, source_target_pairs={{0,8},{8,0},{1,9},{9,1},{2,10},{10,2},{3,11},{11,3},{4,12},{12,4},... | collective-permute-start | bytes 4325384 | tf_op jit(solution)/shard_map/ppermute | solution.py:855
  159.8 7.1 %collective-permute-done.22.n2b.refs_3_.refs_8_ = bf16[80,2048]{1,0:T(8,128)(2,1)S(1)} collective-permute-done((bf16[80,2048]{1,0:T(8,128)(2,1)S(1)}, bf16[80,2048]{1,0:T(8,128)(2,1)S(1)}, u32[]{:S(2)}, u32[]{:S(2)}) %collective-permute-start.22) | collective-permute-done | bytes 327712 | tf_op jit(solution)/shard_map/ppermute | solution.py:75
  166.9 3.1 collective-permute-done.21.n2a.refs_2_.refs_7_
  170.7 20.9 %ffn.1 = (bf16[640,1408]{1,0:T(8,128)(2,1)}, bf16[640,1408]{1,0:T(8,128)(2,1)}, bf16[640,1408]{1,0:T(8,128)(2,1)}) custom-call(s32[4]{0:T(128)} %pad_add_fusion.idx, bf16[160,2048]{1,0:T(8,128)(2,1)} %copy-done.15, bf16[160,2048]{1,0:T(8,128)(2,1)} %copy-done.40, bf16[80,2048]{1,0:T(8,128)(2,1)} %copy-done.52, bf16[80,2048]{1,0:T(8,128)(2,1)} %copy-done.51, ...), custom_call_target="tpu_custom_call" | custom-call | flops 11072962560 | bytes 34000000 | tf_op jit(solution)/shard_map/ffn/pallas_call | solution.py:496
  191.6 20.8 %ffn_grads.1 = bf16[2,16,2112,128]{3,2,1,0:T(8,128)(2,1)} custom-call(bf16[160,2048]{1,0:T(8,128)(2,1)} %copy-done.15, bf16[160,2048]{1,0:T(8,128)(2,1)} %copy-done.40, bf16[80,2048]{1,0:T(8,128)(2,1)} %copy-done.52, bf16[80,2048]{1,0:T(8,128)(2,1)} %copy-done.51, bf16[160,2048]{1,0:T(8,128)(2,1)} %copy-done.39, bf16[160,2048]{1,0:T(8,128)(2,1)} %copy-done.15, ...), custom_call_target="tpu_custom_call" | custom-call | flops 11072962560 | bytes 30000000 | tf_op jit(solution)/shard_map/ffn_grads/pallas_call | solution.py:608
  212.4 16.0 %ffn_back.1 = (bf16[160,2048]{1,0:T(8,128)(2,1)}, bf16[160,2048]{1,0:T(8,128)(2,1)}, bf16[80,2048]{1,0:T(8,128)(2,1)}, bf16[80,2048]{1,0:T(8,128)(2,1)}, bf16[160,2048]{1,0:T(8,128)(2,1)}) custom-call(s32[4]{0:T(128)} %pad_add_fusion.idx, bf16[640,1408]{1,0:T(8,128)(2,1)} %get-tuple-element.122.refs_16_.dgate, ...), custom_call_target="tpu_custom_call" | custom-call | flops 7381975040 | bytes 18000000 | tf_op jit(solution)/shard_map/ffn_back/pallas_call | solution.py:561
  231.2 7.0 %collective-permute-done.24.got_a = bf16[80,2048]{1,0:T(8,128)(2,1)S(1)} collective-permute-done((bf16[80,2048]{1,0:T(8,128)(2,1)}, bf16[80,2048]{1,0:T(8,128)(2,1)S(1)}, u32[]{:S(2)}, u32[]{:S(2)}) %collective-permute-start.24) | collective-permute-done | bytes 327712 | tf_op jit(solution)/shard_map/ppermute | solution.py:88
  239.1 2.8 relay.4
  244.6 13.2 %collective-permute-done.26 = bf16[160,2048]{1,0:T(8,128)(2,1)S(1)} collective-permute-done((bf16[160,2048]{1,0:T(8,128)(2,1)}, bf16[160,2048]{1,0:T(8,128)(2,1)S(1)}, u32[]{:S(2)}, u32[]{:S(2)}) %collective-permute-start.26) | collective-permute-done | bytes 655392 | tf_op jit(solution)/shard_map/ppermute | solution.py:99
  263.1 11.2 %collective-permute-done.29.b1.refs_11_ = bf16[160,2048]{1,0:T(8,128)(2,1)S(1)} collective-permute-done((bf16[160,2048]{1,0:T(8,128)(2,1)S(1)}, bf16[160,2048]{1,0:T(8,128)(2,1)S(1)}, u32[]{:S(2)}, u32[]{:S(2)}) %collective-permute-start.29) | collective-permute-done | bytes 655392 | tf_op jit(solution)/shard_map/ppermute | solution.py:71
  274.4 3.0 collective-permute-done.28.b3.refs_14_
  280.2 10.1 %down_project.1 = (bf16[160,2048]{1,0:T(8,128)(2,1)}, bf16[160,2048]{1,0:T(8,128)(2,1)}, bf16[160,2048]{1,0:T(8,128)(2,1)}, bf16[160,2048]{1,0:T(8,128)(2,1)}) custom-call(s32[4]{0:T(128)} %pad_add_fusion.idx, bf16[640,1408]{1,0:T(8,128)(2,1)} %get-tuple-element.130.refs_15_.hid, bf16[704,2048]{1,0:T(8,128)(2,1)} %w0.9, ...), custom_call_target="tpu_custom_call" | custom-call | flops 3690987520 | bytes 11000000 | tf_op jit(solution)/shard_map/down_project/pallas_call | solution.py:531
  291.8 3.1 collective-permute-start.33
  294.8 19.8 %attend_back.1 = (bf16[4,160,512]{2,1,0:T(8,128)(2,1)}, f32[640,128]{1,0:T(8,128)}, bf16[640,128]{1,0:T(8,128)(2,1)}) custom-call(s32[4]{0:T(128)} %pad_add_fusion.idx, bf16[4,1280,128]{2,1,0:T(8,128)(2,1)} %get-tuple-element.116.qx, bf16[640,128]{1,0:T(8,128)(2,1)} %get-tuple-element.105.kv_own, bf16[640,128]{1,0:T(8,128)(2,1)} %copy-done.54, ...), custom_call_target="tpu_custom_call" | custom-call | flops 30000001024 | bytes 8000000 | tf_op jit(solution)/shard_map/attend_back/pallas_call | solution.py:370
  314.7 8.9 %attn_grads.1 = (bf16[4,2,1024,128]{3,2,1,0:T(8,128)(2,1)}, bf16[4,2,1024,128]{3,2,1,0:T(8,128)(2,1)}) custom-call(s32[4]{0:T(128)} %pad_add_fusion.idx, bf16[160,2048]{1,0:T(8,128)(2,1)} %copy-done.2, bf16[160,2048]{1,0:T(8,128)(2,1)} %copy-done.4, bf16[80,2048]{1,0:T(8,128)(2,1)} %copy-done.19, bf16[80,2048]{1,0:T(8,128)(2,1)} %copy-done.20, ...), custom_call_target="tpu_custom_call" | custom-call | flops 2684354560 | bytes 10000000 | tf_op jit(solution)/shard_map/attn_grads/pallas_call | solution.py:690
  323.7 6.2 %collective-permute-start.40 = (bf16[4,2,1024,128]{3,2,1,0:T(8,128)(2,1)}, bf16[4,2,1024,128]{3,2,1,0:T(8,128)(2,1)}, u32[]{:S(2)}, u32[]{:S(2)}) collective-permute-start(bf16[4,2,1024,128]{3,2,1,0:T(8,128)(2,1)} %get-tuple-element.156), channel_id=1, source_target_pairs={{0,8},{8,0},{1,9},{9,1},{2,10},{10,2},{3,11},{11,3},{4,12},{12,4},... | collective-permute-start | bytes 6291464 | tf_op jit(solution)/shard_map/ppermute | solution.py:761
  329.8 7.1 %qkv_back.1 = (bf16[4,2,144,128]{3,2,1,0:T(8,128)(2,1)}, bf16[4,2,144,128]{3,2,1,0:T(8,128)(2,1)}, bf16[160,2048]{1,0:T(8,128)(2,1)}, bf16[160,2048]{1,0:T(8,128...) custom-call(s32[4]{0:T(128)} %pad_add_fusion.idx, ...), custom_call_target="tpu_custom_call" | custom-call | flops 1677721600 | bytes 13000000 | tf_op jit(solution)/shard_map/qkv_back/pallas_call | solution.py:427
  339.7 7.4 %collective-permute-done.35.got_a = bf16[80,2048]{1,0:T(8,128)(2,1)S(1)} collective-permute-done((bf16[80,2048]{1,0:T(8,128)(2,1)}, bf16[80,2048]{1,0:T(8,128)(2,1)S(1)}, u32[]{:S(2)}, u32[]{:S(2)}) %collective-permute-start.35) | collective-permute-done | bytes 327712 | tf_op jit(solution)/shard_map/ppermute | solution.py:88
  357.4 3.9 sum_core.1
  361.3 2.9 collective-permute-start.42
  370.4 7.4 %collective-permute-done.42.b = bf16[2,1168,128]{2,1,0:T(8,128)(2,1)} collective-permute-done((bf16[2,1168,128]{2,1,0:T(8,128)(2,1)}, bf16[2,1168,128]{2,1,0:T(8,128)(2,1)}, u32[]{:S(2)}, u32[]{:S(2)}) %collective-permute-start.42) | collective-permute-done | bytes 598048 | tf_op jit(solution)/shard_map/ppermute | solution.py:765
  377.8 13.5 %collective-permute-done.43.c = bf16[2,1168,128]{2,1,0:T(8,128)(2,1)} collective-permute-done((bf16[2,1168,128]{2,1,0:T(8,128)(2,1)}, bf16[2,1168,128]{2,1,0:T(8,128)(2,1)}, u32[]{:S(2)}, u32[]{:S(2)}) %collective-permute-start.43) | collective-permute-done | bytes 598048 | tf_op jit(solution)/shard_map/ppermute | solution.py:765
  398.0 12.2 %collective-permute-done.47.d = bf16[1168,128]{1,0:T(8,128)(2,1)S(1)} collective-permute-done((bf16[1168,128]{1,0:T(8,128)(2,1)}, bf16[1168,128]{1,0:T(8,128)(2,1)S(1)}, u32[]{:S(2)}, u32[]{:S(2)}) %collective-permute-start.47) | collective-permute-done | bytes 299040 | tf_op jit(solution)/shard_map/ppermute | solution.py:776
  410.2 4.4 collective-permute-done.45.b
  416.7 5.2 %collective-permute-start.50 = (bf16[1168,128]{1,0:T(8,128)(2,1)}, bf16[1168,128]{1,0:T(8,128)(2,1)S(1)}, u32[]{:S(2)}, u32[]{:S(2)}) collective-permute-start(bf16[1168,128]{1,0:T(8,128)(2,1)} %sum_z.1.refs_0_), channel_id=1, source_target_pairs={{0,96},{32,0},{64,32},{96,64},{1,97},{33,1},{65,33},{97,65},{2,98}... | collective-permute-start | bytes 897032 | tf_op jit(solution)/shard_map/ppermute | solution.py:779
  422.5 4.4 collective-permute-start.51
  426.9 3.2 collective-permute-done.50.refs_3_
  430.1 8.7 %collective-permute-start.54 = (bf16[1168,128]{1,0:T(8,128)(2,1)S(1)}, bf16[1168,128]{1,0:T(8,128)(2,1)S(1)}, u32[]{:S(2)}, u32[]{:S(2)}) collective-permute-start(bf16[1168,128]{1,0:T(8,128)(2,1)S(1)} %collective-permute-done.50.refs_3_), channel_id=1, source_target_pairs={{0,8},{8,0},{1,9},{9,1},{2,10},{10,2},{3,11},{11,3},{4,12},{12,4},... | collective-permute-start | bytes 897032 | tf_op jit(solution)/shard_map/ppermute | solution.py:780
  438.8 5.0 %collective-permute-start.53 = (bf16[1168,128]{1,0:T(8,128)(2,1)S(1)}, bf16[1168,128]{1,0:T(8,128)(2,1)S(1)}, u32[]{:S(2)}, u32[]{:S(2)}) collective-permute-start(bf16[1168,128]{1,0:T(8,128)(2,1)S(1)} %collective-permute-done.49.refs_2_), channel_id=1, source_target_pairs={{0,8},{8,0},{1,9},{9,1},{2,10},{10,2},{3,11},{11,3},{4,12},{12,4},... | collective-permute-start | bytes 897032 | tf_op jit(solution)/shard_map/ppermute | solution.py:780
  446.5 5.0 %collective-permute-start.52 = (bf16[1168,128]{1,0:T(8,128)(2,1)S(1)}, bf16[1168,128]{1,0:T(8,128)(2,1)}, u32[]{:S(2)}, u32[]{:S(2)}) collective-permute-start(bf16[1168,128]{1,0:T(8,128)(2,1)S(1)} %collective-permute-done.48.refs_1_), channel_id=1, source_target_pairs={{0,8},{8,0},{1,9},{9,1},{2,10},{10,2},{3,11},{11,3},{4,12},{12,4},... | collective-permute-start | bytes 897032 | tf_op jit(solution)/shard_map/ppermute | solution.py:780
  455.7 4.2 unpack_tail.1
  466.0 9.8 %unpack.1 = (f32[1024,1408]{1,0:T(8,128)}, f32[1024,1408]{1,0:T(8,128)}, f32[704,2048]{1,0:T(8,128)}) custom-call(bf16[16,2112,128]{2,1,0:T(8,128)(2,1)} %all-gather.5.cloned.1.call-done.piece), custom_call_target="tpu_custom_call" | custom-call | flops 1000000 | bytes 26000000 | tf_op jit(solution)/shard_map/unpack/pallas_call | solution.py:635
  (254 shorter events, 105.6 us)
Async XLA Ops:
  7.2 163.5 %all-gather.3.cloned.1.call-start = ((), (), s32[]{:S(2)}) async-start(), calls=%async_computation.1 | async-start | bytes 6782976 | tf_op jit(solution)/shard_map/all_gather | solution.py:849
  10.0 16.8 %collective-permute-start.2 = (bf16[160,2048]{1,0:T(8,128)(2,1)S(1)}, bf16[160,2048]{1,0:T(8,128)(2,1)S(1)}, u32[]{:S(2)}, u32[]{:S(2)}) collective-permute-start(bf16[160,2048]{1,0:T(8,128)(2,1)S(1)} %multiply_convert_fusion.1.n0.refs_0_.refs_5_), channel_id=1, source_target_pairs={{0,6},{2,0},{4,2},{6,4},{1,7},{3,1},{5,3},{7,5},{8,14},{10,8},{12,... | collective-permute-start | bytes 1966088 | tf_op jit(solution)/shard_map/ppermute | solution.py:71
  13.4 16.6 %collective-permute-start.1 = (bf16[160,2048]{1,0:T(8,128)(2,1)S(1)}, bf16[160,2048]{1,0:T(8,128)(2,1)S(1)}, u32[]{:S(2)}, u32[]{:S(2)}) collective-permute-start(bf16[160,2048]{1,0:T(8,128)(2,1)S(1)} %multiply_convert_fusion.1.n0.refs_0_.refs_5_), channel_id=1, source_target_pairs={{0,2},{2,4},{4,6},{6,0},{1,3},{3,5},{5,7},{7,1},{8,10},{10,12},{12... | collective-permute-start | bytes 1966088 | tf_op jit(solution)/shard_map/ppermute | solution.py:70
  14.3 26.9 %collective-permute-start = (bf16[512,640]{1,0:T(8,128)(2,1)}, bf16[512,640]{1,0:T(8,128)(2,1)}, u32[]{:S(2)}, u32[]{:S(2)}) collective-permute-start(bf16[512,640]{1,0:T(8,128)(2,1)} %constant_dynamic-slice_fusion.4), channel_id=1, source_target_pairs={{0,1},{1,0},{2,3},{3,2},{4,5},{5,4},{6,7},{7,6},{8,9},{9,8},{10,11... | collective-permute-start | bytes 1966088 | tf_op jit(solution)/shard_map/ppermute | solution.py:127
  38.7 19.6 %collective-permute-start.10 = (bf16[160,2048]{1,0:T(8,128)(2,1)S(1)}, bf16[160,2048]{1,0:T(8,128)(2,1)}, u32[]{:S(2)}, u32[]{:S(2)}) collective-permute-start(bf16[160,2048]{1,0:T(8,128)(2,1)S(1)} %copy-done.7), channel_id=1, source_target_pairs={{0,6},{2,0},{4,2},{6,4},{1,7},{3,1},{5,3},{7,5},{8,14},{10,8},{12,... | collective-permute-start | bytes 1966088 | tf_op jit(solution)/shard_map/ppermute | solution.py:71
  41.1 17.2 %collective-permute-start.9 = (bf16[160,2048]{1,0:T(8,128)(2,1)S(1)}, bf16[160,2048]{1,0:T(8,128)(2,1)}, u32[]{:S(2)}, u32[]{:S(2)}) collective-permute-start(bf16[160,2048]{1,0:T(8,128)(2,1)S(1)} %copy-done.7), channel_id=1, source_target_pairs={{0,2},{2,4},{4,6},{6,0},{1,3},{3,5},{5,7},{7,1},{8,10},{10,12},{12... | collective-permute-start | bytes 1966088 | tf_op jit(solution)/shard_map/ppermute | solution.py:70
  41.1 10.5 %collective-permute-start.6 = (bf16[512,640]{1,0:T(8,128)(2,1)}, bf16[512,640]{1,0:T(8,128)(2,1)}, u32[]{:S(2)}, u32[]{:S(2)}) collective-permute-start(bf16[512,640]{1,0:T(8,128)(2,1)} %collective-permute-done.w1), channel_id=1, source_target_pairs={{0,8},{8,0},{1,9},{9,1},{2,10},{10,2},{3,11},{11,3},{4,12},{12,4},... | collective-permute-start | bytes 1966088 | tf_op jit(solution)/shard_map/ppermute | solution.py:817
  44.4 16.0 %collective-permute-start.5 = (bf16[128,2048]{1,0:T(8,128)(2,1)S(1)}, bf16[128,2048]{1,0:T(8,128)(2,1)}, u32[]{:S(2)}, u32[]{:S(2)}) collective-permute-start(bf16[128,2048]{1,0:T(8,128)(2,1)S(1)} %constant_dynamic-slice_fusion.3), channel_id=1, source_target_pairs={{0,1},{1,0},{2,3},{3,2},{4,5},{5,4},{6,7},{7,6},{8,9},{9,8},{10,11... | collective-permute-start | bytes 1572872 | tf_op jit(solution)/shard_map/ppermute | solution.py:127
  60.4 12.3 %collective-permute-start.13 = (bf16[640,128]{1,0:T(8,128)(2,1)S(1)}, bf16[640,128]{1,0:T(8,128)(2,1)S(1)}, u32[]{:S(2)}, u32[]{:S(2)}) collective-permute-start(bf16[640,128]{1,0:T(8,128)(2,1)S(1)} %copy-done.53), channel_id=1, source_target_pairs={{0,1},{1,0},{2,3},{3,2},{4,5},{5,4},{6,7},{7,6},{8,9},{9,8},{10,11... | collective-permute-start | bytes 491528 | tf_op jit(solution)/shard_map/ppermute | solution.py:846
  66.2 17.4 %collective-permute-start.7 = (bf16[128,2944]{1,0:T(8,128)(2,1)S(1)}, bf16[128,2944]{1,0:T(8,128)(2,1)S(1)}, u32[]{:S(2)}, u32[]{:S(2)}) collective-permute-start(bf16[128,2944]{1,0:T(8,128)(2,1)S(1)} %pad_maximum_fusion), channel_id=1, source_target_pairs={{0,17},{1,16},{16,1},{17,0},{2,19},{3,18},{18,3},{19,2},{4,21},{5,... | collective-permute-start | bytes 2261000 | tf_op jit(solution)/shard_map/ppermute | solution.py:834
  84.5 309.8 %reduce-scatter.2.cloned.1.call-start = ((), (), s32[]{:S(2)}) async-start(), calls=%async_computation.2 | async-start | bytes 17842176 | tf_op jit(solution)/shard_map/reduce_scatter | solution.py:858
  89.6 34.9 %collective-permute-start.8 = (bf16[352,2048]{1,0:T(8,128)(2,1)S(1)}, bf16[352,2048]{1,0:T(8,128)(2,1)}, u32[]{:S(2)}, u32[]{:S(2)}) collective-permute-start(bf16[352,2048]{1,0:T(8,128)(2,1)S(1)} %constant_dynamic-slice_fusion.1), channel_id=1, source_target_pairs={{0,1},{1,0},{2,3},{3,2},{4,5},{5,4},{6,7},{7,6},{8,9},{9,8},{10,11... | collective-permute-start | bytes 4325384 | tf_op jit(solution)/shard_map/ppermute | solution.py:127
  96.2 10.5 %collective-permute-start.15 = (bf16[80,2048]{1,0:T(8,128)(2,1)}, bf16[80,2048]{1,0:T(8,128)(2,1)S(1)}, u32[]{:S(2)}, u32[]{:S(2)}) collective-permute-start(bf16[80,2048]{1,0:T(8,128)(2,1)} %get-tuple-element.109), channel_id=1, source_target_pairs={{0,2},{2,4},{4,6},{6,0},{1,3},{3,5},{5,7},{7,1},{8,10},{10,12},{12... | collective-permute-start | bytes 983048 | tf_op jit(solution)/shard_map/ppermute | solution.py:88
  96.2 10.5 %collective-permute-start.16 = (bf16[80,2048]{1,0:T(8,128)(2,1)}, bf16[80,2048]{1,0:T(8,128)(2,1)S(1)}, u32[]{:S(2)}, u32[]{:S(2)}) collective-permute-start(bf16[80,2048]{1,0:T(8,128)(2,1)} %get-tuple-element.111), channel_id=1, source_target_pairs={{0,6},{2,0},{4,2},{6,4},{1,7},{3,1},{5,3},{7,5},{8,14},{10,8},{12,... | collective-permute-start | bytes 983048 | tf_op jit(solution)/shard_map/ppermute | solution.py:89
  110.3 16.6 %collective-permute-start.17 = (bf16[160,2048]{1,0:T(8,128)(2,1)}, bf16[160,2048]{1,0:T(8,128)(2,1)S(1)}, u32[]{:S(2)}, u32[]{:S(2)}) collective-permute-start(bf16[160,2048]{1,0:T(8,128)(2,1)} %get-tuple-element.112), channel_id=1, source_target_pairs={{0,2},{2,4},{4,6},{6,0},{1,3},{3,5},{5,7},{7,1},{8,10},{10,12},{12... | collective-permute-start | bytes 1966088 | tf_op jit(solution)/shard_map/ppermute | solution.py:99
  110.7 16.2 %collective-permute-start.18 = (bf16[160,2048]{1,0:T(8,128)(2,1)}, bf16[160,2048]{1,0:T(8,128)(2,1)S(1)}, u32[]{:S(2)}, u32[]{:S(2)}) collective-permute-start(bf16[160,2048]{1,0:T(8,128)(2,1)} %get-tuple-element.113), channel_id=1, source_target_pairs={{0,6},{2,0},{4,2},{6,4},{1,7},{3,1},{5,3},{7,5},{8,14},{10,8},{12,... | collective-permute-start | bytes 1966088 | tf_op jit(solution)/shard_map/ppermute | solution.py:100
  127.8 15.6 %collective-permute-start.20 = (bf16[160,2048]{1,0:T(8,128)(2,1)S(1)}, bf16[160,2048]{1,0:T(8,128)(2,1)S(1)}, u32[]{:S(2)}, u32[]{:S(2)}) collective-permute-start(bf16[160,2048]{1,0:T(8,128)(2,1)S(1)} %multiply_convert_fusion.n0.refs_0_.refs_5_), channel_id=1, source_target_pairs={{0,2},{2,4},{4,6},{6,0},{1,3},{3,5},{5,7},{7,1},{8,10},{10,12},{12... | collective-permute-start | bytes 1966088 | tf_op jit(solution)/shard_map/ppermute | solution.py:70
  127.9 15.5 %collective-permute-start.19 = (bf16[160,2048]{1,0:T(8,128)(2,1)S(1)}, bf16[160,2048]{1,0:T(8,128)(2,1)S(1)}, u32[]{:S(2)}, u32[]{:S(2)}) collective-permute-start(bf16[160,2048]{1,0:T(8,128)(2,1)S(1)} %multiply_convert_fusion.n0.refs_0_.refs_5_), channel_id=1, source_target_pairs={{0,6},{2,0},{4,2},{6,4},{1,7},{3,1},{5,3},{7,5},{8,14},{10,8},{12,... | collective-permute-start | bytes 1966088 | tf_op jit(solution)/shard_map/ppermute | solution.py:71
  143.4 27.3 %collective-permute-start.23 = (bf16[352,2048]{1,0:T(8,128)(2,1)}, bf16[352,2048]{1,0:T(8,128)(2,1)}, u32[]{:S(2)}, u32[]{:S(2)}) collective-permute-start(bf16[352,2048]{1,0:T(8,128)(2,1)} %collective-permute-done.8.w1), channel_id=1, source_target_pairs={{0,8},{8,0},{1,9},{9,1},{2,10},{10,2},{3,11},{11,3},{4,12},{12,4},... | collective-permute-start | bytes 4325384 | tf_op jit(solution)/shard_map/ppermute | solution.py:855
  159.8 10.2 %collective-permute-start.21 = (bf16[80,2048]{1,0:T(8,128)(2,1)S(1)}, bf16[80,2048]{1,0:T(8,128)(2,1)S(1)}, u32[]{:S(2)}, u32[]{:S(2)}) collective-permute-start(bf16[80,2048]{1,0:T(8,128)(2,1)S(1)} %slice.49), channel_id=1, source_target_pairs={{0,2},{2,4},{4,6},{6,0},{1,3},{3,5},{5,7},{7,1},{8,10},{10,12},{12... | collective-permute-start | bytes 983048 | tf_op jit(solution)/shard_map/ppermute | solution.py:74
  212.4 253.6 %all-gather.5.cloned.1.call-start = ((), (), s32[]{:S(2)}) async-start(), calls=%async_computation.3 | async-start | bytes 9191424 | tf_op jit(solution)/shard_map/all_gather | solution.py:893
  228.5 9.8 %collective-permute-start.24 = (bf16[80,2048]{1,0:T(8,128)(2,1)}, bf16[80,2048]{1,0:T(8,128)(2,1)S(1)}, u32[]{:S(2)}, u32[]{:S(2)}) collective-permute-start(bf16[80,2048]{1,0:T(8,128)(2,1)} %get-tuple-element.125), channel_id=1, source_target_pairs={{0,2},{2,4},{4,6},{6,0},{1,3},{3,5},{5,7},{7,1},{8,10},{10,12},{12... | collective-permute-start | bytes 983048 | tf_op jit(solution)/shard_map/ppermute | solution.py:88
  241.9 15.8 %collective-permute-start.26 = (bf16[160,2048]{1,0:T(8,128)(2,1)}, bf16[160,2048]{1,0:T(8,128)(2,1)S(1)}, u32[]{:S(2)}, u32[]{:S(2)}) collective-permute-start(bf16[160,2048]{1,0:T(8,128)(2,1)} %get-tuple-element.128), channel_id=1, source_target_pairs={{0,2},{2,4},{4,6},{6,0},{1,3},{3,5},{5,7},{7,1},{8,10},{10,12},{12... | collective-permute-start | bytes 1966088 | tf_op jit(solution)/shard_map/ppermute | solution.py:99
  241.9 15.8 %collective-permute-start.27 = (bf16[160,2048]{1,0:T(8,128)(2,1)}, bf16[160,2048]{1,0:T(8,128)(2,1)S(1)}, u32[]{:S(2)}, u32[]{:S(2)}) collective-permute-start(bf16[160,2048]{1,0:T(8,128)(2,1)} %get-tuple-element.129), channel_id=1, source_target_pairs={{0,6},{2,0},{4,2},{6,4},{1,7},{3,1},{5,3},{7,5},{8,14},{10,8},{12,... | collective-permute-start | bytes 1966088 | tf_op jit(solution)/shard_map/ppermute | solution.py:100
  260.7 13.6 %collective-permute-start.29 = (bf16[160,2048]{1,0:T(8,128)(2,1)S(1)}, bf16[160,2048]{1,0:T(8,128)(2,1)S(1)}, u32[]{:S(2)}, u32[]{:S(2)}) collective-permute-start(bf16[160,2048]{1,0:T(8,128)(2,1)S(1)} %get-tuple-element.179.b0.refs_10_), channel_id=1, source_target_pairs={{0,6},{2,0},{4,2},{6,4},{1,7},{3,1},{5,3},{7,5},{8,14},{10,8},{12,... | collective-permute-start | bytes 1966088 | tf_op jit(solution)/shard_map/ppermute | solution.py:71
  263.1 14.3 %collective-permute-start.28 = (bf16[160,2048]{1,0:T(8,128)(2,1)S(1)}, bf16[160,2048]{1,0:T(8,128)(2,1)S(1)}, u32[]{:S(2)}, u32[]{:S(2)}) collective-permute-start(bf16[160,2048]{1,0:T(8,128)(2,1)S(1)} %get-tuple-element.179.b0.refs_10_), channel_id=1, source_target_pairs={{0,2},{2,4},{4,6},{6,0},{1,3},{3,5},{5,7},{7,1},{8,10},{10,12},{12... | collective-permute-start | bytes 1966088 | tf_op jit(solution)/shard_map/ppermute | solution.py:70
  277.4 12.9 %collective-permute-start.30 = (bf16[80,2048]{1,0:T(8,128)(2,1)S(1)}, bf16[80,2048]{1,0:T(8,128)(2,1)S(1)}, u32[]{:S(2)}, u32[]{:S(2)}) collective-permute-start(bf16[80,2048]{1,0:T(8,128)(2,1)S(1)} %slice.51), channel_id=1, source_target_pairs={{0,2},{2,4},{4,6},{6,0},{1,3},{3,5},{5,7},{7,1},{8,10},{10,12},{12... | collective-permute-start | bytes 983048 | tf_op jit(solution)/shard_map/ppermute | solution.py:74
  278.2 12.8 %collective-permute-start.31 = (bf16[80,2048]{1,0:T(8,128)(2,1)S(1)}, bf16[80,2048]{1,0:T(8,128)(2,1)S(1)}, u32[]{:S(2)}, u32[]{:S(2)}) collective-permute-start(bf16[80,2048]{1,0:T(8,128)(2,1)S(1)} %slice.52), channel_id=1, source_target_pairs={{0,6},{2,0},{4,2},{6,4},{1,7},{3,1},{5,3},{7,5},{8,14},{10,8},{12,... | collective-permute-start | bytes 983048 | tf_op jit(solution)/shard_map/ppermute | solution.py:75
  291.8 22.8 %collective-permute-start.32 = (bf16[160,2048]{1,0:T(8,128)(2,1)}, bf16[160,2048]{1,0:T(8,128)(2,1)S(1)}, u32[]{:S(2)}, u32[]{:S(2)}) collective-permute-start(bf16[160,2048]{1,0:T(8,128)(2,1)} %get-tuple-element.135), channel_id=1, source_target_pairs={{0,2},{2,4},{4,6},{6,0},{1,3},{3,5},{5,7},{7,1},{8,10},{10,12},{12... | collective-permute-start | bytes 1966088 | tf_op jit(solution)/shard_map/ppermute | solution.py:870
  291.8 22.9 %collective-permute-start.33 = (bf16[160,2048]{1,0:T(8,128)(2,1)}, bf16[160,2048]{1,0:T(8,128)(2,1)S(1)}, u32[]{:S(2)}, u32[]{:S(2)}) collective-permute-start(bf16[160,2048]{1,0:T(8,128)(2,1)} %get-tuple-element.137), channel_id=1, source_target_pairs={{0,6},{2,0},{4,2},{6,4},{1,7},{3,1},{5,3},{7,5},{8,14},{10,8},{12,... | collective-permute-start | bytes 1966088 | tf_op jit(solution)/shard_map/ppermute | solution.py:870
  323.7 33.0 %collective-permute-start.40 = (bf16[4,2,1024,128]{3,2,1,0:T(8,128)(2,1)}, bf16[4,2,1024,128]{3,2,1,0:T(8,128)(2,1)}, u32[]{:S(2)}, u32[]{:S(2)}) collective-permute-start(bf16[4,2,1024,128]{3,2,1,0:T(8,128)(2,1)} %get-tuple-element.156), channel_id=1, source_target_pairs={{0,8},{8,0},{1,9},{9,1},{2,10},{10,2},{3,11},{11,3},{4,12},{12,4},... | collective-permute-start | bytes 6291464 | tf_op jit(solution)/shard_map/ppermute | solution.py:761
  336.9 10.1 %collective-permute-start.35 = (bf16[80,2048]{1,0:T(8,128)(2,1)}, bf16[80,2048]{1,0:T(8,128)(2,1)S(1)}, u32[]{:S(2)}, u32[]{:S(2)}) collective-permute-start(bf16[80,2048]{1,0:T(8,128)(2,1)} %get-tuple-element.148), channel_id=1, source_target_pairs={{0,2},{2,4},{4,6},{6,0},{1,3},{3,5},{5,7},{7,1},{8,10},{10,12},{12... | collective-permute-start | bytes 983048 | tf_op jit(solution)/shard_map/ppermute | solution.py:88
  337.0 10.1 %collective-permute-start.36 = (bf16[80,2048]{1,0:T(8,128)(2,1)}, bf16[80,2048]{1,0:T(8,128)(2,1)S(1)}, u32[]{:S(2)}, u32[]{:S(2)}) collective-permute-start(bf16[80,2048]{1,0:T(8,128)(2,1)} %get-tuple-element.150), channel_id=1, source_target_pairs={{0,6},{2,0},{4,2},{6,4},{1,7},{3,1},{5,3},{7,5},{8,14},{10,8},{12,... | collective-permute-start | bytes 983048 | tf_op jit(solution)/shard_map/ppermute | solution.py:89
  350.5 16.3 %collective-permute-start.37 = (bf16[160,2048]{1,0:T(8,128)(2,1)}, bf16[160,2048]{1,0:T(8,128)(2,1)S(1)}, u32[]{:S(2)}, u32[]{:S(2)}) collective-permute-start(bf16[160,2048]{1,0:T(8,128)(2,1)} %get-tuple-element.151), channel_id=1, source_target_pairs={{0,2},{2,4},{4,6},{6,0},{1,3},{3,5},{5,7},{7,1},{8,10},{10,12},{12... | collective-permute-start | bytes 1966088 | tf_op jit(solution)/shard_map/ppermute | solution.py:99
  350.5 16.3 %collective-permute-start.38 = (bf16[160,2048]{1,0:T(8,128)(2,1)}, bf16[160,2048]{1,0:T(8,128)(2,1)S(1)}, u32[]{:S(2)}, u32[]{:S(2)}) collective-permute-start(bf16[160,2048]{1,0:T(8,128)(2,1)} %get-tuple-element.152), channel_id=1, source_target_pairs={{0,6},{2,0},{4,2},{6,4},{1,7},{3,1},{5,3},{7,5},{8,14},{10,8},{12,... | collective-permute-start | bytes 1966088 | tf_op jit(solution)/shard_map/ppermute | solution.py:100
  361.3 16.6 %collective-permute-start.42 = (bf16[2,1168,128]{2,1,0:T(8,128)(2,1)}, bf16[2,1168,128]{2,1,0:T(8,128)(2,1)}, u32[]{:S(2)}, u32[]{:S(2)}) collective-permute-start(bf16[2,1168,128]{2,1,0:T(8,128)(2,1)} %get-tuple-element.160), channel_id=1, source_target_pairs={{0,64},{32,96},{64,0},{96,32},{1,65},{33,97},{65,1},{97,33},{2,66}... | collective-permute-start | bytes 1794056 | tf_op jit(solution)/shard_map/ppermute | solution.py:765
  364.1 27.2 %collective-permute-start.43 = (bf16[2,1168,128]{2,1,0:T(8,128)(2,1)}, bf16[2,1168,128]{2,1,0:T(8,128)(2,1)}, u32[]{:S(2)}, u32[]{:S(2)}) collective-permute-start(bf16[2,1168,128]{2,1,0:T(8,128)(2,1)} %get-tuple-element.162), channel_id=1, source_target_pairs={{0,32},{32,64},{64,96},{96,0},{1,33},{33,65},{65,97},{97,1},{2,34}... | collective-permute-start | bytes 1794056 | tf_op jit(solution)/shard_map/ppermute | solution.py:765
  365.3 26.4 %collective-permute-start.44 = (bf16[2,1168,128]{2,1,0:T(8,128)(2,1)}, bf16[2,1168,128]{2,1,0:T(8,128)(2,1)}, u32[]{:S(2)}, u32[]{:S(2)}) collective-permute-start(bf16[2,1168,128]{2,1,0:T(8,128)(2,1)} %get-tuple-element.164), channel_id=1, source_target_pairs={{0,96},{32,0},{64,32},{96,64},{1,97},{33,1},{65,33},{97,65},{2,98}... | collective-permute-start | bytes 1794056 | tf_op jit(solution)/shard_map/ppermute | solution.py:765
  394.4 15.8 %collective-permute-start.47 = (bf16[1168,128]{1,0:T(8,128)(2,1)}, bf16[1168,128]{1,0:T(8,128)(2,1)S(1)}, u32[]{:S(2)}, u32[]{:S(2)}) collective-permute-start(bf16[1168,128]{1,0:T(8,128)(2,1)} %get-tuple-element.167), channel_id=1, source_target_pairs={{0,17},{1,16},{16,1},{17,0},{2,19},{3,18},{18,3},{19,2},{4,21},{5,... | collective-permute-start | bytes 897032 | tf_op jit(solution)/shard_map/ppermute | solution.py:776
  397.2 13.1 %collective-permute-start.46 = (bf16[1168,128]{1,0:T(8,128)(2,1)}, bf16[1168,128]{1,0:T(8,128)(2,1)}, u32[]{:S(2)}, u32[]{:S(2)}) collective-permute-start(bf16[1168,128]{1,0:T(8,128)(2,1)} %get-tuple-element.167), channel_id=1, source_target_pairs={{0,1},{1,0},{2,3},{3,2},{4,5},{5,4},{6,7},{7,6},{8,9},{9,8},{10,11... | collective-permute-start | bytes 897032 | tf_op jit(solution)/shard_map/ppermute | solution.py:775
  397.2 17.5 %collective-permute-start.45 = (bf16[1168,128]{1,0:T(8,128)(2,1)}, bf16[1168,128]{1,0:T(8,128)(2,1)}, u32[]{:S(2)}, u32[]{:S(2)}) collective-permute-start(bf16[1168,128]{1,0:T(8,128)(2,1)} %get-tuple-element.166.a), channel_id=1, source_target_pairs={{0,16},{16,0},{1,17},{17,1},{2,18},{18,2},{3,19},{19,3},{4,20},{20... | collective-permute-start | bytes 897032 | tf_op jit(solution)/shard_map/ppermute | solution.py:774
  416.7 13.3 %collective-permute-start.50 = (bf16[1168,128]{1,0:T(8,128)(2,1)}, bf16[1168,128]{1,0:T(8,128)(2,1)S(1)}, u32[]{:S(2)}, u32[]{:S(2)}) collective-permute-start(bf16[1168,128]{1,0:T(8,128)(2,1)} %sum_z.1.refs_0_), channel_id=1, source_target_pairs={{0,96},{32,0},{64,32},{96,64},{1,97},{33,1},{65,33},{97,65},{2,98}... | collective-permute-start | bytes 897032 | tf_op jit(solution)/shard_map/ppermute | solution.py:779
  421.9 16.9 %collective-permute-start.49 = (bf16[1168,128]{1,0:T(8,128)(2,1)}, bf16[1168,128]{1,0:T(8,128)(2,1)S(1)}, u32[]{:S(2)}, u32[]{:S(2)}) collective-permute-start(bf16[1168,128]{1,0:T(8,128)(2,1)} %sum_z.1.refs_0_), channel_id=1, source_target_pairs={{0,64},{32,96},{64,0},{96,32},{1,65},{33,97},{65,1},{97,33},{2,66}... | collective-permute-start | bytes 897032 | tf_op jit(solution)/shard_map/ppermute | solution.py:779
  421.9 24.6 %collective-permute-start.48 = (bf16[1168,128]{1,0:T(8,128)(2,1)}, bf16[1168,128]{1,0:T(8,128)(2,1)S(1)}, u32[]{:S(2)}, u32[]{:S(2)}) collective-permute-start(bf16[1168,128]{1,0:T(8,128)(2,1)} %sum_z.1.refs_0_), channel_id=1, source_target_pairs={{0,32},{32,64},{64,96},{96,0},{1,33},{33,65},{65,97},{97,1},{2,34}... | collective-permute-start | bytes 897032 | tf_op jit(solution)/shard_map/ppermute | solution.py:779
  422.5 38.9 %collective-permute-start.39 = (bf16[160,2048]{1,0:T(8,128)(2,1)}, bf16[160,2048]{1,0:T(8,128)(2,1)}, u32[]{:S(2)}, u32[]{:S(2)}) collective-permute-start(bf16[160,2048]{1,0:T(8,128)(2,1)} %get-tuple-element.153), channel_id=1, source_target_pairs={{0,4},{2,6},{4,0},{6,2},{1,5},{3,7},{5,1},{7,3},{8,12},{10,14},{12... | collective-permute-start | bytes 1966088 | tf_op jit(solution)/shard_map/ppermute | solution.py:885
  422.5 31.6 %collective-permute-start.51 = (bf16[1168,128]{1,0:T(8,128)(2,1)}, bf16[1168,128]{1,0:T(8,128)(2,1)S(1)}, u32[]{:S(2)}, u32[]{:S(2)}) collective-permute-start(bf16[1168,128]{1,0:T(8,128)(2,1)} %sum_z.1.refs_0_), channel_id=1, source_target_pairs={{0,8},{8,0},{1,9},{9,1},{2,10},{10,2},{3,11},{11,3},{4,12},{12,4},... | collective-permute-start | bytes 897032 | tf_op jit(solution)/shard_map/ppermute | solution.py:780
  430.1 24.1 %collective-permute-start.54 = (bf16[1168,128]{1,0:T(8,128)(2,1)S(1)}, bf16[1168,128]{1,0:T(8,128)(2,1)S(1)}, u32[]{:S(2)}, u32[]{:S(2)}) collective-permute-start(bf16[1168,128]{1,0:T(8,128)(2,1)S(1)} %collective-permute-done.50.refs_3_), channel_id=1, source_target_pairs={{0,8},{8,0},{1,9},{9,1},{2,10},{10,2},{3,11},{11,3},{4,12},{12,4},... | collective-permute-start | bytes 897032 | tf_op jit(solution)/shard_map/ppermute | solution.py:780
  438.8 15.4 %collective-permute-start.53 = (bf16[1168,128]{1,0:T(8,128)(2,1)S(1)}, bf16[1168,128]{1,0:T(8,128)(2,1)S(1)}, u32[]{:S(2)}, u32[]{:S(2)}) collective-permute-start(bf16[1168,128]{1,0:T(8,128)(2,1)S(1)} %collective-permute-done.49.refs_2_), channel_id=1, source_target_pairs={{0,8},{8,0},{1,9},{9,1},{2,10},{10,2},{3,11},{11,3},{4,12},{12,4},... | collective-permute-start | bytes 897032 | tf_op jit(solution)/shard_map/ppermute | solution.py:780
  (68 other events, 549.5 us)
Sparse Core Ops, SparseCore 0:
  84.7 42.4 all-gather.2
  212.5 117.0 reduce-scatter.1
  394.5 68.9 all-gather.4

commit v8 on v7

--- a/solution.py
+++ b/solution.py
@@ -83,7 +83,7 @@
     q3[HALF:, :] = (p3[HALF:, :].astype(F32) + got_b[...].astype(F32)).astype(BF16)
 
 
-def scatter_x(parts):
+def relay(parts):
     p0, p1, p2a, p2b, p3 = parts
     got_a = lax.ppermute(p2a, "x", shift(4, 1))
     got_b = lax.ppermute(p2b, "x", shift(4, -1))
@@ -96,9 +96,14 @@
         cost_estimate=cost(1e6, 3e6),
         name="relay",
     )(p1, got_a, p3, got_b)
+    return p0, q1, q3
+
+
+def scatter_x(parts):
+    p0, q1, q3 = relay(parts)
     from_prev = lax.ppermute(q1, "x", shift(4, 1))
     from_next = lax.ppermute(q3, "x", shift(4, -1))
-    return p0.astype(F32) + from_prev.astype(F32) + from_next.astype(F32), (got_a, got_b)
+    return p0.astype(F32) + from_prev.astype(F32) + from_next.astype(F32), (q1, q3)
 
 
 PIECES = ((0, BLK), (1, BLK), (2, HALF), (2, HALF), (3, BLK))
@@ -578,14 +583,9 @@
 QS = 4
 
 
-def ffn_grads_body(*refs):
-    na, nb, cots = refs[0:5], refs[5:10], refs[10:15]
-    hid, dgate, dup, out, hid_t = refs[15:]
-
-    @pl.when(pl.program_id(0) == 0)
-    def _():
-        hid_t[...] = hid[...].T
-
+def gate_up_grads_body(*refs):
+    na, nb = refs[0:5], refs[5:10]
+    dgate, dup, _, out = refs[10:]
     stack = lambda parts: jnp.concatenate([r[...] for r in parts], 0)
     rows = jnp.concatenate([stack(na), stack(nb)], 1).T
     for k, ref in enumerate((dgate, dup)):
@@ -596,29 +596,52 @@
                 for c in range(FF4 // 128):
                     first = k * GU_ROWS + c * 64
                     out[h, q, first : first + 64, :] = r[:, c * 128 : (c + 1) * 128]
-    g = dot(hid_t[...], stack(cots)).astype(BF16)
-    for h in range(2):
-        for q in range(QS):
-            out[h, q, 2 * GU_ROWS :, :] = g[
-                h * (FF4 // 2) : (h + 1) * (FF4 // 2), q * 128 : (q + 1) * 128
-            ]
-
-
-def ffn_grads(normed, cots, hid, dgate, dup):
-    return pl.pallas_call(
-        ffn_grads_body,
+
+
+def gate_up_grads(normed, dgate, dup, pieces):
+    return pl.pallas_call(
+        gate_up_grads_body,
         grid=(16 // QS,),
         out_shape=sds((2, 16, PIECE, 128)),
         in_specs=[pl.BlockSpec((n, 64 * QS), lambda i: (0, i)) for _, n in PIECES]
         + [pl.BlockSpec((n, 64 * QS), lambda i: (0, i + 16 // QS)) for _, n in PIECES]
-        + [pl.BlockSpec((n, 128 * QS), lambda i: (0, i)) for _, n in PIECES]
-        + [whole(ROWS, FF4)] * 3,
-        out_specs=pl.BlockSpec((2, QS, PIECE, 128), lambda i: (0, i, 0, 0)),
+        + [whole(ROWS, FF4)] * 2
+        + [spec(pl.ANY)],
+        out_specs=pl.BlockSpec((2, QS, 2 * GU_ROWS, 128), lambda i: (0, i, 0, 0)),
+        input_output_aliases={12: 0},
+        compiler_params=params(),
+        cost_estimate=cost(4 * ROWS * D * FF4, 2e7),
+        name="gate_up_grads",
+    )(*normed, *normed, dgate, dup, pieces)
+
+
+def down_grads_body(*refs):
+    cots = refs[0:5]
+    hid, out, hid_t = refs[5:]
+
+    @pl.when(pl.program_id(0) == 0)
+    def _():
+        hid_t[...] = hid[...].T
+
+    g = dot(hid_t[...], jnp.concatenate([r[...] for r in cots], 0)).astype(BF16)
+    for h in range(2):
+        for q in range(QS):
+            out[h, q, :, :] = g[h * (FF4 // 2) : (h + 1) * (FF4 // 2), q * 128 : (q + 1) * 128]
+
+
+def down_grads(cots, hid):
+    return pl.pallas_call(
+        down_grads_body,
+        grid=(16 // QS,),
+        out_shape=sds((2, 16, PIECE, 128)),
+        in_specs=[pl.BlockSpec((n, 128 * QS), lambda i: (0, i)) for _, n in PIECES]
+        + [whole(ROWS, FF4)],
+        out_specs=pl.BlockSpec((2, QS, FF4 // 2, 128), lambda i: (0, i, 2, 0)),
         scratch_shapes=[pltpu.VMEM((FF4, ROWS), BF16)],
         compiler_params=params(),
-        cost_estimate=cost(6 * ROWS * D * FF4, 3e7),
-        name="ffn_grads",
-    )(*normed, *normed, *cots, hid, dgate, dup)
+        cost_estimate=cost(2 * ROWS * D * FF4, 1e7),
+        name="down_grads",
+    )(*cots, hid)
 
 
 def unpack_body(piece, gate, up, down):
@@ -854,13 +877,17 @@
     normed_two = gather_x((after_attn * r_two * gain_two).astype(BF16))
     down_all = down_weight, down_got, lax.ppermute(tie(down_got, normed_two[1], normed_two[4]), "core", shift(2, 1))
     hid, dgate, dup = ffn(idx, normed_two, cots, gate_weight, up_weight, gate_up, down_all)
-    own_grads = ffn_grads(normed_two, cots, hid, dgate, dup)
+    d_parts = ffn_back(idx, dgate, dup, gate_weight, up_weight, gate_up)
+    own_grads = down_grads(cots, tie(hid, d_parts[2]))
+    d_own, q1, q3 = relay(d_parts)
+    own_grads = gate_up_grads(normed_two, tie(dgate, q1, q3), dup, own_grads)
+    from_prev = lax.ppermute(q1, "x", shift(4, 1))
+    from_next = lax.ppermute(q3, "x", shift(4, -1))
     grads = lax.psum_scatter(
-        own_grads.reshape(32, PIECE, 128), ("zh", "zl", "y", "core"), scatter_dimension=0, tiled=True
+        tie(own_grads, from_prev, from_next).reshape(32, PIECE, 128),
+        ("zh", "zl", "y", "core"), scatter_dimension=0, tiled=True,
     )
-    d_two, _ = scatter_x(
-        ffn_back(idx, tie(dgate, own_grads), dup, gate_weight, up_weight, gate_up)
-    )
+    d_two = d_own.astype(F32) + from_prev.astype(F32) + from_next.astype(F32)
     back_two, gain_grad_two = norm_back(after_attn, r_two, gain_two, d_two)
     after_grad = cotangent.astype(F32) + back_two
     branch = gather_x(after_grad.astype(BF16))

time: 486 us -> 477 us (0.981)
  waiting for transfers between devices: 154 us -> 143 us
    ppermute x3 -> x2, waiting for transfers between devices: 15.6 us -> 3.39 us  [scatter_x(): from_prev = lax.ppermute(q1, 'x', shift(4, 1))]
    ppermute x3, waiting for transfers between devices: 21.3 us -> 28.5 us  [sum_tail(): got = [tie(lax.ppermute(g[s], 'y', shift(4, s)), before) for s in (2, 1, 3)]]
    ppermute x6 -> x8, waiting for transfers between devices: 22.3 us -> 16.4 us  [the longest x3 16.4 us: relay(): got_a = lax.ppermute(p2a, 'x', shift(4, 1))]
    ppermute x6 -> x8, starting transfers between devices: 8.14 us -> 11.2 us  [the longest x3 8.35 us: relay(): got_b = lax.ppermute(p2b, 'x', shift(4, -1))]
    pallas_call x4 -> x5, Pallas kernels: 28.9 us -> 31.8 us  [the longest x1 14.6 us: gate_up_grads(): pl.pallas_call(gate_up_grads_body, grid=(16 // QS,), out_shape=sds((2, 16...]
    unnamed x110 -> x102, local copies, waits for them, and re-layouts: 12.7 us -> 11.8 us
  transfers between devices with their start and end apart: 61 -> 61, of which waited for: 26 -> 25; matrix products, arithmetic and copies ran while one was open for 5% -> 5% of each run, Pallas kernels for 21% -> 23%
where the time goes in v8:
time: 477 us; the launch traced here: 473 us
  Pallas kernels  158 us (33%)
  waiting for transfers between devices  143 us (30%)
  starting transfers between devices  117 us (25%)
  local copies, waits for them, and re-layouts  20.4 us (4%)
  other arithmetic  20.1 us (4%)
  between operations  14.6 us (3%)
    ppermute x3, waiting for transfers between devices, sum_tail(): got = [tie(lax.ppermute(g[s], 'y', shift(4, s)), before) for s in (2, 1, 3)]  28.5 us
    ppermute x4, starting transfers between devices, sum_tail(): theirs = [lax.ppermute(v, 'core', shift(2, 1)) for v in mine]  24.4 us
    pallas_call x1, Pallas kernels, ffn(): pl.pallas_call(ffn_body, grid=(TILES,), out_shape=(sds((ROWS, FF4)),) * 3...  20.9 us
    pallas_call x1, Pallas kernels, attend_back(): pl.pallas_call(attend_back_body, out_shape=(sds((4, BLK, AW)), sds((ROWS,...  20.4 us
    ppermute x4, waiting for transfers between devices, gather_x(): from_prev = lax.ppermute(v, 'x', shift(4, 1))  17.8 us
    ppermute x4, waiting for transfers between devices, gather_x(): from_next = lax.ppermute(v, 'x', shift(4, -1))  17.6 us
    ppermute x3, waiting for transfers between devices, relay(): got_a = lax.ppermute(p2a, 'x', shift(4, 1))  16.4 us
    pallas_call x1, Pallas kernels, ffn_back(): pl.pallas_call(ffn_back_body, grid_spec=pltpu.PrefetchScalarGridSpec(num_...  15.4 us
  transfers between devices with their start and end apart: 61, of which 25 were waited for; matrix products, arithmetic and copies ran while one was open for 5% of the time, Pallas kernels for 23%

profile of v8, /device:TPU:1, one launch (start us, length us, event | category | flops | bytes accessed | tf_op | source)
XLA Modules:
  0.0 473.1 jit_solution(16624739311184267462)
XLA Ops:
  10.0 3.4 collective-permute-start.2
  14.3 3.6 collective-permute-start
  21.7 5.1 %collective-permute-done.2.n1.refs_1_.refs_6_ = bf16[160,2048]{1,0:T(8,128)(2,1)S(1)} collective-permute-done((bf16[160,2048]{1,0:T(8,128)(2,1)S(1)}, bf16[160,2048]{1,0:T(8,128)(2,1)S(1)}, u32[]{:S(2)}, u32[]{:S(2)}) %collective-permute-start.2) | collective-permute-done | bytes 655392 | tf_op jit(solution)/shard_map/ppermute | solution.py:71
  26.8 3.2 collective-permute-done.1.n3.refs_4_.refs_9_
  34.5 4.2 collective-permute-done.3.n2a.refs_2_.refs_7_
  41.2 3.2 collective-permute-start.6
  45.3 3.5 collective-permute-start.5
  52.4 6.8 %qkv_forward.1 = (bf16[4,1280,128]{2,1,0:T(8,128)(2,1)}, bf16[640,128]{1,0:T(8,128)(2,1)}) custom-call(s32[4]{0:T(128)} %pad_add_fusion.idx, bf16[160,2048]{1,0:T(8,128)(2,1)} %copy-done.5, bf16[160,2048]{1,0:T(8,128)(2,1)} %copy-done.10, bf16[80,2048]{1,0:T(8,128)(2,1)} %copy-done.24, bf16[80,2048]{1,0:T(8,128)(2,1)} %collective-permute-done.4.n2b.refs_3_.refs_8_, ...), custom_call_target="tpu_custom_call" | custom-call | flops 1677721600 | bytes 7000000 | tf_op jit(solution)/shard_map/qkv_forward/pallas_call | solution.py:173
  61.4 2.8 collective-permute-start.13
  64.2 3.0 collective-permute-start.12
  68.1 6.1 %collective-permute-done.11.c2a.refs_2_ = bf16[80,2048]{1,0:T(8,128)(2,1)S(1)} collective-permute-done((bf16[80,2048]{1,0:T(8,128)(2,1)S(1)}, bf16[80,2048]{1,0:T(8,128)(2,1)S(1)}, u32[]{:S(2)}, u32[]{:S(2)}) %collective-permute-start.11) | collective-permute-done | bytes 327712 | tf_op jit(solution)/shard_map/ppermute | solution.py:74
  76.2 8.7 %attend.1 = (bf16[4,160,512]{2,1,0:T(8,128)(2,1)}, bf16[4,1280,128]{2,1,0:T(8,128)(2,1)}) custom-call(s32[4]{0:T(128)} %pad_add_fusion.idx, bf16[4,1280,128]{2,1,0:T(8,128)(2,1)} %get-tuple-element.106.q, bf16[640,128]{1,0:T(8,128)(2,1)} %get-tuple-element.107.kv_own, bf16[640,128]{1,0:T(8,128)(2,1)} %copy-done.50, s32[1,1280]{1,0:T(1,128)} %reshape_tile.3.first), custom_call_target="tpu_custom_call" | custom-call | flops 12000000000 | bytes 3000000 | tf_op jit(solution)/shard_map/attend/pallas_call | solution.py:266
  91.9 4.8 %out_project.1 = (bf16[160,2048]{1,0:T(8,128)(2,1)}, bf16[160,2048]{1,0:T(8,128)(2,1)}, bf16[80,2048]{1,0:T(8,128)(2,1)}, bf16[80,2048]{1,0:T(8,128)(2,1)}, bf16[160,2048]{1,0:T(8,128)(2,1)}) custom-call(s32[4]{0:T(128)} %pad_add_fusion.idx, bf16[4,160,512]{2,1,0:T(8,128)(2,1)} %get-tuple-element.144.att, bf16[256,2048]{1,0:T(8,128)(2,1)} %w0.10, ...), custom_call_target="tpu_custom_call" | custom-call | flops 1342177280 | bytes 5500000 | tf_op jit(solution)/shard_map/out_project/pallas_call | solution.py:303
  96.7 3.0 collective-permute-start.16
  99.7 8.1 %collective-permute-done.15.got_a = bf16[80,2048]{1,0:T(8,128)(2,1)S(1)} collective-permute-done((bf16[80,2048]{1,0:T(8,128)(2,1)}, bf16[80,2048]{1,0:T(8,128)(2,1)S(1)}, u32[]{:S(2)}, u32[]{:S(2)}) %collective-permute-start.15) | collective-permute-done | bytes 327712 | tf_op jit(solution)/shard_map/ppermute | solution.py:88
  108.7 2.7 relay.3
  114.2 11.3 %collective-permute-done.8.w1 = bf16[352,2048]{1,0:T(8,128)(2,1)} collective-permute-done((bf16[352,2048]{1,0:T(8,128)(2,1)S(1)}, bf16[352,2048]{1,0:T(8,128)(2,1)}, u32[]{:S(2)}, u32[]{:S(2)}) %collective-permute-start.8) | collective-permute-done | bytes 1441824 | tf_op jit(solution)/shard_map/ppermute | solution.py:132
  125.5 2.9 collective-permute-done.17
  132.0 13.2 %collective-permute-done.20.n3.refs_4_.refs_9_ = bf16[160,2048]{1,0:T(8,128)(2,1)S(1)} collective-permute-done((bf16[160,2048]{1,0:T(8,128)(2,1)S(1)}, bf16[160,2048]{1,0:T(8,128)(2,1)S(1)}, u32[]{:S(2)}, u32[]{:S(2)}) %collective-permute-start.20) | collective-permute-done | bytes 655392 | tf_op jit(solution)/shard_map/ppermute | solution.py:70
  145.2 13.5 %collective-permute-start.23 = (bf16[352,2048]{1,0:T(8,128)(2,1)}, bf16[352,2048]{1,0:T(8,128)(2,1)}, u32[]{:S(2)}, u32[]{:S(2)}) collective-permute-start(bf16[352,2048]{1,0:T(8,128)(2,1)} %collective-permute-done.8.w1), channel_id=1, source_target_pairs={{0,8},{8,0},{1,9},{9,1},{2,10},{10,2},{3,11},{11,3},{4,12},{12,4},... | collective-permute-start | bytes 4325384 | tf_op jit(solution)/shard_map/ppermute | solution.py:878
  161.2 7.1 %collective-permute-done.22.n2b.refs_3_.refs_8_ = bf16[80,2048]{1,0:T(8,128)(2,1)} collective-permute-done((bf16[80,2048]{1,0:T(8,128)(2,1)S(1)}, bf16[80,2048]{1,0:T(8,128)(2,1)}, u32[]{:S(2)}, u32[]{:S(2)}) %collective-permute-start.22) | collective-permute-done | bytes 327712 | tf_op jit(solution)/shard_map/ppermute | solution.py:75
  168.3 3.2 collective-permute-done.21.n2a.refs_2_.refs_7_
  171.5 20.9 %ffn.1 = (bf16[640,1408]{1,0:T(8,128)(2,1)}, bf16[640,1408]{1,0:T(8,128)(2,1)}, bf16[640,1408]{1,0:T(8,128)(2,1)}) custom-call(s32[4]{0:T(128)} %pad_add_fusion.idx, bf16[160,2048]{1,0:T(8,128)(2,1)} %copy-done.1, bf16[160,2048]{1,0:T(8,128)(2,1)} %copy-done.3, bf16[80,2048]{1,0:T(8,128)(2,1)} %collective-permute-done.21.n2a.refs_2_.refs_7_, ...), custom_call_target="tpu_custom_call" | custom-call | flops 11072962560 | bytes 34000000 | tf_op jit(solution)/shard_map/ffn/pallas_call | solution.py:501
  192.4 15.4 %ffn_back.1 = (bf16[160,2048]{1,0:T(8,128)(2,1)}, bf16[160,2048]{1,0:T(8,128)(2,1)}, bf16[80,2048]{1,0:T(8,128)(2,1)}, bf16[80,2048]{1,0:T(8,128)(2,1)}, bf16[160,2048]{1,0:T(8,128)(2,1)}) custom-call(s32[4]{0:T(128)} %pad_add_fusion.idx, bf16[640,1408]{1,0:T(8,128)(2,1)} %get-tuple-element.172.dgate.refs_10_, ...), custom_call_target="tpu_custom_call" | custom-call | flops 7381975040 | bytes 18000000 | tf_op jit(solution)/shard_map/ffn_back/pallas_call | solution.py:566
  210.6 9.2 %down_grads.1.refs_12_ = bf16[2,16,2112,128]{3,2,1,0:T(8,128)(2,1)} custom-call(bf16[160,2048]{1,0:T(8,128)(2,1)} %refs_0_, bf16[160,2048]{1,0:T(8,128)(2,1)} %copy-done.12, bf16[80,2048]{1,0:T(8,128)(2,1)} %copy-done.29, bf16[80,2048]{1,0:T(8,128)(2,1)} %copy-done.30, bf16[160,2048]{1,0:T(8,128)(2,1)} %copy-done.13, ...), custom_call_target="tpu_custom_call" | custom-call | flops 3690987520 | bytes 10000000 | tf_op jit(solution)/shard_map/down_grads/pallas_call | solution.py:633
  223.2 2.7 collective-permute-start.27
  225.9 14.6 %gate_up_grads.1 = bf16[2,16,2112,128]{3,2,1,0:T(8,128)(2,1)} custom-call(bf16[160,2048]{1,0:T(8,128)(2,1)} %copy-done.1, bf16[160,2048]{1,0:T(8,128)(2,1)} %copy-done.3, bf16[80,2048]{1,0:T(8,128)(2,1)} %collective-permute-done.21.n2a.refs_2_.refs_7_, bf16[80,2048]{1,0:T(8,128)(2,1)} %collective-permute-done.22.n2b.refs_3_.refs_8_, ...), custom_call_target="tpu_custom_call", output_to_operand_aliasing={{}: (12, {})} | custom-call | flops 7381975040 | bytes 20000000 | tf_op jit(solution)/shard_map/gate_up_grads/pallas_call | solution.py:602
  244.0 2.8 fusion.10
  248.2 12.5 %collective-permute-done.29.b1.refs_11_ = bf16[160,2048]{1,0:T(8,128)(2,1)S(1)} collective-permute-done((bf16[160,2048]{1,0:T(8,128)(2,1)S(1)}, bf16[160,2048]{1,0:T(8,128)(2,1)S(1)}, u32[]{:S(2)}, u32[]{:S(2)}) %collective-permute-start.29) | collective-permute-done | bytes 655392 | tf_op jit(solution)/shard_map/ppermute | solution.py:71
  264.9 10.5 %down_project.1 = (bf16[160,2048]{1,0:T(8,128)(2,1)}, bf16[160,2048]{1,0:T(8,128)(2,1)}, bf16[160,2048]{1,0:T(8,128)(2,1)}, bf16[160,2048]{1,0:T(8,128)(2,1)}) custom-call(s32[4]{0:T(128)} %pad_add_fusion.idx, bf16[640,1408]{1,0:T(8,128)(2,1)} %get-tuple-element.173.hid.refs_5_, bf16[704,2048]{1,0:T(8,128)(2,1)} %w0.9, ...), custom_call_target="tpu_custom_call" | custom-call | flops 3690987520 | bytes 11000000 | tf_op jit(solution)/shard_map/down_project/pallas_call | solution.py:536
  275.6 3.0 collective-permute-start.33
  278.6 20.4 %attend_back.1 = (bf16[4,160,512]{2,1,0:T(8,128)(2,1)}, f32[640,128]{1,0:T(8,128)}, bf16[640,128]{1,0:T(8,128)(2,1)}) custom-call(s32[4]{0:T(128)} %pad_add_fusion.idx, bf16[4,1280,128]{2,1,0:T(8,128)(2,1)} %get-tuple-element.118.qx, bf16[640,128]{1,0:T(8,128)(2,1)} %get-tuple-element.107.kv_own, bf16[640,128]{1,0:T(8,128)(2,1)} %copy-done.50, ...), custom_call_target="tpu_custom_call" | custom-call | flops 30000001024 | bytes 8000000 | tf_op jit(solution)/shard_map/attend_back/pallas_call | solution.py:375
  300.9 9.0 %attn_grads.1 = (bf16[4,2,1024,128]{3,2,1,0:T(8,128)(2,1)}, bf16[4,2,1024,128]{3,2,1,0:T(8,128)(2,1)}) custom-call(s32[4]{0:T(128)} %pad_add_fusion.idx, bf16[160,2048]{1,0:T(8,128)(2,1)} %copy-done.5, bf16[160,2048]{1,0:T(8,128)(2,1)} %copy-done.10, bf16[80,2048]{1,0:T(8,128)(2,1)} %copy-done.24, ...), custom_call_target="tpu_custom_call" | custom-call | flops 2684354560 | bytes 10000000 | tf_op jit(solution)/shard_map/attn_grads/pallas_call | solution.py:713
  310.6 5.1 %collective-permute-start.40 = (bf16[4,2,1024,128]{3,2,1,0:T(8,128)(2,1)}, bf16[4,2,1024,128]{3,2,1,0:T(8,128)(2,1)S(1)}, u32[]{:S(2)}, u32[]{:S(2)}) collective-permute-start(bf16[4,2,1024,128]{3,2,1,0:T(8,128)(2,1)} %get-tuple-element.157), channel_id=1, source_target_pairs={{0,8},{8,0},{1,9},{9,1},{2,10},{10,2},{3,11},{11,3},{4,12},{12,4},... | collective-permute-start | bytes 6291464 | tf_op jit(solution)/shard_map/ppermute | solution.py:784
  315.7 7.5 %qkv_back.1 = (bf16[4,2,144,128]{3,2,1,0:T(8,128)(2,1)}, bf16[4,2,144,128]{3,2,1,0:T(8,128)(2,1)}, bf16[160,2048]{1,0:T(8,128)(2,1)}, bf16[160,2048]{1,0:T(8,128...) custom-call(s32[4]{0:T(128)} %pad_add_fusion.idx, ...), custom_call_target="tpu_custom_call" | custom-call | flops 1677721600 | bytes 13000000 | tf_op jit(solution)/shard_map/qkv_back/pallas_call | solution.py:432
  326.0 8.3 %collective-permute-done.35.got_a = bf16[80,2048]{1,0:T(8,128)(2,1)} collective-permute-done((bf16[80,2048]{1,0:T(8,128)(2,1)}, bf16[80,2048]{1,0:T(8,128)(2,1)}, u32[]{:S(2)}, u32[]{:S(2)}) %collective-permute-start.35) | collective-permute-done | bytes 327712 | tf_op jit(solution)/shard_map/ppermute | solution.py:88
  337.0 2.7 collective-permute-start.38
  344.4 3.9 sum_core.1
  356.0 14.4 %collective-permute-done.42.b = bf16[2,1168,128]{2,1,0:T(8,128)(2,1)} collective-permute-done((bf16[2,1168,128]{2,1,0:T(8,128)(2,1)}, bf16[2,1168,128]{2,1,0:T(8,128)(2,1)}, u32[]{:S(2)}, u32[]{:S(2)}) %collective-permute-start.42) | collective-permute-done | bytes 598048 | tf_op jit(solution)/shard_map/ppermute | solution.py:788
  370.5 14.1 %collective-permute-done.43.c = bf16[2,1168,128]{2,1,0:T(8,128)(2,1)} collective-permute-done((bf16[2,1168,128]{2,1,0:T(8,128)(2,1)}, bf16[2,1168,128]{2,1,0:T(8,128)(2,1)}, u32[]{:S(2)}, u32[]{:S(2)}) %collective-permute-start.43) | collective-permute-done | bytes 598048 | tf_op jit(solution)/shard_map/ppermute | solution.py:788
  390.8 12.3 %collective-permute-done.47.d = bf16[1168,128]{1,0:T(8,128)(2,1)S(1)} collective-permute-done((bf16[1168,128]{1,0:T(8,128)(2,1)}, bf16[1168,128]{1,0:T(8,128)(2,1)S(1)}, u32[]{:S(2)}, u32[]{:S(2)}) %collective-permute-start.47) | collective-permute-done | bytes 299040 | tf_op jit(solution)/shard_map/ppermute | solution.py:799
  403.1 6.1 %collective-permute-done.45.b = bf16[1168,128]{1,0:T(8,128)(2,1)} collective-permute-done((bf16[1168,128]{1,0:T(8,128)(2,1)}, bf16[1168,128]{1,0:T(8,128)(2,1)}, u32[]{:S(2)}, u32[]{:S(2)}) %collective-permute-start.45) | collective-permute-done | bytes 299040 | tf_op jit(solution)/shard_map/ppermute | solution.py:797
  415.0 5.2 %collective-permute-start.51 = (bf16[1168,128]{1,0:T(8,128)(2,1)}, bf16[1168,128]{1,0:T(8,128)(2,1)S(1)}, u32[]{:S(2)}, u32[]{:S(2)}) collective-permute-start(bf16[1168,128]{1,0:T(8,128)(2,1)} %sum_z.1.refs_0_), channel_id=1, source_target_pairs={{0,8},{8,0},{1,9},{9,1},{2,10},{10,2},{3,11},{11,3},{4,12},{12,4},... | collective-permute-start | bytes 897032 | tf_op jit(solution)/shard_map/ppermute | solution.py:803
  420.6 11.1 %collective-permute-start.54 = (bf16[1168,128]{1,0:T(8,128)(2,1)S(1)}, bf16[1168,128]{1,0:T(8,128)(2,1)S(1)}, u32[]{:S(2)}, u32[]{:S(2)}) collective-permute-start(bf16[1168,128]{1,0:T(8,128)(2,1)S(1)} %collective-permute-done.50.refs_3_), channel_id=1, source_target_pairs={{0,8},{8,0},{1,9},{9,1},{2,10},{10,2},{3,11},{11,3},{4,12},{12,4},... | collective-permute-start | bytes 897032 | tf_op jit(solution)/shard_map/ppermute | solution.py:803
  431.7 2.8 collective-permute-start.53
  436.9 5.4 %collective-permute-start.52 = (bf16[1168,128]{1,0:T(8,128)(2,1)S(1)}, bf16[1168,128]{1,0:T(8,128)(2,1)}, u32[]{:S(2)}, u32[]{:S(2)}) collective-permute-start(bf16[1168,128]{1,0:T(8,128)(2,1)S(1)} %collective-permute-done.48.refs_1_), channel_id=1, source_target_pairs={{0,8},{8,0},{1,9},{9,1},{2,10},{10,2},{3,11},{11,3},{4,12},{12,4},... | collective-permute-start | bytes 897032 | tf_op jit(solution)/shard_map/ppermute | solution.py:803
  446.5 4.2 unpack_tail.1
  456.6 9.8 %unpack.1 = (f32[1024,1408]{1,0:T(8,128)}, f32[1024,1408]{1,0:T(8,128)}, f32[704,2048]{1,0:T(8,128)}) custom-call(bf16[16,2112,128]{2,1,0:T(8,128)(2,1)} %all-gather.5.cloned.1.call-done.piece), custom_call_target="tpu_custom_call" | custom-call | flops 1000000 | bytes 26000000 | tf_op jit(solution)/shard_map/unpack/pallas_call | solution.py:658
  (247 shorter events, 101.3 us)
Async XLA Ops:
  7.2 164.3 %all-gather.3.cloned.1.call-start = ((), (), s32[]{:S(2)}) async-start(), calls=%async_computation.1 | async-start | bytes 6782976 | tf_op jit(solution)/shard_map/all_gather | solution.py:872
  10.0 16.8 %collective-permute-start.2 = (bf16[160,2048]{1,0:T(8,128)(2,1)S(1)}, bf16[160,2048]{1,0:T(8,128)(2,1)S(1)}, u32[]{:S(2)}, u32[]{:S(2)}) collective-permute-start(bf16[160,2048]{1,0:T(8,128)(2,1)S(1)} %multiply_convert_fusion.1.n0.refs_0_.refs_5_), channel_id=1, source_target_pairs={{0,6},{2,0},{4,2},{6,4},{1,7},{3,1},{5,3},{7,5},{8,14},{10,8},{12,... | collective-permute-start | bytes 1966088 | tf_op jit(solution)/shard_map/ppermute | solution.py:71
  13.4 16.6 %collective-permute-start.1 = (bf16[160,2048]{1,0:T(8,128)(2,1)S(1)}, bf16[160,2048]{1,0:T(8,128)(2,1)S(1)}, u32[]{:S(2)}, u32[]{:S(2)}) collective-permute-start(bf16[160,2048]{1,0:T(8,128)(2,1)S(1)} %multiply_convert_fusion.1.n0.refs_0_.refs_5_), channel_id=1, source_target_pairs={{0,2},{2,4},{4,6},{6,0},{1,3},{3,5},{5,7},{7,1},{8,10},{10,12},{12... | collective-permute-start | bytes 1966088 | tf_op jit(solution)/shard_map/ppermute | solution.py:70
  14.3 27.0 %collective-permute-start = (bf16[512,640]{1,0:T(8,128)(2,1)}, bf16[512,640]{1,0:T(8,128)(2,1)}, u32[]{:S(2)}, u32[]{:S(2)}) collective-permute-start(bf16[512,640]{1,0:T(8,128)(2,1)} %constant_dynamic-slice_fusion.4), channel_id=1, source_target_pairs={{0,1},{1,0},{2,3},{3,2},{4,5},{5,4},{6,7},{7,6},{8,9},{9,8},{10,11... | collective-permute-start | bytes 1966088 | tf_op jit(solution)/shard_map/ppermute | solution.py:132
  39.5 19.7 %collective-permute-start.10 = (bf16[160,2048]{1,0:T(8,128)(2,1)S(1)}, bf16[160,2048]{1,0:T(8,128)(2,1)S(1)}, u32[]{:S(2)}, u32[]{:S(2)}) collective-permute-start(bf16[160,2048]{1,0:T(8,128)(2,1)S(1)} %copy-done.7), channel_id=1, source_target_pairs={{0,6},{2,0},{4,2},{6,4},{1,7},{3,1},{5,3},{7,5},{8,14},{10,8},{12,... | collective-permute-start | bytes 1966088 | tf_op jit(solution)/shard_map/ppermute | solution.py:71
  41.2 17.9 %collective-permute-start.9 = (bf16[160,2048]{1,0:T(8,128)(2,1)S(1)}, bf16[160,2048]{1,0:T(8,128)(2,1)S(1)}, u32[]{:S(2)}, u32[]{:S(2)}) collective-permute-start(bf16[160,2048]{1,0:T(8,128)(2,1)S(1)} %copy-done.7), channel_id=1, source_target_pairs={{0,2},{2,4},{4,6},{6,0},{1,3},{3,5},{5,7},{7,1},{8,10},{10,12},{12... | collective-permute-start | bytes 1966088 | tf_op jit(solution)/shard_map/ppermute | solution.py:70
  41.2 11.1 %collective-permute-start.6 = (bf16[512,640]{1,0:T(8,128)(2,1)}, bf16[512,640]{1,0:T(8,128)(2,1)}, u32[]{:S(2)}, u32[]{:S(2)}) collective-permute-start(bf16[512,640]{1,0:T(8,128)(2,1)} %collective-permute-done.w1), channel_id=1, source_target_pairs={{0,8},{8,0},{1,9},{9,1},{2,10},{10,2},{3,11},{11,3},{4,12},{12,4},... | collective-permute-start | bytes 1966088 | tf_op jit(solution)/shard_map/ppermute | solution.py:840
  45.3 16.1 %collective-permute-start.5 = (bf16[128,2048]{1,0:T(8,128)(2,1)}, bf16[128,2048]{1,0:T(8,128)(2,1)}, u32[]{:S(2)}, u32[]{:S(2)}) collective-permute-start(bf16[128,2048]{1,0:T(8,128)(2,1)} %constant_dynamic-slice_fusion.3), channel_id=1, source_target_pairs={{0,1},{1,0},{2,3},{3,2},{4,5},{5,4},{6,7},{7,6},{8,9},{9,8},{10,11... | collective-permute-start | bytes 1572872 | tf_op jit(solution)/shard_map/ppermute | solution.py:132
  61.4 14.2 %collective-permute-start.13 = (bf16[640,128]{1,0:T(8,128)(2,1)S(1)}, bf16[640,128]{1,0:T(8,128)(2,1)S(1)}, u32[]{:S(2)}, u32[]{:S(2)}) collective-permute-start(bf16[640,128]{1,0:T(8,128)(2,1)S(1)} %copy-done.49), channel_id=1, source_target_pairs={{0,1},{1,0},{2,3},{3,2},{4,5},{5,4},{6,7},{7,6},{8,9},{9,8},{10,11... | collective-permute-start | bytes 491528 | tf_op jit(solution)/shard_map/ppermute | solution.py:869
  67.3 18.5 %collective-permute-start.7 = (bf16[128,2944]{1,0:T(8,128)(2,1)S(1)}, bf16[128,2944]{1,0:T(8,128)(2,1)S(1)}, u32[]{:S(2)}, u32[]{:S(2)}) collective-permute-start(bf16[128,2944]{1,0:T(8,128)(2,1)S(1)} %pad_maximum_fusion), channel_id=1, source_target_pairs={{0,17},{1,16},{16,1},{17,0},{2,19},{3,18},{18,3},{19,2},{4,21},{5,... | collective-permute-start | bytes 2261000 | tf_op jit(solution)/shard_map/ppermute | solution.py:857
  86.7 300.5 %reduce-scatter.2.cloned.1.call-start = ((), (), s32[]{:S(2)}) async-start(), calls=%async_computation.2 | async-start | bytes 17842176 | tf_op jit(solution)/shard_map/reduce_scatter | solution.py:886
  90.6 34.9 %collective-permute-start.8 = (bf16[352,2048]{1,0:T(8,128)(2,1)S(1)}, bf16[352,2048]{1,0:T(8,128)(2,1)}, u32[]{:S(2)}, u32[]{:S(2)}) collective-permute-start(bf16[352,2048]{1,0:T(8,128)(2,1)S(1)} %constant_dynamic-slice_fusion.1), channel_id=1, source_target_pairs={{0,1},{1,0},{2,3},{3,2},{4,5},{5,4},{6,7},{7,6},{8,9},{9,8},{10,11... | collective-permute-start | bytes 4325384 | tf_op jit(solution)/shard_map/ppermute | solution.py:132
  96.7 11.1 %collective-permute-start.15 = (bf16[80,2048]{1,0:T(8,128)(2,1)}, bf16[80,2048]{1,0:T(8,128)(2,1)S(1)}, u32[]{:S(2)}, u32[]{:S(2)}) collective-permute-start(bf16[80,2048]{1,0:T(8,128)(2,1)} %get-tuple-element.111), channel_id=1, source_target_pairs={{0,2},{2,4},{4,6},{6,0},{1,3},{3,5},{5,7},{7,1},{8,10},{10,12},{12... | collective-permute-start | bytes 983048 | tf_op jit(solution)/shard_map/ppermute | solution.py:88
  96.7 11.1 %collective-permute-start.16 = (bf16[80,2048]{1,0:T(8,128)(2,1)}, bf16[80,2048]{1,0:T(8,128)(2,1)S(1)}, u32[]{:S(2)}, u32[]{:S(2)}) collective-permute-start(bf16[80,2048]{1,0:T(8,128)(2,1)} %get-tuple-element.113), channel_id=1, source_target_pairs={{0,6},{2,0},{4,2},{6,4},{1,7},{3,1},{5,3},{7,5},{8,14},{10,8},{12,... | collective-permute-start | bytes 983048 | tf_op jit(solution)/shard_map/ppermute | solution.py:89
  111.4 17.0 %collective-permute-start.17 = (bf16[160,2048]{1,0:T(8,128)(2,1)}, bf16[160,2048]{1,0:T(8,128)(2,1)S(1)}, u32[]{:S(2)}, u32[]{:S(2)}) collective-permute-start(bf16[160,2048]{1,0:T(8,128)(2,1)} %get-tuple-element.114), channel_id=1, source_target_pairs={{0,2},{2,4},{4,6},{6,0},{1,3},{3,5},{5,7},{7,1},{8,10},{10,12},{12... | collective-permute-start | bytes 1966088 | tf_op jit(solution)/shard_map/ppermute | solution.py:104
  111.9 16.5 %collective-permute-start.18 = (bf16[160,2048]{1,0:T(8,128)(2,1)}, bf16[160,2048]{1,0:T(8,128)(2,1)S(1)}, u32[]{:S(2)}, u32[]{:S(2)}) collective-permute-start(bf16[160,2048]{1,0:T(8,128)(2,1)} %get-tuple-element.115), channel_id=1, source_target_pairs={{0,6},{2,0},{4,2},{6,4},{1,7},{3,1},{5,3},{7,5},{8,14},{10,8},{12,... | collective-permute-start | bytes 1966088 | tf_op jit(solution)/shard_map/ppermute | solution.py:105
  129.3 15.9 %collective-permute-start.20 = (bf16[160,2048]{1,0:T(8,128)(2,1)S(1)}, bf16[160,2048]{1,0:T(8,128)(2,1)S(1)}, u32[]{:S(2)}, u32[]{:S(2)}) collective-permute-start(bf16[160,2048]{1,0:T(8,128)(2,1)S(1)} %multiply_convert_fusion.n0.refs_0_.refs_5_), channel_id=1, source_target_pairs={{0,2},{2,4},{4,6},{6,0},{1,3},{3,5},{5,7},{7,1},{8,10},{10,12},{12... | collective-permute-start | bytes 1966088 | tf_op jit(solution)/shard_map/ppermute | solution.py:70
  129.4 15.8 %collective-permute-start.19 = (bf16[160,2048]{1,0:T(8,128)(2,1)S(1)}, bf16[160,2048]{1,0:T(8,128)(2,1)S(1)}, u32[]{:S(2)}, u32[]{:S(2)}) collective-permute-start(bf16[160,2048]{1,0:T(8,128)(2,1)S(1)} %multiply_convert_fusion.n0.refs_0_.refs_5_), channel_id=1, source_target_pairs={{0,6},{2,0},{4,2},{6,4},{1,7},{3,1},{5,3},{7,5},{8,14},{10,8},{12,... | collective-permute-start | bytes 1966088 | tf_op jit(solution)/shard_map/ppermute | solution.py:71
  145.2 26.3 %collective-permute-start.23 = (bf16[352,2048]{1,0:T(8,128)(2,1)}, bf16[352,2048]{1,0:T(8,128)(2,1)}, u32[]{:S(2)}, u32[]{:S(2)}) collective-permute-start(bf16[352,2048]{1,0:T(8,128)(2,1)} %collective-permute-done.8.w1), channel_id=1, source_target_pairs={{0,8},{8,0},{1,9},{9,1},{2,10},{10,2},{3,11},{11,3},{4,12},{12,4},... | collective-permute-start | bytes 4325384 | tf_op jit(solution)/shard_map/ppermute | solution.py:878
  207.9 11.9 %collective-permute-start.24 = (bf16[80,2048]{1,0:T(8,128)(2,1)}, bf16[80,2048]{1,0:T(8,128)(2,1)S(1)}, u32[]{:S(2)}, u32[]{:S(2)}) collective-permute-start(bf16[80,2048]{1,0:T(8,128)(2,1)} %get-tuple-element.126), channel_id=1, source_target_pairs={{0,2},{2,4},{4,6},{6,0},{1,3},{3,5},{5,7},{7,1},{8,10},{10,12},{12... | collective-permute-start | bytes 983048 | tf_op jit(solution)/shard_map/ppermute | solution.py:88
  207.9 11.8 %collective-permute-start.25 = (bf16[80,2048]{1,0:T(8,128)(2,1)}, bf16[80,2048]{1,0:T(8,128)(2,1)S(1)}, u32[]{:S(2)}, u32[]{:S(2)}) collective-permute-start(bf16[80,2048]{1,0:T(8,128)(2,1)} %get-tuple-element.128), channel_id=1, source_target_pairs={{0,6},{2,0},{4,2},{6,4},{1,7},{3,1},{5,3},{7,5},{8,14},{10,8},{12,... | collective-permute-start | bytes 983048 | tf_op jit(solution)/shard_map/ppermute | solution.py:89
  223.2 17.3 %collective-permute-start.26 = (bf16[160,2048]{1,0:T(8,128)(2,1)}, bf16[160,2048]{1,0:T(8,128)(2,1)S(1)}, u32[]{:S(2)}, u32[]{:S(2)}) collective-permute-start(bf16[160,2048]{1,0:T(8,128)(2,1)} %get-tuple-element.129), channel_id=1, source_target_pairs={{0,2},{2,4},{4,6},{6,0},{1,3},{3,5},{5,7},{7,1},{8,10},{10,12},{12... | collective-permute-start | bytes 1966088 | tf_op jit(solution)/shard_map/ppermute | solution.py:884
  223.2 17.3 %collective-permute-start.27 = (bf16[160,2048]{1,0:T(8,128)(2,1)}, bf16[160,2048]{1,0:T(8,128)(2,1)}, u32[]{:S(2)}, u32[]{:S(2)}) collective-permute-start(bf16[160,2048]{1,0:T(8,128)(2,1)} %get-tuple-element.130), channel_id=1, source_target_pairs={{0,6},{2,0},{4,2},{6,4},{1,7},{3,1},{5,3},{7,5},{8,14},{10,8},{12,... | collective-permute-start | bytes 1966088 | tf_op jit(solution)/shard_map/ppermute | solution.py:885
  240.6 216.0 %all-gather.5.cloned.1.call-start = ((), (), s32[]{:S(2)}) async-start(), calls=%async_computation.3 | async-start | bytes 9191424 | tf_op jit(solution)/shard_map/all_gather | solution.py:920
  246.7 14.0 %collective-permute-start.29 = (bf16[160,2048]{1,0:T(8,128)(2,1)S(1)}, bf16[160,2048]{1,0:T(8,128)(2,1)S(1)}, u32[]{:S(2)}, u32[]{:S(2)}) collective-permute-start(bf16[160,2048]{1,0:T(8,128)(2,1)S(1)} %get-tuple-element.183.b0.refs_10_), channel_id=1, source_target_pairs={{0,6},{2,0},{4,2},{6,4},{1,7},{3,1},{5,3},{7,5},{8,14},{10,8},{12,... | collective-permute-start | bytes 1966088 | tf_op jit(solution)/shard_map/ppermute | solution.py:71
  247.9 14.3 %collective-permute-start.28 = (bf16[160,2048]{1,0:T(8,128)(2,1)S(1)}, bf16[160,2048]{1,0:T(8,128)(2,1)S(1)}, u32[]{:S(2)}, u32[]{:S(2)}) collective-permute-start(bf16[160,2048]{1,0:T(8,128)(2,1)S(1)} %get-tuple-element.183.b0.refs_10_), channel_id=1, source_target_pairs={{0,2},{2,4},{4,6},{6,0},{1,3},{3,5},{5,7},{7,1},{8,10},{10,12},{12... | collective-permute-start | bytes 1966088 | tf_op jit(solution)/shard_map/ppermute | solution.py:70
  262.2 13.3 %collective-permute-start.30 = (bf16[80,2048]{1,0:T(8,128)(2,1)S(1)}, bf16[80,2048]{1,0:T(8,128)(2,1)}, u32[]{:S(2)}, u32[]{:S(2)}) collective-permute-start(bf16[80,2048]{1,0:T(8,128)(2,1)S(1)} %slice.51), channel_id=1, source_target_pairs={{0,2},{2,4},{4,6},{6,0},{1,3},{3,5},{5,7},{7,1},{8,10},{10,12},{12... | collective-permute-start | bytes 983048 | tf_op jit(solution)/shard_map/ppermute | solution.py:74
  262.3 13.2 %collective-permute-start.31 = (bf16[80,2048]{1,0:T(8,128)(2,1)S(1)}, bf16[80,2048]{1,0:T(8,128)(2,1)}, u32[]{:S(2)}, u32[]{:S(2)}) collective-permute-start(bf16[80,2048]{1,0:T(8,128)(2,1)S(1)} %slice.52), channel_id=1, source_target_pairs={{0,6},{2,0},{4,2},{6,4},{1,7},{3,1},{5,3},{7,5},{8,14},{10,8},{12,... | collective-permute-start | bytes 983048 | tf_op jit(solution)/shard_map/ppermute | solution.py:75
  275.5 25.3 %collective-permute-start.32 = (bf16[160,2048]{1,0:T(8,128)(2,1)}, bf16[160,2048]{1,0:T(8,128)(2,1)S(1)}, u32[]{:S(2)}, u32[]{:S(2)}) collective-permute-start(bf16[160,2048]{1,0:T(8,128)(2,1)} %get-tuple-element.136), channel_id=1, source_target_pairs={{0,2},{2,4},{4,6},{6,0},{1,3},{3,5},{5,7},{7,1},{8,10},{10,12},{12... | collective-permute-start | bytes 1966088 | tf_op jit(solution)/shard_map/ppermute | solution.py:897
  275.6 25.3 %collective-permute-start.33 = (bf16[160,2048]{1,0:T(8,128)(2,1)}, bf16[160,2048]{1,0:T(8,128)(2,1)S(1)}, u32[]{:S(2)}, u32[]{:S(2)}) collective-permute-start(bf16[160,2048]{1,0:T(8,128)(2,1)} %get-tuple-element.138), channel_id=1, source_target_pairs={{0,6},{2,0},{4,2},{6,4},{1,7},{3,1},{5,3},{7,5},{8,14},{10,8},{12,... | collective-permute-start | bytes 1966088 | tf_op jit(solution)/shard_map/ppermute | solution.py:897
  299.0 10.9 %collective-permute-start.34 = (bf16[640,128]{1,0:T(8,128)(2,1)}, bf16[640,128]{1,0:T(8,128)(2,1)S(1)}, u32[]{:S(2)}, u32[]{:S(2)}) collective-permute-start(bf16[640,128]{1,0:T(8,128)(2,1)} %get-tuple-element.143), channel_id=1, source_target_pairs={{0,1},{1,0},{2,3},{3,2},{4,5},{5,4},{6,7},{7,6},{8,9},{9,8},{10,11... | collective-permute-start | bytes 491528 | tf_op jit(solution)/shard_map/ppermute | solution.py:902
  310.6 31.8 %collective-permute-start.40 = (bf16[4,2,1024,128]{3,2,1,0:T(8,128)(2,1)}, bf16[4,2,1024,128]{3,2,1,0:T(8,128)(2,1)S(1)}, u32[]{:S(2)}, u32[]{:S(2)}) collective-permute-start(bf16[4,2,1024,128]{3,2,1,0:T(8,128)(2,1)} %get-tuple-element.157), channel_id=1, source_target_pairs={{0,8},{8,0},{1,9},{9,1},{2,10},{10,2},{3,11},{11,3},{4,12},{12,4},... | collective-permute-start | bytes 6291464 | tf_op jit(solution)/shard_map/ppermute | solution.py:784
  323.3 11.1 %collective-permute-start.35 = (bf16[80,2048]{1,0:T(8,128)(2,1)}, bf16[80,2048]{1,0:T(8,128)(2,1)}, u32[]{:S(2)}, u32[]{:S(2)}) collective-permute-start(bf16[80,2048]{1,0:T(8,128)(2,1)} %get-tuple-element.149), channel_id=1, source_target_pairs={{0,2},{2,4},{4,6},{6,0},{1,3},{3,5},{5,7},{7,1},{8,10},{10,12},{12... | collective-permute-start | bytes 983048 | tf_op jit(solution)/shard_map/ppermute | solution.py:88
  323.4 11.0 %collective-permute-start.36 = (bf16[80,2048]{1,0:T(8,128)(2,1)}, bf16[80,2048]{1,0:T(8,128)(2,1)}, u32[]{:S(2)}, u32[]{:S(2)}) collective-permute-start(bf16[80,2048]{1,0:T(8,128)(2,1)} %get-tuple-element.151), channel_id=1, source_target_pairs={{0,6},{2,0},{4,2},{6,4},{1,7},{3,1},{5,3},{7,5},{8,14},{10,8},{12,... | collective-permute-start | bytes 983048 | tf_op jit(solution)/shard_map/ppermute | solution.py:89
  337.0 17.1 %collective-permute-start.37 = (bf16[160,2048]{1,0:T(8,128)(2,1)}, bf16[160,2048]{1,0:T(8,128)(2,1)}, u32[]{:S(2)}, u32[]{:S(2)}) collective-permute-start(bf16[160,2048]{1,0:T(8,128)(2,1)} %get-tuple-element.152), channel_id=1, source_target_pairs={{0,2},{2,4},{4,6},{6,0},{1,3},{3,5},{5,7},{7,1},{8,10},{10,12},{12... | collective-permute-start | bytes 1966088 | tf_op jit(solution)/shard_map/ppermute | solution.py:104
  337.0 17.1 %collective-permute-start.38 = (bf16[160,2048]{1,0:T(8,128)(2,1)}, bf16[160,2048]{1,0:T(8,128)(2,1)}, u32[]{:S(2)}, u32[]{:S(2)}) collective-permute-start(bf16[160,2048]{1,0:T(8,128)(2,1)} %get-tuple-element.153), channel_id=1, source_target_pairs={{0,6},{2,0},{4,2},{6,4},{1,7},{3,1},{5,3},{7,5},{8,14},{10,8},{12,... | collective-permute-start | bytes 1966088 | tf_op jit(solution)/shard_map/ppermute | solution.py:105
  348.3 22.2 %collective-permute-start.42 = (bf16[2,1168,128]{2,1,0:T(8,128)(2,1)}, bf16[2,1168,128]{2,1,0:T(8,128)(2,1)}, u32[]{:S(2)}, u32[]{:S(2)}) collective-permute-start(bf16[2,1168,128]{2,1,0:T(8,128)(2,1)} %get-tuple-element.161), channel_id=1, source_target_pairs={{0,64},{32,96},{64,0},{96,32},{1,65},{33,97},{65,1},{97,33},{2,66}... | collective-permute-start | bytes 1794056 | tf_op jit(solution)/shard_map/ppermute | solution.py:788
  350.9 33.7 %collective-permute-start.43 = (bf16[2,1168,128]{2,1,0:T(8,128)(2,1)}, bf16[2,1168,128]{2,1,0:T(8,128)(2,1)}, u32[]{:S(2)}, u32[]{:S(2)}) collective-permute-start(bf16[2,1168,128]{2,1,0:T(8,128)(2,1)} %get-tuple-element.163), channel_id=1, source_target_pairs={{0,32},{32,64},{64,96},{96,0},{1,33},{33,65},{65,97},{97,1},{2,34}... | collective-permute-start | bytes 1794056 | tf_op jit(solution)/shard_map/ppermute | solution.py:788
  351.5 33.1 %collective-permute-start.44 = (bf16[2,1168,128]{2,1,0:T(8,128)(2,1)}, bf16[2,1168,128]{2,1,0:T(8,128)(2,1)}, u32[]{:S(2)}, u32[]{:S(2)}) collective-permute-start(bf16[2,1168,128]{2,1,0:T(8,128)(2,1)} %get-tuple-element.165), channel_id=1, source_target_pairs={{0,96},{32,0},{64,32},{96,64},{1,97},{33,1},{65,33},{97,65},{2,98}... | collective-permute-start | bytes 1794056 | tf_op jit(solution)/shard_map/ppermute | solution.py:788
  387.2 15.9 %collective-permute-start.47 = (bf16[1168,128]{1,0:T(8,128)(2,1)}, bf16[1168,128]{1,0:T(8,128)(2,1)S(1)}, u32[]{:S(2)}, u32[]{:S(2)}) collective-permute-start(bf16[1168,128]{1,0:T(8,128)(2,1)} %get-tuple-element.168), channel_id=1, source_target_pairs={{0,17},{1,16},{16,1},{17,0},{2,19},{3,18},{18,3},{19,2},{4,21},{5,... | collective-permute-start | bytes 897032 | tf_op jit(solution)/shard_map/ppermute | solution.py:799
  389.7 13.4 %collective-permute-start.46 = (bf16[1168,128]{1,0:T(8,128)(2,1)}, bf16[1168,128]{1,0:T(8,128)(2,1)}, u32[]{:S(2)}, u32[]{:S(2)}) collective-permute-start(bf16[1168,128]{1,0:T(8,128)(2,1)} %get-tuple-element.168), channel_id=1, source_target_pairs={{0,1},{1,0},{2,3},{3,2},{4,5},{5,4},{6,7},{7,6},{8,9},{9,8},{10,11... | collective-permute-start | bytes 897032 | tf_op jit(solution)/shard_map/ppermute | solution.py:798
  390.1 19.1 %collective-permute-start.45 = (bf16[1168,128]{1,0:T(8,128)(2,1)}, bf16[1168,128]{1,0:T(8,128)(2,1)}, u32[]{:S(2)}, u32[]{:S(2)}) collective-permute-start(bf16[1168,128]{1,0:T(8,128)(2,1)} %get-tuple-element.167.a), channel_id=1, source_target_pairs={{0,16},{16,0},{1,17},{17,1},{2,18},{18,2},{3,19},{19,3},{4,20},{20... | collective-permute-start | bytes 897032 | tf_op jit(solution)/shard_map/ppermute | solution.py:797
  412.3 19.4 %collective-permute-start.49 = (bf16[1168,128]{1,0:T(8,128)(2,1)}, bf16[1168,128]{1,0:T(8,128)(2,1)S(1)}, u32[]{:S(2)}, u32[]{:S(2)}) collective-permute-start(bf16[1168,128]{1,0:T(8,128)(2,1)} %sum_z.1.refs_0_), channel_id=1, source_target_pairs={{0,64},{32,96},{64,0},{96,32},{1,65},{33,97},{65,1},{97,33},{2,66}... | collective-permute-start | bytes 897032 | tf_op jit(solution)/shard_map/ppermute | solution.py:802
  412.3 24.6 %collective-permute-start.48 = (bf16[1168,128]{1,0:T(8,128)(2,1)}, bf16[1168,128]{1,0:T(8,128)(2,1)S(1)}, u32[]{:S(2)}, u32[]{:S(2)}) collective-permute-start(bf16[1168,128]{1,0:T(8,128)(2,1)} %sum_z.1.refs_0_), channel_id=1, source_target_pairs={{0,32},{32,64},{64,96},{96,0},{1,33},{33,65},{65,97},{97,1},{2,34}... | collective-permute-start | bytes 897032 | tf_op jit(solution)/shard_map/ppermute | solution.py:802
  412.9 39.5 %collective-permute-start.39 = (bf16[160,2048]{1,0:T(8,128)(2,1)}, bf16[160,2048]{1,0:T(8,128)(2,1)}, u32[]{:S(2)}, u32[]{:S(2)}) collective-permute-start(bf16[160,2048]{1,0:T(8,128)(2,1)} %get-tuple-element.154), channel_id=1, source_target_pairs={{0,4},{2,6},{4,0},{6,2},{1,5},{3,7},{5,1},{7,3},{8,12},{10,14},{12... | collective-permute-start | bytes 1966088 | tf_op jit(solution)/shard_map/ppermute | solution.py:912
  415.0 30.0 %collective-permute-start.51 = (bf16[1168,128]{1,0:T(8,128)(2,1)}, bf16[1168,128]{1,0:T(8,128)(2,1)S(1)}, u32[]{:S(2)}, u32[]{:S(2)}) collective-permute-start(bf16[1168,128]{1,0:T(8,128)(2,1)} %sum_z.1.refs_0_), channel_id=1, source_target_pairs={{0,8},{8,0},{1,9},{9,1},{2,10},{10,2},{3,11},{11,3},{4,12},{12,4},... | collective-permute-start | bytes 897032 | tf_op jit(solution)/shard_map/ppermute | solution.py:803
  420.6 24.3 %collective-permute-start.54 = (bf16[1168,128]{1,0:T(8,128)(2,1)S(1)}, bf16[1168,128]{1,0:T(8,128)(2,1)S(1)}, u32[]{:S(2)}, u32[]{:S(2)}) collective-permute-start(bf16[1168,128]{1,0:T(8,128)(2,1)S(1)} %collective-permute-done.50.refs_3_), channel_id=1, source_target_pairs={{0,8},{8,0},{1,9},{9,1},{2,10},{10,2},{3,11},{11,3},{4,12},{12,4},... | collective-permute-start | bytes 897032 | tf_op jit(solution)/shard_map/ppermute | solution.py:803
  431.7 13.3 %collective-permute-start.53 = (bf16[1168,128]{1,0:T(8,128)(2,1)S(1)}, bf16[1168,128]{1,0:T(8,128)(2,1)S(1)}, u32[]{:S(2)}, u32[]{:S(2)}) collective-permute-start(bf16[1168,128]{1,0:T(8,128)(2,1)S(1)} %collective-permute-done.49.refs_2_), channel_id=1, source_target_pairs={{0,8},{8,0},{1,9},{9,1},{2,10},{10,2},{3,11},{11,3},{4,12},{12,4},... | collective-permute-start | bytes 897032 | tf_op jit(solution)/shard_map/ppermute | solution.py:803
  (64 other events, 527.2 us)
Sparse Core Ops, SparseCore 0:
  86.8 41.2 all-gather.2
  240.7 137.6 reduce-scatter.1
  387.4 68.1 all-gather.4

commit v9 on v7

--- a/solution.py
+++ b/solution.py
@@ -77,28 +77,35 @@
 
 
 def relay_body(p1, got_a, p3, got_b, q1, q3):
-    q1[:HALF, :] = (p1[:HALF, :].astype(F32) + got_a[...].astype(F32)).astype(BF16)
-    q1[HALF:, :] = p1[HALF:, :]
-    q3[:HALF, :] = p3[:HALF, :]
-    q3[HALF:, :] = (p3[HALF:, :].astype(F32) + got_b[...].astype(F32)).astype(BF16)
-
-
-def scatter_x(parts):
+    q1[...] = (p1[...].astype(F32) + got_a[...].astype(F32)).astype(BF16)
+    q3[...] = (p3[...].astype(F32) + got_b[...].astype(F32)).astype(BF16)
+
+
+def relay(parts):
     p0, p1, p2a, p2b, p3 = parts
     got_a = lax.ppermute(p2a, "x", shift(4, 1))
     got_b = lax.ppermute(p2b, "x", shift(4, -1))
+    half = lambda k: pl.BlockSpec((HALF, D), lambda i: (k, 0))
     q1, q3 = pl.pallas_call(
         relay_body,
+        grid=(1,),
         out_shape=(sds((BLK, D)),) * 2,
-        in_specs=[spec()] * 4,
-        out_specs=(spec(),) * 2,
-        compiler_params=params(),
-        cost_estimate=cost(1e6, 3e6),
+        in_specs=[half(0), half(0), half(1), half(0)],
+        out_specs=(half(0), half(1)),
+        input_output_aliases={0: 0, 2: 1},
+        compiler_params=params(),
+        cost_estimate=cost(1e6, 2e6),
         name="relay",
     )(p1, got_a, p3, got_b)
-    from_prev = lax.ppermute(q1, "x", shift(4, 1))
-    from_next = lax.ppermute(q3, "x", shift(4, -1))
-    return p0.astype(F32) + from_prev.astype(F32) + from_next.astype(F32), (got_a, got_b)
+    return p0, q1, q3
+
+
+def scatter_x(parts):
+    return last_step(*relay(parts))
+
+
+def last_step(p0, q1, q3):
+    return p0, lax.ppermute(q1, "x", shift(4, 1)), lax.ppermute(q3, "x", shift(4, -1))
 
 
 PIECES = ((0, BLK), (1, BLK), (2, HALF), (2, HALF), (3, BLK))
@@ -757,39 +764,70 @@
             gains[:, cols] = g[2 * c : 2 * c + 2]
 
 
-def sum_tail(idx, first, second, before):
+def sum_tail(idx, first, second, parts):
     got_a = lax.ppermute(first[1], "core", shift(2, 1))
     got_b = lax.ppermute(second[1], "core", shift(2, 1))
     part = sds((2, TAIL, 128))
     g = small_call(sum_core_body, (part,) * 4, idx, first[0], got_a, second[0], got_b, name="sum_core")
-    got = [tie(lax.ppermute(g[s], "y", shift(4, s)), before) for s in (2, 1, 3)]
+    g_core = g[0]
+    got = [lax.ppermute(g[s], "y", shift(4, s)) for s in (2, 1, 3)]
     part = sds((TAIL, 128))
     own, other = small_call(sum_y_body, (part,) * 2, idx, g[0], *got, name="sum_y")
+    p0, q1, q3 = relay([tie(p, own) for p in parts])
     cross = [(2 * a + b, 2 * (1 - a) + (1 - b)) for a in range(2) for b in range(2)]
     g = small_call(
         sum_z_body,
         part,
         idx,
-        own,
+        tie(own, q1, q3),
         lax.ppermute(own, "zl", shift(2, 1)),
         lax.ppermute(other, "zh", shift(2, 1)),
         lax.ppermute(other, ("zl", "zh"), cross),
         name="sum_z",
     )
-    mine = [g] + [lax.ppermute(g, "y", shift(4, s)) for s in (1, 2, 3)]
-    theirs = [lax.ppermute(v, "core", shift(2, 1)) for v in mine]
+    d_one = last_step(p0, q1, q3)
+    mine = [tie(g, *d_one)] + [lax.ppermute(g, "y", shift(4, s)) for s in (1, 2, 3)]
+    theirs = [lax.ppermute(v, "core", shift(2, 1)) for v in [g] + mine[1:]]
     shapes = (sds((DH, QW), F32), sds((AW // 2, D), F32), sds((2, D), F32))
-    return own, small_call(unpack_tail_body, shapes, idx, *mine, *theirs, name="unpack_tail")
+    return g_core, own, d_one, small_call(unpack_tail_body, shapes, idx, *mine, *theirs, name="unpack_tail")
 
 
 def inverse_rms(v):
     return lax.rsqrt(jnp.mean(v * v, axis=-1, keepdims=True) + EPSILON)
 
 
-def norm_back(v, r, gain, grad):
-    pulled = grad * gain
+def total(terms):
+    return sum((t[...].astype(F32) for t in terms[1:]), terms[0][...].astype(F32))
+
+
+def norm_two_body(tok, a, b, c, gain, after, normed):
+    v = total((tok, a, b, c))
+    after[...] = v
+    normed[...] = (v * inverse_rms(v) * gain[...]).astype(BF16)
+
+
+def norm_back_body(add, v_ref, a, b, c, gain, out, low, gain_grad):
+    v = v_ref[...].astype(F32)
+    grad = total((a, b, c))
+    r = inverse_rms(v)
+    pulled = grad * gain[...]
     inner = jnp.mean(v * pulled, axis=-1, keepdims=True)
-    return r * pulled - v * (r * r * r) * inner, jnp.sum(grad * v * r, axis=0)
+    res = add[...].astype(F32) + r * pulled - v * (r * r * r) * inner
+    out[...] = res
+    low[...] = res.astype(BF16)
+    gain_grad[...] = jnp.sum(grad * v * r, axis=0, keepdims=True)
+
+
+def row_call(body, out_shape, *args, name):
+    return pl.pallas_call(
+        body,
+        out_shape=out_shape,
+        in_specs=[spec()] * len(args),
+        out_specs=tuple(spec() for _ in out_shape),
+        compiler_params=params(),
+        cost_estimate=cost(1e6, 5e6),
+        name=name,
+    )(*args)
 
 
 def replica_layout(lengths, replica, replica_id):
@@ -812,11 +850,6 @@
 
     tok = tokens.astype(F32)
     s_one = inverse_rms(tok)
-    qkv_got = fetch_half(qkv_weight, core)
-    normed_one = gather_x((tok * s_one * gain_one).astype(BF16))
-    qkv_all = qkv_weight, qkv_got, lax.ppermute(tie(qkv_got, normed_one[2], normed_one[3]), "core", shift(2, 1))
-    out_all = fetch_partner(out_weight, core, qkv_got, normed_one[2], normed_one[3])
-
     begin, position = replica_layout(seq_lengths, seq_replica, (y * 2 + zl) * 2 + core)
     half_rows = lambda v: lax.dynamic_index_in_dim(v.reshape(4, 2, BLK), zh, 1, False).reshape(ROWS, 1)
     first = jnp.tile(half_rows(begin)[3 * BLK :, 0], 8).reshape(1, QALL)
@@ -826,6 +859,11 @@
     cosine = jnp.cos(angles)
     sine = jnp.where((lane % HD) < HD // 2, -1.0, 1.0)[None, :] * jnp.sin(angles)
 
+    qkv_got = fetch_half(qkv_weight, core)
+    normed_one = gather_x((tok * s_one * gain_one).astype(BF16), (cosine,))
+    qkv_all = qkv_weight, qkv_got, lax.ppermute(tie(qkv_got, normed_one[2], normed_one[3]), "core", shift(2, 1))
+    out_all = fetch_partner(out_weight, core, qkv_got)
+
     q, kv_own = qkv_forward(idx, normed_one, qkv_all, cosine, sine)
     cots = gather_x(tie(cotangent, normed_one[2], normed_one[3]), (kv_own,))
     rows = DH // 8
@@ -834,7 +872,7 @@
     gate_up = lax.ppermute(
         jnp.concatenate(
             [
-                tie(mine(gate_weight), out_all[1], kv_own),
+                tie(mine(gate_weight), normed_one[2], normed_one[3]),
                 jnp.zeros((rows, GAP - FF4), BF16),
                 mine(up_weight),
             ],
@@ -843,30 +881,34 @@
         ("zl", "zh"),
         cross,
     )
-    kv_par = lax.ppermute(tie(kv_own, cots[1], cots[4]), "zh", shift(2, 1))
+    kv_par = lax.ppermute(kv_own, "zh", shift(2, 1))
     down_got = fetch_half(tie(down_weight, gate_up), core)
-    att, qx = attend(idx, tie(q, cots[2], cots[3]), kv_own, kv_par, first)
+    att, qx = attend(idx, tie(q, cots[2], cots[3], out_all[1]), kv_own, kv_par, first)
     gate_up = lax.all_gather(tie(gate_up, qx), ("y", "core"), axis=0, tiled=True)
     parts = out_project(idx, att, out_all)
-    after_attn = tie(tok, down_got) + scatter_x(parts)[0]
-
-    r_two = inverse_rms(after_attn)
-    normed_two = gather_x((after_attn * r_two * gain_two).astype(BF16))
+    after_attn, normed_two = row_call(
+        norm_two_body,
+        (sds((BLK, D), F32), sds((BLK, D))),
+        tokens, *scatter_x(parts), gain_two.reshape(1, D), name="norm_two",
+    )
+    normed_two = gather_x(tie(normed_two, down_got))
     down_all = down_weight, down_got, lax.ppermute(tie(down_got, normed_two[1], normed_two[4]), "core", shift(2, 1))
     hid, dgate, dup = ffn(idx, normed_two, cots, gate_weight, up_weight, gate_up, down_all)
     own_grads = ffn_grads(normed_two, cots, hid, dgate, dup)
     grads = lax.psum_scatter(
         own_grads.reshape(32, PIECE, 128), ("zh", "zl", "y", "core"), scatter_dimension=0, tiled=True
     )
-    d_two, _ = scatter_x(
-        ffn_back(idx, tie(dgate, own_grads), dup, gate_weight, up_weight, gate_up)
-    )
-    back_two, gain_grad_two = norm_back(after_attn, r_two, gain_two, d_two)
-    after_grad = cotangent.astype(F32) + back_two
-    branch = gather_x(after_grad.astype(BF16))
+    after_grad, branch, gain_grad_two = row_call(
+        norm_back_body,
+        (sds((BLK, D), F32), sds((BLK, D)), sds((1, D), F32)),
+        cotangent, after_attn,
+        *scatter_x(ffn_back(idx, tie(dgate, own_grads), dup, gate_weight, up_weight, gate_up)),
+        gain_two.reshape(1, D), name="norm_back_two",
+    )
+    branch = gather_x(branch)
     layer_parts = down_project(idx, tie(hid, after_grad), down_all)
     att = tie(att, *layer_parts)
-    layer = [layer_parts[0]] + [
+    layer = [
         lax.ppermute(tie(layer_parts[k], branch[2], branch[3]), "x", shift(4, k)) for k in (1, 3)
     ]
     dqm, dkv_own, dkv_par = attend_back(
@@ -881,17 +923,20 @@
         idx, dqm.reshape(ROWS, AW), dkv_own, dkv_got, cosine, sine, qkv_all, normed_one, gain_one,
         gain_grad_two,
     )
-    d_one, first_step = scatter_x(parts)
-    layer.append(lax.ppermute(tie(layer_parts[2], d_one), "x", shift(4, 2)))
-    layer_out = sum((v.astype(F32) for v in layer), after_attn).astype(BF16)
-    back_one, _ = norm_back(tok, s_one, gain_one, d_one)
-    input_grad = (after_grad + back_one).astype(BF16)
-
     over_x = lambda v: sum((lax.ppermute(v, "x", shift(4, s)) for s in (1, 2, 3)), v)
-    tail = tie(tail[0], *first_step), tie(tail[1], dkv_got)
-    summed, (grad_qkv, grad_out, gains) = sum_tail(idx, tail, tail_kv, d_one)
-    grads = lax.all_gather(tie(grads, summed), ("zl", "y", "core"), axis=0, tiled=True)
+    cores_summed, summed, d_one, (grad_qkv, grad_out, gains) = sum_tail(
+        idx, (tail[0], tie(tail[1], dkv_got)), tail_kv, parts
+    )
+    layer.append(lax.ppermute(tie(layer_parts[2], summed), "x", shift(4, 2)))
+    grads = lax.all_gather(tie(grads, cores_summed), ("zl", "y", "core"), axis=0, tiled=True)
     grad_gate, grad_up, grad_down = unpack(grads)
+    _, input_grad, _ = row_call(
+        norm_back_body,
+        (sds((BLK, D), F32), sds((BLK, D)), sds((1, D), F32)),
+        after_grad, tokens, *d_one, gain_one.reshape(1, D), name="norm_back_one",
+    )
+    layer_out = sum((v.astype(F32) for v in layer), after_attn + layer_parts[0].astype(F32))
+    layer_out = layer_out.astype(BF16)
     gains = over_x(gains)
     return (
         layer_out, input_grad, gains[0], grad_qkv, grad_out, grad_gate, grad_up,

time: 486 us -> 486 us (level)
  starting transfers between devices: 120 us -> 100 us
  waiting for transfers between devices: 154 us -> 168 us
  Pallas kernels: 155 us -> 166 us
  other arithmetic: 18 us -> 8.66 us
  local copies, waits for them, and re-layouts: 21 us -> 26 us
    ppermute x25, waiting for transfers between devices: 66.8 us -> 101 us  [the longest x3 44.1 us: sum_tail(): got = [lax.ppermute(g[s], 'y', shift(4, s)) for s in (2, 1, 3)]]
    ppermute x25, starting transfers between devices: 54.2 us -> 35.1 us  [the longest x4 9.18 us: sum_tail(): theirs = [lax.ppermute(v, 'core', shift(2, 1)) for v in [g] + mine[1:]]]
    ppermute x1, waiting for transfers between devices: 12.2 us -> 0.01 us  [sum_tail(): lax.ppermute(other, ('zl', 'zh'), cross)]
    ppermute x4, starting transfers between devices: 9.98 us -> 21.4 us  [gather_x(): opp_b = lax.ppermute(send_b, 'x', shift(4, -1))]
    ppermute x3, waiting for transfers between devices: 11.4 us -> 0.38 us  [fetch_half(): lax.ppermute(lax.dynamic_slice_in_dim(w, core * half, half, 0), 'zh', shi...]
    ppermute x1, starting transfers between devices: 13.9 us -> 2.92 us  [on_device(): lax.ppermute(tie(down_got, normed_two[1], normed_two[4]), 'core', shift(2...]
    pallas_call x3 -> x6, Pallas kernels: 8.13 us -> 19.1 us  [the longest x3 12.2 us: row_call(): pl.pallas_call(body, out_shape=out_shape, in_specs=[spec()] * len(args),...]
    ppermute x1, waiting for transfers between devices: 0.01 us -> 6.93 us  [sum_tail(): lax.ppermute(other, 'zh', shift(2, 1))]
  transfers between devices with their start and end apart: 61 -> 61, of which waited for: 26 -> 27; matrix products, arithmetic and copies ran while one was open for 5% -> 3% of each run, Pallas kernels for 21% -> 24%
where the time goes in v9:
time: 486 us; the launch traced here: 483 us
  waiting for transfers between devices  168 us (35%)
  Pallas kernels  166 us (34%)
  starting transfers between devices  100 us (21%)
  local copies, waits for them, and re-layouts  26 us (5%)
  between operations  14.4 us (3%)
  other arithmetic  8.66 us (2%)
    ppermute x3, waiting for transfers between devices, sum_tail(): got = [lax.ppermute(g[s], 'y', shift(4, s)) for s in (2, 1, 3)]  44.1 us
    ppermute x3, waiting for transfers between devices, last_step(): lax.ppermute(q1, 'x', shift(4, 1))  26.9 us
    ppermute x4, starting transfers between devices, gather_x(): opp_b = lax.ppermute(send_b, 'x', shift(4, -1))  21.4 us
    ppermute x4, waiting for transfers between devices, gather_x(): from_prev = lax.ppermute(v, 'x', shift(4, 1))  21.1 us
    pallas_call x1, Pallas kernels, ffn(): pl.pallas_call(ffn_body, grid=(TILES,), out_shape=(sds((ROWS, FF4)),) * 3...  20.9 us
    pallas_call x1, Pallas kernels, ffn_grads(): pl.pallas_call(ffn_grads_body, grid=(16 // QS,), out_shape=sds((2, 16, PI...  20.8 us
    pallas_call x1, Pallas kernels, attend_back(): pl.pallas_call(attend_back_body, out_shape=(sds((4, BLK, AW)), sds((ROWS,...  19.8 us
    ppermute x3, waiting for transfers between devices, relay(): got_a = lax.ppermute(p2a, 'x', shift(4, 1))  16 us
  transfers between devices with their start and end apart: 61, of which 27 were waited for; matrix products, arithmetic and copies ran while one was open for 3% of the time, Pallas kernels for 24%

profile of v9, /device:TPU:1, one launch (start us, length us, event | category | flops | bytes accessed | tf_op | source)
XLA Modules:
  0.0 483.1 jit_solution(13575971184807929760)
XLA Ops:
  14.3 3.7 collective-permute-start.4
  22.2 5.2 %collective-permute-done.1.n3.refs_4_.refs_9_ = bf16[160,2048]{1,0:T(8,128)(2,1)S(1)} collective-permute-done((bf16[160,2048]{1,0:T(8,128)(2,1)S(1)}, bf16[160,2048]{1,0:T(8,128)(2,1)S(1)}, u32[]{:S(2)}, u32[]{:S(2)}) %collective-permute-start.1) | collective-permute-done | bytes 655392 | tf_op jit(solution)/shard_map/ppermute | solution.py:70
  32.1 4.0 collective-permute-done.3.n2b.refs_3_.refs_8_
  36.1 2.9 collective-permute-done.2.n2a.refs_2_.refs_7_
  39.0 3.1 collective-permute-start.5
  47.9 3.8 collective-permute-start.10
  52.5 6.8 %qkv_forward.1 = (bf16[4,1280,128]{2,1,0:T(8,128)(2,1)}, bf16[640,128]{1,0:T(8,128)(2,1)}) custom-call(s32[4]{0:T(128)} %pad_add_fusion.idx, bf16[160,2048]{1,0:T(8,128)(2,1)} %copy-done.2, bf16[160,2048]{1,0:T(8,128)(2,1)} %copy-done.5, bf16[80,2048]{1,0:T(8,128)(2,1)} %collective-permute-done.2.n2a.refs_2_.refs_7_, bf16[80,2048]{1,0:T(8,128)(2,1)} %copy-done.17, ...), custom_call_target="tpu_custom_call" | custom-call | flops 1677721600 | bytes 7000000 | tf_op jit(solution)/shard_map/qkv_forward/pallas_call | solution.py:175
  64.2 3.7 collective-permute-start.17
  67.9 3.0 collective-permute-done.8.c2a.refs_12_
  73.0 8.7 %attend.1 = (bf16[4,160,512]{2,1,0:T(8,128)(2,1)}, bf16[4,1280,128]{2,1,0:T(8,128)(2,1)}) custom-call(s32[4]{0:T(128)} %pad_add_fusion.idx, bf16[4,1280,128]{2,1,0:T(8,128)(2,1)} %get-tuple-element.109.q, bf16[640,128]{1,0:T(8,128)(2,1)} %get-tuple-element.105.kv_own, bf16[640,128]{1,0:T(8,128)(2,1)} %copy-done.51, s32[1,1280]{1,0:T(1,128)} %reshape_tile.3.first), custom_call_target="tpu_custom_call" | custom-call | flops 12000000000 | bytes 3000000 | tf_op jit(solution)/shard_map/attend/pallas_call | solution.py:268
  90.8 4.8 out_project.1
  98.2 7.9 %collective-permute-done.13.got_a = bf16[80,2048]{1,0:T(8,128)(2,1)S(1)} collective-permute-done((bf16[80,2048]{1,0:T(8,128)(2,1)}, bf16[80,2048]{1,0:T(8,128)(2,1)S(1)}, u32[]{:S(2)}, u32[]{:S(2)}) %collective-permute-start.13) | collective-permute-done | bytes 327712 | tf_op jit(solution)/shard_map/ppermute | solution.py:86
  109.1 2.7 collective-permute-start.16
  111.8 14.0 %collective-permute-done.15.b = bf16[160,2048]{1,0:T(8,128)(2,1)S(1)} collective-permute-done((bf16[160,2048]{1,0:T(8,128)(2,1)}, bf16[160,2048]{1,0:T(8,128)(2,1)S(1)}, u32[]{:S(2)}, u32[]{:S(2)}) %collective-permute-start.15) | collective-permute-done | bytes 655392 | tf_op jit(solution)/shard_map/ppermute | solution.py:108
  126.8 3.3 norm_two.1
  132.8 13.1 %collective-permute-done.20.n3.refs_4_.refs_9_ = bf16[160,2048]{1,0:T(8,128)(2,1)S(1)} collective-permute-done((bf16[160,2048]{1,0:T(8,128)(2,1)}, bf16[160,2048]{1,0:T(8,128)(2,1)S(1)}, u32[]{:S(2)}, u32[]{:S(2)}) %collective-permute-start.20) | collective-permute-done | bytes 655392 | tf_op jit(solution)/shard_map/ppermute | solution.py:70
  145.9 2.9 collective-permute-start.23
  148.9 13.6 %collective-permute-start.22 = (bf16[80,2048]{1,0:T(8,128)(2,1)S(1)}, bf16[80,2048]{1,0:T(8,128)(2,1)S(1)}, u32[]{:S(2)}, u32[]{:S(2)}) collective-permute-start(bf16[80,2048]{1,0:T(8,128)(2,1)S(1)} %slice.50), channel_id=1, source_target_pairs={{0,6},{2,0},{4,2},{6,4},{1,7},{3,1},{5,3},{7,5},{8,14},{10,8},{12,... | collective-permute-start | bytes 983048 | tf_op jit(solution)/shard_map/ppermute | solution.py:75
  162.5 7.1 %collective-permute-done.22.n2b.refs_3_.refs_8_ = bf16[80,2048]{1,0:T(8,128)(2,1)S(1)} collective-permute-done((bf16[80,2048]{1,0:T(8,128)(2,1)S(1)}, bf16[80,2048]{1,0:T(8,128)(2,1)S(1)}, u32[]{:S(2)}, u32[]{:S(2)}) %collective-permute-start.22) | collective-permute-done | bytes 327712 | tf_op jit(solution)/shard_map/ppermute | solution.py:75
  169.6 3.1 collective-permute-done.21.n2a.refs_2_.refs_7_
  173.9 20.9 %ffn.1 = (bf16[640,1408]{1,0:T(8,128)(2,1)}, bf16[640,1408]{1,0:T(8,128)(2,1)}, bf16[640,1408]{1,0:T(8,128)(2,1)}) custom-call(s32[4]{0:T(128)} %pad_add_fusion.idx, bf16[160,2048]{1,0:T(8,128)(2,1)} %get-tuple-element.122.n0.refs_0_.refs_5_, bf16[160,2048]{1,0:T(8,128)(2,1)} %copy-done.38, bf16[80,2048]{1,0:T(8,128)(2,1)} %copy-done.50, ...), custom_call_target="tpu_custom_call" | custom-call | flops 11072962560 | bytes 34000000 | tf_op jit(solution)/shard_map/ffn/pallas_call | solution.py:503
  194.8 20.8 %ffn_grads.1 = bf16[2,16,2112,128]{3,2,1,0:T(8,128)(2,1)} custom-call(bf16[160,2048]{1,0:T(8,128)(2,1)} %get-tuple-element.122.n0.refs_0_.refs_5_, bf16[160,2048]{1,0:T(8,128)(2,1)} %copy-done.38, bf16[80,2048]{1,0:T(8,128)(2,1)} %copy-done.50, bf16[80,2048]{1,0:T(8,128)(2,1)} %copy-done.49, bf16[160,2048]{1,0:T(8,128)(2,1)} %copy-done.37, ...), custom_call_target="tpu_custom_call" | custom-call | flops 11072962560 | bytes 30000000 | tf_op jit(solution)/shard_map/ffn_grads/pallas_call | solution.py:615
  215.7 16.0 %ffn_back.1 = (bf16[160,2048]{1,0:T(8,128)(2,1)}, bf16[160,2048]{1,0:T(8,128)(2,1)}, bf16[80,2048]{1,0:T(8,128)(2,1)}, bf16[80,2048]{1,0:T(8,128)(2,1)}, bf16[160,2048]{1,0:T(8,128)(2,1)}) custom-call(s32[4]{0:T(128)} %pad_add_fusion.idx, bf16[640,1408]{1,0:T(8,128)(2,1)} %get-tuple-element.131.refs_16_.dgate, ...), custom_call_target="tpu_custom_call" | custom-call | flops 7381975040 | bytes 18000000 | tf_op jit(solution)/shard_map/ffn_back/pallas_call | solution.py:568
  234.4 6.9 %collective-permute-done.24.got_a = bf16[80,2048]{1,0:T(8,128)(2,1)S(1)} collective-permute-done((bf16[80,2048]{1,0:T(8,128)(2,1)}, bf16[80,2048]{1,0:T(8,128)(2,1)S(1)}, u32[]{:S(2)}, u32[]{:S(2)}) %collective-permute-start.24) | collective-permute-done | bytes 327712 | tf_op jit(solution)/shard_map/ppermute | solution.py:86
  244.4 2.7 collective-permute-start.27
  247.1 13.0 %collective-permute-done.26.b = bf16[160,2048]{1,0:T(8,128)(2,1)S(1)} collective-permute-done((bf16[160,2048]{1,0:T(8,128)(2,1)}, bf16[160,2048]{1,0:T(8,128)(2,1)S(1)}, u32[]{:S(2)}, u32[]{:S(2)}) %collective-permute-start.26) | collective-permute-done | bytes 655392 | tf_op jit(solution)/shard_map/ppermute | solution.py:108
  261.1 4.4 norm_back_two.1
  267.8 11.4 %collective-permute-done.29.b1.refs_11_ = bf16[160,2048]{1,0:T(8,128)(2,1)S(1)} collective-permute-done((bf16[160,2048]{1,0:T(8,128)(2,1)}, bf16[160,2048]{1,0:T(8,128)(2,1)S(1)}, u32[]{:S(2)}, u32[]{:S(2)}) %collective-permute-start.29) | collective-permute-done | bytes 655392 | tf_op jit(solution)/shard_map/ppermute | solution.py:71
  279.2 2.8 collective-permute-done.28.b3.refs_14_
  284.8 10.3 %down_project.1 = (bf16[160,2048]{1,0:T(8,128)(2,1)}, bf16[160,2048]{1,0:T(8,128)(2,1)}, bf16[160,2048]{1,0:T(8,128)(2,1)}, bf16[160,2048]{1,0:T(8,128)(2,1)}) custom-call(s32[4]{0:T(128)} %pad_add_fusion.idx, bf16[640,1408]{1,0:T(8,128)(2,1)} %get-tuple-element.140.refs_15_.hid, bf16[704,2048]{1,0:T(8,128)(2,1)} %w0.9, ...), custom_call_target="tpu_custom_call" | custom-call | flops 3690987520 | bytes 11000000 | tf_op jit(solution)/shard_map/down_project/pallas_call | solution.py:538
  295.3 3.0 collective-permute-start.33
  298.3 19.8 %attend_back.1 = (bf16[4,160,512]{2,1,0:T(8,128)(2,1)}, f32[640,128]{1,0:T(8,128)}, bf16[640,128]{1,0:T(8,128)(2,1)}) custom-call(s32[4]{0:T(128)} %pad_add_fusion.idx, bf16[4,1280,128]{2,1,0:T(8,128)(2,1)} %get-tuple-element.125.qx, bf16[640,128]{1,0:T(8,128)(2,1)} %get-tuple-element.105.kv_own, bf16[640,128]{1,0:T(8,128)(2,1)} %copy-done.51, ...), custom_call_target="tpu_custom_call" | custom-call | flops 30000001024 | bytes 8000000 | tf_op jit(solution)/shard_map/attend_back/pallas_call | solution.py:377
  318.1 8.9 %attn_grads.1 = (bf16[4,2,1024,128]{3,2,1,0:T(8,128)(2,1)}, bf16[4,2,1024,128]{3,2,1,0:T(8,128)(2,1)}) custom-call(s32[4]{0:T(128)} %pad_add_fusion.idx, bf16[160,2048]{1,0:T(8,128)(2,1)} %copy-done.2, bf16[160,2048]{1,0:T(8,128)(2,1)} %copy-done.5, bf16[80,2048]{1,0:T(8,128)(2,1)} %collective-permute-done.2.n2a.refs_2_.refs_7_, ...), custom_call_target="tpu_custom_call" | custom-call | flops 2684354560 | bytes 10000000 | tf_op jit(solution)/shard_map/attn_grads/pallas_call | solution.py:697
  327.1 6.5 %collective-permute-start.35 = (bf16[4,2,1024,128]{3,2,1,0:T(8,128)(2,1)}, bf16[4,2,1024,128]{3,2,1,0:T(8,128)(2,1)S(1)}, u32[]{:S(2)}, u32[]{:S(2)}) collective-permute-start(bf16[4,2,1024,128]{3,2,1,0:T(8,128)(2,1)} %get-tuple-element.157), channel_id=1, source_target_pairs={{0,8},{8,0},{1,9},{9,1},{2,10},{10,2},{3,11},{11,3},{4,12},{12,4},... | collective-permute-start | bytes 6291464 | tf_op jit(solution)/shard_map/ppermute | solution.py:768
  333.5 7.1 %qkv_back.1 = (bf16[4,2,144,128]{3,2,1,0:T(8,128)(2,1)}, bf16[4,2,144,128]{3,2,1,0:T(8,128)(2,1)}, bf16[160,2048]{1,0:T(8,128)(2,1)}, bf16[160,2048]{1,0:T(8,128...) custom-call(s32[4]{0:T(128)} %pad_add_fusion.idx, ...), custom_call_target="tpu_custom_call" | custom-call | flops 1677721600 | bytes 13000000 | tf_op jit(solution)/shard_map/qkv_back/pallas_call | solution.py:434
  344.2 3.9 sum_core.1
  348.1 2.8 collective-permute-start.37
  353.6 17.7 %collective-permute-done.37.b = bf16[2,1168,128]{2,1,0:T(8,128)(2,1)S(1)} collective-permute-done((bf16[2,1168,128]{2,1,0:T(8,128)(2,1)}, bf16[2,1168,128]{2,1,0:T(8,128)(2,1)S(1)}, u32[]{:S(2)}, u32[]{:S(2)}) %collective-permute-start.37) | collective-permute-done | bytes 598048 | tf_op jit(solution)/shard_map/ppermute | solution.py:773
  371.2 25.6 %collective-permute-done.38.c = bf16[2,1168,128]{2,1,0:T(8,128)(2,1)S(1)} collective-permute-done((bf16[2,1168,128]{2,1,0:T(8,128)(2,1)}, bf16[2,1168,128]{2,1,0:T(8,128)(2,1)S(1)}, u32[]{:S(2)}, u32[]{:S(2)}) %collective-permute-start.38) | collective-permute-done | bytes 598048 | tf_op jit(solution)/shard_map/ppermute | solution.py:773
  403.9 3.0 collective-permute-start.47
  415.2 6.9 %collective-permute-done.46.c = bf16[1168,128]{1,0:T(8,128)(2,1)S(1)} collective-permute-done((bf16[1168,128]{1,0:T(8,128)(2,1)}, bf16[1168,128]{1,0:T(8,128)(2,1)S(1)}, u32[]{:S(2)}, u32[]{:S(2)}) %collective-permute-start.46) | collective-permute-done | bytes 299040 | tf_op jit(solution)/shard_map/ppermute | solution.py:784
  422.1 6.1 %collective-permute-done.45.b = bf16[1168,128]{1,0:T(8,128)(2,1)S(1)} collective-permute-done((bf16[1168,128]{1,0:T(8,128)(2,1)}, bf16[1168,128]{1,0:T(8,128)(2,1)S(1)}, u32[]{:S(2)}, u32[]{:S(2)}) %collective-permute-start.45) | collective-permute-done | bytes 299040 | tf_op jit(solution)/shard_map/ppermute | solution.py:783
  431.8 6.6 %collective-permute-done.50.refs_3_ = bf16[1168,128]{1,0:T(8,128)(2,1)S(1)} collective-permute-done((bf16[1168,128]{1,0:T(8,128)(2,1)}, bf16[1168,128]{1,0:T(8,128)(2,1)S(1)}, u32[]{:S(2)}, u32[]{:S(2)}) %collective-permute-start.50) | collective-permute-done | bytes 299040 | tf_op jit(solution)/shard_map/ppermute | solution.py:789
  440.3 3.1 collective-permute-start.51
  445.8 5.6 %collective-permute-start.54 = (bf16[1168,128]{1,0:T(8,128)(2,1)S(1)}, bf16[1168,128]{1,0:T(8,128)(2,1)S(1)}, u32[]{:S(2)}, u32[]{:S(2)}) collective-permute-start(bf16[1168,128]{1,0:T(8,128)(2,1)S(1)} %collective-permute-done.50.refs_3_), channel_id=1, source_target_pairs={{0,8},{8,0},{1,9},{9,1},{2,10},{10,2},{3,11},{11,3},{4,12},{12,4},... | collective-permute-start | bytes 897032 | tf_op jit(solution)/shard_map/ppermute | solution.py:790
  454.1 4.2 unpack_tail.1
  461.4 4.5 norm_back_one.1
  466.6 9.8 %unpack.1 = (f32[1024,1408]{1,0:T(8,128)}, f32[1024,1408]{1,0:T(8,128)}, f32[704,2048]{1,0:T(8,128)}) custom-call(bf16[16,2112,128]{2,1,0:T(8,128)(2,1)} %all-gather.5.cloned.1.call-done.piece), custom_call_target="tpu_custom_call" | custom-call | flops 1000000 | bytes 26000000 | tf_op jit(solution)/shard_map/unpack/pallas_call | solution.py:642
  (241 shorter events, 97.0 us)
Async XLA Ops:
  7.2 165.6 %all-gather.3.cloned.1.call-start = ((), (), s32[]{:S(2)}) async-start(), calls=%async_computation.1 | async-start | bytes 6782976 | tf_op jit(solution)/shard_map/all_gather | solution.py:887
  10.0 17.4 %collective-permute-start.1 = (bf16[160,2048]{1,0:T(8,128)(2,1)S(1)}, bf16[160,2048]{1,0:T(8,128)(2,1)S(1)}, u32[]{:S(2)}, u32[]{:S(2)}) collective-permute-start(bf16[160,2048]{1,0:T(8,128)(2,1)S(1)} %fusion.2.n0.refs_0_.refs_5_), channel_id=1, source_target_pairs={{0,2},{2,4},{4,6},{6,0},{1,3},{3,5},{5,7},{7,1},{8,10},{10,12},{12... | collective-permute-start | bytes 1966088 | tf_op jit(solution)/shard_map/ppermute | solution.py:70
  12.1 15.3 %collective-permute-start = (bf16[160,2048]{1,0:T(8,128)(2,1)S(1)}, bf16[160,2048]{1,0:T(8,128)(2,1)S(1)}, u32[]{:S(2)}, u32[]{:S(2)}) collective-permute-start(bf16[160,2048]{1,0:T(8,128)(2,1)S(1)} %fusion.2.n0.refs_0_.refs_5_), channel_id=1, source_target_pairs={{0,6},{2,0},{4,2},{6,4},{1,7},{3,1},{5,3},{7,5},{8,14},{10,8},{12,... | collective-permute-start | bytes 1966088 | tf_op jit(solution)/shard_map/ppermute | solution.py:71
  14.3 17.7 %collective-permute-start.4 = (bf16[512,640]{1,0:T(8,128)(2,1)}, bf16[512,640]{1,0:T(8,128)(2,1)S(1)}, u32[]{:S(2)}, u32[]{:S(2)}) collective-permute-start(bf16[512,640]{1,0:T(8,128)(2,1)} %constant_dynamic-slice_fusion.5), channel_id=1, source_target_pairs={{0,1},{1,0},{2,3},{3,2},{4,5},{5,4},{6,7},{7,6},{8,9},{9,8},{10,11... | collective-permute-start | bytes 1966088 | tf_op jit(solution)/shard_map/ppermute | solution.py:134
  30.7 8.3 %collective-permute-start.2 = (bf16[80,2048]{1,0:T(8,128)(2,1)S(1)}, bf16[80,2048]{1,0:T(8,128)(2,1)}, u32[]{:S(2)}, u32[]{:S(2)}) collective-permute-start(bf16[80,2048]{1,0:T(8,128)(2,1)S(1)} %slice.45), channel_id=1, source_target_pairs={{0,2},{2,4},{4,6},{6,0},{1,3},{3,5},{5,7},{7,1},{8,10},{10,12},{12... | collective-permute-start | bytes 983048 | tf_op jit(solution)/shard_map/ppermute | solution.py:74
  39.0 12.6 %collective-permute-start.5 = (bf16[512,640]{1,0:T(8,128)(2,1)S(1)}, bf16[512,640]{1,0:T(8,128)(2,1)S(1)}, u32[]{:S(2)}, u32[]{:S(2)}) collective-permute-start(bf16[512,640]{1,0:T(8,128)(2,1)S(1)} %collective-permute-done.4.w1), channel_id=1, source_target_pairs={{0,8},{8,0},{1,9},{9,1},{2,10},{10,2},{3,11},{11,3},{4,12},{12,4},... | collective-permute-start | bytes 1966088 | tf_op jit(solution)/shard_map/ppermute | solution.py:864
  42.1 17.1 %collective-permute-start.7 = (bf16[160,2048]{1,0:T(8,128)(2,1)}, bf16[160,2048]{1,0:T(8,128)(2,1)}, u32[]{:S(2)}, u32[]{:S(2)}) collective-permute-start(bf16[160,2048]{1,0:T(8,128)(2,1)} %add.149), channel_id=1, source_target_pairs={{0,6},{2,0},{4,2},{6,4},{1,7},{3,1},{5,3},{7,5},{8,14},{10,8},{12,... | collective-permute-start | bytes 1966088 | tf_op jit(solution)/shard_map/ppermute | solution.py:71
  42.3 18.0 %collective-permute-start.6 = (bf16[160,2048]{1,0:T(8,128)(2,1)}, bf16[160,2048]{1,0:T(8,128)(2,1)}, u32[]{:S(2)}, u32[]{:S(2)}) collective-permute-start(bf16[160,2048]{1,0:T(8,128)(2,1)} %add.149), channel_id=1, source_target_pairs={{0,2},{2,4},{4,6},{6,0},{1,3},{3,5},{5,7},{7,1},{8,10},{10,12},{12... | collective-permute-start | bytes 1966088 | tf_op jit(solution)/shard_map/ppermute | solution.py:70
  47.9 20.0 %collective-permute-start.10 = (bf16[128,2048]{1,0:T(8,128)(2,1)}, bf16[128,2048]{1,0:T(8,128)(2,1)}, u32[]{:S(2)}, u32[]{:S(2)}) collective-permute-start(bf16[128,2048]{1,0:T(8,128)(2,1)} %constant_dynamic-slice_fusion.4), channel_id=1, source_target_pairs={{0,1},{1,0},{2,3},{3,2},{4,5},{5,4},{6,7},{7,6},{8,9},{9,8},{10,11... | collective-permute-start | bytes 1572872 | tf_op jit(solution)/shard_map/ppermute | solution.py:134
  59.3 13.1 %collective-permute-start.11 = (bf16[640,128]{1,0:T(8,128)(2,1)}, bf16[640,128]{1,0:T(8,128)(2,1)S(1)}, u32[]{:S(2)}, u32[]{:S(2)}) collective-permute-start(bf16[640,128]{1,0:T(8,128)(2,1)} %get-tuple-element.105.kv_own), channel_id=1, source_target_pairs={{0,1},{1,0},{2,3},{3,2},{4,5},{5,4},{6,7},{7,6},{8,9},{9,8},{10,11... | collective-permute-start | bytes 491528 | tf_op jit(solution)/shard_map/ppermute | solution.py:884
  61.3 9.6 %collective-permute-start.8 = (bf16[80,2048]{1,0:T(8,128)(2,1)S(1)}, bf16[80,2048]{1,0:T(8,128)(2,1)S(1)}, u32[]{:S(2)}, u32[]{:S(2)}) collective-permute-start(bf16[80,2048]{1,0:T(8,128)(2,1)S(1)} %slice.47), channel_id=1, source_target_pairs={{0,2},{2,4},{4,6},{6,0},{1,3},{3,5},{5,7},{7,1},{8,10},{10,12},{12... | collective-permute-start | bytes 983048 | tf_op jit(solution)/shard_map/ppermute | solution.py:74
  61.4 9.5 %collective-permute-start.9 = (bf16[80,2048]{1,0:T(8,128)(2,1)S(1)}, bf16[80,2048]{1,0:T(8,128)(2,1)S(1)}, u32[]{:S(2)}, u32[]{:S(2)}) collective-permute-start(bf16[80,2048]{1,0:T(8,128)(2,1)S(1)} %slice.48), channel_id=1, source_target_pairs={{0,6},{2,0},{4,2},{6,4},{1,7},{3,1},{5,3},{7,5},{8,14},{10,8},{12,... | collective-permute-start | bytes 983048 | tf_op jit(solution)/shard_map/ppermute | solution.py:75
  64.2 19.1 %collective-permute-start.17 = (bf16[128,2944]{1,0:T(8,128)(2,1)S(1)}, bf16[128,2944]{1,0:T(8,128)(2,1)S(1)}, u32[]{:S(2)}, u32[]{:S(2)}) collective-permute-start(bf16[128,2944]{1,0:T(8,128)(2,1)S(1)} %pad_maximum_fusion), channel_id=1, source_target_pairs={{0,17},{1,16},{16,1},{17,0},{2,19},{3,18},{18,3},{19,2},{4,21},{5,... | collective-permute-start | bytes 2261000 | tf_op jit(solution)/shard_map/ppermute | solution.py:872
  84.2 263.9 %reduce-scatter.2.cloned.1.call-start = ((), (), s32[]{:S(2)}) async-start(), calls=%async_computation.2 | async-start | bytes 17842176 | tf_op jit(solution)/shard_map/reduce_scatter | solution.py:898
  88.2 41.9 %collective-permute-start.18 = (bf16[352,2048]{1,0:T(8,128)(2,1)S(1)}, bf16[352,2048]{1,0:T(8,128)(2,1)}, u32[]{:S(2)}, u32[]{:S(2)}) collective-permute-start(bf16[352,2048]{1,0:T(8,128)(2,1)S(1)} %constant_dynamic-slice_fusion), channel_id=1, source_target_pairs={{0,1},{1,0},{2,3},{3,2},{4,5},{5,4},{6,7},{7,6},{8,9},{9,8},{10,11... | collective-permute-start | bytes 4325384 | tf_op jit(solution)/shard_map/ppermute | solution.py:134
  95.6 10.5 %collective-permute-start.13 = (bf16[80,2048]{1,0:T(8,128)(2,1)}, bf16[80,2048]{1,0:T(8,128)(2,1)S(1)}, u32[]{:S(2)}, u32[]{:S(2)}) collective-permute-start(bf16[80,2048]{1,0:T(8,128)(2,1)} %get-tuple-element.113), channel_id=1, source_target_pairs={{0,2},{2,4},{4,6},{6,0},{1,3},{3,5},{5,7},{7,1},{8,10},{10,12},{12... | collective-permute-start | bytes 983048 | tf_op jit(solution)/shard_map/ppermute | solution.py:86
  95.6 10.5 %collective-permute-start.14 = (bf16[80,2048]{1,0:T(8,128)(2,1)}, bf16[80,2048]{1,0:T(8,128)(2,1)S(1)}, u32[]{:S(2)}, u32[]{:S(2)}) collective-permute-start(bf16[80,2048]{1,0:T(8,128)(2,1)} %get-tuple-element.115), channel_id=1, source_target_pairs={{0,6},{2,0},{4,2},{6,4},{1,7},{3,1},{5,3},{7,5},{8,14},{10,8},{12,... | collective-permute-start | bytes 983048 | tf_op jit(solution)/shard_map/ppermute | solution.py:87
  109.1 16.6 %collective-permute-start.15 = (bf16[160,2048]{1,0:T(8,128)(2,1)}, bf16[160,2048]{1,0:T(8,128)(2,1)S(1)}, u32[]{:S(2)}, u32[]{:S(2)}) collective-permute-start(bf16[160,2048]{1,0:T(8,128)(2,1)} %get-tuple-element.116), channel_id=1, source_target_pairs={{0,2},{2,4},{4,6},{6,0},{1,3},{3,5},{5,7},{7,1},{8,10},{10,12},{12... | collective-permute-start | bytes 1966088 | tf_op jit(solution)/shard_map/ppermute | solution.py:108
  109.1 16.7 %collective-permute-start.16 = (bf16[160,2048]{1,0:T(8,128)(2,1)}, bf16[160,2048]{1,0:T(8,128)(2,1)S(1)}, u32[]{:S(2)}, u32[]{:S(2)}) collective-permute-start(bf16[160,2048]{1,0:T(8,128)(2,1)} %get-tuple-element.117), channel_id=1, source_target_pairs={{0,6},{2,0},{4,2},{6,4},{1,7},{3,1},{5,3},{7,5},{8,14},{10,8},{12,... | collective-permute-start | bytes 1966088 | tf_op jit(solution)/shard_map/ppermute | solution.py:108
  130.2 15.7 %collective-permute-start.20 = (bf16[160,2048]{1,0:T(8,128)(2,1)}, bf16[160,2048]{1,0:T(8,128)(2,1)S(1)}, u32[]{:S(2)}, u32[]{:S(2)}) collective-permute-start(bf16[160,2048]{1,0:T(8,128)(2,1)} %get-tuple-element.122.n0.refs_0_.refs_5_), channel_id=1, source_target_pairs={{0,2},{2,4},{4,6},{6,0},{1,3},{3,5},{5,7},{7,1},{8,10},{10,12},{12... | collective-permute-start | bytes 1966088 | tf_op jit(solution)/shard_map/ppermute | solution.py:70
  130.2 15.7 %collective-permute-start.19 = (bf16[160,2048]{1,0:T(8,128)(2,1)}, bf16[160,2048]{1,0:T(8,128)(2,1)S(1)}, u32[]{:S(2)}, u32[]{:S(2)}) collective-permute-start(bf16[160,2048]{1,0:T(8,128)(2,1)} %get-tuple-element.122.n0.refs_0_.refs_5_), channel_id=1, source_target_pairs={{0,6},{2,0},{4,2},{6,4},{1,7},{3,1},{5,3},{7,5},{8,14},{10,8},{12,... | collective-permute-start | bytes 1966088 | tf_op jit(solution)/shard_map/ppermute | solution.py:71
  145.9 26.8 %collective-permute-start.23 = (bf16[352,2048]{1,0:T(8,128)(2,1)}, bf16[352,2048]{1,0:T(8,128)(2,1)S(1)}, u32[]{:S(2)}, u32[]{:S(2)}) collective-permute-start(bf16[352,2048]{1,0:T(8,128)(2,1)} %collective-permute-done.18.w1), channel_id=1, source_target_pairs={{0,8},{8,0},{1,9},{9,1},{2,10},{10,2},{3,11},{11,3},{4,12},{12,4},... | collective-permute-start | bytes 4325384 | tf_op jit(solution)/shard_map/ppermute | solution.py:895
  148.9 20.8 %collective-permute-start.22 = (bf16[80,2048]{1,0:T(8,128)(2,1)S(1)}, bf16[80,2048]{1,0:T(8,128)(2,1)S(1)}, u32[]{:S(2)}, u32[]{:S(2)}) collective-permute-start(bf16[80,2048]{1,0:T(8,128)(2,1)S(1)} %slice.50), channel_id=1, source_target_pairs={{0,6},{2,0},{4,2},{6,4},{1,7},{3,1},{5,3},{7,5},{8,14},{10,8},{12,... | collective-permute-start | bytes 983048 | tf_op jit(solution)/shard_map/ppermute | solution.py:75
  162.5 10.2 %collective-permute-start.21 = (bf16[80,2048]{1,0:T(8,128)(2,1)S(1)}, bf16[80,2048]{1,0:T(8,128)(2,1)S(1)}, u32[]{:S(2)}, u32[]{:S(2)}) collective-permute-start(bf16[80,2048]{1,0:T(8,128)(2,1)S(1)} %slice.49), channel_id=1, source_target_pairs={{0,2},{2,4},{4,6},{6,0},{1,3},{3,5},{5,7},{7,1},{8,10},{10,12},{12... | collective-permute-start | bytes 983048 | tf_op jit(solution)/shard_map/ppermute | solution.py:74
  215.6 251.0 %all-gather.5.cloned.1.call-start = ((), (), s32[]{:S(2)}) async-start(), calls=%async_computation.3 | async-start | bytes 9191424 | tf_op jit(solution)/shard_map/all_gather | solution.py:931
  231.6 9.6 %collective-permute-start.24 = (bf16[80,2048]{1,0:T(8,128)(2,1)}, bf16[80,2048]{1,0:T(8,128)(2,1)S(1)}, u32[]{:S(2)}, u32[]{:S(2)}) collective-permute-start(bf16[80,2048]{1,0:T(8,128)(2,1)} %get-tuple-element.134), channel_id=1, source_target_pairs={{0,2},{2,4},{4,6},{6,0},{1,3},{3,5},{5,7},{7,1},{8,10},{10,12},{12... | collective-permute-start | bytes 983048 | tf_op jit(solution)/shard_map/ppermute | solution.py:86
  231.7 9.5 %collective-permute-start.25 = (bf16[80,2048]{1,0:T(8,128)(2,1)}, bf16[80,2048]{1,0:T(8,128)(2,1)S(1)}, u32[]{:S(2)}, u32[]{:S(2)}) collective-permute-start(bf16[80,2048]{1,0:T(8,128)(2,1)} %get-tuple-element.136), channel_id=1, source_target_pairs={{0,6},{2,0},{4,2},{6,4},{1,7},{3,1},{5,3},{7,5},{8,14},{10,8},{12,... | collective-permute-start | bytes 983048 | tf_op jit(solution)/shard_map/ppermute | solution.py:87
  244.4 15.7 %collective-permute-start.26 = (bf16[160,2048]{1,0:T(8,128)(2,1)}, bf16[160,2048]{1,0:T(8,128)(2,1)S(1)}, u32[]{:S(2)}, u32[]{:S(2)}) collective-permute-start(bf16[160,2048]{1,0:T(8,128)(2,1)} %get-tuple-element.137), channel_id=1, source_target_pairs={{0,2},{2,4},{4,6},{6,0},{1,3},{3,5},{5,7},{7,1},{8,10},{10,12},{12... | collective-permute-start | bytes 1966088 | tf_op jit(solution)/shard_map/ppermute | solution.py:108
  244.4 15.7 %collective-permute-start.27 = (bf16[160,2048]{1,0:T(8,128)(2,1)}, bf16[160,2048]{1,0:T(8,128)(2,1)S(1)}, u32[]{:S(2)}, u32[]{:S(2)}) collective-permute-start(bf16[160,2048]{1,0:T(8,128)(2,1)} %get-tuple-element.138), channel_id=1, source_target_pairs={{0,6},{2,0},{4,2},{6,4},{1,7},{3,1},{5,3},{7,5},{8,14},{10,8},{12,... | collective-permute-start | bytes 1966088 | tf_op jit(solution)/shard_map/ppermute | solution.py:108
  265.6 13.6 %collective-permute-start.29 = (bf16[160,2048]{1,0:T(8,128)(2,1)}, bf16[160,2048]{1,0:T(8,128)(2,1)S(1)}, u32[]{:S(2)}, u32[]{:S(2)}) collective-permute-start(bf16[160,2048]{1,0:T(8,128)(2,1)} %get-tuple-element.143.b0.refs_10_), channel_id=1, source_target_pairs={{0,6},{2,0},{4,2},{6,4},{1,7},{3,1},{5,3},{7,5},{8,14},{10,8},{12,... | collective-permute-start | bytes 1966088 | tf_op jit(solution)/shard_map/ppermute | solution.py:71
  267.8 14.3 %collective-permute-start.28 = (bf16[160,2048]{1,0:T(8,128)(2,1)}, bf16[160,2048]{1,0:T(8,128)(2,1)S(1)}, u32[]{:S(2)}, u32[]{:S(2)}) collective-permute-start(bf16[160,2048]{1,0:T(8,128)(2,1)} %get-tuple-element.143.b0.refs_10_), channel_id=1, source_target_pairs={{0,2},{2,4},{4,6},{6,0},{1,3},{3,5},{5,7},{7,1},{8,10},{10,12},{12... | collective-permute-start | bytes 1966088 | tf_op jit(solution)/shard_map/ppermute | solution.py:70
  282.1 13.1 %collective-permute-start.30 = (bf16[80,2048]{1,0:T(8,128)(2,1)S(1)}, bf16[80,2048]{1,0:T(8,128)(2,1)S(1)}, u32[]{:S(2)}, u32[]{:S(2)}) collective-permute-start(bf16[80,2048]{1,0:T(8,128)(2,1)S(1)} %slice.51), channel_id=1, source_target_pairs={{0,2},{2,4},{4,6},{6,0},{1,3},{3,5},{5,7},{7,1},{8,10},{10,12},{12... | collective-permute-start | bytes 983048 | tf_op jit(solution)/shard_map/ppermute | solution.py:74
  282.1 13.0 %collective-permute-start.31 = (bf16[80,2048]{1,0:T(8,128)(2,1)S(1)}, bf16[80,2048]{1,0:T(8,128)(2,1)}, u32[]{:S(2)}, u32[]{:S(2)}) collective-permute-start(bf16[80,2048]{1,0:T(8,128)(2,1)S(1)} %slice.52), channel_id=1, source_target_pairs={{0,6},{2,0},{4,2},{6,4},{1,7},{3,1},{5,3},{7,5},{8,14},{10,8},{12,... | collective-permute-start | bytes 983048 | tf_op jit(solution)/shard_map/ppermute | solution.py:75
  295.2 22.9 %collective-permute-start.32 = (bf16[160,2048]{1,0:T(8,128)(2,1)}, bf16[160,2048]{1,0:T(8,128)(2,1)S(1)}, u32[]{:S(2)}, u32[]{:S(2)}) collective-permute-start(bf16[160,2048]{1,0:T(8,128)(2,1)} %get-tuple-element.146), channel_id=1, source_target_pairs={{0,2},{2,4},{4,6},{6,0},{1,3},{3,5},{5,7},{7,1},{8,10},{10,12},{12... | collective-permute-start | bytes 1966088 | tf_op jit(solution)/shard_map/ppermute | solution.py:912
  295.3 22.8 %collective-permute-start.33 = (bf16[160,2048]{1,0:T(8,128)(2,1)}, bf16[160,2048]{1,0:T(8,128)(2,1)S(1)}, u32[]{:S(2)}, u32[]{:S(2)}) collective-permute-start(bf16[160,2048]{1,0:T(8,128)(2,1)} %get-tuple-element.148), channel_id=1, source_target_pairs={{0,6},{2,0},{4,2},{6,4},{1,7},{3,1},{5,3},{7,5},{8,14},{10,8},{12,... | collective-permute-start | bytes 1966088 | tf_op jit(solution)/shard_map/ppermute | solution.py:912
  318.1 9.0 %collective-permute-start.34 = (bf16[640,128]{1,0:T(8,128)(2,1)}, bf16[640,128]{1,0:T(8,128)(2,1)S(1)}, u32[]{:S(2)}, u32[]{:S(2)}) collective-permute-start(bf16[640,128]{1,0:T(8,128)(2,1)} %get-tuple-element.155), channel_id=1, source_target_pairs={{0,1},{1,0},{2,3},{3,2},{4,5},{5,4},{6,7},{7,6},{8,9},{9,8},{10,11... | collective-permute-start | bytes 491528 | tf_op jit(solution)/shard_map/ppermute | solution.py:917
  327.1 15.7 %collective-permute-start.35 = (bf16[4,2,1024,128]{3,2,1,0:T(8,128)(2,1)}, bf16[4,2,1024,128]{3,2,1,0:T(8,128)(2,1)S(1)}, u32[]{:S(2)}, u32[]{:S(2)}) collective-permute-start(bf16[4,2,1024,128]{3,2,1,0:T(8,128)(2,1)} %get-tuple-element.157), channel_id=1, source_target_pairs={{0,8},{8,0},{1,9},{9,1},{2,10},{10,2},{3,11},{11,3},{4,12},{12,4},... | collective-permute-start | bytes 6291464 | tf_op jit(solution)/shard_map/ppermute | solution.py:768
  348.1 23.2 %collective-permute-start.37 = (bf16[2,1168,128]{2,1,0:T(8,128)(2,1)}, bf16[2,1168,128]{2,1,0:T(8,128)(2,1)S(1)}, u32[]{:S(2)}, u32[]{:S(2)}) collective-permute-start(bf16[2,1168,128]{2,1,0:T(8,128)(2,1)} %get-tuple-element.163), channel_id=1, source_target_pairs={{0,64},{32,96},{64,0},{96,32},{1,65},{33,97},{65,1},{97,33},{2,66}... | collective-permute-start | bytes 1794056 | tf_op jit(solution)/shard_map/ppermute | solution.py:773
  350.9 46.0 %collective-permute-start.38 = (bf16[2,1168,128]{2,1,0:T(8,128)(2,1)}, bf16[2,1168,128]{2,1,0:T(8,128)(2,1)S(1)}, u32[]{:S(2)}, u32[]{:S(2)}) collective-permute-start(bf16[2,1168,128]{2,1,0:T(8,128)(2,1)} %get-tuple-element.164), channel_id=1, source_target_pairs={{0,32},{32,64},{64,96},{96,0},{1,33},{33,65},{65,97},{97,1},{2,34}... | collective-permute-start | bytes 1794056 | tf_op jit(solution)/shard_map/ppermute | solution.py:773
  352.4 45.2 %collective-permute-start.39 = (bf16[2,1168,128]{2,1,0:T(8,128)(2,1)}, bf16[2,1168,128]{2,1,0:T(8,128)(2,1)S(1)}, u32[]{:S(2)}, u32[]{:S(2)}) collective-permute-start(bf16[2,1168,128]{2,1,0:T(8,128)(2,1)} %get-tuple-element.165), channel_id=1, source_target_pairs={{0,96},{32,0},{64,32},{96,64},{1,97},{33,1},{65,33},{97,65},{2,98}... | collective-permute-start | bytes 1794056 | tf_op jit(solution)/shard_map/ppermute | solution.py:773
  403.9 11.3 %collective-permute-start.47 = (bf16[1168,128]{1,0:T(8,128)(2,1)}, bf16[1168,128]{1,0:T(8,128)(2,1)S(1)}, u32[]{:S(2)}, u32[]{:S(2)}) collective-permute-start(bf16[1168,128]{1,0:T(8,128)(2,1)} %get-tuple-element.182), channel_id=1, source_target_pairs={{0,17},{1,16},{16,1},{17,0},{2,19},{3,18},{18,3},{19,2},{4,21},{5,... | collective-permute-start | bytes 897032 | tf_op jit(solution)/shard_map/ppermute | solution.py:785
  406.9 15.3 %collective-permute-start.46 = (bf16[1168,128]{1,0:T(8,128)(2,1)}, bf16[1168,128]{1,0:T(8,128)(2,1)S(1)}, u32[]{:S(2)}, u32[]{:S(2)}) collective-permute-start(bf16[1168,128]{1,0:T(8,128)(2,1)} %get-tuple-element.182), channel_id=1, source_target_pairs={{0,1},{1,0},{2,3},{3,2},{4,5},{5,4},{6,7},{7,6},{8,9},{9,8},{10,11... | collective-permute-start | bytes 897032 | tf_op jit(solution)/shard_map/ppermute | solution.py:784
  406.9 21.4 %collective-permute-start.45 = (bf16[1168,128]{1,0:T(8,128)(2,1)}, bf16[1168,128]{1,0:T(8,128)(2,1)S(1)}, u32[]{:S(2)}, u32[]{:S(2)}) collective-permute-start(bf16[1168,128]{1,0:T(8,128)(2,1)} %get-tuple-element.181.a), channel_id=1, source_target_pairs={{0,16},{16,0},{1,17},{17,1},{2,18},{18,2},{3,19},{19,3},{4,20},{20... | collective-permute-start | bytes 897032 | tf_op jit(solution)/shard_map/ppermute | solution.py:783
  412.5 38.9 %collective-permute-start.43 = (bf16[160,2048]{1,0:T(8,128)(2,1)}, bf16[160,2048]{1,0:T(8,128)(2,1)}, u32[]{:S(2)}, u32[]{:S(2)}) collective-permute-start(bf16[160,2048]{1,0:T(8,128)(2,1)} %get-tuple-element.178), channel_id=1, source_target_pairs={{0,2},{2,4},{4,6},{6,0},{1,3},{3,5},{5,7},{7,1},{8,10},{10,12},{12... | collective-permute-start | bytes 1966088 | tf_op jit(solution)/shard_map/ppermute | solution.py:108
  412.5 39.0 %collective-permute-start.44 = (bf16[160,2048]{1,0:T(8,128)(2,1)}, bf16[160,2048]{1,0:T(8,128)(2,1)}, u32[]{:S(2)}, u32[]{:S(2)}) collective-permute-start(bf16[160,2048]{1,0:T(8,128)(2,1)} %get-tuple-element.179), channel_id=1, source_target_pairs={{0,6},{2,0},{4,2},{6,4},{1,7},{3,1},{5,3},{7,5},{8,14},{10,8},{12,... | collective-permute-start | bytes 1966088 | tf_op jit(solution)/shard_map/ppermute | solution.py:108
  431.8 28.3 %collective-permute-start.40 = (bf16[160,2048]{1,0:T(8,128)(2,1)}, bf16[160,2048]{1,0:T(8,128)(2,1)S(1)}, u32[]{:S(2)}, u32[]{:S(2)}) collective-permute-start(bf16[160,2048]{1,0:T(8,128)(2,1)} %get-tuple-element.167), channel_id=1, source_target_pairs={{0,4},{2,6},{4,0},{6,2},{1,5},{3,7},{5,1},{7,3},{8,12},{10,14},{12... | collective-permute-start | bytes 1966088 | tf_op jit(solution)/shard_map/ppermute | solution.py:930
  431.8 8.5 %collective-permute-start.49 = (bf16[1168,128]{1,0:T(8,128)(2,1)}, bf16[1168,128]{1,0:T(8,128)(2,1)S(1)}, u32[]{:S(2)}, u32[]{:S(2)}) collective-permute-start(bf16[1168,128]{1,0:T(8,128)(2,1)} %sum_z.1.refs_0_), channel_id=1, source_target_pairs={{0,64},{32,96},{64,0},{96,32},{1,65},{33,97},{65,1},{97,33},{2,66}... | collective-permute-start | bytes 897032 | tf_op jit(solution)/shard_map/ppermute | solution.py:789
  440.3 11.7 %collective-permute-start.51 = (bf16[1168,128]{1,0:T(8,128)(2,1)}, bf16[1168,128]{1,0:T(8,128)(2,1)S(1)}, u32[]{:S(2)}, u32[]{:S(2)}) collective-permute-start(bf16[1168,128]{1,0:T(8,128)(2,1)} %sum_z.1.refs_0_), channel_id=1, source_target_pairs={{0,8},{8,0},{1,9},{9,1},{2,10},{10,2},{3,11},{11,3},{4,12},{12,4},... | collective-permute-start | bytes 897032 | tf_op jit(solution)/shard_map/ppermute | solution.py:790
  (65 other events, 556.7 us)
Sparse Core Ops, SparseCore 0:
  84.3 40.9 all-gather.2
  215.7 116.3 reduce-scatter.1
  348.2 77.6 all-gather.4

commit v10 on v9

--- a/solution.py
+++ b/solution.py
@@ -464,7 +464,7 @@
 
 
 def ffn_body(
-    idx, n0, n1, n2a, n2b, n3, c0, c1, c2a, c2b, c3, gate_own, up_own, gate_par, up_par, w0, w1, w2,
+    idx, n0, n1, n2a, n2b, n3, c0, c1, c2, c3, gate_own, up_own, gate_par, up_par, w0, w1, w2,
     hid, dgate, dup, n_all, c_all, down, sem,
 ):
     i = pl.program_id(0)
@@ -475,9 +475,10 @@
         copies = load_down(idx, (w0, w1, w2), down, sem)
         for c in copies:
             c.start()
-        for refs, dst in (((n0, n1, n2a, n2b, n3), n_all), ((c0, c1, c2a, c2b, c3), c_all)):
-            for ref, row, (_, n) in zip(refs, PIECE_ROW, PIECES):
-                dst[row : row + n, :] = ref[...]
+        for ref, row, (_, n) in zip((n0, n1, n2a, n2b, n3), PIECE_ROW, PIECES):
+            n_all[row : row + n, :] = ref[...]
+        for d, ref in enumerate((c0, c1, c2, c3)):
+            c_all[d * BLK : (d + 1) * BLK, :] = ref[...]
         for c in copies:
             c.wait()
 
@@ -505,7 +506,8 @@
         grid=(TILES,),
         out_shape=(sds((ROWS, FF4)),) * 3,
         in_specs=[spec(pltpu.SMEM)]
-        + [whole(n, D) for _, n in PIECES] * 2
+        + [whole(n, D) for _, n in PIECES]
+        + [whole(BLK, D)] * 4
         + [column(0), column(0), column(0), column(TILES)]
         + [spec(pl.ANY)] * 3,
         out_specs=[hidden] * 3,
@@ -585,14 +587,9 @@
 QS = 4
 
 
-def ffn_grads_body(*refs):
-    na, nb, cots = refs[0:5], refs[5:10], refs[10:15]
-    hid, dgate, dup, out, hid_t = refs[15:]
-
-    @pl.when(pl.program_id(0) == 0)
-    def _():
-        hid_t[...] = hid[...].T
-
+def gate_up_grads_body(*refs):
+    na, nb = refs[0:5], refs[5:10]
+    dgate, dup, _, out = refs[10:]
     stack = lambda parts: jnp.concatenate([r[...] for r in parts], 0)
     rows = jnp.concatenate([stack(na), stack(nb)], 1).T
     for k, ref in enumerate((dgate, dup)):
@@ -603,29 +600,51 @@
                 for c in range(FF4 // 128):
                     first = k * GU_ROWS + c * 64
                     out[h, q, first : first + 64, :] = r[:, c * 128 : (c + 1) * 128]
-    g = dot(hid_t[...], stack(cots)).astype(BF16)
-    for h in range(2):
-        for q in range(QS):
-            out[h, q, 2 * GU_ROWS :, :] = g[
-                h * (FF4 // 2) : (h + 1) * (FF4 // 2), q * 128 : (q + 1) * 128
-            ]
-
-
-def ffn_grads(normed, cots, hid, dgate, dup):
-    return pl.pallas_call(
-        ffn_grads_body,
+
+
+def gate_up_grads(normed, dgate, dup, pieces):
+    return pl.pallas_call(
+        gate_up_grads_body,
         grid=(16 // QS,),
         out_shape=sds((2, 16, PIECE, 128)),
         in_specs=[pl.BlockSpec((n, 64 * QS), lambda i: (0, i)) for _, n in PIECES]
         + [pl.BlockSpec((n, 64 * QS), lambda i: (0, i + 16 // QS)) for _, n in PIECES]
-        + [pl.BlockSpec((n, 128 * QS), lambda i: (0, i)) for _, n in PIECES]
-        + [whole(ROWS, FF4)] * 3,
-        out_specs=pl.BlockSpec((2, QS, PIECE, 128), lambda i: (0, i, 0, 0)),
+        + [whole(ROWS, FF4)] * 2
+        + [spec(pl.ANY)],
+        out_specs=pl.BlockSpec((2, QS, 2 * GU_ROWS, 128), lambda i: (0, i, 0, 0)),
+        input_output_aliases={12: 0},
+        compiler_params=params(),
+        cost_estimate=cost(4 * ROWS * D * FF4, 2e7),
+        name="gate_up_grads",
+    )(*normed, *normed, dgate, dup, pieces)
+
+
+def down_grads_body(*refs):
+    cots = refs[0:4]
+    hid, out, hid_t = refs[4:]
+
+    @pl.when(pl.program_id(0) == 0)
+    def _():
+        hid_t[...] = hid[...].T
+
+    g = dot(hid_t[...], jnp.concatenate([r[...] for r in cots], 0)).astype(BF16)
+    for h in range(2):
+        for q in range(QS):
+            out[h, q, :, :] = g[h * (FF4 // 2) : (h + 1) * (FF4 // 2), q * 128 : (q + 1) * 128]
+
+
+def down_grads(cots, hid):
+    return pl.pallas_call(
+        down_grads_body,
+        grid=(16 // QS,),
+        out_shape=sds((2, 16, PIECE, 128)),
+        in_specs=[pl.BlockSpec((BLK, 128 * QS), lambda i: (0, i))] * 4 + [whole(ROWS, FF4)],
+        out_specs=pl.BlockSpec((2, QS, FF4 // 2, 128), lambda i: (0, i, 2, 0)),
         scratch_shapes=[pltpu.VMEM((FF4, ROWS), BF16)],
         compiler_params=params(),
-        cost_estimate=cost(6 * ROWS * D * FF4, 3e7),
-        name="ffn_grads",
-    )(*normed, *normed, *cots, hid, dgate, dup)
+        cost_estimate=cost(2 * ROWS * D * FF4, 1e7),
+        name="down_grads",
+    )(*cots, hid)
 
 
 def unpack_body(piece, gate, up, down):
@@ -815,15 +834,29 @@
     res = add[...].astype(F32) + r * pulled - v * (r * r * r) * inner
     out[...] = res
     low[...] = res.astype(BF16)
-    gain_grad[...] = jnp.sum(grad * v * r, axis=0, keepdims=True)
+    part = jnp.sum(grad * v * r, axis=0, keepdims=True)
+
+    @pl.when(pl.program_id(0) == 0)
+    def _():
+        gain_grad[...] = part
+
+    @pl.when(pl.program_id(0) > 0)
+    def _():
+        gain_grad[...] += part
 
 
 def row_call(body, out_shape, *args, name):
+    block = lambda v: (
+        pl.BlockSpec((HALF, D), lambda i: (i, 0))
+        if v.shape[0] == BLK
+        else pl.BlockSpec((1, D), lambda i: (0, 0))
+    )
     return pl.pallas_call(
         body,
+        grid=(2,),
         out_shape=out_shape,
-        in_specs=[spec()] * len(args),
-        out_specs=tuple(spec() for _ in out_shape),
+        in_specs=[block(v) for v in args],
+        out_specs=tuple(block(v) for v in out_shape),
         compiler_params=params(),
         cost_estimate=cost(1e6, 5e6),
         name=name,
@@ -861,31 +894,34 @@
 
     qkv_got = fetch_half(qkv_weight, core)
     normed_one = gather_x((tok * s_one * gain_one).astype(BF16), (cosine,))
-    qkv_all = qkv_weight, qkv_got, lax.ppermute(tie(qkv_got, normed_one[2], normed_one[3]), "core", shift(2, 1))
-    out_all = fetch_partner(out_weight, core, qkv_got)
+    out_got = fetch_half(out_weight, core)
+    swap = lambda v, *deps: lax.ppermute(tie(v, *deps), "core", shift(2, 1))
+    qkv_all = qkv_weight, qkv_got, swap(qkv_got, out_got, normed_one[2], normed_one[3])
 
     q, kv_own = qkv_forward(idx, normed_one, qkv_all, cosine, sine)
-    cots = gather_x(tie(cotangent, normed_one[2], normed_one[3]), (kv_own,))
+    cot = tie(cotangent, normed_one[2], normed_one[3])
+    cots = [cotangent] + [lax.ppermute(cot, "x", shift(4, -k)) for k in (1, 2, 3)]
+    kv_par = lax.ppermute(kv_own, "zh", shift(2, 1))
+    out_all = out_weight, out_got, swap(out_got, kv_own)
     rows = DH // 8
     mine = lambda w: lax.dynamic_slice_in_dim(w, (y * 2 + core) * rows, rows, 0)
     cross = [(2 * a + b, 2 * (1 - a) + (1 - b)) for a in range(2) for b in range(2)]
     gate_up = lax.ppermute(
         jnp.concatenate(
             [
-                tie(mine(gate_weight), normed_one[2], normed_one[3]),
+                mine(tie(gate_weight, kv_own)),
                 jnp.zeros((rows, GAP - FF4), BF16),
-                mine(up_weight),
+                mine(tie(up_weight, kv_own)),
             ],
             1,
         ),
         ("zl", "zh"),
         cross,
     )
-    kv_par = lax.ppermute(kv_own, "zh", shift(2, 1))
-    down_got = fetch_half(tie(down_weight, gate_up), core)
-    att, qx = attend(idx, tie(q, cots[2], cots[3], out_all[1]), kv_own, kv_par, first)
-    gate_up = lax.all_gather(tie(gate_up, qx), ("y", "core"), axis=0, tiled=True)
-    parts = out_project(idx, att, out_all)
+    att, qx = attend(idx, q, kv_own, kv_par, first)
+    parts = out_project(idx, tie(att, *cots), out_all)
+    down_got = fetch_half(tie(down_weight, parts[2]), core)
+    gate_up = lax.all_gather(tie(gate_up, parts[2]), ("y", "core"), axis=0, tiled=True)
     after_attn, normed_two = row_call(
         norm_two_body,
         (sds((BLK, D), F32), sds((BLK, D))),
@@ -894,16 +930,19 @@
     normed_two = gather_x(tie(normed_two, down_got))
     down_all = down_weight, down_got, lax.ppermute(tie(down_got, normed_two[1], normed_two[4]), "core", shift(2, 1))
     hid, dgate, dup = ffn(idx, normed_two, cots, gate_weight, up_weight, gate_up, down_all)
-    own_grads = ffn_grads(normed_two, cots, hid, dgate, dup)
+    d_parts = ffn_back(idx, dgate, dup, gate_weight, up_weight, gate_up)
+    own_grads = down_grads(cots, tie(hid, d_parts[2]))
+    d_own, q1, q3 = relay(d_parts)
+    own_grads = gate_up_grads(normed_two, tie(dgate, q1, q3), dup, own_grads)
+    d_two = last_step(d_own, q1, q3)
     grads = lax.psum_scatter(
-        own_grads.reshape(32, PIECE, 128), ("zh", "zl", "y", "core"), scatter_dimension=0, tiled=True
+        tie(own_grads, *d_two).reshape(32, PIECE, 128),
+        ("zh", "zl", "y", "core"), scatter_dimension=0, tiled=True,
     )
     after_grad, branch, gain_grad_two = row_call(
         norm_back_body,
         (sds((BLK, D), F32), sds((BLK, D)), sds((1, D), F32)),
-        cotangent, after_attn,
-        *scatter_x(ffn_back(idx, tie(dgate, own_grads), dup, gate_weight, up_weight, gate_up)),
-        gain_two.reshape(1, D), name="norm_back_two",
+        cotangent, after_attn, *d_two, gain_two.reshape(1, D), name="norm_back_two",
     )
     branch = gather_x(branch)
     layer_parts = down_project(idx, tie(hid, after_grad), down_all)
@@ -928,7 +967,7 @@
         idx, (tail[0], tie(tail[1], dkv_got)), tail_kv, parts
     )
     layer.append(lax.ppermute(tie(layer_parts[2], summed), "x", shift(4, 2)))
-    grads = lax.all_gather(tie(grads, cores_summed), ("zl", "y", "core"), axis=0, tiled=True)
+    grads = lax.all_gather(tie(grads, summed), ("zl", "y", "core"), axis=0, tiled=True)
     grad_gate, grad_up, grad_down = unpack(grads)
     _, input_grad, _ = row_call(
         norm_back_body,

time: 486 us -> 466 us (0.959); the launches traced: 483 us -> 458 us
  waiting for transfers between devices: 168 us -> 139 us
  starting transfers between devices: 100 us -> 106 us
    ppermute x3, waiting for transfers between devices: 44.1 us -> 28.9 us  [sum_tail(): got = [lax.ppermute(g[s], 'y', shift(4, s)) for s in (2, 1, 3)]]
    ppermute x3, waiting for transfers between devices: 26.9 us -> 13.2 us  [last_step(): lax.ppermute(q1, 'x', shift(4, 1))]
    ppermute x4 -> x3, starting transfers between devices: 21.4 us -> 7.81 us  [gather_x(): opp_b = lax.ppermute(send_b, 'x', shift(4, -1))]
    ppermute x3, waiting for transfers between devices: 0.38 us -> 13.2 us  [fetch_half(): lax.ppermute(lax.dynamic_slice_in_dim(w, core * half, half, 0), 'zh', shi...]
    ppermute x4, starting transfers between devices: 9.18 us -> 21.5 us  [sum_tail(): theirs = [lax.ppermute(v, 'core', shift(2, 1)) for v in [g] + mine[1:]]]
    reduce_scatter x1, waiting for transfers between devices: 0.01 us -> 10.9 us  [on_device(): lax.psum_scatter(tie(own_grads, *d_two).reshape(32, PIECE, 128), ('zh', '...]
    ppermute x3, waiting for transfers between devices: 16 us -> 5.86 us  [relay(): got_a = lax.ppermute(p2a, 'x', shift(4, 1))]
    ppermute x1, waiting for transfers between devices: 6.93 us -> 0.01 us  [sum_tail(): lax.ppermute(other, 'zh', shift(2, 1))]
  transfers between devices with their start and end apart: 61 -> 60, of which waited for: 27 -> 24; matrix products, arithmetic and copies ran while one was open for 3% -> 3% of each run, Pallas kernels for 24% -> 26%
where the time goes in v10:
time: 466 us; the launch traced here: 458 us
  Pallas kernels  167 us (36%)
  waiting for transfers between devices  139 us (30%)
  starting transfers between devices  106 us (23%)
  local copies, waits for them, and re-layouts  22.3 us (5%)
  between operations  14.7 us (3%)
  other arithmetic  8.57 us (2%)
    ppermute x3, waiting for transfers between devices, sum_tail(): got = [lax.ppermute(g[s], 'y', shift(4, s)) for s in (2, 1, 3)]  28.9 us
    ppermute x4, starting transfers between devices, sum_tail(): theirs = [lax.ppermute(v, 'core', shift(2, 1)) for v in [g] + mine[1:]]  21.5 us
    pallas_call x1, Pallas kernels, ffn(): pl.pallas_call(ffn_body, grid=(TILES,), out_shape=(sds((ROWS, FF4)),) * 3...  20.8 us
    pallas_call x1, Pallas kernels, attend_back(): pl.pallas_call(attend_back_body, out_shape=(sds((4, BLK, AW)), sds((ROWS,...  20.4 us
    ppermute x3, waiting for transfers between devices, gather_x(): from_prev = lax.ppermute(v, 'x', shift(4, 1))  16.8 us
    pallas_call x1, Pallas kernels, ffn_back(): pl.pallas_call(ffn_back_body, grid_spec=pltpu.PrefetchScalarGridSpec(num_...  15.4 us
    pallas_call x1, Pallas kernels, gate_up_grads(): pl.pallas_call(gate_up_grads_body, grid=(16 // QS,), out_shape=sds((2, 16...  14.6 us
    ppermute x3, waiting for transfers between devices, fetch_half(): lax.ppermute(lax.dynamic_slice_in_dim(w, core * half, half, 0), 'zh', shi...  13.2 us
  transfers between devices with their start and end apart: 60, of which 24 were waited for; matrix products, arithmetic and copies ran while one was open for 3% of the time, Pallas kernels for 26%

profile of v10, /device:TPU:1, one launch (start us, length us, event | category | flops | bytes accessed | tf_op | source)
XLA Modules:
  0.0 458.1 jit_solution(5726151718931744912)
XLA Ops:
  15.3 3.7 collective-permute-start.5
  24.1 3.4 collective-permute-done.1.n3.refs_4_.refs_9_
  31.1 13.2 %collective-permute-done.4.w1 = bf16[512,640]{1,0:T(8,128)(2,1)S(1)} collective-permute-done((bf16[512,640]{1,0:T(8,128)(2,1)}, bf16[512,640]{1,0:T(8,128)(2,1)S(1)}, u32[]{:S(2)}, u32[]{:S(2)}) %collective-permute-start.4) | collective-permute-done | bytes 655392 | tf_op jit(solution)/shard_map/ppermute | solution.py:134
  52.0 6.8 %qkv_forward.1 = (bf16[4,1280,128]{2,1,0:T(8,128)(2,1)}, bf16[640,128]{1,0:T(8,128)(2,1)}) custom-call(s32[4]{0:T(128)} %pad_add_fusion.idx, bf16[160,2048]{1,0:T(8,128)(2,1)} %copy-done.4, bf16[160,2048]{1,0:T(8,128)(2,1)} %collective-permute-done.n1.refs_1_.refs_6_, bf16[80,2048]{1,0:T(8,128)(2,1)} %copy-done.22, bf16[80,2048]{1,0:T(8,128)(2,1)} %copy-done.21, ...), custom_call_target="tpu_custom_call" | custom-call | flops 1677721600 | bytes 7000000 | tf_op jit(solution)/shard_map/qkv_forward/pallas_call | solution.py:175
  58.7 3.0 collective-permute-start.7
  65.3 3.0 collective-permute-start.21
  68.4 8.6 %attend.1 = (bf16[4,160,512]{2,1,0:T(8,128)(2,1)}, bf16[4,1280,128]{2,1,0:T(8,128)(2,1)}) custom-call(s32[4]{0:T(128)} %pad_add_fusion.idx, bf16[4,1280,128]{2,1,0:T(8,128)(2,1)} %get-tuple-element.104.q, bf16[640,128]{1,0:T(8,128)(2,1)} %get-tuple-element.105.kv_own, bf16[640,128]{1,0:T(8,128)(2,1)} %copy-done.52, s32[1,1280]{1,0:T(1,128)} %reshape_tile.3.first), custom_call_target="tpu_custom_call" | custom-call | flops 12000000000 | bytes 3000000 | tf_op jit(solution)/shard_map/attend/pallas_call | solution.py:268
  80.1 4.8 %out_project.1 = (bf16[160,2048]{1,0:T(8,128)(2,1)}, bf16[160,2048]{1,0:T(8,128)(2,1)}, bf16[80,2048]{1,0:T(8,128)(2,1)}, bf16[80,2048]{1,0:T(8,128)(2,1)}, bf16[160,2048]{1,0:T(8,128)(2,1)}) custom-call(s32[4]{0:T(128)} %pad_add_fusion.idx, bf16[4,160,512]{2,1,0:T(8,128)(2,1)} %get-tuple-element.151.att, bf16[256,2048]{1,0:T(8,128)(2,1)} %w0.10, ...), custom_call_target="tpu_custom_call" | custom-call | flops 1342177280 | bytes 5500000 | tf_op jit(solution)/shard_map/out_project/pallas_call | solution.py:305
  87.4 3.1 collective-permute-start.16
  90.5 3.2 collective-permute-start.13
  93.7 6.3 %collective-permute-done.13.got_b = bf16[80,2048]{1,0:T(8,128)(2,1)S(1)} collective-permute-done((bf16[80,2048]{1,0:T(8,128)(2,1)S(1)}, bf16[80,2048]{1,0:T(8,128)(2,1)S(1)}, u32[]{:S(2)}, u32[]{:S(2)}) %collective-permute-start.13) | collective-permute-done | bytes 327712 | tf_op jit(solution)/shard_map/ppermute | solution.py:87
  100.0 3.2 collective-permute-done.12.got_a
  106.1 2.7 collective-permute-start.15
  108.8 13.2 %collective-permute-done.14.b = bf16[160,2048]{1,0:T(8,128)(2,1)S(1)} collective-permute-done((bf16[160,2048]{1,0:T(8,128)(2,1)}, bf16[160,2048]{1,0:T(8,128)(2,1)S(1)}, u32[]{:S(2)}, u32[]{:S(2)}) %collective-permute-start.14) | collective-permute-done | bytes 655392 | tf_op jit(solution)/shard_map/ppermute | solution.py:108
  123.0 2.9 norm_two.1
  126.0 2.7 collective-permute-start.17
  128.7 12.3 %collective-permute-done.18.n3.refs_4_.refs_9_ = bf16[160,2048]{1,0:T(8,128)(2,1)S(1)} collective-permute-done((bf16[160,2048]{1,0:T(8,128)(2,1)}, bf16[160,2048]{1,0:T(8,128)(2,1)S(1)}, u32[]{:S(2)}, u32[]{:S(2)}) %collective-permute-start.18) | collective-permute-done | bytes 655392 | tf_op jit(solution)/shard_map/ppermute | solution.py:70
  141.0 3.7 collective-permute-start.22
  144.7 2.7 collective-permute-start.20
  147.8 6.7 %collective-permute-done.20.n2b.refs_3_.refs_8_ = bf16[80,2048]{1,0:T(8,128)(2,1)S(1)} collective-permute-done((bf16[80,2048]{1,0:T(8,128)(2,1)S(1)}, bf16[80,2048]{1,0:T(8,128)(2,1)S(1)}, u32[]{:S(2)}, u32[]{:S(2)}) %collective-permute-start.20) | collective-permute-done | bytes 327712 | tf_op jit(solution)/shard_map/ppermute | solution.py:75
  154.5 3.5 collective-permute-done.19.n2a.refs_2_.refs_7_
  159.3 20.8 %ffn.1 = (bf16[640,1408]{1,0:T(8,128)(2,1)}, bf16[640,1408]{1,0:T(8,128)(2,1)}, bf16[640,1408]{1,0:T(8,128)(2,1)}) custom-call(s32[4]{0:T(128)} %pad_add_fusion.idx, bf16[160,2048]{1,0:T(8,128)(2,1)} %get-tuple-element.120.n0.refs_0_.refs_5_, bf16[160,2048]{1,0:T(8,128)(2,1)} %copy-done.2, bf16[80,2048]{1,0:T(8,128)(2,1)} %copy-done.9, ...), custom_call_target="tpu_custom_call" | custom-call | flops 11072962560 | bytes 34000000 | tf_op jit(solution)/shard_map/ffn/pallas_call | solution.py:504
  180.1 15.4 %ffn_back.1 = (bf16[160,2048]{1,0:T(8,128)(2,1)}, bf16[160,2048]{1,0:T(8,128)(2,1)}, bf16[80,2048]{1,0:T(8,128)(2,1)}, bf16[80,2048]{1,0:T(8,128)(2,1)}, bf16[160,2048]{1,0:T(8,128)(2,1)}) custom-call(s32[4]{0:T(128)} %pad_add_fusion.idx, bf16[640,1408]{1,0:T(8,128)(2,1)} %get-tuple-element.186.dgate.refs_10_, ...), custom_call_target="tpu_custom_call" | custom-call | flops 7381975040 | bytes 18000000 | tf_op jit(solution)/shard_map/ffn_back/pallas_call | solution.py:570
  198.2 9.1 %down_grads.1.refs_12_ = bf16[2,16,2112,128]{3,2,1,0:T(8,128)(2,1)} custom-call(bf16[160,2048]{1,0:T(8,128)(2,1)} %refs_0_.1, bf16[160,2048]{1,0:T(8,128)(2,1)} %collective-permute-done.8.c1.refs_1_, bf16[160,2048]{1,0:T(8,128)(2,1)} %collective-permute-done.9.c2.refs_2_, bf16[160,2048]{1,0:T(8,128)(2,1)} %collective-permute-done.10.c3.refs_3_, ...), custom_call_target="tpu_custom_call" | custom-call | flops 3690987520 | bytes 10000000 | tf_op jit(solution)/shard_map/down_grads/pallas_call | solution.py:637
  210.5 2.7 collective-permute-start.26
  213.2 14.6 %gate_up_grads.1 = bf16[2,16,2112,128]{3,2,1,0:T(8,128)(2,1)} custom-call(bf16[160,2048]{1,0:T(8,128)(2,1)} %get-tuple-element.120.n0.refs_0_.refs_5_, bf16[160,2048]{1,0:T(8,128)(2,1)} %copy-done.2, bf16[80,2048]{1,0:T(8,128)(2,1)} %copy-done.9, bf16[80,2048]{1,0:T(8,128)(2,1)} %copy-done.8, ...), custom_call_target="tpu_custom_call", output_to_operand_aliasing={{}: (12, {})} | custom-call | flops 7381975040 | bytes 20000000 | tf_op jit(solution)/shard_map/gate_up_grads/pallas_call | solution.py:606
  228.9 4.0 norm_back_two.1
  234.5 12.7 %collective-permute-done.28.b1.refs_11_ = bf16[160,2048]{1,0:T(8,128)(2,1)S(1)} collective-permute-done((bf16[160,2048]{1,0:T(8,128)(2,1)}, bf16[160,2048]{1,0:T(8,128)(2,1)S(1)}, u32[]{:S(2)}, u32[]{:S(2)}) %collective-permute-start.28) | collective-permute-done | bytes 655392 | tf_op jit(solution)/shard_map/ppermute | solution.py:71
  248.5 2.8 collective-permute-start.30
  251.3 10.5 %down_project.1 = (bf16[160,2048]{1,0:T(8,128)(2,1)}, bf16[160,2048]{1,0:T(8,128)(2,1)}, bf16[160,2048]{1,0:T(8,128)(2,1)}, bf16[160,2048]{1,0:T(8,128)(2,1)}) custom-call(s32[4]{0:T(128)} %pad_add_fusion.idx, bf16[640,1408]{1,0:T(8,128)(2,1)} %get-tuple-element.187.hid.refs_4_, bf16[704,2048]{1,0:T(8,128)(2,1)} %w0.9, ...), custom_call_target="tpu_custom_call" | custom-call | flops 3690987520 | bytes 11000000 | tf_op jit(solution)/shard_map/down_project/pallas_call | solution.py:540
  264.6 20.4 %attend_back.1 = (bf16[4,160,512]{2,1,0:T(8,128)(2,1)}, f32[640,128]{1,0:T(8,128)}, bf16[640,128]{1,0:T(8,128)(2,1)}) custom-call(s32[4]{0:T(128)} %pad_add_fusion.idx, bf16[4,1280,128]{2,1,0:T(8,128)(2,1)} %get-tuple-element.148.qx, bf16[640,128]{1,0:T(8,128)(2,1)} %get-tuple-element.105.kv_own, bf16[640,128]{1,0:T(8,128)(2,1)} %copy-done.52, ...), custom_call_target="tpu_custom_call" | custom-call | flops 30000001024 | bytes 8000000 | tf_op jit(solution)/shard_map/attend_back/pallas_call | solution.py:377
  285.1 8.9 %attn_grads.1 = (bf16[4,2,1024,128]{3,2,1,0:T(8,128)(2,1)}, bf16[4,2,1024,128]{3,2,1,0:T(8,128)(2,1)}) custom-call(s32[4]{0:T(128)} %pad_add_fusion.idx, bf16[160,2048]{1,0:T(8,128)(2,1)} %copy-done.4, bf16[160,2048]{1,0:T(8,128)(2,1)} %collective-permute-done.n1.refs_1_.refs_6_, bf16[80,2048]{1,0:T(8,128)(2,1)} %copy-done.22, bf16[80,2048]{1,0:T(8,128)(2,1)} %copy-done.21, ...), custom_call_target="tpu_custom_call" | custom-call | flops 2684354560 | bytes 10000000 | tf_op jit(solution)/shard_map/attn_grads/pallas_call | solution.py:716
  294.4 6.0 %collective-permute-start.34 = (bf16[4,2,1024,128]{3,2,1,0:T(8,128)(2,1)}, bf16[4,2,1024,128]{3,2,1,0:T(8,128)(2,1)S(1)}, u32[]{:S(2)}, u32[]{:S(2)}) collective-permute-start(bf16[4,2,1024,128]{3,2,1,0:T(8,128)(2,1)} %get-tuple-element.156), channel_id=1, source_target_pairs={{0,8},{8,0},{1,9},{9,1},{2,10},{10,2},{3,11},{11,3},{4,12},{12,4},... | collective-permute-start | bytes 6291464 | tf_op jit(solution)/shard_map/ppermute | solution.py:787
  300.5 7.2 %qkv_back.1 = (bf16[4,2,144,128]{3,2,1,0:T(8,128)(2,1)}, bf16[4,2,144,128]{3,2,1,0:T(8,128)(2,1)}, bf16[160,2048]{1,0:T(8,128)(2,1)}, bf16[160,2048]{1,0:T(8,128...) custom-call(s32[4]{0:T(128)} %pad_add_fusion.idx, ...), custom_call_target="tpu_custom_call" | custom-call | flops 1677721600 | bytes 13000000 | tf_op jit(solution)/shard_map/qkv_back/pallas_call | solution.py:434
  311.2 4.0 sum_core.1
  315.2 3.0 collective-permute-start.36
  320.9 16.1 %collective-permute-done.36.b = bf16[2,1168,128]{2,1,0:T(8,128)(2,1)S(1)} collective-permute-done((bf16[2,1168,128]{2,1,0:T(8,128)(2,1)}, bf16[2,1168,128]{2,1,0:T(8,128)(2,1)S(1)}, u32[]{:S(2)}, u32[]{:S(2)}) %collective-permute-start.36) | collective-permute-done | bytes 598048 | tf_op jit(solution)/shard_map/ppermute | solution.py:792
  337.0 12.8 %collective-permute-done.37.c = bf16[2,1168,128]{2,1,0:T(8,128)(2,1)S(1)} collective-permute-done((bf16[2,1168,128]{2,1,0:T(8,128)(2,1)}, bf16[2,1168,128]{2,1,0:T(8,128)(2,1)S(1)}, u32[]{:S(2)}, u32[]{:S(2)}) %collective-permute-start.37) | collective-permute-done | bytes 598048 | tf_op jit(solution)/shard_map/ppermute | solution.py:792
  350.8 2.7 sum_y.1
  353.5 10.9 %reduce-scatter.2.cloned.1.call-done = bf16[1,2112,128]{2,1,0:T(8,128)(2,1)} async-done(((bf16[32,2112,128]{2,1,0:T(8,128)(2,1)}), bf16[1,2112,128]{2,1,0:T(8,128)(2,1)}) %reduce-scatter.2.cloned.1.call-update) | async-done | bytes 540688 | tf_op jit(solution)/shard_map/reduce_scatter | solution.py:938
  381.2 4.1 collective-permute-done.44.b
  390.9 9.2 %collective-permute-done.49.refs_3_ = bf16[1168,128]{1,0:T(8,128)(2,1)S(1)} collective-permute-done((bf16[1168,128]{1,0:T(8,128)(2,1)}, bf16[1168,128]{1,0:T(8,128)(2,1)S(1)}, u32[]{:S(2)}, u32[]{:S(2)}) %collective-permute-start.49) | collective-permute-done | bytes 299040 | tf_op jit(solution)/shard_map/ppermute | solution.py:808
  400.1 3.3 collective-permute-start.47
  404.4 13.9 %collective-permute-start.50 = (bf16[1168,128]{1,0:T(8,128)(2,1)}, bf16[1168,128]{1,0:T(8,128)(2,1)S(1)}, u32[]{:S(2)}, u32[]{:S(2)}) collective-permute-start(bf16[1168,128]{1,0:T(8,128)(2,1)} %sum_z.1.refs_0_), channel_id=1, source_target_pairs={{0,8},{8,0},{1,9},{9,1},{2,10},{10,2},{3,11},{11,3},{4,12},{12,4},... | collective-permute-start | bytes 897032 | tf_op jit(solution)/shard_map/ppermute | solution.py:809
  418.3 7.1 %collective-permute-start.53 = (bf16[1168,128]{1,0:T(8,128)(2,1)S(1)}, bf16[1168,128]{1,0:T(8,128)(2,1)S(1)}, u32[]{:S(2)}, u32[]{:S(2)}) collective-permute-start(bf16[1168,128]{1,0:T(8,128)(2,1)S(1)} %collective-permute-done.49.refs_3_), channel_id=1, source_target_pairs={{0,8},{8,0},{1,9},{9,1},{2,10},{10,2},{3,11},{11,3},{4,12},{12,4},... | collective-permute-start | bytes 897032 | tf_op jit(solution)/shard_map/ppermute | solution.py:809
  428.1 4.2 unpack_tail.1
  436.8 3.9 norm_back_one.1
  441.4 9.8 %unpack.1 = (f32[1024,1408]{1,0:T(8,128)}, f32[1024,1408]{1,0:T(8,128)}, f32[704,2048]{1,0:T(8,128)}) custom-call(bf16[16,2112,128]{2,1,0:T(8,128)(2,1)} %all-gather.5.cloned.1.call-done.piece), custom_call_target="tpu_custom_call" | custom-call | flops 1000000 | bytes 26000000 | tf_op jit(solution)/shard_map/unpack/pallas_call | solution.py:661
  (240 shorter events, 90.7 us)
Async XLA Ops:
  7.2 150.9 %all-gather.3.cloned.1.call-start = ((), (), s32[]{:S(2)}) async-start(), calls=%async_computation.1 | async-start | bytes 6782976 | tf_op jit(solution)/shard_map/all_gather | solution.py:924
  10.0 17.5 %collective-permute-start.1 = (bf16[160,2048]{1,0:T(8,128)(2,1)S(1)}, bf16[160,2048]{1,0:T(8,128)(2,1)S(1)}, u32[]{:S(2)}, u32[]{:S(2)}) collective-permute-start(bf16[160,2048]{1,0:T(8,128)(2,1)S(1)} %fusion.2.n0.refs_0_.refs_5_), channel_id=1, source_target_pairs={{0,2},{2,4},{4,6},{6,0},{1,3},{3,5},{5,7},{7,1},{8,10},{10,12},{12... | collective-permute-start | bytes 1966088 | tf_op jit(solution)/shard_map/ppermute | solution.py:70
  12.1 15.4 %collective-permute-start = (bf16[160,2048]{1,0:T(8,128)(2,1)S(1)}, bf16[160,2048]{1,0:T(8,128)(2,1)}, u32[]{:S(2)}, u32[]{:S(2)}) collective-permute-start(bf16[160,2048]{1,0:T(8,128)(2,1)S(1)} %fusion.2.n0.refs_0_.refs_5_), channel_id=1, source_target_pairs={{0,6},{2,0},{4,2},{6,4},{1,7},{3,1},{5,3},{7,5},{8,14},{10,8},{12,... | collective-permute-start | bytes 1966088 | tf_op jit(solution)/shard_map/ppermute | solution.py:71
  15.3 15.8 %collective-permute-start.5 = (bf16[128,2048]{1,0:T(8,128)(2,1)}, bf16[128,2048]{1,0:T(8,128)(2,1)}, u32[]{:S(2)}, u32[]{:S(2)}) collective-permute-start(bf16[128,2048]{1,0:T(8,128)(2,1)} %constant_dynamic-slice_fusion.4), channel_id=1, source_target_pairs={{0,1},{1,0},{2,3},{3,2},{4,5},{5,4},{6,7},{7,6},{8,9},{9,8},{10,11... | collective-permute-start | bytes 1572872 | tf_op jit(solution)/shard_map/ppermute | solution.py:134
  19.9 24.4 %collective-permute-start.4 = (bf16[512,640]{1,0:T(8,128)(2,1)}, bf16[512,640]{1,0:T(8,128)(2,1)S(1)}, u32[]{:S(2)}, u32[]{:S(2)}) collective-permute-start(bf16[512,640]{1,0:T(8,128)(2,1)} %constant_dynamic-slice_fusion.5), channel_id=1, source_target_pairs={{0,1},{1,0},{2,3},{3,2},{4,5},{5,4},{6,7},{7,6},{8,9},{9,8},{10,11... | collective-permute-start | bytes 1966088 | tf_op jit(solution)/shard_map/ppermute | solution.py:134
  28.7 15.6 %collective-permute-start.3 = (bf16[80,2048]{1,0:T(8,128)(2,1)S(1)}, bf16[80,2048]{1,0:T(8,128)(2,1)S(1)}, u32[]{:S(2)}, u32[]{:S(2)}) collective-permute-start(bf16[80,2048]{1,0:T(8,128)(2,1)S(1)} %slice.38), channel_id=1, source_target_pairs={{0,6},{2,0},{4,2},{6,4},{1,7},{3,1},{5,3},{7,5},{8,14},{10,8},{12,... | collective-permute-start | bytes 983048 | tf_op jit(solution)/shard_map/ppermute | solution.py:75
  31.1 13.2 %collective-permute-start.2 = (bf16[80,2048]{1,0:T(8,128)(2,1)S(1)}, bf16[80,2048]{1,0:T(8,128)(2,1)S(1)}, u32[]{:S(2)}, u32[]{:S(2)}) collective-permute-start(bf16[80,2048]{1,0:T(8,128)(2,1)S(1)} %slice.37), channel_id=1, source_target_pairs={{0,2},{2,4},{4,6},{6,0},{1,3},{3,5},{5,7},{7,1},{8,10},{10,12},{12... | collective-permute-start | bytes 983048 | tf_op jit(solution)/shard_map/ppermute | solution.py:74
  47.5 29.5 %collective-permute-start.10 = (bf16[160,2048]{1,0:T(8,128)(2,1)S(1)}, bf16[160,2048]{1,0:T(8,128)(2,1)}, u32[]{:S(2)}, u32[]{:S(2)}) collective-permute-start(bf16[160,2048]{1,0:T(8,128)(2,1)S(1)} %copy-done.5), channel_id=1, source_target_pairs={{0,2},{2,4},{4,6},{6,0},{1,3},{3,5},{5,7},{7,1},{8,10},{10,12},{12... | collective-permute-start | bytes 1966088 | tf_op jit(solution)/shard_map/ppermute | solution.py:903
  47.5 31.3 %collective-permute-start.9 = (bf16[160,2048]{1,0:T(8,128)(2,1)S(1)}, bf16[160,2048]{1,0:T(8,128)(2,1)}, u32[]{:S(2)}, u32[]{:S(2)}) collective-permute-start(bf16[160,2048]{1,0:T(8,128)(2,1)S(1)} %copy-done.5), channel_id=1, source_target_pairs={{0,4},{2,6},{4,0},{6,2},{1,5},{3,7},{5,1},{7,3},{8,12},{10,14},{12... | collective-permute-start | bytes 1966088 | tf_op jit(solution)/shard_map/ppermute | solution.py:903
  50.0 29.3 %collective-permute-start.8 = (bf16[160,2048]{1,0:T(8,128)(2,1)S(1)}, bf16[160,2048]{1,0:T(8,128)(2,1)}, u32[]{:S(2)}, u32[]{:S(2)}) collective-permute-start(bf16[160,2048]{1,0:T(8,128)(2,1)S(1)} %copy-done.5), channel_id=1, source_target_pairs={{0,6},{2,0},{4,2},{6,4},{1,7},{3,1},{5,3},{7,5},{8,14},{10,8},{12,... | collective-permute-start | bytes 1966088 | tf_op jit(solution)/shard_map/ppermute | solution.py:903
  63.7 15.5 %collective-permute-start.11 = (bf16[128,2048]{1,0:T(8,128)(2,1)}, bf16[128,2048]{1,0:T(8,128)(2,1)S(1)}, u32[]{:S(2)}, u32[]{:S(2)}) collective-permute-start(bf16[128,2048]{1,0:T(8,128)(2,1)} %collective-permute-done.5.w1), channel_id=1, source_target_pairs={{0,8},{8,0},{1,9},{9,1},{2,10},{10,2},{3,11},{11,3},{4,12},{12,4},... | collective-permute-start | bytes 1572872 | tf_op jit(solution)/shard_map/ppermute | solution.py:898
  65.3 19.5 %collective-permute-start.21 = (bf16[128,2944]{1,0:T(8,128)(2,1)S(1)}, bf16[128,2944]{1,0:T(8,128)(2,1)S(1)}, u32[]{:S(2)}, u32[]{:S(2)}) collective-permute-start(bf16[128,2944]{1,0:T(8,128)(2,1)S(1)} %pad_maximum_fusion), channel_id=1, source_target_pairs={{0,17},{1,16},{16,1},{17,0},{2,19},{3,18},{18,3},{19,2},{4,21},{5,... | collective-permute-start | bytes 2261000 | tf_op jit(solution)/shard_map/ppermute | solution.py:909
  85.7 278.7 %reduce-scatter.2.cloned.1.call-start = ((), (), s32[]{:S(2)}) async-start(), calls=%async_computation.2 | async-start | bytes 17842176 | tf_op jit(solution)/shard_map/reduce_scatter | solution.py:938
  87.4 38.5 %collective-permute-start.16 = (bf16[352,2048]{1,0:T(8,128)(2,1)S(1)}, bf16[352,2048]{1,0:T(8,128)(2,1)}, u32[]{:S(2)}, u32[]{:S(2)}) collective-permute-start(bf16[352,2048]{1,0:T(8,128)(2,1)S(1)} %constant_dynamic-slice_fusion.2), channel_id=1, source_target_pairs={{0,1},{1,0},{2,3},{3,2},{4,5},{5,4},{6,7},{7,6},{8,9},{9,8},{10,11... | collective-permute-start | bytes 4325384 | tf_op jit(solution)/shard_map/ppermute | solution.py:134
  90.5 9.5 %collective-permute-start.13 = (bf16[80,2048]{1,0:T(8,128)(2,1)S(1)}, bf16[80,2048]{1,0:T(8,128)(2,1)S(1)}, u32[]{:S(2)}, u32[]{:S(2)}) collective-permute-start(bf16[80,2048]{1,0:T(8,128)(2,1)S(1)} %copy-done.51), channel_id=1, source_target_pairs={{0,6},{2,0},{4,2},{6,4},{1,7},{3,1},{5,3},{7,5},{8,14},{10,8},{12,... | collective-permute-start | bytes 983048 | tf_op jit(solution)/shard_map/ppermute | solution.py:87
  93.7 9.5 %collective-permute-start.12 = (bf16[80,2048]{1,0:T(8,128)(2,1)S(1)}, bf16[80,2048]{1,0:T(8,128)(2,1)S(1)}, u32[]{:S(2)}, u32[]{:S(2)}) collective-permute-start(bf16[80,2048]{1,0:T(8,128)(2,1)S(1)} %copy-done.50), channel_id=1, source_target_pairs={{0,2},{2,4},{4,6},{6,0},{1,3},{3,5},{5,7},{7,1},{8,10},{10,12},{12... | collective-permute-start | bytes 983048 | tf_op jit(solution)/shard_map/ppermute | solution.py:86
  106.1 15.9 %collective-permute-start.14 = (bf16[160,2048]{1,0:T(8,128)(2,1)}, bf16[160,2048]{1,0:T(8,128)(2,1)S(1)}, u32[]{:S(2)}, u32[]{:S(2)}) collective-permute-start(bf16[160,2048]{1,0:T(8,128)(2,1)} %get-tuple-element.115), channel_id=1, source_target_pairs={{0,2},{2,4},{4,6},{6,0},{1,3},{3,5},{5,7},{7,1},{8,10},{10,12},{12... | collective-permute-start | bytes 1966088 | tf_op jit(solution)/shard_map/ppermute | solution.py:108
  106.1 15.9 %collective-permute-start.15 = (bf16[160,2048]{1,0:T(8,128)(2,1)}, bf16[160,2048]{1,0:T(8,128)(2,1)S(1)}, u32[]{:S(2)}, u32[]{:S(2)}) collective-permute-start(bf16[160,2048]{1,0:T(8,128)(2,1)} %get-tuple-element.116), channel_id=1, source_target_pairs={{0,6},{2,0},{4,2},{6,4},{1,7},{3,1},{5,3},{7,5},{8,14},{10,8},{12,... | collective-permute-start | bytes 1966088 | tf_op jit(solution)/shard_map/ppermute | solution.py:108
  125.9 15.0 %collective-permute-start.18 = (bf16[160,2048]{1,0:T(8,128)(2,1)}, bf16[160,2048]{1,0:T(8,128)(2,1)S(1)}, u32[]{:S(2)}, u32[]{:S(2)}) collective-permute-start(bf16[160,2048]{1,0:T(8,128)(2,1)} %get-tuple-element.120.n0.refs_0_.refs_5_), channel_id=1, source_target_pairs={{0,2},{2,4},{4,6},{6,0},{1,3},{3,5},{5,7},{7,1},{8,10},{10,12},{12... | collective-permute-start | bytes 1966088 | tf_op jit(solution)/shard_map/ppermute | solution.py:70
  126.0 15.0 %collective-permute-start.17 = (bf16[160,2048]{1,0:T(8,128)(2,1)}, bf16[160,2048]{1,0:T(8,128)(2,1)S(1)}, u32[]{:S(2)}, u32[]{:S(2)}) collective-permute-start(bf16[160,2048]{1,0:T(8,128)(2,1)} %get-tuple-element.120.n0.refs_0_.refs_5_), channel_id=1, source_target_pairs={{0,6},{2,0},{4,2},{6,4},{1,7},{3,1},{5,3},{7,5},{8,14},{10,8},{12,... | collective-permute-start | bytes 1966088 | tf_op jit(solution)/shard_map/ppermute | solution.py:71
  141.0 17.1 %collective-permute-start.22 = (bf16[352,2048]{1,0:T(8,128)(2,1)}, bf16[352,2048]{1,0:T(8,128)(2,1)S(1)}, u32[]{:S(2)}, u32[]{:S(2)}) collective-permute-start(bf16[352,2048]{1,0:T(8,128)(2,1)} %collective-permute-done.16.w1), channel_id=1, source_target_pairs={{0,8},{8,0},{1,9},{9,1},{2,10},{10,2},{3,11},{11,3},{4,12},{12,4},... | collective-permute-start | bytes 4325384 | tf_op jit(solution)/shard_map/ppermute | solution.py:931
  144.7 9.8 %collective-permute-start.20 = (bf16[80,2048]{1,0:T(8,128)(2,1)S(1)}, bf16[80,2048]{1,0:T(8,128)(2,1)S(1)}, u32[]{:S(2)}, u32[]{:S(2)}) collective-permute-start(bf16[80,2048]{1,0:T(8,128)(2,1)S(1)} %slice.40), channel_id=1, source_target_pairs={{0,6},{2,0},{4,2},{6,4},{1,7},{3,1},{5,3},{7,5},{8,14},{10,8},{12,... | collective-permute-start | bytes 983048 | tf_op jit(solution)/shard_map/ppermute | solution.py:75
  147.4 10.7 %collective-permute-start.19 = (bf16[80,2048]{1,0:T(8,128)(2,1)S(1)}, bf16[80,2048]{1,0:T(8,128)(2,1)S(1)}, u32[]{:S(2)}, u32[]{:S(2)}) collective-permute-start(bf16[80,2048]{1,0:T(8,128)(2,1)S(1)} %slice.39), channel_id=1, source_target_pairs={{0,2},{2,4},{4,6},{6,0},{1,3},{3,5},{5,7},{7,1},{8,10},{10,12},{12... | collective-permute-start | bytes 983048 | tf_op jit(solution)/shard_map/ppermute | solution.py:74
  195.5 11.9 %collective-permute-start.23 = (bf16[80,2048]{1,0:T(8,128)(2,1)}, bf16[80,2048]{1,0:T(8,128)(2,1)S(1)}, u32[]{:S(2)}, u32[]{:S(2)}) collective-permute-start(bf16[80,2048]{1,0:T(8,128)(2,1)} %get-tuple-element.132), channel_id=1, source_target_pairs={{0,2},{2,4},{4,6},{6,0},{1,3},{3,5},{5,7},{7,1},{8,10},{10,12},{12... | collective-permute-start | bytes 983048 | tf_op jit(solution)/shard_map/ppermute | solution.py:86
  195.6 11.8 %collective-permute-start.24 = (bf16[80,2048]{1,0:T(8,128)(2,1)}, bf16[80,2048]{1,0:T(8,128)(2,1)S(1)}, u32[]{:S(2)}, u32[]{:S(2)}) collective-permute-start(bf16[80,2048]{1,0:T(8,128)(2,1)} %get-tuple-element.134), channel_id=1, source_target_pairs={{0,6},{2,0},{4,2},{6,4},{1,7},{3,1},{5,3},{7,5},{8,14},{10,8},{12,... | collective-permute-start | bytes 983048 | tf_op jit(solution)/shard_map/ppermute | solution.py:87
  210.5 17.3 %collective-permute-start.25 = (bf16[160,2048]{1,0:T(8,128)(2,1)}, bf16[160,2048]{1,0:T(8,128)(2,1)S(1)}, u32[]{:S(2)}, u32[]{:S(2)}) collective-permute-start(bf16[160,2048]{1,0:T(8,128)(2,1)} %get-tuple-element.135), channel_id=1, source_target_pairs={{0,2},{2,4},{4,6},{6,0},{1,3},{3,5},{5,7},{7,1},{8,10},{10,12},{12... | collective-permute-start | bytes 1966088 | tf_op jit(solution)/shard_map/ppermute | solution.py:108
  210.5 17.3 %collective-permute-start.26 = (bf16[160,2048]{1,0:T(8,128)(2,1)}, bf16[160,2048]{1,0:T(8,128)(2,1)S(1)}, u32[]{:S(2)}, u32[]{:S(2)}) collective-permute-start(bf16[160,2048]{1,0:T(8,128)(2,1)} %get-tuple-element.136), channel_id=1, source_target_pairs={{0,6},{2,0},{4,2},{6,4},{1,7},{3,1},{5,3},{7,5},{8,14},{10,8},{12,... | collective-permute-start | bytes 1966088 | tf_op jit(solution)/shard_map/ppermute | solution.py:108
  228.9 212.5 %all-gather.5.cloned.1.call-start = ((), (), s32[]{:S(2)}) async-start(), calls=%async_computation.3 | async-start | bytes 9191424 | tf_op jit(solution)/shard_map/all_gather | solution.py:970
  232.9 14.3 %collective-permute-start.28 = (bf16[160,2048]{1,0:T(8,128)(2,1)}, bf16[160,2048]{1,0:T(8,128)(2,1)S(1)}, u32[]{:S(2)}, u32[]{:S(2)}) collective-permute-start(bf16[160,2048]{1,0:T(8,128)(2,1)} %get-tuple-element.141.b0.refs_10_), channel_id=1, source_target_pairs={{0,6},{2,0},{4,2},{6,4},{1,7},{3,1},{5,3},{7,5},{8,14},{10,8},{12,... | collective-permute-start | bytes 1966088 | tf_op jit(solution)/shard_map/ppermute | solution.py:71
  233.9 14.5 %collective-permute-start.27 = (bf16[160,2048]{1,0:T(8,128)(2,1)}, bf16[160,2048]{1,0:T(8,128)(2,1)S(1)}, u32[]{:S(2)}, u32[]{:S(2)}) collective-permute-start(bf16[160,2048]{1,0:T(8,128)(2,1)} %get-tuple-element.141.b0.refs_10_), channel_id=1, source_target_pairs={{0,2},{2,4},{4,6},{6,0},{1,3},{3,5},{5,7},{7,1},{8,10},{10,12},{12... | collective-permute-start | bytes 1966088 | tf_op jit(solution)/shard_map/ppermute | solution.py:70
  248.4 13.4 %collective-permute-start.29 = (bf16[80,2048]{1,0:T(8,128)(2,1)S(1)}, bf16[80,2048]{1,0:T(8,128)(2,1)S(1)}, u32[]{:S(2)}, u32[]{:S(2)}) collective-permute-start(bf16[80,2048]{1,0:T(8,128)(2,1)S(1)} %slice.41), channel_id=1, source_target_pairs={{0,2},{2,4},{4,6},{6,0},{1,3},{3,5},{5,7},{7,1},{8,10},{10,12},{12... | collective-permute-start | bytes 983048 | tf_op jit(solution)/shard_map/ppermute | solution.py:74
  248.5 13.4 %collective-permute-start.30 = (bf16[80,2048]{1,0:T(8,128)(2,1)S(1)}, bf16[80,2048]{1,0:T(8,128)(2,1)}, u32[]{:S(2)}, u32[]{:S(2)}) collective-permute-start(bf16[80,2048]{1,0:T(8,128)(2,1)S(1)} %slice.42), channel_id=1, source_target_pairs={{0,6},{2,0},{4,2},{6,4},{1,7},{3,1},{5,3},{7,5},{8,14},{10,8},{12,... | collective-permute-start | bytes 983048 | tf_op jit(solution)/shard_map/ppermute | solution.py:75
  261.9 23.3 %collective-permute-start.31 = (bf16[160,2048]{1,0:T(8,128)(2,1)}, bf16[160,2048]{1,0:T(8,128)(2,1)S(1)}, u32[]{:S(2)}, u32[]{:S(2)}) collective-permute-start(bf16[160,2048]{1,0:T(8,128)(2,1)} %get-tuple-element.144), channel_id=1, source_target_pairs={{0,2},{2,4},{4,6},{6,0},{1,3},{3,5},{5,7},{7,1},{8,10},{10,12},{12... | collective-permute-start | bytes 1966088 | tf_op jit(solution)/shard_map/ppermute | solution.py:951
  262.0 23.2 %collective-permute-start.32 = (bf16[160,2048]{1,0:T(8,128)(2,1)}, bf16[160,2048]{1,0:T(8,128)(2,1)S(1)}, u32[]{:S(2)}, u32[]{:S(2)}) collective-permute-start(bf16[160,2048]{1,0:T(8,128)(2,1)} %get-tuple-element.146), channel_id=1, source_target_pairs={{0,6},{2,0},{4,2},{6,4},{1,7},{3,1},{5,3},{7,5},{8,14},{10,8},{12,... | collective-permute-start | bytes 1966088 | tf_op jit(solution)/shard_map/ppermute | solution.py:951
  294.4 15.4 %collective-permute-start.34 = (bf16[4,2,1024,128]{3,2,1,0:T(8,128)(2,1)}, bf16[4,2,1024,128]{3,2,1,0:T(8,128)(2,1)S(1)}, u32[]{:S(2)}, u32[]{:S(2)}) collective-permute-start(bf16[4,2,1024,128]{3,2,1,0:T(8,128)(2,1)} %get-tuple-element.156), channel_id=1, source_target_pairs={{0,8},{8,0},{1,9},{9,1},{2,10},{10,2},{3,11},{11,3},{4,12},{12,4},... | collective-permute-start | bytes 6291464 | tf_op jit(solution)/shard_map/ppermute | solution.py:787
  315.2 21.8 %collective-permute-start.36 = (bf16[2,1168,128]{2,1,0:T(8,128)(2,1)}, bf16[2,1168,128]{2,1,0:T(8,128)(2,1)S(1)}, u32[]{:S(2)}, u32[]{:S(2)}) collective-permute-start(bf16[2,1168,128]{2,1,0:T(8,128)(2,1)} %get-tuple-element.162), channel_id=1, source_target_pairs={{0,64},{32,96},{64,0},{96,32},{1,65},{33,97},{65,1},{97,33},{2,66}... | collective-permute-start | bytes 1794056 | tf_op jit(solution)/shard_map/ppermute | solution.py:792
  318.2 31.6 %collective-permute-start.37 = (bf16[2,1168,128]{2,1,0:T(8,128)(2,1)}, bf16[2,1168,128]{2,1,0:T(8,128)(2,1)S(1)}, u32[]{:S(2)}, u32[]{:S(2)}) collective-permute-start(bf16[2,1168,128]{2,1,0:T(8,128)(2,1)} %get-tuple-element.163), channel_id=1, source_target_pairs={{0,32},{32,64},{64,96},{96,0},{1,33},{33,65},{65,97},{97,1},{2,34}... | collective-permute-start | bytes 1794056 | tf_op jit(solution)/shard_map/ppermute | solution.py:792
  318.6 31.2 %collective-permute-start.38 = (bf16[2,1168,128]{2,1,0:T(8,128)(2,1)}, bf16[2,1168,128]{2,1,0:T(8,128)(2,1)S(1)}, u32[]{:S(2)}, u32[]{:S(2)}) collective-permute-start(bf16[2,1168,128]{2,1,0:T(8,128)(2,1)} %get-tuple-element.164), channel_id=1, source_target_pairs={{0,96},{32,0},{64,32},{96,64},{1,97},{33,1},{65,33},{97,65},{2,98}... | collective-permute-start | bytes 1794056 | tf_op jit(solution)/shard_map/ppermute | solution.py:792
  367.2 14.0 %collective-permute-start.46 = (bf16[1168,128]{1,0:T(8,128)(2,1)}, bf16[1168,128]{1,0:T(8,128)(2,1)S(1)}, u32[]{:S(2)}, u32[]{:S(2)}) collective-permute-start(bf16[1168,128]{1,0:T(8,128)(2,1)} %get-tuple-element.181), channel_id=1, source_target_pairs={{0,17},{1,16},{16,1},{17,0},{2,19},{3,18},{18,3},{19,2},{4,21},{5,... | collective-permute-start | bytes 897032 | tf_op jit(solution)/shard_map/ppermute | solution.py:804
  369.4 11.8 %collective-permute-start.45 = (bf16[1168,128]{1,0:T(8,128)(2,1)}, bf16[1168,128]{1,0:T(8,128)(2,1)S(1)}, u32[]{:S(2)}, u32[]{:S(2)}) collective-permute-start(bf16[1168,128]{1,0:T(8,128)(2,1)} %get-tuple-element.181), channel_id=1, source_target_pairs={{0,1},{1,0},{2,3},{3,2},{4,5},{5,4},{6,7},{7,6},{8,9},{9,8},{10,11... | collective-permute-start | bytes 897032 | tf_op jit(solution)/shard_map/ppermute | solution.py:803
  369.9 15.3 %collective-permute-start.44 = (bf16[1168,128]{1,0:T(8,128)(2,1)}, bf16[1168,128]{1,0:T(8,128)(2,1)S(1)}, u32[]{:S(2)}, u32[]{:S(2)}) collective-permute-start(bf16[1168,128]{1,0:T(8,128)(2,1)} %get-tuple-element.180.a), channel_id=1, source_target_pairs={{0,16},{16,0},{1,17},{17,1},{2,18},{18,2},{3,19},{19,3},{4,20},{20... | collective-permute-start | bytes 897032 | tf_op jit(solution)/shard_map/ppermute | solution.py:802
  376.8 48.6 %collective-permute-start.42 = (bf16[160,2048]{1,0:T(8,128)(2,1)}, bf16[160,2048]{1,0:T(8,128)(2,1)}, u32[]{:S(2)}, u32[]{:S(2)}) collective-permute-start(bf16[160,2048]{1,0:T(8,128)(2,1)} %get-tuple-element.177), channel_id=1, source_target_pairs={{0,2},{2,4},{4,6},{6,0},{1,3},{3,5},{5,7},{7,1},{8,10},{10,12},{12... | collective-permute-start | bytes 1966088 | tf_op jit(solution)/shard_map/ppermute | solution.py:108
  376.9 48.5 %collective-permute-start.43 = (bf16[160,2048]{1,0:T(8,128)(2,1)}, bf16[160,2048]{1,0:T(8,128)(2,1)}, u32[]{:S(2)}, u32[]{:S(2)}) collective-permute-start(bf16[160,2048]{1,0:T(8,128)(2,1)} %get-tuple-element.178), channel_id=1, source_target_pairs={{0,6},{2,0},{4,2},{6,4},{1,7},{3,1},{5,3},{7,5},{8,14},{10,8},{12,... | collective-permute-start | bytes 1966088 | tf_op jit(solution)/shard_map/ppermute | solution.py:108
  388.1 12.0 %collective-permute-start.49 = (bf16[1168,128]{1,0:T(8,128)(2,1)}, bf16[1168,128]{1,0:T(8,128)(2,1)S(1)}, u32[]{:S(2)}, u32[]{:S(2)}) collective-permute-start(bf16[1168,128]{1,0:T(8,128)(2,1)} %sum_z.1.refs_0_), channel_id=1, source_target_pairs={{0,96},{32,0},{64,32},{96,64},{1,97},{33,1},{65,33},{97,65},{2,98}... | collective-permute-start | bytes 897032 | tf_op jit(solution)/shard_map/ppermute | solution.py:808
  390.0 45.5 %collective-permute-start.39 = (bf16[160,2048]{1,0:T(8,128)(2,1)}, bf16[160,2048]{1,0:T(8,128)(2,1)S(1)}, u32[]{:S(2)}, u32[]{:S(2)}) collective-permute-start(bf16[160,2048]{1,0:T(8,128)(2,1)} %get-tuple-element.166), channel_id=1, source_target_pairs={{0,4},{2,6},{4,0},{6,2},{1,5},{3,7},{5,1},{7,3},{8,12},{10,14},{12... | collective-permute-start | bytes 1966088 | tf_op jit(solution)/shard_map/ppermute | solution.py:969
  390.7 13.7 %collective-permute-start.48 = (bf16[1168,128]{1,0:T(8,128)(2,1)}, bf16[1168,128]{1,0:T(8,128)(2,1)S(1)}, u32[]{:S(2)}, u32[]{:S(2)}) collective-permute-start(bf16[1168,128]{1,0:T(8,128)(2,1)} %sum_z.1.refs_0_), channel_id=1, source_target_pairs={{0,64},{32,96},{64,0},{96,32},{1,65},{33,97},{65,1},{97,33},{2,66}... | collective-permute-start | bytes 897032 | tf_op jit(solution)/shard_map/ppermute | solution.py:808
  400.1 18.2 %collective-permute-start.47 = (bf16[1168,128]{1,0:T(8,128)(2,1)}, bf16[1168,128]{1,0:T(8,128)(2,1)S(1)}, u32[]{:S(2)}, u32[]{:S(2)}) collective-permute-start(bf16[1168,128]{1,0:T(8,128)(2,1)} %sum_z.1.refs_0_), channel_id=1, source_target_pairs={{0,32},{32,64},{64,96},{96,0},{1,33},{33,65},{65,97},{97,1},{2,34}... | collective-permute-start | bytes 897032 | tf_op jit(solution)/shard_map/ppermute | solution.py:808
  404.4 21.5 %collective-permute-start.50 = (bf16[1168,128]{1,0:T(8,128)(2,1)}, bf16[1168,128]{1,0:T(8,128)(2,1)S(1)}, u32[]{:S(2)}, u32[]{:S(2)}) collective-permute-start(bf16[1168,128]{1,0:T(8,128)(2,1)} %sum_z.1.refs_0_), channel_id=1, source_target_pairs={{0,8},{8,0},{1,9},{9,1},{2,10},{10,2},{3,11},{11,3},{4,12},{12,4},... | collective-permute-start | bytes 897032 | tf_op jit(solution)/shard_map/ppermute | solution.py:809
  (65 other events, 504.2 us)
Sparse Core Ops, SparseCore 0:
  85.8 42.3 all-gather.2
  228.0 136.4 reduce-scatter.1
  366.1 68.4 all-gather.4

commit v11 on v10

--- a/solution.py
+++ b/solution.py
@@ -463,64 +463,81 @@
     return copies
 
 
-def ffn_body(
-    idx, n0, n1, n2a, n2b, n3, c0, c1, c2, c3, gate_own, up_own, gate_par, up_par, w0, w1, w2,
-    hid, dgate, dup, n_all, c_all, down, sem,
-):
-    i = pl.program_id(0)
-    zh = idx[1]
-
-    @pl.when(i == 0)
-    def _():
-        copies = load_down(idx, (w0, w1, w2), down, sem)
-        for c in copies:
-            c.start()
-        for ref, row, (_, n) in zip((n0, n1, n2a, n2b, n3), PIECE_ROW, PIECES):
-            n_all[row : row + n, :] = ref[...]
-        for d, ref in enumerate((c0, c1, c2, c3)):
-            c_all[d * BLK : (d + 1) * BLK, :] = ref[...]
-        for c in copies:
-            c.wait()
-
-    own = n_all[:, pl.ds(pl.multiple_of(zh * DH, DH), DH)]
-    par = n_all[:, pl.ds(pl.multiple_of((1 - zh) * DH, DH), DH)]
-    gate = dot(own, gate_own[...]) + dot(par, gate_par[...])
-    up = dot(own, up_own[...]) + dot(par, up_par[...])
-    dh = dot_t(c_all[...], down[pl.ds(pl.multiple_of(i * TILE, TILE), TILE), :])
-    sig = 1.0 / (1.0 + jnp.exp(-gate))
-    act = gate * sig
-    hid[...] = (act * up).astype(BF16)
-    dgate[...] = (dh * up * sig * (1.0 + gate * (1.0 - sig))).astype(BF16)
-    dup[...] = (dh * act).astype(BF16)
+FFN_ORDER = (0, 1, 3, 2)
+EARLY = 3 * BLK
+
+
+def ffn_parts(refs):
+    o0, o1, o2a, o2b, o3 = refs
+    return (o0, 0, BLK), (o1, BLK, BLK), (o3, 2 * BLK, BLK), (o2a, EARLY, HALF), (o2b, EARLY + HALF, HALF)
+
+
+def ffn_kernel(n_rows, n_cots, aliased):
+    def body(idx, *refs):
+        pieces, cots = refs[:n_rows], refs[n_rows : n_rows + n_cots]
+        refs = refs[n_rows + n_cots :]
+        gate_own, up_own, gate_par, up_par, w0, w1, w2 = refs[:7]
+        hid, dgate, dup, n_all, c_all, down, sem = refs[7 + aliased :]
+        i = pl.program_id(0)
+        zh = idx[1]
+
+        @pl.when(i == 0)
+        def _():
+            copies = load_down(idx, (w0, w1, w2), down, sem)
+            for c in copies:
+                c.start()
+            for group, dst in ((pieces, n_all), (cots, c_all)):
+                row = 0
+                for ref in group:
+                    dst[row : row + ref.shape[0], :] = ref[...]
+                    row += ref.shape[0]
+            for c in copies:
+                c.wait()
+
+        own = n_all[:, pl.ds(pl.multiple_of(zh * DH, DH), DH)]
+        par = n_all[:, pl.ds(pl.multiple_of((1 - zh) * DH, DH), DH)]
+        gate = dot(own, gate_own[...]) + dot(par, gate_par[...])
+        up = dot(own, up_own[...]) + dot(par, up_par[...])
+        dh = dot_t(c_all[...], down[pl.ds(pl.multiple_of(i * TILE, TILE), TILE), :])
+        sig = 1.0 / (1.0 + jnp.exp(-gate))
+        act = gate * sig
+        hid[...] = (act * up).astype(BF16)
+        dgate[...] = (dh * up * sig * (1.0 + gate * (1.0 - sig))).astype(BF16)
+        dup[...] = (dh * act).astype(BF16)
+
+    return body
 
 
 def whole(n, w):
     return pl.BlockSpec((n, w), lambda i: (0, 0))
 
 
-def ffn(idx, normed, cots, gate, up, gate_up, down):
+def ffn(idx, pieces, cots, gate, up, gate_up, down, earlier=()):
+    rows = sum(v.shape[0] for v in pieces)
     column = lambda first: pl.BlockSpec((DH, TILE), lambda i: (0, i + first))
-    hidden = pl.BlockSpec((ROWS, TILE), lambda i: (0, i))
-    return pl.pallas_call(
-        ffn_body,
+    place = EARLY // rows if earlier else 0
+    hidden = pl.BlockSpec((rows, TILE), lambda i: (place, i))
+    n = len(pieces) + len(cots)
+    return pl.pallas_call(
+        ffn_kernel(len(pieces), len(cots), len(earlier)),
         grid=(TILES,),
         out_shape=(sds((ROWS, FF4)),) * 3,
         in_specs=[spec(pltpu.SMEM)]
-        + [whole(n, D) for _, n in PIECES]
-        + [whole(BLK, D)] * 4
+        + [whole(v.shape[0], D) for v in (*pieces, *cots)]
         + [column(0), column(0), column(0), column(TILES)]
-        + [spec(pl.ANY)] * 3,
+        + [spec(pl.ANY)] * (3 + len(earlier)),
         out_specs=[hidden] * 3,
         scratch_shapes=[
-            pltpu.VMEM((ROWS, D), BF16),
-            pltpu.VMEM((ROWS, D), BF16),
+            pltpu.VMEM((rows, D), BF16),
+            pltpu.VMEM((rows, D), BF16),
             pltpu.VMEM((GAP, D), BF16),
             pltpu.SemaphoreType.DMA((3,)),
         ],
-        compiler_params=params(),
-        cost_estimate=cost(6 * ROWS * D * FF4, 3.4e7),
-        name="ffn",
-    )(idx, *normed, *cots, gate, up, gate_up, gate_up, *down)
+        input_output_aliases={n + 8 + k: k for k in range(len(earlier))},
+        compiler_params=params(),
+        cost_estimate=cost(6 * rows * D * FF4, 2.5e7),
+        name="ffn_last" if earlier else "ffn",
+    )(idx, *pieces, *cots, gate, up, gate_up, gate_up, *down, *earlier)
 
 
 def down_body(idx, hid, w0, w1, w2, o0, o1, o2, o3, down, sem):
@@ -532,8 +549,8 @@
     for n in range(D // 512):
         cols = slice(n * 512, (n + 1) * 512)
         res = dot(hid[...], down[:, cols]).astype(BF16)
-        for d, ref in enumerate((o0, o1, o2, o3)):
-            ref[:, cols] = res[d * BLK : (d + 1) * BLK]
+        for k, ref in enumerate((o0, o1, o3, o2)):
+            ref[:, cols] = res[k * BLK : (k + 1) * BLK]
 
 
 def down_project(idx, hid, down):
@@ -552,13 +569,17 @@
 def ffn_back_body(idx, dgate, dup, gate_own, up_own, par, *refs):
     half = pl.num_programs(0) // 2
 
+    def store(res):
+        for ref, row, n in ffn_parts(refs):
+            ref[...] = res[row : row + n].astype(BF16)
+
     @pl.when(pl.program_id(0) < half)
     def _():
-        store_parts(dot_t(dgate[...], gate_own[...]) + dot_t(dup[...], up_own[...]), refs)
+        store(dot_t(dgate[...], gate_own[...]) + dot_t(dup[...], up_own[...]))
 
     @pl.when(pl.program_id(0) >= half)
     def _():
-        store_parts(dot_t(dgate[...], par[:, :FF4]) + dot_t(dup[...], par[:, GAP:]), refs)
+        store(dot_t(dgate[...], par[:, :FF4]) + dot_t(dup[...], par[:, GAP:]))
 
 
 def ffn_back(idx, dgate, dup, gate, up, gate_up):
@@ -607,8 +628,8 @@
         gate_up_grads_body,
         grid=(16 // QS,),
         out_shape=sds((2, 16, PIECE, 128)),
-        in_specs=[pl.BlockSpec((n, 64 * QS), lambda i: (0, i)) for _, n in PIECES]
-        + [pl.BlockSpec((n, 64 * QS), lambda i: (0, i + 16 // QS)) for _, n in PIECES]
+        in_specs=[pl.BlockSpec((v.shape[0], 64 * QS), lambda i: (0, i)) for v in normed]
+        + [pl.BlockSpec((v.shape[0], 64 * QS), lambda i: (0, i + 16 // QS)) for v in normed]
         + [whole(ROWS, FF4)] * 2
         + [spec(pl.ANY)],
         out_specs=pl.BlockSpec((2, QS, 2 * GU_ROWS, 128), lambda i: (0, i, 0, 0)),
@@ -788,7 +809,6 @@
     got_b = lax.ppermute(second[1], "core", shift(2, 1))
     part = sds((2, TAIL, 128))
     g = small_call(sum_core_body, (part,) * 4, idx, first[0], got_a, second[0], got_b, name="sum_core")
-    g_core = g[0]
     got = [lax.ppermute(g[s], "y", shift(4, s)) for s in (2, 1, 3)]
     part = sds((TAIL, 128))
     own, other = small_call(sum_y_body, (part,) * 2, idx, g[0], *got, name="sum_y")
@@ -808,7 +828,7 @@
     mine = [tie(g, *d_one)] + [lax.ppermute(g, "y", shift(4, s)) for s in (1, 2, 3)]
     theirs = [lax.ppermute(v, "core", shift(2, 1)) for v in [g] + mine[1:]]
     shapes = (sds((DH, QW), F32), sds((AW // 2, D), F32), sds((2, D), F32))
-    return g_core, own, d_one, small_call(unpack_tail_body, shapes, idx, *mine, *theirs, name="unpack_tail")
+    return g, own, d_one, small_call(unpack_tail_body, shapes, idx, *mine, *theirs, name="unpack_tail")
 
 
 def inverse_rms(v):
@@ -928,8 +948,12 @@
         tokens, *scatter_x(parts), gain_two.reshape(1, D), name="norm_two",
     )
     normed_two = gather_x(tie(normed_two, down_got))
-    down_all = down_weight, down_got, lax.ppermute(tie(down_got, normed_two[1], normed_two[4]), "core", shift(2, 1))
-    hid, dgate, dup = ffn(idx, normed_two, cots, gate_weight, up_weight, gate_up, down_all)
+    down_all = down_weight, down_got, lax.ppermute(tie(down_got, normed_two[0]), "core", shift(2, 1))
+    normed_two = [normed_two[k] for k in (0, 1, 4, 2, 3)]
+    cots = [cots[k] for k in FFN_ORDER]
+    weights = gate_weight, up_weight, gate_up, down_all
+    early = ffn(idx, normed_two[:3], cots[:3], *weights)
+    hid, dgate, dup = ffn(idx, normed_two[3:], cots[3:], *weights, early)
     d_parts = ffn_back(idx, dgate, dup, gate_weight, up_weight, gate_up)
     own_grads = down_grads(cots, tie(hid, d_parts[2]))
     d_own, q1, q3 = relay(d_parts)
@@ -963,11 +987,11 @@
         gain_grad_two,
     )
     over_x = lambda v: sum((lax.ppermute(v, "x", shift(4, s)) for s in (1, 2, 3)), v)
-    cores_summed, summed, d_one, (grad_qkv, grad_out, gains) = sum_tail(
+    z_summed, summed, d_one, (grad_qkv, grad_out, gains) = sum_tail(
         idx, (tail[0], tie(tail[1], dkv_got)), tail_kv, parts
     )
     layer.append(lax.ppermute(tie(layer_parts[2], summed), "x", shift(4, 2)))
-    grads = lax.all_gather(tie(grads, summed), ("zl", "y", "core"), axis=0, tiled=True)
+    grads = lax.all_gather(tie(grads, z_summed), ("zl", "y", "core"), axis=0, tiled=True)
     grad_gate, grad_up, grad_down = unpack(grads)
     _, input_grad, _ = row_call(
         norm_back_body,

time: 466 us -> 469 us (level)
  starting transfers between devices: 106 us -> 90.8 us
  Pallas kernels: 167 us -> 177 us
  waiting for transfers between devices: 139 us -> 144 us
    ppermute x3, waiting for transfers between devices: 12.8 us -> 26.5 us  [gather_x(): from_next = lax.ppermute(v, 'x', shift(4, -1))]
    all_gather x1, waiting for transfers between devices: 0.01 us -> 11.8 us  [on_device(): lax.all_gather(tie(grads, z_summed), ('zl', 'y', 'core'), axis=0, tiled=T...]
    reduce_scatter x1, waiting for transfers between devices: 10.9 us -> 0.01 us  [on_device(): lax.psum_scatter(tie(own_grads, *d_two).reshape(32, PIECE, 128), ('zh', '...]
    ppermute x3, waiting for transfers between devices: 16.8 us -> 6.12 us  [gather_x(): from_prev = lax.ppermute(v, 'x', shift(4, 1))]
    ppermute x4, starting transfers between devices: 21.5 us -> 11.1 us  [sum_tail(): theirs = [lax.ppermute(v, 'core', shift(2, 1)) for v in [g] + mine[1:]]]
    pallas_call x1 -> x2, Pallas kernels: 20.8 us -> 29.8 us  [ffn(): pl.pallas_call(ffn_kernel(len(pieces), len(cots), len(earlier)), grid=(TI...]
    ppermute x3, waiting for transfers between devices: 6.69 us -> 0.01 us  [gather_x(): opp_b = lax.ppermute(send_b, 'x', shift(4, -1))]
    ppermute x1, waiting for transfers between devices: 1.75 us -> 8.06 us  [sum_tail(): lax.ppermute(other, ('zl', 'zh'), cross)]
  transfers between devices with their start and end apart: 60 -> 60, of which waited for: 24 -> 23; matrix products, arithmetic and copies ran while one was open for 3% -> 4% of each run, Pallas kernels for 26% -> 30%
where the time goes in v11:
time: 469 us; the launch traced here: 460 us
  Pallas kernels  177 us (38%)
  waiting for transfers between devices  144 us (31%)
  starting transfers between devices  90.8 us (19%)
  local copies, waits for them, and re-layouts  23.8 us (5%)
  between operations  14.7 us (3%)
  other arithmetic  10.6 us (2%)
    pallas_call x2, Pallas kernels, ffn(): pl.pallas_call(ffn_kernel(len(pieces), len(cots), len(earlier)), grid=(TI...  29.8 us
    ppermute x3, waiting for transfers between devices, sum_tail(): got = [lax.ppermute(g[s], 'y', shift(4, s)) for s in (2, 1, 3)]  29.4 us
    ppermute x3, waiting for transfers between devices, gather_x(): from_next = lax.ppermute(v, 'x', shift(4, -1))  26.5 us
    pallas_call x1, Pallas kernels, attend_back(): pl.pallas_call(attend_back_body, out_shape=(sds((4, BLK, AW)), sds((ROWS,...  20.4 us
    ppermute x3, waiting for transfers between devices, sum_tail(): lax.ppermute(g, 'y', shift(4, s))  16.5 us
    pallas_call x1, Pallas kernels, ffn_back(): pl.pallas_call(ffn_back_body, grid_spec=pltpu.PrefetchScalarGridSpec(num_...  15.5 us
    pallas_call x1, Pallas kernels, gate_up_grads(): pl.pallas_call(gate_up_grads_body, grid=(16 // QS,), out_shape=sds((2, 16...  14.6 us
    unnamed x102, local copies, waits for them, and re-layouts  13.4 us
  transfers between devices with their start and end apart: 60, of which 23 were waited for; matrix products, arithmetic and copies ran while one was open for 4% of the time, Pallas kernels for 30%

profile of v11, /device:TPU:1, one launch (start us, length us, event | category | flops | bytes accessed | tf_op | source)
XLA Modules:
  0.0 460.4 jit_solution(9274351894237896704)
XLA Ops:
  15.3 3.7 collective-permute-start.5
  24.1 3.4 collective-permute-done.1.n3.refs_4_.refs_9_
  31.1 13.2 %collective-permute-done.4.w1 = bf16[512,640]{1,0:T(8,128)(2,1)S(1)} collective-permute-done((bf16[512,640]{1,0:T(8,128)(2,1)}, bf16[512,640]{1,0:T(8,128)(2,1)S(1)}, u32[]{:S(2)}, u32[]{:S(2)}) %collective-permute-start.4) | collective-permute-done | bytes 655392 | tf_op jit(solution)/shard_map/ppermute | solution.py:134
  52.7 6.8 %qkv_forward.1 = (bf16[4,1280,128]{2,1,0:T(8,128)(2,1)}, bf16[640,128]{1,0:T(8,128)(2,1)}) custom-call(s32[4]{0:T(128)} %pad_add_fusion.idx, bf16[160,2048]{1,0:T(8,128)(2,1)} %copy-done.7, bf16[160,2048]{1,0:T(8,128)(2,1)} %collective-permute-done.n1.refs_1_.refs_6_, bf16[80,2048]{1,0:T(8,128)(2,1)} %collective-permute-done.2.n2a.refs_2_.refs_7_, ...), custom_call_target="tpu_custom_call" | custom-call | flops 1677721600 | bytes 7000000 | tf_op jit(solution)/shard_map/qkv_forward/pallas_call | solution.py:175
  59.5 3.0 collective-permute-start.7
  66.7 2.7 collective-permute-start.21
  69.4 8.6 %attend.1 = (bf16[4,160,512]{2,1,0:T(8,128)(2,1)}, bf16[4,1280,128]{2,1,0:T(8,128)(2,1)}) custom-call(s32[4]{0:T(128)} %pad_add_fusion.idx, bf16[4,1280,128]{2,1,0:T(8,128)(2,1)} %get-tuple-element.107.q, bf16[640,128]{1,0:T(8,128)(2,1)} %get-tuple-element.108.kv_own, bf16[640,128]{1,0:T(8,128)(2,1)} %copy-done.50, s32[1,1280]{1,0:T(1,128)} %reshape_tile.3.first), custom_call_target="tpu_custom_call" | custom-call | flops 12000000000 | bytes 3000000 | tf_op jit(solution)/shard_map/attend/pallas_call | solution.py:268
  81.1 4.9 %out_project.1 = (bf16[160,2048]{1,0:T(8,128)(2,1)}, bf16[160,2048]{1,0:T(8,128)(2,1)}, bf16[80,2048]{1,0:T(8,128)(2,1)}, bf16[80,2048]{1,0:T(8,128)(2,1)}, bf16[160,2048]{1,0:T(8,128)(2,1)}) custom-call(s32[4]{0:T(128)} %pad_add_fusion.idx, bf16[4,160,512]{2,1,0:T(8,128)(2,1)} %get-tuple-element.157.att, bf16[256,2048]{1,0:T(8,128)(2,1)} %w0.8, ...), custom_call_target="tpu_custom_call" | custom-call | flops 1342177280 | bytes 5500000 | tf_op jit(solution)/shard_map/out_project/pallas_call | solution.py:305
  87.3 3.0 collective-permute-start.16
  90.3 3.0 collective-permute-start.13
  93.3 6.6 %collective-permute-done.13.got_b = bf16[80,2048]{1,0:T(8,128)(2,1)S(1)} collective-permute-done((bf16[80,2048]{1,0:T(8,128)(2,1)}, bf16[80,2048]{1,0:T(8,128)(2,1)S(1)}, u32[]{:S(2)}, u32[]{:S(2)}) %collective-permute-start.13) | collective-permute-done | bytes 327712 | tf_op jit(solution)/shard_map/ppermute | solution.py:87
  99.9 3.1 collective-permute-done.12.got_a
  105.9 2.7 collective-permute-start.15
  108.6 13.2 %collective-permute-done.14.b = bf16[160,2048]{1,0:T(8,128)(2,1)S(1)} collective-permute-done((bf16[160,2048]{1,0:T(8,128)(2,1)}, bf16[160,2048]{1,0:T(8,128)(2,1)S(1)}, u32[]{:S(2)}, u32[]{:S(2)}) %collective-permute-start.14) | collective-permute-done | bytes 655392 | tf_op jit(solution)/shard_map/ppermute | solution.py:108
  122.8 2.9 norm_two.1
  125.7 2.8 collective-permute-start.22
  131.0 14.4 %collective-permute-done.18.refs_1_.refs_6_ = bf16[160,2048]{1,0:T(8,128)(2,1)S(1)} collective-permute-done((bf16[160,2048]{1,0:T(8,128)(2,1)}, bf16[160,2048]{1,0:T(8,128)(2,1)S(1)}, u32[]{:S(2)}, u32[]{:S(2)}) %collective-permute-start.18) | collective-permute-done | bytes 655392 | tf_op jit(solution)/shard_map/ppermute | solution.py:71
  149.1 3.1 collective-permute-start.20
  152.3 17.4 %ffn.1 = (bf16[640,1408]{1,0:T(8,128)(2,1)}, bf16[640,1408]{1,0:T(8,128)(2,1)}, bf16[640,1408]{1,0:T(8,128)(2,1)}) custom-call(s32[4]{0:T(128)} %pad_add_fusion.idx, bf16[160,2048]{1,0:T(8,128)(2,1)} %get-tuple-element.123.refs_0_.refs_5_, bf16[160,2048]{1,0:T(8,128)(2,1)} %copy-done.2, bf16[160,2048]{1,0:T(8,128)(2,1)} %copy-done.3, ...), custom_call_target="tpu_custom_call" | custom-call | flops 8304721920 | bytes 25000000 | tf_op jit(solution)/shard_map/ffn/pallas_call | solution.py:521
  170.6 12.4 %ffn_last.1 = (bf16[640,1408]{1,0:T(8,128)(2,1)}, bf16[640,1408]{1,0:T(8,128)(2,1)}, bf16[640,1408]{1,0:T(8,128)(2,1)}) custom-call(s32[4]{0:T(128)} %pad_add_fusion.idx, bf16[80,2048]{1,0:T(8,128)(2,1)} %copy-done.4, bf16[80,2048]{1,0:T(8,128)(2,1)} %copy-done.5, ...), custom_call_target="tpu_custom_call", output_to_operand_aliasing={{0}: (11, {}), {1}: (12, {}), {2}: (13, {})} | custom-call | flops 2768240640 | bytes 25000000 | tf_op jit(solution)/shard_map/ffn_last/pallas_call | solution.py:521
  183.0 15.5 %ffn_back.1 = (bf16[160,2048]{1,0:T(8,128)(2,1)}, bf16[160,2048]{1,0:T(8,128)(2,1)}, bf16[80,2048]{1,0:T(8,128)(2,1)}, bf16[80,2048]{1,0:T(8,128)(2,1)}, bf16[160,2048]{1,0:T(8,128)(2,1)}) custom-call(s32[4]{0:T(128)} %pad_add_fusion.idx, bf16[640,1408]{1,0:T(8,128)(2,1)} %get-tuple-element.192.dgate.refs_10_, ...), custom_call_target="tpu_custom_call" | custom-call | flops 7381975040 | bytes 18000000 | tf_op jit(solution)/shard_map/ffn_back/pallas_call | solution.py:591
  198.5 2.7 collective-permute-start.24
  201.2 9.1 %down_grads.1.refs_12_ = bf16[2,16,2112,128]{3,2,1,0:T(8,128)(2,1)} custom-call(bf16[160,2048]{1,0:T(8,128)(2,1)} %refs_0_.1, bf16[160,2048]{1,0:T(8,128)(2,1)} %collective-permute-done.8.refs_4_.refs_1_, bf16[160,2048]{1,0:T(8,128)(2,1)} %collective-permute-done.10.refs_5_.refs_2_, bf16[160,2048]{1,0:T(8,128)(2,1)} %copy-done.9, ...), custom_call_target="tpu_custom_call" | custom-call | flops 3690987520 | bytes 10000000 | tf_op jit(solution)/shard_map/down_grads/pallas_call | solution.py:658
  213.4 2.7 collective-permute-start.26
  216.1 14.6 %gate_up_grads.1 = bf16[2,16,2112,128]{3,2,1,0:T(8,128)(2,1)} custom-call(bf16[160,2048]{1,0:T(8,128)(2,1)} %get-tuple-element.123.refs_0_.refs_5_, bf16[160,2048]{1,0:T(8,128)(2,1)} %copy-done.2, bf16[160,2048]{1,0:T(8,128)(2,1)} %copy-done.3, bf16[80,2048]{1,0:T(8,128)(2,1)} %copy-done.4, ...), custom_call_target="tpu_custom_call", output_to_operand_aliasing={{}: (12, {})} | custom-call | flops 7381975040 | bytes 20000000 | tf_op jit(solution)/shard_map/gate_up_grads/pallas_call | solution.py:627
  231.8 4.0 norm_back_two.1
  237.4 12.1 %collective-permute-done.28.b1.refs_11_ = bf16[160,2048]{1,0:T(8,128)(2,1)S(1)} collective-permute-done((bf16[160,2048]{1,0:T(8,128)(2,1)}, bf16[160,2048]{1,0:T(8,128)(2,1)S(1)}, u32[]{:S(2)}, u32[]{:S(2)}) %collective-permute-start.28) | collective-permute-done | bytes 655392 | tf_op jit(solution)/shard_map/ppermute | solution.py:71
  253.0 10.6 %down_project.1 = (bf16[160,2048]{1,0:T(8,128)(2,1)}, bf16[160,2048]{1,0:T(8,128)(2,1)}, bf16[160,2048]{1,0:T(8,128)(2,1)}, bf16[160,2048]{1,0:T(8,128)(2,1)}) custom-call(s32[4]{0:T(128)} %pad_add_fusion.idx, bf16[640,1408]{1,0:T(8,128)(2,1)} %get-tuple-element.193.hid.refs_4_, bf16[704,2048]{1,0:T(8,128)(2,1)} %w0.7, bf16[352,2048]{1,0:T(8,128)(2,1)} %copy-done.12, ...), custom_call_target="tpu_custom_call" | custom-call | flops 3690987520 | bytes 11000000 | tf_op jit(solution)/shard_map/down_project/pallas_call | solution.py:557
  266.4 20.4 %attend_back.1 = (bf16[4,160,512]{2,1,0:T(8,128)(2,1)}, f32[640,128]{1,0:T(8,128)}, bf16[640,128]{1,0:T(8,128)(2,1)}) custom-call(s32[4]{0:T(128)} %pad_add_fusion.idx, bf16[4,1280,128]{2,1,0:T(8,128)(2,1)} %get-tuple-element.154.qx, bf16[640,128]{1,0:T(8,128)(2,1)} %get-tuple-element.108.kv_own, bf16[640,128]{1,0:T(8,128)(2,1)} %copy-done.50, ...), custom_call_target="tpu_custom_call" | custom-call | flops 30000001024 | bytes 8000000 | tf_op jit(solution)/shard_map/attend_back/pallas_call | solution.py:377
  286.8 9.0 %attn_grads.1 = (bf16[4,2,1024,128]{3,2,1,0:T(8,128)(2,1)}, bf16[4,2,1024,128]{3,2,1,0:T(8,128)(2,1)}) custom-call(s32[4]{0:T(128)} %pad_add_fusion.idx, bf16[160,2048]{1,0:T(8,128)(2,1)} %copy-done.7, bf16[160,2048]{1,0:T(8,128)(2,1)} %collective-permute-done.n1.refs_1_.refs_6_, bf16[80,2048]{1,0:T(8,128)(2,1)} %collective-permute-done.2.n2a.refs_2_.refs_7_, ...), custom_call_target="tpu_custom_call" | custom-call | flops 2684354560 | bytes 10000000 | tf_op jit(solution)/shard_map/attn_grads/pallas_call | solution.py:737
  296.1 7.0 %collective-permute-start.34 = (bf16[4,2,1024,128]{3,2,1,0:T(8,128)(2,1)}, bf16[4,2,1024,128]{3,2,1,0:T(8,128)(2,1)S(1)}, u32[]{:S(2)}, u32[]{:S(2)}) collective-permute-start(bf16[4,2,1024,128]{3,2,1,0:T(8,128)(2,1)} %get-tuple-element.162), channel_id=1, source_target_pairs={{0,8},{8,0},{1,9},{9,1},{2,10},{10,2},{3,11},{11,3},{4,12},{12,4},... | collective-permute-start | bytes 6291464 | tf_op jit(solution)/shard_map/ppermute | solution.py:808
  303.1 7.2 %qkv_back.1 = (bf16[4,2,144,128]{3,2,1,0:T(8,128)(2,1)}, bf16[4,2,144,128]{3,2,1,0:T(8,128)(2,1)}, bf16[160,2048]{1,0:T(8,128)(2,1)}, bf16[160,2048]{1,0:T(8,128...) custom-call(s32[4]{0:T(128)} %pad_add_fusion.idx, ...), custom_call_target="tpu_custom_call" | custom-call | flops 1677721600 | bytes 13000000 | tf_op jit(solution)/shard_map/qkv_back/pallas_call | solution.py:434
  314.0 4.0 sum_core.1
  317.9 2.8 collective-permute-start.36
  323.4 16.7 %collective-permute-done.36.b = bf16[2,1168,128]{2,1,0:T(8,128)(2,1)S(1)} collective-permute-done((bf16[2,1168,128]{2,1,0:T(8,128)(2,1)}, bf16[2,1168,128]{2,1,0:T(8,128)(2,1)S(1)}, u32[]{:S(2)}, u32[]{:S(2)}) %collective-permute-start.36) | collective-permute-done | bytes 598048 | tf_op jit(solution)/shard_map/ppermute | solution.py:812
  340.1 12.7 %collective-permute-done.37.c = bf16[2,1168,128]{2,1,0:T(8,128)(2,1)S(1)} collective-permute-done((bf16[2,1168,128]{2,1,0:T(8,128)(2,1)}, bf16[2,1168,128]{2,1,0:T(8,128)(2,1)S(1)}, u32[]{:S(2)}, u32[]{:S(2)}) %collective-permute-start.37) | collective-permute-done | bytes 598048 | tf_op jit(solution)/shard_map/ppermute | solution.py:812
  353.8 2.7 sum_y.1
  362.4 4.1 collective-permute-done.40.got_a
  370.2 8.1 %collective-permute-done.46.d = bf16[1168,128]{1,0:T(8,128)(2,1)S(1)} collective-permute-done((bf16[1168,128]{1,0:T(8,128)(2,1)}, bf16[1168,128]{1,0:T(8,128)(2,1)S(1)}, u32[]{:S(2)}, u32[]{:S(2)}) %collective-permute-start.46) | collective-permute-done | bytes 299040 | tf_op jit(solution)/shard_map/ppermute | solution.py:824
  388.4 4.0 collective-permute-done.49.refs_3_
  393.1 6.6 %collective-permute-done.48.refs_2_ = bf16[1168,128]{1,0:T(8,128)(2,1)S(1)} collective-permute-done((bf16[1168,128]{1,0:T(8,128)(2,1)}, bf16[1168,128]{1,0:T(8,128)(2,1)S(1)}, u32[]{:S(2)}, u32[]{:S(2)}) %collective-permute-start.48) | collective-permute-done | bytes 299040 | tf_op jit(solution)/shard_map/ppermute | solution.py:828
  399.7 6.9 %collective-permute-start.50 = (bf16[1168,128]{1,0:T(8,128)(2,1)}, bf16[1168,128]{1,0:T(8,128)(2,1)S(1)}, u32[]{:S(2)}, u32[]{:S(2)}) collective-permute-start(bf16[1168,128]{1,0:T(8,128)(2,1)} %sum_z.1.refs_0_), channel_id=1, source_target_pairs={{0,8},{8,0},{1,9},{9,1},{2,10},{10,2},{3,11},{11,3},{4,12},{12,4},... | collective-permute-start | bytes 897032 | tf_op jit(solution)/shard_map/ppermute | solution.py:829
  406.7 5.9 %collective-permute-done.47.refs_1_ = bf16[1168,128]{1,0:T(8,128)(2,1)S(1)} collective-permute-done((bf16[1168,128]{1,0:T(8,128)(2,1)}, bf16[1168,128]{1,0:T(8,128)(2,1)S(1)}, u32[]{:S(2)}, u32[]{:S(2)}) %collective-permute-start.47) | collective-permute-done | bytes 299040 | tf_op jit(solution)/shard_map/ppermute | solution.py:828
  412.6 3.7 collective-permute-start.53
  418.9 4.3 unpack_tail.1
  427.4 3.9 norm_back_one.1
  431.9 11.8 %all-gather.5.cloned.1.call-done.piece = bf16[16,2112,128]{2,1,0:T(8,128)(2,1)} async-done(((bf16[1,2112,128]{2,1,0:T(8,128)(2,1)}), bf16[16,2112,128]{2,1,0:T(8,128)(2,1)}) %all-gather.5.cloned.1.call-update) | async-done | bytes 8650768 | tf_op jit(solution)/shard_map/all_gather | solution.py:994
  443.7 9.8 %unpack.1 = (f32[1024,1408]{1,0:T(8,128)}, f32[1024,1408]{1,0:T(8,128)}, f32[704,2048]{1,0:T(8,128)}) custom-call(bf16[16,2112,128]{2,1,0:T(8,128)(2,1)} %all-gather.5.cloned.1.call-done.piece), custom_call_target="tpu_custom_call" | custom-call | flops 1000000 | bytes 26000000 | tf_op jit(solution)/shard_map/unpack/pallas_call | solution.py:682
  (237 shorter events, 92.4 us)
Async XLA Ops:
  7.2 145.1 %all-gather.3.cloned.1.call-start = ((), (), s32[]{:S(2)}) async-start(), calls=%async_computation.1 | async-start | bytes 6782976 | tf_op jit(solution)/shard_map/all_gather | solution.py:944
  10.0 17.5 %collective-permute-start.1 = (bf16[160,2048]{1,0:T(8,128)(2,1)S(1)}, bf16[160,2048]{1,0:T(8,128)(2,1)S(1)}, u32[]{:S(2)}, u32[]{:S(2)}) collective-permute-start(bf16[160,2048]{1,0:T(8,128)(2,1)S(1)} %fusion.2.n0.refs_0_.refs_5_), channel_id=1, source_target_pairs={{0,2},{2,4},{4,6},{6,0},{1,3},{3,5},{5,7},{7,1},{8,10},{10,12},{12... | collective-permute-start | bytes 1966088 | tf_op jit(solution)/shard_map/ppermute | solution.py:70
  12.1 15.4 %collective-permute-start = (bf16[160,2048]{1,0:T(8,128)(2,1)S(1)}, bf16[160,2048]{1,0:T(8,128)(2,1)}, u32[]{:S(2)}, u32[]{:S(2)}) collective-permute-start(bf16[160,2048]{1,0:T(8,128)(2,1)S(1)} %fusion.2.n0.refs_0_.refs_5_), channel_id=1, source_target_pairs={{0,6},{2,0},{4,2},{6,4},{1,7},{3,1},{5,3},{7,5},{8,14},{10,8},{12,... | collective-permute-start | bytes 1966088 | tf_op jit(solution)/shard_map/ppermute | solution.py:71
  15.3 15.8 %collective-permute-start.5 = (bf16[128,2048]{1,0:T(8,128)(2,1)}, bf16[128,2048]{1,0:T(8,128)(2,1)}, u32[]{:S(2)}, u32[]{:S(2)}) collective-permute-start(bf16[128,2048]{1,0:T(8,128)(2,1)} %constant_dynamic-slice_fusion.4), channel_id=1, source_target_pairs={{0,1},{1,0},{2,3},{3,2},{4,5},{5,4},{6,7},{7,6},{8,9},{9,8},{10,11... | collective-permute-start | bytes 1572872 | tf_op jit(solution)/shard_map/ppermute | solution.py:134
  19.9 24.4 %collective-permute-start.4 = (bf16[512,640]{1,0:T(8,128)(2,1)}, bf16[512,640]{1,0:T(8,128)(2,1)S(1)}, u32[]{:S(2)}, u32[]{:S(2)}) collective-permute-start(bf16[512,640]{1,0:T(8,128)(2,1)} %constant_dynamic-slice_fusion.5), channel_id=1, source_target_pairs={{0,1},{1,0},{2,3},{3,2},{4,5},{5,4},{6,7},{7,6},{8,9},{9,8},{10,11... | collective-permute-start | bytes 1966088 | tf_op jit(solution)/shard_map/ppermute | solution.py:134
  28.7 15.6 %collective-permute-start.3 = (bf16[80,2048]{1,0:T(8,128)(2,1)S(1)}, bf16[80,2048]{1,0:T(8,128)(2,1)S(1)}, u32[]{:S(2)}, u32[]{:S(2)}) collective-permute-start(bf16[80,2048]{1,0:T(8,128)(2,1)S(1)} %slice.38), channel_id=1, source_target_pairs={{0,6},{2,0},{4,2},{6,4},{1,7},{3,1},{5,3},{7,5},{8,14},{10,8},{12,... | collective-permute-start | bytes 983048 | tf_op jit(solution)/shard_map/ppermute | solution.py:75
  31.1 14.0 %collective-permute-start.2 = (bf16[80,2048]{1,0:T(8,128)(2,1)S(1)}, bf16[80,2048]{1,0:T(8,128)(2,1)}, u32[]{:S(2)}, u32[]{:S(2)}) collective-permute-start(bf16[80,2048]{1,0:T(8,128)(2,1)S(1)} %slice.37), channel_id=1, source_target_pairs={{0,2},{2,4},{4,6},{6,0},{1,3},{3,5},{5,7},{7,1},{8,10},{10,12},{12... | collective-permute-start | bytes 983048 | tf_op jit(solution)/shard_map/ppermute | solution.py:74
  48.3 29.7 %collective-permute-start.10 = (bf16[160,2048]{1,0:T(8,128)(2,1)S(1)}, bf16[160,2048]{1,0:T(8,128)(2,1)}, u32[]{:S(2)}, u32[]{:S(2)}) collective-permute-start(bf16[160,2048]{1,0:T(8,128)(2,1)S(1)} %copy-done.8), channel_id=1, source_target_pairs={{0,2},{2,4},{4,6},{6,0},{1,3},{3,5},{5,7},{7,1},{8,10},{10,12},{12... | collective-permute-start | bytes 1966088 | tf_op jit(solution)/shard_map/ppermute | solution.py:923
  48.3 31.4 %collective-permute-start.9 = (bf16[160,2048]{1,0:T(8,128)(2,1)S(1)}, bf16[160,2048]{1,0:T(8,128)(2,1)S(1)}, u32[]{:S(2)}, u32[]{:S(2)}) collective-permute-start(bf16[160,2048]{1,0:T(8,128)(2,1)S(1)} %copy-done.8), channel_id=1, source_target_pairs={{0,4},{2,6},{4,0},{6,2},{1,5},{3,7},{5,1},{7,3},{8,12},{10,14},{12... | collective-permute-start | bytes 1966088 | tf_op jit(solution)/shard_map/ppermute | solution.py:923
  50.7 29.6 %collective-permute-start.8 = (bf16[160,2048]{1,0:T(8,128)(2,1)S(1)}, bf16[160,2048]{1,0:T(8,128)(2,1)}, u32[]{:S(2)}, u32[]{:S(2)}) collective-permute-start(bf16[160,2048]{1,0:T(8,128)(2,1)S(1)} %copy-done.8), channel_id=1, source_target_pairs={{0,6},{2,0},{4,2},{6,4},{1,7},{3,1},{5,3},{7,5},{8,14},{10,8},{12,... | collective-permute-start | bytes 1966088 | tf_op jit(solution)/shard_map/ppermute | solution.py:923
  64.5 15.8 %collective-permute-start.11 = (bf16[128,2048]{1,0:T(8,128)(2,1)}, bf16[128,2048]{1,0:T(8,128)(2,1)S(1)}, u32[]{:S(2)}, u32[]{:S(2)}) collective-permute-start(bf16[128,2048]{1,0:T(8,128)(2,1)} %collective-permute-done.5.w1), channel_id=1, source_target_pairs={{0,8},{8,0},{1,9},{9,1},{2,10},{10,2},{3,11},{11,3},{4,12},{12,4},... | collective-permute-start | bytes 1572872 | tf_op jit(solution)/shard_map/ppermute | solution.py:918
  66.7 19.3 %collective-permute-start.21 = (bf16[128,2944]{1,0:T(8,128)(2,1)}, bf16[128,2944]{1,0:T(8,128)(2,1)}, u32[]{:S(2)}, u32[]{:S(2)}) collective-permute-start(bf16[128,2944]{1,0:T(8,128)(2,1)} %pad_maximum_fusion), channel_id=1, source_target_pairs={{0,17},{1,16},{16,1},{17,0},{2,19},{3,18},{18,3},{19,2},{4,21},{5,... | collective-permute-start | bytes 2261000 | tf_op jit(solution)/shard_map/ppermute | solution.py:929
  86.0 295.9 %reduce-scatter.2.cloned.1.call-start = ((), (), s32[]{:S(2)}) async-start(), calls=%async_computation.2 | async-start | bytes 17842176 | tf_op jit(solution)/shard_map/reduce_scatter | solution.py:962
  87.3 38.4 %collective-permute-start.16 = (bf16[352,2048]{1,0:T(8,128)(2,1)}, bf16[352,2048]{1,0:T(8,128)(2,1)S(1)}, u32[]{:S(2)}, u32[]{:S(2)}) collective-permute-start(bf16[352,2048]{1,0:T(8,128)(2,1)} %constant_dynamic-slice_fusion.2), channel_id=1, source_target_pairs={{0,1},{1,0},{2,3},{3,2},{4,5},{5,4},{6,7},{7,6},{8,9},{9,8},{10,11... | collective-permute-start | bytes 4325384 | tf_op jit(solution)/shard_map/ppermute | solution.py:134
  90.3 9.6 %collective-permute-start.13 = (bf16[80,2048]{1,0:T(8,128)(2,1)}, bf16[80,2048]{1,0:T(8,128)(2,1)S(1)}, u32[]{:S(2)}, u32[]{:S(2)}) collective-permute-start(bf16[80,2048]{1,0:T(8,128)(2,1)} %get-tuple-element.117), channel_id=1, source_target_pairs={{0,6},{2,0},{4,2},{6,4},{1,7},{3,1},{5,3},{7,5},{8,14},{10,8},{12,... | collective-permute-start | bytes 983048 | tf_op jit(solution)/shard_map/ppermute | solution.py:87
  93.3 9.7 %collective-permute-start.12 = (bf16[80,2048]{1,0:T(8,128)(2,1)}, bf16[80,2048]{1,0:T(8,128)(2,1)S(1)}, u32[]{:S(2)}, u32[]{:S(2)}) collective-permute-start(bf16[80,2048]{1,0:T(8,128)(2,1)} %get-tuple-element.115), channel_id=1, source_target_pairs={{0,2},{2,4},{4,6},{6,0},{1,3},{3,5},{5,7},{7,1},{8,10},{10,12},{12... | collective-permute-start | bytes 983048 | tf_op jit(solution)/shard_map/ppermute | solution.py:86
  105.9 15.9 %collective-permute-start.14 = (bf16[160,2048]{1,0:T(8,128)(2,1)}, bf16[160,2048]{1,0:T(8,128)(2,1)S(1)}, u32[]{:S(2)}, u32[]{:S(2)}) collective-permute-start(bf16[160,2048]{1,0:T(8,128)(2,1)} %get-tuple-element.118), channel_id=1, source_target_pairs={{0,2},{2,4},{4,6},{6,0},{1,3},{3,5},{5,7},{7,1},{8,10},{10,12},{12... | collective-permute-start | bytes 1966088 | tf_op jit(solution)/shard_map/ppermute | solution.py:108
  105.9 15.9 %collective-permute-start.15 = (bf16[160,2048]{1,0:T(8,128)(2,1)}, bf16[160,2048]{1,0:T(8,128)(2,1)S(1)}, u32[]{:S(2)}, u32[]{:S(2)}) collective-permute-start(bf16[160,2048]{1,0:T(8,128)(2,1)} %get-tuple-element.119), channel_id=1, source_target_pairs={{0,6},{2,0},{4,2},{6,4},{1,7},{3,1},{5,3},{7,5},{8,14},{10,8},{12,... | collective-permute-start | bytes 1966088 | tf_op jit(solution)/shard_map/ppermute | solution.py:108
  125.7 26.6 %collective-permute-start.22 = (bf16[352,2048]{1,0:T(8,128)(2,1)S(1)}, bf16[352,2048]{1,0:T(8,128)(2,1)}, u32[]{:S(2)}, u32[]{:S(2)}) collective-permute-start(bf16[352,2048]{1,0:T(8,128)(2,1)S(1)} %collective-permute-done.16.refs_11_.refs_8_.w1), channel_id=1, source_target_pairs={{0,8},{8,0},{1,9},{9,1},{2,10},{10,2},{3,11},{11,3},{4,12},{12,4},... | collective-permute-start | bytes 4325384 | tf_op jit(solution)/shard_map/ppermute | solution.py:951
  128.5 16.9 %collective-permute-start.18 = (bf16[160,2048]{1,0:T(8,128)(2,1)}, bf16[160,2048]{1,0:T(8,128)(2,1)S(1)}, u32[]{:S(2)}, u32[]{:S(2)}) collective-permute-start(bf16[160,2048]{1,0:T(8,128)(2,1)} %get-tuple-element.123.refs_0_.refs_5_), channel_id=1, source_target_pairs={{0,6},{2,0},{4,2},{6,4},{1,7},{3,1},{5,3},{7,5},{8,14},{10,8},{12,... | collective-permute-start | bytes 1966088 | tf_op jit(solution)/shard_map/ppermute | solution.py:71
  131.0 17.4 %collective-permute-start.17 = (bf16[160,2048]{1,0:T(8,128)(2,1)}, bf16[160,2048]{1,0:T(8,128)(2,1)S(1)}, u32[]{:S(2)}, u32[]{:S(2)}) collective-permute-start(bf16[160,2048]{1,0:T(8,128)(2,1)} %get-tuple-element.123.refs_0_.refs_5_), channel_id=1, source_target_pairs={{0,2},{2,4},{4,6},{6,0},{1,3},{3,5},{5,7},{7,1},{8,10},{10,12},{12... | collective-permute-start | bytes 1966088 | tf_op jit(solution)/shard_map/ppermute | solution.py:70
  149.1 20.6 %collective-permute-start.19 = (bf16[80,2048]{1,0:T(8,128)(2,1)}, bf16[80,2048]{1,0:T(8,128)(2,1)S(1)}, u32[]{:S(2)}, u32[]{:S(2)}) collective-permute-start(bf16[80,2048]{1,0:T(8,128)(2,1)} %slice.39), channel_id=1, source_target_pairs={{0,2},{2,4},{4,6},{6,0},{1,3},{3,5},{5,7},{7,1},{8,10},{10,12},{12... | collective-permute-start | bytes 983048 | tf_op jit(solution)/shard_map/ppermute | solution.py:74
  149.1 20.6 %collective-permute-start.20 = (bf16[80,2048]{1,0:T(8,128)(2,1)}, bf16[80,2048]{1,0:T(8,128)(2,1)S(1)}, u32[]{:S(2)}, u32[]{:S(2)}) collective-permute-start(bf16[80,2048]{1,0:T(8,128)(2,1)} %slice.40), channel_id=1, source_target_pairs={{0,6},{2,0},{4,2},{6,4},{1,7},{3,1},{5,3},{7,5},{8,14},{10,8},{12,... | collective-permute-start | bytes 983048 | tf_op jit(solution)/shard_map/ppermute | solution.py:75
  198.5 11.8 %collective-permute-start.23 = (bf16[80,2048]{1,0:T(8,128)(2,1)}, bf16[80,2048]{1,0:T(8,128)(2,1)S(1)}, u32[]{:S(2)}, u32[]{:S(2)}) collective-permute-start(bf16[80,2048]{1,0:T(8,128)(2,1)} %get-tuple-element.138), channel_id=1, source_target_pairs={{0,2},{2,4},{4,6},{6,0},{1,3},{3,5},{5,7},{7,1},{8,10},{10,12},{12... | collective-permute-start | bytes 983048 | tf_op jit(solution)/shard_map/ppermute | solution.py:86
  198.5 11.8 %collective-permute-start.24 = (bf16[80,2048]{1,0:T(8,128)(2,1)}, bf16[80,2048]{1,0:T(8,128)(2,1)S(1)}, u32[]{:S(2)}, u32[]{:S(2)}) collective-permute-start(bf16[80,2048]{1,0:T(8,128)(2,1)} %get-tuple-element.140), channel_id=1, source_target_pairs={{0,6},{2,0},{4,2},{6,4},{1,7},{3,1},{5,3},{7,5},{8,14},{10,8},{12,... | collective-permute-start | bytes 983048 | tf_op jit(solution)/shard_map/ppermute | solution.py:87
  213.4 17.3 %collective-permute-start.25 = (bf16[160,2048]{1,0:T(8,128)(2,1)}, bf16[160,2048]{1,0:T(8,128)(2,1)S(1)}, u32[]{:S(2)}, u32[]{:S(2)}) collective-permute-start(bf16[160,2048]{1,0:T(8,128)(2,1)} %get-tuple-element.141), channel_id=1, source_target_pairs={{0,2},{2,4},{4,6},{6,0},{1,3},{3,5},{5,7},{7,1},{8,10},{10,12},{12... | collective-permute-start | bytes 1966088 | tf_op jit(solution)/shard_map/ppermute | solution.py:108
  213.4 17.3 %collective-permute-start.26 = (bf16[160,2048]{1,0:T(8,128)(2,1)}, bf16[160,2048]{1,0:T(8,128)(2,1)S(1)}, u32[]{:S(2)}, u32[]{:S(2)}) collective-permute-start(bf16[160,2048]{1,0:T(8,128)(2,1)} %get-tuple-element.142), channel_id=1, source_target_pairs={{0,6},{2,0},{4,2},{6,4},{1,7},{3,1},{5,3},{7,5},{8,14},{10,8},{12,... | collective-permute-start | bytes 1966088 | tf_op jit(solution)/shard_map/ppermute | solution.py:108
  231.8 211.9 %all-gather.5.cloned.1.call-start = ((), (), s32[]{:S(2)}) async-start(), calls=%async_computation.3 | async-start | bytes 9191424 | tf_op jit(solution)/shard_map/all_gather | solution.py:994
  235.9 13.6 %collective-permute-start.28 = (bf16[160,2048]{1,0:T(8,128)(2,1)}, bf16[160,2048]{1,0:T(8,128)(2,1)S(1)}, u32[]{:S(2)}, u32[]{:S(2)}) collective-permute-start(bf16[160,2048]{1,0:T(8,128)(2,1)} %get-tuple-element.147.b0.refs_10_), channel_id=1, source_target_pairs={{0,6},{2,0},{4,2},{6,4},{1,7},{3,1},{5,3},{7,5},{8,14},{10,8},{12,... | collective-permute-start | bytes 1966088 | tf_op jit(solution)/shard_map/ppermute | solution.py:71
  236.2 13.9 %collective-permute-start.27 = (bf16[160,2048]{1,0:T(8,128)(2,1)}, bf16[160,2048]{1,0:T(8,128)(2,1)S(1)}, u32[]{:S(2)}, u32[]{:S(2)}) collective-permute-start(bf16[160,2048]{1,0:T(8,128)(2,1)} %get-tuple-element.147.b0.refs_10_), channel_id=1, source_target_pairs={{0,2},{2,4},{4,6},{6,0},{1,3},{3,5},{5,7},{7,1},{8,10},{10,12},{12... | collective-permute-start | bytes 1966088 | tf_op jit(solution)/shard_map/ppermute | solution.py:70
  250.1 13.5 %collective-permute-start.29 = (bf16[80,2048]{1,0:T(8,128)(2,1)S(1)}, bf16[80,2048]{1,0:T(8,128)(2,1)S(1)}, u32[]{:S(2)}, u32[]{:S(2)}) collective-permute-start(bf16[80,2048]{1,0:T(8,128)(2,1)S(1)} %slice.41), channel_id=1, source_target_pairs={{0,2},{2,4},{4,6},{6,0},{1,3},{3,5},{5,7},{7,1},{8,10},{10,12},{12... | collective-permute-start | bytes 983048 | tf_op jit(solution)/shard_map/ppermute | solution.py:74
  250.8 12.8 %collective-permute-start.30 = (bf16[80,2048]{1,0:T(8,128)(2,1)S(1)}, bf16[80,2048]{1,0:T(8,128)(2,1)}, u32[]{:S(2)}, u32[]{:S(2)}) collective-permute-start(bf16[80,2048]{1,0:T(8,128)(2,1)S(1)} %slice.42), channel_id=1, source_target_pairs={{0,6},{2,0},{4,2},{6,4},{1,7},{3,1},{5,3},{7,5},{8,14},{10,8},{12,... | collective-permute-start | bytes 983048 | tf_op jit(solution)/shard_map/ppermute | solution.py:75
  263.6 23.1 %collective-permute-start.31 = (bf16[160,2048]{1,0:T(8,128)(2,1)}, bf16[160,2048]{1,0:T(8,128)(2,1)S(1)}, u32[]{:S(2)}, u32[]{:S(2)}) collective-permute-start(bf16[160,2048]{1,0:T(8,128)(2,1)} %get-tuple-element.150), channel_id=1, source_target_pairs={{0,2},{2,4},{4,6},{6,0},{1,3},{3,5},{5,7},{7,1},{8,10},{10,12},{12... | collective-permute-start | bytes 1966088 | tf_op jit(solution)/shard_map/ppermute | solution.py:975
  263.7 23.1 %collective-permute-start.32 = (bf16[160,2048]{1,0:T(8,128)(2,1)}, bf16[160,2048]{1,0:T(8,128)(2,1)S(1)}, u32[]{:S(2)}, u32[]{:S(2)}) collective-permute-start(bf16[160,2048]{1,0:T(8,128)(2,1)} %get-tuple-element.152), channel_id=1, source_target_pairs={{0,6},{2,0},{4,2},{6,4},{1,7},{3,1},{5,3},{7,5},{8,14},{10,8},{12,... | collective-permute-start | bytes 1966088 | tf_op jit(solution)/shard_map/ppermute | solution.py:975
  296.1 16.4 %collective-permute-start.34 = (bf16[4,2,1024,128]{3,2,1,0:T(8,128)(2,1)}, bf16[4,2,1024,128]{3,2,1,0:T(8,128)(2,1)S(1)}, u32[]{:S(2)}, u32[]{:S(2)}) collective-permute-start(bf16[4,2,1024,128]{3,2,1,0:T(8,128)(2,1)} %get-tuple-element.162), channel_id=1, source_target_pairs={{0,8},{8,0},{1,9},{9,1},{2,10},{10,2},{3,11},{11,3},{4,12},{12,4},... | collective-permute-start | bytes 6291464 | tf_op jit(solution)/shard_map/ppermute | solution.py:808
  317.9 22.2 %collective-permute-start.36 = (bf16[2,1168,128]{2,1,0:T(8,128)(2,1)}, bf16[2,1168,128]{2,1,0:T(8,128)(2,1)S(1)}, u32[]{:S(2)}, u32[]{:S(2)}) collective-permute-start(bf16[2,1168,128]{2,1,0:T(8,128)(2,1)} %get-tuple-element.168), channel_id=1, source_target_pairs={{0,64},{32,96},{64,0},{96,32},{1,65},{33,97},{65,1},{97,33},{2,66}... | collective-permute-start | bytes 1794056 | tf_op jit(solution)/shard_map/ppermute | solution.py:812
  320.8 32.1 %collective-permute-start.37 = (bf16[2,1168,128]{2,1,0:T(8,128)(2,1)}, bf16[2,1168,128]{2,1,0:T(8,128)(2,1)S(1)}, u32[]{:S(2)}, u32[]{:S(2)}) collective-permute-start(bf16[2,1168,128]{2,1,0:T(8,128)(2,1)} %get-tuple-element.169), channel_id=1, source_target_pairs={{0,32},{32,64},{64,96},{96,0},{1,33},{33,65},{65,97},{97,1},{2,34}... | collective-permute-start | bytes 1794056 | tf_op jit(solution)/shard_map/ppermute | solution.py:812
  321.2 31.6 %collective-permute-start.38 = (bf16[2,1168,128]{2,1,0:T(8,128)(2,1)}, bf16[2,1168,128]{2,1,0:T(8,128)(2,1)S(1)}, u32[]{:S(2)}, u32[]{:S(2)}) collective-permute-start(bf16[2,1168,128]{2,1,0:T(8,128)(2,1)} %get-tuple-element.170), channel_id=1, source_target_pairs={{0,96},{32,0},{64,32},{96,64},{1,97},{33,1},{65,33},{97,65},{2,98}... | collective-permute-start | bytes 1794056 | tf_op jit(solution)/shard_map/ppermute | solution.py:812
  356.5 10.1 %collective-permute-start.40 = (bf16[80,2048]{1,0:T(8,128)(2,1)S(1)}, bf16[80,2048]{1,0:T(8,128)(2,1)S(1)}, u32[]{:S(2)}, u32[]{:S(2)}) collective-permute-start(bf16[80,2048]{1,0:T(8,128)(2,1)S(1)} %copy-done.48), channel_id=1, source_target_pairs={{0,2},{2,4},{4,6},{6,0},{1,3},{3,5},{5,7},{7,1},{8,10},{10,12},{12... | collective-permute-start | bytes 983048 | tf_op jit(solution)/shard_map/ppermute | solution.py:86
  359.2 19.1 %collective-permute-start.46 = (bf16[1168,128]{1,0:T(8,128)(2,1)}, bf16[1168,128]{1,0:T(8,128)(2,1)S(1)}, u32[]{:S(2)}, u32[]{:S(2)}) collective-permute-start(bf16[1168,128]{1,0:T(8,128)(2,1)} %get-tuple-element.187), channel_id=1, source_target_pairs={{0,17},{1,16},{16,1},{17,0},{2,19},{3,18},{18,3},{19,2},{4,21},{5,... | collective-permute-start | bytes 897032 | tf_op jit(solution)/shard_map/ppermute | solution.py:824
  360.0 18.3 %collective-permute-start.45 = (bf16[1168,128]{1,0:T(8,128)(2,1)}, bf16[1168,128]{1,0:T(8,128)(2,1)S(1)}, u32[]{:S(2)}, u32[]{:S(2)}) collective-permute-start(bf16[1168,128]{1,0:T(8,128)(2,1)} %get-tuple-element.187), channel_id=1, source_target_pairs={{0,1},{1,0},{2,3},{3,2},{4,5},{5,4},{6,7},{7,6},{8,9},{9,8},{10,11... | collective-permute-start | bytes 897032 | tf_op jit(solution)/shard_map/ppermute | solution.py:823
  360.9 17.4 %collective-permute-start.44 = (bf16[1168,128]{1,0:T(8,128)(2,1)}, bf16[1168,128]{1,0:T(8,128)(2,1)S(1)}, u32[]{:S(2)}, u32[]{:S(2)}) collective-permute-start(bf16[1168,128]{1,0:T(8,128)(2,1)} %get-tuple-element.186.a), channel_id=1, source_target_pairs={{0,16},{16,0},{1,17},{17,1},{2,18},{18,2},{3,19},{19,3},{4,20},{20... | collective-permute-start | bytes 897032 | tf_op jit(solution)/shard_map/ppermute | solution.py:822
  381.9 34.3 %collective-permute-start.42 = (bf16[160,2048]{1,0:T(8,128)(2,1)}, bf16[160,2048]{1,0:T(8,128)(2,1)}, u32[]{:S(2)}, u32[]{:S(2)}) collective-permute-start(bf16[160,2048]{1,0:T(8,128)(2,1)} %get-tuple-element.183), channel_id=1, source_target_pairs={{0,2},{2,4},{4,6},{6,0},{1,3},{3,5},{5,7},{7,1},{8,10},{10,12},{12... | collective-permute-start | bytes 1966088 | tf_op jit(solution)/shard_map/ppermute | solution.py:108
  383.3 33.1 %collective-permute-start.43 = (bf16[160,2048]{1,0:T(8,128)(2,1)}, bf16[160,2048]{1,0:T(8,128)(2,1)}, u32[]{:S(2)}, u32[]{:S(2)}) collective-permute-start(bf16[160,2048]{1,0:T(8,128)(2,1)} %get-tuple-element.184), channel_id=1, source_target_pairs={{0,6},{2,0},{4,2},{6,4},{1,7},{3,1},{5,3},{7,5},{8,14},{10,8},{12,... | collective-permute-start | bytes 1966088 | tf_op jit(solution)/shard_map/ppermute | solution.py:108
  385.7 39.3 %collective-permute-start.39 = (bf16[160,2048]{1,0:T(8,128)(2,1)}, bf16[160,2048]{1,0:T(8,128)(2,1)}, u32[]{:S(2)}, u32[]{:S(2)}) collective-permute-start(bf16[160,2048]{1,0:T(8,128)(2,1)} %get-tuple-element.172), channel_id=1, source_target_pairs={{0,4},{2,6},{4,0},{6,2},{1,5},{3,7},{5,1},{7,3},{8,12},{10,14},{12... | collective-permute-start | bytes 1966088 | tf_op jit(solution)/shard_map/ppermute | solution.py:993
  387.2 12.6 %collective-permute-start.48 = (bf16[1168,128]{1,0:T(8,128)(2,1)}, bf16[1168,128]{1,0:T(8,128)(2,1)S(1)}, u32[]{:S(2)}, u32[]{:S(2)}) collective-permute-start(bf16[1168,128]{1,0:T(8,128)(2,1)} %sum_z.1.refs_0_), channel_id=1, source_target_pairs={{0,64},{32,96},{64,0},{96,32},{1,65},{33,97},{65,1},{97,33},{2,66}... | collective-permute-start | bytes 897032 | tf_op jit(solution)/shard_map/ppermute | solution.py:828
  392.4 20.2 %collective-permute-start.47 = (bf16[1168,128]{1,0:T(8,128)(2,1)}, bf16[1168,128]{1,0:T(8,128)(2,1)S(1)}, u32[]{:S(2)}, u32[]{:S(2)}) collective-permute-start(bf16[1168,128]{1,0:T(8,128)(2,1)} %sum_z.1.refs_0_), channel_id=1, source_target_pairs={{0,32},{32,64},{64,96},{96,0},{1,33},{33,65},{65,97},{97,1},{2,34}... | collective-permute-start | bytes 897032 | tf_op jit(solution)/shard_map/ppermute | solution.py:828
  399.7 17.0 %collective-permute-start.50 = (bf16[1168,128]{1,0:T(8,128)(2,1)}, bf16[1168,128]{1,0:T(8,128)(2,1)S(1)}, u32[]{:S(2)}, u32[]{:S(2)}) collective-permute-start(bf16[1168,128]{1,0:T(8,128)(2,1)} %sum_z.1.refs_0_), channel_id=1, source_target_pairs={{0,8},{8,0},{1,9},{9,1},{2,10},{10,2},{3,11},{11,3},{4,12},{12,4},... | collective-permute-start | bytes 897032 | tf_op jit(solution)/shard_map/ppermute | solution.py:829
  (63 other events, 524.3 us)
Sparse Core Ops, SparseCore 0:
  86.2 42.0 all-gather.2
  230.9 143.6 reduce-scatter.1
  382.1 61.5 all-gather.4

commit v12 on v10

--- a/solution.py
+++ b/solution.py
@@ -134,9 +134,10 @@
     return lax.ppermute(lax.dynamic_slice_in_dim(w, core * half, half, 0), "zh", shift(2, 1))
 
 
-def fetch_partner(w, core, *deps):
-    got = fetch_half(tie(w, *deps), core)
-    return w, got, lax.ppermute(got, "core", shift(2, 1))
+def own_and_partner(idx, rows):
+    zh = idx[1]
+    at = lambda k: pl.ds(pl.multiple_of(k * rows, rows), rows)
+    return at(zh), at(1 - zh)
 
 
 def weight_rows(idx, rows):
@@ -288,12 +289,11 @@
         ref[...] = res[row : row + n].astype(BF16)
 
 
-def out_body(idx, att, w0, w1, w2, o0, o1, o2a, o2b, o3):
-    s0, s1, s2 = weight_rows(idx, AW // 2)
+def out_body(idx, att, w0, w1, o0, o1, o2a, o2b, o3):
+    slots = own_and_partner(idx, AW // 2)
     for d, ref in ((2, None), (1, o1), (3, o3), (0, o0)):
         a = att.at[d]
-        res = dot(a[:, s0], w0[...]) + dot(a[:, s1], w1[...]) + dot(a[:, s2], w2[...])
-        res = res.astype(BF16)
+        res = sum(dot(a[:, s], w[...]) for s, w in zip(slots, (w0, w1))).astype(BF16)
         if d == 2:
             o2a[...] = res[:HALF]
             o2b[...] = res[HALF:]
@@ -305,7 +305,7 @@
     return pl.pallas_call(
         out_body,
         out_shape=part_shapes(D),
-        in_specs=[spec(pltpu.SMEM)] + [spec()] * 4,
+        in_specs=[spec(pltpu.SMEM)] + [spec()] * 3,
         out_specs=(spec(),) * 5,
         compiler_params=params(),
         cost_estimate=cost(2 * ROWS * D * AW, 5.5e6),
@@ -318,19 +318,19 @@
 
 
 def attend_back_body(
-    idx, qx, kv_own, kv_par, first, att, cosine, sine, b0, b1, b2a, b2b, b3, w0, w1, w2,
+    idx, qx, kv_own, kv_par, first, att, cosine, sine, b0, b1, b2a, b2b, b3, w0, w1,
     dq_ref, dkv_own, dkv_par, kk, vv, dout, do_all, dkk, dvv, e_ref, ds_ref, dq_acc,
 ):
     x, zh = idx[0], idx[1]
     spread_keys(zh, kv_own, kv_par, kk, vv, lambda lane: jnp.where(lane < 3, -1.0, 0.0))
-    s0, s1, s2 = weight_rows(idx, AW // 2)
+    slots = own_and_partner(idx, AW // 2)
     for d in range(4):
         if d == 2:
             rows = jnp.concatenate([b2a[...], b2b[...]], 0)
         else:
             rows = (b0, b1, None, b3)[d][...]
         at = rows_at((x + d) & 3)
-        for s, w in ((s0, w0), (s1, w1), (s2, w2)):
+        for s, w in zip(slots, (w0, w1)):
             dout[at, s] = dot_t(rows, w[...]).astype(BF16)
     lo = low_lanes((BLK, 128))
     for j in range(4):
@@ -377,7 +377,7 @@
     return pl.pallas_call(
         attend_back_body,
         out_shape=(sds((4, BLK, AW)), sds((ROWS, 128), F32), sds((ROWS, 128))),
-        in_specs=[spec(pltpu.SMEM)] + [spec()] * 15,
+        in_specs=[spec(pltpu.SMEM)] + [spec()] * 14,
         out_specs=(spec(),) * 3,
         scratch_shapes=[
             pltpu.VMEM((CAP, 128), BF16),
@@ -783,12 +783,11 @@
             gains[:, cols] = g[2 * c : 2 * c + 2]
 
 
-def sum_tail(idx, first, second, parts):
+def sum_tail(idx, first, second, parts, finish):
     got_a = lax.ppermute(first[1], "core", shift(2, 1))
     got_b = lax.ppermute(second[1], "core", shift(2, 1))
     part = sds((2, TAIL, 128))
     g = small_call(sum_core_body, (part,) * 4, idx, first[0], got_a, second[0], got_b, name="sum_core")
-    g_core = g[0]
     got = [lax.ppermute(g[s], "y", shift(4, s)) for s in (2, 1, 3)]
     part = sds((TAIL, 128))
     own, other = small_call(sum_y_body, (part,) * 2, idx, g[0], *got, name="sum_y")
@@ -805,10 +804,11 @@
         name="sum_z",
     )
     d_one = last_step(p0, q1, q3)
-    mine = [tie(g, *d_one)] + [lax.ppermute(g, "y", shift(4, s)) for s in (1, 2, 3)]
+    input_grad = finish(d_one)
+    mine = [tie(g, input_grad)] + [lax.ppermute(g, "y", shift(4, s)) for s in (1, 2, 3)]
     theirs = [lax.ppermute(v, "core", shift(2, 1)) for v in [g] + mine[1:]]
     shapes = (sds((DH, QW), F32), sds((AW // 2, D), F32), sds((2, D), F32))
-    return g_core, own, d_one, small_call(unpack_tail_body, shapes, idx, *mine, *theirs, name="unpack_tail")
+    return own, input_grad, small_call(unpack_tail_body, shapes, idx, *mine, *theirs, name="unpack_tail")
 
 
 def inverse_rms(v):
@@ -894,7 +894,11 @@
 
     qkv_got = fetch_half(qkv_weight, core)
     normed_one = gather_x((tok * s_one * gain_one).astype(BF16), (cosine,))
-    out_got = fetch_half(out_weight, core)
+    eighth = lambda w: lax.dynamic_slice_in_dim(w, (y * 2 + core) * (w.shape[0] // 8), w.shape[0] // 8, 0)
+    spread = lambda v: lax.all_gather(v, ("y", "core"), axis=0, tiled=True)
+    fetch = lambda w: lax.ppermute(eighth(w), "zh", shift(2, 1))
+    out_got = fetch(out_weight)
+    out_all = out_weight, spread(tie(out_got, normed_one[1], normed_one[4]))
     swap = lambda v, *deps: lax.ppermute(tie(v, *deps), "core", shift(2, 1))
     qkv_all = qkv_weight, qkv_got, swap(qkv_got, out_got, normed_one[2], normed_one[3])
 
@@ -902,16 +906,15 @@
     cot = tie(cotangent, normed_one[2], normed_one[3])
     cots = [cotangent] + [lax.ppermute(cot, "x", shift(4, -k)) for k in (1, 2, 3)]
     kv_par = lax.ppermute(kv_own, "zh", shift(2, 1))
-    out_all = out_weight, out_got, swap(out_got, kv_own)
+    down_got = fetch_half(tie(down_weight, kv_par), core)
     rows = DH // 8
-    mine = lambda w: lax.dynamic_slice_in_dim(w, (y * 2 + core) * rows, rows, 0)
     cross = [(2 * a + b, 2 * (1 - a) + (1 - b)) for a in range(2) for b in range(2)]
     gate_up = lax.ppermute(
         jnp.concatenate(
             [
-                mine(tie(gate_weight, kv_own)),
+                eighth(tie(gate_weight, kv_own)),
                 jnp.zeros((rows, GAP - FF4), BF16),
-                mine(tie(up_weight, kv_own)),
+                eighth(tie(up_weight, kv_own)),
             ],
             1,
         ),
@@ -920,15 +923,15 @@
     )
     att, qx = attend(idx, q, kv_own, kv_par, first)
     parts = out_project(idx, tie(att, *cots), out_all)
-    down_got = fetch_half(tie(down_weight, parts[2]), core)
-    gate_up = lax.all_gather(tie(gate_up, parts[2]), ("y", "core"), axis=0, tiled=True)
+    gate_up = spread(tie(gate_up, parts[2]))
+    p0, q1, q3 = relay(parts)
     after_attn, normed_two = row_call(
         norm_two_body,
         (sds((BLK, D), F32), sds((BLK, D))),
-        tokens, *scatter_x(parts), gain_two.reshape(1, D), name="norm_two",
+        tokens, *last_step(p0, q1, q3), gain_two.reshape(1, D), name="norm_two",
     )
     normed_two = gather_x(tie(normed_two, down_got))
-    down_all = down_weight, down_got, lax.ppermute(tie(down_got, normed_two[1], normed_two[4]), "core", shift(2, 1))
+    down_all = down_weight, down_got, swap(down_got, normed_two[1], normed_two[4])
     hid, dgate, dup = ffn(idx, normed_two, cots, gate_weight, up_weight, gate_up, down_all)
     d_parts = ffn_back(idx, dgate, dup, gate_weight, up_weight, gate_up)
     own_grads = down_grads(cots, tie(hid, d_parts[2]))
@@ -963,17 +966,17 @@
         gain_grad_two,
     )
     over_x = lambda v: sum((lax.ppermute(v, "x", shift(4, s)) for s in (1, 2, 3)), v)
-    cores_summed, summed, d_one, (grad_qkv, grad_out, gains) = sum_tail(
-        idx, (tail[0], tie(tail[1], dkv_got)), tail_kv, parts
+    finish = lambda d_one: row_call(
+        norm_back_body,
+        (sds((BLK, D), F32), sds((BLK, D)), sds((1, D), F32)),
+        after_grad, tokens, *d_one, gain_one.reshape(1, D), name="norm_back_one",
+    )[1]
+    summed, input_grad, (grad_qkv, grad_out, gains) = sum_tail(
+        idx, (tail[0], tie(tail[1], dkv_got)), tail_kv, parts, finish
     )
     layer.append(lax.ppermute(tie(layer_parts[2], summed), "x", shift(4, 2)))
     grads = lax.all_gather(tie(grads, summed), ("zl", "y", "core"), axis=0, tiled=True)
     grad_gate, grad_up, grad_down = unpack(grads)
-    _, input_grad, _ = row_call(
-        norm_back_body,
-        (sds((BLK, D), F32), sds((BLK, D)), sds((1, D), F32)),
-        after_grad, tokens, *d_one, gain_one.reshape(1, D), name="norm_back_one",
-    )
     layer_out = sum((v.astype(F32) for v in layer), after_attn + layer_parts[0].astype(F32))
     layer_out = layer_out.astype(BF16)
     gains = over_x(gains)

time: 466 us -> 462 us (level)
    ppermute x3 -> x2, waiting for transfers between devices: 13.2 us -> 0.01 us  [fetch_half(): lax.ppermute(lax.dynamic_slice_in_dim(w, core * half, half, 0), 'zh', shi...]
    unnamed x106 -> x94, local copies, waits for them, and re-layouts: 13 us -> 12.4 us
  transfers between devices with their start and end apart: 60 -> 60, of which waited for: 24 -> 25; matrix products, arithmetic and copies ran while one was open for 3% -> 3% of each run, Pallas kernels for 26% -> 26%
where the time goes in v12:
time: 462 us; the launch traced here: 453 us
  Pallas kernels  167 us (36%)
  waiting for transfers between devices  135 us (29%)
  starting transfers between devices  107 us (23%)
  local copies, waits for them, and re-layouts  21.1 us (5%)
  between operations  14.7 us (3%)
  other arithmetic  8.57 us (2%)
    ppermute x3, waiting for transfers between devices, sum_tail(): got = [lax.ppermute(g[s], 'y', shift(4, s)) for s in (2, 1, 3)]  28.7 us
    ppermute x4, starting transfers between devices, sum_tail(): theirs = [lax.ppermute(v, 'core', shift(2, 1)) for v in [g] + mine[1:]]  21.8 us
    pallas_call x1, Pallas kernels, ffn(): pl.pallas_call(ffn_body, grid=(TILES,), out_shape=(sds((ROWS, FF4)),) * 3...  20.8 us
    pallas_call x1, Pallas kernels, attend_back(): pl.pallas_call(attend_back_body, out_shape=(sds((4, BLK, AW)), sds((ROWS,...  20.6 us
    ppermute x3, waiting for transfers between devices, gather_x(): from_prev = lax.ppermute(v, 'x', shift(4, 1))  18.4 us
    pallas_call x1, Pallas kernels, ffn_back(): pl.pallas_call(ffn_back_body, grid_spec=pltpu.PrefetchScalarGridSpec(num_...  15.4 us
    pallas_call x1, Pallas kernels, gate_up_grads(): pl.pallas_call(gate_up_grads_body, grid=(16 // QS,), out_shape=sds((2, 16...  14.6 us
    pallas_call x4, Pallas kernels, small_call(): pl.pallas_call(body, out_shape=out_shape, in_specs=[spec(pltpu.SMEM)] + [...  13.2 us
  transfers between devices with their start and end apart: 60, of which 25 were waited for; matrix products, arithmetic and copies ran while one was open for 3% of the time, Pallas kernels for 26%

profile of v12, /device:TPU:1, one launch (start us, length us, event | category | flops | bytes accessed | tf_op | source)
XLA Modules:
  0.0 453.2 jit_solution(17683587408259803017)
XLA Ops:
  14.3 3.7 collective-permute-start.4
  22.1 5.2 %collective-permute-done.1.n3.refs_4_.refs_9_ = bf16[160,2048]{1,0:T(8,128)(2,1)S(1)} collective-permute-done((bf16[160,2048]{1,0:T(8,128)(2,1)S(1)}, bf16[160,2048]{1,0:T(8,128)(2,1)S(1)}, u32[]{:S(2)}, u32[]{:S(2)}) %collective-permute-start.1) | collective-permute-done | bytes 655392 | tf_op jit(solution)/shard_map/ppermute | solution.py:70
  31.6 3.8 collective-permute-start.5
  39.2 3.1 collective-permute-start.6
  43.8 2.7 collective-permute-start.9
  47.4 6.7 %qkv_forward.1 = (bf16[4,1280,128]{2,1,0:T(8,128)(2,1)}, bf16[640,128]{1,0:T(8,128)(2,1)}) custom-call(s32[4]{0:T(128)} %pad_add_fusion.idx, bf16[160,2048]{1,0:T(8,128)(2,1)} %copy-done.4, bf16[160,2048]{1,0:T(8,128)(2,1)} %copy-done.8, bf16[80,2048]{1,0:T(8,128)(2,1)} %collective-permute-done.2.n2a.refs_2_.refs_7_, ...), custom_call_target="tpu_custom_call" | custom-call | flops 1677721600 | bytes 7000000 | tf_op jit(solution)/shard_map/qkv_forward/pallas_call | solution.py:176
  54.1 3.7 collective-permute-start.7
  62.8 8.6 %attend.1 = (bf16[4,160,512]{2,1,0:T(8,128)(2,1)}, bf16[4,1280,128]{2,1,0:T(8,128)(2,1)}) custom-call(s32[4]{0:T(128)} %pad_add_fusion.idx, bf16[4,1280,128]{2,1,0:T(8,128)(2,1)} %get-tuple-element.104.q, bf16[640,128]{1,0:T(8,128)(2,1)} %get-tuple-element.105.kv_own, bf16[640,128]{1,0:T(8,128)(2,1)} %copy-done.46, s32[1,1280]{1,0:T(1,128)} %reshape_tile.3.first), custom_call_target="tpu_custom_call" | custom-call | flops 12000000000 | bytes 3000000 | tf_op jit(solution)/shard_map/attend/pallas_call | solution.py:269
  71.4 4.1 collective-permute-done.9.c2.refs_2_
  75.8 4.1 out_project.1
  82.5 3.8 collective-permute-start.15
  88.8 6.0 %collective-permute-done.12.got_b = bf16[80,2048]{1,0:T(8,128)(2,1)S(1)} collective-permute-done((bf16[80,2048]{1,0:T(8,128)(2,1)S(1)}, bf16[80,2048]{1,0:T(8,128)(2,1)S(1)}, u32[]{:S(2)}, u32[]{:S(2)}) %collective-permute-start.12) | collective-permute-done | bytes 327712 | tf_op jit(solution)/shard_map/ppermute | solution.py:87
  94.8 3.2 collective-permute-done.11.got_a
  100.9 2.7 collective-permute-start.14
  103.6 12.9 %collective-permute-done.13.b = bf16[160,2048]{1,0:T(8,128)(2,1)S(1)} collective-permute-done((bf16[160,2048]{1,0:T(8,128)(2,1)}, bf16[160,2048]{1,0:T(8,128)(2,1)S(1)}, u32[]{:S(2)}, u32[]{:S(2)}) %collective-permute-start.13) | collective-permute-done | bytes 655392 | tf_op jit(solution)/shard_map/ppermute | solution.py:108
  117.6 2.9 norm_two.1
  123.3 12.0 %collective-permute-done.17.n3.refs_4_.refs_9_ = bf16[160,2048]{1,0:T(8,128)(2,1)S(1)} collective-permute-done((bf16[160,2048]{1,0:T(8,128)(2,1)}, bf16[160,2048]{1,0:T(8,128)(2,1)S(1)}, u32[]{:S(2)}, u32[]{:S(2)}) %collective-permute-start.17) | collective-permute-done | bytes 655392 | tf_op jit(solution)/shard_map/ppermute | solution.py:70
  135.3 4.0 collective-permute-start.21
  142.4 6.7 %collective-permute-done.19.n2b.refs_3_.refs_8_ = bf16[80,2048]{1,0:T(8,128)(2,1)S(1)} collective-permute-done((bf16[80,2048]{1,0:T(8,128)(2,1)S(1)}, bf16[80,2048]{1,0:T(8,128)(2,1)S(1)}, u32[]{:S(2)}, u32[]{:S(2)}) %collective-permute-start.19) | collective-permute-done | bytes 327712 | tf_op jit(solution)/shard_map/ppermute | solution.py:75
  149.1 3.5 collective-permute-done.18.n2a.refs_2_.refs_7_
  153.9 20.8 %ffn.1 = (bf16[640,1408]{1,0:T(8,128)(2,1)}, bf16[640,1408]{1,0:T(8,128)(2,1)}, bf16[640,1408]{1,0:T(8,128)(2,1)}) custom-call(s32[4]{0:T(128)} %pad_add_fusion.idx, bf16[160,2048]{1,0:T(8,128)(2,1)} %get-tuple-element.120.n0.refs_0_.refs_5_, bf16[160,2048]{1,0:T(8,128)(2,1)} %copy-done.2, bf16[80,2048]{1,0:T(8,128)(2,1)} %copy-done.10, ...), custom_call_target="tpu_custom_call" | custom-call | flops 11072962560 | bytes 34000000 | tf_op jit(solution)/shard_map/ffn/pallas_call | solution.py:504
  174.7 15.4 %ffn_back.1 = (bf16[160,2048]{1,0:T(8,128)(2,1)}, bf16[160,2048]{1,0:T(8,128)(2,1)}, bf16[80,2048]{1,0:T(8,128)(2,1)}, bf16[80,2048]{1,0:T(8,128)(2,1)}, bf16[160,2048]{1,0:T(8,128)(2,1)}) custom-call(s32[4]{0:T(128)} %pad_add_fusion.idx, bf16[640,1408]{1,0:T(8,128)(2,1)} %get-tuple-element.186.dgate.refs_10_, ...), custom_call_target="tpu_custom_call" | custom-call | flops 7381975040 | bytes 18000000 | tf_op jit(solution)/shard_map/ffn_back/pallas_call | solution.py:570
  192.8 9.1 %down_grads.1.refs_12_ = bf16[2,16,2112,128]{3,2,1,0:T(8,128)(2,1)} custom-call(bf16[160,2048]{1,0:T(8,128)(2,1)} %refs_0_.1, bf16[160,2048]{1,0:T(8,128)(2,1)} %collective-permute-done.8.c1.refs_1_, bf16[160,2048]{1,0:T(8,128)(2,1)} %collective-permute-done.9.c2.refs_2_, bf16[160,2048]{1,0:T(8,128)(2,1)} %collective-permute-done.10.c3.refs_3_, ...), custom_call_target="tpu_custom_call" | custom-call | flops 3690987520 | bytes 10000000 | tf_op jit(solution)/shard_map/down_grads/pallas_call | solution.py:637
  205.0 2.7 collective-permute-start.25
  207.6 14.6 %gate_up_grads.1 = bf16[2,16,2112,128]{3,2,1,0:T(8,128)(2,1)} custom-call(bf16[160,2048]{1,0:T(8,128)(2,1)} %get-tuple-element.120.n0.refs_0_.refs_5_, bf16[160,2048]{1,0:T(8,128)(2,1)} %copy-done.2, bf16[80,2048]{1,0:T(8,128)(2,1)} %copy-done.10, bf16[80,2048]{1,0:T(8,128)(2,1)} %copy-done.9, ...), custom_call_target="tpu_custom_call", output_to_operand_aliasing={{}: (12, {})} | custom-call | flops 7381975040 | bytes 20000000 | tf_op jit(solution)/shard_map/gate_up_grads/pallas_call | solution.py:606
  223.4 4.0 norm_back_two.1
  228.9 12.7 %collective-permute-done.27.b1.refs_11_ = bf16[160,2048]{1,0:T(8,128)(2,1)S(1)} collective-permute-done((bf16[160,2048]{1,0:T(8,128)(2,1)}, bf16[160,2048]{1,0:T(8,128)(2,1)S(1)}, u32[]{:S(2)}, u32[]{:S(2)}) %collective-permute-start.27) | collective-permute-done | bytes 655392 | tf_op jit(solution)/shard_map/ppermute | solution.py:71
  245.6 10.5 %down_project.1 = (bf16[160,2048]{1,0:T(8,128)(2,1)}, bf16[160,2048]{1,0:T(8,128)(2,1)}, bf16[160,2048]{1,0:T(8,128)(2,1)}, bf16[160,2048]{1,0:T(8,128)(2,1)}) custom-call(s32[4]{0:T(128)} %pad_add_fusion.idx, bf16[640,1408]{1,0:T(8,128)(2,1)} %get-tuple-element.187.hid.refs_4_, bf16[704,2048]{1,0:T(8,128)(2,1)} %w0.9, ...), custom_call_target="tpu_custom_call" | custom-call | flops 3690987520 | bytes 11000000 | tf_op jit(solution)/shard_map/down_project/pallas_call | solution.py:540
  256.3 2.8 collective-permute-start.31
  259.1 20.6 %attend_back.1 = (bf16[4,160,512]{2,1,0:T(8,128)(2,1)}, f32[640,128]{1,0:T(8,128)}, bf16[640,128]{1,0:T(8,128)(2,1)}) custom-call(s32[4]{0:T(128)} %pad_add_fusion.idx, bf16[4,1280,128]{2,1,0:T(8,128)(2,1)} %get-tuple-element.148.qx, bf16[640,128]{1,0:T(8,128)(2,1)} %get-tuple-element.105.kv_own, bf16[640,128]{1,0:T(8,128)(2,1)} %copy-done.46, ...), custom_call_target="tpu_custom_call" | custom-call | flops 30000001024 | bytes 8000000 | tf_op jit(solution)/shard_map/attend_back/pallas_call | solution.py:377
  280.2 8.9 %attn_grads.1 = (bf16[4,2,1024,128]{3,2,1,0:T(8,128)(2,1)}, bf16[4,2,1024,128]{3,2,1,0:T(8,128)(2,1)}) custom-call(s32[4]{0:T(128)} %pad_add_fusion.idx, bf16[160,2048]{1,0:T(8,128)(2,1)} %copy-done.4, bf16[160,2048]{1,0:T(8,128)(2,1)} %copy-done.8, bf16[80,2048]{1,0:T(8,128)(2,1)} %collective-permute-done.2.n2a.refs_2_.refs_7_, ...), custom_call_target="tpu_custom_call" | custom-call | flops 2684354560 | bytes 10000000 | tf_op jit(solution)/shard_map/attn_grads/pallas_call | solution.py:716
  289.1 6.0 %collective-permute-start.33 = (bf16[4,2,1024,128]{3,2,1,0:T(8,128)(2,1)}, bf16[4,2,1024,128]{3,2,1,0:T(8,128)(2,1)S(1)}, u32[]{:S(2)}, u32[]{:S(2)}) collective-permute-start(bf16[4,2,1024,128]{3,2,1,0:T(8,128)(2,1)} %get-tuple-element.156), channel_id=1, source_target_pairs={{0,8},{8,0},{1,9},{9,1},{2,10},{10,2},{3,11},{11,3},{4,12},{12,4},... | collective-permute-start | bytes 6291464 | tf_op jit(solution)/shard_map/ppermute | solution.py:787
  295.1 7.2 %qkv_back.1 = (bf16[4,2,144,128]{3,2,1,0:T(8,128)(2,1)}, bf16[4,2,144,128]{3,2,1,0:T(8,128)(2,1)}, bf16[160,2048]{1,0:T(8,128)(2,1)}, bf16[160,2048]{1,0:T(8,128...) custom-call(s32[4]{0:T(128)} %pad_add_fusion.idx, ...), custom_call_target="tpu_custom_call" | custom-call | flops 1677721600 | bytes 13000000 | tf_op jit(solution)/shard_map/qkv_back/pallas_call | solution.py:434
  305.9 4.0 sum_core.1
  309.9 2.9 collective-permute-start.35
  315.4 15.9 %collective-permute-done.35.b = bf16[2,1168,128]{2,1,0:T(8,128)(2,1)S(1)} collective-permute-done((bf16[2,1168,128]{2,1,0:T(8,128)(2,1)}, bf16[2,1168,128]{2,1,0:T(8,128)(2,1)S(1)}, u32[]{:S(2)}, u32[]{:S(2)}) %collective-permute-start.35) | collective-permute-done | bytes 598048 | tf_op jit(solution)/shard_map/ppermute | solution.py:791
  331.4 12.8 %collective-permute-done.36.c = bf16[2,1168,128]{2,1,0:T(8,128)(2,1)S(1)} collective-permute-done((bf16[2,1168,128]{2,1,0:T(8,128)(2,1)}, bf16[2,1168,128]{2,1,0:T(8,128)(2,1)S(1)}, u32[]{:S(2)}, u32[]{:S(2)}) %collective-permute-start.36) | collective-permute-done | bytes 598048 | tf_op jit(solution)/shard_map/ppermute | solution.py:791
  345.2 2.7 sum_y.1
  347.9 11.1 %reduce-scatter.2.cloned.1.call-done = bf16[1,2112,128]{2,1,0:T(8,128)(2,1)} async-done(((bf16[32,2112,128]{2,1,0:T(8,128)(2,1)}), bf16[1,2112,128]{2,1,0:T(8,128)(2,1)}) %reduce-scatter.2.cloned.1.call-update) | async-done | bytes 540688 | tf_op jit(solution)/shard_map/reduce_scatter | solution.py:941
  365.1 2.9 collective-permute-done.39.got_a
  376.0 4.2 collective-permute-done.43.b
  385.3 9.0 %collective-permute-done.48.refs_3_ = bf16[1168,128]{1,0:T(8,128)(2,1)} collective-permute-done((bf16[1168,128]{1,0:T(8,128)(2,1)}, bf16[1168,128]{1,0:T(8,128)(2,1)}, u32[]{:S(2)}, u32[]{:S(2)}) %collective-permute-start.48) | collective-permute-done | bytes 299040 | tf_op jit(solution)/shard_map/ppermute | solution.py:808
  394.3 3.6 collective-permute-start.46
  398.8 14.2 %collective-permute-start.49 = (bf16[1168,128]{1,0:T(8,128)(2,1)}, bf16[1168,128]{1,0:T(8,128)(2,1)}, u32[]{:S(2)}, u32[]{:S(2)}) collective-permute-start(bf16[1168,128]{1,0:T(8,128)(2,1)} %sum_z.1.refs_0_), channel_id=1, source_target_pairs={{0,8},{8,0},{1,9},{9,1},{2,10},{10,2},{3,11},{11,3},{4,12},{12,4},... | collective-permute-start | bytes 897032 | tf_op jit(solution)/shard_map/ppermute | solution.py:809
  413.0 7.0 %collective-permute-start.52 = (bf16[1168,128]{1,0:T(8,128)(2,1)}, bf16[1168,128]{1,0:T(8,128)(2,1)}, u32[]{:S(2)}, u32[]{:S(2)}) collective-permute-start(bf16[1168,128]{1,0:T(8,128)(2,1)} %collective-permute-done.48.refs_3_), channel_id=1, source_target_pairs={{0,8},{8,0},{1,9},{9,1},{2,10},{10,2},{3,11},{11,3},{4,12},{12,4},... | collective-permute-start | bytes 897032 | tf_op jit(solution)/shard_map/ppermute | solution.py:809
  421.1 3.9 norm_back_one.1
  425.0 4.4 unpack_tail.1
  436.5 9.8 %unpack.1 = (f32[1024,1408]{1,0:T(8,128)}, f32[1024,1408]{1,0:T(8,128)}, f32[704,2048]{1,0:T(8,128)}) custom-call(bf16[16,2112,128]{2,1,0:T(8,128)(2,1)} %all-gather.8.cloned.1.call-done.piece), custom_call_target="tpu_custom_call" | custom-call | flops 1000000 | bytes 26000000 | tf_op jit(solution)/shard_map/unpack/pallas_call | solution.py:661
  (229 shorter events, 90.9 us)
Async XLA Ops:
  7.2 68.7 %all-gather.4.cloned.1.call-start = ((), (), s32[]{:S(2)}) async-start(), calls=%async_computation.1 | async-start | bytes 1179648 | tf_op jit(solution)/shard_map/all_gather | solution.py:898
  10.0 17.4 %collective-permute-start.1 = (bf16[160,2048]{1,0:T(8,128)(2,1)S(1)}, bf16[160,2048]{1,0:T(8,128)(2,1)S(1)}, u32[]{:S(2)}, u32[]{:S(2)}) collective-permute-start(bf16[160,2048]{1,0:T(8,128)(2,1)S(1)} %fusion.2.n0.refs_0_.refs_5_), channel_id=1, source_target_pairs={{0,2},{2,4},{4,6},{6,0},{1,3},{3,5},{5,7},{7,1},{8,10},{10,12},{12... | collective-permute-start | bytes 1966088 | tf_op jit(solution)/shard_map/ppermute | solution.py:70
  12.1 16.1 %collective-permute-start = (bf16[160,2048]{1,0:T(8,128)(2,1)S(1)}, bf16[160,2048]{1,0:T(8,128)(2,1)S(1)}, u32[]{:S(2)}, u32[]{:S(2)}) collective-permute-start(bf16[160,2048]{1,0:T(8,128)(2,1)S(1)} %fusion.2.n0.refs_0_.refs_5_), channel_id=1, source_target_pairs={{0,6},{2,0},{4,2},{6,4},{1,7},{3,1},{5,3},{7,5},{8,14},{10,8},{12,... | collective-permute-start | bytes 1966088 | tf_op jit(solution)/shard_map/ppermute | solution.py:71
  14.3 23.5 %collective-permute-start.4 = (bf16[512,640]{1,0:T(8,128)(2,1)}, bf16[512,640]{1,0:T(8,128)(2,1)S(1)}, u32[]{:S(2)}, u32[]{:S(2)}) collective-permute-start(bf16[512,640]{1,0:T(8,128)(2,1)} %constant_dynamic-slice_fusion.5), channel_id=1, source_target_pairs={{0,1},{1,0},{2,3},{3,2},{4,5},{5,4},{6,7},{7,6},{8,9},{9,8},{10,11... | collective-permute-start | bytes 1966088 | tf_op jit(solution)/shard_map/ppermute | solution.py:134
  29.0 8.8 %collective-permute-start.3 = (bf16[80,2048]{1,0:T(8,128)(2,1)}, bf16[80,2048]{1,0:T(8,128)(2,1)}, u32[]{:S(2)}, u32[]{:S(2)}) collective-permute-start(bf16[80,2048]{1,0:T(8,128)(2,1)} %slice.38), channel_id=1, source_target_pairs={{0,6},{2,0},{4,2},{6,4},{1,7},{3,1},{5,3},{7,5},{8,14},{10,8},{12,... | collective-permute-start | bytes 983048 | tf_op jit(solution)/shard_map/ppermute | solution.py:75
  43.7 109.0 %all-gather.6.cloned.1.call-start = ((), (), s32[]{:S(2)}) async-start(), calls=%async_computation.2 | async-start | bytes 6782976 | tf_op jit(solution)/shard_map/all_gather | solution.py:898
  43.8 27.7 %collective-permute-start.10 = (bf16[160,2048]{1,0:T(8,128)(2,1)S(1)}, bf16[160,2048]{1,0:T(8,128)(2,1)}, u32[]{:S(2)}, u32[]{:S(2)}) collective-permute-start(bf16[160,2048]{1,0:T(8,128)(2,1)S(1)} %copy-done.5), channel_id=1, source_target_pairs={{0,2},{2,4},{4,6},{6,0},{1,3},{3,5},{5,7},{7,1},{8,10},{10,12},{12... | collective-permute-start | bytes 1966088 | tf_op jit(solution)/shard_map/ppermute | solution.py:907
  43.8 31.7 %collective-permute-start.9 = (bf16[160,2048]{1,0:T(8,128)(2,1)S(1)}, bf16[160,2048]{1,0:T(8,128)(2,1)}, u32[]{:S(2)}, u32[]{:S(2)}) collective-permute-start(bf16[160,2048]{1,0:T(8,128)(2,1)S(1)} %copy-done.5), channel_id=1, source_target_pairs={{0,4},{2,6},{4,0},{6,2},{1,5},{3,7},{5,1},{7,3},{8,12},{10,14},{12... | collective-permute-start | bytes 1966088 | tf_op jit(solution)/shard_map/ppermute | solution.py:907
  46.5 29.3 %collective-permute-start.8 = (bf16[160,2048]{1,0:T(8,128)(2,1)S(1)}, bf16[160,2048]{1,0:T(8,128)(2,1)}, u32[]{:S(2)}, u32[]{:S(2)}) collective-permute-start(bf16[160,2048]{1,0:T(8,128)(2,1)S(1)} %copy-done.5), channel_id=1, source_target_pairs={{0,6},{2,0},{4,2},{6,4},{1,7},{3,1},{5,3},{7,5},{8,14},{10,8},{12,... | collective-permute-start | bytes 1966088 | tf_op jit(solution)/shard_map/ppermute | solution.py:907
  60.0 19.9 %collective-permute-start.20 = (bf16[128,2944]{1,0:T(8,128)(2,1)S(1)}, bf16[128,2944]{1,0:T(8,128)(2,1)S(1)}, u32[]{:S(2)}, u32[]{:S(2)}) collective-permute-start(bf16[128,2944]{1,0:T(8,128)(2,1)S(1)} %pad_maximum_fusion), channel_id=1, source_target_pairs={{0,17},{1,16},{16,1},{17,0},{2,19},{3,18},{18,3},{19,2},{4,21},{5,... | collective-permute-start | bytes 2261000 | tf_op jit(solution)/shard_map/ppermute | solution.py:912
  80.9 278.1 %reduce-scatter.2.cloned.1.call-start = ((), (), s32[]{:S(2)}) async-start(), calls=%async_computation.3 | async-start | bytes 17842176 | tf_op jit(solution)/shard_map/reduce_scatter | solution.py:941
  82.5 38.0 %collective-permute-start.15 = (bf16[352,2048]{1,0:T(8,128)(2,1)S(1)}, bf16[352,2048]{1,0:T(8,128)(2,1)}, u32[]{:S(2)}, u32[]{:S(2)}) collective-permute-start(bf16[352,2048]{1,0:T(8,128)(2,1)S(1)} %constant_dynamic-slice_fusion.2), channel_id=1, source_target_pairs={{0,1},{1,0},{2,3},{3,2},{4,5},{5,4},{6,7},{7,6},{8,9},{9,8},{10,11... | collective-permute-start | bytes 4325384 | tf_op jit(solution)/shard_map/ppermute | solution.py:134
  88.8 9.2 %collective-permute-start.11 = (bf16[80,2048]{1,0:T(8,128)(2,1)S(1)}, bf16[80,2048]{1,0:T(8,128)(2,1)S(1)}, u32[]{:S(2)}, u32[]{:S(2)}) collective-permute-start(bf16[80,2048]{1,0:T(8,128)(2,1)S(1)} %copy-done.44), channel_id=1, source_target_pairs={{0,2},{2,4},{4,6},{6,0},{1,3},{3,5},{5,7},{7,1},{8,10},{10,12},{12... | collective-permute-start | bytes 983048 | tf_op jit(solution)/shard_map/ppermute | solution.py:86
  100.9 15.6 %collective-permute-start.13 = (bf16[160,2048]{1,0:T(8,128)(2,1)}, bf16[160,2048]{1,0:T(8,128)(2,1)S(1)}, u32[]{:S(2)}, u32[]{:S(2)}) collective-permute-start(bf16[160,2048]{1,0:T(8,128)(2,1)} %get-tuple-element.115), channel_id=1, source_target_pairs={{0,2},{2,4},{4,6},{6,0},{1,3},{3,5},{5,7},{7,1},{8,10},{10,12},{12... | collective-permute-start | bytes 1966088 | tf_op jit(solution)/shard_map/ppermute | solution.py:108
  100.9 15.6 %collective-permute-start.14 = (bf16[160,2048]{1,0:T(8,128)(2,1)}, bf16[160,2048]{1,0:T(8,128)(2,1)S(1)}, u32[]{:S(2)}, u32[]{:S(2)}) collective-permute-start(bf16[160,2048]{1,0:T(8,128)(2,1)} %get-tuple-element.116), channel_id=1, source_target_pairs={{0,6},{2,0},{4,2},{6,4},{1,7},{3,1},{5,3},{7,5},{8,14},{10,8},{12,... | collective-permute-start | bytes 1966088 | tf_op jit(solution)/shard_map/ppermute | solution.py:108
  120.5 14.7 %collective-permute-start.17 = (bf16[160,2048]{1,0:T(8,128)(2,1)}, bf16[160,2048]{1,0:T(8,128)(2,1)S(1)}, u32[]{:S(2)}, u32[]{:S(2)}) collective-permute-start(bf16[160,2048]{1,0:T(8,128)(2,1)} %get-tuple-element.120.n0.refs_0_.refs_5_), channel_id=1, source_target_pairs={{0,2},{2,4},{4,6},{6,0},{1,3},{3,5},{5,7},{7,1},{8,10},{10,12},{12... | collective-permute-start | bytes 1966088 | tf_op jit(solution)/shard_map/ppermute | solution.py:70
  120.6 14.7 %collective-permute-start.16 = (bf16[160,2048]{1,0:T(8,128)(2,1)}, bf16[160,2048]{1,0:T(8,128)(2,1)S(1)}, u32[]{:S(2)}, u32[]{:S(2)}) collective-permute-start(bf16[160,2048]{1,0:T(8,128)(2,1)} %get-tuple-element.120.n0.refs_0_.refs_5_), channel_id=1, source_target_pairs={{0,6},{2,0},{4,2},{6,4},{1,7},{3,1},{5,3},{7,5},{8,14},{10,8},{12,... | collective-permute-start | bytes 1966088 | tf_op jit(solution)/shard_map/ppermute | solution.py:71
  135.3 17.4 %collective-permute-start.21 = (bf16[352,2048]{1,0:T(8,128)(2,1)}, bf16[352,2048]{1,0:T(8,128)(2,1)S(1)}, u32[]{:S(2)}, u32[]{:S(2)}) collective-permute-start(bf16[352,2048]{1,0:T(8,128)(2,1)} %collective-permute-done.15.w1), channel_id=1, source_target_pairs={{0,8},{8,0},{1,9},{9,1},{2,10},{10,2},{3,11},{11,3},{4,12},{12,4},... | collective-permute-start | bytes 4325384 | tf_op jit(solution)/shard_map/ppermute | solution.py:902
  139.3 9.8 %collective-permute-start.19 = (bf16[80,2048]{1,0:T(8,128)(2,1)S(1)}, bf16[80,2048]{1,0:T(8,128)(2,1)S(1)}, u32[]{:S(2)}, u32[]{:S(2)}) collective-permute-start(bf16[80,2048]{1,0:T(8,128)(2,1)S(1)} %slice.40), channel_id=1, source_target_pairs={{0,6},{2,0},{4,2},{6,4},{1,7},{3,1},{5,3},{7,5},{8,14},{10,8},{12,... | collective-permute-start | bytes 983048 | tf_op jit(solution)/shard_map/ppermute | solution.py:75
  142.0 10.7 %collective-permute-start.18 = (bf16[80,2048]{1,0:T(8,128)(2,1)S(1)}, bf16[80,2048]{1,0:T(8,128)(2,1)S(1)}, u32[]{:S(2)}, u32[]{:S(2)}) collective-permute-start(bf16[80,2048]{1,0:T(8,128)(2,1)S(1)} %slice.39), channel_id=1, source_target_pairs={{0,2},{2,4},{4,6},{6,0},{1,3},{3,5},{5,7},{7,1},{8,10},{10,12},{12... | collective-permute-start | bytes 983048 | tf_op jit(solution)/shard_map/ppermute | solution.py:74
  190.1 11.8 %collective-permute-start.22 = (bf16[80,2048]{1,0:T(8,128)(2,1)}, bf16[80,2048]{1,0:T(8,128)(2,1)S(1)}, u32[]{:S(2)}, u32[]{:S(2)}) collective-permute-start(bf16[80,2048]{1,0:T(8,128)(2,1)} %get-tuple-element.132), channel_id=1, source_target_pairs={{0,2},{2,4},{4,6},{6,0},{1,3},{3,5},{5,7},{7,1},{8,10},{10,12},{12... | collective-permute-start | bytes 983048 | tf_op jit(solution)/shard_map/ppermute | solution.py:86
  190.1 11.8 %collective-permute-start.23 = (bf16[80,2048]{1,0:T(8,128)(2,1)}, bf16[80,2048]{1,0:T(8,128)(2,1)S(1)}, u32[]{:S(2)}, u32[]{:S(2)}) collective-permute-start(bf16[80,2048]{1,0:T(8,128)(2,1)} %get-tuple-element.134), channel_id=1, source_target_pairs={{0,6},{2,0},{4,2},{6,4},{1,7},{3,1},{5,3},{7,5},{8,14},{10,8},{12,... | collective-permute-start | bytes 983048 | tf_op jit(solution)/shard_map/ppermute | solution.py:87
  205.0 17.3 %collective-permute-start.24 = (bf16[160,2048]{1,0:T(8,128)(2,1)}, bf16[160,2048]{1,0:T(8,128)(2,1)S(1)}, u32[]{:S(2)}, u32[]{:S(2)}) collective-permute-start(bf16[160,2048]{1,0:T(8,128)(2,1)} %get-tuple-element.135), channel_id=1, source_target_pairs={{0,2},{2,4},{4,6},{6,0},{1,3},{3,5},{5,7},{7,1},{8,10},{10,12},{12... | collective-permute-start | bytes 1966088 | tf_op jit(solution)/shard_map/ppermute | solution.py:108
  205.0 17.3 %collective-permute-start.25 = (bf16[160,2048]{1,0:T(8,128)(2,1)}, bf16[160,2048]{1,0:T(8,128)(2,1)S(1)}, u32[]{:S(2)}, u32[]{:S(2)}) collective-permute-start(bf16[160,2048]{1,0:T(8,128)(2,1)} %get-tuple-element.136), channel_id=1, source_target_pairs={{0,6},{2,0},{4,2},{6,4},{1,7},{3,1},{5,3},{7,5},{8,14},{10,8},{12,... | collective-permute-start | bytes 1966088 | tf_op jit(solution)/shard_map/ppermute | solution.py:108
  223.3 213.1 %all-gather.8.cloned.1.call-start = ((), (), s32[]{:S(2)}) async-start(), calls=%async_computation.4 | async-start | bytes 9191424 | tf_op jit(solution)/shard_map/all_gather | solution.py:978
  227.4 14.2 %collective-permute-start.27 = (bf16[160,2048]{1,0:T(8,128)(2,1)}, bf16[160,2048]{1,0:T(8,128)(2,1)S(1)}, u32[]{:S(2)}, u32[]{:S(2)}) collective-permute-start(bf16[160,2048]{1,0:T(8,128)(2,1)} %get-tuple-element.141.b0.refs_10_), channel_id=1, source_target_pairs={{0,6},{2,0},{4,2},{6,4},{1,7},{3,1},{5,3},{7,5},{8,14},{10,8},{12,... | collective-permute-start | bytes 1966088 | tf_op jit(solution)/shard_map/ppermute | solution.py:71
  228.3 14.5 %collective-permute-start.26 = (bf16[160,2048]{1,0:T(8,128)(2,1)}, bf16[160,2048]{1,0:T(8,128)(2,1)S(1)}, u32[]{:S(2)}, u32[]{:S(2)}) collective-permute-start(bf16[160,2048]{1,0:T(8,128)(2,1)} %get-tuple-element.141.b0.refs_10_), channel_id=1, source_target_pairs={{0,2},{2,4},{4,6},{6,0},{1,3},{3,5},{5,7},{7,1},{8,10},{10,12},{12... | collective-permute-start | bytes 1966088 | tf_op jit(solution)/shard_map/ppermute | solution.py:70
  242.9 13.3 %collective-permute-start.28 = (bf16[80,2048]{1,0:T(8,128)(2,1)S(1)}, bf16[80,2048]{1,0:T(8,128)(2,1)S(1)}, u32[]{:S(2)}, u32[]{:S(2)}) collective-permute-start(bf16[80,2048]{1,0:T(8,128)(2,1)S(1)} %slice.41), channel_id=1, source_target_pairs={{0,2},{2,4},{4,6},{6,0},{1,3},{3,5},{5,7},{7,1},{8,10},{10,12},{12... | collective-permute-start | bytes 983048 | tf_op jit(solution)/shard_map/ppermute | solution.py:74
  242.9 13.2 %collective-permute-start.29 = (bf16[80,2048]{1,0:T(8,128)(2,1)S(1)}, bf16[80,2048]{1,0:T(8,128)(2,1)}, u32[]{:S(2)}, u32[]{:S(2)}) collective-permute-start(bf16[80,2048]{1,0:T(8,128)(2,1)S(1)} %slice.42), channel_id=1, source_target_pairs={{0,6},{2,0},{4,2},{6,4},{1,7},{3,1},{5,3},{7,5},{8,14},{10,8},{12,... | collective-permute-start | bytes 983048 | tf_op jit(solution)/shard_map/ppermute | solution.py:75
  256.2 24.0 %collective-permute-start.30 = (bf16[160,2048]{1,0:T(8,128)(2,1)}, bf16[160,2048]{1,0:T(8,128)(2,1)S(1)}, u32[]{:S(2)}, u32[]{:S(2)}) collective-permute-start(bf16[160,2048]{1,0:T(8,128)(2,1)} %get-tuple-element.144), channel_id=1, source_target_pairs={{0,2},{2,4},{4,6},{6,0},{1,3},{3,5},{5,7},{7,1},{8,10},{10,12},{12... | collective-permute-start | bytes 1966088 | tf_op jit(solution)/shard_map/ppermute | solution.py:954
  256.3 23.9 %collective-permute-start.31 = (bf16[160,2048]{1,0:T(8,128)(2,1)}, bf16[160,2048]{1,0:T(8,128)(2,1)S(1)}, u32[]{:S(2)}, u32[]{:S(2)}) collective-permute-start(bf16[160,2048]{1,0:T(8,128)(2,1)} %get-tuple-element.146), channel_id=1, source_target_pairs={{0,6},{2,0},{4,2},{6,4},{1,7},{3,1},{5,3},{7,5},{8,14},{10,8},{12,... | collective-permute-start | bytes 1966088 | tf_op jit(solution)/shard_map/ppermute | solution.py:954
  279.7 9.4 %collective-permute-start.32 = (bf16[640,128]{1,0:T(8,128)(2,1)}, bf16[640,128]{1,0:T(8,128)(2,1)S(1)}, u32[]{:S(2)}, u32[]{:S(2)}) collective-permute-start(bf16[640,128]{1,0:T(8,128)(2,1)} %get-tuple-element.154), channel_id=1, source_target_pairs={{0,1},{1,0},{2,3},{3,2},{4,5},{5,4},{6,7},{7,6},{8,9},{9,8},{10,11... | collective-permute-start | bytes 491528 | tf_op jit(solution)/shard_map/ppermute | solution.py:959
  289.1 15.4 %collective-permute-start.33 = (bf16[4,2,1024,128]{3,2,1,0:T(8,128)(2,1)}, bf16[4,2,1024,128]{3,2,1,0:T(8,128)(2,1)S(1)}, u32[]{:S(2)}, u32[]{:S(2)}) collective-permute-start(bf16[4,2,1024,128]{3,2,1,0:T(8,128)(2,1)} %get-tuple-element.156), channel_id=1, source_target_pairs={{0,8},{8,0},{1,9},{9,1},{2,10},{10,2},{3,11},{11,3},{4,12},{12,4},... | collective-permute-start | bytes 6291464 | tf_op jit(solution)/shard_map/ppermute | solution.py:787
  309.9 21.5 %collective-permute-start.35 = (bf16[2,1168,128]{2,1,0:T(8,128)(2,1)}, bf16[2,1168,128]{2,1,0:T(8,128)(2,1)S(1)}, u32[]{:S(2)}, u32[]{:S(2)}) collective-permute-start(bf16[2,1168,128]{2,1,0:T(8,128)(2,1)} %get-tuple-element.162), channel_id=1, source_target_pairs={{0,64},{32,96},{64,0},{96,32},{1,65},{33,97},{65,1},{97,33},{2,66}... | collective-permute-start | bytes 1794056 | tf_op jit(solution)/shard_map/ppermute | solution.py:791
  312.8 31.4 %collective-permute-start.36 = (bf16[2,1168,128]{2,1,0:T(8,128)(2,1)}, bf16[2,1168,128]{2,1,0:T(8,128)(2,1)S(1)}, u32[]{:S(2)}, u32[]{:S(2)}) collective-permute-start(bf16[2,1168,128]{2,1,0:T(8,128)(2,1)} %get-tuple-element.163), channel_id=1, source_target_pairs={{0,32},{32,64},{64,96},{96,0},{1,33},{33,65},{65,97},{97,1},{2,34}... | collective-permute-start | bytes 1794056 | tf_op jit(solution)/shard_map/ppermute | solution.py:791
  313.2 31.0 %collective-permute-start.37 = (bf16[2,1168,128]{2,1,0:T(8,128)(2,1)}, bf16[2,1168,128]{2,1,0:T(8,128)(2,1)S(1)}, u32[]{:S(2)}, u32[]{:S(2)}) collective-permute-start(bf16[2,1168,128]{2,1,0:T(8,128)(2,1)} %get-tuple-element.164), channel_id=1, source_target_pairs={{0,96},{32,0},{64,32},{96,64},{1,97},{33,1},{65,33},{97,65},{2,98}... | collective-permute-start | bytes 1794056 | tf_op jit(solution)/shard_map/ppermute | solution.py:791
  359.1 8.9 %collective-permute-start.39 = (bf16[80,2048]{1,0:T(8,128)(2,1)}, bf16[80,2048]{1,0:T(8,128)(2,1)S(1)}, u32[]{:S(2)}, u32[]{:S(2)}) collective-permute-start(bf16[80,2048]{1,0:T(8,128)(2,1)} %get-tuple-element.172), channel_id=1, source_target_pairs={{0,2},{2,4},{4,6},{6,0},{1,3},{3,5},{5,7},{7,1},{8,10},{10,12},{12... | collective-permute-start | bytes 983048 | tf_op jit(solution)/shard_map/ppermute | solution.py:86
  361.8 14.2 %collective-permute-start.45 = (bf16[1168,128]{1,0:T(8,128)(2,1)}, bf16[1168,128]{1,0:T(8,128)(2,1)S(1)}, u32[]{:S(2)}, u32[]{:S(2)}) collective-permute-start(bf16[1168,128]{1,0:T(8,128)(2,1)} %get-tuple-element.181), channel_id=1, source_target_pairs={{0,17},{1,16},{16,1},{17,0},{2,19},{3,18},{18,3},{19,2},{4,21},{5,... | collective-permute-start | bytes 897032 | tf_op jit(solution)/shard_map/ppermute | solution.py:803
  364.1 11.9 %collective-permute-start.44 = (bf16[1168,128]{1,0:T(8,128)(2,1)}, bf16[1168,128]{1,0:T(8,128)(2,1)S(1)}, u32[]{:S(2)}, u32[]{:S(2)}) collective-permute-start(bf16[1168,128]{1,0:T(8,128)(2,1)} %get-tuple-element.181), channel_id=1, source_target_pairs={{0,1},{1,0},{2,3},{3,2},{4,5},{5,4},{6,7},{7,6},{8,9},{9,8},{10,11... | collective-permute-start | bytes 897032 | tf_op jit(solution)/shard_map/ppermute | solution.py:802
  364.6 15.6 %collective-permute-start.43 = (bf16[1168,128]{1,0:T(8,128)(2,1)}, bf16[1168,128]{1,0:T(8,128)(2,1)S(1)}, u32[]{:S(2)}, u32[]{:S(2)}) collective-permute-start(bf16[1168,128]{1,0:T(8,128)(2,1)} %get-tuple-element.180.a), channel_id=1, source_target_pairs={{0,16},{16,0},{1,17},{17,1},{2,18},{18,2},{3,19},{19,3},{4,20},{20... | collective-permute-start | bytes 897032 | tf_op jit(solution)/shard_map/ppermute | solution.py:801
  371.8 48.2 %collective-permute-start.41 = (bf16[160,2048]{1,0:T(8,128)(2,1)}, bf16[160,2048]{1,0:T(8,128)(2,1)S(1)}, u32[]{:S(2)}, u32[]{:S(2)}) collective-permute-start(bf16[160,2048]{1,0:T(8,128)(2,1)} %get-tuple-element.177), channel_id=1, source_target_pairs={{0,2},{2,4},{4,6},{6,0},{1,3},{3,5},{5,7},{7,1},{8,10},{10,12},{12... | collective-permute-start | bytes 1966088 | tf_op jit(solution)/shard_map/ppermute | solution.py:108
  371.8 48.3 %collective-permute-start.42 = (bf16[160,2048]{1,0:T(8,128)(2,1)}, bf16[160,2048]{1,0:T(8,128)(2,1)S(1)}, u32[]{:S(2)}, u32[]{:S(2)}) collective-permute-start(bf16[160,2048]{1,0:T(8,128)(2,1)} %get-tuple-element.178), channel_id=1, source_target_pairs={{0,6},{2,0},{4,2},{6,4},{1,7},{3,1},{5,3},{7,5},{8,14},{10,8},{12,... | collective-permute-start | bytes 1966088 | tf_op jit(solution)/shard_map/ppermute | solution.py:108
  383.0 11.2 %collective-permute-start.48 = (bf16[1168,128]{1,0:T(8,128)(2,1)}, bf16[1168,128]{1,0:T(8,128)(2,1)}, u32[]{:S(2)}, u32[]{:S(2)}) collective-permute-start(bf16[1168,128]{1,0:T(8,128)(2,1)} %sum_z.1.refs_0_), channel_id=1, source_target_pairs={{0,96},{32,0},{64,32},{96,64},{1,97},{33,1},{65,33},{97,65},{2,98}... | collective-permute-start | bytes 897032 | tf_op jit(solution)/shard_map/ppermute | solution.py:808
  384.5 48.1 %collective-permute-start.38 = (bf16[160,2048]{1,0:T(8,128)(2,1)}, bf16[160,2048]{1,0:T(8,128)(2,1)S(1)}, u32[]{:S(2)}, u32[]{:S(2)}) collective-permute-start(bf16[160,2048]{1,0:T(8,128)(2,1)} %get-tuple-element.166), channel_id=1, source_target_pairs={{0,4},{2,6},{4,0},{6,2},{1,5},{3,7},{5,1},{7,3},{8,12},{10,14},{12... | collective-permute-start | bytes 1966088 | tf_op jit(solution)/shard_map/ppermute | solution.py:977
  385.3 13.5 %collective-permute-start.47 = (bf16[1168,128]{1,0:T(8,128)(2,1)}, bf16[1168,128]{1,0:T(8,128)(2,1)}, u32[]{:S(2)}, u32[]{:S(2)}) collective-permute-start(bf16[1168,128]{1,0:T(8,128)(2,1)} %sum_z.1.refs_0_), channel_id=1, source_target_pairs={{0,64},{32,96},{64,0},{96,32},{1,65},{33,97},{65,1},{97,33},{2,66}... | collective-permute-start | bytes 897032 | tf_op jit(solution)/shard_map/ppermute | solution.py:808
  394.3 18.7 %collective-permute-start.46 = (bf16[1168,128]{1,0:T(8,128)(2,1)}, bf16[1168,128]{1,0:T(8,128)(2,1)}, u32[]{:S(2)}, u32[]{:S(2)}) collective-permute-start(bf16[1168,128]{1,0:T(8,128)(2,1)} %sum_z.1.refs_0_), channel_id=1, source_target_pairs={{0,32},{32,64},{64,96},{96,0},{1,33},{33,65},{65,97},{97,1},{2,34}... | collective-permute-start | bytes 897032 | tf_op jit(solution)/shard_map/ppermute | solution.py:808
  398.8 26.2 %collective-permute-start.49 = (bf16[1168,128]{1,0:T(8,128)(2,1)}, bf16[1168,128]{1,0:T(8,128)(2,1)}, u32[]{:S(2)}, u32[]{:S(2)}) collective-permute-start(bf16[1168,128]{1,0:T(8,128)(2,1)} %sum_z.1.refs_0_), channel_id=1, source_target_pairs={{0,8},{8,0},{1,9},{9,1},{2,10},{10,2},{3,11},{11,3},{4,12},{12,4},... | collective-permute-start | bytes 897032 | tf_op jit(solution)/shard_map/ppermute | solution.py:809
  413.0 12.0 %collective-permute-start.52 = (bf16[1168,128]{1,0:T(8,128)(2,1)}, bf16[1168,128]{1,0:T(8,128)(2,1)}, u32[]{:S(2)}, u32[]{:S(2)}) collective-permute-start(bf16[1168,128]{1,0:T(8,128)(2,1)} %collective-permute-done.48.refs_3_), channel_id=1, source_target_pairs={{0,8},{8,0},{1,9},{9,1},{2,10},{10,2},{3,11},{11,3},{4,12},{12,4},... | collective-permute-start | bytes 897032 | tf_op jit(solution)/shard_map/ppermute | solution.py:809
  (59 other events, 364.9 us)
Sparse Core Ops, SparseCore 0:
  43.8 24.0 all-gather.3
  81.0 42.5 all-gather.5
  222.4 136.5 reduce-scatter.1
  360.6 68.3 all-gather.7

commit v13 on v12

--- a/solution.py
+++ b/solution.py
@@ -132,6 +132,14 @@
 def fetch_half(w, core):
     half = w.shape[0] // 2
     return lax.ppermute(lax.dynamic_slice_in_dim(w, core * half, half, 0), "zh", shift(2, 1))
+
+
+OUT_ROWS = AW // 2 // 8
+DOWN_ROWS = 96
+
+
+def out_rows_spec():
+    return pl.BlockSpec((8, OUT_ROWS, D), lambda i: (0, 0, 0))
 
 
 def own_and_partner(idx, rows):
@@ -291,9 +299,10 @@
 
 def out_body(idx, att, w0, w1, o0, o1, o2a, o2b, o3):
     slots = own_and_partner(idx, AW // 2)
+    weights = w0[...], w1[...].reshape(AW // 2, D)
     for d, ref in ((2, None), (1, o1), (3, o3), (0, o0)):
         a = att.at[d]
-        res = sum(dot(a[:, s], w[...]) for s, w in zip(slots, (w0, w1))).astype(BF16)
+        res = sum(dot(a[:, s], w) for s, w in zip(slots, weights)).astype(BF16)
         if d == 2:
             o2a[...] = res[:HALF]
             o2b[...] = res[HALF:]
@@ -304,8 +313,9 @@
 def out_project(idx, att, weight):
     return pl.pallas_call(
         out_body,
+        grid=(1,),
         out_shape=part_shapes(D),
-        in_specs=[spec(pltpu.SMEM)] + [spec()] * 3,
+        in_specs=[spec(pltpu.SMEM), spec(), spec(), out_rows_spec()],
         out_specs=(spec(),) * 5,
         compiler_params=params(),
         cost_estimate=cost(2 * ROWS * D * AW, 5.5e6),
@@ -324,14 +334,15 @@
     x, zh = idx[0], idx[1]
     spread_keys(zh, kv_own, kv_par, kk, vv, lambda lane: jnp.where(lane < 3, -1.0, 0.0))
     slots = own_and_partner(idx, AW // 2)
+    weights = w0[...], w1[...].reshape(AW // 2, D)
     for d in range(4):
         if d == 2:
             rows = jnp.concatenate([b2a[...], b2b[...]], 0)
         else:
             rows = (b0, b1, None, b3)[d][...]
         at = rows_at((x + d) & 3)
-        for s, w in zip(slots, (w0, w1)):
-            dout[at, s] = dot_t(rows, w[...]).astype(BF16)
+        for s, w in zip(slots, weights):
+            dout[at, s] = dot_t(rows, w).astype(BF16)
     lo = low_lanes((BLK, 128))
     for j in range(4):
         rel = (j - x) & 3
@@ -376,8 +387,9 @@
 def attend_back(idx, qx, kv_own, kv_par, first, att, cosine, sine, branch, weight):
     return pl.pallas_call(
         attend_back_body,
+        grid=(1,),
         out_shape=(sds((4, BLK, AW)), sds((ROWS, 128), F32), sds((ROWS, 128))),
-        in_specs=[spec(pltpu.SMEM)] + [spec()] * 14,
+        in_specs=[spec(pltpu.SMEM)] + [spec()] * 13 + [out_rows_spec()],
         out_specs=(spec(),) * 3,
         scratch_shapes=[
             pltpu.VMEM((CAP, 128), BF16),
@@ -456,15 +468,22 @@
 GAP = TILES * TILE
 
 
-def load_down(idx, refs, dst, sem):
-    copies = []
-    for k, (s, ref) in enumerate(zip(weight_rows(idx, FF4 // 2), refs)):
-        copies.append(pltpu.make_async_copy(ref, dst.at[s], sem.at[k]))
+def load_down(idx, own, far, dst, sem):
+    half = FF4 // 2
+    zh = idx[1]
+    at = lambda first, n: pl.ds(pl.multiple_of(first, 32), n)
+    copies = [pltpu.make_async_copy(own, dst.at[at(zh * half, half)], sem.at[8])]
+    for k in range(8):
+        first = min(k * DOWN_ROWS, half - DOWN_ROWS)
+        skip = k * DOWN_ROWS - first
+        n = DOWN_ROWS - skip
+        source = far.at[k, OUT_ROWS + skip : OUT_ROWS + DOWN_ROWS]
+        copies.append(pltpu.make_async_copy(source, dst.at[at((1 - zh) * half + first + skip, n)], sem.at[k]))
     return copies
 
 
 def ffn_body(
-    idx, n0, n1, n2a, n2b, n3, c0, c1, c2, c3, gate_own, up_own, gate_par, up_par, w0, w1, w2,
+    idx, n0, n1, n2a, n2b, n3, c0, c1, c2, c3, gate_own, up_own, gate_par, up_par, w0, w1,
     hid, dgate, dup, n_all, c_all, down, sem,
 ):
     i = pl.program_id(0)
@@ -472,7 +491,7 @@
 
     @pl.when(i == 0)
     def _():
-        copies = load_down(idx, (w0, w1, w2), down, sem)
+        copies = load_down(idx, w0, w1, down, sem)
         for c in copies:
             c.start()
         for ref, row, (_, n) in zip((n0, n1, n2a, n2b, n3), PIECE_ROW, PIECES):
@@ -509,13 +528,13 @@
         + [whole(n, D) for _, n in PIECES]
         + [whole(BLK, D)] * 4
         + [column(0), column(0), column(0), column(TILES)]
-        + [spec(pl.ANY)] * 3,
+        + [spec(pl.ANY)] * 2,
         out_specs=[hidden] * 3,
         scratch_shapes=[
             pltpu.VMEM((ROWS, D), BF16),
             pltpu.VMEM((ROWS, D), BF16),
             pltpu.VMEM((GAP, D), BF16),
-            pltpu.SemaphoreType.DMA((3,)),
+            pltpu.SemaphoreType.DMA((9,)),
         ],
         compiler_params=params(),
         cost_estimate=cost(6 * ROWS * D * FF4, 3.4e7),
@@ -523,8 +542,8 @@
     )(idx, *normed, *cots, gate, up, gate_up, gate_up, *down)
 
 
-def down_body(idx, hid, w0, w1, w2, o0, o1, o2, o3, down, sem):
-    copies = load_down(idx, (w0, w1, w2), down, sem)
+def down_body(idx, hid, w0, w1, o0, o1, o2, o3, down, sem):
+    copies = load_down(idx, w0, w1, down, sem)
     for c in copies:
         c.start()
     for c in copies:
@@ -540,9 +559,9 @@
     return pl.pallas_call(
         down_body,
         out_shape=(sds((BLK, D)),) * 4,
-        in_specs=[spec(pltpu.SMEM), spec()] + [spec(pl.ANY)] * 3,
+        in_specs=[spec(pltpu.SMEM), spec()] + [spec(pl.ANY)] * 2,
         out_specs=(spec(),) * 4,
-        scratch_shapes=[pltpu.VMEM((FF4, D), BF16), pltpu.SemaphoreType.DMA((3,))],
+        scratch_shapes=[pltpu.VMEM((FF4, D), BF16), pltpu.SemaphoreType.DMA((9,))],
         compiler_params=params(),
         cost_estimate=cost(2 * ROWS * D * FF4, 1.1e7),
         name="down_project",
@@ -894,19 +913,23 @@
 
     qkv_got = fetch_half(qkv_weight, core)
     normed_one = gather_x((tok * s_one * gain_one).astype(BF16), (cosine,))
-    eighth = lambda w: lax.dynamic_slice_in_dim(w, (y * 2 + core) * (w.shape[0] // 8), w.shape[0] // 8, 0)
+    slot = y * 2 + core
+    eighth = lambda w: lax.dynamic_slice_in_dim(w, slot * (w.shape[0] // 8), w.shape[0] // 8, 0)
     spread = lambda v: lax.all_gather(v, ("y", "core"), axis=0, tiled=True)
-    fetch = lambda w: lax.ppermute(eighth(w), "zh", shift(2, 1))
-    out_got = fetch(out_weight)
-    out_all = out_weight, spread(tie(out_got, normed_one[1], normed_one[4]))
+    first_row = jnp.minimum(slot * DOWN_ROWS, FF4 // 2 - DOWN_ROWS)
+    some = jnp.concatenate(
+        [eighth(out_weight), lax.dynamic_slice_in_dim(down_weight, first_row, DOWN_ROWS, 0)], 0
+    )
+    some = lax.ppermute(some, "zh", shift(2, 1))
+    far_rows = spread(tie(some, qkv_got, normed_one[2], normed_one[3])).reshape(8, OUT_ROWS + DOWN_ROWS, D)
+    out_all, down_all = (out_weight, far_rows), (down_weight, far_rows)
     swap = lambda v, *deps: lax.ppermute(tie(v, *deps), "core", shift(2, 1))
-    qkv_all = qkv_weight, qkv_got, swap(qkv_got, out_got, normed_one[2], normed_one[3])
+    qkv_all = qkv_weight, qkv_got, swap(qkv_got, some, normed_one[2], normed_one[3])
 
     q, kv_own = qkv_forward(idx, normed_one, qkv_all, cosine, sine)
     cot = tie(cotangent, normed_one[2], normed_one[3])
     cots = [cotangent] + [lax.ppermute(cot, "x", shift(4, -k)) for k in (1, 2, 3)]
     kv_par = lax.ppermute(kv_own, "zh", shift(2, 1))
-    down_got = fetch_half(tie(down_weight, kv_par), core)
     rows = DH // 8
     cross = [(2 * a + b, 2 * (1 - a) + (1 - b)) for a in range(2) for b in range(2)]
     gate_up = lax.ppermute(
@@ -930,8 +953,7 @@
         (sds((BLK, D), F32), sds((BLK, D))),
         tokens, *last_step(p0, q1, q3), gain_two.reshape(1, D), name="norm_two",
     )
-    normed_two = gather_x(tie(normed_two, down_got))
-    down_all = down_weight, down_got, swap(down_got, normed_two[1], normed_two[4])
+    normed_two = gather_x(normed_two)
     hid, dgate, dup = ffn(idx, normed_two, cots, gate_weight, up_weight, gate_up, down_all)
     d_parts = ffn_back(idx, dgate, dup, gate_weight, up_weight, gate_up)
     own_grads = down_grads(cots, tie(hid, d_parts[2]))
@@ -965,7 +987,7 @@
         idx, dqm.reshape(ROWS, AW), dkv_own, dkv_got, cosine, sine, qkv_all, normed_one, gain_one,
         gain_grad_two,
     )
-    over_x = lambda v: sum((lax.ppermute(v, "x", shift(4, s)) for s in (1, 2, 3)), v)
+    over_x = lambda v: sum((tie(lax.ppermute(v, "x", shift(4, s)), grad_gate) for s in (1, 2, 3)), v)
     finish = lambda d_one: row_call(
         norm_back_body,
         (sds((BLK, D), F32), sds((BLK, D)), sds((1, D), F32)),

time: 462 us -> 451 us (0.976)
  starting transfers between devices: 107 us -> 93.1 us
    ppermute x3, waiting for transfers between devices: 12.8 us -> 0.01 us  [gather_x(): from_next = lax.ppermute(v, 'x', shift(4, -1))]
    ppermute x3, waiting for transfers between devices: 9.87 us -> 19.5 us  [sum_tail(): lax.ppermute(g, 'y', shift(4, s))]
    ppermute x4, starting transfers between devices: 21.8 us -> 12.3 us  [sum_tail(): theirs = [lax.ppermute(v, 'core', shift(2, 1)) for v in [g] + mine[1:]]]
    ppermute x3, waiting for transfers between devices: 18.4 us -> 27.1 us  [gather_x(): from_prev = lax.ppermute(v, 'x', shift(4, 1))]
    ppermute x1, waiting for transfers between devices: 2.36 us -> 9 us  [on_device(): some = lax.ppermute(some, 'zh', shift(2, 1))]
    ppermute x3, waiting for transfers between devices: 6.69 us -> 0.12 us  [gather_x(): opp_b = lax.ppermute(send_b, 'x', shift(4, -1))]
    ppermute x3, waiting for transfers between devices: 5.98 us -> 0.01 us  [relay(): got_b = lax.ppermute(p2b, 'x', shift(4, -1))]
    ppermute x2 -> x1, starting transfers between devices: 7.07 us -> 1.55 us  [on_device(): swap = lambda v, *deps: lax.ppermute(tie(v, *deps), 'core', shift(2, 1))]
  transfers between devices with their start and end apart: 60 -> 58, of which waited for: 25 -> 19; matrix products, arithmetic and copies ran while one was open for 3% -> 3% of each run, Pallas kernels for 26% -> 29%
where the time goes in v13:
time: 451 us; the launch traced here: 443 us
  Pallas kernels  168 us (37%)
  waiting for transfers between devices  136 us (30%)
  starting transfers between devices  93.1 us (21%)
  local copies, waits for them, and re-layouts  22.1 us (5%)
  between operations  14.7 us (3%)
  other arithmetic  9.49 us (2%)
    ppermute x3, waiting for transfers between devices, sum_tail(): got = [lax.ppermute(g[s], 'y', shift(4, s)) for s in (2, 1, 3)]  28 us
    ppermute x3, waiting for transfers between devices, gather_x(): from_prev = lax.ppermute(v, 'x', shift(4, 1))  27.1 us
    pallas_call x1, Pallas kernels, ffn(): pl.pallas_call(ffn_body, grid=(TILES,), out_shape=(sds((ROWS, FF4)),) * 3...  20.8 us
    pallas_call x1, Pallas kernels, attend_back(): pl.pallas_call(attend_back_body, grid=(1,), out_shape=(sds((4, BLK, AW)),...  20.6 us
    ppermute x3, waiting for transfers between devices, sum_tail(): lax.ppermute(g, 'y', shift(4, s))  19.5 us
    pallas_call x1, Pallas kernels, ffn_back(): pl.pallas_call(ffn_back_body, grid_spec=pltpu.PrefetchScalarGridSpec(num_...  15.5 us
    pallas_call x1, Pallas kernels, gate_up_grads(): pl.pallas_call(gate_up_grads_body, grid=(16 // QS,), out_shape=sds((2, 16...  14.6 us
    unnamed x90, local copies, waits for them, and re-layouts  13.7 us
  transfers between devices with their start and end apart: 58, of which 19 were waited for; matrix products, arithmetic and copies ran while one was open for 3% of the time, Pallas kernels for 29%

profile of v13, /device:TPU:1, one launch (start us, length us, event | category | flops | bytes accessed | tf_op | source)
XLA Modules:
  0.0 443.4 jit_solution(15690247787687747400)
XLA Ops:
  10.0 3.4 collective-permute-start
  14.3 3.6 collective-permute-start.4
  24.8 5.1 %collective-permute-done.1.n3.refs_4_.refs_9_ = bf16[160,2048]{1,0:T(8,128)(2,1)} collective-permute-done((bf16[160,2048]{1,0:T(8,128)(2,1)S(1)}, bf16[160,2048]{1,0:T(8,128)(2,1)}, u32[]{:S(2)}, u32[]{:S(2)}) %collective-permute-start.1) | collective-permute-done | bytes 655392 | tf_op jit(solution)/shard_map/ppermute | solution.py:70
  31.7 2.7 collective-permute-start.3
  34.4 9.0 %collective-permute-done.5 = bf16[128,2048]{1,0:T(8,128)(2,1)S(1)} collective-permute-done((bf16[128,2048]{1,0:T(8,128)(2,1)}, bf16[128,2048]{1,0:T(8,128)(2,1)S(1)}, u32[]{:S(2)}, u32[]{:S(2)}) %collective-permute-start.5) | collective-permute-done | bytes 524320 | tf_op jit(solution)/shard_map/ppermute | solution.py:923
  51.5 6.8 %qkv_forward.1 = (bf16[4,1280,128]{2,1,0:T(8,128)(2,1)}, bf16[640,128]{1,0:T(8,128)(2,1)}) custom-call(s32[4]{0:T(128)} %pad_add_fusion.idx, bf16[160,2048]{1,0:T(8,128)(2,1)} %copy-done.4, bf16[160,2048]{1,0:T(8,128)(2,1)} %copy-done.7, bf16[80,2048]{1,0:T(8,128)(2,1)} %copy-done.24, bf16[80,2048]{1,0:T(8,128)(2,1)} %copy-done.25, ...), custom_call_target="tpu_custom_call" | custom-call | flops 1677721600 | bytes 7000000 | tf_op jit(solution)/shard_map/qkv_forward/pallas_call | solution.py:184
  58.2 3.0 collective-permute-start.7
  65.9 8.6 %attend.1 = (bf16[4,160,512]{2,1,0:T(8,128)(2,1)}, bf16[4,1280,128]{2,1,0:T(8,128)(2,1)}) custom-call(s32[4]{0:T(128)} %pad_add_fusion.idx, bf16[4,1280,128]{2,1,0:T(8,128)(2,1)} %get-tuple-element.104.q, bf16[640,128]{1,0:T(8,128)(2,1)} %get-tuple-element.105.kv_own, bf16[640,128]{1,0:T(8,128)(2,1)} %copy-done.44, s32[1,1280]{1,0:T(1,128)} %reshape_tile.3.first), custom_call_target="tpu_custom_call" | custom-call | flops 12000000000 | bytes 3000000 | tf_op jit(solution)/shard_map/attend/pallas_call | solution.py:277
  74.6 3.5 collective-permute-done.8.c1.refs_1_
  78.1 3.7 collective-permute-done.10.c3.refs_3_
  81.8 4.2 out_project.1
  89.6 7.2 %collective-permute-done.11.got_a = bf16[80,2048]{1,0:T(8,128)(2,1)S(1)} collective-permute-done((bf16[80,2048]{1,0:T(8,128)(2,1)}, bf16[80,2048]{1,0:T(8,128)(2,1)S(1)}, u32[]{:S(2)}, u32[]{:S(2)}) %collective-permute-start.11) | collective-permute-done | bytes 327712 | tf_op jit(solution)/shard_map/ppermute | solution.py:86
  100.0 2.7 collective-permute-start.14
  102.7 13.6 %collective-permute-done.13.b = bf16[160,2048]{1,0:T(8,128)(2,1)S(1)} collective-permute-done((bf16[160,2048]{1,0:T(8,128)(2,1)}, bf16[160,2048]{1,0:T(8,128)(2,1)S(1)}, u32[]{:S(2)}, u32[]{:S(2)}) %collective-permute-start.13) | collective-permute-done | bytes 655392 | tf_op jit(solution)/shard_map/ppermute | solution.py:108
  117.3 2.9 norm_two.1
  122.9 12.6 %collective-permute-done.16.n3.refs_4_.refs_9_ = bf16[160,2048]{1,0:T(8,128)(2,1)S(1)} collective-permute-done((bf16[160,2048]{1,0:T(8,128)(2,1)}, bf16[160,2048]{1,0:T(8,128)(2,1)S(1)}, u32[]{:S(2)}, u32[]{:S(2)}) %collective-permute-start.16) | collective-permute-done | bytes 655392 | tf_op jit(solution)/shard_map/ppermute | solution.py:70
  135.7 3.2 collective-permute-start.18
  138.9 3.9 collective-permute-done.17.n2a.refs_2_.refs_7_
  143.6 20.8 %ffn.1 = (bf16[640,1408]{1,0:T(8,128)(2,1)}, bf16[640,1408]{1,0:T(8,128)(2,1)}, bf16[640,1408]{1,0:T(8,128)(2,1)}) custom-call(s32[4]{0:T(128)} %pad_add_fusion.idx, bf16[160,2048]{1,0:T(8,128)(2,1)} %get-tuple-element.118.n0.refs_0_.refs_5_, bf16[160,2048]{1,0:T(8,128)(2,1)} %copy-done.2, bf16[80,2048]{1,0:T(8,128)(2,1)} %copy-done.8, ...), custom_call_target="tpu_custom_call" | custom-call | flops 11072962560 | bytes 34000000 | tf_op jit(solution)/shard_map/ffn/pallas_call | solution.py:523
  164.5 15.5 %ffn_back.1 = (bf16[160,2048]{1,0:T(8,128)(2,1)}, bf16[160,2048]{1,0:T(8,128)(2,1)}, bf16[80,2048]{1,0:T(8,128)(2,1)}, bf16[80,2048]{1,0:T(8,128)(2,1)}, bf16[160,2048]{1,0:T(8,128)(2,1)}) custom-call(s32[4]{0:T(128)} %pad_add_fusion.idx, bf16[640,1408]{1,0:T(8,128)(2,1)} %get-tuple-element.181.dgate.refs_10_, ...), custom_call_target="tpu_custom_call" | custom-call | flops 7381975040 | bytes 18000000 | tf_op jit(solution)/shard_map/ffn_back/pallas_call | solution.py:589
  183.1 9.1 %down_grads.1.refs_12_ = bf16[2,16,2112,128]{3,2,1,0:T(8,128)(2,1)} custom-call(bf16[160,2048]{1,0:T(8,128)(2,1)} %refs_0_.1, bf16[160,2048]{1,0:T(8,128)(2,1)} %collective-permute-done.8.c1.refs_1_, bf16[160,2048]{1,0:T(8,128)(2,1)} %collective-permute-done.9.c2.refs_2_, bf16[160,2048]{1,0:T(8,128)(2,1)} %collective-permute-done.10.c3.refs_3_, ...), custom_call_target="tpu_custom_call" | custom-call | flops 3690987520 | bytes 10000000 | tf_op jit(solution)/shard_map/down_grads/pallas_call | solution.py:656
  195.3 2.7 collective-permute-start.23
  198.0 14.6 %gate_up_grads.1 = bf16[2,16,2112,128]{3,2,1,0:T(8,128)(2,1)} custom-call(bf16[160,2048]{1,0:T(8,128)(2,1)} %get-tuple-element.118.n0.refs_0_.refs_5_, bf16[160,2048]{1,0:T(8,128)(2,1)} %copy-done.2, bf16[80,2048]{1,0:T(8,128)(2,1)} %copy-done.8, bf16[80,2048]{1,0:T(8,128)(2,1)} %copy-done.9, ...), custom_call_target="tpu_custom_call", output_to_operand_aliasing={{}: (12, {})} | custom-call | flops 7381975040 | bytes 20000000 | tf_op jit(solution)/shard_map/gate_up_grads/pallas_call | solution.py:625
  213.7 4.0 norm_back_two.1
  220.5 9.4 %collective-permute-done.24.b3.refs_14_ = bf16[160,2048]{1,0:T(8,128)(2,1)S(1)} collective-permute-done((bf16[160,2048]{1,0:T(8,128)(2,1)}, bf16[160,2048]{1,0:T(8,128)(2,1)S(1)}, u32[]{:S(2)}, u32[]{:S(2)}) %collective-permute-start.24) | collective-permute-done | bytes 655392 | tf_op jit(solution)/shard_map/ppermute | solution.py:70
  230.0 2.7 collective-permute-start.27
  232.8 10.6 %down_project.1 = (bf16[160,2048]{1,0:T(8,128)(2,1)}, bf16[160,2048]{1,0:T(8,128)(2,1)}, bf16[160,2048]{1,0:T(8,128)(2,1)}, bf16[160,2048]{1,0:T(8,128)(2,1)}) custom-call(s32[4]{0:T(128)} %pad_add_fusion.idx, bf16[640,1408]{1,0:T(8,128)(2,1)} %get-tuple-element.182.hid.refs_4_, bf16[704,2048]{1,0:T(8,128)(2,1)} %w0.9, bf16[8,128,2048]{2,1,0:T(8,128)(2,1)} %bitcast.17), custom_call_target="tpu_custom_call" | custom-call | flops 3690987520 | bytes 11000000 | tf_op jit(solution)/shard_map/down_project/pallas_call | solution.py:559
  243.5 2.8 collective-permute-start.29
  246.3 20.6 %attend_back.1 = (bf16[4,160,512]{2,1,0:T(8,128)(2,1)}, f32[640,128]{1,0:T(8,128)}, bf16[640,128]{1,0:T(8,128)(2,1)}) custom-call(s32[4]{0:T(128)} %pad_add_fusion.idx, bf16[4,1280,128]{2,1,0:T(8,128)(2,1)} %get-tuple-element.145.qx, bf16[640,128]{1,0:T(8,128)(2,1)} %get-tuple-element.105.kv_own, bf16[640,128]{1,0:T(8,128)(2,1)} %copy-done.44, ...), custom_call_target="tpu_custom_call" | custom-call | flops 30000001024 | bytes 8000000 | tf_op jit(solution)/shard_map/attend_back/pallas_call | solution.py:388
  266.9 3.1 collective-permute-start.30
  270.0 9.6 %attn_grads.1 = (bf16[4,2,1024,128]{3,2,1,0:T(8,128)(2,1)}, bf16[4,2,1024,128]{3,2,1,0:T(8,128)(2,1)}) custom-call(s32[4]{0:T(128)} %pad_add_fusion.idx, bf16[160,2048]{1,0:T(8,128)(2,1)} %copy-done.4, bf16[160,2048]{1,0:T(8,128)(2,1)} %copy-done.7, bf16[80,2048]{1,0:T(8,128)(2,1)} %copy-done.24, bf16[80,2048]{1,0:T(8,128)(2,1)} %copy-done.25, ...), custom_call_target="tpu_custom_call" | custom-call | flops 2684354560 | bytes 10000000 | tf_op jit(solution)/shard_map/attn_grads/pallas_call | solution.py:735
  279.7 9.3 %collective-permute-start.31 = (bf16[4,2,1024,128]{3,2,1,0:T(8,128)(2,1)}, bf16[4,2,1024,128]{3,2,1,0:T(8,128)(2,1)S(1)}, u32[]{:S(2)}, u32[]{:S(2)}) collective-permute-start(bf16[4,2,1024,128]{3,2,1,0:T(8,128)(2,1)} %get-tuple-element.153), channel_id=1, source_target_pairs={{0,8},{8,0},{1,9},{9,1},{2,10},{10,2},{3,11},{11,3},{4,12},{12,4},... | collective-permute-start | bytes 6291464 | tf_op jit(solution)/shard_map/ppermute | solution.py:806
  288.9 7.5 %qkv_back.1 = (bf16[4,2,144,128]{3,2,1,0:T(8,128)(2,1)}, bf16[4,2,144,128]{3,2,1,0:T(8,128)(2,1)}, bf16[160,2048]{1,0:T(8,128)(2,1)}, bf16[160,2048]{1,0:T(8,128...) custom-call(s32[4]{0:T(128)} %pad_add_fusion.idx, ...), custom_call_target="tpu_custom_call" | custom-call | flops 1677721600 | bytes 13000000 | tf_op jit(solution)/shard_map/qkv_back/pallas_call | solution.py:446
  299.7 4.0 sum_core.1
  303.7 2.9 collective-permute-start.33
  309.3 15.2 %collective-permute-done.33.b = bf16[2,1168,128]{2,1,0:T(8,128)(2,1)S(1)} collective-permute-done((bf16[2,1168,128]{2,1,0:T(8,128)(2,1)}, bf16[2,1168,128]{2,1,0:T(8,128)(2,1)S(1)}, u32[]{:S(2)}, u32[]{:S(2)}) %collective-permute-start.33) | collective-permute-done | bytes 598048 | tf_op jit(solution)/shard_map/ppermute | solution.py:810
  324.5 12.8 %collective-permute-done.34.c = bf16[2,1168,128]{2,1,0:T(8,128)(2,1)S(1)} collective-permute-done((bf16[2,1168,128]{2,1,0:T(8,128)(2,1)}, bf16[2,1168,128]{2,1,0:T(8,128)(2,1)S(1)}, u32[]{:S(2)}, u32[]{:S(2)}) %collective-permute-start.34) | collective-permute-done | bytes 598048 | tf_op jit(solution)/shard_map/ppermute | solution.py:810
  340.9 10.8 %reduce-scatter.2.cloned.1.call-done = bf16[1,2112,128]{2,1,0:T(8,128)(2,1)} async-done(((bf16[32,2112,128]{2,1,0:T(8,128)(2,1)}), bf16[1,2112,128]{2,1,0:T(8,128)(2,1)}) %reduce-scatter.2.cloned.1.call-update) | async-done | bytes 540688 | tf_op jit(solution)/shard_map/reduce_scatter | solution.py:963
  364.6 2.7 collective-permute-start.40
  367.3 4.0 collective-permute-done.42.c
  378.5 7.0 %collective-permute-done.44.refs_1_ = bf16[1168,128]{1,0:T(8,128)(2,1)} collective-permute-done((bf16[1168,128]{1,0:T(8,128)(2,1)}, bf16[1168,128]{1,0:T(8,128)(2,1)}, u32[]{:S(2)}, u32[]{:S(2)}) %collective-permute-start.44) | collective-permute-done | bytes 299040 | tf_op jit(solution)/shard_map/ppermute | solution.py:827
  385.5 3.4 collective-permute-start.46
  388.9 12.5 %collective-permute-done.45.refs_2_ = bf16[1168,128]{1,0:T(8,128)(2,1)} collective-permute-done((bf16[1168,128]{1,0:T(8,128)(2,1)}, bf16[1168,128]{1,0:T(8,128)(2,1)}, u32[]{:S(2)}, u32[]{:S(2)}) %collective-permute-start.45) | collective-permute-done | bytes 299040 | tf_op jit(solution)/shard_map/ppermute | solution.py:827
  401.5 8.1 %collective-permute-start.47 = (bf16[1168,128]{1,0:T(8,128)(2,1)}, bf16[1168,128]{1,0:T(8,128)(2,1)}, u32[]{:S(2)}, u32[]{:S(2)}) collective-permute-start(bf16[1168,128]{1,0:T(8,128)(2,1)} %sum_z.1.refs_0_), channel_id=1, source_target_pairs={{0,8},{8,0},{1,9},{9,1},{2,10},{10,2},{3,11},{11,3},{4,12},{12,4},... | collective-permute-start | bytes 897032 | tf_op jit(solution)/shard_map/ppermute | solution.py:828
  409.5 3.8 collective-permute-start.48
  414.3 3.9 norm_back_one.1
  418.3 4.3 unpack_tail.1
  426.0 9.8 %unpack.1 = (f32[1024,1408]{1,0:T(8,128)}, f32[1024,1408]{1,0:T(8,128)}, f32[704,2048]{1,0:T(8,128)}) custom-call(bf16[16,2112,128]{2,1,0:T(8,128)(2,1)} %all-gather.8.cloned.1.call-done.piece), custom_call_target="tpu_custom_call" | custom-call | flops 1000000 | bytes 26000000 | tf_op jit(solution)/shard_map/unpack/pallas_call | solution.py:680
  (222 shorter events, 81.6 us)
Async XLA Ops:
  7.2 74.6 %all-gather.4.cloned.1.call-start = ((), (), s32[]{:S(2)}) async-start(), calls=%async_computation.1 | async-start | bytes 4718592 | tf_op jit(solution)/shard_map/all_gather | solution.py:918
  10.0 21.7 %collective-permute-start = (bf16[160,2048]{1,0:T(8,128)(2,1)S(1)}, bf16[160,2048]{1,0:T(8,128)(2,1)S(1)}, u32[]{:S(2)}, u32[]{:S(2)}) collective-permute-start(bf16[160,2048]{1,0:T(8,128)(2,1)S(1)} %fusion.2.n0.refs_0_.refs_5_), channel_id=1, source_target_pairs={{0,6},{2,0},{4,2},{6,4},{1,7},{3,1},{5,3},{7,5},{8,14},{10,8},{12,... | collective-permute-start | bytes 1966088 | tf_op jit(solution)/shard_map/ppermute | solution.py:71
  13.3 16.6 %collective-permute-start.1 = (bf16[160,2048]{1,0:T(8,128)(2,1)S(1)}, bf16[160,2048]{1,0:T(8,128)(2,1)}, u32[]{:S(2)}, u32[]{:S(2)}) collective-permute-start(bf16[160,2048]{1,0:T(8,128)(2,1)S(1)} %fusion.2.n0.refs_0_.refs_5_), channel_id=1, source_target_pairs={{0,2},{2,4},{4,6},{6,0},{1,3},{3,5},{5,7},{7,1},{8,10},{10,12},{12... | collective-permute-start | bytes 1966088 | tf_op jit(solution)/shard_map/ppermute | solution.py:70
  14.3 29.2 %collective-permute-start.4 = (bf16[512,640]{1,0:T(8,128)(2,1)}, bf16[512,640]{1,0:T(8,128)(2,1)S(1)}, u32[]{:S(2)}, u32[]{:S(2)}) collective-permute-start(bf16[512,640]{1,0:T(8,128)(2,1)} %constant_dynamic-slice_fusion.5), channel_id=1, source_target_pairs={{0,1},{1,0},{2,3},{3,2},{4,5},{5,4},{6,7},{7,6},{8,9},{9,8},{10,11... | collective-permute-start | bytes 1966088 | tf_op jit(solution)/shard_map/ppermute | solution.py:134
  20.7 22.7 %collective-permute-start.5 = (bf16[128,2048]{1,0:T(8,128)(2,1)}, bf16[128,2048]{1,0:T(8,128)(2,1)S(1)}, u32[]{:S(2)}, u32[]{:S(2)}) collective-permute-start(bf16[128,2048]{1,0:T(8,128)(2,1)} %pad_maximum_fusion.1), channel_id=1, source_target_pairs={{0,1},{1,0},{2,3},{3,2},{4,5},{5,4},{6,7},{7,6},{8,9},{9,8},{10,11... | collective-permute-start | bytes 1572872 | tf_op jit(solution)/shard_map/ppermute | solution.py:923
  31.7 11.8 %collective-permute-start.2 = (bf16[80,2048]{1,0:T(8,128)(2,1)}, bf16[80,2048]{1,0:T(8,128)(2,1)S(1)}, u32[]{:S(2)}, u32[]{:S(2)}) collective-permute-start(bf16[80,2048]{1,0:T(8,128)(2,1)} %slice.37), channel_id=1, source_target_pairs={{0,2},{2,4},{4,6},{6,0},{1,3},{3,5},{5,7},{7,1},{8,10},{10,12},{12... | collective-permute-start | bytes 983048 | tf_op jit(solution)/shard_map/ppermute | solution.py:74
  31.7 11.8 %collective-permute-start.3 = (bf16[80,2048]{1,0:T(8,128)(2,1)S(1)}, bf16[80,2048]{1,0:T(8,128)(2,1)S(1)}, u32[]{:S(2)}, u32[]{:S(2)}) collective-permute-start(bf16[80,2048]{1,0:T(8,128)(2,1)S(1)} %slice.38), channel_id=1, source_target_pairs={{0,6},{2,0},{4,2},{6,4},{1,7},{3,1},{5,3},{7,5},{8,14},{10,8},{12,... | collective-permute-start | bytes 983048 | tf_op jit(solution)/shard_map/ppermute | solution.py:75
  44.4 98.5 %all-gather.6.cloned.1.call-start = ((), (), s32[]{:S(2)}) async-start(), calls=%async_computation.2 | async-start | bytes 6782976 | tf_op jit(solution)/shard_map/all_gather | solution.py:918
  47.3 30.7 %collective-permute-start.8 = (bf16[160,2048]{1,0:T(8,128)(2,1)S(1)}, bf16[160,2048]{1,0:T(8,128)(2,1)}, u32[]{:S(2)}, u32[]{:S(2)}) collective-permute-start(bf16[160,2048]{1,0:T(8,128)(2,1)S(1)} %copy-done.5), channel_id=1, source_target_pairs={{0,6},{2,0},{4,2},{6,4},{1,7},{3,1},{5,3},{7,5},{8,14},{10,8},{12,... | collective-permute-start | bytes 1966088 | tf_op jit(solution)/shard_map/ppermute | solution.py:931
  50.0 28.1 %collective-permute-start.9 = (bf16[160,2048]{1,0:T(8,128)(2,1)S(1)}, bf16[160,2048]{1,0:T(8,128)(2,1)}, u32[]{:S(2)}, u32[]{:S(2)}) collective-permute-start(bf16[160,2048]{1,0:T(8,128)(2,1)S(1)} %copy-done.5), channel_id=1, source_target_pairs={{0,4},{2,6},{4,0},{6,2},{1,5},{3,7},{5,1},{7,3},{8,12},{10,14},{12... | collective-permute-start | bytes 1966088 | tf_op jit(solution)/shard_map/ppermute | solution.py:931
  50.0 31.8 %collective-permute-start.10 = (bf16[160,2048]{1,0:T(8,128)(2,1)S(1)}, bf16[160,2048]{1,0:T(8,128)(2,1)}, u32[]{:S(2)}, u32[]{:S(2)}) collective-permute-start(bf16[160,2048]{1,0:T(8,128)(2,1)S(1)} %copy-done.5), channel_id=1, source_target_pairs={{0,2},{2,4},{4,6},{6,0},{1,3},{3,5},{5,7},{7,1},{8,10},{10,12},{12... | collective-permute-start | bytes 1966088 | tf_op jit(solution)/shard_map/ppermute | solution.py:931
  63.4 22.6 %collective-permute-start.19 = (bf16[128,2944]{1,0:T(8,128)(2,1)S(1)}, bf16[128,2944]{1,0:T(8,128)(2,1)S(1)}, u32[]{:S(2)}, u32[]{:S(2)}) collective-permute-start(bf16[128,2944]{1,0:T(8,128)(2,1)S(1)} %pad_maximum_fusion), channel_id=1, source_target_pairs={{0,17},{1,16},{16,1},{17,0},{2,19},{3,18},{18,3},{19,2},{4,21},{5,... | collective-permute-start | bytes 2261000 | tf_op jit(solution)/shard_map/ppermute | solution.py:935
  86.8 264.9 %reduce-scatter.2.cloned.1.call-start = ((), (), s32[]{:S(2)}) async-start(), calls=%async_computation.3 | async-start | bytes 17842176 | tf_op jit(solution)/shard_map/reduce_scatter | solution.py:963
  86.9 10.0 %collective-permute-start.11 = (bf16[80,2048]{1,0:T(8,128)(2,1)}, bf16[80,2048]{1,0:T(8,128)(2,1)S(1)}, u32[]{:S(2)}, u32[]{:S(2)}) collective-permute-start(bf16[80,2048]{1,0:T(8,128)(2,1)} %get-tuple-element.112), channel_id=1, source_target_pairs={{0,2},{2,4},{4,6},{6,0},{1,3},{3,5},{5,7},{7,1},{8,10},{10,12},{12... | collective-permute-start | bytes 983048 | tf_op jit(solution)/shard_map/ppermute | solution.py:86
  87.0 9.9 %collective-permute-start.12 = (bf16[80,2048]{1,0:T(8,128)(2,1)}, bf16[80,2048]{1,0:T(8,128)(2,1)S(1)}, u32[]{:S(2)}, u32[]{:S(2)}) collective-permute-start(bf16[80,2048]{1,0:T(8,128)(2,1)} %get-tuple-element.114), channel_id=1, source_target_pairs={{0,6},{2,0},{4,2},{6,4},{1,7},{3,1},{5,3},{7,5},{8,14},{10,8},{12,... | collective-permute-start | bytes 983048 | tf_op jit(solution)/shard_map/ppermute | solution.py:87
  100.0 16.2 %collective-permute-start.13 = (bf16[160,2048]{1,0:T(8,128)(2,1)}, bf16[160,2048]{1,0:T(8,128)(2,1)S(1)}, u32[]{:S(2)}, u32[]{:S(2)}) collective-permute-start(bf16[160,2048]{1,0:T(8,128)(2,1)} %get-tuple-element.115), channel_id=1, source_target_pairs={{0,2},{2,4},{4,6},{6,0},{1,3},{3,5},{5,7},{7,1},{8,10},{10,12},{12... | collective-permute-start | bytes 1966088 | tf_op jit(solution)/shard_map/ppermute | solution.py:108
  100.0 16.2 %collective-permute-start.14 = (bf16[160,2048]{1,0:T(8,128)(2,1)}, bf16[160,2048]{1,0:T(8,128)(2,1)S(1)}, u32[]{:S(2)}, u32[]{:S(2)}) collective-permute-start(bf16[160,2048]{1,0:T(8,128)(2,1)} %get-tuple-element.116), channel_id=1, source_target_pairs={{0,6},{2,0},{4,2},{6,4},{1,7},{3,1},{5,3},{7,5},{8,14},{10,8},{12,... | collective-permute-start | bytes 1966088 | tf_op jit(solution)/shard_map/ppermute | solution.py:108
  120.2 15.3 %collective-permute-start.16 = (bf16[160,2048]{1,0:T(8,128)(2,1)}, bf16[160,2048]{1,0:T(8,128)(2,1)S(1)}, u32[]{:S(2)}, u32[]{:S(2)}) collective-permute-start(bf16[160,2048]{1,0:T(8,128)(2,1)} %get-tuple-element.118.n0.refs_0_.refs_5_), channel_id=1, source_target_pairs={{0,2},{2,4},{4,6},{6,0},{1,3},{3,5},{5,7},{7,1},{8,10},{10,12},{12... | collective-permute-start | bytes 1966088 | tf_op jit(solution)/shard_map/ppermute | solution.py:70
  120.7 14.9 %collective-permute-start.15 = (bf16[160,2048]{1,0:T(8,128)(2,1)}, bf16[160,2048]{1,0:T(8,128)(2,1)S(1)}, u32[]{:S(2)}, u32[]{:S(2)}) collective-permute-start(bf16[160,2048]{1,0:T(8,128)(2,1)} %get-tuple-element.118.n0.refs_0_.refs_5_), channel_id=1, source_target_pairs={{0,6},{2,0},{4,2},{6,4},{1,7},{3,1},{5,3},{7,5},{8,14},{10,8},{12,... | collective-permute-start | bytes 1966088 | tf_op jit(solution)/shard_map/ppermute | solution.py:71
  179.9 12.3 %collective-permute-start.20 = (bf16[80,2048]{1,0:T(8,128)(2,1)}, bf16[80,2048]{1,0:T(8,128)(2,1)S(1)}, u32[]{:S(2)}, u32[]{:S(2)}) collective-permute-start(bf16[80,2048]{1,0:T(8,128)(2,1)} %get-tuple-element.129), channel_id=1, source_target_pairs={{0,2},{2,4},{4,6},{6,0},{1,3},{3,5},{5,7},{7,1},{8,10},{10,12},{12... | collective-permute-start | bytes 983048 | tf_op jit(solution)/shard_map/ppermute | solution.py:86
  181.1 11.1 %collective-permute-start.21 = (bf16[80,2048]{1,0:T(8,128)(2,1)}, bf16[80,2048]{1,0:T(8,128)(2,1)S(1)}, u32[]{:S(2)}, u32[]{:S(2)}) collective-permute-start(bf16[80,2048]{1,0:T(8,128)(2,1)} %get-tuple-element.131), channel_id=1, source_target_pairs={{0,6},{2,0},{4,2},{6,4},{1,7},{3,1},{5,3},{7,5},{8,14},{10,8},{12,... | collective-permute-start | bytes 983048 | tf_op jit(solution)/shard_map/ppermute | solution.py:87
  195.3 17.3 %collective-permute-start.22 = (bf16[160,2048]{1,0:T(8,128)(2,1)}, bf16[160,2048]{1,0:T(8,128)(2,1)S(1)}, u32[]{:S(2)}, u32[]{:S(2)}) collective-permute-start(bf16[160,2048]{1,0:T(8,128)(2,1)} %get-tuple-element.132), channel_id=1, source_target_pairs={{0,2},{2,4},{4,6},{6,0},{1,3},{3,5},{5,7},{7,1},{8,10},{10,12},{12... | collective-permute-start | bytes 1966088 | tf_op jit(solution)/shard_map/ppermute | solution.py:108
  195.3 17.3 %collective-permute-start.23 = (bf16[160,2048]{1,0:T(8,128)(2,1)}, bf16[160,2048]{1,0:T(8,128)(2,1)S(1)}, u32[]{:S(2)}, u32[]{:S(2)}) collective-permute-start(bf16[160,2048]{1,0:T(8,128)(2,1)} %get-tuple-element.133), channel_id=1, source_target_pairs={{0,6},{2,0},{4,2},{6,4},{1,7},{3,1},{5,3},{7,5},{8,14},{10,8},{12,... | collective-permute-start | bytes 1966088 | tf_op jit(solution)/shard_map/ppermute | solution.py:108
  213.7 212.4 %all-gather.8.cloned.1.call-start = ((), (), s32[]{:S(2)}) async-start(), calls=%async_computation.4 | async-start | bytes 9191424 | tf_op jit(solution)/shard_map/all_gather | solution.py:1000
  217.7 12.2 %collective-permute-start.24 = (bf16[160,2048]{1,0:T(8,128)(2,1)}, bf16[160,2048]{1,0:T(8,128)(2,1)S(1)}, u32[]{:S(2)}, u32[]{:S(2)}) collective-permute-start(bf16[160,2048]{1,0:T(8,128)(2,1)} %get-tuple-element.138.b0.refs_10_), channel_id=1, source_target_pairs={{0,2},{2,4},{4,6},{6,0},{1,3},{3,5},{5,7},{7,1},{8,10},{10,12},{12... | collective-permute-start | bytes 1966088 | tf_op jit(solution)/shard_map/ppermute | solution.py:70
  217.8 12.1 %collective-permute-start.25 = (bf16[160,2048]{1,0:T(8,128)(2,1)}, bf16[160,2048]{1,0:T(8,128)(2,1)S(1)}, u32[]{:S(2)}, u32[]{:S(2)}) collective-permute-start(bf16[160,2048]{1,0:T(8,128)(2,1)} %get-tuple-element.138.b0.refs_10_), channel_id=1, source_target_pairs={{0,6},{2,0},{4,2},{6,4},{1,7},{3,1},{5,3},{7,5},{8,14},{10,8},{12,... | collective-permute-start | bytes 1966088 | tf_op jit(solution)/shard_map/ppermute | solution.py:71
  229.9 13.4 %collective-permute-start.26 = (bf16[80,2048]{1,0:T(8,128)(2,1)S(1)}, bf16[80,2048]{1,0:T(8,128)(2,1)S(1)}, u32[]{:S(2)}, u32[]{:S(2)}) collective-permute-start(bf16[80,2048]{1,0:T(8,128)(2,1)S(1)} %slice.41), channel_id=1, source_target_pairs={{0,2},{2,4},{4,6},{6,0},{1,3},{3,5},{5,7},{7,1},{8,10},{10,12},{12... | collective-permute-start | bytes 983048 | tf_op jit(solution)/shard_map/ppermute | solution.py:74
  230.0 13.3 %collective-permute-start.27 = (bf16[80,2048]{1,0:T(8,128)(2,1)S(1)}, bf16[80,2048]{1,0:T(8,128)(2,1)}, u32[]{:S(2)}, u32[]{:S(2)}) collective-permute-start(bf16[80,2048]{1,0:T(8,128)(2,1)S(1)} %slice.42), channel_id=1, source_target_pairs={{0,6},{2,0},{4,2},{6,4},{1,7},{3,1},{5,3},{7,5},{8,14},{10,8},{12,... | collective-permute-start | bytes 983048 | tf_op jit(solution)/shard_map/ppermute | solution.py:75
  243.4 26.6 %collective-permute-start.28 = (bf16[160,2048]{1,0:T(8,128)(2,1)}, bf16[160,2048]{1,0:T(8,128)(2,1)S(1)}, u32[]{:S(2)}, u32[]{:S(2)}) collective-permute-start(bf16[160,2048]{1,0:T(8,128)(2,1)} %get-tuple-element.141), channel_id=1, source_target_pairs={{0,2},{2,4},{4,6},{6,0},{1,3},{3,5},{5,7},{7,1},{8,10},{10,12},{12... | collective-permute-start | bytes 1966088 | tf_op jit(solution)/shard_map/ppermute | solution.py:976
  243.5 26.6 %collective-permute-start.29 = (bf16[160,2048]{1,0:T(8,128)(2,1)}, bf16[160,2048]{1,0:T(8,128)(2,1)S(1)}, u32[]{:S(2)}, u32[]{:S(2)}) collective-permute-start(bf16[160,2048]{1,0:T(8,128)(2,1)} %get-tuple-element.143), channel_id=1, source_target_pairs={{0,6},{2,0},{4,2},{6,4},{1,7},{3,1},{5,3},{7,5},{8,14},{10,8},{12,... | collective-permute-start | bytes 1966088 | tf_op jit(solution)/shard_map/ppermute | solution.py:976
  266.9 12.7 %collective-permute-start.30 = (bf16[640,128]{1,0:T(8,128)(2,1)}, bf16[640,128]{1,0:T(8,128)(2,1)S(1)}, u32[]{:S(2)}, u32[]{:S(2)}) collective-permute-start(bf16[640,128]{1,0:T(8,128)(2,1)} %get-tuple-element.151), channel_id=1, source_target_pairs={{0,1},{1,0},{2,3},{3,2},{4,5},{5,4},{6,7},{7,6},{8,9},{9,8},{10,11... | collective-permute-start | bytes 491528 | tf_op jit(solution)/shard_map/ppermute | solution.py:981
  279.7 18.7 %collective-permute-start.31 = (bf16[4,2,1024,128]{3,2,1,0:T(8,128)(2,1)}, bf16[4,2,1024,128]{3,2,1,0:T(8,128)(2,1)S(1)}, u32[]{:S(2)}, u32[]{:S(2)}) collective-permute-start(bf16[4,2,1024,128]{3,2,1,0:T(8,128)(2,1)} %get-tuple-element.153), channel_id=1, source_target_pairs={{0,8},{8,0},{1,9},{9,1},{2,10},{10,2},{3,11},{11,3},{4,12},{12,4},... | collective-permute-start | bytes 6291464 | tf_op jit(solution)/shard_map/ppermute | solution.py:806
  303.7 20.8 %collective-permute-start.33 = (bf16[2,1168,128]{2,1,0:T(8,128)(2,1)}, bf16[2,1168,128]{2,1,0:T(8,128)(2,1)S(1)}, u32[]{:S(2)}, u32[]{:S(2)}) collective-permute-start(bf16[2,1168,128]{2,1,0:T(8,128)(2,1)} %get-tuple-element.159), channel_id=1, source_target_pairs={{0,64},{32,96},{64,0},{96,32},{1,65},{33,97},{65,1},{97,33},{2,66}... | collective-permute-start | bytes 1794056 | tf_op jit(solution)/shard_map/ppermute | solution.py:810
  306.6 30.7 %collective-permute-start.34 = (bf16[2,1168,128]{2,1,0:T(8,128)(2,1)}, bf16[2,1168,128]{2,1,0:T(8,128)(2,1)S(1)}, u32[]{:S(2)}, u32[]{:S(2)}) collective-permute-start(bf16[2,1168,128]{2,1,0:T(8,128)(2,1)} %get-tuple-element.160), channel_id=1, source_target_pairs={{0,32},{32,64},{64,96},{96,0},{1,33},{33,65},{65,97},{97,1},{2,34}... | collective-permute-start | bytes 1794056 | tf_op jit(solution)/shard_map/ppermute | solution.py:810
  307.0 30.3 %collective-permute-start.35 = (bf16[2,1168,128]{2,1,0:T(8,128)(2,1)}, bf16[2,1168,128]{2,1,0:T(8,128)(2,1)S(1)}, u32[]{:S(2)}, u32[]{:S(2)}) collective-permute-start(bf16[2,1168,128]{2,1,0:T(8,128)(2,1)} %get-tuple-element.161), channel_id=1, source_target_pairs={{0,96},{32,0},{64,32},{96,64},{1,97},{33,1},{65,33},{97,65},{2,98}... | collective-permute-start | bytes 1794056 | tf_op jit(solution)/shard_map/ppermute | solution.py:810
  354.5 12.8 %collective-permute-start.41 = (bf16[1168,128]{1,0:T(8,128)(2,1)}, bf16[1168,128]{1,0:T(8,128)(2,1)S(1)}, u32[]{:S(2)}, u32[]{:S(2)}) collective-permute-start(bf16[1168,128]{1,0:T(8,128)(2,1)} %get-tuple-element.177.a), channel_id=1, source_target_pairs={{0,16},{16,0},{1,17},{17,1},{2,18},{18,2},{3,19},{19,3},{4,20},{20... | collective-permute-start | bytes 897032 | tf_op jit(solution)/shard_map/ppermute | solution.py:820
  355.4 15.9 %collective-permute-start.42 = (bf16[1168,128]{1,0:T(8,128)(2,1)}, bf16[1168,128]{1,0:T(8,128)(2,1)S(1)}, u32[]{:S(2)}, u32[]{:S(2)}) collective-permute-start(bf16[1168,128]{1,0:T(8,128)(2,1)} %get-tuple-element.178), channel_id=1, source_target_pairs={{0,1},{1,0},{2,3},{3,2},{4,5},{5,4},{6,7},{7,6},{8,9},{9,8},{10,11... | collective-permute-start | bytes 897032 | tf_op jit(solution)/shard_map/ppermute | solution.py:821
  357.8 13.5 %collective-permute-start.43 = (bf16[1168,128]{1,0:T(8,128)(2,1)}, bf16[1168,128]{1,0:T(8,128)(2,1)S(1)}, u32[]{:S(2)}, u32[]{:S(2)}) collective-permute-start(bf16[1168,128]{1,0:T(8,128)(2,1)} %get-tuple-element.178), channel_id=1, source_target_pairs={{0,17},{1,16},{16,1},{17,0},{2,19},{3,18},{18,3},{19,2},{4,21},{5,... | collective-permute-start | bytes 897032 | tf_op jit(solution)/shard_map/ppermute | solution.py:822
  364.6 48.7 %collective-permute-start.39 = (bf16[160,2048]{1,0:T(8,128)(2,1)}, bf16[160,2048]{1,0:T(8,128)(2,1)S(1)}, u32[]{:S(2)}, u32[]{:S(2)}) collective-permute-start(bf16[160,2048]{1,0:T(8,128)(2,1)} %get-tuple-element.174), channel_id=1, source_target_pairs={{0,2},{2,4},{4,6},{6,0},{1,3},{3,5},{5,7},{7,1},{8,10},{10,12},{12... | collective-permute-start | bytes 1966088 | tf_op jit(solution)/shard_map/ppermute | solution.py:108
  364.6 48.8 %collective-permute-start.40 = (bf16[160,2048]{1,0:T(8,128)(2,1)}, bf16[160,2048]{1,0:T(8,128)(2,1)S(1)}, u32[]{:S(2)}, u32[]{:S(2)}) collective-permute-start(bf16[160,2048]{1,0:T(8,128)(2,1)} %get-tuple-element.175), channel_id=1, source_target_pairs={{0,6},{2,0},{4,2},{6,4},{1,7},{3,1},{5,3},{7,5},{8,14},{10,8},{12,... | collective-permute-start | bytes 1966088 | tf_op jit(solution)/shard_map/ppermute | solution.py:108
  374.8 10.6 %collective-permute-start.44 = (bf16[1168,128]{1,0:T(8,128)(2,1)}, bf16[1168,128]{1,0:T(8,128)(2,1)}, u32[]{:S(2)}, u32[]{:S(2)}) collective-permute-start(bf16[1168,128]{1,0:T(8,128)(2,1)} %sum_z.1.refs_0_), channel_id=1, source_target_pairs={{0,32},{32,64},{64,96},{96,0},{1,33},{33,65},{65,97},{97,1},{2,34}... | collective-permute-start | bytes 897032 | tf_op jit(solution)/shard_map/ppermute | solution.py:827
  375.4 49.3 %collective-permute-start.36 = (bf16[160,2048]{1,0:T(8,128)(2,1)}, bf16[160,2048]{1,0:T(8,128)(2,1)S(1)}, u32[]{:S(2)}, u32[]{:S(2)}) collective-permute-start(bf16[160,2048]{1,0:T(8,128)(2,1)} %get-tuple-element.163), channel_id=1, source_target_pairs={{0,4},{2,6},{4,0},{6,2},{1,5},{3,7},{5,1},{7,3},{8,12},{10,14},{12... | collective-permute-start | bytes 1966088 | tf_op jit(solution)/shard_map/ppermute | solution.py:999
  377.1 24.3 %collective-permute-start.45 = (bf16[1168,128]{1,0:T(8,128)(2,1)}, bf16[1168,128]{1,0:T(8,128)(2,1)}, u32[]{:S(2)}, u32[]{:S(2)}) collective-permute-start(bf16[1168,128]{1,0:T(8,128)(2,1)} %sum_z.1.refs_0_), channel_id=1, source_target_pairs={{0,64},{32,96},{64,0},{96,32},{1,65},{33,97},{65,1},{97,33},{2,66}... | collective-permute-start | bytes 897032 | tf_op jit(solution)/shard_map/ppermute | solution.py:827
  385.5 24.0 %collective-permute-start.46 = (bf16[1168,128]{1,0:T(8,128)(2,1)}, bf16[1168,128]{1,0:T(8,128)(2,1)}, u32[]{:S(2)}, u32[]{:S(2)}) collective-permute-start(bf16[1168,128]{1,0:T(8,128)(2,1)} %sum_z.1.refs_0_), channel_id=1, source_target_pairs={{0,96},{32,0},{64,32},{96,64},{1,97},{33,1},{65,33},{97,65},{2,98}... | collective-permute-start | bytes 897032 | tf_op jit(solution)/shard_map/ppermute | solution.py:827
  401.5 16.8 %collective-permute-start.47 = (bf16[1168,128]{1,0:T(8,128)(2,1)}, bf16[1168,128]{1,0:T(8,128)(2,1)}, u32[]{:S(2)}, u32[]{:S(2)}) collective-permute-start(bf16[1168,128]{1,0:T(8,128)(2,1)} %sum_z.1.refs_0_), channel_id=1, source_target_pairs={{0,8},{8,0},{1,9},{9,1},{2,10},{10,2},{3,11},{11,3},{4,12},{12,4},... | collective-permute-start | bytes 897032 | tf_op jit(solution)/shard_map/ppermute | solution.py:828
  422.6 13.2 %collective-permute-start.53 = (f32[2,2048]{1,0:T(2,128)}, f32[2,2048]{1,0:T(2,128)S(1)}, u32[]{:S(2)}, u32[]{:S(2)}) collective-permute-start(f32[2,2048]{1,0:T(2,128)} %get-tuple-element.180), channel_id=1, source_target_pairs={{0,6},{2,0},{4,2},{6,4},{1,7},{3,1},{5,3},{7,5},{8,14},{10,8},{12,... | collective-permute-start | bytes 49160 | tf_op jit(solution)/shard_map/ppermute | solution.py:990
  423.3 12.5 %collective-permute-start.52 = (f32[2,2048]{1,0:T(2,128)}, f32[2,2048]{1,0:T(2,128)S(1)}, u32[]{:S(2)}, u32[]{:S(2)}) collective-permute-start(f32[2,2048]{1,0:T(2,128)} %get-tuple-element.180), channel_id=1, source_target_pairs={{0,4},{2,6},{4,0},{6,2},{1,5},{3,7},{5,1},{7,3},{8,12},{10,14},{12... | collective-permute-start | bytes 49160 | tf_op jit(solution)/shard_map/ppermute | solution.py:990
  424.0 11.8 %collective-permute-start.51 = (f32[2,2048]{1,0:T(2,128)}, f32[2,2048]{1,0:T(2,128)S(1)}, u32[]{:S(2)}, u32[]{:S(2)}) collective-permute-start(f32[2,2048]{1,0:T(2,128)} %get-tuple-element.180), channel_id=1, source_target_pairs={{0,2},{2,4},{4,6},{6,0},{1,3},{3,5},{5,7},{7,1},{8,10},{10,12},{12... | collective-permute-start | bytes 49160 | tf_op jit(solution)/shard_map/ppermute | solution.py:990
  (55 other events, 320.2 us)
Sparse Core Ops, SparseCore 0:
  44.4 35.0 all-gather.3
  87.0 39.9 all-gather.5
  212.8 138.9 reduce-scatter.1
  353.3 67.5 all-gather.7

commit v14 on v13

--- a/solution.py
+++ b/solution.py
@@ -823,11 +823,12 @@
         name="sum_z",
     )
     d_one = last_step(p0, q1, q3)
-    input_grad = finish(d_one)
-    mine = [tie(g, input_grad)] + [lax.ppermute(g, "y", shift(4, s)) for s in (1, 2, 3)]
-    theirs = [lax.ppermute(v, "core", shift(2, 1)) for v in [g] + mine[1:]]
+    outputs = own, *finish(d_one, own)
+    mine = [g] + [lax.ppermute(g, "y", shift(4, s)) for s in (1, 2, 3)]
+    mine[1:] = [tie(v, *outputs[1:]) for v in mine[1:]]
+    theirs = [lax.ppermute(v, "core", shift(2, 1)) for v in mine]
     shapes = (sds((DH, QW), F32), sds((AW // 2, D), F32), sds((2, D), F32))
-    return own, input_grad, small_call(unpack_tail_body, shapes, idx, *mine, *theirs, name="unpack_tail")
+    return outputs, small_call(unpack_tail_body, shapes, idx, *mine, *theirs, name="unpack_tail")
 
 
 def inverse_rms(v):
@@ -988,19 +989,22 @@
         gain_grad_two,
     )
     over_x = lambda v: sum((tie(lax.ppermute(v, "x", shift(4, s)), grad_gate) for s in (1, 2, 3)), v)
-    finish = lambda d_one: row_call(
-        norm_back_body,
-        (sds((BLK, D), F32), sds((BLK, D)), sds((1, D), F32)),
-        after_grad, tokens, *d_one, gain_one.reshape(1, D), name="norm_back_one",
-    )[1]
-    summed, input_grad, (grad_qkv, grad_out, gains) = sum_tail(
+    def finish(d_one, own):
+        last = lax.ppermute(tie(layer_parts[2], own), "x", shift(4, 2))
+        terms = [layer_parts[0], *layer, last]
+        layer_out = sum((v.astype(F32) for v in terms), after_attn).astype(BF16)
+        _, input_grad, _ = row_call(
+            norm_back_body,
+            (sds((BLK, D), F32), sds((BLK, D)), sds((1, D), F32)),
+            after_grad, tokens, *d_one, gain_one.reshape(1, D), name="norm_back_one",
+        )
+        return input_grad, layer_out
+
+    (own_sum, input_grad, layer_out), (grad_qkv, grad_out, gains) = sum_tail(
         idx, (tail[0], tie(tail[1], dkv_got)), tail_kv, parts, finish
     )
-    layer.append(lax.ppermute(tie(layer_parts[2], summed), "x", shift(4, 2)))
-    grads = lax.all_gather(tie(grads, summed), ("zl", "y", "core"), axis=0, tiled=True)
+    grads = lax.all_gather(tie(grads, own_sum), ("zl", "y", "core"), axis=0, tiled=True)
     grad_gate, grad_up, grad_down = unpack(grads)
-    layer_out = sum((v.astype(F32) for v in layer), after_attn + layer_parts[0].astype(F32))
-    layer_out = layer_out.astype(BF16)
     gains = over_x(gains)
     return (
         layer_out, input_grad, gains[0], grad_qkv, grad_out, grad_gate, grad_up,

time: 451 us -> 456 us (1.011)
  waiting for transfers between devices: 136 us -> 150 us
  starting transfers between devices: 93.1 us -> 84.7 us
    ppermute x3, waiting for transfers between devices: 9.56 us -> 23.9 us  [relay(): got_a = lax.ppermute(p2a, 'x', shift(4, 1))]
    ppermute x8, starting transfers between devices: 19.4 us -> 10 us  [the longest x4 4.1 us: sum_tail(): theirs = [lax.ppermute(v, 'core', shift(2, 1)) for v in mine]]
    unnamed x90 -> x92, local copies, waits for them, and re-layouts: 13.7 us -> 11.4 us
  transfers between devices with their start and end apart: 58 -> 58, of which waited for: 19 -> 22; matrix products, arithmetic and copies ran while one was open for 3% -> 3% of each run, Pallas kernels for 29% -> 29%
where the time goes in v14:
time: 456 us; the launch traced here: 448 us
  Pallas kernels  168 us (37%)
  waiting for transfers between devices  150 us (33%)
  starting transfers between devices  84.7 us (19%)
  local copies, waits for them, and re-layouts  19.9 us (4%)
  between operations  14.7 us (3%)
  other arithmetic  10.5 us (2%)
    ppermute x3, waiting for transfers between devices, sum_tail(): got = [lax.ppermute(g[s], 'y', shift(4, s)) for s in (2, 1, 3)]  28 us
    ppermute x3, waiting for transfers between devices, gather_x(): from_prev = lax.ppermute(v, 'x', shift(4, 1))  27.2 us
    ppermute x3, waiting for transfers between devices, relay(): got_a = lax.ppermute(p2a, 'x', shift(4, 1))  23.9 us
    pallas_call x1, Pallas kernels, ffn(): pl.pallas_call(ffn_body, grid=(TILES,), out_shape=(sds((ROWS, FF4)),) * 3...  20.8 us
    pallas_call x1, Pallas kernels, attend_back(): pl.pallas_call(attend_back_body, grid=(1,), out_shape=(sds((4, BLK, AW)),...  20.6 us
    ppermute x3, waiting for transfers between devices, last_step(): lax.ppermute(q1, 'x', shift(4, 1))  16 us
    pallas_call x1, Pallas kernels, ffn_back(): pl.pallas_call(ffn_back_body, grid_spec=pltpu.PrefetchScalarGridSpec(num_...  15.4 us
    ppermute x3, waiting for transfers between devices, sum_tail(): mine = [g] + [lax.ppermute(g, 'y', shift(4, s)) for s in (1, 2, 3)]  15.3 us
  transfers between devices with their start and end apart: 58, of which 22 were waited for; matrix products, arithmetic and copies ran while one was open for 3% of the time, Pallas kernels for 29%

profile of v14, /device:TPU:1, one launch (start us, length us, event | category | flops | bytes accessed | tf_op | source)
XLA Modules:
  0.0 448.0 jit_solution(5153169254436633951)
XLA Ops:
  10.0 3.4 collective-permute-start
  14.3 3.6 collective-permute-start.4
  24.8 5.1 %collective-permute-done.1.n3.refs_4_.refs_9_ = bf16[160,2048]{1,0:T(8,128)(2,1)} collective-permute-done((bf16[160,2048]{1,0:T(8,128)(2,1)S(1)}, bf16[160,2048]{1,0:T(8,128)(2,1)}, u32[]{:S(2)}, u32[]{:S(2)}) %collective-permute-start.1) | collective-permute-done | bytes 655392 | tf_op jit(solution)/shard_map/ppermute | solution.py:70
  34.5 9.0 %collective-permute-done.5 = bf16[128,2048]{1,0:T(8,128)(2,1)S(1)} collective-permute-done((bf16[128,2048]{1,0:T(8,128)(2,1)}, bf16[128,2048]{1,0:T(8,128)(2,1)S(1)}, u32[]{:S(2)}, u32[]{:S(2)}) %collective-permute-start.5) | collective-permute-done | bytes 524320 | tf_op jit(solution)/shard_map/ppermute | solution.py:924
  51.5 6.7 %qkv_forward.1 = (bf16[4,1280,128]{2,1,0:T(8,128)(2,1)}, bf16[640,128]{1,0:T(8,128)(2,1)}) custom-call(s32[4]{0:T(128)} %pad_add_fusion.idx, bf16[160,2048]{1,0:T(8,128)(2,1)} %copy-done.4, bf16[160,2048]{1,0:T(8,128)(2,1)} %copy-done.7, bf16[80,2048]{1,0:T(8,128)(2,1)} %copy-done.24, bf16[80,2048]{1,0:T(8,128)(2,1)} %copy-done.25, ...), custom_call_target="tpu_custom_call" | custom-call | flops 1677721600 | bytes 7000000 | tf_op jit(solution)/shard_map/qkv_forward/pallas_call | solution.py:184
  58.2 3.0 collective-permute-start.7
  65.9 8.6 %attend.1 = (bf16[4,160,512]{2,1,0:T(8,128)(2,1)}, bf16[4,1280,128]{2,1,0:T(8,128)(2,1)}) custom-call(s32[4]{0:T(128)} %pad_add_fusion.idx, bf16[4,1280,128]{2,1,0:T(8,128)(2,1)} %get-tuple-element.106.q, bf16[640,128]{1,0:T(8,128)(2,1)} %get-tuple-element.107.kv_own, bf16[640,128]{1,0:T(8,128)(2,1)} %copy-done.45, s32[1,1280]{1,0:T(1,128)} %reshape_tile.3.first), custom_call_target="tpu_custom_call" | custom-call | flops 12000000000 | bytes 3000000 | tf_op jit(solution)/shard_map/attend/pallas_call | solution.py:277
  74.5 3.5 collective-permute-done.8.c1.refs_1_
  78.1 3.7 collective-permute-done.10.c3.refs_3_
  81.8 4.2 out_project.1
  87.0 2.7 collective-permute-start.12
  89.6 7.2 %collective-permute-done.11.got_a = bf16[80,2048]{1,0:T(8,128)(2,1)S(1)} collective-permute-done((bf16[80,2048]{1,0:T(8,128)(2,1)}, bf16[80,2048]{1,0:T(8,128)(2,1)S(1)}, u32[]{:S(2)}, u32[]{:S(2)}) %collective-permute-start.11) | collective-permute-done | bytes 327712 | tf_op jit(solution)/shard_map/ppermute | solution.py:86
  100.0 2.7 collective-permute-start.14
  102.7 13.6 %collective-permute-done.13.b = bf16[160,2048]{1,0:T(8,128)(2,1)S(1)} collective-permute-done((bf16[160,2048]{1,0:T(8,128)(2,1)}, bf16[160,2048]{1,0:T(8,128)(2,1)S(1)}, u32[]{:S(2)}, u32[]{:S(2)}) %collective-permute-start.13) | collective-permute-done | bytes 655392 | tf_op jit(solution)/shard_map/ppermute | solution.py:108
  117.3 2.9 norm_two.1
  122.9 12.6 %collective-permute-done.16.n3.refs_4_.refs_9_ = bf16[160,2048]{1,0:T(8,128)(2,1)S(1)} collective-permute-done((bf16[160,2048]{1,0:T(8,128)(2,1)}, bf16[160,2048]{1,0:T(8,128)(2,1)S(1)}, u32[]{:S(2)}, u32[]{:S(2)}) %collective-permute-start.16) | collective-permute-done | bytes 655392 | tf_op jit(solution)/shard_map/ppermute | solution.py:70
  135.7 3.2 collective-permute-start.18
  138.9 3.9 collective-permute-done.17.n2a.refs_2_.refs_7_
  143.6 20.8 %ffn.1 = (bf16[640,1408]{1,0:T(8,128)(2,1)}, bf16[640,1408]{1,0:T(8,128)(2,1)}, bf16[640,1408]{1,0:T(8,128)(2,1)}) custom-call(s32[4]{0:T(128)} %pad_add_fusion.idx, bf16[160,2048]{1,0:T(8,128)(2,1)} %get-tuple-element.120.n0.refs_0_.refs_5_, bf16[160,2048]{1,0:T(8,128)(2,1)} %copy-done.2, bf16[80,2048]{1,0:T(8,128)(2,1)} %copy-done.8, ...), custom_call_target="tpu_custom_call" | custom-call | flops 11072962560 | bytes 34000000 | tf_op jit(solution)/shard_map/ffn/pallas_call | solution.py:523
  164.5 15.4 %ffn_back.1 = (bf16[160,2048]{1,0:T(8,128)(2,1)}, bf16[160,2048]{1,0:T(8,128)(2,1)}, bf16[80,2048]{1,0:T(8,128)(2,1)}, bf16[80,2048]{1,0:T(8,128)(2,1)}, bf16[160,2048]{1,0:T(8,128)(2,1)}) custom-call(s32[4]{0:T(128)} %pad_add_fusion.idx, bf16[640,1408]{1,0:T(8,128)(2,1)} %get-tuple-element.185.dgate.refs_10_, ...), custom_call_target="tpu_custom_call" | custom-call | flops 7381975040 | bytes 18000000 | tf_op jit(solution)/shard_map/ffn_back/pallas_call | solution.py:589
  183.1 9.1 %down_grads.1.refs_12_ = bf16[2,16,2112,128]{3,2,1,0:T(8,128)(2,1)} custom-call(bf16[160,2048]{1,0:T(8,128)(2,1)} %refs_0_.1, bf16[160,2048]{1,0:T(8,128)(2,1)} %copy-done.19, bf16[160,2048]{1,0:T(8,128)(2,1)} %collective-permute-done.9.c2.refs_2_, bf16[160,2048]{1,0:T(8,128)(2,1)} %collective-permute-done.10.c3.refs_3_, ...), custom_call_target="tpu_custom_call" | custom-call | flops 3690987520 | bytes 10000000 | tf_op jit(solution)/shard_map/down_grads/pallas_call | solution.py:656
  195.3 2.7 collective-permute-start.23
  198.0 14.6 %gate_up_grads.1 = bf16[2,16,2112,128]{3,2,1,0:T(8,128)(2,1)} custom-call(bf16[160,2048]{1,0:T(8,128)(2,1)} %get-tuple-element.120.n0.refs_0_.refs_5_, bf16[160,2048]{1,0:T(8,128)(2,1)} %copy-done.2, bf16[80,2048]{1,0:T(8,128)(2,1)} %copy-done.8, bf16[80,2048]{1,0:T(8,128)(2,1)} %copy-done.9, ...), custom_call_target="tpu_custom_call", output_to_operand_aliasing={{}: (12, {})} | custom-call | flops 7381975040 | bytes 20000000 | tf_op jit(solution)/shard_map/gate_up_grads/pallas_call | solution.py:625
  213.7 4.1 norm_back_two.1
  217.8 2.7 collective-permute-start.25
  220.5 9.4 %collective-permute-done.24.b3.refs_14_ = bf16[160,2048]{1,0:T(8,128)(2,1)S(1)} collective-permute-done((bf16[160,2048]{1,0:T(8,128)(2,1)}, bf16[160,2048]{1,0:T(8,128)(2,1)S(1)}, u32[]{:S(2)}, u32[]{:S(2)}) %collective-permute-start.24) | collective-permute-done | bytes 655392 | tf_op jit(solution)/shard_map/ppermute | solution.py:70
  230.1 2.7 collective-permute-start.27
  232.8 10.5 %down_project.1 = (bf16[160,2048]{1,0:T(8,128)(2,1)}, bf16[160,2048]{1,0:T(8,128)(2,1)}, bf16[160,2048]{1,0:T(8,128)(2,1)}, bf16[160,2048]{1,0:T(8,128)(2,1)}) custom-call(s32[4]{0:T(128)} %pad_add_fusion.idx, bf16[640,1408]{1,0:T(8,128)(2,1)} %get-tuple-element.186.hid.refs_4_, bf16[704,2048]{1,0:T(8,128)(2,1)} %w0.9, bf16[8,128,2048]{2,1,0:T(8,128)(2,1)} %bitcast.17), custom_call_target="tpu_custom_call" | custom-call | flops 3690987520 | bytes 11000000 | tf_op jit(solution)/shard_map/down_project/pallas_call | solution.py:559
  243.5 2.8 collective-permute-start.29
  246.3 20.6 %attend_back.1 = (bf16[4,160,512]{2,1,0:T(8,128)(2,1)}, f32[640,128]{1,0:T(8,128)}, bf16[640,128]{1,0:T(8,128)(2,1)}) custom-call(s32[4]{0:T(128)} %pad_add_fusion.idx, bf16[4,1280,128]{2,1,0:T(8,128)(2,1)} %get-tuple-element.147.qx, bf16[640,128]{1,0:T(8,128)(2,1)} %get-tuple-element.107.kv_own, bf16[640,128]{1,0:T(8,128)(2,1)} %copy-done.45, ...), custom_call_target="tpu_custom_call" | custom-call | flops 30000001024 | bytes 8000000 | tf_op jit(solution)/shard_map/attend_back/pallas_call | solution.py:388
  267.0 3.3 collective-permute-start.30
  270.3 9.5 %attn_grads.1 = (bf16[4,2,1024,128]{3,2,1,0:T(8,128)(2,1)}, bf16[4,2,1024,128]{3,2,1,0:T(8,128)(2,1)}) custom-call(s32[4]{0:T(128)} %pad_add_fusion.idx, bf16[160,2048]{1,0:T(8,128)(2,1)} %copy-done.4, bf16[160,2048]{1,0:T(8,128)(2,1)} %copy-done.7, bf16[80,2048]{1,0:T(8,128)(2,1)} %copy-done.24, bf16[80,2048]{1,0:T(8,128)(2,1)} %copy-done.25, ...), custom_call_target="tpu_custom_call" | custom-call | flops 2684354560 | bytes 10000000 | tf_op jit(solution)/shard_map/attn_grads/pallas_call | solution.py:735
  279.8 9.2 %collective-permute-start.31 = (bf16[4,2,1024,128]{3,2,1,0:T(8,128)(2,1)}, bf16[4,2,1024,128]{3,2,1,0:T(8,128)(2,1)S(1)}, u32[]{:S(2)}, u32[]{:S(2)}) collective-permute-start(bf16[4,2,1024,128]{3,2,1,0:T(8,128)(2,1)} %get-tuple-element.155), channel_id=1, source_target_pairs={{0,8},{8,0},{1,9},{9,1},{2,10},{10,2},{3,11},{11,3},{4,12},{12,4},... | collective-permute-start | bytes 6291464 | tf_op jit(solution)/shard_map/ppermute | solution.py:806
  289.0 7.5 %qkv_back.1 = (bf16[4,2,144,128]{3,2,1,0:T(8,128)(2,1)}, bf16[4,2,144,128]{3,2,1,0:T(8,128)(2,1)}, bf16[160,2048]{1,0:T(8,128)(2,1)}, bf16[160,2048]{1,0:T(8,128...) custom-call(s32[4]{0:T(128)} %pad_add_fusion.idx, ...), custom_call_target="tpu_custom_call" | custom-call | flops 1677721600 | bytes 13000000 | tf_op jit(solution)/shard_map/qkv_back/pallas_call | solution.py:446
  299.8 4.0 sum_core.1
  303.8 2.8 collective-permute-start.33
  309.3 15.1 %collective-permute-done.33.b = bf16[2,1168,128]{2,1,0:T(8,128)(2,1)S(1)} collective-permute-done((bf16[2,1168,128]{2,1,0:T(8,128)(2,1)}, bf16[2,1168,128]{2,1,0:T(8,128)(2,1)S(1)}, u32[]{:S(2)}, u32[]{:S(2)}) %collective-permute-start.33) | collective-permute-done | bytes 598048 | tf_op jit(solution)/shard_map/ppermute | solution.py:810
  324.5 12.8 %collective-permute-done.34.c = bf16[2,1168,128]{2,1,0:T(8,128)(2,1)S(1)} collective-permute-done((bf16[2,1168,128]{2,1,0:T(8,128)(2,1)}, bf16[2,1168,128]{2,1,0:T(8,128)(2,1)S(1)}, u32[]{:S(2)}, u32[]{:S(2)}) %collective-permute-start.34) | collective-permute-done | bytes 598048 | tf_op jit(solution)/shard_map/ppermute | solution.py:810
  338.3 2.7 sum_y.1
  341.0 10.5 %reduce-scatter.2.cloned.1.call-done = bf16[1,2112,128]{2,1,0:T(8,128)(2,1)} async-done(((bf16[32,2112,128]{2,1,0:T(8,128)(2,1)}), bf16[1,2112,128]{2,1,0:T(8,128)(2,1)}) %reduce-scatter.2.cloned.1.call-update) | async-done | bytes 540688 | tf_op jit(solution)/shard_map/reduce_scatter | solution.py:964
  351.5 2.9 collective-permute-start.36
  360.4 16.7 %collective-permute-done.37.got_a = bf16[80,2048]{1,0:T(8,128)(2,1)S(1)} collective-permute-done((bf16[80,2048]{1,0:T(8,128)(2,1)S(1)}, bf16[80,2048]{1,0:T(8,128)(2,1)S(1)}, u32[]{:S(2)}, u32[]{:S(2)}) %collective-permute-start.37) | collective-permute-done | bytes 327712 | tf_op jit(solution)/shard_map/ppermute | solution.py:86
  381.7 2.7 collective-permute-start.40
  384.4 4.4 collective-permute-done.43.d
  400.4 3.9 norm_back_one.1
  404.3 15.3 %collective-permute-done.45.refs_2_ = bf16[1168,128]{1,0:T(8,128)(2,1)} collective-permute-done((bf16[1168,128]{1,0:T(8,128)(2,1)}, bf16[1168,128]{1,0:T(8,128)(2,1)}, u32[]{:S(2)}, u32[]{:S(2)}) %collective-permute-start.45) | collective-permute-done | bytes 299040 | tf_op jit(solution)/shard_map/ppermute | solution.py:827
  425.0 4.2 unpack_tail.1
  430.6 9.8 %unpack.1 = (f32[1024,1408]{1,0:T(8,128)}, f32[1024,1408]{1,0:T(8,128)}, f32[704,2048]{1,0:T(8,128)}) custom-call(bf16[16,2112,128]{2,1,0:T(8,128)(2,1)} %all-gather.8.cloned.1.call-done.piece), custom_call_target="tpu_custom_call" | custom-call | flops 1000000 | bytes 26000000 | tf_op jit(solution)/shard_map/unpack/pallas_call | solution.py:680
  (224 shorter events, 81.0 us)
Async XLA Ops:
  7.2 74.6 %all-gather.4.cloned.1.call-start = ((), (), s32[]{:S(2)}) async-start(), calls=%async_computation.1 | async-start | bytes 4718592 | tf_op jit(solution)/shard_map/all_gather | solution.py:919
  10.0 21.0 %collective-permute-start = (bf16[160,2048]{1,0:T(8,128)(2,1)S(1)}, bf16[160,2048]{1,0:T(8,128)(2,1)S(1)}, u32[]{:S(2)}, u32[]{:S(2)}) collective-permute-start(bf16[160,2048]{1,0:T(8,128)(2,1)S(1)} %fusion.2.n0.refs_0_.refs_5_), channel_id=1, source_target_pairs={{0,6},{2,0},{4,2},{6,4},{1,7},{3,1},{5,3},{7,5},{8,14},{10,8},{12,... | collective-permute-start | bytes 1966088 | tf_op jit(solution)/shard_map/ppermute | solution.py:71
  13.3 16.6 %collective-permute-start.1 = (bf16[160,2048]{1,0:T(8,128)(2,1)S(1)}, bf16[160,2048]{1,0:T(8,128)(2,1)}, u32[]{:S(2)}, u32[]{:S(2)}) collective-permute-start(bf16[160,2048]{1,0:T(8,128)(2,1)S(1)} %fusion.2.n0.refs_0_.refs_5_), channel_id=1, source_target_pairs={{0,2},{2,4},{4,6},{6,0},{1,3},{3,5},{5,7},{7,1},{8,10},{10,12},{12... | collective-permute-start | bytes 1966088 | tf_op jit(solution)/shard_map/ppermute | solution.py:70
  14.3 29.2 %collective-permute-start.4 = (bf16[512,640]{1,0:T(8,128)(2,1)}, bf16[512,640]{1,0:T(8,128)(2,1)S(1)}, u32[]{:S(2)}, u32[]{:S(2)}) collective-permute-start(bf16[512,640]{1,0:T(8,128)(2,1)} %constant_dynamic-slice_fusion.5), channel_id=1, source_target_pairs={{0,1},{1,0},{2,3},{3,2},{4,5},{5,4},{6,7},{7,6},{8,9},{9,8},{10,11... | collective-permute-start | bytes 1966088 | tf_op jit(solution)/shard_map/ppermute | solution.py:134
  20.7 22.7 %collective-permute-start.5 = (bf16[128,2048]{1,0:T(8,128)(2,1)}, bf16[128,2048]{1,0:T(8,128)(2,1)S(1)}, u32[]{:S(2)}, u32[]{:S(2)}) collective-permute-start(bf16[128,2048]{1,0:T(8,128)(2,1)} %pad_maximum_fusion.1), channel_id=1, source_target_pairs={{0,1},{1,0},{2,3},{3,2},{4,5},{5,4},{6,7},{7,6},{8,9},{9,8},{10,11... | collective-permute-start | bytes 1572872 | tf_op jit(solution)/shard_map/ppermute | solution.py:924
  31.0 12.5 %collective-permute-start.2 = (bf16[80,2048]{1,0:T(8,128)(2,1)S(1)}, bf16[80,2048]{1,0:T(8,128)(2,1)S(1)}, u32[]{:S(2)}, u32[]{:S(2)}) collective-permute-start(bf16[80,2048]{1,0:T(8,128)(2,1)S(1)} %slice.37), channel_id=1, source_target_pairs={{0,2},{2,4},{4,6},{6,0},{1,3},{3,5},{5,7},{7,1},{8,10},{10,12},{12... | collective-permute-start | bytes 983048 | tf_op jit(solution)/shard_map/ppermute | solution.py:74
  31.9 11.6 %collective-permute-start.3 = (bf16[80,2048]{1,0:T(8,128)(2,1)}, bf16[80,2048]{1,0:T(8,128)(2,1)S(1)}, u32[]{:S(2)}, u32[]{:S(2)}) collective-permute-start(bf16[80,2048]{1,0:T(8,128)(2,1)} %slice.38), channel_id=1, source_target_pairs={{0,6},{2,0},{4,2},{6,4},{1,7},{3,1},{5,3},{7,5},{8,14},{10,8},{12,... | collective-permute-start | bytes 983048 | tf_op jit(solution)/shard_map/ppermute | solution.py:75
  44.5 98.4 %all-gather.6.cloned.1.call-start = ((), (), s32[]{:S(2)}) async-start(), calls=%async_computation.2 | async-start | bytes 6782976 | tf_op jit(solution)/shard_map/all_gather | solution.py:919
  47.3 30.7 %collective-permute-start.8 = (bf16[160,2048]{1,0:T(8,128)(2,1)S(1)}, bf16[160,2048]{1,0:T(8,128)(2,1)S(1)}, u32[]{:S(2)}, u32[]{:S(2)}) collective-permute-start(bf16[160,2048]{1,0:T(8,128)(2,1)S(1)} %copy-done.5), channel_id=1, source_target_pairs={{0,6},{2,0},{4,2},{6,4},{1,7},{3,1},{5,3},{7,5},{8,14},{10,8},{12,... | collective-permute-start | bytes 1966088 | tf_op jit(solution)/shard_map/ppermute | solution.py:932
  50.0 28.1 %collective-permute-start.9 = (bf16[160,2048]{1,0:T(8,128)(2,1)S(1)}, bf16[160,2048]{1,0:T(8,128)(2,1)}, u32[]{:S(2)}, u32[]{:S(2)}) collective-permute-start(bf16[160,2048]{1,0:T(8,128)(2,1)S(1)} %copy-done.5), channel_id=1, source_target_pairs={{0,4},{2,6},{4,0},{6,2},{1,5},{3,7},{5,1},{7,3},{8,12},{10,14},{12... | collective-permute-start | bytes 1966088 | tf_op jit(solution)/shard_map/ppermute | solution.py:932
  50.0 31.8 %collective-permute-start.10 = (bf16[160,2048]{1,0:T(8,128)(2,1)S(1)}, bf16[160,2048]{1,0:T(8,128)(2,1)}, u32[]{:S(2)}, u32[]{:S(2)}) collective-permute-start(bf16[160,2048]{1,0:T(8,128)(2,1)S(1)} %copy-done.5), channel_id=1, source_target_pairs={{0,2},{2,4},{4,6},{6,0},{1,3},{3,5},{5,7},{7,1},{8,10},{10,12},{12... | collective-permute-start | bytes 1966088 | tf_op jit(solution)/shard_map/ppermute | solution.py:932
  63.4 22.6 %collective-permute-start.19 = (bf16[128,2944]{1,0:T(8,128)(2,1)S(1)}, bf16[128,2944]{1,0:T(8,128)(2,1)S(1)}, u32[]{:S(2)}, u32[]{:S(2)}) collective-permute-start(bf16[128,2944]{1,0:T(8,128)(2,1)S(1)} %pad_maximum_fusion), channel_id=1, source_target_pairs={{0,17},{1,16},{16,1},{17,0},{2,19},{3,18},{18,3},{19,2},{4,21},{5,... | collective-permute-start | bytes 2261000 | tf_op jit(solution)/shard_map/ppermute | solution.py:936
  86.8 264.6 %reduce-scatter.2.cloned.1.call-start = ((), (), s32[]{:S(2)}) async-start(), calls=%async_computation.3 | async-start | bytes 17842176 | tf_op jit(solution)/shard_map/reduce_scatter | solution.py:964
  100.0 16.2 %collective-permute-start.13 = (bf16[160,2048]{1,0:T(8,128)(2,1)}, bf16[160,2048]{1,0:T(8,128)(2,1)S(1)}, u32[]{:S(2)}, u32[]{:S(2)}) collective-permute-start(bf16[160,2048]{1,0:T(8,128)(2,1)} %get-tuple-element.117), channel_id=1, source_target_pairs={{0,2},{2,4},{4,6},{6,0},{1,3},{3,5},{5,7},{7,1},{8,10},{10,12},{12... | collective-permute-start | bytes 1966088 | tf_op jit(solution)/shard_map/ppermute | solution.py:108
  100.0 16.2 %collective-permute-start.14 = (bf16[160,2048]{1,0:T(8,128)(2,1)}, bf16[160,2048]{1,0:T(8,128)(2,1)S(1)}, u32[]{:S(2)}, u32[]{:S(2)}) collective-permute-start(bf16[160,2048]{1,0:T(8,128)(2,1)} %get-tuple-element.118), channel_id=1, source_target_pairs={{0,6},{2,0},{4,2},{6,4},{1,7},{3,1},{5,3},{7,5},{8,14},{10,8},{12,... | collective-permute-start | bytes 1966088 | tf_op jit(solution)/shard_map/ppermute | solution.py:108
  120.2 15.3 %collective-permute-start.16 = (bf16[160,2048]{1,0:T(8,128)(2,1)}, bf16[160,2048]{1,0:T(8,128)(2,1)S(1)}, u32[]{:S(2)}, u32[]{:S(2)}) collective-permute-start(bf16[160,2048]{1,0:T(8,128)(2,1)} %get-tuple-element.120.n0.refs_0_.refs_5_), channel_id=1, source_target_pairs={{0,2},{2,4},{4,6},{6,0},{1,3},{3,5},{5,7},{7,1},{8,10},{10,12},{12... | collective-permute-start | bytes 1966088 | tf_op jit(solution)/shard_map/ppermute | solution.py:70
  120.7 14.8 %collective-permute-start.15 = (bf16[160,2048]{1,0:T(8,128)(2,1)}, bf16[160,2048]{1,0:T(8,128)(2,1)S(1)}, u32[]{:S(2)}, u32[]{:S(2)}) collective-permute-start(bf16[160,2048]{1,0:T(8,128)(2,1)} %get-tuple-element.120.n0.refs_0_.refs_5_), channel_id=1, source_target_pairs={{0,6},{2,0},{4,2},{6,4},{1,7},{3,1},{5,3},{7,5},{8,14},{10,8},{12,... | collective-permute-start | bytes 1966088 | tf_op jit(solution)/shard_map/ppermute | solution.py:71
  179.9 12.3 %collective-permute-start.20 = (bf16[80,2048]{1,0:T(8,128)(2,1)}, bf16[80,2048]{1,0:T(8,128)(2,1)S(1)}, u32[]{:S(2)}, u32[]{:S(2)}) collective-permute-start(bf16[80,2048]{1,0:T(8,128)(2,1)} %get-tuple-element.131), channel_id=1, source_target_pairs={{0,2},{2,4},{4,6},{6,0},{1,3},{3,5},{5,7},{7,1},{8,10},{10,12},{12... | collective-permute-start | bytes 983048 | tf_op jit(solution)/shard_map/ppermute | solution.py:86
  181.1 11.1 %collective-permute-start.21 = (bf16[80,2048]{1,0:T(8,128)(2,1)}, bf16[80,2048]{1,0:T(8,128)(2,1)S(1)}, u32[]{:S(2)}, u32[]{:S(2)}) collective-permute-start(bf16[80,2048]{1,0:T(8,128)(2,1)} %get-tuple-element.133), channel_id=1, source_target_pairs={{0,6},{2,0},{4,2},{6,4},{1,7},{3,1},{5,3},{7,5},{8,14},{10,8},{12,... | collective-permute-start | bytes 983048 | tf_op jit(solution)/shard_map/ppermute | solution.py:87
  195.3 17.2 %collective-permute-start.22 = (bf16[160,2048]{1,0:T(8,128)(2,1)}, bf16[160,2048]{1,0:T(8,128)(2,1)S(1)}, u32[]{:S(2)}, u32[]{:S(2)}) collective-permute-start(bf16[160,2048]{1,0:T(8,128)(2,1)} %get-tuple-element.134), channel_id=1, source_target_pairs={{0,2},{2,4},{4,6},{6,0},{1,3},{3,5},{5,7},{7,1},{8,10},{10,12},{12... | collective-permute-start | bytes 1966088 | tf_op jit(solution)/shard_map/ppermute | solution.py:108
  195.3 17.3 %collective-permute-start.23 = (bf16[160,2048]{1,0:T(8,128)(2,1)}, bf16[160,2048]{1,0:T(8,128)(2,1)S(1)}, u32[]{:S(2)}, u32[]{:S(2)}) collective-permute-start(bf16[160,2048]{1,0:T(8,128)(2,1)} %get-tuple-element.135), channel_id=1, source_target_pairs={{0,6},{2,0},{4,2},{6,4},{1,7},{3,1},{5,3},{7,5},{8,14},{10,8},{12,... | collective-permute-start | bytes 1966088 | tf_op jit(solution)/shard_map/ppermute | solution.py:108
  213.7 217.0 %all-gather.8.cloned.1.call-start = ((), (), s32[]{:S(2)}) async-start(), calls=%async_computation.4 | async-start | bytes 9191424 | tf_op jit(solution)/shard_map/all_gather | solution.py:1006
  217.8 12.2 %collective-permute-start.24 = (bf16[160,2048]{1,0:T(8,128)(2,1)}, bf16[160,2048]{1,0:T(8,128)(2,1)S(1)}, u32[]{:S(2)}, u32[]{:S(2)}) collective-permute-start(bf16[160,2048]{1,0:T(8,128)(2,1)} %get-tuple-element.140.b0.refs_10_), channel_id=1, source_target_pairs={{0,2},{2,4},{4,6},{6,0},{1,3},{3,5},{5,7},{7,1},{8,10},{10,12},{12... | collective-permute-start | bytes 1966088 | tf_op jit(solution)/shard_map/ppermute | solution.py:70
  217.8 12.1 %collective-permute-start.25 = (bf16[160,2048]{1,0:T(8,128)(2,1)}, bf16[160,2048]{1,0:T(8,128)(2,1)S(1)}, u32[]{:S(2)}, u32[]{:S(2)}) collective-permute-start(bf16[160,2048]{1,0:T(8,128)(2,1)} %get-tuple-element.140.b0.refs_10_), channel_id=1, source_target_pairs={{0,6},{2,0},{4,2},{6,4},{1,7},{3,1},{5,3},{7,5},{8,14},{10,8},{12,... | collective-permute-start | bytes 1966088 | tf_op jit(solution)/shard_map/ppermute | solution.py:71
  230.0 13.4 %collective-permute-start.26 = (bf16[80,2048]{1,0:T(8,128)(2,1)S(1)}, bf16[80,2048]{1,0:T(8,128)(2,1)S(1)}, u32[]{:S(2)}, u32[]{:S(2)}) collective-permute-start(bf16[80,2048]{1,0:T(8,128)(2,1)S(1)} %slice.41), channel_id=1, source_target_pairs={{0,2},{2,4},{4,6},{6,0},{1,3},{3,5},{5,7},{7,1},{8,10},{10,12},{12... | collective-permute-start | bytes 983048 | tf_op jit(solution)/shard_map/ppermute | solution.py:74
  230.1 13.3 %collective-permute-start.27 = (bf16[80,2048]{1,0:T(8,128)(2,1)S(1)}, bf16[80,2048]{1,0:T(8,128)(2,1)S(1)}, u32[]{:S(2)}, u32[]{:S(2)}) collective-permute-start(bf16[80,2048]{1,0:T(8,128)(2,1)S(1)} %slice.42), channel_id=1, source_target_pairs={{0,6},{2,0},{4,2},{6,4},{1,7},{3,1},{5,3},{7,5},{8,14},{10,8},{12,... | collective-permute-start | bytes 983048 | tf_op jit(solution)/shard_map/ppermute | solution.py:75
  243.4 26.8 %collective-permute-start.28 = (bf16[160,2048]{1,0:T(8,128)(2,1)}, bf16[160,2048]{1,0:T(8,128)(2,1)S(1)}, u32[]{:S(2)}, u32[]{:S(2)}) collective-permute-start(bf16[160,2048]{1,0:T(8,128)(2,1)} %get-tuple-element.143), channel_id=1, source_target_pairs={{0,2},{2,4},{4,6},{6,0},{1,3},{3,5},{5,7},{7,1},{8,10},{10,12},{12... | collective-permute-start | bytes 1966088 | tf_op jit(solution)/shard_map/ppermute | solution.py:977
  243.5 26.7 %collective-permute-start.29 = (bf16[160,2048]{1,0:T(8,128)(2,1)}, bf16[160,2048]{1,0:T(8,128)(2,1)S(1)}, u32[]{:S(2)}, u32[]{:S(2)}) collective-permute-start(bf16[160,2048]{1,0:T(8,128)(2,1)} %get-tuple-element.145), channel_id=1, source_target_pairs={{0,6},{2,0},{4,2},{6,4},{1,7},{3,1},{5,3},{7,5},{8,14},{10,8},{12,... | collective-permute-start | bytes 1966088 | tf_op jit(solution)/shard_map/ppermute | solution.py:977
  267.0 12.8 %collective-permute-start.30 = (bf16[640,128]{1,0:T(8,128)(2,1)}, bf16[640,128]{1,0:T(8,128)(2,1)S(1)}, u32[]{:S(2)}, u32[]{:S(2)}) collective-permute-start(bf16[640,128]{1,0:T(8,128)(2,1)} %get-tuple-element.153), channel_id=1, source_target_pairs={{0,1},{1,0},{2,3},{3,2},{4,5},{5,4},{6,7},{7,6},{8,9},{9,8},{10,11... | collective-permute-start | bytes 491528 | tf_op jit(solution)/shard_map/ppermute | solution.py:982
  279.8 18.6 %collective-permute-start.31 = (bf16[4,2,1024,128]{3,2,1,0:T(8,128)(2,1)}, bf16[4,2,1024,128]{3,2,1,0:T(8,128)(2,1)S(1)}, u32[]{:S(2)}, u32[]{:S(2)}) collective-permute-start(bf16[4,2,1024,128]{3,2,1,0:T(8,128)(2,1)} %get-tuple-element.155), channel_id=1, source_target_pairs={{0,8},{8,0},{1,9},{9,1},{2,10},{10,2},{3,11},{11,3},{4,12},{12,4},... | collective-permute-start | bytes 6291464 | tf_op jit(solution)/shard_map/ppermute | solution.py:806
  303.8 20.6 %collective-permute-start.33 = (bf16[2,1168,128]{2,1,0:T(8,128)(2,1)}, bf16[2,1168,128]{2,1,0:T(8,128)(2,1)S(1)}, u32[]{:S(2)}, u32[]{:S(2)}) collective-permute-start(bf16[2,1168,128]{2,1,0:T(8,128)(2,1)} %get-tuple-element.161), channel_id=1, source_target_pairs={{0,64},{32,96},{64,0},{96,32},{1,65},{33,97},{65,1},{97,33},{2,66}... | collective-permute-start | bytes 1794056 | tf_op jit(solution)/shard_map/ppermute | solution.py:810
  306.6 30.7 %collective-permute-start.34 = (bf16[2,1168,128]{2,1,0:T(8,128)(2,1)}, bf16[2,1168,128]{2,1,0:T(8,128)(2,1)S(1)}, u32[]{:S(2)}, u32[]{:S(2)}) collective-permute-start(bf16[2,1168,128]{2,1,0:T(8,128)(2,1)} %get-tuple-element.162), channel_id=1, source_target_pairs={{0,32},{32,64},{64,96},{96,0},{1,33},{33,65},{65,97},{97,1},{2,34}... | collective-permute-start | bytes 1794056 | tf_op jit(solution)/shard_map/ppermute | solution.py:810
  307.1 30.2 %collective-permute-start.35 = (bf16[2,1168,128]{2,1,0:T(8,128)(2,1)}, bf16[2,1168,128]{2,1,0:T(8,128)(2,1)S(1)}, u32[]{:S(2)}, u32[]{:S(2)}) collective-permute-start(bf16[2,1168,128]{2,1,0:T(8,128)(2,1)} %get-tuple-element.163), channel_id=1, source_target_pairs={{0,96},{32,0},{64,32},{96,64},{1,97},{33,1},{65,33},{97,65},{2,98}... | collective-permute-start | bytes 1794056 | tf_op jit(solution)/shard_map/ppermute | solution.py:810
  351.5 42.0 %collective-permute-start.36 = (bf16[160,2048]{1,0:T(8,128)(2,1)}, bf16[160,2048]{1,0:T(8,128)(2,1)}, u32[]{:S(2)}, u32[]{:S(2)}) collective-permute-start(bf16[160,2048]{1,0:T(8,128)(2,1)} %get-tuple-element.165), channel_id=1, source_target_pairs={{0,4},{2,6},{4,0},{6,2},{1,5},{3,7},{5,1},{7,3},{8,12},{10,14},{12... | collective-permute-start | bytes 1966088 | tf_op jit(solution)/shard_map/ppermute | solution.py:993
  354.3 22.7 %collective-permute-start.37 = (bf16[80,2048]{1,0:T(8,128)(2,1)S(1)}, bf16[80,2048]{1,0:T(8,128)(2,1)S(1)}, u32[]{:S(2)}, u32[]{:S(2)}) collective-permute-start(bf16[80,2048]{1,0:T(8,128)(2,1)S(1)} %copy-done.42), channel_id=1, source_target_pairs={{0,2},{2,4},{4,6},{6,0},{1,3},{3,5},{5,7},{7,1},{8,10},{10,12},{12... | collective-permute-start | bytes 983048 | tf_op jit(solution)/shard_map/ppermute | solution.py:86
  354.6 24.8 %collective-permute-start.38 = (bf16[80,2048]{1,0:T(8,128)(2,1)}, bf16[80,2048]{1,0:T(8,128)(2,1)}, u32[]{:S(2)}, u32[]{:S(2)}) collective-permute-start(bf16[80,2048]{1,0:T(8,128)(2,1)} %get-tuple-element.175), channel_id=1, source_target_pairs={{0,6},{2,0},{4,2},{6,4},{1,7},{3,1},{5,3},{7,5},{8,14},{10,8},{12,... | collective-permute-start | bytes 983048 | tf_op jit(solution)/shard_map/ppermute | solution.py:87
  357.0 24.7 %collective-permute-start.41 = (bf16[1168,128]{1,0:T(8,128)(2,1)}, bf16[1168,128]{1,0:T(8,128)(2,1)}, u32[]{:S(2)}, u32[]{:S(2)}) collective-permute-start(bf16[1168,128]{1,0:T(8,128)(2,1)} %get-tuple-element.179.a), channel_id=1, source_target_pairs={{0,16},{16,0},{1,17},{17,1},{2,18},{18,2},{3,19},{19,3},{4,20},{20... | collective-permute-start | bytes 897032 | tf_op jit(solution)/shard_map/ppermute | solution.py:820
  358.0 26.4 %collective-permute-start.42 = (bf16[1168,128]{1,0:T(8,128)(2,1)}, bf16[1168,128]{1,0:T(8,128)(2,1)}, u32[]{:S(2)}, u32[]{:S(2)}) collective-permute-start(bf16[1168,128]{1,0:T(8,128)(2,1)} %get-tuple-element.180), channel_id=1, source_target_pairs={{0,1},{1,0},{2,3},{3,2},{4,5},{5,4},{6,7},{7,6},{8,9},{9,8},{10,11... | collective-permute-start | bytes 897032 | tf_op jit(solution)/shard_map/ppermute | solution.py:821
  377.1 11.7 %collective-permute-start.43 = (bf16[1168,128]{1,0:T(8,128)(2,1)}, bf16[1168,128]{1,0:T(8,128)(2,1)}, u32[]{:S(2)}, u32[]{:S(2)}) collective-permute-start(bf16[1168,128]{1,0:T(8,128)(2,1)} %get-tuple-element.180), channel_id=1, source_target_pairs={{0,17},{1,16},{16,1},{17,0},{2,19},{3,18},{18,3},{19,2},{4,21},{5,... | collective-permute-start | bytes 897032 | tf_op jit(solution)/shard_map/ppermute | solution.py:822
  381.7 17.1 %collective-permute-start.39 = (bf16[160,2048]{1,0:T(8,128)(2,1)}, bf16[160,2048]{1,0:T(8,128)(2,1)}, u32[]{:S(2)}, u32[]{:S(2)}) collective-permute-start(bf16[160,2048]{1,0:T(8,128)(2,1)} %get-tuple-element.176), channel_id=1, source_target_pairs={{0,2},{2,4},{4,6},{6,0},{1,3},{3,5},{5,7},{7,1},{8,10},{10,12},{12... | collective-permute-start | bytes 1966088 | tf_op jit(solution)/shard_map/ppermute | solution.py:108
  381.7 18.7 %collective-permute-start.40 = (bf16[160,2048]{1,0:T(8,128)(2,1)}, bf16[160,2048]{1,0:T(8,128)(2,1)}, u32[]{:S(2)}, u32[]{:S(2)}) collective-permute-start(bf16[160,2048]{1,0:T(8,128)(2,1)} %get-tuple-element.177), channel_id=1, source_target_pairs={{0,6},{2,0},{4,2},{6,4},{1,7},{3,1},{5,3},{7,5},{8,14},{10,8},{12,... | collective-permute-start | bytes 1966088 | tf_op jit(solution)/shard_map/ppermute | solution.py:108
  391.0 13.3 %collective-permute-start.44 = (bf16[1168,128]{1,0:T(8,128)(2,1)}, bf16[1168,128]{1,0:T(8,128)(2,1)}, u32[]{:S(2)}, u32[]{:S(2)}) collective-permute-start(bf16[1168,128]{1,0:T(8,128)(2,1)} %sum_z.1.refs_0_), channel_id=1, source_target_pairs={{0,32},{32,64},{64,96},{96,0},{1,33},{33,65},{65,97},{97,1},{2,34}... | collective-permute-start | bytes 897032 | tf_op jit(solution)/shard_map/ppermute | solution.py:827
  391.0 28.6 %collective-permute-start.45 = (bf16[1168,128]{1,0:T(8,128)(2,1)}, bf16[1168,128]{1,0:T(8,128)(2,1)}, u32[]{:S(2)}, u32[]{:S(2)}) collective-permute-start(bf16[1168,128]{1,0:T(8,128)(2,1)} %sum_z.1.refs_0_), channel_id=1, source_target_pairs={{0,64},{32,96},{64,0},{96,32},{1,65},{33,97},{65,1},{97,33},{2,66}... | collective-permute-start | bytes 897032 | tf_op jit(solution)/shard_map/ppermute | solution.py:827
  393.4 26.1 %collective-permute-start.46 = (bf16[1168,128]{1,0:T(8,128)(2,1)}, bf16[1168,128]{1,0:T(8,128)(2,1)}, u32[]{:S(2)}, u32[]{:S(2)}) collective-permute-start(bf16[1168,128]{1,0:T(8,128)(2,1)} %sum_z.1.refs_0_), channel_id=1, source_target_pairs={{0,96},{32,0},{64,32},{96,64},{1,97},{33,1},{65,33},{97,65},{2,98}... | collective-permute-start | bytes 897032 | tf_op jit(solution)/shard_map/ppermute | solution.py:827
  398.8 23.3 %collective-permute-start.47 = (bf16[1168,128]{1,0:T(8,128)(2,1)S(1)}, bf16[1168,128]{1,0:T(8,128)(2,1)S(1)}, u32[]{:S(2)}, u32[]{:S(2)}) collective-permute-start(bf16[1168,128]{1,0:T(8,128)(2,1)S(1)} %copy-done.10), channel_id=1, source_target_pairs={{0,8},{8,0},{1,9},{9,1},{2,10},{10,2},{3,11},{11,3},{4,12},{12,4},... | collective-permute-start | bytes 897032 | tf_op jit(solution)/shard_map/ppermute | solution.py:829
  429.2 11.2 %collective-permute-start.53 = (f32[2,2048]{1,0:T(2,128)}, f32[2,2048]{1,0:T(2,128)S(1)}, u32[]{:S(2)}, u32[]{:S(2)}) collective-permute-start(f32[2,2048]{1,0:T(2,128)} %get-tuple-element.184), channel_id=1, source_target_pairs={{0,6},{2,0},{4,2},{6,4},{1,7},{3,1},{5,3},{7,5},{8,14},{10,8},{12,... | collective-permute-start | bytes 49160 | tf_op jit(solution)/shard_map/ppermute | solution.py:991
  429.2 11.2 %collective-permute-start.52 = (f32[2,2048]{1,0:T(2,128)}, f32[2,2048]{1,0:T(2,128)S(1)}, u32[]{:S(2)}, u32[]{:S(2)}) collective-permute-start(f32[2,2048]{1,0:T(2,128)} %get-tuple-element.184), channel_id=1, source_target_pairs={{0,4},{2,6},{4,0},{6,2},{1,5},{3,7},{5,1},{7,3},{8,12},{10,14},{12... | collective-permute-start | bytes 49160 | tf_op jit(solution)/shard_map/ppermute | solution.py:991
  429.3 11.1 %collective-permute-start.51 = (f32[2,2048]{1,0:T(2,128)}, f32[2,2048]{1,0:T(2,128)S(1)}, u32[]{:S(2)}, u32[]{:S(2)}) collective-permute-start(f32[2,2048]{1,0:T(2,128)} %get-tuple-element.184), channel_id=1, source_target_pairs={{0,2},{2,4},{4,6},{6,0},{1,3},{3,5},{5,7},{7,1},{8,10},{10,12},{12... | collective-permute-start | bytes 49160 | tf_op jit(solution)/shard_map/ppermute | solution.py:991
  (56 other events, 342.5 us)
Sparse Core Ops, SparseCore 0:
  44.4 35.0 all-gather.3
  87.0 39.9 all-gather.5
  212.7 138.6 reduce-scatter.1
  353.0 70.9 all-gather.7

commit v15 on v13

--- a/solution.py
+++ b/solution.py
@@ -810,22 +810,20 @@
     got = [lax.ppermute(g[s], "y", shift(4, s)) for s in (2, 1, 3)]
     part = sds((TAIL, 128))
     own, other = small_call(sum_y_body, (part,) * 2, idx, g[0], *got, name="sum_y")
-    p0, q1, q3 = relay([tie(p, own) for p in parts])
     cross = [(2 * a + b, 2 * (1 - a) + (1 - b)) for a in range(2) for b in range(2)]
     g = small_call(
         sum_z_body,
         part,
         idx,
-        tie(own, q1, q3),
+        own,
         lax.ppermute(own, "zl", shift(2, 1)),
         lax.ppermute(other, "zh", shift(2, 1)),
         lax.ppermute(other, ("zl", "zh"), cross),
         name="sum_z",
     )
-    d_one = last_step(p0, q1, q3)
-    input_grad = finish(d_one)
-    mine = [tie(g, input_grad)] + [lax.ppermute(g, "y", shift(4, s)) for s in (1, 2, 3)]
-    theirs = [lax.ppermute(v, "core", shift(2, 1)) for v in [g] + mine[1:]]
+    input_grad = finish(last_step(*relay([tie(p, g) for p in parts])))
+    mine = [g] + [lax.ppermute(g, "y", shift(4, s)) for s in (1, 2, 3)]
+    theirs = [lax.ppermute(v, "core", shift(2, 1)) for v in mine]
     shapes = (sds((DH, QW), F32), sds((AW // 2, D), F32), sds((2, D), F32))
     return own, input_grad, small_call(unpack_tail_body, shapes, idx, *mine, *theirs, name="unpack_tail")
 

time: 451 us -> 457 us (1.013)
  waiting for transfers between devices: 136 us -> 147 us
    ppermute x3, waiting for transfers between devices: 13.6 us -> 20.5 us  [last_step(): lax.ppermute(q1, 'x', shift(4, 1))]
    ppermute x7, starting transfers between devices: 17.8 us -> 12.7 us  [the longest x4 7.4 us: sum_tail(): theirs = [lax.ppermute(v, 'core', shift(2, 1)) for v in mine]]
    unnamed x90 -> x88, local copies, waits for them, and re-layouts: 13.7 us -> 11.8 us
  transfers between devices with their start and end apart: 58 -> 58, of which waited for: 19 -> 21; matrix products, arithmetic and copies ran while one was open for 3% -> 3% of each run, Pallas kernels for 29% -> 29%
where the time goes in v15:
time: 457 us; the launch traced here: 449 us
  Pallas kernels  168 us (37%)
  waiting for transfers between devices  147 us (32%)
  starting transfers between devices  89.5 us (20%)
  local copies, waits for them, and re-layouts  20.1 us (4%)
  between operations  14.7 us (3%)
  other arithmetic  9.45 us (2%)
    ppermute x3, waiting for transfers between devices, sum_tail(): got = [lax.ppermute(g[s], 'y', shift(4, s)) for s in (2, 1, 3)]  28 us
    ppermute x3, waiting for transfers between devices, gather_x(): from_prev = lax.ppermute(v, 'x', shift(4, 1))  27.1 us
    pallas_call x1, Pallas kernels, ffn(): pl.pallas_call(ffn_body, grid=(TILES,), out_shape=(sds((ROWS, FF4)),) * 3...  20.8 us
    pallas_call x1, Pallas kernels, attend_back(): pl.pallas_call(attend_back_body, grid=(1,), out_shape=(sds((4, BLK, AW)),...  20.6 us
    ppermute x3, waiting for transfers between devices, last_step(): lax.ppermute(q1, 'x', shift(4, 1))  20.5 us
    ppermute x3, waiting for transfers between devices, sum_tail(): mine = [g] + [lax.ppermute(g, 'y', shift(4, s)) for s in (1, 2, 3)]  18.5 us
    pallas_call x1, Pallas kernels, ffn_back(): pl.pallas_call(ffn_back_body, grid_spec=pltpu.PrefetchScalarGridSpec(num_...  15.4 us
    pallas_call x1, Pallas kernels, gate_up_grads(): pl.pallas_call(gate_up_grads_body, grid=(16 // QS,), out_shape=sds((2, 16...  14.6 us
  transfers between devices with their start and end apart: 58, of which 21 were waited for; matrix products, arithmetic and copies ran while one was open for 3% of the time, Pallas kernels for 29%

profile of v15, /device:TPU:1, one launch (start us, length us, event | category | flops | bytes accessed | tf_op | source)
XLA Modules:
  0.0 448.9 jit_solution(9156937567716226866)
XLA Ops:
  10.0 3.4 collective-permute-start
  14.3 3.6 collective-permute-start.4
  24.8 5.1 %collective-permute-done.1.n3.refs_4_.refs_9_ = bf16[160,2048]{1,0:T(8,128)(2,1)} collective-permute-done((bf16[160,2048]{1,0:T(8,128)(2,1)S(1)}, bf16[160,2048]{1,0:T(8,128)(2,1)}, u32[]{:S(2)}, u32[]{:S(2)}) %collective-permute-start.1) | collective-permute-done | bytes 655392 | tf_op jit(solution)/shard_map/ppermute | solution.py:70
  31.7 2.7 collective-permute-start.3
  34.4 9.0 %collective-permute-done.5 = bf16[128,2048]{1,0:T(8,128)(2,1)S(1)} collective-permute-done((bf16[128,2048]{1,0:T(8,128)(2,1)}, bf16[128,2048]{1,0:T(8,128)(2,1)S(1)}, u32[]{:S(2)}, u32[]{:S(2)}) %collective-permute-start.5) | collective-permute-done | bytes 524320 | tf_op jit(solution)/shard_map/ppermute | solution.py:921
  51.4 6.7 %qkv_forward.1 = (bf16[4,1280,128]{2,1,0:T(8,128)(2,1)}, bf16[640,128]{1,0:T(8,128)(2,1)}) custom-call(s32[4]{0:T(128)} %pad_add_fusion.idx, bf16[160,2048]{1,0:T(8,128)(2,1)} %copy-done.4, bf16[160,2048]{1,0:T(8,128)(2,1)} %copy-done.7, bf16[80,2048]{1,0:T(8,128)(2,1)} %copy-done.22, bf16[80,2048]{1,0:T(8,128)(2,1)} %copy-done.23, ...), custom_call_target="tpu_custom_call" | custom-call | flops 1677721600 | bytes 7000000 | tf_op jit(solution)/shard_map/qkv_forward/pallas_call | solution.py:184
  58.2 3.0 collective-permute-start.7
  65.8 8.6 %attend.1 = (bf16[4,160,512]{2,1,0:T(8,128)(2,1)}, bf16[4,1280,128]{2,1,0:T(8,128)(2,1)}) custom-call(s32[4]{0:T(128)} %pad_add_fusion.idx, bf16[4,1280,128]{2,1,0:T(8,128)(2,1)} %get-tuple-element.102.q, bf16[640,128]{1,0:T(8,128)(2,1)} %get-tuple-element.103.kv_own, bf16[640,128]{1,0:T(8,128)(2,1)} %copy-done.43, s32[1,1280]{1,0:T(1,128)} %reshape_tile.3.first), custom_call_target="tpu_custom_call" | custom-call | flops 12000000000 | bytes 3000000 | tf_op jit(solution)/shard_map/attend/pallas_call | solution.py:277
  74.4 3.5 collective-permute-done.8.c1.refs_1_
  78.0 3.7 collective-permute-done.10.c3.refs_3_
  81.7 4.2 out_project.1
  89.6 7.2 %collective-permute-done.11.got_a = bf16[80,2048]{1,0:T(8,128)(2,1)S(1)} collective-permute-done((bf16[80,2048]{1,0:T(8,128)(2,1)}, bf16[80,2048]{1,0:T(8,128)(2,1)S(1)}, u32[]{:S(2)}, u32[]{:S(2)}) %collective-permute-start.11) | collective-permute-done | bytes 327712 | tf_op jit(solution)/shard_map/ppermute | solution.py:86
  99.9 2.7 collective-permute-start.14
  102.6 13.6 %collective-permute-done.13.b = bf16[160,2048]{1,0:T(8,128)(2,1)S(1)} collective-permute-done((bf16[160,2048]{1,0:T(8,128)(2,1)}, bf16[160,2048]{1,0:T(8,128)(2,1)S(1)}, u32[]{:S(2)}, u32[]{:S(2)}) %collective-permute-start.13) | collective-permute-done | bytes 655392 | tf_op jit(solution)/shard_map/ppermute | solution.py:108
  117.2 2.9 norm_two.1
  122.8 12.6 %collective-permute-done.16.n3.refs_4_.refs_9_ = bf16[160,2048]{1,0:T(8,128)(2,1)S(1)} collective-permute-done((bf16[160,2048]{1,0:T(8,128)(2,1)}, bf16[160,2048]{1,0:T(8,128)(2,1)S(1)}, u32[]{:S(2)}, u32[]{:S(2)}) %collective-permute-start.16) | collective-permute-done | bytes 655392 | tf_op jit(solution)/shard_map/ppermute | solution.py:70
  135.6 3.2 collective-permute-start.18
  138.8 3.9 collective-permute-done.17.n2a.refs_2_.refs_7_
  143.5 20.8 %ffn.1 = (bf16[640,1408]{1,0:T(8,128)(2,1)}, bf16[640,1408]{1,0:T(8,128)(2,1)}, bf16[640,1408]{1,0:T(8,128)(2,1)}) custom-call(s32[4]{0:T(128)} %pad_add_fusion.idx, bf16[160,2048]{1,0:T(8,128)(2,1)} %get-tuple-element.116.n0.refs_0_.refs_5_, bf16[160,2048]{1,0:T(8,128)(2,1)} %copy-done.2, bf16[80,2048]{1,0:T(8,128)(2,1)} %copy-done.8, ...), custom_call_target="tpu_custom_call" | custom-call | flops 11072962560 | bytes 34000000 | tf_op jit(solution)/shard_map/ffn/pallas_call | solution.py:523
  164.3 15.4 %ffn_back.1 = (bf16[160,2048]{1,0:T(8,128)(2,1)}, bf16[160,2048]{1,0:T(8,128)(2,1)}, bf16[80,2048]{1,0:T(8,128)(2,1)}, bf16[80,2048]{1,0:T(8,128)(2,1)}, bf16[160,2048]{1,0:T(8,128)(2,1)}) custom-call(s32[4]{0:T(128)} %pad_add_fusion.idx, bf16[640,1408]{1,0:T(8,128)(2,1)} %get-tuple-element.177.dgate.refs_10_, ...), custom_call_target="tpu_custom_call" | custom-call | flops 7381975040 | bytes 18000000 | tf_op jit(solution)/shard_map/ffn_back/pallas_call | solution.py:589
  183.0 9.1 %down_grads.1.refs_12_ = bf16[2,16,2112,128]{3,2,1,0:T(8,128)(2,1)} custom-call(bf16[160,2048]{1,0:T(8,128)(2,1)} %refs_0_.1, bf16[160,2048]{1,0:T(8,128)(2,1)} %collective-permute-done.8.c1.refs_1_, bf16[160,2048]{1,0:T(8,128)(2,1)} %collective-permute-done.9.c2.refs_2_, bf16[160,2048]{1,0:T(8,128)(2,1)} %collective-permute-done.10.c3.refs_3_, ...), custom_call_target="tpu_custom_call" | custom-call | flops 3690987520 | bytes 10000000 | tf_op jit(solution)/shard_map/down_grads/pallas_call | solution.py:656
  197.9 14.6 %gate_up_grads.1 = bf16[2,16,2112,128]{3,2,1,0:T(8,128)(2,1)} custom-call(bf16[160,2048]{1,0:T(8,128)(2,1)} %get-tuple-element.116.n0.refs_0_.refs_5_, bf16[160,2048]{1,0:T(8,128)(2,1)} %copy-done.2, bf16[80,2048]{1,0:T(8,128)(2,1)} %copy-done.8, bf16[80,2048]{1,0:T(8,128)(2,1)} %copy-done.9, ...), custom_call_target="tpu_custom_call", output_to_operand_aliasing={{}: (12, {})} | custom-call | flops 7381975040 | bytes 20000000 | tf_op jit(solution)/shard_map/gate_up_grads/pallas_call | solution.py:625
  213.6 4.1 norm_back_two.1
  220.4 9.4 %collective-permute-done.24.b3.refs_14_ = bf16[160,2048]{1,0:T(8,128)(2,1)S(1)} collective-permute-done((bf16[160,2048]{1,0:T(8,128)(2,1)}, bf16[160,2048]{1,0:T(8,128)(2,1)S(1)}, u32[]{:S(2)}, u32[]{:S(2)}) %collective-permute-start.24) | collective-permute-done | bytes 655392 | tf_op jit(solution)/shard_map/ppermute | solution.py:70
  230.0 2.7 collective-permute-start.27
  232.7 10.5 %down_project.1 = (bf16[160,2048]{1,0:T(8,128)(2,1)}, bf16[160,2048]{1,0:T(8,128)(2,1)}, bf16[160,2048]{1,0:T(8,128)(2,1)}, bf16[160,2048]{1,0:T(8,128)(2,1)}) custom-call(s32[4]{0:T(128)} %pad_add_fusion.idx, bf16[640,1408]{1,0:T(8,128)(2,1)} %get-tuple-element.178.hid.refs_4_, bf16[704,2048]{1,0:T(8,128)(2,1)} %w0.9, bf16[8,128,2048]{2,1,0:T(8,128)(2,1)} %bitcast.17), custom_call_target="tpu_custom_call" | custom-call | flops 3690987520 | bytes 11000000 | tf_op jit(solution)/shard_map/down_project/pallas_call | solution.py:559
  243.4 2.8 collective-permute-start.29
  246.2 20.6 %attend_back.1 = (bf16[4,160,512]{2,1,0:T(8,128)(2,1)}, f32[640,128]{1,0:T(8,128)}, bf16[640,128]{1,0:T(8,128)(2,1)}) custom-call(s32[4]{0:T(128)} %pad_add_fusion.idx, bf16[4,1280,128]{2,1,0:T(8,128)(2,1)} %get-tuple-element.143.qx, bf16[640,128]{1,0:T(8,128)(2,1)} %get-tuple-element.103.kv_own, bf16[640,128]{1,0:T(8,128)(2,1)} %copy-done.43, ...), custom_call_target="tpu_custom_call" | custom-call | flops 30000001024 | bytes 8000000 | tf_op jit(solution)/shard_map/attend_back/pallas_call | solution.py:388
  266.8 3.3 collective-permute-start.30
  270.1 9.5 %attn_grads.1 = (bf16[4,2,1024,128]{3,2,1,0:T(8,128)(2,1)}, bf16[4,2,1024,128]{3,2,1,0:T(8,128)(2,1)}) custom-call(s32[4]{0:T(128)} %pad_add_fusion.idx, bf16[160,2048]{1,0:T(8,128)(2,1)} %copy-done.4, bf16[160,2048]{1,0:T(8,128)(2,1)} %copy-done.7, bf16[80,2048]{1,0:T(8,128)(2,1)} %copy-done.22, bf16[80,2048]{1,0:T(8,128)(2,1)} %copy-done.23, ...), custom_call_target="tpu_custom_call" | custom-call | flops 2684354560 | bytes 10000000 | tf_op jit(solution)/shard_map/attn_grads/pallas_call | solution.py:735
  279.7 9.2 %collective-permute-start.31 = (bf16[4,2,1024,128]{3,2,1,0:T(8,128)(2,1)}, bf16[4,2,1024,128]{3,2,1,0:T(8,128)(2,1)S(1)}, u32[]{:S(2)}, u32[]{:S(2)}) collective-permute-start(bf16[4,2,1024,128]{3,2,1,0:T(8,128)(2,1)} %get-tuple-element.151), channel_id=1, source_target_pairs={{0,8},{8,0},{1,9},{9,1},{2,10},{10,2},{3,11},{11,3},{4,12},{12,4},... | collective-permute-start | bytes 6291464 | tf_op jit(solution)/shard_map/ppermute | solution.py:806
  288.8 7.5 %qkv_back.1 = (bf16[4,2,144,128]{3,2,1,0:T(8,128)(2,1)}, bf16[4,2,144,128]{3,2,1,0:T(8,128)(2,1)}, bf16[160,2048]{1,0:T(8,128)(2,1)}, bf16[160,2048]{1,0:T(8,128...) custom-call(s32[4]{0:T(128)} %pad_add_fusion.idx, ...), custom_call_target="tpu_custom_call" | custom-call | flops 1677721600 | bytes 13000000 | tf_op jit(solution)/shard_map/qkv_back/pallas_call | solution.py:446
  299.6 4.0 sum_core.1
  303.6 2.9 collective-permute-start.33
  309.1 15.3 %collective-permute-done.33.b = bf16[2,1168,128]{2,1,0:T(8,128)(2,1)S(1)} collective-permute-done((bf16[2,1168,128]{2,1,0:T(8,128)(2,1)}, bf16[2,1168,128]{2,1,0:T(8,128)(2,1)S(1)}, u32[]{:S(2)}, u32[]{:S(2)}) %collective-permute-start.33) | collective-permute-done | bytes 598048 | tf_op jit(solution)/shard_map/ppermute | solution.py:810
  324.4 12.7 %collective-permute-done.34.c = bf16[2,1168,128]{2,1,0:T(8,128)(2,1)S(1)} collective-permute-done((bf16[2,1168,128]{2,1,0:T(8,128)(2,1)}, bf16[2,1168,128]{2,1,0:T(8,128)(2,1)S(1)}, u32[]{:S(2)}, u32[]{:S(2)}) %collective-permute-start.34) | collective-permute-done | bytes 598048 | tf_op jit(solution)/shard_map/ppermute | solution.py:810
  338.1 2.7 sum_y.1
  340.8 10.8 %reduce-scatter.2.cloned.1.call-done = bf16[1,2112,128]{2,1,0:T(8,128)(2,1)} async-done(((bf16[32,2112,128]{2,1,0:T(8,128)(2,1)}), bf16[1,2112,128]{2,1,0:T(8,128)(2,1)}) %reduce-scatter.2.cloned.1.call-update) | async-done | bytes 540688 | tf_op jit(solution)/shard_map/reduce_scatter | solution.py:961
  355.6 3.2 collective-permute-done.37.b
  358.7 8.5 %collective-permute-done.38.c = bf16[1168,128]{1,0:T(8,128)(2,1)S(1)} collective-permute-done((bf16[1168,128]{1,0:T(8,128)(2,1)}, bf16[1168,128]{1,0:T(8,128)(2,1)S(1)}, u32[]{:S(2)}, u32[]{:S(2)}) %collective-permute-start.38) | collective-permute-done | bytes 299040 | tf_op jit(solution)/shard_map/ppermute | solution.py:820
  379.1 4.6 %collective-permute-done.44.refs_1_ = bf16[1168,128]{1,0:T(8,128)(2,1)} collective-permute-done((bf16[1168,128]{1,0:T(8,128)(2,1)}, bf16[1168,128]{1,0:T(8,128)(2,1)}, u32[]{:S(2)}, u32[]{:S(2)}) %collective-permute-start.44) | collective-permute-done | bytes 299040 | tf_op jit(solution)/shard_map/ppermute | solution.py:825
  386.2 13.9 %collective-permute-done.45.refs_2_ = bf16[1168,128]{1,0:T(8,128)(2,1)} collective-permute-done((bf16[1168,128]{1,0:T(8,128)(2,1)}, bf16[1168,128]{1,0:T(8,128)(2,1)}, u32[]{:S(2)}, u32[]{:S(2)}) %collective-permute-start.45) | collective-permute-done | bytes 299040 | tf_op jit(solution)/shard_map/ppermute | solution.py:825
  400.1 3.8 collective-permute-start.47
  403.9 3.1 collective-permute-start.48
  412.8 4.2 unpack_tail.1
  420.7 6.9 %collective-permute-done.42.b = bf16[160,2048]{1,0:T(8,128)(2,1)} collective-permute-done((bf16[160,2048]{1,0:T(8,128)(2,1)}, bf16[160,2048]{1,0:T(8,128)(2,1)}, u32[]{:S(2)}, u32[]{:S(2)}) %collective-permute-start.42) | collective-permute-done | bytes 655392 | tf_op jit(solution)/shard_map/ppermute | solution.py:108
  427.6 3.8 norm_back_one.1
  431.5 9.8 %unpack.1 = (f32[1024,1408]{1,0:T(8,128)}, f32[1024,1408]{1,0:T(8,128)}, f32[704,2048]{1,0:T(8,128)}) custom-call(bf16[16,2112,128]{2,1,0:T(8,128)(2,1)} %all-gather.8.cloned.1.call-done.piece), custom_call_target="tpu_custom_call" | custom-call | flops 1000000 | bytes 26000000 | tf_op jit(solution)/shard_map/unpack/pallas_call | solution.py:680
  (220 shorter events, 84.8 us)
Async XLA Ops:
  7.2 74.5 %all-gather.4.cloned.1.call-start = ((), (), s32[]{:S(2)}) async-start(), calls=%async_computation.1 | async-start | bytes 4718592 | tf_op jit(solution)/shard_map/all_gather | solution.py:916
  10.0 21.7 %collective-permute-start = (bf16[160,2048]{1,0:T(8,128)(2,1)S(1)}, bf16[160,2048]{1,0:T(8,128)(2,1)S(1)}, u32[]{:S(2)}, u32[]{:S(2)}) collective-permute-start(bf16[160,2048]{1,0:T(8,128)(2,1)S(1)} %fusion.2.n0.refs_0_.refs_5_), channel_id=1, source_target_pairs={{0,6},{2,0},{4,2},{6,4},{1,7},{3,1},{5,3},{7,5},{8,14},{10,8},{12,... | collective-permute-start | bytes 1966088 | tf_op jit(solution)/shard_map/ppermute | solution.py:71
  13.3 16.6 %collective-permute-start.1 = (bf16[160,2048]{1,0:T(8,128)(2,1)S(1)}, bf16[160,2048]{1,0:T(8,128)(2,1)}, u32[]{:S(2)}, u32[]{:S(2)}) collective-permute-start(bf16[160,2048]{1,0:T(8,128)(2,1)S(1)} %fusion.2.n0.refs_0_.refs_5_), channel_id=1, source_target_pairs={{0,2},{2,4},{4,6},{6,0},{1,3},{3,5},{5,7},{7,1},{8,10},{10,12},{12... | collective-permute-start | bytes 1966088 | tf_op jit(solution)/shard_map/ppermute | solution.py:70
  14.3 29.2 %collective-permute-start.4 = (bf16[512,640]{1,0:T(8,128)(2,1)}, bf16[512,640]{1,0:T(8,128)(2,1)S(1)}, u32[]{:S(2)}, u32[]{:S(2)}) collective-permute-start(bf16[512,640]{1,0:T(8,128)(2,1)} %constant_dynamic-slice_fusion.5), channel_id=1, source_target_pairs={{0,1},{1,0},{2,3},{3,2},{4,5},{5,4},{6,7},{7,6},{8,9},{9,8},{10,11... | collective-permute-start | bytes 1966088 | tf_op jit(solution)/shard_map/ppermute | solution.py:134
  20.7 22.7 %collective-permute-start.5 = (bf16[128,2048]{1,0:T(8,128)(2,1)}, bf16[128,2048]{1,0:T(8,128)(2,1)S(1)}, u32[]{:S(2)}, u32[]{:S(2)}) collective-permute-start(bf16[128,2048]{1,0:T(8,128)(2,1)} %pad_maximum_fusion.1), channel_id=1, source_target_pairs={{0,1},{1,0},{2,3},{3,2},{4,5},{5,4},{6,7},{7,6},{8,9},{9,8},{10,11... | collective-permute-start | bytes 1572872 | tf_op jit(solution)/shard_map/ppermute | solution.py:921
  31.7 11.8 %collective-permute-start.2 = (bf16[80,2048]{1,0:T(8,128)(2,1)}, bf16[80,2048]{1,0:T(8,128)(2,1)S(1)}, u32[]{:S(2)}, u32[]{:S(2)}) collective-permute-start(bf16[80,2048]{1,0:T(8,128)(2,1)} %slice.37), channel_id=1, source_target_pairs={{0,2},{2,4},{4,6},{6,0},{1,3},{3,5},{5,7},{7,1},{8,10},{10,12},{12... | collective-permute-start | bytes 983048 | tf_op jit(solution)/shard_map/ppermute | solution.py:74
  31.7 11.8 %collective-permute-start.3 = (bf16[80,2048]{1,0:T(8,128)(2,1)S(1)}, bf16[80,2048]{1,0:T(8,128)(2,1)S(1)}, u32[]{:S(2)}, u32[]{:S(2)}) collective-permute-start(bf16[80,2048]{1,0:T(8,128)(2,1)S(1)} %slice.38), channel_id=1, source_target_pairs={{0,6},{2,0},{4,2},{6,4},{1,7},{3,1},{5,3},{7,5},{8,14},{10,8},{12,... | collective-permute-start | bytes 983048 | tf_op jit(solution)/shard_map/ppermute | solution.py:75
  44.4 98.4 %all-gather.6.cloned.1.call-start = ((), (), s32[]{:S(2)}) async-start(), calls=%async_computation.2 | async-start | bytes 6782976 | tf_op jit(solution)/shard_map/all_gather | solution.py:916
  47.3 30.7 %collective-permute-start.8 = (bf16[160,2048]{1,0:T(8,128)(2,1)S(1)}, bf16[160,2048]{1,0:T(8,128)(2,1)}, u32[]{:S(2)}, u32[]{:S(2)}) collective-permute-start(bf16[160,2048]{1,0:T(8,128)(2,1)S(1)} %copy-done.5), channel_id=1, source_target_pairs={{0,6},{2,0},{4,2},{6,4},{1,7},{3,1},{5,3},{7,5},{8,14},{10,8},{12,... | collective-permute-start | bytes 1966088 | tf_op jit(solution)/shard_map/ppermute | solution.py:929
  49.9 28.0 %collective-permute-start.9 = (bf16[160,2048]{1,0:T(8,128)(2,1)S(1)}, bf16[160,2048]{1,0:T(8,128)(2,1)}, u32[]{:S(2)}, u32[]{:S(2)}) collective-permute-start(bf16[160,2048]{1,0:T(8,128)(2,1)S(1)} %copy-done.5), channel_id=1, source_target_pairs={{0,4},{2,6},{4,0},{6,2},{1,5},{3,7},{5,1},{7,3},{8,12},{10,14},{12... | collective-permute-start | bytes 1966088 | tf_op jit(solution)/shard_map/ppermute | solution.py:929
  49.9 31.8 %collective-permute-start.10 = (bf16[160,2048]{1,0:T(8,128)(2,1)S(1)}, bf16[160,2048]{1,0:T(8,128)(2,1)}, u32[]{:S(2)}, u32[]{:S(2)}) collective-permute-start(bf16[160,2048]{1,0:T(8,128)(2,1)S(1)} %copy-done.5), channel_id=1, source_target_pairs={{0,2},{2,4},{4,6},{6,0},{1,3},{3,5},{5,7},{7,1},{8,10},{10,12},{12... | collective-permute-start | bytes 1966088 | tf_op jit(solution)/shard_map/ppermute | solution.py:929
  63.3 22.6 %collective-permute-start.19 = (bf16[128,2944]{1,0:T(8,128)(2,1)S(1)}, bf16[128,2944]{1,0:T(8,128)(2,1)S(1)}, u32[]{:S(2)}, u32[]{:S(2)}) collective-permute-start(bf16[128,2944]{1,0:T(8,128)(2,1)S(1)} %pad_maximum_fusion), channel_id=1, source_target_pairs={{0,17},{1,16},{16,1},{17,0},{2,19},{3,18},{18,3},{19,2},{4,21},{5,... | collective-permute-start | bytes 2261000 | tf_op jit(solution)/shard_map/ppermute | solution.py:933
  86.8 264.8 %reduce-scatter.2.cloned.1.call-start = ((), (), s32[]{:S(2)}) async-start(), calls=%async_computation.3 | async-start | bytes 17842176 | tf_op jit(solution)/shard_map/reduce_scatter | solution.py:961
  86.8 10.0 %collective-permute-start.11 = (bf16[80,2048]{1,0:T(8,128)(2,1)}, bf16[80,2048]{1,0:T(8,128)(2,1)S(1)}, u32[]{:S(2)}, u32[]{:S(2)}) collective-permute-start(bf16[80,2048]{1,0:T(8,128)(2,1)} %get-tuple-element.110), channel_id=1, source_target_pairs={{0,2},{2,4},{4,6},{6,0},{1,3},{3,5},{5,7},{7,1},{8,10},{10,12},{12... | collective-permute-start | bytes 983048 | tf_op jit(solution)/shard_map/ppermute | solution.py:86
  99.9 16.2 %collective-permute-start.13 = (bf16[160,2048]{1,0:T(8,128)(2,1)}, bf16[160,2048]{1,0:T(8,128)(2,1)S(1)}, u32[]{:S(2)}, u32[]{:S(2)}) collective-permute-start(bf16[160,2048]{1,0:T(8,128)(2,1)} %get-tuple-element.113), channel_id=1, source_target_pairs={{0,2},{2,4},{4,6},{6,0},{1,3},{3,5},{5,7},{7,1},{8,10},{10,12},{12... | collective-permute-start | bytes 1966088 | tf_op jit(solution)/shard_map/ppermute | solution.py:108
  99.9 16.2 %collective-permute-start.14 = (bf16[160,2048]{1,0:T(8,128)(2,1)}, bf16[160,2048]{1,0:T(8,128)(2,1)S(1)}, u32[]{:S(2)}, u32[]{:S(2)}) collective-permute-start(bf16[160,2048]{1,0:T(8,128)(2,1)} %get-tuple-element.114), channel_id=1, source_target_pairs={{0,6},{2,0},{4,2},{6,4},{1,7},{3,1},{5,3},{7,5},{8,14},{10,8},{12,... | collective-permute-start | bytes 1966088 | tf_op jit(solution)/shard_map/ppermute | solution.py:108
  120.1 15.3 %collective-permute-start.16 = (bf16[160,2048]{1,0:T(8,128)(2,1)}, bf16[160,2048]{1,0:T(8,128)(2,1)S(1)}, u32[]{:S(2)}, u32[]{:S(2)}) collective-permute-start(bf16[160,2048]{1,0:T(8,128)(2,1)} %get-tuple-element.116.n0.refs_0_.refs_5_), channel_id=1, source_target_pairs={{0,2},{2,4},{4,6},{6,0},{1,3},{3,5},{5,7},{7,1},{8,10},{10,12},{12... | collective-permute-start | bytes 1966088 | tf_op jit(solution)/shard_map/ppermute | solution.py:70
  120.6 14.9 %collective-permute-start.15 = (bf16[160,2048]{1,0:T(8,128)(2,1)}, bf16[160,2048]{1,0:T(8,128)(2,1)S(1)}, u32[]{:S(2)}, u32[]{:S(2)}) collective-permute-start(bf16[160,2048]{1,0:T(8,128)(2,1)} %get-tuple-element.116.n0.refs_0_.refs_5_), channel_id=1, source_target_pairs={{0,6},{2,0},{4,2},{6,4},{1,7},{3,1},{5,3},{7,5},{8,14},{10,8},{12,... | collective-permute-start | bytes 1966088 | tf_op jit(solution)/shard_map/ppermute | solution.py:71
  179.8 12.3 %collective-permute-start.20 = (bf16[80,2048]{1,0:T(8,128)(2,1)}, bf16[80,2048]{1,0:T(8,128)(2,1)S(1)}, u32[]{:S(2)}, u32[]{:S(2)}) collective-permute-start(bf16[80,2048]{1,0:T(8,128)(2,1)} %get-tuple-element.127), channel_id=1, source_target_pairs={{0,2},{2,4},{4,6},{6,0},{1,3},{3,5},{5,7},{7,1},{8,10},{10,12},{12... | collective-permute-start | bytes 983048 | tf_op jit(solution)/shard_map/ppermute | solution.py:86
  181.0 11.1 %collective-permute-start.21 = (bf16[80,2048]{1,0:T(8,128)(2,1)}, bf16[80,2048]{1,0:T(8,128)(2,1)S(1)}, u32[]{:S(2)}, u32[]{:S(2)}) collective-permute-start(bf16[80,2048]{1,0:T(8,128)(2,1)} %get-tuple-element.129), channel_id=1, source_target_pairs={{0,6},{2,0},{4,2},{6,4},{1,7},{3,1},{5,3},{7,5},{8,14},{10,8},{12,... | collective-permute-start | bytes 983048 | tf_op jit(solution)/shard_map/ppermute | solution.py:87
  195.2 17.3 %collective-permute-start.22 = (bf16[160,2048]{1,0:T(8,128)(2,1)}, bf16[160,2048]{1,0:T(8,128)(2,1)S(1)}, u32[]{:S(2)}, u32[]{:S(2)}) collective-permute-start(bf16[160,2048]{1,0:T(8,128)(2,1)} %get-tuple-element.130), channel_id=1, source_target_pairs={{0,2},{2,4},{4,6},{6,0},{1,3},{3,5},{5,7},{7,1},{8,10},{10,12},{12... | collective-permute-start | bytes 1966088 | tf_op jit(solution)/shard_map/ppermute | solution.py:108
  195.2 17.3 %collective-permute-start.23 = (bf16[160,2048]{1,0:T(8,128)(2,1)}, bf16[160,2048]{1,0:T(8,128)(2,1)S(1)}, u32[]{:S(2)}, u32[]{:S(2)}) collective-permute-start(bf16[160,2048]{1,0:T(8,128)(2,1)} %get-tuple-element.131), channel_id=1, source_target_pairs={{0,6},{2,0},{4,2},{6,4},{1,7},{3,1},{5,3},{7,5},{8,14},{10,8},{12,... | collective-permute-start | bytes 1966088 | tf_op jit(solution)/shard_map/ppermute | solution.py:108
  213.6 217.9 %all-gather.8.cloned.1.call-start = ((), (), s32[]{:S(2)}) async-start(), calls=%async_computation.4 | async-start | bytes 9191424 | tf_op jit(solution)/shard_map/all_gather | solution.py:998
  217.7 12.2 %collective-permute-start.24 = (bf16[160,2048]{1,0:T(8,128)(2,1)}, bf16[160,2048]{1,0:T(8,128)(2,1)S(1)}, u32[]{:S(2)}, u32[]{:S(2)}) collective-permute-start(bf16[160,2048]{1,0:T(8,128)(2,1)} %get-tuple-element.136.b0.refs_10_), channel_id=1, source_target_pairs={{0,2},{2,4},{4,6},{6,0},{1,3},{3,5},{5,7},{7,1},{8,10},{10,12},{12... | collective-permute-start | bytes 1966088 | tf_op jit(solution)/shard_map/ppermute | solution.py:70
  217.7 12.1 %collective-permute-start.25 = (bf16[160,2048]{1,0:T(8,128)(2,1)}, bf16[160,2048]{1,0:T(8,128)(2,1)S(1)}, u32[]{:S(2)}, u32[]{:S(2)}) collective-permute-start(bf16[160,2048]{1,0:T(8,128)(2,1)} %get-tuple-element.136.b0.refs_10_), channel_id=1, source_target_pairs={{0,6},{2,0},{4,2},{6,4},{1,7},{3,1},{5,3},{7,5},{8,14},{10,8},{12,... | collective-permute-start | bytes 1966088 | tf_op jit(solution)/shard_map/ppermute | solution.py:71
  229.9 13.4 %collective-permute-start.26 = (bf16[80,2048]{1,0:T(8,128)(2,1)S(1)}, bf16[80,2048]{1,0:T(8,128)(2,1)S(1)}, u32[]{:S(2)}, u32[]{:S(2)}) collective-permute-start(bf16[80,2048]{1,0:T(8,128)(2,1)S(1)} %slice.41), channel_id=1, source_target_pairs={{0,2},{2,4},{4,6},{6,0},{1,3},{3,5},{5,7},{7,1},{8,10},{10,12},{12... | collective-permute-start | bytes 983048 | tf_op jit(solution)/shard_map/ppermute | solution.py:74
  230.0 13.3 %collective-permute-start.27 = (bf16[80,2048]{1,0:T(8,128)(2,1)S(1)}, bf16[80,2048]{1,0:T(8,128)(2,1)}, u32[]{:S(2)}, u32[]{:S(2)}) collective-permute-start(bf16[80,2048]{1,0:T(8,128)(2,1)S(1)} %slice.42), channel_id=1, source_target_pairs={{0,6},{2,0},{4,2},{6,4},{1,7},{3,1},{5,3},{7,5},{8,14},{10,8},{12,... | collective-permute-start | bytes 983048 | tf_op jit(solution)/shard_map/ppermute | solution.py:75
  243.3 26.8 %collective-permute-start.28 = (bf16[160,2048]{1,0:T(8,128)(2,1)}, bf16[160,2048]{1,0:T(8,128)(2,1)S(1)}, u32[]{:S(2)}, u32[]{:S(2)}) collective-permute-start(bf16[160,2048]{1,0:T(8,128)(2,1)} %get-tuple-element.139), channel_id=1, source_target_pairs={{0,2},{2,4},{4,6},{6,0},{1,3},{3,5},{5,7},{7,1},{8,10},{10,12},{12... | collective-permute-start | bytes 1966088 | tf_op jit(solution)/shard_map/ppermute | solution.py:974
  243.4 26.7 %collective-permute-start.29 = (bf16[160,2048]{1,0:T(8,128)(2,1)}, bf16[160,2048]{1,0:T(8,128)(2,1)S(1)}, u32[]{:S(2)}, u32[]{:S(2)}) collective-permute-start(bf16[160,2048]{1,0:T(8,128)(2,1)} %get-tuple-element.141), channel_id=1, source_target_pairs={{0,6},{2,0},{4,2},{6,4},{1,7},{3,1},{5,3},{7,5},{8,14},{10,8},{12,... | collective-permute-start | bytes 1966088 | tf_op jit(solution)/shard_map/ppermute | solution.py:974
  266.8 12.8 %collective-permute-start.30 = (bf16[640,128]{1,0:T(8,128)(2,1)}, bf16[640,128]{1,0:T(8,128)(2,1)S(1)}, u32[]{:S(2)}, u32[]{:S(2)}) collective-permute-start(bf16[640,128]{1,0:T(8,128)(2,1)} %get-tuple-element.149), channel_id=1, source_target_pairs={{0,1},{1,0},{2,3},{3,2},{4,5},{5,4},{6,7},{7,6},{8,9},{9,8},{10,11... | collective-permute-start | bytes 491528 | tf_op jit(solution)/shard_map/ppermute | solution.py:979
  279.7 18.5 %collective-permute-start.31 = (bf16[4,2,1024,128]{3,2,1,0:T(8,128)(2,1)}, bf16[4,2,1024,128]{3,2,1,0:T(8,128)(2,1)S(1)}, u32[]{:S(2)}, u32[]{:S(2)}) collective-permute-start(bf16[4,2,1024,128]{3,2,1,0:T(8,128)(2,1)} %get-tuple-element.151), channel_id=1, source_target_pairs={{0,8},{8,0},{1,9},{9,1},{2,10},{10,2},{3,11},{11,3},{4,12},{12,4},... | collective-permute-start | bytes 6291464 | tf_op jit(solution)/shard_map/ppermute | solution.py:806
  303.6 20.8 %collective-permute-start.33 = (bf16[2,1168,128]{2,1,0:T(8,128)(2,1)}, bf16[2,1168,128]{2,1,0:T(8,128)(2,1)S(1)}, u32[]{:S(2)}, u32[]{:S(2)}) collective-permute-start(bf16[2,1168,128]{2,1,0:T(8,128)(2,1)} %get-tuple-element.157), channel_id=1, source_target_pairs={{0,64},{32,96},{64,0},{96,32},{1,65},{33,97},{65,1},{97,33},{2,66}... | collective-permute-start | bytes 1794056 | tf_op jit(solution)/shard_map/ppermute | solution.py:810
  306.5 30.7 %collective-permute-start.34 = (bf16[2,1168,128]{2,1,0:T(8,128)(2,1)}, bf16[2,1168,128]{2,1,0:T(8,128)(2,1)S(1)}, u32[]{:S(2)}, u32[]{:S(2)}) collective-permute-start(bf16[2,1168,128]{2,1,0:T(8,128)(2,1)} %get-tuple-element.158), channel_id=1, source_target_pairs={{0,32},{32,64},{64,96},{96,0},{1,33},{33,65},{65,97},{97,1},{2,34}... | collective-permute-start | bytes 1794056 | tf_op jit(solution)/shard_map/ppermute | solution.py:810
  306.9 30.3 %collective-permute-start.35 = (bf16[2,1168,128]{2,1,0:T(8,128)(2,1)}, bf16[2,1168,128]{2,1,0:T(8,128)(2,1)S(1)}, u32[]{:S(2)}, u32[]{:S(2)}) collective-permute-start(bf16[2,1168,128]{2,1,0:T(8,128)(2,1)} %get-tuple-element.159), channel_id=1, source_target_pairs={{0,96},{32,0},{64,32},{96,64},{1,97},{33,1},{65,33},{97,65},{2,98}... | collective-permute-start | bytes 1794056 | tf_op jit(solution)/shard_map/ppermute | solution.py:810
  352.7 14.6 %collective-permute-start.38 = (bf16[1168,128]{1,0:T(8,128)(2,1)}, bf16[1168,128]{1,0:T(8,128)(2,1)S(1)}, u32[]{:S(2)}, u32[]{:S(2)}) collective-permute-start(bf16[1168,128]{1,0:T(8,128)(2,1)} %get-tuple-element.163), channel_id=1, source_target_pairs={{0,1},{1,0},{2,3},{3,2},{4,5},{5,4},{6,7},{7,6},{8,9},{9,8},{10,11... | collective-permute-start | bytes 897032 | tf_op jit(solution)/shard_map/ppermute | solution.py:820
  355.1 12.4 %collective-permute-start.39 = (bf16[1168,128]{1,0:T(8,128)(2,1)}, bf16[1168,128]{1,0:T(8,128)(2,1)S(1)}, u32[]{:S(2)}, u32[]{:S(2)}) collective-permute-start(bf16[1168,128]{1,0:T(8,128)(2,1)} %get-tuple-element.163), channel_id=1, source_target_pairs={{0,17},{1,16},{16,1},{17,0},{2,19},{3,18},{18,3},{19,2},{4,21},{5,... | collective-permute-start | bytes 897032 | tf_op jit(solution)/shard_map/ppermute | solution.py:821
  370.8 12.9 %collective-permute-start.44 = (bf16[1168,128]{1,0:T(8,128)(2,1)}, bf16[1168,128]{1,0:T(8,128)(2,1)}, u32[]{:S(2)}, u32[]{:S(2)}) collective-permute-start(bf16[1168,128]{1,0:T(8,128)(2,1)} %sum_z.1.refs_0_), channel_id=1, source_target_pairs={{0,32},{32,64},{64,96},{96,0},{1,33},{33,65},{65,97},{97,1},{2,34}... | collective-permute-start | bytes 897032 | tf_op jit(solution)/shard_map/ppermute | solution.py:825
  372.7 27.4 %collective-permute-start.45 = (bf16[1168,128]{1,0:T(8,128)(2,1)}, bf16[1168,128]{1,0:T(8,128)(2,1)}, u32[]{:S(2)}, u32[]{:S(2)}) collective-permute-start(bf16[1168,128]{1,0:T(8,128)(2,1)} %sum_z.1.refs_0_), channel_id=1, source_target_pairs={{0,64},{32,96},{64,0},{96,32},{1,65},{33,97},{65,1},{97,33},{2,66}... | collective-permute-start | bytes 897032 | tf_op jit(solution)/shard_map/ppermute | solution.py:825
  374.0 29.8 %collective-permute-start.46 = (bf16[1168,128]{1,0:T(8,128)(2,1)}, bf16[1168,128]{1,0:T(8,128)(2,1)}, u32[]{:S(2)}, u32[]{:S(2)}) collective-permute-start(bf16[1168,128]{1,0:T(8,128)(2,1)} %sum_z.1.refs_0_), channel_id=1, source_target_pairs={{0,96},{32,0},{64,32},{96,64},{1,97},{33,1},{65,33},{97,65},{2,98}... | collective-permute-start | bytes 897032 | tf_op jit(solution)/shard_map/ppermute | solution.py:825
  376.1 42.6 %collective-permute-start.36 = (bf16[160,2048]{1,0:T(8,128)(2,1)}, bf16[160,2048]{1,0:T(8,128)(2,1)S(1)}, u32[]{:S(2)}, u32[]{:S(2)}) collective-permute-start(bf16[160,2048]{1,0:T(8,128)(2,1)} %get-tuple-element.161), channel_id=1, source_target_pairs={{0,4},{2,6},{4,0},{6,2},{1,5},{3,7},{5,1},{7,3},{8,12},{10,14},{12... | collective-permute-start | bytes 1966088 | tf_op jit(solution)/shard_map/ppermute | solution.py:997
  378.8 28.2 %collective-permute-start.40 = (bf16[80,2048]{1,0:T(8,128)(2,1)S(1)}, bf16[80,2048]{1,0:T(8,128)(2,1)S(1)}, u32[]{:S(2)}, u32[]{:S(2)}) collective-permute-start(bf16[80,2048]{1,0:T(8,128)(2,1)S(1)} %copy-done.41), channel_id=1, source_target_pairs={{0,2},{2,4},{4,6},{6,0},{1,3},{3,5},{5,7},{7,1},{8,10},{10,12},{12... | collective-permute-start | bytes 983048 | tf_op jit(solution)/shard_map/ppermute | solution.py:86
  383.7 23.4 %collective-permute-start.41 = (bf16[80,2048]{1,0:T(8,128)(2,1)S(1)}, bf16[80,2048]{1,0:T(8,128)(2,1)S(1)}, u32[]{:S(2)}, u32[]{:S(2)}) collective-permute-start(bf16[80,2048]{1,0:T(8,128)(2,1)S(1)} %copy-done.40), channel_id=1, source_target_pairs={{0,6},{2,0},{4,2},{6,4},{1,7},{3,1},{5,3},{7,5},{8,14},{10,8},{12,... | collective-permute-start | bytes 983048 | tf_op jit(solution)/shard_map/ppermute | solution.py:87
  400.1 10.0 %collective-permute-start.47 = (bf16[1168,128]{1,0:T(8,128)(2,1)}, bf16[1168,128]{1,0:T(8,128)(2,1)}, u32[]{:S(2)}, u32[]{:S(2)}) collective-permute-start(bf16[1168,128]{1,0:T(8,128)(2,1)} %sum_z.1.refs_0_), channel_id=1, source_target_pairs={{0,8},{8,0},{1,9},{9,1},{2,10},{10,2},{3,11},{11,3},{4,12},{12,4},... | collective-permute-start | bytes 897032 | tf_op jit(solution)/shard_map/ppermute | solution.py:826
  410.0 17.6 %collective-permute-start.42 = (bf16[160,2048]{1,0:T(8,128)(2,1)}, bf16[160,2048]{1,0:T(8,128)(2,1)}, u32[]{:S(2)}, u32[]{:S(2)}) collective-permute-start(bf16[160,2048]{1,0:T(8,128)(2,1)} %get-tuple-element.173), channel_id=1, source_target_pairs={{0,2},{2,4},{4,6},{6,0},{1,3},{3,5},{5,7},{7,1},{8,10},{10,12},{12... | collective-permute-start | bytes 1966088 | tf_op jit(solution)/shard_map/ppermute | solution.py:108
  411.3 16.3 %collective-permute-start.43 = (bf16[160,2048]{1,0:T(8,128)(2,1)}, bf16[160,2048]{1,0:T(8,128)(2,1)}, u32[]{:S(2)}, u32[]{:S(2)}) collective-permute-start(bf16[160,2048]{1,0:T(8,128)(2,1)} %get-tuple-element.174), channel_id=1, source_target_pairs={{0,6},{2,0},{4,2},{6,4},{1,7},{3,1},{5,3},{7,5},{8,14},{10,8},{12,... | collective-permute-start | bytes 1966088 | tf_op jit(solution)/shard_map/ppermute | solution.py:108
  417.0 24.2 %collective-permute-start.53 = (f32[2,2048]{1,0:T(2,128)}, f32[2,2048]{1,0:T(2,128)S(1)}, u32[]{:S(2)}, u32[]{:S(2)}) collective-permute-start(f32[2,2048]{1,0:T(2,128)} %get-tuple-element.176), channel_id=1, source_target_pairs={{0,6},{2,0},{4,2},{6,4},{1,7},{3,1},{5,3},{7,5},{8,14},{10,8},{12,... | collective-permute-start | bytes 49160 | tf_op jit(solution)/shard_map/ppermute | solution.py:988
  418.2 23.0 %collective-permute-start.52 = (f32[2,2048]{1,0:T(2,128)}, f32[2,2048]{1,0:T(2,128)S(1)}, u32[]{:S(2)}, u32[]{:S(2)}) collective-permute-start(f32[2,2048]{1,0:T(2,128)} %get-tuple-element.176), channel_id=1, source_target_pairs={{0,4},{2,6},{4,0},{6,2},{1,5},{3,7},{5,1},{7,3},{8,12},{10,14},{12... | collective-permute-start | bytes 49160 | tf_op jit(solution)/shard_map/ppermute | solution.py:988
  418.8 22.5 %collective-permute-start.51 = (f32[2,2048]{1,0:T(2,128)}, f32[2,2048]{1,0:T(2,128)S(1)}, u32[]{:S(2)}, u32[]{:S(2)}) collective-permute-start(f32[2,2048]{1,0:T(2,128)} %get-tuple-element.176), channel_id=1, source_target_pairs={{0,2},{2,4},{4,6},{6,0},{1,3},{3,5},{5,7},{7,1},{8,10},{10,12},{12... | collective-permute-start | bytes 49160 | tf_op jit(solution)/shard_map/ppermute | solution.py:988
  (54 other events, 360.5 us)
Sparse Core Ops, SparseCore 0:
  44.4 35.0 all-gather.3
  86.9 39.9 all-gather.5
  212.7 138.8 reduce-scatter.1
  353.2 66.7 all-gather.7

commit v16 on v13

--- a/solution.py
+++ b/solution.py
@@ -824,8 +824,9 @@
     )
     d_one = last_step(p0, q1, q3)
     input_grad = finish(d_one)
-    mine = [tie(g, input_grad)] + [lax.ppermute(g, "y", shift(4, s)) for s in (1, 2, 3)]
-    theirs = [lax.ppermute(v, "core", shift(2, 1)) for v in [g] + mine[1:]]
+    mine = [g] + [lax.ppermute(g, "y", shift(4, s)) for s in (1, 2, 3)]
+    mine[3] = tie(mine[3], input_grad)
+    theirs = [lax.ppermute(v, "core", shift(2, 1)) for v in mine]
     shapes = (sds((DH, QW), F32), sds((AW // 2, D), F32), sds((2, D), F32))
     return own, input_grad, small_call(unpack_tail_body, shapes, idx, *mine, *theirs, name="unpack_tail")
 

time: 451 us -> 449 us (level)
  transfers between devices with their start and end apart: 58 -> 58, of which waited for: 19 -> 20; matrix products, arithmetic and copies ran while one was open for 3% -> 3% of each run, Pallas kernels for 29% -> 29%
where the time goes in v16:
time: 449 us; the launch traced here: 441 us
  Pallas kernels  168 us (37%)
  waiting for transfers between devices  137 us (31%)
  starting transfers between devices  89.1 us (20%)
  local copies, waits for them, and re-layouts  22.1 us (5%)
  between operations  14.7 us (3%)
  other arithmetic  9.49 us (2%)
    ppermute x3, waiting for transfers between devices, sum_tail(): got = [lax.ppermute(g[s], 'y', shift(4, s)) for s in (2, 1, 3)]  28 us
    ppermute x3, waiting for transfers between devices, gather_x(): from_prev = lax.ppermute(v, 'x', shift(4, 1))  27.1 us
    pallas_call x1, Pallas kernels, ffn(): pl.pallas_call(ffn_body, grid=(TILES,), out_shape=(sds((ROWS, FF4)),) * 3...  20.8 us
    pallas_call x1, Pallas kernels, attend_back(): pl.pallas_call(attend_back_body, grid=(1,), out_shape=(sds((4, BLK, AW)),...  20.6 us
    ppermute x3, waiting for transfers between devices, sum_tail(): mine = [g] + [lax.ppermute(g, 'y', shift(4, s)) for s in (1, 2, 3)]  19.5 us
    pallas_call x1, Pallas kernels, ffn_back(): pl.pallas_call(ffn_back_body, grid_spec=pltpu.PrefetchScalarGridSpec(num_...  15.5 us
    pallas_call x1, Pallas kernels, gate_up_grads(): pl.pallas_call(gate_up_grads_body, grid=(16 // QS,), out_shape=sds((2, 16...  14.6 us
    unnamed x90, local copies, waits for them, and re-layouts  13.7 us
  transfers between devices with their start and end apart: 58, of which 20 were waited for; matrix products, arithmetic and copies ran while one was open for 3% of the time, Pallas kernels for 29%

profile of v16, /device:TPU:1, one launch (start us, length us, event | category | flops | bytes accessed | tf_op | source)
XLA Modules:
  0.0 440.9 jit_solution(7218757457329685967)
XLA Ops:
  10.0 3.4 collective-permute-start
  14.3 3.6 collective-permute-start.4
  24.8 5.1 %collective-permute-done.1.n3.refs_4_.refs_9_ = bf16[160,2048]{1,0:T(8,128)(2,1)} collective-permute-done((bf16[160,2048]{1,0:T(8,128)(2,1)S(1)}, bf16[160,2048]{1,0:T(8,128)(2,1)}, u32[]{:S(2)}, u32[]{:S(2)}) %collective-permute-start.1) | collective-permute-done | bytes 655392 | tf_op jit(solution)/shard_map/ppermute | solution.py:70
  31.7 2.7 collective-permute-start.3
  34.4 9.0 %collective-permute-done.5 = bf16[128,2048]{1,0:T(8,128)(2,1)S(1)} collective-permute-done((bf16[128,2048]{1,0:T(8,128)(2,1)}, bf16[128,2048]{1,0:T(8,128)(2,1)S(1)}, u32[]{:S(2)}, u32[]{:S(2)}) %collective-permute-start.5) | collective-permute-done | bytes 524320 | tf_op jit(solution)/shard_map/ppermute | solution.py:924
  51.5 6.8 %qkv_forward.1 = (bf16[4,1280,128]{2,1,0:T(8,128)(2,1)}, bf16[640,128]{1,0:T(8,128)(2,1)}) custom-call(s32[4]{0:T(128)} %pad_add_fusion.idx, bf16[160,2048]{1,0:T(8,128)(2,1)} %copy-done.4, bf16[160,2048]{1,0:T(8,128)(2,1)} %copy-done.7, bf16[80,2048]{1,0:T(8,128)(2,1)} %copy-done.24, bf16[80,2048]{1,0:T(8,128)(2,1)} %copy-done.25, ...), custom_call_target="tpu_custom_call" | custom-call | flops 1677721600 | bytes 7000000 | tf_op jit(solution)/shard_map/qkv_forward/pallas_call | solution.py:184
  58.2 3.0 collective-permute-start.7
  65.9 8.6 %attend.1 = (bf16[4,160,512]{2,1,0:T(8,128)(2,1)}, bf16[4,1280,128]{2,1,0:T(8,128)(2,1)}) custom-call(s32[4]{0:T(128)} %pad_add_fusion.idx, bf16[4,1280,128]{2,1,0:T(8,128)(2,1)} %get-tuple-element.104.q, bf16[640,128]{1,0:T(8,128)(2,1)} %get-tuple-element.105.kv_own, bf16[640,128]{1,0:T(8,128)(2,1)} %copy-done.44, s32[1,1280]{1,0:T(1,128)} %reshape_tile.3.first), custom_call_target="tpu_custom_call" | custom-call | flops 12000000000 | bytes 3000000 | tf_op jit(solution)/shard_map/attend/pallas_call | solution.py:277
  74.6 3.5 collective-permute-done.8.c1.refs_1_
  78.1 3.7 collective-permute-done.10.c3.refs_3_
  81.8 4.2 out_project.1
  87.0 2.7 collective-permute-start.12
  89.6 7.2 %collective-permute-done.11.got_a = bf16[80,2048]{1,0:T(8,128)(2,1)S(1)} collective-permute-done((bf16[80,2048]{1,0:T(8,128)(2,1)}, bf16[80,2048]{1,0:T(8,128)(2,1)S(1)}, u32[]{:S(2)}, u32[]{:S(2)}) %collective-permute-start.11) | collective-permute-done | bytes 327712 | tf_op jit(solution)/shard_map/ppermute | solution.py:86
  100.0 2.7 collective-permute-start.14
  102.7 13.6 %collective-permute-done.13.b = bf16[160,2048]{1,0:T(8,128)(2,1)S(1)} collective-permute-done((bf16[160,2048]{1,0:T(8,128)(2,1)}, bf16[160,2048]{1,0:T(8,128)(2,1)S(1)}, u32[]{:S(2)}, u32[]{:S(2)}) %collective-permute-start.13) | collective-permute-done | bytes 655392 | tf_op jit(solution)/shard_map/ppermute | solution.py:108
  117.3 2.9 norm_two.1
  122.9 12.6 %collective-permute-done.16.n3.refs_4_.refs_9_ = bf16[160,2048]{1,0:T(8,128)(2,1)S(1)} collective-permute-done((bf16[160,2048]{1,0:T(8,128)(2,1)}, bf16[160,2048]{1,0:T(8,128)(2,1)S(1)}, u32[]{:S(2)}, u32[]{:S(2)}) %collective-permute-start.16) | collective-permute-done | bytes 655392 | tf_op jit(solution)/shard_map/ppermute | solution.py:70
  135.7 3.2 collective-permute-start.18
  138.9 3.9 collective-permute-done.17.n2a.refs_2_.refs_7_
  143.6 20.8 %ffn.1 = (bf16[640,1408]{1,0:T(8,128)(2,1)}, bf16[640,1408]{1,0:T(8,128)(2,1)}, bf16[640,1408]{1,0:T(8,128)(2,1)}) custom-call(s32[4]{0:T(128)} %pad_add_fusion.idx, bf16[160,2048]{1,0:T(8,128)(2,1)} %get-tuple-element.118.n0.refs_0_.refs_5_, bf16[160,2048]{1,0:T(8,128)(2,1)} %copy-done.2, bf16[80,2048]{1,0:T(8,128)(2,1)} %copy-done.8, ...), custom_call_target="tpu_custom_call" | custom-call | flops 11072962560 | bytes 34000000 | tf_op jit(solution)/shard_map/ffn/pallas_call | solution.py:523
  164.5 15.5 %ffn_back.1 = (bf16[160,2048]{1,0:T(8,128)(2,1)}, bf16[160,2048]{1,0:T(8,128)(2,1)}, bf16[80,2048]{1,0:T(8,128)(2,1)}, bf16[80,2048]{1,0:T(8,128)(2,1)}, bf16[160,2048]{1,0:T(8,128)(2,1)}) custom-call(s32[4]{0:T(128)} %pad_add_fusion.idx, bf16[640,1408]{1,0:T(8,128)(2,1)} %get-tuple-element.181.dgate.refs_10_, ...), custom_call_target="tpu_custom_call" | custom-call | flops 7381975040 | bytes 18000000 | tf_op jit(solution)/shard_map/ffn_back/pallas_call | solution.py:589
  183.1 9.1 %down_grads.1.refs_12_ = bf16[2,16,2112,128]{3,2,1,0:T(8,128)(2,1)} custom-call(bf16[160,2048]{1,0:T(8,128)(2,1)} %refs_0_.1, bf16[160,2048]{1,0:T(8,128)(2,1)} %collective-permute-done.8.c1.refs_1_, bf16[160,2048]{1,0:T(8,128)(2,1)} %collective-permute-done.9.c2.refs_2_, bf16[160,2048]{1,0:T(8,128)(2,1)} %collective-permute-done.10.c3.refs_3_, ...), custom_call_target="tpu_custom_call" | custom-call | flops 3690987520 | bytes 10000000 | tf_op jit(solution)/shard_map/down_grads/pallas_call | solution.py:656
  195.3 2.7 collective-permute-start.23
  198.0 14.6 %gate_up_grads.1 = bf16[2,16,2112,128]{3,2,1,0:T(8,128)(2,1)} custom-call(bf16[160,2048]{1,0:T(8,128)(2,1)} %get-tuple-element.118.n0.refs_0_.refs_5_, bf16[160,2048]{1,0:T(8,128)(2,1)} %copy-done.2, bf16[80,2048]{1,0:T(8,128)(2,1)} %copy-done.8, bf16[80,2048]{1,0:T(8,128)(2,1)} %copy-done.9, ...), custom_call_target="tpu_custom_call", output_to_operand_aliasing={{}: (12, {})} | custom-call | flops 7381975040 | bytes 20000000 | tf_op jit(solution)/shard_map/gate_up_grads/pallas_call | solution.py:625
  213.7 4.0 norm_back_two.1
  220.5 9.4 %collective-permute-done.24.b3.refs_14_ = bf16[160,2048]{1,0:T(8,128)(2,1)S(1)} collective-permute-done((bf16[160,2048]{1,0:T(8,128)(2,1)}, bf16[160,2048]{1,0:T(8,128)(2,1)S(1)}, u32[]{:S(2)}, u32[]{:S(2)}) %collective-permute-start.24) | collective-permute-done | bytes 655392 | tf_op jit(solution)/shard_map/ppermute | solution.py:70
  230.0 2.7 collective-permute-start.27
  232.8 10.6 %down_project.1 = (bf16[160,2048]{1,0:T(8,128)(2,1)}, bf16[160,2048]{1,0:T(8,128)(2,1)}, bf16[160,2048]{1,0:T(8,128)(2,1)}, bf16[160,2048]{1,0:T(8,128)(2,1)}) custom-call(s32[4]{0:T(128)} %pad_add_fusion.idx, bf16[640,1408]{1,0:T(8,128)(2,1)} %get-tuple-element.182.hid.refs_4_, bf16[704,2048]{1,0:T(8,128)(2,1)} %w0.9, bf16[8,128,2048]{2,1,0:T(8,128)(2,1)} %bitcast.17), custom_call_target="tpu_custom_call" | custom-call | flops 3690987520 | bytes 11000000 | tf_op jit(solution)/shard_map/down_project/pallas_call | solution.py:559
  243.5 2.8 collective-permute-start.29
  246.3 20.6 %attend_back.1 = (bf16[4,160,512]{2,1,0:T(8,128)(2,1)}, f32[640,128]{1,0:T(8,128)}, bf16[640,128]{1,0:T(8,128)(2,1)}) custom-call(s32[4]{0:T(128)} %pad_add_fusion.idx, bf16[4,1280,128]{2,1,0:T(8,128)(2,1)} %get-tuple-element.145.qx, bf16[640,128]{1,0:T(8,128)(2,1)} %get-tuple-element.105.kv_own, bf16[640,128]{1,0:T(8,128)(2,1)} %copy-done.44, ...), custom_call_target="tpu_custom_call" | custom-call | flops 30000001024 | bytes 8000000 | tf_op jit(solution)/shard_map/attend_back/pallas_call | solution.py:388
  266.9 3.1 collective-permute-start.30
  270.0 9.6 %attn_grads.1 = (bf16[4,2,1024,128]{3,2,1,0:T(8,128)(2,1)}, bf16[4,2,1024,128]{3,2,1,0:T(8,128)(2,1)}) custom-call(s32[4]{0:T(128)} %pad_add_fusion.idx, bf16[160,2048]{1,0:T(8,128)(2,1)} %copy-done.4, bf16[160,2048]{1,0:T(8,128)(2,1)} %copy-done.7, bf16[80,2048]{1,0:T(8,128)(2,1)} %copy-done.24, bf16[80,2048]{1,0:T(8,128)(2,1)} %copy-done.25, ...), custom_call_target="tpu_custom_call" | custom-call | flops 2684354560 | bytes 10000000 | tf_op jit(solution)/shard_map/attn_grads/pallas_call | solution.py:735
  279.7 9.3 %collective-permute-start.31 = (bf16[4,2,1024,128]{3,2,1,0:T(8,128)(2,1)}, bf16[4,2,1024,128]{3,2,1,0:T(8,128)(2,1)S(1)}, u32[]{:S(2)}, u32[]{:S(2)}) collective-permute-start(bf16[4,2,1024,128]{3,2,1,0:T(8,128)(2,1)} %get-tuple-element.153), channel_id=1, source_target_pairs={{0,8},{8,0},{1,9},{9,1},{2,10},{10,2},{3,11},{11,3},{4,12},{12,4},... | collective-permute-start | bytes 6291464 | tf_op jit(solution)/shard_map/ppermute | solution.py:806
  288.9 7.5 %qkv_back.1 = (bf16[4,2,144,128]{3,2,1,0:T(8,128)(2,1)}, bf16[4,2,144,128]{3,2,1,0:T(8,128)(2,1)}, bf16[160,2048]{1,0:T(8,128)(2,1)}, bf16[160,2048]{1,0:T(8,128...) custom-call(s32[4]{0:T(128)} %pad_add_fusion.idx, ...), custom_call_target="tpu_custom_call" | custom-call | flops 1677721600 | bytes 13000000 | tf_op jit(solution)/shard_map/qkv_back/pallas_call | solution.py:446
  299.7 4.0 sum_core.1
  303.7 2.9 collective-permute-start.33
  309.3 15.2 %collective-permute-done.33.b = bf16[2,1168,128]{2,1,0:T(8,128)(2,1)S(1)} collective-permute-done((bf16[2,1168,128]{2,1,0:T(8,128)(2,1)}, bf16[2,1168,128]{2,1,0:T(8,128)(2,1)S(1)}, u32[]{:S(2)}, u32[]{:S(2)}) %collective-permute-start.33) | collective-permute-done | bytes 598048 | tf_op jit(solution)/shard_map/ppermute | solution.py:810
  324.5 12.8 %collective-permute-done.34.c = bf16[2,1168,128]{2,1,0:T(8,128)(2,1)S(1)} collective-permute-done((bf16[2,1168,128]{2,1,0:T(8,128)(2,1)}, bf16[2,1168,128]{2,1,0:T(8,128)(2,1)S(1)}, u32[]{:S(2)}, u32[]{:S(2)}) %collective-permute-start.34) | collective-permute-done | bytes 598048 | tf_op jit(solution)/shard_map/ppermute | solution.py:810
  340.9 10.8 %reduce-scatter.2.cloned.1.call-done = bf16[1,2112,128]{2,1,0:T(8,128)(2,1)} async-done(((bf16[32,2112,128]{2,1,0:T(8,128)(2,1)}), bf16[1,2112,128]{2,1,0:T(8,128)(2,1)}) %reduce-scatter.2.cloned.1.call-update) | async-done | bytes 540688 | tf_op jit(solution)/shard_map/reduce_scatter | solution.py:964
  364.6 2.7 collective-permute-start.40
  367.3 4.0 collective-permute-done.42.c
  378.5 7.0 %collective-permute-done.44.refs_1_ = bf16[1168,128]{1,0:T(8,128)(2,1)} collective-permute-done((bf16[1168,128]{1,0:T(8,128)(2,1)}, bf16[1168,128]{1,0:T(8,128)(2,1)}, u32[]{:S(2)}, u32[]{:S(2)}) %collective-permute-start.44) | collective-permute-done | bytes 299040 | tf_op jit(solution)/shard_map/ppermute | solution.py:827
  385.5 3.4 collective-permute-start.46
  388.9 12.5 %collective-permute-done.45.refs_2_ = bf16[1168,128]{1,0:T(8,128)(2,1)} collective-permute-done((bf16[1168,128]{1,0:T(8,128)(2,1)}, bf16[1168,128]{1,0:T(8,128)(2,1)}, u32[]{:S(2)}, u32[]{:S(2)}) %collective-permute-start.45) | collective-permute-done | bytes 299040 | tf_op jit(solution)/shard_map/ppermute | solution.py:827
  401.5 8.1 %collective-permute-start.47 = (bf16[1168,128]{1,0:T(8,128)(2,1)}, bf16[1168,128]{1,0:T(8,128)(2,1)}, u32[]{:S(2)}, u32[]{:S(2)}) collective-permute-start(bf16[1168,128]{1,0:T(8,128)(2,1)} %sum_z.1.refs_0_), channel_id=1, source_target_pairs={{0,8},{8,0},{1,9},{9,1},{2,10},{10,2},{3,11},{11,3},{4,12},{12,4},... | collective-permute-start | bytes 897032 | tf_op jit(solution)/shard_map/ppermute | solution.py:829
  410.6 3.8 norm_back_one.1
  416.4 4.2 unpack_tail.1
  423.5 9.8 %unpack.1 = (f32[1024,1408]{1,0:T(8,128)}, f32[1024,1408]{1,0:T(8,128)}, f32[704,2048]{1,0:T(8,128)}) custom-call(bf16[16,2112,128]{2,1,0:T(8,128)(2,1)} %all-gather.8.cloned.1.call-done.piece), custom_call_target="tpu_custom_call" | custom-call | flops 1000000 | bytes 26000000 | tf_op jit(solution)/shard_map/unpack/pallas_call | solution.py:680
  (222 shorter events, 80.3 us)
Async XLA Ops:
  7.2 74.6 %all-gather.4.cloned.1.call-start = ((), (), s32[]{:S(2)}) async-start(), calls=%async_computation.1 | async-start | bytes 4718592 | tf_op jit(solution)/shard_map/all_gather | solution.py:919
  10.0 21.7 %collective-permute-start = (bf16[160,2048]{1,0:T(8,128)(2,1)S(1)}, bf16[160,2048]{1,0:T(8,128)(2,1)S(1)}, u32[]{:S(2)}, u32[]{:S(2)}) collective-permute-start(bf16[160,2048]{1,0:T(8,128)(2,1)S(1)} %fusion.2.n0.refs_0_.refs_5_), channel_id=1, source_target_pairs={{0,6},{2,0},{4,2},{6,4},{1,7},{3,1},{5,3},{7,5},{8,14},{10,8},{12,... | collective-permute-start | bytes 1966088 | tf_op jit(solution)/shard_map/ppermute | solution.py:71
  13.3 16.6 %collective-permute-start.1 = (bf16[160,2048]{1,0:T(8,128)(2,1)S(1)}, bf16[160,2048]{1,0:T(8,128)(2,1)}, u32[]{:S(2)}, u32[]{:S(2)}) collective-permute-start(bf16[160,2048]{1,0:T(8,128)(2,1)S(1)} %fusion.2.n0.refs_0_.refs_5_), channel_id=1, source_target_pairs={{0,2},{2,4},{4,6},{6,0},{1,3},{3,5},{5,7},{7,1},{8,10},{10,12},{12... | collective-permute-start | bytes 1966088 | tf_op jit(solution)/shard_map/ppermute | solution.py:70
  14.3 29.2 %collective-permute-start.4 = (bf16[512,640]{1,0:T(8,128)(2,1)}, bf16[512,640]{1,0:T(8,128)(2,1)S(1)}, u32[]{:S(2)}, u32[]{:S(2)}) collective-permute-start(bf16[512,640]{1,0:T(8,128)(2,1)} %constant_dynamic-slice_fusion.5), channel_id=1, source_target_pairs={{0,1},{1,0},{2,3},{3,2},{4,5},{5,4},{6,7},{7,6},{8,9},{9,8},{10,11... | collective-permute-start | bytes 1966088 | tf_op jit(solution)/shard_map/ppermute | solution.py:134
  20.7 22.7 %collective-permute-start.5 = (bf16[128,2048]{1,0:T(8,128)(2,1)}, bf16[128,2048]{1,0:T(8,128)(2,1)S(1)}, u32[]{:S(2)}, u32[]{:S(2)}) collective-permute-start(bf16[128,2048]{1,0:T(8,128)(2,1)} %pad_maximum_fusion.1), channel_id=1, source_target_pairs={{0,1},{1,0},{2,3},{3,2},{4,5},{5,4},{6,7},{7,6},{8,9},{9,8},{10,11... | collective-permute-start | bytes 1572872 | tf_op jit(solution)/shard_map/ppermute | solution.py:924
  31.7 11.8 %collective-permute-start.2 = (bf16[80,2048]{1,0:T(8,128)(2,1)}, bf16[80,2048]{1,0:T(8,128)(2,1)S(1)}, u32[]{:S(2)}, u32[]{:S(2)}) collective-permute-start(bf16[80,2048]{1,0:T(8,128)(2,1)} %slice.37), channel_id=1, source_target_pairs={{0,2},{2,4},{4,6},{6,0},{1,3},{3,5},{5,7},{7,1},{8,10},{10,12},{12... | collective-permute-start | bytes 983048 | tf_op jit(solution)/shard_map/ppermute | solution.py:74
  31.7 11.8 %collective-permute-start.3 = (bf16[80,2048]{1,0:T(8,128)(2,1)S(1)}, bf16[80,2048]{1,0:T(8,128)(2,1)S(1)}, u32[]{:S(2)}, u32[]{:S(2)}) collective-permute-start(bf16[80,2048]{1,0:T(8,128)(2,1)S(1)} %slice.38), channel_id=1, source_target_pairs={{0,6},{2,0},{4,2},{6,4},{1,7},{3,1},{5,3},{7,5},{8,14},{10,8},{12,... | collective-permute-start | bytes 983048 | tf_op jit(solution)/shard_map/ppermute | solution.py:75
  44.4 98.5 %all-gather.6.cloned.1.call-start = ((), (), s32[]{:S(2)}) async-start(), calls=%async_computation.2 | async-start | bytes 6782976 | tf_op jit(solution)/shard_map/all_gather | solution.py:919
  47.3 30.7 %collective-permute-start.8 = (bf16[160,2048]{1,0:T(8,128)(2,1)S(1)}, bf16[160,2048]{1,0:T(8,128)(2,1)}, u32[]{:S(2)}, u32[]{:S(2)}) collective-permute-start(bf16[160,2048]{1,0:T(8,128)(2,1)S(1)} %copy-done.5), channel_id=1, source_target_pairs={{0,6},{2,0},{4,2},{6,4},{1,7},{3,1},{5,3},{7,5},{8,14},{10,8},{12,... | collective-permute-start | bytes 1966088 | tf_op jit(solution)/shard_map/ppermute | solution.py:932
  50.0 28.1 %collective-permute-start.9 = (bf16[160,2048]{1,0:T(8,128)(2,1)S(1)}, bf16[160,2048]{1,0:T(8,128)(2,1)}, u32[]{:S(2)}, u32[]{:S(2)}) collective-permute-start(bf16[160,2048]{1,0:T(8,128)(2,1)S(1)} %copy-done.5), channel_id=1, source_target_pairs={{0,4},{2,6},{4,0},{6,2},{1,5},{3,7},{5,1},{7,3},{8,12},{10,14},{12... | collective-permute-start | bytes 1966088 | tf_op jit(solution)/shard_map/ppermute | solution.py:932
  50.0 31.8 %collective-permute-start.10 = (bf16[160,2048]{1,0:T(8,128)(2,1)S(1)}, bf16[160,2048]{1,0:T(8,128)(2,1)}, u32[]{:S(2)}, u32[]{:S(2)}) collective-permute-start(bf16[160,2048]{1,0:T(8,128)(2,1)S(1)} %copy-done.5), channel_id=1, source_target_pairs={{0,2},{2,4},{4,6},{6,0},{1,3},{3,5},{5,7},{7,1},{8,10},{10,12},{12... | collective-permute-start | bytes 1966088 | tf_op jit(solution)/shard_map/ppermute | solution.py:932
  63.4 22.6 %collective-permute-start.19 = (bf16[128,2944]{1,0:T(8,128)(2,1)S(1)}, bf16[128,2944]{1,0:T(8,128)(2,1)S(1)}, u32[]{:S(2)}, u32[]{:S(2)}) collective-permute-start(bf16[128,2944]{1,0:T(8,128)(2,1)S(1)} %pad_maximum_fusion), channel_id=1, source_target_pairs={{0,17},{1,16},{16,1},{17,0},{2,19},{3,18},{18,3},{19,2},{4,21},{5,... | collective-permute-start | bytes 2261000 | tf_op jit(solution)/shard_map/ppermute | solution.py:936
  86.8 264.9 %reduce-scatter.2.cloned.1.call-start = ((), (), s32[]{:S(2)}) async-start(), calls=%async_computation.3 | async-start | bytes 17842176 | tf_op jit(solution)/shard_map/reduce_scatter | solution.py:964
  86.9 10.0 %collective-permute-start.11 = (bf16[80,2048]{1,0:T(8,128)(2,1)}, bf16[80,2048]{1,0:T(8,128)(2,1)S(1)}, u32[]{:S(2)}, u32[]{:S(2)}) collective-permute-start(bf16[80,2048]{1,0:T(8,128)(2,1)} %get-tuple-element.112), channel_id=1, source_target_pairs={{0,2},{2,4},{4,6},{6,0},{1,3},{3,5},{5,7},{7,1},{8,10},{10,12},{12... | collective-permute-start | bytes 983048 | tf_op jit(solution)/shard_map/ppermute | solution.py:86
  87.0 9.9 %collective-permute-start.12 = (bf16[80,2048]{1,0:T(8,128)(2,1)}, bf16[80,2048]{1,0:T(8,128)(2,1)S(1)}, u32[]{:S(2)}, u32[]{:S(2)}) collective-permute-start(bf16[80,2048]{1,0:T(8,128)(2,1)} %get-tuple-element.114), channel_id=1, source_target_pairs={{0,6},{2,0},{4,2},{6,4},{1,7},{3,1},{5,3},{7,5},{8,14},{10,8},{12,... | collective-permute-start | bytes 983048 | tf_op jit(solution)/shard_map/ppermute | solution.py:87
  100.0 16.2 %collective-permute-start.13 = (bf16[160,2048]{1,0:T(8,128)(2,1)}, bf16[160,2048]{1,0:T(8,128)(2,1)S(1)}, u32[]{:S(2)}, u32[]{:S(2)}) collective-permute-start(bf16[160,2048]{1,0:T(8,128)(2,1)} %get-tuple-element.115), channel_id=1, source_target_pairs={{0,2},{2,4},{4,6},{6,0},{1,3},{3,5},{5,7},{7,1},{8,10},{10,12},{12... | collective-permute-start | bytes 1966088 | tf_op jit(solution)/shard_map/ppermute | solution.py:108
  100.0 16.2 %collective-permute-start.14 = (bf16[160,2048]{1,0:T(8,128)(2,1)}, bf16[160,2048]{1,0:T(8,128)(2,1)S(1)}, u32[]{:S(2)}, u32[]{:S(2)}) collective-permute-start(bf16[160,2048]{1,0:T(8,128)(2,1)} %get-tuple-element.116), channel_id=1, source_target_pairs={{0,6},{2,0},{4,2},{6,4},{1,7},{3,1},{5,3},{7,5},{8,14},{10,8},{12,... | collective-permute-start | bytes 1966088 | tf_op jit(solution)/shard_map/ppermute | solution.py:108
  120.2 15.3 %collective-permute-start.16 = (bf16[160,2048]{1,0:T(8,128)(2,1)}, bf16[160,2048]{1,0:T(8,128)(2,1)S(1)}, u32[]{:S(2)}, u32[]{:S(2)}) collective-permute-start(bf16[160,2048]{1,0:T(8,128)(2,1)} %get-tuple-element.118.n0.refs_0_.refs_5_), channel_id=1, source_target_pairs={{0,2},{2,4},{4,6},{6,0},{1,3},{3,5},{5,7},{7,1},{8,10},{10,12},{12... | collective-permute-start | bytes 1966088 | tf_op jit(solution)/shard_map/ppermute | solution.py:70
  120.7 14.9 %collective-permute-start.15 = (bf16[160,2048]{1,0:T(8,128)(2,1)}, bf16[160,2048]{1,0:T(8,128)(2,1)S(1)}, u32[]{:S(2)}, u32[]{:S(2)}) collective-permute-start(bf16[160,2048]{1,0:T(8,128)(2,1)} %get-tuple-element.118.n0.refs_0_.refs_5_), channel_id=1, source_target_pairs={{0,6},{2,0},{4,2},{6,4},{1,7},{3,1},{5,3},{7,5},{8,14},{10,8},{12,... | collective-permute-start | bytes 1966088 | tf_op jit(solution)/shard_map/ppermute | solution.py:71
  179.9 12.3 %collective-permute-start.20 = (bf16[80,2048]{1,0:T(8,128)(2,1)}, bf16[80,2048]{1,0:T(8,128)(2,1)S(1)}, u32[]{:S(2)}, u32[]{:S(2)}) collective-permute-start(bf16[80,2048]{1,0:T(8,128)(2,1)} %get-tuple-element.129), channel_id=1, source_target_pairs={{0,2},{2,4},{4,6},{6,0},{1,3},{3,5},{5,7},{7,1},{8,10},{10,12},{12... | collective-permute-start | bytes 983048 | tf_op jit(solution)/shard_map/ppermute | solution.py:86
  181.1 11.1 %collective-permute-start.21 = (bf16[80,2048]{1,0:T(8,128)(2,1)}, bf16[80,2048]{1,0:T(8,128)(2,1)S(1)}, u32[]{:S(2)}, u32[]{:S(2)}) collective-permute-start(bf16[80,2048]{1,0:T(8,128)(2,1)} %get-tuple-element.131), channel_id=1, source_target_pairs={{0,6},{2,0},{4,2},{6,4},{1,7},{3,1},{5,3},{7,5},{8,14},{10,8},{12,... | collective-permute-start | bytes 983048 | tf_op jit(solution)/shard_map/ppermute | solution.py:87
  195.3 17.3 %collective-permute-start.22 = (bf16[160,2048]{1,0:T(8,128)(2,1)}, bf16[160,2048]{1,0:T(8,128)(2,1)S(1)}, u32[]{:S(2)}, u32[]{:S(2)}) collective-permute-start(bf16[160,2048]{1,0:T(8,128)(2,1)} %get-tuple-element.132), channel_id=1, source_target_pairs={{0,2},{2,4},{4,6},{6,0},{1,3},{3,5},{5,7},{7,1},{8,10},{10,12},{12... | collective-permute-start | bytes 1966088 | tf_op jit(solution)/shard_map/ppermute | solution.py:108
  195.3 17.3 %collective-permute-start.23 = (bf16[160,2048]{1,0:T(8,128)(2,1)}, bf16[160,2048]{1,0:T(8,128)(2,1)S(1)}, u32[]{:S(2)}, u32[]{:S(2)}) collective-permute-start(bf16[160,2048]{1,0:T(8,128)(2,1)} %get-tuple-element.133), channel_id=1, source_target_pairs={{0,6},{2,0},{4,2},{6,4},{1,7},{3,1},{5,3},{7,5},{8,14},{10,8},{12,... | collective-permute-start | bytes 1966088 | tf_op jit(solution)/shard_map/ppermute | solution.py:108
  213.7 209.8 %all-gather.8.cloned.1.call-start = ((), (), s32[]{:S(2)}) async-start(), calls=%async_computation.4 | async-start | bytes 9191424 | tf_op jit(solution)/shard_map/all_gather | solution.py:1001
  217.7 12.2 %collective-permute-start.24 = (bf16[160,2048]{1,0:T(8,128)(2,1)}, bf16[160,2048]{1,0:T(8,128)(2,1)S(1)}, u32[]{:S(2)}, u32[]{:S(2)}) collective-permute-start(bf16[160,2048]{1,0:T(8,128)(2,1)} %get-tuple-element.138.b0.refs_10_), channel_id=1, source_target_pairs={{0,2},{2,4},{4,6},{6,0},{1,3},{3,5},{5,7},{7,1},{8,10},{10,12},{12... | collective-permute-start | bytes 1966088 | tf_op jit(solution)/shard_map/ppermute | solution.py:70
  217.8 12.1 %collective-permute-start.25 = (bf16[160,2048]{1,0:T(8,128)(2,1)}, bf16[160,2048]{1,0:T(8,128)(2,1)S(1)}, u32[]{:S(2)}, u32[]{:S(2)}) collective-permute-start(bf16[160,2048]{1,0:T(8,128)(2,1)} %get-tuple-element.138.b0.refs_10_), channel_id=1, source_target_pairs={{0,6},{2,0},{4,2},{6,4},{1,7},{3,1},{5,3},{7,5},{8,14},{10,8},{12,... | collective-permute-start | bytes 1966088 | tf_op jit(solution)/shard_map/ppermute | solution.py:71
  229.9 13.4 %collective-permute-start.26 = (bf16[80,2048]{1,0:T(8,128)(2,1)S(1)}, bf16[80,2048]{1,0:T(8,128)(2,1)S(1)}, u32[]{:S(2)}, u32[]{:S(2)}) collective-permute-start(bf16[80,2048]{1,0:T(8,128)(2,1)S(1)} %slice.41), channel_id=1, source_target_pairs={{0,2},{2,4},{4,6},{6,0},{1,3},{3,5},{5,7},{7,1},{8,10},{10,12},{12... | collective-permute-start | bytes 983048 | tf_op jit(solution)/shard_map/ppermute | solution.py:74
  230.0 13.3 %collective-permute-start.27 = (bf16[80,2048]{1,0:T(8,128)(2,1)S(1)}, bf16[80,2048]{1,0:T(8,128)(2,1)}, u32[]{:S(2)}, u32[]{:S(2)}) collective-permute-start(bf16[80,2048]{1,0:T(8,128)(2,1)S(1)} %slice.42), channel_id=1, source_target_pairs={{0,6},{2,0},{4,2},{6,4},{1,7},{3,1},{5,3},{7,5},{8,14},{10,8},{12,... | collective-permute-start | bytes 983048 | tf_op jit(solution)/shard_map/ppermute | solution.py:75
  243.4 26.6 %collective-permute-start.28 = (bf16[160,2048]{1,0:T(8,128)(2,1)}, bf16[160,2048]{1,0:T(8,128)(2,1)S(1)}, u32[]{:S(2)}, u32[]{:S(2)}) collective-permute-start(bf16[160,2048]{1,0:T(8,128)(2,1)} %get-tuple-element.141), channel_id=1, source_target_pairs={{0,2},{2,4},{4,6},{6,0},{1,3},{3,5},{5,7},{7,1},{8,10},{10,12},{12... | collective-permute-start | bytes 1966088 | tf_op jit(solution)/shard_map/ppermute | solution.py:977
  243.5 26.6 %collective-permute-start.29 = (bf16[160,2048]{1,0:T(8,128)(2,1)}, bf16[160,2048]{1,0:T(8,128)(2,1)S(1)}, u32[]{:S(2)}, u32[]{:S(2)}) collective-permute-start(bf16[160,2048]{1,0:T(8,128)(2,1)} %get-tuple-element.143), channel_id=1, source_target_pairs={{0,6},{2,0},{4,2},{6,4},{1,7},{3,1},{5,3},{7,5},{8,14},{10,8},{12,... | collective-permute-start | bytes 1966088 | tf_op jit(solution)/shard_map/ppermute | solution.py:977
  266.9 12.7 %collective-permute-start.30 = (bf16[640,128]{1,0:T(8,128)(2,1)}, bf16[640,128]{1,0:T(8,128)(2,1)S(1)}, u32[]{:S(2)}, u32[]{:S(2)}) collective-permute-start(bf16[640,128]{1,0:T(8,128)(2,1)} %get-tuple-element.151), channel_id=1, source_target_pairs={{0,1},{1,0},{2,3},{3,2},{4,5},{5,4},{6,7},{7,6},{8,9},{9,8},{10,11... | collective-permute-start | bytes 491528 | tf_op jit(solution)/shard_map/ppermute | solution.py:982
  279.7 18.7 %collective-permute-start.31 = (bf16[4,2,1024,128]{3,2,1,0:T(8,128)(2,1)}, bf16[4,2,1024,128]{3,2,1,0:T(8,128)(2,1)S(1)}, u32[]{:S(2)}, u32[]{:S(2)}) collective-permute-start(bf16[4,2,1024,128]{3,2,1,0:T(8,128)(2,1)} %get-tuple-element.153), channel_id=1, source_target_pairs={{0,8},{8,0},{1,9},{9,1},{2,10},{10,2},{3,11},{11,3},{4,12},{12,4},... | collective-permute-start | bytes 6291464 | tf_op jit(solution)/shard_map/ppermute | solution.py:806
  303.7 20.8 %collective-permute-start.33 = (bf16[2,1168,128]{2,1,0:T(8,128)(2,1)}, bf16[2,1168,128]{2,1,0:T(8,128)(2,1)S(1)}, u32[]{:S(2)}, u32[]{:S(2)}) collective-permute-start(bf16[2,1168,128]{2,1,0:T(8,128)(2,1)} %get-tuple-element.159), channel_id=1, source_target_pairs={{0,64},{32,96},{64,0},{96,32},{1,65},{33,97},{65,1},{97,33},{2,66}... | collective-permute-start | bytes 1794056 | tf_op jit(solution)/shard_map/ppermute | solution.py:810
  306.6 30.7 %collective-permute-start.34 = (bf16[2,1168,128]{2,1,0:T(8,128)(2,1)}, bf16[2,1168,128]{2,1,0:T(8,128)(2,1)S(1)}, u32[]{:S(2)}, u32[]{:S(2)}) collective-permute-start(bf16[2,1168,128]{2,1,0:T(8,128)(2,1)} %get-tuple-element.160), channel_id=1, source_target_pairs={{0,32},{32,64},{64,96},{96,0},{1,33},{33,65},{65,97},{97,1},{2,34}... | collective-permute-start | bytes 1794056 | tf_op jit(solution)/shard_map/ppermute | solution.py:810
  307.0 30.3 %collective-permute-start.35 = (bf16[2,1168,128]{2,1,0:T(8,128)(2,1)}, bf16[2,1168,128]{2,1,0:T(8,128)(2,1)S(1)}, u32[]{:S(2)}, u32[]{:S(2)}) collective-permute-start(bf16[2,1168,128]{2,1,0:T(8,128)(2,1)} %get-tuple-element.161), channel_id=1, source_target_pairs={{0,96},{32,0},{64,32},{96,64},{1,97},{33,1},{65,33},{97,65},{2,98}... | collective-permute-start | bytes 1794056 | tf_op jit(solution)/shard_map/ppermute | solution.py:810
  354.5 12.8 %collective-permute-start.41 = (bf16[1168,128]{1,0:T(8,128)(2,1)}, bf16[1168,128]{1,0:T(8,128)(2,1)S(1)}, u32[]{:S(2)}, u32[]{:S(2)}) collective-permute-start(bf16[1168,128]{1,0:T(8,128)(2,1)} %get-tuple-element.177.a), channel_id=1, source_target_pairs={{0,16},{16,0},{1,17},{17,1},{2,18},{18,2},{3,19},{19,3},{4,20},{20... | collective-permute-start | bytes 897032 | tf_op jit(solution)/shard_map/ppermute | solution.py:820
  355.4 15.9 %collective-permute-start.42 = (bf16[1168,128]{1,0:T(8,128)(2,1)}, bf16[1168,128]{1,0:T(8,128)(2,1)S(1)}, u32[]{:S(2)}, u32[]{:S(2)}) collective-permute-start(bf16[1168,128]{1,0:T(8,128)(2,1)} %get-tuple-element.178), channel_id=1, source_target_pairs={{0,1},{1,0},{2,3},{3,2},{4,5},{5,4},{6,7},{7,6},{8,9},{9,8},{10,11... | collective-permute-start | bytes 897032 | tf_op jit(solution)/shard_map/ppermute | solution.py:821
  357.8 13.5 %collective-permute-start.43 = (bf16[1168,128]{1,0:T(8,128)(2,1)}, bf16[1168,128]{1,0:T(8,128)(2,1)S(1)}, u32[]{:S(2)}, u32[]{:S(2)}) collective-permute-start(bf16[1168,128]{1,0:T(8,128)(2,1)} %get-tuple-element.178), channel_id=1, source_target_pairs={{0,17},{1,16},{16,1},{17,0},{2,19},{3,18},{18,3},{19,2},{4,21},{5,... | collective-permute-start | bytes 897032 | tf_op jit(solution)/shard_map/ppermute | solution.py:822
  364.6 44.9 %collective-permute-start.39 = (bf16[160,2048]{1,0:T(8,128)(2,1)}, bf16[160,2048]{1,0:T(8,128)(2,1)S(1)}, u32[]{:S(2)}, u32[]{:S(2)}) collective-permute-start(bf16[160,2048]{1,0:T(8,128)(2,1)} %get-tuple-element.174), channel_id=1, source_target_pairs={{0,2},{2,4},{4,6},{6,0},{1,3},{3,5},{5,7},{7,1},{8,10},{10,12},{12... | collective-permute-start | bytes 1966088 | tf_op jit(solution)/shard_map/ppermute | solution.py:108
  364.6 45.0 %collective-permute-start.40 = (bf16[160,2048]{1,0:T(8,128)(2,1)}, bf16[160,2048]{1,0:T(8,128)(2,1)S(1)}, u32[]{:S(2)}, u32[]{:S(2)}) collective-permute-start(bf16[160,2048]{1,0:T(8,128)(2,1)} %get-tuple-element.175), channel_id=1, source_target_pairs={{0,6},{2,0},{4,2},{6,4},{1,7},{3,1},{5,3},{7,5},{8,14},{10,8},{12,... | collective-permute-start | bytes 1966088 | tf_op jit(solution)/shard_map/ppermute | solution.py:108
  374.8 10.6 %collective-permute-start.44 = (bf16[1168,128]{1,0:T(8,128)(2,1)}, bf16[1168,128]{1,0:T(8,128)(2,1)}, u32[]{:S(2)}, u32[]{:S(2)}) collective-permute-start(bf16[1168,128]{1,0:T(8,128)(2,1)} %sum_z.1.refs_0_), channel_id=1, source_target_pairs={{0,32},{32,64},{64,96},{96,0},{1,33},{33,65},{65,97},{97,1},{2,34}... | collective-permute-start | bytes 897032 | tf_op jit(solution)/shard_map/ppermute | solution.py:827
  375.4 46.7 %collective-permute-start.36 = (bf16[160,2048]{1,0:T(8,128)(2,1)}, bf16[160,2048]{1,0:T(8,128)(2,1)S(1)}, u32[]{:S(2)}, u32[]{:S(2)}) collective-permute-start(bf16[160,2048]{1,0:T(8,128)(2,1)} %get-tuple-element.163), channel_id=1, source_target_pairs={{0,4},{2,6},{4,0},{6,2},{1,5},{3,7},{5,1},{7,3},{8,12},{10,14},{12... | collective-permute-start | bytes 1966088 | tf_op jit(solution)/shard_map/ppermute | solution.py:1000
  377.1 24.3 %collective-permute-start.45 = (bf16[1168,128]{1,0:T(8,128)(2,1)}, bf16[1168,128]{1,0:T(8,128)(2,1)}, u32[]{:S(2)}, u32[]{:S(2)}) collective-permute-start(bf16[1168,128]{1,0:T(8,128)(2,1)} %sum_z.1.refs_0_), channel_id=1, source_target_pairs={{0,64},{32,96},{64,0},{96,32},{1,65},{33,97},{65,1},{97,33},{2,66}... | collective-permute-start | bytes 897032 | tf_op jit(solution)/shard_map/ppermute | solution.py:827
  385.5 28.9 %collective-permute-start.46 = (bf16[1168,128]{1,0:T(8,128)(2,1)}, bf16[1168,128]{1,0:T(8,128)(2,1)}, u32[]{:S(2)}, u32[]{:S(2)}) collective-permute-start(bf16[1168,128]{1,0:T(8,128)(2,1)} %sum_z.1.refs_0_), channel_id=1, source_target_pairs={{0,96},{32,0},{64,32},{96,64},{1,97},{33,1},{65,33},{97,65},{2,98}... | collective-permute-start | bytes 897032 | tf_op jit(solution)/shard_map/ppermute | solution.py:827
  401.5 13.4 %collective-permute-start.47 = (bf16[1168,128]{1,0:T(8,128)(2,1)}, bf16[1168,128]{1,0:T(8,128)(2,1)}, u32[]{:S(2)}, u32[]{:S(2)}) collective-permute-start(bf16[1168,128]{1,0:T(8,128)(2,1)} %sum_z.1.refs_0_), channel_id=1, source_target_pairs={{0,8},{8,0},{1,9},{9,1},{2,10},{10,2},{3,11},{11,3},{4,12},{12,4},... | collective-permute-start | bytes 897032 | tf_op jit(solution)/shard_map/ppermute | solution.py:829
  420.7 12.6 %collective-permute-start.53 = (f32[2,2048]{1,0:T(2,128)}, f32[2,2048]{1,0:T(2,128)S(1)}, u32[]{:S(2)}, u32[]{:S(2)}) collective-permute-start(f32[2,2048]{1,0:T(2,128)} %get-tuple-element.180), channel_id=1, source_target_pairs={{0,6},{2,0},{4,2},{6,4},{1,7},{3,1},{5,3},{7,5},{8,14},{10,8},{12,... | collective-permute-start | bytes 49160 | tf_op jit(solution)/shard_map/ppermute | solution.py:991
  420.8 12.4 %collective-permute-start.52 = (f32[2,2048]{1,0:T(2,128)}, f32[2,2048]{1,0:T(2,128)S(1)}, u32[]{:S(2)}, u32[]{:S(2)}) collective-permute-start(f32[2,2048]{1,0:T(2,128)} %get-tuple-element.180), channel_id=1, source_target_pairs={{0,4},{2,6},{4,0},{6,2},{1,5},{3,7},{5,1},{7,3},{8,12},{10,14},{12... | collective-permute-start | bytes 49160 | tf_op jit(solution)/shard_map/ppermute | solution.py:991
  421.5 11.7 %collective-permute-start.51 = (f32[2,2048]{1,0:T(2,128)}, f32[2,2048]{1,0:T(2,128)S(1)}, u32[]{:S(2)}, u32[]{:S(2)}) collective-permute-start(f32[2,2048]{1,0:T(2,128)} %get-tuple-element.180), channel_id=1, source_target_pairs={{0,2},{2,4},{4,6},{6,0},{1,3},{3,5},{5,7},{7,1},{8,10},{10,12},{12... | collective-permute-start | bytes 49160 | tf_op jit(solution)/shard_map/ppermute | solution.py:991
  (55 other events, 316.6 us)
Sparse Core Ops, SparseCore 0:
  44.4 35.0 all-gather.3
  87.0 39.9 all-gather.5
  212.8 138.9 reduce-scatter.1
  353.3 67.5 all-gather.7
